TPU v7x, 32 devices: a whole 2x2x4 slice. The times are simulated.
32 devices in a mesh: cand: 8 (over y, x, core), tensor: 4 (over z).
Axes of the slice: x: 2, y: 2, z: 4, core: 2. Of those that a mesh axis runs over, the one named last changes fastest.
Arguments:
- hidden_in: bfloat16 [4096, 5120], P('cand', 'tensor')
- lengths: int32 [8], P('cand'), may hold values from 256 to 512, as said below
- summary_pos: int32 [8, 128], P('cand'), may hold values from 0 to 511, as said below
- w_query: bfloat16 [5120, 4096], P(None, 'tensor')
- w_key: bfloat16 [5120, 512], P(None, 'tensor')
- w_value: bfloat16 [5120, 512], P(None, 'tensor'), may hold values from -0.078125 to 0.078125
- w_out: bfloat16 [4096, 5120], P('tensor'), may hold values from -0.09375 to 0.09375
- q_gain: float32 [128], replicated
- k_gain: float32 [128], replicated
Outputs:
- mixed: bfloat16 [4096, 5120], P(('cand', 'tensor'))
Inputs may be any that keep to these rules, and one draw needn't show every extreme that they name: `lengths`: some candidate has exactly 512 valid tokens and some exactly half of 512. `summary_pos`: each candidate's positions are distinct, ascending and below its length; the first is 0 and the last is its length minus one.
All inputs are finite; a program needn't handle non-finite values.
Results may differ from a plain program's by a relative error of at most 0.013.
The roundings to bfloat16 on the way count: a program that leaves them out, or rounds other values in their place, can miss the bound.
Values may be sent and summed in bfloat16 or wider, within the bound.
No kernel may reach another device: no remote copies, remote signals or barrier semaphores. Data moves between devices by JAX's collectives and lax.ppermute only.
A program may use at most 128 MiB of HBM per device.

v0:
```python
import jax
import jax.numpy as jnp
from jax import lax
from jax.sharding import PartitionSpec as P


def passed_along(array, axis, by):
    peers = lax.axis_size(axis)
    return lax.ppermute(array, axis, [(i, (i + by) % peers) for i in range(peers)])


def rope_tables(rows, width):
    half_width = width // 2
    frequency = 1000000.0 ** (-(jnp.arange(half_width, dtype=jnp.float32) * 2.0 / width))
    angle = jnp.arange(rows, dtype=jnp.float32)[:, None] * frequency[None, :]
    angle = jnp.concatenate([angle, angle], axis=1)
    return (jnp.cos(angle), jnp.sin(angle))


def rotate(vectors, cosine, sine):
    half_width = vectors.shape[-1] // 2
    turned = jnp.concatenate([-vectors[..., half_width:], vectors[..., :half_width]], axis=-1)
    return vectors * cosine + turned * sine


def head_norm(vectors, gain):
    return vectors * lax.rsqrt(jnp.mean(vectors * vectors, axis=-1, keepdims=True) + 1e-06) * gain


def absorb(state, queries, keys_in, values_in, allowed):
    running_max, running_sum, numerator = state
    scores = jnp.einsum("kgth,ksh->kgts", queries, keys_in, preferred_element_type=jnp.float32)
    scores = scores * queries.shape[-1] ** (-0.5)
    if allowed is not None:
        scores = jnp.where(allowed, scores, -1e30)
    new_max = jnp.maximum(running_max, jnp.max(scores, axis=-1))
    factor = jnp.exp(running_max - new_max)
    expo = jnp.exp(scores - new_max[..., None])
    running_sum = running_sum * factor + jnp.sum(expo, axis=-1)
    numerator = numerator * factor[..., None] + jnp.einsum(
        "kgts,ksh->kgth", expo.astype(jnp.bfloat16), values_in, preferred_element_type=jnp.float32
    )
    return (new_max, running_sum, numerator)


def shards(hidden_in, lengths, summary_pos, w_query, w_key, w_value, w_out, q_gain, k_gain):
    rows_here = hidden_in.shape[0]
    head_width = q_gain.shape[0]
    heads_here = w_query.shape[1] // head_width
    groups_here = w_key.shape[1] // head_width
    per_group = heads_here // groups_here
    piece = lax.all_gather(hidden_in, "tensor", axis=1, tiled=True)
    proj_query = jnp.dot(piece, w_query, preferred_element_type=jnp.float32)
    proj_key = jnp.dot(piece, w_key, preferred_element_type=jnp.float32)
    proj_value = jnp.dot(piece, w_value, preferred_element_type=jnp.float32)
    cosine, sine = rope_tables(rows_here, head_width)
    queries = proj_query.reshape(rows_here, heads_here, head_width).transpose(1, 0, 2)
    queries = rotate(head_norm(queries, q_gain), cosine, sine).astype(jnp.bfloat16)
    queries = queries.reshape(groups_here, per_group, rows_here, head_width)
    keys_self = proj_key.reshape(rows_here, groups_here, head_width).transpose(1, 0, 2)
    keys_self = rotate(head_norm(keys_self, k_gain), cosine, sine).astype(jnp.bfloat16)
    values_self = (
        proj_value.astype(jnp.bfloat16)
        .reshape(rows_here, groups_here, head_width)
        .transpose(1, 0, 2)
    )
    length = lengths[0]
    positions = jnp.arange(rows_here, dtype=jnp.int32)
    allowed = (positions[None, :] <= positions[:, None]) & (positions[None, :] < length)
    state = (
        jnp.full((groups_here, per_group, rows_here), -1e30, jnp.float32),
        jnp.zeros((groups_here, per_group, rows_here), jnp.float32),
        jnp.zeros((groups_here, per_group, rows_here, head_width), jnp.float32),
    )
    state = absorb(state, queries, keys_self, values_self, allowed)
    chosen = summary_pos[0]
    travel = jnp.stack([keys_self[:, chosen, :], values_self[:, chosen, :]])
    n_cand = lax.axis_size("cand")

    def hop(turn_index, carry):
        moving, current = carry
        moving = passed_along(moving, "cand", 1)
        return (moving, absorb(current, queries, moving[0], moving[1], None))

    travel, state = lax.fori_loop(0, n_cand - 1, hop, (travel, state))
    running_max, running_sum, numerator = state
    attended = (numerator / running_sum[..., None]).reshape(heads_here, rows_here, head_width)
    attended = attended.transpose(1, 0, 2).reshape(rows_here, heads_here * head_width)
    attended = jnp.where(positions[:, None] < length, attended, 0.0).astype(jnp.bfloat16)
    return lax.psum_scatter(
        jnp.dot(attended, w_out, preferred_element_type=jnp.float32).astype(jnp.bfloat16),
        "tensor",
        scatter_dimension=0,
        tiled=True,
    )


def solution(mesh):
    return jax.shard_map(
        shards,
        mesh=mesh,
        in_specs=(
            P("cand", "tensor"),
            P("cand"),
            P("cand", None),
            P(None, "tensor"),
            P(None, "tensor"),
            P(None, "tensor"),
            P("tensor", None),
            P(),
            P(),
        ),
        out_specs=P(("cand", "tensor"), None),
        check_vma=False,
    )
```

profile of v0, /device:TPU:0, one launch (start us, length us, event | category | flops | bytes accessed | tf_op | source)
XLA Modules:
  0.0 325.9 jit_solution(8280208525922859417)
XLA Ops:
  6.5 0.7 all-gather.2.cloned.1.call-update
  8.0 0.7 fusion.34
  8.7 0.1 iota_multiply_fusion
  8.7 0.8 fusion.24
  9.6 100.1 %all-gather.2.cloned.1.call-done = bf16[512,5120]{1,0:T(8,128)(2,1)} async-done(((bf16[512,1280]{1,0:T(8,128)(2,1)}), bf16[512,5120]{1,0:T(8,128)(2,1)}) %all-gather.2.cloned.1.call-update) | async-done | bytes 5242896 | tf_op jit(solution)/shard_map/all_gather | solution.py:52
  109.7 4.4 %multiply_reduce_fusion.1 = (f32[512]{0:T(512)S(1)}, f32[512,128]{0,1:T(8,128)S(1)}) fusion(bf16[512,5120]{1,0:T(8,128)(2,1)} %all-gather.2.cloned.1.call-done, bf16[5120,128]{1,0:T(8,128)(2,1)S(1)} %copy-done), kind=kOutput, calls=%fused_computation.50 | convolution fusion | flops 671219200 | bytes 6817792 | tf_op jit(solution)/shard_map/dot_general | solution.py:54
  114.1 0.1 fusion.29
  114.2 1.9 fusion.26
  116.1 0.1 copy.17
  116.2 4.0 %convolution_convert_fusion.1 = bf16[512,128]{1,0:T(8,128)(2,1)S(1)} fusion(bf16[512,5120]{1,0:T(8,128)(2,1)} %all-gather.2.cloned.1.call-done, bf16[5120,128]{1,0:T(8,128)(2,1)S(1)} %copy-done.11), kind=kOutput, calls=%fused_computation.39 | convolution fusion | flops 671154176 | bytes 6684672 | tf_op jit(solution)/shard_map/dot_general | solution.py:55
  120.3 1.3 gather_fusion.1
  121.6 1.3 gather_fusion
  122.9 9.8 %convolution_bitcast_fusion = f32[64,8,8,128]{3,2,1,0:T(8,128)S(1)} fusion(bf16[512,5120]{1,0:T(8,128)(2,1)} %all-gather.2.cloned.1.call-done, bf16[5120,1024]{1,0:T(8,128)(2,1)} %param.14), kind=kOutput, calls=%fused_computation.38 | convolution fusion | flops 5368709120 | bytes 17825792 | tf_op jit(solution)/shard_map/dot_general | solution.py:53
  132.7 0.6 fusion.17
  133.4 0.6 fusion.18
  134.0 2.6 slice_negate_fusion
  136.6 1.8 copy.20
  138.4 1.8 copy.19
  140.2 3.0 fusion.20
  143.2 1.9 fusion.9
  145.2 1.7 fusion.11
  147.0 2.8 add_bitcast_fusion
  149.9 0.6 pad_maximum_fusion.1
  150.5 61.8 %while.16 = (s32[]{:T(128)}, bf16[2,1,128,128]{3,2,1,0:T(8,128)(2,1)}, f32[1,8,512]{2,1,0:T(8,128)S(1)}, f32[1,8,512]{2,1,0:T(8,128)S(1)}, f32[1,8,512,128]{3,2,...) while((s32[]{:T(128)}, bf16[2,1,128,128]{3,2,1,0:T(8,128)(2,1)}, f32[1,8,512]{2,1,0:T(8,128)S(1)}, ...), condition=%wide.region_7.8_spmd, body=%wide.region_4.7_spmd.sunk | while | flops 273690624 | bytes 12255349 | solution.py:85
  150.5 4.8 %collective-permute-done = bf16[2,1,128,128]{3,2,1,0:T(8,128)(2,1)S(1)} collective-permute-done((bf16[2,1,128,128]{3,2,1,0:T(8,128)(2,1)}, bf16[2,1,128,128]{3,2,1,0:T(8,128)(2,1)S(1)}, u32[]{:S(2)}, u32[]{:S(2)}) %collective-permute-start) | collective-permute-done | bytes 65568 | tf_op jit(solution)/shard_map/while/body/eval_jaxpr/ppermute | solution.py:9
  155.3 1.7 multiply_reduce_fusion.3
  157.0 0.4 fusion.52
  157.4 0.6 copy.41
  158.0 1.2 bitcast_add_fusion.6
  159.3 4.8 %collective-permute-done = bf16[2,1,128,128]{3,2,1,0:T(8,128)(2,1)S(1)} collective-permute-done((bf16[2,1,128,128]{3,2,1,0:T(8,128)(2,1)}, bf16[2,1,128,128]{3,2,1,0:T(8,128)(2,1)S(1)}, u32[]{:S(2)}, u32[]{:S(2)}) %collective-permute-start) | collective-permute-done | bytes 65568 | tf_op jit(solution)/shard_map/while/body/eval_jaxpr/ppermute | solution.py:9
  164.1 1.7 multiply_reduce_fusion.3
  165.8 0.4 fusion.52
  166.2 0.6 copy.41
  166.8 1.2 bitcast_add_fusion.6
  168.2 4.8 %collective-permute-done = bf16[2,1,128,128]{3,2,1,0:T(8,128)(2,1)S(1)} collective-permute-done((bf16[2,1,128,128]{3,2,1,0:T(8,128)(2,1)}, bf16[2,1,128,128]{3,2,1,0:T(8,128)(2,1)S(1)}, u32[]{:S(2)}, u32[]{:S(2)}) %collective-permute-start) | collective-permute-done | bytes 65568 | tf_op jit(solution)/shard_map/while/body/eval_jaxpr/ppermute | solution.py:9
  173.0 1.7 multiply_reduce_fusion.3
  174.7 0.4 fusion.52
  175.1 0.6 copy.41
  175.7 1.2 bitcast_add_fusion.6
  177.0 4.8 %collective-permute-done = bf16[2,1,128,128]{3,2,1,0:T(8,128)(2,1)S(1)} collective-permute-done((bf16[2,1,128,128]{3,2,1,0:T(8,128)(2,1)}, bf16[2,1,128,128]{3,2,1,0:T(8,128)(2,1)S(1)}, u32[]{:S(2)}, u32[]{:S(2)}) %collective-permute-start) | collective-permute-done | bytes 65568 | tf_op jit(solution)/shard_map/while/body/eval_jaxpr/ppermute | solution.py:9
  181.8 1.7 multiply_reduce_fusion.3
  183.5 0.4 fusion.52
  183.9 0.6 copy.41
  184.5 1.2 bitcast_add_fusion.6
  185.9 4.8 %collective-permute-done = bf16[2,1,128,128]{3,2,1,0:T(8,128)(2,1)S(1)} collective-permute-done((bf16[2,1,128,128]{3,2,1,0:T(8,128)(2,1)}, bf16[2,1,128,128]{3,2,1,0:T(8,128)(2,1)S(1)}, u32[]{:S(2)}, u32[]{:S(2)}) %collective-permute-start) | collective-permute-done | bytes 65568 | tf_op jit(solution)/shard_map/while/body/eval_jaxpr/ppermute | solution.py:9
  190.7 1.7 multiply_reduce_fusion.3
  192.3 0.4 fusion.52
  192.8 0.6 copy.41
  193.4 1.2 bitcast_add_fusion.6
  194.7 4.8 %collective-permute-done = bf16[2,1,128,128]{3,2,1,0:T(8,128)(2,1)S(1)} collective-permute-done((bf16[2,1,128,128]{3,2,1,0:T(8,128)(2,1)}, bf16[2,1,128,128]{3,2,1,0:T(8,128)(2,1)S(1)}, u32[]{:S(2)}, u32[]{:S(2)}) %collective-permute-start) | collective-permute-done | bytes 65568 | tf_op jit(solution)/shard_map/while/body/eval_jaxpr/ppermute | solution.py:9
  199.5 1.7 multiply_reduce_fusion.3
  201.2 0.4 fusion.52
  201.6 0.6 copy.41
  202.2 1.2 bitcast_add_fusion.6
  203.5 4.8 %collective-permute-done = bf16[2,1,128,128]{3,2,1,0:T(8,128)(2,1)S(1)} collective-permute-done((bf16[2,1,128,128]{3,2,1,0:T(8,128)(2,1)}, bf16[2,1,128,128]{3,2,1,0:T(8,128)(2,1)S(1)}, u32[]{:S(2)}, u32[]{:S(2)}) %collective-permute-start) | collective-permute-done | bytes 65568 | tf_op jit(solution)/shard_map/while/body/eval_jaxpr/ppermute | solution.py:9
  208.3 1.7 multiply_reduce_fusion.3
  210.0 0.4 fusion.52
  210.4 0.6 copy.41
  211.1 1.2 bitcast_add_fusion.6
  212.3 1.9 copy.22
  214.2 1.9 broadcast_divide_fusion
  216.1 0.3 fusion.21
  216.3 11.4 %convolution_convert_fusion = bf16[512,5120]{1,0:T(8,128)(2,1)} fusion(bf16[512,1024]{0,1:T(8,128)(2,1)S(1)} %fusion.21, bf16[1024,5120]{1,0:T(8,128)(2,1)} %param.17), kind=kOutput, calls=%fused_computation.20 | convolution fusion | flops 5371330560 | bytes 16777216 | tf_op jit(solution)/shard_map/dot_general | solution.py:91
  227.8 91.3 %reduce-scatter.2.cloned.1.call-done = bf16[128,5120]{1,0:T(8,128)(2,1)} async-done(((bf16[512,5120]{1,0:T(8,128)(2,1)}), bf16[128,5120]{1,0:T(8,128)(2,1)}) %reduce-scatter.2.cloned.1.call-update) | async-done | bytes 1310736 | tf_op jit(solution)/shard_map/reduce_scatter | solution.py:90
  (63 shorter events, 0.7 us)
Async XLA Ops:
  6.5 103.2 %copy-start = (bf16[5120,128]{1,0:T(8,128)(2,1)S(1)}, bf16[5120,128]{1,0:T(8,128)(2,1)}, u32[]{:S(2)}) copy-start(bf16[5120,128]{1,0:T(8,128)(2,1)} %param.15) | copy-start | bytes 3932164
  6.5 103.2 %all-gather.2.cloned.1.call-start = ((), (), s32[]{:S(2)}) async-start(), calls=%async_computation.1 | async-start | bytes 6553600 | tf_op jit(solution)/shard_map/all_gather | solution.py:52
  7.3 311.8 %reduce-scatter.2.cloned.1.call-start = ((), (), s32[]{:S(2)}) async-start(), calls=%async_computation.2 | async-start | bytes 6553600 | tf_op jit(solution)/shard_map/reduce_scatter | solution.py:90
  8.0 1.6 copy-start.9
  9.6 104.5 %copy-start.7 = (f32[128]{0:T(128)S(1)}, f32[128]{0:T(128)}, u32[]{:S(2)}) copy-start(f32[128]{0:T(128)} %param.19) | copy-start | bytes 1540
  114.1 2.2 copy-start.11
  120.3 1.3 copy-start.3
  132.7 0.7 copy-start.8
  140.2 3.0 copy-start.2
  143.2 2.0 copy-start.1
  145.2 1.8 copy-start.4
  147.0 2.9 copy-start.5
  147.0 2.9 copy-start.6
  150.5 4.8 %collective-permute-start = (bf16[2,1,128,128]{3,2,1,0:T(8,128)(2,1)}, bf16[2,1,128,128]{3,2,1,0:T(8,128)(2,1)S(1)}, u32[]{:S(2)}, u32[]{:S(2)}) collective-permute-start(bf16[2,1,128,128]{3,2,1,0:T(8,128)(2,1)} %get-tuple-element.123), channel_id=1, source_target_pairs={{0,4},{4,8},{8,12},{12,16},{16,20},{20,24},{24,28},{28,0},{1,5},{5... | collective-permute-start | bytes 196616 | tf_op jit(solution)/shard_map/while/body/eval_jaxpr/ppermute | solution.py:9
  159.3 4.9 %collective-permute-start = (bf16[2,1,128,128]{3,2,1,0:T(8,128)(2,1)}, bf16[2,1,128,128]{3,2,1,0:T(8,128)(2,1)S(1)}, u32[]{:S(2)}, u32[]{:S(2)}) collective-permute-start(bf16[2,1,128,128]{3,2,1,0:T(8,128)(2,1)} %get-tuple-element.123), channel_id=1, source_target_pairs={{0,4},{4,8},{8,12},{12,16},{16,20},{20,24},{24,28},{28,0},{1,5},{5... | collective-permute-start | bytes 196616 | tf_op jit(solution)/shard_map/while/body/eval_jaxpr/ppermute | solution.py:9
  168.1 4.9 %collective-permute-start = (bf16[2,1,128,128]{3,2,1,0:T(8,128)(2,1)}, bf16[2,1,128,128]{3,2,1,0:T(8,128)(2,1)S(1)}, u32[]{:S(2)}, u32[]{:S(2)}) collective-permute-start(bf16[2,1,128,128]{3,2,1,0:T(8,128)(2,1)} %get-tuple-element.123), channel_id=1, source_target_pairs={{0,4},{4,8},{8,12},{12,16},{16,20},{20,24},{24,28},{28,0},{1,5},{5... | collective-permute-start | bytes 196616 | tf_op jit(solution)/shard_map/while/body/eval_jaxpr/ppermute | solution.py:9
  177.0 4.9 %collective-permute-start = (bf16[2,1,128,128]{3,2,1,0:T(8,128)(2,1)}, bf16[2,1,128,128]{3,2,1,0:T(8,128)(2,1)S(1)}, u32[]{:S(2)}, u32[]{:S(2)}) collective-permute-start(bf16[2,1,128,128]{3,2,1,0:T(8,128)(2,1)} %get-tuple-element.123), channel_id=1, source_target_pairs={{0,4},{4,8},{8,12},{12,16},{16,20},{20,24},{24,28},{28,0},{1,5},{5... | collective-permute-start | bytes 196616 | tf_op jit(solution)/shard_map/while/body/eval_jaxpr/ppermute | solution.py:9
  185.8 4.9 %collective-permute-start = (bf16[2,1,128,128]{3,2,1,0:T(8,128)(2,1)}, bf16[2,1,128,128]{3,2,1,0:T(8,128)(2,1)S(1)}, u32[]{:S(2)}, u32[]{:S(2)}) collective-permute-start(bf16[2,1,128,128]{3,2,1,0:T(8,128)(2,1)} %get-tuple-element.123), channel_id=1, source_target_pairs={{0,4},{4,8},{8,12},{12,16},{16,20},{20,24},{24,28},{28,0},{1,5},{5... | collective-permute-start | bytes 196616 | tf_op jit(solution)/shard_map/while/body/eval_jaxpr/ppermute | solution.py:9
  194.6 4.9 %collective-permute-start = (bf16[2,1,128,128]{3,2,1,0:T(8,128)(2,1)}, bf16[2,1,128,128]{3,2,1,0:T(8,128)(2,1)S(1)}, u32[]{:S(2)}, u32[]{:S(2)}) collective-permute-start(bf16[2,1,128,128]{3,2,1,0:T(8,128)(2,1)} %get-tuple-element.123), channel_id=1, source_target_pairs={{0,4},{4,8},{8,12},{12,16},{16,20},{20,24},{24,28},{28,0},{1,5},{5... | collective-permute-start | bytes 196616 | tf_op jit(solution)/shard_map/while/body/eval_jaxpr/ppermute | solution.py:9
  203.5 4.9 %collective-permute-start = (bf16[2,1,128,128]{3,2,1,0:T(8,128)(2,1)}, bf16[2,1,128,128]{3,2,1,0:T(8,128)(2,1)S(1)}, u32[]{:S(2)}, u32[]{:S(2)}) collective-permute-start(bf16[2,1,128,128]{3,2,1,0:T(8,128)(2,1)} %get-tuple-element.123), channel_id=1, source_target_pairs={{0,4},{4,8},{8,12},{12,16},{16,20},{20,24},{24,28},{28,0},{1,5},{5... | collective-permute-start | bytes 196616 | tf_op jit(solution)/shard_map/while/body/eval_jaxpr/ppermute | solution.py:9
  214.2 1.9 copy-start.10
Sparse Core Ops, SparseCore 0:
  8.9 100.7 all-gather.1
  227.9 91.1 reduce-scatter.1
where the time goes:
time: 327 us; the launch traced here: 326 us
  waiting for transfers between devices  226 us (69%)
  matrix products  54.7 us (17%)
  other arithmetic  17.7 us (5%)
  between operations  14.3 us (4%)
  local copies, waits for them, and re-layouts  12.6 us (4%)
    all_gather x1, waiting for transfers between devices, shards(): piece = lax.all_gather(hidden_in, 'tensor', axis=1, tiled=True)  100 us
    reduce_scatter x1, waiting for transfers between devices, shards(): lax.psum_scatter(jnp.dot(attended, w_out, preferred_element_type=jnp.floa...  91.3 us
    ppermute x7, waiting for transfers between devices, passed_along(): lax.ppermute(array, axis, [(i, (i + by) % peers) for i in range(peers)])  33.5 us
    dot_general x8, matrix products, absorb(): jnp.einsum('kgth,ksh->kgts', queries, keys_in, preferred_element_type=jnp...  13.6 us
    dot_general x8, matrix products, absorb(): jnp.einsum('kgts,ksh->kgth', expo.astype(jnp.bfloat16), values_in, prefer...  11.6 us
    dot_general x1, matrix products, shards(): jnp.dot(attended, w_out, preferred_element_type=jnp.float32)  11.4 us
    dot_general x1, matrix products, shards(): proj_query = jnp.dot(piece, w_query, preferred_element_type=jnp.float32)  9.81 us
  transfers between devices with their start and end apart: 9, of which 9 were waited for; matrix products, arithmetic and copies ran while one was open for 0% of the time, Pallas kernels for 0%

commit v1 on v0

v1 whole, which is shorter than its diff:
```python
import functools

import jax
import jax.numpy as jnp
from jax import lax
from jax.experimental import pallas as pl
from jax.experimental.pallas import tpu as pltpu
from jax.sharding import PartitionSpec as P

VMEM_LIMIT = 48 * 1024 * 1024
LOG2E = 1.4426950408889634


def rope_tables(rows, width):
    half_width = width // 2
    frequency = 1000000.0 ** (-(jnp.arange(half_width, dtype=jnp.float32) * 2.0 / width))
    angle = jnp.arange(rows, dtype=jnp.float32)[:, None] * frequency[None, :]
    cosine, sine = jnp.cos(angle), jnp.sin(angle)
    return (
        jnp.concatenate([cosine, cosine], axis=1),
        jnp.concatenate([-sine, sine], axis=1),
    )


def norm_rope(vectors, gain, cosine, sine):
    scale = lax.rsqrt(jnp.mean(vectors * vectors, axis=-1, keepdims=True) + 1e-06)
    vectors = vectors * scale * gain
    return vectors * cosine + pltpu.roll(vectors, vectors.shape[-1] // 2, 1) * sine


def params():
    return pltpu.CompilerParams(vmem_limit_bytes=VMEM_LIMIT)


def partial_kernel(n_hidden, with_acc, block_ref, *refs):
    hidden = refs[0][...]
    for ref in refs[1:n_hidden]:
        hidden = hidden + ref[...]
    w_ref, out_ref = refs[n_hidden], refs[-1]
    product = jnp.dot(hidden, w_ref[...], preferred_element_type=jnp.float32)
    if with_acc:
        product = product + refs[n_hidden + 1][...]
    out_ref[...] = product


def partial_projection(block, hidden, weights, acc):
    rows, features = hidden[0].shape
    width = weights.shape[1]
    tile = 256
    in_specs = [pl.BlockSpec((rows, features), lambda i, b: (0, 0)) for _ in hidden]
    in_specs.append(pl.BlockSpec((features, tile), lambda i, b: (b[0], i)))
    operands = [*hidden, weights]
    if acc is not None:
        in_specs.append(pl.BlockSpec((rows, tile), lambda i, b: (0, i)))
        operands.append(acc)
    return pl.pallas_call(
        functools.partial(partial_kernel, len(hidden), acc is not None),
        grid_spec=pltpu.PrefetchScalarGridSpec(
            num_scalar_prefetch=1,
            grid=(width // tile,),
            in_specs=in_specs,
            out_specs=pl.BlockSpec((rows, tile), lambda i, b: (0, i)),
        ),
        out_shape=jax.ShapeDtypeStruct((rows, width), jnp.float32),
        compiler_params=params(),
        cost_estimate=pl.CostEstimate(
            flops=2 * rows * features * width,
            bytes_accessed=2 * features * (rows + width) + 8 * rows * width,
            transcendentals=0,
        ),
        name="partial_projection",
    )(block, *operands)


def keys_values_kernel(
    n_hidden, head, block_ref, *refs
):
    hidden = refs[0][...]
    for ref in refs[1:n_hidden]:
        hidden = hidden + ref[...]
    w_ref, acc_ref, gain_ref, cos_ref, sin_ref, pos_ref, k_ref, v_ref, s_ref = refs[n_hidden:]
    proj = acc_ref[...] + jnp.dot(hidden, w_ref[...], preferred_element_type=jnp.float32)
    keys = norm_rope(proj[:, :head], gain_ref[...], cos_ref[...], sin_ref[...])
    keys = keys.astype(jnp.bfloat16)
    values = proj[:, head:].astype(jnp.bfloat16)
    k_ref[...] = keys
    v_ref[...] = values
    picks = pos_ref.shape[0]
    rows = keys.shape[0]
    chosen = lax.broadcasted_iota(jnp.int32, (picks, rows), 1) == pos_ref[...]
    chosen = jnp.where(chosen, 1.0, 0.0).astype(jnp.bfloat16)
    both = jnp.concatenate([keys, values], axis=1)
    picked = jnp.dot(chosen, both, preferred_element_type=jnp.float32).astype(jnp.bfloat16)
    s_ref[:picks, :] = picked[:, :head]
    s_ref[picks:, :] = picked[:, head:]


def keys_values(block, hidden, weights, acc, gain, cosine, sine, positions):
    rows, features = hidden[0].shape
    head = gain.shape[1]
    picks = positions.shape[0]
    whole = lambda *shape: pl.BlockSpec(shape, lambda i, b: (0, 0))
    return pl.pallas_call(
        functools.partial(keys_values_kernel, len(hidden), head),
        grid_spec=pltpu.PrefetchScalarGridSpec(
            num_scalar_prefetch=1,
            grid=(1,),
            in_specs=[whole(rows, features) for _ in hidden]
            + [
                pl.BlockSpec((features, 2 * head), lambda i, b: (b[0], 0)),
                whole(rows, 2 * head),
                whole(1, head),
                whole(rows, head),
                whole(rows, head),
                whole(picks, 1),
            ],
            out_specs=[whole(rows, head), whole(rows, head), whole(2 * picks, head)],
        ),
        out_shape=[
            jax.ShapeDtypeStruct((rows, head), jnp.bfloat16),
            jax.ShapeDtypeStruct((rows, head), jnp.bfloat16),
            jax.ShapeDtypeStruct((2 * picks, head), jnp.bfloat16),
        ],
        compiler_params=params(),
        cost_estimate=pl.CostEstimate(
            flops=4 * rows * features * head,
            bytes_accessed=2 * features * (rows + 2 * head) + 12 * rows * head,
            transcendentals=0,
        ),
        name="keys_values",
    )(block, *hidden, weights, acc, gain, cosine, sine, positions)


def queries_kernel(n_hidden, head, block_ref, *refs):
    hidden = refs[0][...]
    for ref in refs[1:n_hidden]:
        hidden = hidden + ref[...]
    w_ref, acc_ref, gain_ref, cos_ref, sin_ref, q_ref = refs[n_hidden:]
    proj = acc_ref[...] + jnp.dot(hidden, w_ref[...], preferred_element_type=jnp.float32)
    for start in range(0, proj.shape[1], head):
        one = norm_rope(proj[:, start : start + head], gain_ref[...], cos_ref[...], sin_ref[...])
        q_ref[:, start : start + head] = one.astype(jnp.bfloat16)


def queries_of(block, hidden, weights, acc, gain, cosine, sine):
    rows, features = hidden[0].shape
    head = gain.shape[1]
    skip = 1
    tile = 2 * head
    width = weights.shape[1] - tile
    whole = lambda *shape: pl.BlockSpec(shape, lambda i, b: (0, 0))
    return pl.pallas_call(
        functools.partial(queries_kernel, len(hidden), head),
        grid_spec=pltpu.PrefetchScalarGridSpec(
            num_scalar_prefetch=1,
            grid=(width // tile,),
            in_specs=[whole(rows, features) for _ in hidden]
            + [
                pl.BlockSpec((features, tile), lambda i, b: (b[0], i + skip)),
                pl.BlockSpec((rows, tile), lambda i, b: (0, i + skip)),
                whole(1, head),
                whole(rows, head),
                whole(rows, head),
            ],
            out_specs=pl.BlockSpec((rows, tile), lambda i, b: (0, i)),
        ),
        out_shape=jax.ShapeDtypeStruct((rows, width), jnp.bfloat16),
        compiler_params=params(),
        cost_estimate=pl.CostEstimate(
            flops=2 * rows * features * width,
            bytes_accessed=2 * features * (rows + width) + 6 * rows * width,
            transcendentals=0,
        ),
        name="queries",
    )(block, *hidden, weights, acc, gain, cosine, sine)


def attention_kernel(n_others, length_ref, q_ref, k_ref, v_ref, *refs):
    others = refs[:n_others]
    o_ref, keys_all, values_all = refs[n_others:]
    rows, head = q_ref.shape
    picks = others[0].shape[0] // 2
    cross = n_others * picks

    @pl.when(pl.program_id(0) == 0)
    def _():
        for index, ref in enumerate(others):
            keys_all[index * picks : (index + 1) * picks, :] = ref[:picks, :]
            values_all[index * picks : (index + 1) * picks, :] = ref[picks:, :]
        keys_all[cross:, :] = k_ref[...]
        values_all[cross:, :] = v_ref[...]

    scale = head ** (-0.5) * LOG2E
    tile = 256
    for start in range(0, rows, tile):
        reach = cross + start + tile
        scores = lax.dot_general(
            q_ref[start : start + tile, :],
            keys_all[:reach, :],
            (((1,), (1,)), ((), ())),
            preferred_element_type=jnp.float32,
        )
        row = lax.broadcasted_iota(jnp.int32, (tile, tile), 0)
        column = lax.broadcasted_iota(jnp.int32, (tile, tile), 1)
        own = jnp.where(column <= row, scores[:, reach - tile :], -1e30)
        free = scores[:, : reach - tile]
        largest = jnp.maximum(
            jnp.max(free, axis=1, keepdims=True), jnp.max(own, axis=1, keepdims=True)
        )
        free = jnp.exp2((free - largest) * scale)
        own = jnp.exp2((own - largest) * scale)
        total = jnp.sum(free, axis=1, keepdims=True) + jnp.sum(own, axis=1, keepdims=True)
        mixed = jnp.dot(
            free.astype(jnp.bfloat16),
            values_all[: reach - tile, :],
            preferred_element_type=jnp.float32,
        ) + jnp.dot(
            own.astype(jnp.bfloat16),
            values_all[reach - tile : reach, :],
            preferred_element_type=jnp.float32,
        )
        position = lax.broadcasted_iota(jnp.int32, (tile, head), 0) + start
        mixed = jnp.where(position < length_ref[0], mixed / total, 0.0)
        o_ref[start : start + tile, :] = mixed.astype(jnp.bfloat16)


def attention(lengths, queries, keys, values, others):
    rows, width = queries.shape
    head = keys.shape[1]
    picks = others[0].shape[0] // 2
    reach = rows + len(others) * picks
    whole = lambda *shape: pl.BlockSpec(shape, lambda i, b: (0, 0))
    one_head = pl.BlockSpec((rows, head), lambda i, b: (0, i))
    return pl.pallas_call(
        functools.partial(attention_kernel, len(others)),
        grid_spec=pltpu.PrefetchScalarGridSpec(
            num_scalar_prefetch=1,
            grid=(width // head,),
            in_specs=[one_head, whole(rows, head), whole(rows, head)]
            + [whole(2 * picks, head) for _ in others],
            out_specs=one_head,
            scratch_shapes=[
                pltpu.VMEM((reach, head), jnp.bfloat16),
                pltpu.VMEM((reach, head), jnp.bfloat16),
            ],
        ),
        out_shape=jax.ShapeDtypeStruct((rows, width), jnp.bfloat16),
        compiler_params=params(),
        cost_estimate=pl.CostEstimate(
            flops=4 * rows * width * reach,
            bytes_accessed=4 * rows * width + 4 * reach * head,
            transcendentals=rows * width // head * reach,
        ),
        name="attention",
    )(lengths, queries, keys, values, *others)


def shards(hidden_in, lengths, summary_pos, w_query, w_key, w_value, w_out, q_gain, k_gain):
    rows_here = hidden_in.shape[0]
    head_width = q_gain.shape[0]
    place = lax.axis_index("tensor")
    n_cand = lax.axis_size("cand")
    assert lax.axis_size("tensor") == 4 and w_key.shape[1] == head_width

    def swap(array):
        return lax.ppermute(array, "tensor", [(0, 1), (1, 0), (2, 3), (3, 2)])

    def across(array):
        return lax.ppermute(array, "tensor", [(1, 2), (2, 1)])

    def outward(array):
        return lax.ppermute(array, "tensor", [(1, 0), (2, 3)])

    def inward(array):
        return lax.ppermute(array, "tensor", [(0, 1), (3, 2)])

    low = place < 2
    near = jnp.bitwise_xor(place, 1)
    third = jnp.where(low, 2, 1)
    last = jnp.where(low, 3, 0)
    index = lambda block: block.astype(jnp.int32).reshape(1)

    weights = jnp.concatenate([w_key, w_value, w_query], axis=1)
    cosine, sine = rope_tables(rows_here, head_width)

    from_near = swap(hidden_in)
    from_mid = across(hidden_in)
    acc = partial_projection(index(place), [hidden_in], weights, None)
    to_outer = outward(from_mid)
    to_inner = across(from_near)
    acc = partial_projection(index(near), [from_near], weights, acc)
    end = outward(to_inner)
    acc = partial_projection(index(third), [from_mid, to_outer], weights, acc)
    final = [to_inner, end]
    keys, values, summary = keys_values(
        index(last), final, weights, acc, k_gain[None], cosine, sine, summary_pos.reshape(-1, 1)
    )
    others = [
        lax.ppermute(summary, "cand", [(i, (i + by) % n_cand) for i in range(n_cand)])
        for by in range(1, n_cand)
    ]
    queries = queries_of(index(last), final, weights, acc, q_gain[None], cosine, sine)
    attended = attention(lengths, queries, keys, values, others)

    part = rows_here // 4

    def mix(block):
        rows = lax.dynamic_slice_in_dim(attended, block * part, part, 0)
        return jnp.dot(rows, w_out, preferred_element_type=jnp.float32)

    far_sum = mix(last)
    far_sum = across((far_sum + inward(far_sum.astype(jnp.bfloat16))).astype(jnp.bfloat16))
    third_sum = mix(third)
    third_sum = across((third_sum + inward(third_sum.astype(jnp.bfloat16))).astype(jnp.bfloat16))
    near_sum = swap((mix(near) + far_sum).astype(jnp.bfloat16))
    return (mix(place) + near_sum + third_sum).astype(jnp.bfloat16)


def solution(mesh):
    return jax.shard_map(
        shards,
        mesh=mesh,
        in_specs=(
            P("cand", "tensor"),
            P("cand"),
            P("cand", None),
            P(None, "tensor"),
            P(None, "tensor"),
            P(None, "tensor"),
            P("tensor", None),
            P(),
            P(),
        ),
        out_specs=P(("cand", "tensor"), None),
        check_vma=False,
    )
```

time: 327 us -> 241 us (0.74)
  waiting for transfers between devices: 226 us -> 126 us
  Pallas kernels: 0 us -> 38.9 us
  matrix products: 54.7 us -> 24 us
  starting transfers between devices: 0.39 us -> 27.2 us
  between operations: 14.3 us -> 0.93 us
  other arithmetic: 17.7 us -> 7.27 us
  local copies, waits for them, and re-layouts: 12.6 us -> 16.3 us
    all_gather x1 -> x0, waiting for transfers between devices: 100 us -> none  [shards(): piece = lax.all_gather(hidden_in, 'tensor', axis=1, tiled=True)]
    ppermute x7 -> x17, waiting for transfers between devices: 33.5 us -> 126 us  [the longest x2 57.1 us: swap(): return lax.ppermute(array, 'tensor', [(0, 1), (1, 0), (2, 3), (3, 2)])]
    reduce_scatter x1 -> x0, waiting for transfers between devices: 91.3 us -> none  [shards(): lax.psum_scatter(jnp.dot(attended, w_out, preferred_element_type=jnp.floa...]
    pallas_call x0 -> x6, Pallas kernels: none -> 38.9 us  [the longest x3 16.4 us: partial_projection(): pl.pallas_call(functools.partial(partial_kernel, len(hidden), acc is not...]
    dot_general x20 -> x4, matrix products: 54.7 us -> 24 us  [mix(): return jnp.dot(rows, w_out, preferred_element_type=jnp.float32)]
    ppermute x7 -> x17, starting transfers between devices: 0.35 us -> 27.2 us  [the longest x2 7.78 us: swap(): return lax.ppermute(array, 'tensor', [(0, 1), (1, 0), (2, 3), (3, 2)])]
    concatenate x0 -> x1, local copies, waits for them, and re-layouts: none -> 9.3 us  [shards(): weights = jnp.concatenate([w_key, w_value, w_query], axis=1)]
    unnamed x24 -> x34, local copies, waits for them, and re-layouts: 0.06 us -> 6.85 us
  transfers between devices with their start and end apart: 9 -> 17, of which waited for: 9 -> 6; matrix products, arithmetic and copies ran while one was open for 0% -> 14% of each run, Pallas kernels for 0% -> 10%
where the time goes in v1:
time: 241 us; the launch traced here: 240 us
  waiting for transfers between devices  126 us (52%)
  Pallas kernels  38.9 us (16%)
  starting transfers between devices  27.2 us (11%)
  matrix products  24 us (10%)
  local copies, waits for them, and re-layouts  16.3 us (7%)
  other arithmetic  7.27 us (3%)
    ppermute x2, waiting for transfers between devices, swap(): return lax.ppermute(array, 'tensor', [(0, 1), (1, 0), (2, 3), (3, 2)])  57.1 us
    ppermute x2, waiting for transfers between devices, inward(): return lax.ppermute(array, 'tensor', [(0, 1), (3, 2)])  40.7 us
    ppermute x2, waiting for transfers between devices, outward(): return lax.ppermute(array, 'tensor', [(1, 0), (2, 3)])  27.9 us
    dot_general x4, matrix products, mix(): return jnp.dot(rows, w_out, preferred_element_type=jnp.float32)  24 us
    pallas_call x3, Pallas kernels, partial_projection(): pl.pallas_call(functools.partial(partial_kernel, len(hidden), acc is not...  16.4 us
    pallas_call x1, Pallas kernels, attention(): pl.pallas_call(functools.partial(attention_kernel, len(others)), grid_spe...  11.9 us
    concatenate x1, local copies, waits for them, and re-layouts, shards(): weights = jnp.concatenate([w_key, w_value, w_query], axis=1)  9.3 us
    ppermute x2, starting transfers between devices, swap(): return lax.ppermute(array, 'tensor', [(0, 1), (1, 0), (2, 3), (3, 2)])  7.78 us
  transfers between devices with their start and end apart: 17, of which 6 were waited for; matrix products, arithmetic and copies ran while one was open for 14% of the time, Pallas kernels for 10%

profile of v1, /device:TPU:0, one launch (start us, length us, event | category | flops | bytes accessed | tf_op | source)
XLA Modules:
  0.0 240.3 jit_solution(12404881891199665511)
XLA Ops:
  0.0 3.0 %collective-permute-start = (bf16[512,1280]{1,0:T(8,128)(2,1)}, bf16[512,1280]{1,0:T(8,128)(2,1)S(1)}, u32[]{:S(2)}, u32[]{:S(2)}) collective-permute-start(bf16[512,1280]{1,0:T(8,128)(2,1)} %refs_0_.1), channel_id=1, source_target_pairs={{0,1},{1,0},{2,3},{3,2},{4,5},{5,4},{6,7},{7,6},{8,9},{9,8},{10,11... | collective-permute-start | bytes 3932168 | tf_op jit(solution)/shard_map/ppermute | solution.py:266
  3.0 0.7 collective-permute-start.3
  3.8 28.2 %collective-permute-done.refs_0_ = bf16[512,1280]{1,0:T(8,128)(2,1)S(1)} collective-permute-done((bf16[512,1280]{1,0:T(8,128)(2,1)}, bf16[512,1280]{1,0:T(8,128)(2,1)S(1)}, u32[]{:S(2)}, u32[]{:S(2)}) %collective-permute-start) | collective-permute-done | bytes 1310752 | tf_op jit(solution)/shard_map/ppermute | solution.py:266
  32.0 1.7 collective-permute-start.1
  33.7 2.5 %constant_dynamic-update-slice_fusion.2 = bf16[5120,1280]{1,0:T(8,128)(2,1)} fusion(bf16[5120,128]{1,0:T(8,128)(2,1)} %param.13), kind=kLoop, calls=%fused_computation.21 | loop fusion | bytes 2621440
  36.3 0.0 copy-done.11
  36.3 1.3 constant_dynamic-update-slice_fusion.1
  37.6 0.0 collective-permute-done.3.refs_0_
  37.6 1.3 collective-permute-start.4
  38.9 1.0 fusion.11
  39.9 0.0 collective-permute-done.1.refs_0_
  39.9 1.3 collective-permute-start.2
  41.2 0.2 pad_maximum_fusion
  41.4 0.1 copy.10.refs_7_
  41.5 0.0 copy-start.3
  41.5 9.3 %constant_dynamic-update-slice_fusion.refs_1_.refs_2_ = bf16[5120,1280]{1,0:T(8,128)(2,1)} fusion(bf16[5120,1280]{1,0:T(8,128)(2,1)} %constant_dynamic-update-slice_fusion.1, bf16[5120,1024]{1,0:T(8,128)(2,1)} %param.12), kind=kLoop, calls=%fused_computation.19 | loop fusion | bytes 20971520 | tf_op jit(solution)/shard_map/concatenate | solution.py:283
  50.8 0.0 copy-done.3
  50.8 5.0 %partial_projection.3.refs_2_ = f32[512,1280]{1,0:T(8,128)S(1)} custom-call(s32[1]{0:T(128)} %bitcast.3.block_ref, bf16[512,1280]{1,0:T(8,128)(2,1)S(1)} %copy-done.3, bf16[5120,1280]{1,0:T(8,128)(2,1)} %constant_dynamic-update-slice_fusion.refs_1_.refs_2_), custom_call_target="tpu_custom_call" | custom-call | flops 1677721600 | bytes 9830400 | tf_op jit(solution)/shard_map/partial_projection/pallas_call | solution.py:56
  55.9 0.0 copy-start.2
  55.9 1.5 copy-done.2
  57.3 0.0 copy-done.7
  57.3 5.5 %partial_projection.4.refs_3_ = f32[512,1280]{1,0:T(8,128)S(1)} custom-call(s32[1]{0:T(128)} %bitcast.2.block_ref, bf16[512,1280]{1,0:T(8,128)(2,1)S(1)} %copy-done.7, bf16[5120,1280]{1,0:T(8,128)(2,1)} %constant_dynamic-update-slice_fusion.refs_1_.refs_2_, f32[512,1280]{1,0:T(8,128)} %copy-done.2), custom_call_target="tpu_custom_call" | custom-call | flops 1677721600 | bytes 9830400 | tf_op jit(solution)/shard_map/partial_projection/pallas_call | solution.py:56
  62.9 0.0 copy-start.1
  62.9 1.5 copy-done.1
  64.4 7.8 %collective-permute-done.4.refs_1_ = bf16[512,1280]{1,0:T(8,128)(2,1)} collective-permute-done((bf16[512,1280]{1,0:T(8,128)(2,1)S(1)}, bf16[512,1280]{1,0:T(8,128)(2,1)}, u32[]{:S(2)}, u32[]{:S(2)}) %collective-permute-start.4) | collective-permute-done | bytes 1310752 | tf_op jit(solution)/shard_map/ppermute | solution.py:272
  72.2 5.9 %partial_projection.5.refs_3_ = f32[512,1280]{1,0:T(8,128)S(1)} custom-call(s32[1]{0:T(128)} %bitcast.1.block_ref, bf16[512,1280]{1,0:T(8,128)(2,1)S(1)} %copy-done.5, bf16[512,1280]{1,0:T(8,128)(2,1)} %collective-permute-done.4.refs_1_, bf16[5120,1280]{1,0:T(8,128)(2,1)} %constant_dynamic-update-slice_fusion.refs_1_.refs_2_, f32[512,1280]{1,0:T(8,128)} %copy-done.1), custom_call_target="tpu_custom_call" | custom-call | flops 1677721600 | bytes 9830400 | tf_op jit(solution)/shard_map/partial_projection/pallas_call | solution.py:56
  78.1 20.1 %collective-permute-done.2.refs_1_ = bf16[512,1280]{1,0:T(8,128)(2,1)} collective-permute-done((bf16[512,1280]{1,0:T(8,128)(2,1)}, bf16[512,1280]{1,0:T(8,128)(2,1)}, u32[]{:S(2)}, u32[]{:S(2)}) %collective-permute-start.2) | collective-permute-done | bytes 1310752 | tf_op jit(solution)/shard_map/ppermute | solution.py:272
  98.2 0.0 copy-done.8
  98.2 3.0 %keys_values.1 = (bf16[512,128]{1,0:T(8,128)(2,1)S(1)}, bf16[512,128]{1,0:T(8,128)(2,1)S(1)}, bf16[256,128]{1,0:T(8,128)(2,1)S(1)}) custom-call(s32[1]{0:T(128)} %bitcast.block_ref, bf16[512,1280]{1,0:T(8,128)(2,1)} %collective-permute-done.1.refs_0_, bf16[512,1280]{1,0:T(8,128)(2,1)} %collective-permute-done.2.refs_1_, ...), custom_call_target="tpu_custom_call" | custom-call | flops 335544320 | bytes 2752512 | tf_op jit(solution)/shard_map/keys_values/pallas_call | solution.py:103
  101.2 2.5 %collective-permute-start.10 = (bf16[256,128]{1,0:T(8,128)(2,1)S(1)}, bf16[256,128]{1,0:T(8,128)(2,1)S(1)}, u32[]{:S(2)}, u32[]{:S(2)}) collective-permute-start(bf16[256,128]{1,0:T(8,128)(2,1)S(1)} %get-tuple-element.10), channel_id=1, source_target_pairs={{0,24},{4,28},{8,0},{12,4},{16,8},{20,12},{24,16},{28,20},{1,25},{... | collective-permute-start | bytes 196616 | tf_op jit(solution)/shard_map/ppermute | solution.py:299
  103.7 0.0 collective-permute-start.11
  104.3 0.6 collective-permute-start.5
  104.9 0.0 collective-permute-start.6
  104.9 1.5 collective-permute-start.7
  106.4 0.0 collective-permute-done.10.refs_5_
  106.4 1.4 collective-permute-start.8
  107.8 0.0 collective-permute-done.11.refs_6_
  107.8 0.0 collective-permute-start.9
  107.8 0.0 slice-start
  107.8 0.0 slice-start.1
  107.8 7.5 %queries.1.q_ref = bf16[512,1024]{1,0:T(8,128)(2,1)S(1)} custom-call(s32[1]{0:T(128)} %bitcast.block_ref, bf16[512,1280]{1,0:T(8,128)(2,1)} %collective-permute-done.1.refs_0_, bf16[512,1280]{1,0:T(8,128)(2,1)} %collective-permute-done.2.refs_1_, bf16[5120,1280]{1,0:T(8,128)(2,1)} %constant_dynamic-update-slice_fusion.refs_1_.refs_2_, f32[512,1280]{1,0:T(8,128)} %copy-done, ...), custom_call_target="tpu_custom_call" | custom-call | flops 1342177280 | bytes 7077888 | tf_op jit(solution)/shard_map/queries/pallas_call | solution.py:152
  115.4 0.0 collective-permute-done.5.refs_0_
  115.4 0.0 collective-permute-done.6.refs_1_
  115.4 0.0 collective-permute-done.7.refs_2_
  115.4 0.0 collective-permute-done.8.refs_3_
  115.4 0.0 collective-permute-done.9.refs_4_
  115.4 0.0 slice-start.2
  115.4 11.9 %attention.1 = bf16[512,1024]{1,0:T(8,128)(2,1)S(1)} custom-call(s32[1]{0:T(128)S(6)} %copy.13.length_ref, bf16[512,1024]{1,0:T(8,128)(2,1)S(1)} %queries.1.q_ref, bf16[512,128]{1,0:T(8,128)(2,1)S(1)} %get-tuple-element.8.k_ref, bf16[512,128]{1,0:T(8,128)(2,1)S(1)} %get-tuple-element.9.v_ref, bf16[256,128]{1,0:T(8,128)(2,1)S(1)} %collective-permute-done.5.refs_0_, ...), custom_call_target="tpu_custom_call" | custom-call | flops 2952790016 | bytes 2818048 | tf_op jit(solution)/shard_map/attention/pallas_call | solution.py:234
  127.4 3.5 %fusion.17 = (bf16[128,5120]{1,0:T(8,128)(2,1)}, f32[128,5120]{1,0:T(8,128)}) fusion(bf16[1024,5120]{1,0:T(8,128)(2,1)S(1)} %bitcast.14, bf16[512,1024]{1,0:T(8,128)(2,1)S(1)} %attention.1, s32[]{:T(128)S(6)} %select_n.23), kind=kOutput, calls=%fused_computation.28 | convolution fusion | flops 1342832640 | bytes 14680068 | tf_op jit(solution)/shard_map/dot_general | solution.py:309
  130.9 2.6 %collective-permute-start.12 = (bf16[128,5120]{1,0:T(8,128)(2,1)}, bf16[128,5120]{1,0:T(8,128)(2,1)}, u32[]{:S(2)}, u32[]{:S(2)}) collective-permute-start(bf16[128,5120]{1,0:T(8,128)(2,1)} %get-tuple-element.16), channel_id=1, source_target_pairs={{0,1},{3,2},{4,5},{7,6},{8,9},{11,10},{12,13},{15,14},{16,17},{19,... | collective-permute-start | bytes 3932168 | tf_op jit(solution)/shard_map/ppermute | solution.py:275
  133.5 7.2 %fusion.16 = (bf16[128,5120]{1,0:T(8,128)(2,1)S(1)}, f32[128,5120]{1,0:T(8,128)}) fusion(bf16[1024,5120]{1,0:T(8,128)(2,1)} %param.15, bf16[512,1024]{1,0:T(8,128)(2,1)S(1)} %attention.1, s32[]{:T(128)S(6)} %select_n.24), kind=kOutput, calls=%fused_computation.27 | convolution fusion | flops 1342832640 | bytes 14680068 | tf_op jit(solution)/shard_map/dot_general | solution.py:309
  140.6 2.4 collective-permute-start.15
  143.0 17.1 %collective-permute-done.12 = bf16[128,5120]{1,0:T(8,128)(2,1)} collective-permute-done((bf16[128,5120]{1,0:T(8,128)(2,1)}, bf16[128,5120]{1,0:T(8,128)(2,1)}, u32[]{:S(2)}, u32[]{:S(2)}) %collective-permute-start.12) | collective-permute-done | bytes 1310752 | tf_op jit(solution)/shard_map/ppermute | solution.py:275
  160.1 2.6 %add_convert_fusion.1 = bf16[128,5120]{1,0:T(8,128)(2,1)} fusion(f32[128,5120]{1,0:T(8,128)S(1)} %copy-done.10, bf16[128,5120]{1,0:T(8,128)(2,1)} %collective-permute-done.12), kind=kLoop, calls=%fused_computation.6 | loop fusion | flops 1966080 | bytes 5242880 | tf_op jit(solution)/shard_map/convert_element_type | solution.py:312
  162.8 1.7 collective-permute-start.13
  164.5 23.6 %collective-permute-done.15 = bf16[128,5120]{1,0:T(8,128)(2,1)} collective-permute-done((bf16[128,5120]{1,0:T(8,128)(2,1)S(1)}, bf16[128,5120]{1,0:T(8,128)(2,1)}, u32[]{:S(2)}, u32[]{:S(2)}) %collective-permute-start.15) | collective-permute-done | bytes 1310752 | tf_op jit(solution)/shard_map/ppermute | solution.py:275
  188.1 3.4 %add_convert_fusion = bf16[128,5120]{1,0:T(8,128)(2,1)} fusion(f32[128,5120]{1,0:T(8,128)} %get-tuple-element.15, bf16[128,5120]{1,0:T(8,128)(2,1)} %collective-permute-done.15), kind=kLoop, calls=%fused_computation.5 | loop fusion | flops 1966080 | bytes 5242880 | tf_op jit(solution)/shard_map/convert_element_type | solution.py:314
  191.5 1.7 collective-permute-start.16
  193.3 0.0 collective-permute-done.13
  193.3 5.8 %fusion.2 = bf16[128,5120]{1,0:T(8,128)(2,1)S(1)} fusion(bf16[1024,5120]{1,0:T(8,128)(2,1)} %param.15, bf16[128,5120]{1,0:T(8,128)(2,1)} %collective-permute-done.13, bf16[512,1024]{1,0:T(8,128)(2,1)S(1)} %attention.1, s32[]{:T(128)S(6)} %select_n.22), kind=kOutput, calls=%fused_computation.4 | convolution fusion | flops 1344143360 | bytes 13369348 | tf_op jit(solution)/shard_map/dot_general | solution.py:309
  199.1 4.8 %collective-permute-start.14 = (bf16[128,5120]{1,0:T(8,128)(2,1)S(1)}, bf16[128,5120]{1,0:T(8,128)(2,1)}, u32[]{:S(2)}, u32[]{:S(2)}) collective-permute-start(bf16[128,5120]{1,0:T(8,128)(2,1)S(1)} %fusion.2), channel_id=1, source_target_pairs={{0,1},{1,0},{2,3},{3,2},{4,5},{5,4},{6,7},{7,6},{8,9},{9,8},{10,11... | collective-permute-start | bytes 3932168 | tf_op jit(solution)/shard_map/ppermute | solution.py:266
  203.9 0.0 collective-permute-done.16
  203.9 28.8 %collective-permute-done.14 = bf16[128,5120]{1,0:T(8,128)(2,1)} collective-permute-done((bf16[128,5120]{1,0:T(8,128)(2,1)S(1)}, bf16[128,5120]{1,0:T(8,128)(2,1)}, u32[]{:S(2)}, u32[]{:S(2)}) %collective-permute-start.14) | collective-permute-done | bytes 1310752 | tf_op jit(solution)/shard_map/ppermute | solution.py:266
  232.7 7.6 %fusion.1 = bf16[128,5120]{1,0:T(8,128)(2,1)} fusion(bf16[1024,5120]{1,0:T(8,128)(2,1)} %param.15, bf16[128,5120]{1,0:T(8,128)(2,1)} %collective-permute-done.16, bf16[128,5120]{1,0:T(8,128)(2,1)} %collective-permute-done.14, bf16[512,1024]{1,0:T(8,128)(2,1)S(1)} %attention.1, s32[]{:T(128)S(6)} %select_n.21), kind=kOutput, calls=%fused_computation.3 | convolution fusion | flops 1345454080 | bytes 14680068 | tf_op jit(solution)/shard_map/dot_general | solution.py:309
  (22 shorter events, 0.0 us)
Async XLA Ops:
  0.0 36.3 %copy-start.11 = (bf16[5120,128]{1,0:T(8,128)(2,1)S(1)}, bf16[5120,128]{1,0:T(8,128)(2,1)}, u32[]{:S(2)}) copy-start(bf16[5120,128]{1,0:T(8,128)(2,1)} %param.14) | copy-start | bytes 3932164
  0.0 32.0 %collective-permute-start = (bf16[512,1280]{1,0:T(8,128)(2,1)}, bf16[512,1280]{1,0:T(8,128)(2,1)S(1)}, u32[]{:S(2)}, u32[]{:S(2)}) collective-permute-start(bf16[512,1280]{1,0:T(8,128)(2,1)} %refs_0_.1), channel_id=1, source_target_pairs={{0,1},{1,0},{2,3},{3,2},{4,5},{5,4},{6,7},{7,6},{8,9},{9,8},{10,11... | collective-permute-start | bytes 3932168 | tf_op jit(solution)/shard_map/ppermute | solution.py:266
  3.0 34.6 %collective-permute-start.3 = (bf16[512,1280]{1,0:T(8,128)(2,1)}, bf16[512,1280]{1,0:T(8,128)(2,1)S(1)}, u32[]{:S(2)}, u32[]{:S(2)}) collective-permute-start(bf16[512,1280]{1,0:T(8,128)(2,1)} %refs_0_.1), channel_id=1, source_target_pairs={{1,2},{2,1},{5,6},{6,5},{9,10},{10,9},{13,14},{14,13},{17,18},{18,... | collective-permute-start | bytes 3932168 | tf_op jit(solution)/shard_map/ppermute | solution.py:269
  32.0 5.6 %copy-start.6 = (bf16[512,1280]{1,0:T(8,128)(2,1)}, bf16[512,1280]{1,0:T(8,128)(2,1)S(1)}, u32[]{:S(2)}) copy-start(bf16[512,1280]{1,0:T(8,128)(2,1)S(1)} %collective-permute-done.refs_0_) | copy-start | bytes 3932164
  32.0 7.9 %collective-permute-start.1 = (bf16[512,1280]{1,0:T(8,128)(2,1)S(1)}, bf16[512,1280]{1,0:T(8,128)(2,1)}, u32[]{:S(2)}, u32[]{:S(2)}) collective-permute-start(bf16[512,1280]{1,0:T(8,128)(2,1)S(1)} %collective-permute-done.refs_0_), channel_id=1, source_target_pairs={{1,2},{2,1},{5,6},{6,5},{9,10},{10,9},{13,14},{14,13},{17,18},{18,... | collective-permute-start | bytes 3932168 | tf_op jit(solution)/shard_map/ppermute | solution.py:269
  36.3 5.1 %copy-start.12 = (s32[1,128]{1,0:T(1,128)S(1)}, s32[1,128]{1,0:T(1,128)}, u32[]{:S(2)}) copy-start(s32[1,128]{1,0:T(1,128)} %param.11) | copy-start | bytes 1540
  37.6 13.3 %copy-start.4 = (bf16[512,1280]{1,0:T(8,128)(2,1)}, bf16[512,1280]{1,0:T(8,128)(2,1)S(1)}, u32[]{:S(2)}) copy-start(bf16[512,1280]{1,0:T(8,128)(2,1)S(1)} %collective-permute-done.3.refs_0_) | copy-start | bytes 3932164
  37.6 34.6 %collective-permute-start.4 = (bf16[512,1280]{1,0:T(8,128)(2,1)S(1)}, bf16[512,1280]{1,0:T(8,128)(2,1)}, u32[]{:S(2)}, u32[]{:S(2)}) collective-permute-start(bf16[512,1280]{1,0:T(8,128)(2,1)S(1)} %collective-permute-done.3.refs_0_), channel_id=1, source_target_pairs={{1,0},{2,3},{5,4},{6,7},{9,8},{10,11},{13,12},{14,15},{17,16},{18,... | collective-permute-start | bytes 3932168 | tf_op jit(solution)/shard_map/ppermute | solution.py:272
  39.9 58.3 %collective-permute-start.2 = (bf16[512,1280]{1,0:T(8,128)(2,1)}, bf16[512,1280]{1,0:T(8,128)(2,1)}, u32[]{:S(2)}, u32[]{:S(2)}) collective-permute-start(bf16[512,1280]{1,0:T(8,128)(2,1)} %collective-permute-done.1.refs_0_), channel_id=1, source_target_pairs={{1,0},{2,3},{5,4},{6,7},{9,8},{10,11},{13,12},{14,15},{17,16},{18,... | collective-permute-start | bytes 3932168 | tf_op jit(solution)/shard_map/ppermute | solution.py:272
  41.5 9.3 %copy-start.3 = (bf16[512,1280]{1,0:T(8,128)(2,1)S(1)}, bf16[512,1280]{1,0:T(8,128)(2,1)}, u32[]{:S(2)}) copy-start(bf16[512,1280]{1,0:T(8,128)(2,1)} %refs_0_.1) | copy-start | bytes 3932164
  50.8 6.5 %copy-start.7 = (bf16[512,1280]{1,0:T(8,128)(2,1)S(1)}, bf16[512,1280]{1,0:T(8,128)(2,1)}, u32[]{:S(2)}) copy-start(bf16[512,1280]{1,0:T(8,128)(2,1)} %copy-done.6) | copy-start | bytes 3932164
  55.9 1.5 copy-start.2
  57.3 14.8 %copy-start.5 = (bf16[512,1280]{1,0:T(8,128)(2,1)S(1)}, bf16[512,1280]{1,0:T(8,128)(2,1)}, u32[]{:S(2)}) copy-start(bf16[512,1280]{1,0:T(8,128)(2,1)} %copy-done.4) | copy-start | bytes 3932164
  62.9 1.5 copy-start.1
  72.2 26.0 %copy-start.8 = (f32[128]{0:T(128)S(1)}, f32[128]{0:T(128)}, u32[]{:S(2)}) copy-start(f32[128]{0:T(128)} %param.17) | copy-start | bytes 1540
  78.1 23.1 %copy-start = (f32[512,1280]{1,0:T(8,128)}, f32[512,1280]{1,0:T(8,128)S(1)}, u32[]{:S(2)}) copy-start(f32[512,1280]{1,0:T(8,128)S(1)} %partial_projection.5.refs_3_) | copy-start | bytes 7864324
  98.2 9.6 %copy-start.9 = (f32[128]{0:T(128)S(1)}, f32[128]{0:T(128)}, u32[]{:S(2)}) copy-start(f32[128]{0:T(128)} %param.16) | copy-start | bytes 1540
  101.2 5.2 %collective-permute-start.10 = (bf16[256,128]{1,0:T(8,128)(2,1)S(1)}, bf16[256,128]{1,0:T(8,128)(2,1)S(1)}, u32[]{:S(2)}, u32[]{:S(2)}) collective-permute-start(bf16[256,128]{1,0:T(8,128)(2,1)S(1)} %get-tuple-element.10), channel_id=1, source_target_pairs={{0,24},{4,28},{8,0},{12,4},{16,8},{20,12},{24,16},{28,20},{1,25},{... | collective-permute-start | bytes 196616 | tf_op jit(solution)/shard_map/ppermute | solution.py:299
  103.7 4.1 %collective-permute-start.11 = (bf16[256,128]{1,0:T(8,128)(2,1)S(1)}, bf16[256,128]{1,0:T(8,128)(2,1)S(1)}, u32[]{:S(2)}, u32[]{:S(2)}) collective-permute-start(bf16[256,128]{1,0:T(8,128)(2,1)S(1)} %get-tuple-element.10), channel_id=1, source_target_pairs={{0,28},{4,0},{8,4},{12,8},{16,12},{20,16},{24,20},{28,24},{1,29},{... | collective-permute-start | bytes 196616 | tf_op jit(solution)/shard_map/ppermute | solution.py:299
  104.3 11.0 %collective-permute-start.5 = (bf16[256,128]{1,0:T(8,128)(2,1)S(1)}, bf16[256,128]{1,0:T(8,128)(2,1)S(1)}, u32[]{:S(2)}, u32[]{:S(2)}) collective-permute-start(bf16[256,128]{1,0:T(8,128)(2,1)S(1)} %get-tuple-element.10), channel_id=1, source_target_pairs={{0,4},{4,8},{8,12},{12,16},{16,20},{20,24},{24,28},{28,0},{1,5},{5... | collective-permute-start | bytes 196616 | tf_op jit(solution)/shard_map/ppermute | solution.py:299
  104.9 10.5 %collective-permute-start.6 = (bf16[256,128]{1,0:T(8,128)(2,1)S(1)}, bf16[256,128]{1,0:T(8,128)(2,1)S(1)}, u32[]{:S(2)}, u32[]{:S(2)}) collective-permute-start(bf16[256,128]{1,0:T(8,128)(2,1)S(1)} %get-tuple-element.10), channel_id=1, source_target_pairs={{0,8},{4,12},{8,16},{12,20},{16,24},{20,28},{24,0},{28,4},{1,9},{5... | collective-permute-start | bytes 196616 | tf_op jit(solution)/shard_map/ppermute | solution.py:299
  104.9 10.5 %collective-permute-start.7 = (bf16[256,128]{1,0:T(8,128)(2,1)S(1)}, bf16[256,128]{1,0:T(8,128)(2,1)S(1)}, u32[]{:S(2)}, u32[]{:S(2)}) collective-permute-start(bf16[256,128]{1,0:T(8,128)(2,1)S(1)} %get-tuple-element.10), channel_id=1, source_target_pairs={{0,12},{4,16},{8,20},{12,24},{16,28},{20,0},{24,4},{28,8},{1,13},{... | collective-permute-start | bytes 196616 | tf_op jit(solution)/shard_map/ppermute | solution.py:299
  106.4 9.0 %collective-permute-start.8 = (bf16[256,128]{1,0:T(8,128)(2,1)S(1)}, bf16[256,128]{1,0:T(8,128)(2,1)S(1)}, u32[]{:S(2)}, u32[]{:S(2)}) collective-permute-start(bf16[256,128]{1,0:T(8,128)(2,1)S(1)} %get-tuple-element.10), channel_id=1, source_target_pairs={{0,16},{4,20},{8,24},{12,28},{16,0},{20,4},{24,8},{28,12},{1,17},{... | collective-permute-start | bytes 196616 | tf_op jit(solution)/shard_map/ppermute | solution.py:299
  107.8 7.6 %collective-permute-start.9 = (bf16[256,128]{1,0:T(8,128)(2,1)S(1)}, bf16[256,128]{1,0:T(8,128)(2,1)S(1)}, u32[]{:S(2)}, u32[]{:S(2)}) collective-permute-start(bf16[256,128]{1,0:T(8,128)(2,1)S(1)} %get-tuple-element.10), channel_id=1, source_target_pairs={{0,20},{4,24},{8,28},{12,0},{16,4},{20,8},{24,12},{28,16},{1,21},{... | collective-permute-start | bytes 196616 | tf_op jit(solution)/shard_map/ppermute | solution.py:299
  107.8 19.6 %slice-start = ((s8[10485760]{0:T(1024)(128)(4,1)}), s8[4194304]{0:T(1024)(128)(4,1)S(1)}, s32[]{:S(2)}) async-start(s8[10485760]{0:T(1024)(128)(4,1)} %bitcast.13), calls=%async_computation | async-start | bytes 8388608
  107.8 19.6 %slice-start.1 = ((s8[10485760]{0:T(1024)(128)(4,1)}), s8[2097152]{0:T(1024)(128)(4,1)S(1)}, s32[]{:S(2)}) async-start(s8[10485760]{0:T(1024)(128)(4,1)} %bitcast.13), calls=%async_computation.1 | async-start | bytes 4194304
  115.4 12.0 %slice-start.2 = ((s8[10485760]{0:T(1024)(128)(4,1)}), s8[4194304]{0:T(1024)(128)(4,1)S(1)}, s32[]{:S(2)}) async-start(s8[10485760]{0:T(1024)(128)(4,1)} %bitcast.13), calls=%async_computation.2 | async-start | bytes 8388608
  130.9 29.2 %collective-permute-start.12 = (bf16[128,5120]{1,0:T(8,128)(2,1)}, bf16[128,5120]{1,0:T(8,128)(2,1)}, u32[]{:S(2)}, u32[]{:S(2)}) collective-permute-start(bf16[128,5120]{1,0:T(8,128)(2,1)} %get-tuple-element.16), channel_id=1, source_target_pairs={{0,1},{3,2},{4,5},{7,6},{8,9},{11,10},{12,13},{15,14},{16,17},{19,... | collective-permute-start | bytes 3932168 | tf_op jit(solution)/shard_map/ppermute | solution.py:275
  133.5 26.7 %copy-start.10 = (f32[128,5120]{1,0:T(8,128)S(1)}, f32[128,5120]{1,0:T(8,128)}, u32[]{:S(2)}) copy-start(f32[128,5120]{1,0:T(8,128)} %get-tuple-element.17) | copy-start | bytes 7864324
  140.6 47.5 %collective-permute-start.15 = (bf16[128,5120]{1,0:T(8,128)(2,1)S(1)}, bf16[128,5120]{1,0:T(8,128)(2,1)}, u32[]{:S(2)}, u32[]{:S(2)}) collective-permute-start(bf16[128,5120]{1,0:T(8,128)(2,1)S(1)} %get-tuple-element.14), channel_id=1, source_target_pairs={{0,1},{3,2},{4,5},{7,6},{8,9},{11,10},{12,13},{15,14},{16,17},{19,... | collective-permute-start | bytes 3932168 | tf_op jit(solution)/shard_map/ppermute | solution.py:275
  162.8 30.5 %collective-permute-start.13 = (bf16[128,5120]{1,0:T(8,128)(2,1)}, bf16[128,5120]{1,0:T(8,128)(2,1)}, u32[]{:S(2)}, u32[]{:S(2)}) collective-permute-start(bf16[128,5120]{1,0:T(8,128)(2,1)} %add_convert_fusion.1), channel_id=1, source_target_pairs={{1,2},{2,1},{5,6},{6,5},{9,10},{10,9},{13,14},{14,13},{17,18},{18,... | collective-permute-start | bytes 3932168 | tf_op jit(solution)/shard_map/ppermute | solution.py:269
  191.5 12.3 %collective-permute-start.16 = (bf16[128,5120]{1,0:T(8,128)(2,1)}, bf16[128,5120]{1,0:T(8,128)(2,1)}, u32[]{:S(2)}, u32[]{:S(2)}) collective-permute-start(bf16[128,5120]{1,0:T(8,128)(2,1)} %add_convert_fusion), channel_id=1, source_target_pairs={{1,2},{2,1},{5,6},{6,5},{9,10},{10,9},{13,14},{14,13},{17,18},{18,... | collective-permute-start | bytes 3932168 | tf_op jit(solution)/shard_map/ppermute | solution.py:269
  199.1 33.6 %collective-permute-start.14 = (bf16[128,5120]{1,0:T(8,128)(2,1)S(1)}, bf16[128,5120]{1,0:T(8,128)(2,1)}, u32[]{:S(2)}, u32[]{:S(2)}) collective-permute-start(bf16[128,5120]{1,0:T(8,128)(2,1)S(1)} %fusion.2), channel_id=1, source_target_pairs={{0,1},{1,0},{2,3},{3,2},{4,5},{5,4},{6,7},{7,6},{8,9},{9,8},{10,11... | collective-permute-start | bytes 3932168 | tf_op jit(solution)/shard_map/ppermute | solution.py:266

commit v2 on v1

v2 whole, which is shorter than its diff:
```python
import functools

import jax
import jax.numpy as jnp
from jax import lax
from jax.experimental import pallas as pl
from jax.experimental.pallas import tpu as pltpu
from jax.sharding import PartitionSpec as P

VMEM_LIMIT = 48 * 1024 * 1024
LOG2E = 1.4426950408889634
OFFSETS = (0, 6, 2, 4, 1, 7, 3, 5)


def rope_tables(rows, width):
    half_width = width // 2
    frequency = 1000000.0 ** (-(jnp.arange(half_width, dtype=jnp.float32) * 2.0 / width))
    angle = jnp.arange(rows, dtype=jnp.float32)[:, None] * frequency[None, :]
    cosine, sine = jnp.cos(angle), jnp.sin(angle)
    return (
        jnp.concatenate([cosine, cosine], axis=1),
        jnp.concatenate([-sine, sine], axis=1),
    )


def norm_rope(vectors, gain, cosine, sine):
    scale = lax.rsqrt(jnp.mean(vectors * vectors, axis=-1, keepdims=True) + 1e-06)
    vectors = vectors * scale * gain
    return vectors * cosine + pltpu.roll(vectors, vectors.shape[-1] // 2, 1) * sine


def params():
    return pltpu.CompilerParams(vmem_limit_bytes=VMEM_LIMIT)


def after(array, cue):
    return lax.optimization_barrier((array, cue))[0]


def whole(*shape):
    return pl.BlockSpec(shape, lambda *_: (0,) * len(shape))


def summed(refs):
    total = refs[0][...]
    for ref in refs[1:]:
        total = total + ref[...]
    return total


def partial_kernel(counts, with_acc, block_ref, *refs):
    rows = []
    for count in counts:
        rows.append(summed(refs[:count]))
        refs = refs[count:]
    w_ref, out_ref = refs[0], refs[-1]
    start = 0
    for hidden in rows:
        stop = start + hidden.shape[0]
        product = jnp.dot(hidden, w_ref[...], preferred_element_type=jnp.float32)
        if with_acc:
            product = product + refs[1][start:stop, :]
        out_ref[start:stop, :] = product
        start = stop


def partial_projection(block, parts, weights, acc, tile):
    features = parts[0][0].shape[1]
    rows = sum(part[0].shape[0] for part in parts)
    width = weights.shape[1]
    arrivals = [array for part in parts for array in part]
    in_specs = [whole(*array.shape) for array in arrivals]
    in_specs.append(pl.BlockSpec((features, tile), lambda i, b: (b[0], i)))
    operands = [*arrivals, weights]
    if acc is not None:
        in_specs.append(pl.BlockSpec((rows, tile), lambda i, b: (0, i)))
        operands.append(acc)
    return pl.pallas_call(
        functools.partial(partial_kernel, [len(part) for part in parts], acc is not None),
        grid_spec=pltpu.PrefetchScalarGridSpec(
            num_scalar_prefetch=1,
            grid=(width // tile,),
            in_specs=in_specs,
            out_specs=pl.BlockSpec((rows, tile), lambda i, b: (0, i)),
        ),
        out_shape=jax.ShapeDtypeStruct((rows, width), jnp.float32),
        compiler_params=params(),
        name="partial_projection",
    )(block, *operands)


def keys_values_kernel(count, head, block_ref, *refs):
    hidden = summed(refs[:count])
    w_ref, acc_ref, gain_ref, cos_ref, sin_ref, out_ref = refs[count:]
    proj = acc_ref[...] + jnp.dot(hidden, w_ref[...], preferred_element_type=jnp.float32)
    keys = norm_rope(proj[:, :head], gain_ref[...], cos_ref[...], sin_ref[...])
    out_ref[:, :head] = keys.astype(jnp.bfloat16)
    out_ref[:, head:] = proj[:, head:].astype(jnp.bfloat16)


def last_keys_values_kernel(count, head, n_before, block_ref, *refs):
    before, (pos_ref, summary_ref) = refs[:n_before], (refs[n_before], refs[-1])
    refs = refs[n_before + 1 : -1]
    keys_values_kernel(count, head, block_ref, *refs)
    out_ref = refs[-1]
    picks = pos_ref.shape[0]
    picked, start = None, 0
    for ref in (*before, out_ref):
        rows = ref.shape[0]
        column = lax.broadcasted_iota(jnp.int32, (picks, rows), 1) + start
        chosen = jnp.where(column == pos_ref[...], 1.0, 0.0).astype(jnp.bfloat16)
        found = jnp.dot(chosen, ref[...], preferred_element_type=jnp.float32)
        picked = found if picked is None else picked + found
        start += rows
    summary_ref[...] = picked.astype(jnp.bfloat16)


def keys_values(block, hidden, part, weights, acc, gain, cosine, sine, before=(), positions=None):
    rows, features = hidden[0].shape
    head = gain.shape[1]
    row_part = lambda width: pl.BlockSpec((rows, width), lambda i, b: (part, 0))
    in_specs = [whole(rows, features) for _ in hidden] + [
        pl.BlockSpec((features, 2 * head), lambda i, b: (b[0], 0)),
        row_part(2 * head),
        whole(1, head),
        row_part(head),
        row_part(head),
    ]
    operands = [*hidden, weights, acc, gain, cosine, sine]
    out_shape = [jax.ShapeDtypeStruct((rows, 2 * head), jnp.bfloat16)]
    kernel = functools.partial(keys_values_kernel, len(hidden), head)
    if positions is not None:
        picks = positions.shape[0]
        in_specs = [whole(*array.shape) for array in (*before, positions)] + in_specs
        operands = [*before, positions, *operands]
        out_shape.append(jax.ShapeDtypeStruct((picks, 2 * head), jnp.bfloat16))
        kernel = functools.partial(last_keys_values_kernel, len(hidden), head, len(before))
    return pl.pallas_call(
        kernel,
        grid_spec=pltpu.PrefetchScalarGridSpec(
            num_scalar_prefetch=1,
            grid=(1,),
            in_specs=in_specs,
            out_specs=[whole(*shape.shape) for shape in out_shape],
        ),
        out_shape=out_shape,
        compiler_params=params(),
        name="keys_values",
    )(block, *operands)


def queries_kernel(count, head, block_ref, *refs):
    hidden = summed(refs[:count])
    w_ref, acc_ref, gain_ref, cos_ref, sin_ref, q_ref = refs[count:]
    proj = acc_ref[...] + jnp.dot(hidden, w_ref[...], preferred_element_type=jnp.float32)
    for start in range(0, proj.shape[1], head):
        one = norm_rope(proj[:, start : start + head], gain_ref[...], cos_ref[...], sin_ref[...])
        q_ref[:, start : start + head] = one.astype(jnp.bfloat16)


def queries_of(block, hidden, part, weights, acc, gain, cosine, sine):
    rows, features = hidden[0].shape
    head = gain.shape[1]
    width = weights.shape[1]
    tile = 4 * head
    row_part = pl.BlockSpec((rows, head), lambda i, b: (part, 0))
    return pl.pallas_call(
        functools.partial(queries_kernel, len(hidden), head),
        grid_spec=pltpu.PrefetchScalarGridSpec(
            num_scalar_prefetch=1,
            grid=(width // tile,),
            in_specs=[whole(rows, features) for _ in hidden]
            + [
                pl.BlockSpec((features, tile), lambda i, b: (b[0], i)),
                pl.BlockSpec((rows, tile), lambda i, b: (part, i)),
                whole(1, head),
                row_part,
                row_part,
            ],
            out_specs=pl.BlockSpec((rows, tile), lambda i, b: (0, i)),
        ),
        out_shape=jax.ShapeDtypeStruct((rows, width), jnp.bfloat16),
        compiler_params=params(),
        name="queries",
    )(block, *hidden, weights, acc, gain, cosine, sine)


def attention_kernel(n_parts, n_others, per_step, place_ref, heads_ref, length_ref, *refs):
    q_parts, refs = refs[: n_parts * per_step], refs[n_parts * per_step :]
    own_parts, refs = refs[:n_parts], refs[n_parts:]
    others, refs = refs[:n_others], refs[n_others:]
    o_ref, keys_all, values_all = refs
    part_rows, width = own_parts[0].shape
    head = width // 2
    picks = others[0].shape[0]
    cross = n_others * picks
    rows = o_ref.shape[0]

    @pl.when(pl.program_id(0) == 0)
    def _():
        start = 0
        for ref in (*others, *own_parts):
            stop = start + ref.shape[0]
            keys_all[start:stop, :] = ref[:, :head]
            values_all[start:stop, :] = ref[:, head:]
            start = stop

    scale = head ** (-0.5) * LOG2E
    first = place_ref[0] * rows
    own_rows = n_parts * part_rows
    for step in range(per_step):
        queries = q_parts[step * n_parts][...]
        if n_parts > 1:
            in_first = first < part_rows
            queries = jnp.where(in_first, queries, q_parts[step * n_parts + 1][...])
        scores = lax.dot_general(
            queries, keys_all[...], (((1,), (1,)), ((), ())), preferred_element_type=jnp.float32
        )
        row = lax.broadcasted_iota(jnp.int32, (rows, own_rows), 0) + first
        column = lax.broadcasted_iota(jnp.int32, (rows, own_rows), 1)
        own = jnp.where(column <= row, scores[:, cross:], -1e30)
        free = scores[:, :cross]
        largest = jnp.maximum(
            jnp.max(free, axis=1, keepdims=True), jnp.max(own, axis=1, keepdims=True)
        )
        free = jnp.exp2((free - largest) * scale)
        own = jnp.exp2((own - largest) * scale)
        total = jnp.sum(free, axis=1, keepdims=True) + jnp.sum(own, axis=1, keepdims=True)
        mixed = jnp.dot(
            free.astype(jnp.bfloat16), values_all[:cross, :], preferred_element_type=jnp.float32
        ) + jnp.dot(
            own.astype(jnp.bfloat16), values_all[cross:, :], preferred_element_type=jnp.float32
        )
        position = lax.broadcasted_iota(jnp.int32, (rows, head), 0) + first
        mixed = jnp.where(position < length_ref[0], mixed / total, 0.0)
        o_ref[:, step * head : (step + 1) * head] = mixed.astype(jnp.bfloat16)


def attention(place, rows, heads, lengths, queries, own, others):
    n_parts = len(own)
    part_rows, width = queries[0].shape
    head = own[0].shape[1] // 2
    picks = others[0].shape[0]
    reach = n_parts * part_rows + len(others) * picks
    per_step = 2
    per_part = part_rows // rows

    def query_spec(step, part):
        def place_of(i, p, h, n):
            at = jnp.clip(p[0] - part * per_part, 0, per_part - 1)
            return (at, h[per_step * i + step])

        return pl.BlockSpec((rows, head), place_of)

    return pl.pallas_call(
        functools.partial(attention_kernel, n_parts, len(others), per_step),
        grid_spec=pltpu.PrefetchScalarGridSpec(
            num_scalar_prefetch=3,
            grid=(width // head // per_step,),
            in_specs=[query_spec(s, p) for s in range(per_step) for p in range(n_parts)]
            + [whole(part_rows, 2 * head) for _ in own]
            + [whole(picks, 2 * head) for _ in others],
            out_specs=pl.BlockSpec((rows, per_step * head), lambda i, p, h, n: (0, i)),
            scratch_shapes=[
                pltpu.VMEM((reach, head), jnp.bfloat16),
                pltpu.VMEM((reach, head), jnp.bfloat16),
            ],
        ),
        out_shape=jax.ShapeDtypeStruct((rows, width), jnp.bfloat16),
        compiler_params=params(),
        name="attention",
    )(place, heads, lengths, *(q for _ in range(per_step) for q in queries), *own, *others)


def mix_kernel(own_ref, sent_ref, w_ref, *refs):
    pieces, out_ref = refs[:-1], refs[-1]
    sent_w = jnp.concatenate([ref[...] for ref in pieces], axis=0)
    total = jnp.dot(own_ref[...], w_ref[...], preferred_element_type=jnp.float32)
    total = total + jnp.dot(sent_ref[...], sent_w, preferred_element_type=jnp.float32)
    out_ref[...] = total.astype(out_ref.dtype)


def mix(own, sent, w_own, pieces, tile, dtype):
    rows, depth = own.shape
    width = w_own.shape[1]
    column = lambda height: pl.BlockSpec((height, tile), lambda i: (0, i))
    return pl.pallas_call(
        mix_kernel,
        grid=(width // tile,),
        in_specs=[whole(rows, depth), whole(rows, depth), column(depth)]
        + [column(piece.shape[0]) for piece in pieces],
        out_specs=column(rows),
        out_shape=jax.ShapeDtypeStruct((rows, width), dtype),
        compiler_params=params(),
        name="mix",
    )(own, sent, w_own, *pieces)


def shards(hidden_in, lengths, summary_pos, w_query, w_key, w_value, w_out, q_gain, k_gain):
    rows_here = hidden_in.shape[0]
    head_width = q_gain.shape[0]
    heads_here = w_query.shape[1] // head_width
    place = lax.axis_index("tensor")
    cand = lax.axis_index("cand")
    n_cand = lax.axis_size("cand")
    assert lax.axis_size("tensor") == 4 and w_key.shape[1] == head_width

    def swap(array):
        return lax.ppermute(array, "tensor", [(0, 1), (1, 0), (2, 3), (3, 2)])

    def across(array):
        return lax.ppermute(array, "tensor", [(1, 2), (2, 1)])

    def outward(array):
        return lax.ppermute(array, "tensor", [(1, 0), (2, 3)])

    def inward(array):
        return lax.ppermute(array, "tensor", [(0, 1), (3, 2)])

    def between(array, offset):
        return lax.ppermute(array, "cand", [(i, i ^ offset) for i in range(n_cand)])

    low = place < 2
    inner = (place == 1) | (place == 2)
    near = jnp.bitwise_xor(place, 1)
    third = jnp.where(low, 2, 1)
    last = jnp.where(low, 3, 0)
    index = lambda block: block.astype(jnp.int32).reshape(1)

    w_kv = jnp.concatenate([w_key, w_value], axis=1)
    cosine, sine = rope_tables(rows_here, head_width)
    half = rows_here // 2

    from_near, from_mid = lax.optimization_barrier((swap(hidden_in), across(hidden_in)))
    to_outer = outward(from_mid)
    to_inner = [across(lax.slice_in_dim(from_near, i * half, (i + 1) * half)) for i in (0, 1)]
    end = [outward(array) for array in to_inner]

    share = w_out.shape[0] // n_cand
    spread = n_cand == 8 and share == head_width

    def eighth(offset, cue):
        start = jnp.bitwise_xor(cand, offset) * share
        piece = lax.dynamic_slice_in_dim(w_out, start, share, 0)
        return inward(after(piece, cue))

    if spread:
        pieces = {0: eighth(0, from_near), 6: eighth(6, to_inner[0])}
        pieces[2], pieces[4] = between(pieces[0], 2), between(pieces[0], 4)
        pieces[1] = between(after(pieces[0], end[0]), 1)
        moved = jnp.bitwise_xor(cand, jnp.array(OFFSETS, jnp.int32))
        heads = jnp.where(inner, jnp.arange(heads_here, dtype=jnp.int32), moved)
    else:
        pieces = {0: lax.all_gather(eighth(0, from_near), "cand", axis=0, tiled=True)}
        heads = jnp.arange(heads_here, dtype=jnp.int32)

    steps = [(place, [[hidden_in]]), (near, [[from_near]])]
    steps.append((third, [[from_mid, to_outer]]))
    acc_q = acc_kv = None
    for block, parts in steps:
        acc_kv = partial_projection(index(block), parts, w_kv, acc_kv, 2 * head_width)
        acc_q = partial_projection(index(block), parts, w_query, acc_q, 4 * head_width)
    acc_kv, acc_q = lax.optimization_barrier((acc_kv, acc_q))

    final = [[a, b] for a, b in zip(to_inner, end)]
    tables = (cosine, sine)
    k_gain, q_gain = k_gain[None], q_gain[None]
    (own_first,) = keys_values(index(last), final[0], 0, w_kv, acc_kv, k_gain, *tables)
    first_queries = queries_of(index(last), final[0], 0, w_query, acc_q, q_gain, *tables)
    acc_kv = after(acc_kv, first_queries)
    own_second, summary = keys_values(
        index(last), final[1], 1, w_kv, acc_kv, k_gain, *tables, [own_first], summary_pos.reshape(-1, 1)
    )
    own = [own_first, own_second]
    summary, pieces = lax.optimization_barrier((summary, pieces))
    others = [between(summary, offset) for offset in range(1, n_cand)]
    second_queries = queries_of(index(last), final[1], 1, w_query, acc_q, q_gain, *tables)
    queries = [first_queries, second_queries]
    if spread:
        for offset in (6, 2, 4):
            pieces[offset ^ 1] = between(after(pieces[offset], (others, second_queries)), 1)
        pieces = [pieces[offset] for offset in OFFSETS]
    else:
        pieces = list(pieces.values())

    part = rows_here // 4
    columns = w_out.shape[1]
    tile = columns // 10

    def attend(where, rows):
        attended = attention(index(where), rows, heads, lengths, queries, own, others)
        return attended, inward(attended)

    def mixed(rows, dtype):
        return mix(*rows, w_out, pieces, columns // 10, dtype)

    far_rows = attend(last, part)
    third_rows = attend(after(third, far_rows[0]), part)
    far_rows = (after(far_rows[0], third_rows[0]), far_rows[1])
    far = mixed(far_rows, jnp.bfloat16)
    third_rows = (after(third_rows[0], far), third_rows[1])
    far_inner = mixed(third_rows, jnp.bfloat16)
    rest_rows = attend(after(place // 2, far_inner), 2 * part)
    far, far_inner = across(far), across(far_inner)
    rest = mixed(rest_rows, jnp.float32)
    outer_at = jnp.where(low, 0, part)
    outer_rest = lax.dynamic_slice_in_dim(rest, outer_at, part, 0)
    inner_rest = lax.dynamic_slice_in_dim(rest, part - outer_at, part, 0)
    sent = outward((outer_rest + far).astype(jnp.bfloat16))
    kept = (inner_rest + far_inner).astype(jnp.bfloat16)
    return jnp.where(inner, kept, sent)


def solution(mesh):
    return jax.shard_map(
        shards,
        mesh=mesh,
        in_specs=(
            P("cand", "tensor"),
            P("cand"),
            P("cand", None),
            P(None, "tensor"),
            P(None, "tensor"),
            P(None, "tensor"),
            P("tensor", None),
            P(),
            P(),
        ),
        out_specs=P(("cand", "tensor"), None),
        check_vma=False,
    )
```

time: 241 us -> 260 us (1.079)
  Pallas kernels: 38.9 us -> 77.2 us
  starting transfers between devices: 27.2 us -> 64.4 us
  waiting for transfers between devices: 126 us -> 93.7 us
  matrix products: 24 us -> 0 us
    pallas_call x5 -> x14, Pallas kernels: 31.4 us -> 70.9 us  [the longest x3 37.2 us: mix(): pl.pallas_call(mix_kernel, grid=(width // tile,), in_specs=[whole(rows, d...]
    ppermute x2 -> x5, starting transfers between devices: 4.95 us -> 40.5 us  [inward(): return lax.ppermute(array, 'tensor', [(0, 1), (3, 2)])]
    ppermute x2 -> x1, waiting for transfers between devices: 57.1 us -> 24.3 us  [swap(): return lax.ppermute(array, 'tensor', [(0, 1), (1, 0), (2, 3), (3, 2)])]
    ppermute x2 -> x5, waiting for transfers between devices: 40.7 us -> 13.4 us  [inward(): return lax.ppermute(array, 'tensor', [(0, 1), (3, 2)])]
    ppermute x2 -> x4, waiting for transfers between devices: 27.9 us -> 54.3 us  [outward(): return lax.ppermute(array, 'tensor', [(1, 0), (2, 3)])]
    dot_general x4 -> x0, matrix products: 24 us -> none  [mix(): return jnp.dot(rows, w_out, preferred_element_type=jnp.float32)]
    concatenate x1, local copies, waits for them, and re-layouts: 9.3 us -> 0.31 us  [shards(): w_kv = jnp.concatenate([w_key, w_value], axis=1)]
    ppermute x2 -> x1, starting transfers between devices: 7.78 us -> 3.02 us  [swap(): return lax.ppermute(array, 'tensor', [(0, 1), (1, 0), (2, 3), (3, 2)])]
  transfers between devices with their start and end apart: 17 -> 28, of which waited for: 6 -> 8; matrix products, arithmetic and copies ran while one was open for 14% -> 3% of each run, Pallas kernels for 10% -> 25%
where the time goes in v2:
time: 260 us; the launch traced here: 259 us
  waiting for transfers between devices  93.7 us (36%)
  Pallas kernels  77.2 us (30%)
  starting transfers between devices  64.4 us (25%)
  local copies, waits for them, and re-layouts  14.6 us (6%)
  other arithmetic  7.27 us (3%)
    ppermute x4, waiting for transfers between devices, outward(): return lax.ppermute(array, 'tensor', [(1, 0), (2, 3)])  54.3 us
    ppermute x5, starting transfers between devices, inward(): return lax.ppermute(array, 'tensor', [(0, 1), (3, 2)])  40.5 us
    pallas_call x3, Pallas kernels, mix(): pl.pallas_call(mix_kernel, grid=(width // tile,), in_specs=[whole(rows, d...  37.2 us
    ppermute x1, waiting for transfers between devices, swap(): return lax.ppermute(array, 'tensor', [(0, 1), (1, 0), (2, 3), (3, 2)])  24.3 us
    pallas_call x3, Pallas kernels, attention(): pl.pallas_call(functools.partial(attention_kernel, n_parts, len(others),...  17.8 us
    pallas_call x6, Pallas kernels, partial_projection(): pl.pallas_call(functools.partial(partial_kernel, [len(part) for part in p...  13.5 us
    ppermute x5, waiting for transfers between devices, inward(): return lax.ppermute(array, 'tensor', [(0, 1), (3, 2)])  13.4 us
    unnamed x67, local copies, waits for them, and re-layouts  11.1 us
  transfers between devices with their start and end apart: 28, of which 8 were waited for; matrix products, arithmetic and copies ran while one was open for 3% of the time, Pallas kernels for 25%

profile of v2, /device:TPU:0, one launch (start us, length us, event | category | flops | bytes accessed | tf_op | source)
XLA Modules:
  0.0 258.5 jit_solution(277746375789007982)
XLA Ops:
  0.0 3.0 %collective-permute-start = (bf16[512,1280]{1,0:T(8,128)(2,1)}, bf16[512,1280]{1,0:T(8,128)(2,1)S(1)}, u32[]{:S(2)}, u32[]{:S(2)}) collective-permute-start(bf16[512,1280]{1,0:T(8,128)(2,1)} %refs_0_.3), channel_id=1, source_target_pairs={{0,1},{1,0},{2,3},{3,2},{4,5},{5,4},{6,7},{7,6},{8,9},{9,8},{10,11... | collective-permute-start | bytes 3932168 | tf_op jit(solution)/shard_map/ppermute | solution.py:309
  3.0 1.7 collective-permute-start.1
  4.8 3.0 %constant_dynamic-slice_fusion = (bf16[128,5120]{1,0:T(8,128)(2,1)}, bf16[128,5120]{1,0:T(8,128)(2,1)S(1)}) fusion(bf16[1024,5120]{1,0:T(8,128)(2,1)} %w_ref.5, s32[]{:T(128)S(6)} %select_n.48, s32[]{:T(128)S(6)} %select_n.47), kind=kLoop, calls=%fused_computation.11 | loop fusion | bytes 5242888 | tf_op jit(solution)/shard_map/dynamic_slice | solution.py:344
  7.7 24.3 %collective-permute-done.refs_0_ = bf16[512,1280]{1,0:T(8,128)(2,1)S(1)} collective-permute-done((bf16[512,1280]{1,0:T(8,128)(2,1)}, bf16[512,1280]{1,0:T(8,128)(2,1)S(1)}, u32[]{:S(2)}, u32[]{:S(2)}) %collective-permute-start) | collective-permute-done | bytes 1310752 | tf_op jit(solution)/shard_map/ppermute | solution.py:309
  32.1 1.0 copy-done.2
  33.1 0.7 collective-permute-start.2
  33.8 9.8 %collective-permute-start.7 = (bf16[128,5120]{1,0:T(8,128)(2,1)S(1)}, bf16[128,5120]{1,0:T(8,128)(2,1)}, u32[]{:S(2)}, u32[]{:S(2)}) collective-permute-start(bf16[128,5120]{1,0:T(8,128)(2,1)S(1)} %get-tuple-element.35), channel_id=1, source_target_pairs={{0,1},{3,2},{4,5},{7,6},{8,9},{11,10},{12,13},{15,14},{16,17},{19,... | collective-permute-start | bytes 3932168 | tf_op jit(solution)/shard_map/ppermute | solution.py:318
  43.6 1.3 collective-permute-start.4
  44.9 1.3 collective-permute-start.3
  46.2 0.8 copy-done.10
  47.1 0.7 collective-permute-start.5
  47.8 15.4 %collective-permute-start.11 = (bf16[128,5120]{1,0:T(8,128)(2,1)}, bf16[128,5120]{1,0:T(8,128)(2,1)}, u32[]{:S(2)}, u32[]{:S(2)}) collective-permute-start(bf16[128,5120]{1,0:T(8,128)(2,1)} %get-tuple-element.37), channel_id=1, source_target_pairs={{0,1},{3,2},{4,5},{7,6},{8,9},{11,10},{12,13},{15,14},{16,17},{19,... | collective-permute-start | bytes 3932168 | tf_op jit(solution)/shard_map/ppermute | solution.py:318
  63.2 25.3 %collective-permute-done.3.refs_1_ = bf16[256,1280]{1,0:T(8,128)(2,1)S(1)} collective-permute-done((bf16[256,1280]{1,0:T(8,128)(2,1)S(1)}, bf16[256,1280]{1,0:T(8,128)(2,1)S(1)}, u32[]{:S(2)}, u32[]{:S(2)}) %collective-permute-start.3) | collective-permute-done | bytes 655392 | tf_op jit(solution)/shard_map/ppermute | solution.py:315
  88.5 0.9 copy-done.12
  89.4 1.5 collective-permute-start.10
  90.9 1.5 collective-permute-start.9
  92.4 0.2 constant_dynamic-update-slice_fusion.1
  92.7 1.0 copy-done.7
  93.7 1.3 collective-permute-start.6
  95.0 0.3 constant_dynamic-update-slice_fusion.refs_1_.refs_2_.refs_4_
  95.4 2.3 copy-done.9
  97.6 0.5 partial_projection.6.refs_2_
  98.1 0.8 copy-done.14
  98.9 3.2 %partial_projection.9.refs_2_ = f32[512,1024]{1,0:T(8,128)S(1)} custom-call(s32[1]{0:T(128)} %bitcast.3.block_ref, bf16[512,1280]{1,0:T(8,128)(2,1)S(1)} %copy-done.9, bf16[5120,1024]{1,0:T(8,128)(2,1)} %refs_2_.5), custom_call_target="tpu_custom_call" | custom-call | tf_op jit(solution)/shard_map/partial_projection/pallas_call | solution.py:78
  102.1 1.3 copy-done.5
  103.6 1.0 fusion.3
  104.6 0.2 pad_maximum_fusion
  105.0 0.5 partial_projection.7.refs_3_
  105.5 1.1 copy-done.6
  106.6 3.3 %partial_projection.10.refs_3_ = f32[512,1024]{1,0:T(8,128)S(1)} custom-call(s32[1]{0:T(128)} %bitcast.2.block_ref, bf16[512,1280]{1,0:T(8,128)(2,1)S(1)} %copy-done.3, bf16[5120,1024]{1,0:T(8,128)(2,1)} %refs_2_.5, f32[512,1024]{1,0:T(8,128)S(1)} %copy-done.6), custom_call_target="tpu_custom_call" | custom-call | tf_op jit(solution)/shard_map/partial_projection/pallas_call | solution.py:78
  109.9 1.3 copy-done.4
  111.2 2.0 partial_projection.8.refs_3_.refs_5_
  113.3 4.1 %partial_projection.11.refs_3_ = f32[512,1024]{1,0:T(8,128)S(1)} custom-call(s32[1]{0:T(128)} %bitcast.1.block_ref, bf16[512,1280]{1,0:T(8,128)(2,1)} %collective-permute-done.1.refs_0_, bf16[512,1280]{1,0:T(8,128)(2,1)S(1)} %copy-done.8, bf16[5120,1024]{1,0:T(8,128)(2,1)} %refs_2_.5, f32[512,1024]{1,0:T(8,128)} %copy-done.4), custom_call_target="tpu_custom_call" | custom-call | tf_op jit(solution)/shard_map/partial_projection/pallas_call | solution.py:78
  117.4 3.2 %queries.2.refs_0_.refs_2_ = bf16[256,1024]{1,0:T(8,128)(2,1)S(1)} custom-call(s32[1]{0:T(128)} %bitcast.block_ref.place_ref, bf16[256,1280]{1,0:T(8,128)(2,1)S(1)} %copy-done.11, bf16[256,1280]{1,0:T(8,128)(2,1)S(1)} %copy-done.13, bf16[5120,1024]{1,0:T(8,128)(2,1)} %refs_2_.5, f32[512,1024]{1,0:T(8,128)S(1)} %partial_projection.11.refs_3_, ...), custom_call_target="tpu_custom_call" | custom-call | tf_op jit(solution)/shard_map/queries/pallas_call | solution.py:167
  120.6 0.5 keys_values.2.refs_0_.refs_4_
  121.1 1.9 keys_values.3
  123.1 0.6 collective-permute-start.13
  123.7 1.3 collective-permute-start.14
  125.0 0.5 collective-permute-start.15
  125.5 1.2 collective-permute-start.16
  126.7 0.5 collective-permute-start.17
  127.2 0.9 collective-permute-done.13.refs_7_
  128.1 1.3 collective-permute-start.18
  129.4 3.1 %queries.3.refs_1_.refs_3_ = bf16[256,1024]{1,0:T(8,128)(2,1)S(1)} custom-call(s32[1]{0:T(128)} %bitcast.block_ref.place_ref, bf16[256,1280]{1,0:T(8,128)(2,1)S(1)} %collective-permute-done.5.refs_0_.refs_2_, bf16[256,1280]{1,0:T(8,128)(2,1)} %collective-permute-done.6.refs_1_.refs_3_, bf16[5120,1024]{1,0:T(8,128)(2,1)} %refs_2_.5, ...), custom_call_target="tpu_custom_call" | custom-call | tf_op jit(solution)/shard_map/queries/pallas_call | solution.py:167
  132.6 0.8 collective-permute-done.18.refs_12_
  133.5 0.4 collective-permute-start.21
  134.7 5.3 %attention.3.own_ref = bf16[128,1024]{1,0:T(8,128)(2,1)S(1)} custom-call(s32[1]{0:T(128)} %bitcast.block_ref.place_ref, s32[8]{0:T(128)S(1)} %broadcast_select_fusion.heads_ref, s32[1]{0:T(128)S(6)} %copy.13.length_ref, bf16[256,1024]{1,0:T(8,128)(2,1)S(1)} %queries.2.refs_0_.refs_2_, bf16[256,1024]{1,0:T(8,128)(2,1)S(1)} %queries.3.refs_1_.refs_3_, ...), custom_call_target="tpu_custom_call" | custom-call | tf_op jit(solution)/shard_map/attention/pallas_call | solution.py:255
  140.0 5.6 %collective-permute-start.19 = (bf16[128,1024]{1,0:T(8,128)(2,1)S(1)}, bf16[128,1024]{1,0:T(8,128)(2,1)S(1)}, u32[]{:S(2)}, u32[]{:S(2)}) collective-permute-start(bf16[128,1024]{1,0:T(8,128)(2,1)S(1)} %attention.3.own_ref), channel_id=1, source_target_pairs={{0,1},{3,2},{4,5},{7,6},{8,9},{11,10},{12,13},{15,14},{16,17},{19,... | collective-permute-start | bytes 786440 | tf_op jit(solution)/shard_map/ppermute | solution.py:318
  145.7 5.3 %attention.4.own_ref = bf16[128,1024]{1,0:T(8,128)(2,1)S(1)} custom-call(s32[1]{0:T(128)} %bitcast.7.place_ref, s32[8]{0:T(128)S(1)} %broadcast_select_fusion.heads_ref, s32[1]{0:T(128)S(6)} %copy.13.length_ref, bf16[256,1024]{1,0:T(8,128)(2,1)S(1)} %queries.2.refs_0_.refs_2_, bf16[256,1024]{1,0:T(8,128)(2,1)S(1)} %queries.3.refs_1_.refs_3_, ...), custom_call_target="tpu_custom_call" | custom-call | tf_op jit(solution)/shard_map/attention/pallas_call | solution.py:255
  151.0 0.5 collective-permute-done.19.sent_ref
  151.5 11.3 %mix.3 = bf16[128,5120]{1,0:T(8,128)(2,1)S(1)} custom-call(bf16[128,1024]{1,0:T(8,128)(2,1)S(1)} %attention.3.own_ref, bf16[128,1024]{1,0:T(8,128)(2,1)S(1)} %collective-permute-done.19.sent_ref, bf16[1024,5120]{1,0:T(8,128)(2,1)} %w_ref.5, bf16[128,5120]{1,0:T(8,128)(2,1)} %collective-permute-done.7.refs_0_, ...), custom_call_target="tpu_custom_call" | custom-call | tf_op jit(solution)/shard_map/mix/pallas_call | solution.py:287
  162.8 1.7 collective-permute-start.26
  164.6 5.2 %collective-permute-start.23 = (bf16[128,1024]{1,0:T(8,128)(2,1)S(1)}, bf16[128,1024]{1,0:T(8,128)(2,1)S(1)}, u32[]{:S(2)}, u32[]{:S(2)}) collective-permute-start(bf16[128,1024]{1,0:T(8,128)(2,1)S(1)} %attention.4.own_ref), channel_id=1, source_target_pairs={{0,1},{3,2},{4,5},{7,6},{8,9},{11,10},{12,13},{15,14},{16,17},{19,... | collective-permute-start | bytes 786440 | tf_op jit(solution)/shard_map/ppermute | solution.py:318
  169.8 4.9 %collective-permute-done.23.sent_ref = bf16[128,1024]{1,0:T(8,128)(2,1)S(1)} collective-permute-done((bf16[128,1024]{1,0:T(8,128)(2,1)S(1)}, bf16[128,1024]{1,0:T(8,128)(2,1)S(1)}, u32[]{:S(2)}, u32[]{:S(2)}) %collective-permute-start.23) | collective-permute-done | bytes 262176 | tf_op jit(solution)/shard_map/ppermute | solution.py:318
  174.7 11.3 %mix.4 = bf16[128,5120]{1,0:T(8,128)(2,1)S(1)} custom-call(bf16[128,1024]{1,0:T(8,128)(2,1)S(1)} %attention.4.own_ref, bf16[128,1024]{1,0:T(8,128)(2,1)S(1)} %collective-permute-done.23.sent_ref, bf16[1024,5120]{1,0:T(8,128)(2,1)} %w_ref.5, bf16[128,5120]{1,0:T(8,128)(2,1)} %collective-permute-done.7.refs_0_, ...), custom_call_target="tpu_custom_call" | custom-call | tf_op jit(solution)/shard_map/mix/pallas_call | solution.py:287
  186.1 7.2 %attention.5.own_ref = bf16[256,1024]{1,0:T(8,128)(2,1)S(1)} custom-call(s32[1]{0:T(128)} %bitcast.8.place_ref, s32[8]{0:T(128)S(1)} %broadcast_select_fusion.heads_ref, s32[1]{0:T(128)S(6)} %copy.13.length_ref, bf16[256,1024]{1,0:T(8,128)(2,1)S(1)} %queries.2.refs_0_.refs_2_, bf16[256,1024]{1,0:T(8,128)(2,1)S(1)} %queries.3.refs_1_.refs_3_, ...), custom_call_target="tpu_custom_call" | custom-call | tf_op jit(solution)/shard_map/attention/pallas_call | solution.py:255
  193.3 4.4 %collective-permute-start.24 = (bf16[256,1024]{1,0:T(8,128)(2,1)S(1)}, bf16[256,1024]{1,0:T(8,128)(2,1)S(1)}, u32[]{:S(2)}, u32[]{:S(2)}) collective-permute-start(bf16[256,1024]{1,0:T(8,128)(2,1)S(1)} %attention.5.own_ref), channel_id=1, source_target_pairs={{0,1},{3,2},{4,5},{7,6},{8,9},{11,10},{12,13},{15,14},{16,17},{19,... | collective-permute-start | bytes 1572872 | tf_op jit(solution)/shard_map/ppermute | solution.py:318
  197.8 1.8 collective-permute-start.25
  199.5 8.0 %collective-permute-done.24.sent_ref = bf16[256,1024]{1,0:T(8,128)(2,1)S(1)} collective-permute-done((bf16[256,1024]{1,0:T(8,128)(2,1)S(1)}, bf16[256,1024]{1,0:T(8,128)(2,1)S(1)}, u32[]{:S(2)}, u32[]{:S(2)}) %collective-permute-start.24) | collective-permute-done | bytes 524320 | tf_op jit(solution)/shard_map/ppermute | solution.py:318
  207.5 14.6 %mix.5 = f32[256,5120]{1,0:T(8,128)} custom-call(bf16[256,1024]{1,0:T(8,128)(2,1)S(1)} %attention.5.own_ref, bf16[256,1024]{1,0:T(8,128)(2,1)S(1)} %collective-permute-done.24.sent_ref, bf16[1024,5120]{1,0:T(8,128)(2,1)} %w_ref.5, bf16[128,5120]{1,0:T(8,128)(2,1)} %collective-permute-done.7.refs_0_, bf16[128,5120]{1,0:T(8,128)(2,1)} %collective-permute-done.11.refs_1_, ...), custom_call_target="tpu_custom_call" | custom-call | tf_op jit(solution)/shard_map/mix/pallas_call | solution.py:287
  222.1 2.4 add_convert_fusion
  224.5 1.3 collective-permute-start.27
  225.8 29.0 %collective-permute-done.27 = bf16[128,5120]{1,0:T(8,128)(2,1)S(1)} collective-permute-done((bf16[128,5120]{1,0:T(8,128)(2,1)S(1)}, bf16[128,5120]{1,0:T(8,128)(2,1)S(1)}, u32[]{:S(2)}, u32[]{:S(2)}) %collective-permute-start.27) | collective-permute-done | bytes 1310752 | tf_op jit(solution)/shard_map/ppermute | solution.py:315
  254.8 3.7 %fusion = bf16[128,5120]{1,0:T(8,128)(2,1)} fusion(bf16[128,5120]{1,0:T(8,128)(2,1)S(1)} %collective-permute-done.27, bf16[128,5120]{1,0:T(8,128)(2,1)} %collective-permute-done.25, f32[256,5120]{1,0:T(8,128)} %mix.5, s32[]{:T(128)S(6)} %select_n.50, pred[]{:T(512)S(6)} %or.3), kind=kLoop, calls=%fused_computation.2 | loop fusion | flops 2621440 | bytes 6553605 | tf_op jit(solution)/shard_map/jit(_where)/select_n | solution.py:411
  (85 shorter events, 0.9 us)
Async XLA Ops:
  0.0 32.0 %collective-permute-start = (bf16[512,1280]{1,0:T(8,128)(2,1)}, bf16[512,1280]{1,0:T(8,128)(2,1)S(1)}, u32[]{:S(2)}, u32[]{:S(2)}) collective-permute-start(bf16[512,1280]{1,0:T(8,128)(2,1)} %refs_0_.3), channel_id=1, source_target_pairs={{0,1},{1,0},{2,3},{3,2},{4,5},{5,4},{6,7},{7,6},{8,9},{9,8},{10,11... | collective-permute-start | bytes 3932168 | tf_op jit(solution)/shard_map/ppermute | solution.py:309
  3.0 29.0 %collective-permute-start.1 = (bf16[512,1280]{1,0:T(8,128)(2,1)}, bf16[512,1280]{1,0:T(8,128)(2,1)}, u32[]{:S(2)}, u32[]{:S(2)}) collective-permute-start(bf16[512,1280]{1,0:T(8,128)(2,1)} %refs_0_.3), channel_id=1, source_target_pairs={{1,2},{2,1},{5,6},{6,5},{9,10},{10,9},{13,14},{14,13},{17,18},{18,... | collective-permute-start | bytes 3932168 | tf_op jit(solution)/shard_map/ppermute | solution.py:312
  7.7 84.7 %copy-start.29 = (bf16[5120,128]{1,0:T(8,128)(2,1)S(1)}, bf16[5120,128]{1,0:T(8,128)(2,1)}, u32[]{:S(2)}) copy-start(bf16[5120,128]{1,0:T(8,128)(2,1)} %param.14) | copy-start | bytes 3932164
  32.0 1.1 copy-start.2
  33.1 11.8 %collective-permute-start.2 = (bf16[256,1280]{1,0:T(8,128)(2,1)S(1)}, bf16[256,1280]{1,0:T(8,128)(2,1)S(1)}, u32[]{:S(2)}, u32[]{:S(2)}) collective-permute-start(bf16[256,1280]{1,0:T(8,128)(2,1)S(1)} %get-tuple-element.54), channel_id=1, source_target_pairs={{1,2},{2,1},{5,6},{6,5},{9,10},{10,9},{13,14},{14,13},{17,18},{18,... | collective-permute-start | bytes 1966088 | tf_op jit(solution)/shard_map/ppermute | solution.py:312
  33.8 55.6 %collective-permute-start.7 = (bf16[128,5120]{1,0:T(8,128)(2,1)S(1)}, bf16[128,5120]{1,0:T(8,128)(2,1)}, u32[]{:S(2)}, u32[]{:S(2)}) collective-permute-start(bf16[128,5120]{1,0:T(8,128)(2,1)S(1)} %get-tuple-element.35), channel_id=1, source_target_pairs={{0,1},{3,2},{4,5},{7,6},{8,9},{11,10},{12,13},{15,14},{16,17},{19,... | collective-permute-start | bytes 3932168 | tf_op jit(solution)/shard_map/ppermute | solution.py:318
  43.6 49.0 %collective-permute-start.4 = (bf16[512,1280]{1,0:T(8,128)(2,1)}, bf16[512,1280]{1,0:T(8,128)(2,1)S(1)}, u32[]{:S(2)}, u32[]{:S(2)}) collective-permute-start(bf16[512,1280]{1,0:T(8,128)(2,1)} %collective-permute-done.1.refs_0_), channel_id=1, source_target_pairs={{1,0},{2,3},{5,4},{6,7},{9,8},{10,11},{13,12},{14,15},{17,16},{18,... | collective-permute-start | bytes 3932168 | tf_op jit(solution)/shard_map/ppermute | solution.py:315
  44.9 43.6 %collective-permute-start.3 = (bf16[256,1280]{1,0:T(8,128)(2,1)S(1)}, bf16[256,1280]{1,0:T(8,128)(2,1)S(1)}, u32[]{:S(2)}, u32[]{:S(2)}) collective-permute-start(bf16[256,1280]{1,0:T(8,128)(2,1)S(1)} %collective-permute-done.2.refs_0_), channel_id=1, source_target_pairs={{1,0},{2,3},{5,4},{6,7},{9,8},{10,11},{13,12},{14,15},{17,16},{18,... | collective-permute-start | bytes 1966088 | tf_op jit(solution)/shard_map/ppermute | solution.py:315
  46.2 0.9 copy-start.10
  47.1 43.8 %collective-permute-start.5 = (bf16[256,1280]{1,0:T(8,128)(2,1)S(1)}, bf16[256,1280]{1,0:T(8,128)(2,1)S(1)}, u32[]{:S(2)}, u32[]{:S(2)}) collective-permute-start(bf16[256,1280]{1,0:T(8,128)(2,1)S(1)} %get-tuple-element.53), channel_id=1, source_target_pairs={{1,2},{2,1},{5,6},{6,5},{9,10},{10,9},{13,14},{14,13},{17,18},{18,... | collective-permute-start | bytes 1966088 | tf_op jit(solution)/shard_map/ppermute | solution.py:312
  47.8 47.2 %copy-start.30 = (bf16[5120,128]{1,0:T(8,128)(2,1)S(1)}, bf16[5120,128]{1,0:T(8,128)(2,1)}, u32[]{:S(2)}) copy-start(bf16[5120,128]{1,0:T(8,128)(2,1)} %param.15) | copy-start | bytes 3932164
  47.8 75.2 %collective-permute-start.11 = (bf16[128,5120]{1,0:T(8,128)(2,1)}, bf16[128,5120]{1,0:T(8,128)(2,1)}, u32[]{:S(2)}, u32[]{:S(2)}) collective-permute-start(bf16[128,5120]{1,0:T(8,128)(2,1)} %get-tuple-element.37), channel_id=1, source_target_pairs={{0,1},{3,2},{4,5},{7,6},{8,9},{11,10},{12,13},{15,14},{16,17},{19,... | collective-permute-start | bytes 3932168 | tf_op jit(solution)/shard_map/ppermute | solution.py:318
  88.5 0.9 copy-start.12
  89.4 33.6 %collective-permute-start.8 = (bf16[128,5120]{1,0:T(8,128)(2,1)}, bf16[128,5120]{1,0:T(8,128)(2,1)}, u32[]{:S(2)}, u32[]{:S(2)}) collective-permute-start(bf16[128,5120]{1,0:T(8,128)(2,1)} %collective-permute-done.7.refs_0_), channel_id=1, source_target_pairs={{0,4},{4,0},{8,12},{12,8},{16,20},{20,16},{24,28},{28,24},{1,5},{5... | collective-permute-start | bytes 3932168 | tf_op jit(solution)/shard_map/ppermute | solution.py:321
  89.4 33.6 %collective-permute-start.10 = (bf16[128,5120]{1,0:T(8,128)(2,1)}, bf16[128,5120]{1,0:T(8,128)(2,1)}, u32[]{:S(2)}, u32[]{:S(2)}) collective-permute-start(bf16[128,5120]{1,0:T(8,128)(2,1)} %collective-permute-done.7.refs_0_), channel_id=1, source_target_pairs={{0,16},{4,20},{8,24},{12,28},{16,0},{20,4},{24,8},{28,12},{1,17},{... | collective-permute-start | bytes 3932168 | tf_op jit(solution)/shard_map/ppermute | solution.py:321
  90.9 32.1 %collective-permute-start.9 = (bf16[128,5120]{1,0:T(8,128)(2,1)}, bf16[128,5120]{1,0:T(8,128)(2,1)}, u32[]{:S(2)}, u32[]{:S(2)}) collective-permute-start(bf16[128,5120]{1,0:T(8,128)(2,1)} %collective-permute-done.7.refs_0_), channel_id=1, source_target_pairs={{0,8},{4,12},{8,0},{12,4},{16,24},{20,28},{24,16},{28,20},{1,9},{5... | collective-permute-start | bytes 3932168 | tf_op jit(solution)/shard_map/ppermute | solution.py:321
  92.6 1.1 copy-start.7
  93.7 27.4 %collective-permute-start.6 = (bf16[256,1280]{1,0:T(8,128)(2,1)S(1)}, bf16[256,1280]{1,0:T(8,128)(2,1)}, u32[]{:S(2)}, u32[]{:S(2)}) collective-permute-start(bf16[256,1280]{1,0:T(8,128)(2,1)S(1)} %collective-permute-done.5.refs_0_.refs_2_), channel_id=1, source_target_pairs={{1,0},{2,3},{5,4},{6,7},{9,8},{10,11},{13,12},{14,15},{17,16},{18,... | collective-permute-start | bytes 1966088 | tf_op jit(solution)/shard_map/ppermute | solution.py:315
  95.3 9.5 %copy-start = (bf16[5120,256]{1,0:T(8,128)(2,1)}, bf16[5120,256]{1,0:T(8,128)(2,1)S(1)}, u32[]{:S(2)}) copy-start(bf16[5120,256]{1,0:T(8,128)(2,1)S(1)} %constant_dynamic-update-slice_fusion.refs_1_.refs_2_.refs_4_) | copy-start | bytes 7864324
  95.3 2.3 copy-start.9
  98.1 0.8 copy-start.14
  98.9 4.5 %copy-start.31 = (s32[1,128]{1,0:T(1,128)S(1)}, s32[1,128]{1,0:T(1,128)}, u32[]{:S(2)}) copy-start(s32[1,128]{1,0:T(1,128)} %param.12) | copy-start | bytes 1540
  102.1 1.3 copy-start.5
  103.6 1.3 copy-start.3
  103.6 1.4 copy-start.15
  105.0 1.6 copy-start.6
  106.6 4.6 %copy-start.8 = (bf16[512,1280]{1,0:T(8,128)(2,1)S(1)}, bf16[512,1280]{1,0:T(8,128)(2,1)}, u32[]{:S(2)}) copy-start(bf16[512,1280]{1,0:T(8,128)(2,1)} %copy-done.7) | copy-start | bytes 3932164
  109.9 1.3 copy-start.4
  113.2 4.1 %copy-start.11 = (bf16[256,1280]{1,0:T(8,128)(2,1)S(1)}, bf16[256,1280]{1,0:T(8,128)(2,1)}, u32[]{:S(2)}) copy-start(bf16[256,1280]{1,0:T(8,128)(2,1)} %copy-done.10) | copy-start | bytes 1966084
  113.2 4.1 %copy-start.13 = (bf16[256,1280]{1,0:T(8,128)(2,1)S(1)}, bf16[256,1280]{1,0:T(8,128)(2,1)}, u32[]{:S(2)}) copy-start(bf16[256,1280]{1,0:T(8,128)(2,1)} %copy-done.12) | copy-start | bytes 1966084
  113.2 4.1 %copy-start.28 = (f32[128]{0:T(128)S(1)}, f32[128]{0:T(128)}, u32[]{:S(2)}) copy-start(f32[128]{0:T(128)} %param.17) | copy-start | bytes 1540
  117.4 3.2 %copy-start.1 = (bf16[5120,256]{1,0:T(8,128)(2,1)S(1)}, bf16[5120,256]{1,0:T(8,128)(2,1)}, u32[]{:S(2)}) copy-start(bf16[5120,256]{1,0:T(8,128)(2,1)} %copy-done) | copy-start | bytes 7864324
  117.4 3.2 %copy-start.27 = (f32[128]{0:T(128)S(1)}, f32[128]{0:T(128)}, u32[]{:S(2)}) copy-start(f32[128]{0:T(128)} %param.18) | copy-start | bytes 1540
  123.0 11.7 %copy-start.32 = (s32[8]{0:T(128)S(1)}, s32[8]{0:T(128)}, u32[]{:S(2)}) copy-start(s32[8]{0:T(128)} %constant.47.clone) | copy-start | bytes 100
  123.0 3.6 %collective-permute-start.12 = (bf16[128,256]{1,0:T(8,128)(2,1)S(1)}, bf16[128,256]{1,0:T(8,128)(2,1)S(1)}, u32[]{:S(2)}, u32[]{:S(2)}) collective-permute-start(bf16[128,256]{1,0:T(8,128)(2,1)S(1)} %get-tuple-element.38), channel_id=1, source_target_pairs={{0,4},{4,0},{8,12},{12,8},{16,20},{20,16},{24,28},{28,24},{1,5},{5... | collective-permute-start | bytes 196616 | tf_op jit(solution)/shard_map/ppermute | solution.py:321
  123.1 5.0 %collective-permute-start.13 = (bf16[128,256]{1,0:T(8,128)(2,1)S(1)}, bf16[128,256]{1,0:T(8,128)(2,1)S(1)}, u32[]{:S(2)}, u32[]{:S(2)}) collective-permute-start(bf16[128,256]{1,0:T(8,128)(2,1)S(1)} %get-tuple-element.38), channel_id=1, source_target_pairs={{0,8},{4,12},{8,0},{12,4},{16,24},{20,28},{24,16},{28,20},{1,9},{5... | collective-permute-start | bytes 196616 | tf_op jit(solution)/shard_map/ppermute | solution.py:321
  123.7 8.8 %collective-permute-start.14 = (bf16[128,256]{1,0:T(8,128)(2,1)S(1)}, bf16[128,256]{1,0:T(8,128)(2,1)S(1)}, u32[]{:S(2)}, u32[]{:S(2)}) collective-permute-start(bf16[128,256]{1,0:T(8,128)(2,1)S(1)} %get-tuple-element.38), channel_id=1, source_target_pairs={{0,12},{4,8},{8,4},{12,0},{16,28},{20,24},{24,20},{28,16},{1,13},{... | collective-permute-start | bytes 196616 | tf_op jit(solution)/shard_map/ppermute | solution.py:321
  125.0 7.6 %collective-permute-start.15 = (bf16[128,256]{1,0:T(8,128)(2,1)S(1)}, bf16[128,256]{1,0:T(8,128)(2,1)S(1)}, u32[]{:S(2)}, u32[]{:S(2)}) collective-permute-start(bf16[128,256]{1,0:T(8,128)(2,1)S(1)} %get-tuple-element.38), channel_id=1, source_target_pairs={{0,16},{4,20},{8,24},{12,28},{16,0},{20,4},{24,8},{28,12},{1,17},{... | collective-permute-start | bytes 196616 | tf_op jit(solution)/shard_map/ppermute | solution.py:321
  125.5 7.1 %collective-permute-start.16 = (bf16[128,256]{1,0:T(8,128)(2,1)S(1)}, bf16[128,256]{1,0:T(8,128)(2,1)S(1)}, u32[]{:S(2)}, u32[]{:S(2)}) collective-permute-start(bf16[128,256]{1,0:T(8,128)(2,1)S(1)} %get-tuple-element.38), channel_id=1, source_target_pairs={{0,20},{4,16},{8,28},{12,24},{16,4},{20,0},{24,12},{28,8},{1,21},{... | collective-permute-start | bytes 196616 | tf_op jit(solution)/shard_map/ppermute | solution.py:321
  126.7 5.9 %collective-permute-start.17 = (bf16[128,256]{1,0:T(8,128)(2,1)S(1)}, bf16[128,256]{1,0:T(8,128)(2,1)S(1)}, u32[]{:S(2)}, u32[]{:S(2)}) collective-permute-start(bf16[128,256]{1,0:T(8,128)(2,1)S(1)} %get-tuple-element.38), channel_id=1, source_target_pairs={{0,24},{4,28},{8,16},{12,20},{16,8},{20,12},{24,0},{28,4},{1,25},{... | collective-permute-start | bytes 196616 | tf_op jit(solution)/shard_map/ppermute | solution.py:321
  128.1 5.3 %collective-permute-start.18 = (bf16[128,256]{1,0:T(8,128)(2,1)S(1)}, bf16[128,256]{1,0:T(8,128)(2,1)S(1)}, u32[]{:S(2)}, u32[]{:S(2)}) collective-permute-start(bf16[128,256]{1,0:T(8,128)(2,1)S(1)} %get-tuple-element.38), channel_id=1, source_target_pairs={{0,28},{4,24},{8,20},{12,16},{16,12},{20,8},{24,4},{28,0},{1,29},{... | collective-permute-start | bytes 196616 | tf_op jit(solution)/shard_map/ppermute | solution.py:321
  132.5 13.1 %copy-start.17 = (bf16[128,256]{1,0:T(8,128)(2,1)}, bf16[128,256]{1,0:T(8,128)(2,1)S(1)}, u32[]{:S(2)}) copy-start(bf16[128,256]{1,0:T(8,128)(2,1)S(1)} %collective-permute-done.14.refs_8_) | copy-start | bytes 196612
  132.6 13.1 %copy-start.19 = (bf16[128,256]{1,0:T(8,128)(2,1)}, bf16[128,256]{1,0:T(8,128)(2,1)S(1)}, u32[]{:S(2)}) copy-start(bf16[128,256]{1,0:T(8,128)(2,1)S(1)} %collective-permute-done.15.refs_9_) | copy-start | bytes 196612
  132.6 13.1 %copy-start.21 = (bf16[128,256]{1,0:T(8,128)(2,1)}, bf16[128,256]{1,0:T(8,128)(2,1)S(1)}, u32[]{:S(2)}) copy-start(bf16[128,256]{1,0:T(8,128)(2,1)S(1)} %collective-permute-done.16.refs_10_) | copy-start | bytes 196612
  132.6 13.1 %copy-start.23 = (bf16[128,256]{1,0:T(8,128)(2,1)}, bf16[128,256]{1,0:T(8,128)(2,1)S(1)}, u32[]{:S(2)}) copy-start(bf16[128,256]{1,0:T(8,128)(2,1)S(1)} %collective-permute-done.17.refs_11_) | copy-start | bytes 196612
  133.4 12.3 %copy-start.25 = (bf16[128,256]{1,0:T(8,128)(2,1)}, bf16[128,256]{1,0:T(8,128)(2,1)S(1)}, u32[]{:S(2)}) copy-start(bf16[128,256]{1,0:T(8,128)(2,1)S(1)} %collective-permute-done.18.refs_12_) | copy-start | bytes 196612
  133.4 18.1 %collective-permute-start.22 = (bf16[128,5120]{1,0:T(8,128)(2,1)}, bf16[128,5120]{1,0:T(8,128)(2,1)}, u32[]{:S(2)}, u32[]{:S(2)}) collective-permute-start(bf16[128,5120]{1,0:T(8,128)(2,1)} %collective-permute-done.10.refs_3_), channel_id=1, source_target_pairs={{0,4},{4,0},{8,12},{12,8},{16,20},{20,16},{24,28},{28,24},{1,5},{5... | collective-permute-start | bytes 3932168 | tf_op jit(solution)/shard_map/ppermute | solution.py:321
  133.5 18.0 %collective-permute-start.21 = (bf16[128,5120]{1,0:T(8,128)(2,1)}, bf16[128,5120]{1,0:T(8,128)(2,1)}, u32[]{:S(2)}, u32[]{:S(2)}) collective-permute-start(bf16[128,5120]{1,0:T(8,128)(2,1)} %collective-permute-done.9.refs_2_), channel_id=1, source_target_pairs={{0,4},{4,0},{8,12},{12,8},{16,20},{20,16},{24,28},{28,24},{1,5},{5... | collective-permute-start | bytes 3932168 | tf_op jit(solution)/shard_map/ppermute | solution.py:321
  133.9 17.6 %collective-permute-start.20 = (bf16[128,5120]{1,0:T(8,128)(2,1)}, bf16[128,5120]{1,0:T(8,128)(2,1)}, u32[]{:S(2)}, u32[]{:S(2)}) collective-permute-start(bf16[128,5120]{1,0:T(8,128)(2,1)} %collective-permute-done.11.refs_1_), channel_id=1, source_target_pairs={{0,4},{4,0},{8,12},{12,8},{16,20},{20,16},{24,28},{28,24},{1,5},{5... | collective-permute-start | bytes 3932168 | tf_op jit(solution)/shard_map/ppermute | solution.py:321
  140.0 11.5 %collective-permute-start.19 = (bf16[128,1024]{1,0:T(8,128)(2,1)S(1)}, bf16[128,1024]{1,0:T(8,128)(2,1)S(1)}, u32[]{:S(2)}, u32[]{:S(2)}) collective-permute-start(bf16[128,1024]{1,0:T(8,128)(2,1)S(1)} %attention.3.own_ref), channel_id=1, source_target_pairs={{0,1},{3,2},{4,5},{7,6},{8,9},{11,10},{12,13},{15,14},{16,17},{19,... | collective-permute-start | bytes 786440 | tf_op jit(solution)/shard_map/ppermute | solution.py:318
  162.8 59.3 %collective-permute-start.26 = (bf16[128,5120]{1,0:T(8,128)(2,1)S(1)}, bf16[128,5120]{1,0:T(8,128)(2,1)}, u32[]{:S(2)}, u32[]{:S(2)}) collective-permute-start(bf16[128,5120]{1,0:T(8,128)(2,1)S(1)} %mix.3), channel_id=1, source_target_pairs={{1,2},{2,1},{5,6},{6,5},{9,10},{10,9},{13,14},{14,13},{17,18},{18,... | collective-permute-start | bytes 3932168 | tf_op jit(solution)/shard_map/ppermute | solution.py:312
  164.6 10.2 %collective-permute-start.23 = (bf16[128,1024]{1,0:T(8,128)(2,1)S(1)}, bf16[128,1024]{1,0:T(8,128)(2,1)S(1)}, u32[]{:S(2)}, u32[]{:S(2)}) collective-permute-start(bf16[128,1024]{1,0:T(8,128)(2,1)S(1)} %attention.4.own_ref), channel_id=1, source_target_pairs={{0,1},{3,2},{4,5},{7,6},{8,9},{11,10},{12,13},{15,14},{16,17},{19,... | collective-permute-start | bytes 786440 | tf_op jit(solution)/shard_map/ppermute | solution.py:318
  169.8 16.3 %copy-start.18 = (bf16[128,256]{1,0:T(8,128)(2,1)S(1)}, bf16[128,256]{1,0:T(8,128)(2,1)}, u32[]{:S(2)}) copy-start(bf16[128,256]{1,0:T(8,128)(2,1)} %copy-done.17) | copy-start | bytes 196612
  169.8 16.3 %copy-start.20 = (bf16[128,256]{1,0:T(8,128)(2,1)S(1)}, bf16[128,256]{1,0:T(8,128)(2,1)}, u32[]{:S(2)}) copy-start(bf16[128,256]{1,0:T(8,128)(2,1)} %copy-done.19) | copy-start | bytes 196612
  169.8 16.3 %copy-start.22 = (bf16[128,256]{1,0:T(8,128)(2,1)S(1)}, bf16[128,256]{1,0:T(8,128)(2,1)}, u32[]{:S(2)}) copy-start(bf16[128,256]{1,0:T(8,128)(2,1)} %copy-done.21) | copy-start | bytes 196612
  169.8 16.3 %copy-start.24 = (bf16[128,256]{1,0:T(8,128)(2,1)S(1)}, bf16[128,256]{1,0:T(8,128)(2,1)}, u32[]{:S(2)}) copy-start(bf16[128,256]{1,0:T(8,128)(2,1)} %copy-done.23) | copy-start | bytes 196612
  169.8 16.3 %copy-start.26 = (bf16[128,256]{1,0:T(8,128)(2,1)S(1)}, bf16[128,256]{1,0:T(8,128)(2,1)}, u32[]{:S(2)}) copy-start(bf16[128,256]{1,0:T(8,128)(2,1)} %copy-done.25) | copy-start | bytes 196612
  186.0 7.3 %copy-start.16 = (bf16[128,5120]{1,0:T(8,128)(2,1)}, bf16[128,5120]{1,0:T(8,128)(2,1)S(1)}, u32[]{:S(2)}) copy-start(bf16[128,5120]{1,0:T(8,128)(2,1)S(1)} %mix.4) | copy-start | bytes 3932164
  193.3 14.2 %collective-permute-start.24 = (bf16[256,1024]{1,0:T(8,128)(2,1)S(1)}, bf16[256,1024]{1,0:T(8,128)(2,1)S(1)}, u32[]{:S(2)}, u32[]{:S(2)}) collective-permute-start(bf16[256,1024]{1,0:T(8,128)(2,1)S(1)} %attention.5.own_ref), channel_id=1, source_target_pairs={{0,1},{3,2},{4,5},{7,6},{8,9},{11,10},{12,13},{15,14},{16,17},{19,... | collective-permute-start | bytes 1572872 | tf_op jit(solution)/shard_map/ppermute | solution.py:318
  197.8 28.1 %collective-permute-start.25 = (bf16[128,5120]{1,0:T(8,128)(2,1)}, bf16[128,5120]{1,0:T(8,128)(2,1)}, u32[]{:S(2)}, u32[]{:S(2)}) collective-permute-start(bf16[128,5120]{1,0:T(8,128)(2,1)} %copy-done.16), channel_id=1, source_target_pairs={{1,2},{2,1},{5,6},{6,5},{9,10},{10,9},{13,14},{14,13},{17,18},{18,... | collective-permute-start | bytes 3932168 | tf_op jit(solution)/shard_map/ppermute | solution.py:312
  224.5 30.3 %collective-permute-start.27 = (bf16[128,5120]{1,0:T(8,128)(2,1)S(1)}, bf16[128,5120]{1,0:T(8,128)(2,1)S(1)}, u32[]{:S(2)}, u32[]{:S(2)}) collective-permute-start(bf16[128,5120]{1,0:T(8,128)(2,1)S(1)} %add_convert_fusion), channel_id=1, source_target_pairs={{1,0},{2,3},{5,4},{6,7},{9,8},{10,11},{13,12},{14,15},{17,16},{18,... | collective-permute-start | bytes 3932168 | tf_op jit(solution)/shard_map/ppermute | solution.py:315

commit v3 on v2

--- a/solution.py
+++ b/solution.py
@@ -7,9 +7,8 @@
 from jax.experimental.pallas import tpu as pltpu
 from jax.sharding import PartitionSpec as P
 
-VMEM_LIMIT = 48 * 1024 * 1024
+VMEM_LIMIT = 28 * 1024 * 1024
 LOG2E = 1.4426950408889634
-OFFSETS = (0, 6, 2, 4, 1, 7, 3, 5)
 
 
 def rope_tables(rows, width):
@@ -185,8 +184,8 @@
     )(block, *hidden, weights, acc, gain, cosine, sine)
 
 
-def attention_kernel(n_parts, n_others, per_step, place_ref, heads_ref, length_ref, *refs):
-    q_parts, refs = refs[: n_parts * per_step], refs[n_parts * per_step :]
+def attention_kernel(n_parts, n_others, stack, place_ref, length_ref, *refs):
+    q_parts, refs = refs[:n_parts], refs[n_parts:]
     own_parts, refs = refs[:n_parts], refs[n_parts:]
     others, refs = refs[:n_others], refs[n_others:]
     o_ref, keys_all, values_all = refs
@@ -196,29 +195,38 @@
     cross = n_others * picks
     rows = o_ref.shape[0]
 
-    @pl.when(pl.program_id(0) == 0)
-    def _():
-        start = 0
-        for ref in (*others, *own_parts):
-            stop = start + ref.shape[0]
-            keys_all[start:stop, :] = ref[:, :head]
-            values_all[start:stop, :] = ref[:, head:]
-            start = stop
+    start = 0
+    for ref in (*others, *own_parts):
+        stop = start + ref.shape[0]
+        keys_all[start:stop, :] = ref[:, :head]
+        values_all[start:stop, :] = ref[:, head:]
+        start = stop
 
     scale = head ** (-0.5) * LOG2E
     first = place_ref[0] * rows
     own_rows = n_parts * part_rows
-    for step in range(per_step):
-        queries = q_parts[step * n_parts][...]
-        if n_parts > 1:
-            in_first = first < part_rows
-            queries = jnp.where(in_first, queries, q_parts[step * n_parts + 1][...])
+    offset = pl.multiple_of(lax.rem(first, part_rows), rows)
+    row = lax.broadcasted_iota(jnp.int32, (rows, own_rows), 0) + first
+    column = lax.broadcasted_iota(jnp.int32, (rows, own_rows), 1)
+    allowed = jnp.concatenate([column <= row] * stack, axis=0)
+    position = lax.broadcasted_iota(jnp.int32, (rows, head), 0) + first
+    kept = jnp.concatenate([position < length_ref[0]] * stack, axis=0)
+    for left in range(0, o_ref.shape[1], stack * head):
+        lanes = [slice(left + i * head, left + (i + 1) * head) for i in range(stack)]
+        queries = [q_parts[0][pl.ds(offset, rows), lane] for lane in lanes]
+        for part in range(1, n_parts):
+            here = first >= part * part_rows
+            queries = [
+                jnp.where(here, q_parts[part][pl.ds(offset, rows), lane], query)
+                for lane, query in zip(lanes, queries)
+            ]
         scores = lax.dot_general(
-            queries, keys_all[...], (((1,), (1,)), ((), ())), preferred_element_type=jnp.float32
+            jnp.concatenate(queries, axis=0),
+            keys_all[...],
+            (((1,), (1,)), ((), ())),
+            preferred_element_type=jnp.float32,
         )
-        row = lax.broadcasted_iota(jnp.int32, (rows, own_rows), 0) + first
-        column = lax.broadcasted_iota(jnp.int32, (rows, own_rows), 1)
-        own = jnp.where(column <= row, scores[:, cross:], -1e30)
+        own = jnp.where(allowed, scores[:, cross:], -1e30)
         free = scores[:, :cross]
         largest = jnp.maximum(
             jnp.max(free, axis=1, keepdims=True), jnp.max(own, axis=1, keepdims=True)
@@ -231,36 +239,25 @@
         ) + jnp.dot(
             own.astype(jnp.bfloat16), values_all[cross:, :], preferred_element_type=jnp.float32
         )
-        position = lax.broadcasted_iota(jnp.int32, (rows, head), 0) + first
-        mixed = jnp.where(position < length_ref[0], mixed / total, 0.0)
-        o_ref[:, step * head : (step + 1) * head] = mixed.astype(jnp.bfloat16)
-
-
-def attention(place, rows, heads, lengths, queries, own, others):
+        mixed = jnp.where(kept, mixed / total, 0.0).astype(jnp.bfloat16)
+        for index, lane in enumerate(lanes):
+            o_ref[:, lane] = mixed[index * rows : (index + 1) * rows, :]
+
+
+def attention(place, rows, lengths, queries, own, others):
     n_parts = len(own)
     part_rows, width = queries[0].shape
     head = own[0].shape[1] // 2
     picks = others[0].shape[0]
     reach = n_parts * part_rows + len(others) * picks
-    per_step = 2
-    per_part = part_rows // rows
-
-    def query_spec(step, part):
-        def place_of(i, p, h, n):
-            at = jnp.clip(p[0] - part * per_part, 0, per_part - 1)
-            return (at, h[per_step * i + step])
-
-        return pl.BlockSpec((rows, head), place_of)
-
+    stack = 512 // rows
     return pl.pallas_call(
-        functools.partial(attention_kernel, n_parts, len(others), per_step),
+        functools.partial(attention_kernel, n_parts, len(others), stack),
         grid_spec=pltpu.PrefetchScalarGridSpec(
-            num_scalar_prefetch=3,
-            grid=(width // head // per_step,),
-            in_specs=[query_spec(s, p) for s in range(per_step) for p in range(n_parts)]
-            + [whole(part_rows, 2 * head) for _ in own]
-            + [whole(picks, 2 * head) for _ in others],
-            out_specs=pl.BlockSpec((rows, per_step * head), lambda i, p, h, n: (0, i)),
+            num_scalar_prefetch=2,
+            grid=(1,),
+            in_specs=[whole(*array.shape) for array in (*queries, *own, *others)],
+            out_specs=whole(rows, width),
             scratch_shapes=[
                 pltpu.VMEM((reach, head), jnp.bfloat16),
                 pltpu.VMEM((reach, head), jnp.bfloat16),
@@ -269,39 +266,31 @@
         out_shape=jax.ShapeDtypeStruct((rows, width), jnp.bfloat16),
         compiler_params=params(),
         name="attention",
-    )(place, heads, lengths, *(q for _ in range(per_step) for q in queries), *own, *others)
-
-
-def mix_kernel(own_ref, sent_ref, w_ref, *refs):
-    pieces, out_ref = refs[:-1], refs[-1]
-    sent_w = jnp.concatenate([ref[...] for ref in pieces], axis=0)
+    )(place, lengths, *queries, *own, *others)
+
+
+def mix_kernel(own_ref, w_ref, out_ref):
     total = jnp.dot(own_ref[...], w_ref[...], preferred_element_type=jnp.float32)
-    total = total + jnp.dot(sent_ref[...], sent_w, preferred_element_type=jnp.float32)
     out_ref[...] = total.astype(out_ref.dtype)
 
 
-def mix(own, sent, w_own, pieces, tile, dtype):
-    rows, depth = own.shape
-    width = w_own.shape[1]
-    column = lambda height: pl.BlockSpec((height, tile), lambda i: (0, i))
+def mix(attended, w_out, first, tiles, tile):
+    rows, depth = attended.shape
     return pl.pallas_call(
         mix_kernel,
-        grid=(width // tile,),
-        in_specs=[whole(rows, depth), whole(rows, depth), column(depth)]
-        + [column(piece.shape[0]) for piece in pieces],
-        out_specs=column(rows),
-        out_shape=jax.ShapeDtypeStruct((rows, width), dtype),
+        grid=(tiles,),
+        in_specs=[whole(rows, depth), pl.BlockSpec((depth, tile), lambda i: (0, i + first))],
+        out_specs=pl.BlockSpec((rows, tile), lambda i: (0, i)),
+        out_shape=jax.ShapeDtypeStruct((rows, tiles * tile), jnp.bfloat16),
         compiler_params=params(),
         name="mix",
-    )(own, sent, w_own, *pieces)
+    )(attended, w_out)
 
 
 def shards(hidden_in, lengths, summary_pos, w_query, w_key, w_value, w_out, q_gain, k_gain):
     rows_here = hidden_in.shape[0]
     head_width = q_gain.shape[0]
-    heads_here = w_query.shape[1] // head_width
     place = lax.axis_index("tensor")
-    cand = lax.axis_index("cand")
     n_cand = lax.axis_size("cand")
     assert lax.axis_size("tensor") == 4 and w_key.shape[1] == head_width
 
@@ -321,7 +310,6 @@
         return lax.ppermute(array, "cand", [(i, i ^ offset) for i in range(n_cand)])
 
     low = place < 2
-    inner = (place == 1) | (place == 2)
     near = jnp.bitwise_xor(place, 1)
     third = jnp.where(low, 2, 1)
     last = jnp.where(low, 3, 0)
@@ -331,36 +319,22 @@
     cosine, sine = rope_tables(rows_here, head_width)
     half = rows_here // 2
 
-    from_near, from_mid = lax.optimization_barrier((swap(hidden_in), across(hidden_in)))
+    def project(accs, block, arrivals):
+        return (
+            partial_projection(index(block), [arrivals], w_kv, accs[0], 2 * head_width),
+            partial_projection(index(block), [arrivals], w_query, accs[1], 4 * head_width),
+        )
+
+    from_near, from_mid = swap(hidden_in), across(hidden_in)
+    accs = project((None, None), place, [hidden_in])
+    from_near, from_mid, accs = lax.optimization_barrier((from_near, from_mid, accs))
     to_outer = outward(from_mid)
     to_inner = [across(lax.slice_in_dim(from_near, i * half, (i + 1) * half)) for i in (0, 1)]
+    accs = project(accs, near, [from_near])
+    to_inner[0], accs = lax.optimization_barrier((to_inner[0], accs))
     end = [outward(array) for array in to_inner]
-
-    share = w_out.shape[0] // n_cand
-    spread = n_cand == 8 and share == head_width
-
-    def eighth(offset, cue):
-        start = jnp.bitwise_xor(cand, offset) * share
-        piece = lax.dynamic_slice_in_dim(w_out, start, share, 0)
-        return inward(after(piece, cue))
-
-    if spread:
-        pieces = {0: eighth(0, from_near), 6: eighth(6, to_inner[0])}
-        pieces[2], pieces[4] = between(pieces[0], 2), between(pieces[0], 4)
-        pieces[1] = between(after(pieces[0], end[0]), 1)
-        moved = jnp.bitwise_xor(cand, jnp.array(OFFSETS, jnp.int32))
-        heads = jnp.where(inner, jnp.arange(heads_here, dtype=jnp.int32), moved)
-    else:
-        pieces = {0: lax.all_gather(eighth(0, from_near), "cand", axis=0, tiled=True)}
-        heads = jnp.arange(heads_here, dtype=jnp.int32)
-
-    steps = [(place, [[hidden_in]]), (near, [[from_near]])]
-    steps.append((third, [[from_mid, to_outer]]))
-    acc_q = acc_kv = None
-    for block, parts in steps:
-        acc_kv = partial_projection(index(block), parts, w_kv, acc_kv, 2 * head_width)
-        acc_q = partial_projection(index(block), parts, w_query, acc_q, 4 * head_width)
-    acc_kv, acc_q = lax.optimization_barrier((acc_kv, acc_q))
+    accs = project(accs, third, [from_mid, to_outer])
+    acc_kv, acc_q = lax.optimization_barrier(accs)
 
     final = [[a, b] for a, b in zip(to_inner, end)]
     tables = (cosine, sine)
@@ -372,43 +346,41 @@
         index(last), final[1], 1, w_kv, acc_kv, k_gain, *tables, [own_first], summary_pos.reshape(-1, 1)
     )
     own = [own_first, own_second]
-    summary, pieces = lax.optimization_barrier((summary, pieces))
     others = [between(summary, offset) for offset in range(1, n_cand)]
     second_queries = queries_of(index(last), final[1], 1, w_query, acc_q, q_gain, *tables)
     queries = [first_queries, second_queries]
-    if spread:
-        for offset in (6, 2, 4):
-            pieces[offset ^ 1] = between(after(pieces[offset], (others, second_queries)), 1)
-        pieces = [pieces[offset] for offset in OFFSETS]
-    else:
-        pieces = list(pieces.values())
 
     part = rows_here // 4
-    columns = w_out.shape[1]
-    tile = columns // 10
+    tiles = 5
+    tile = w_out.shape[1] // (2 * tiles)
 
     def attend(where, rows):
-        attended = attention(index(where), rows, heads, lengths, queries, own, others)
-        return attended, inward(attended)
-
-    def mixed(rows, dtype):
-        return mix(*rows, w_out, pieces, columns // 10, dtype)
-
-    far_rows = attend(last, part)
-    third_rows = attend(after(third, far_rows[0]), part)
-    far_rows = (after(far_rows[0], third_rows[0]), far_rows[1])
-    far = mixed(far_rows, jnp.bfloat16)
-    third_rows = (after(third_rows[0], far), third_rows[1])
-    far_inner = mixed(third_rows, jnp.bfloat16)
-    rest_rows = attend(after(place // 2, far_inner), 2 * part)
-    far, far_inner = across(far), across(far_inner)
-    rest = mixed(rest_rows, jnp.float32)
-    outer_at = jnp.where(low, 0, part)
-    outer_rest = lax.dynamic_slice_in_dim(rest, outer_at, part, 0)
-    inner_rest = lax.dynamic_slice_in_dim(rest, part - outer_at, part, 0)
-    sent = outward((outer_rest + far).astype(jnp.bfloat16))
-    kept = (inner_rest + far_inner).astype(jnp.bfloat16)
-    return jnp.where(inner, kept, sent)
+        return attention(index(where), rows, lengths, queries, own, others)
+
+    def mixed(rows):
+        return [mix(rows, w_out, first, tiles, tile) for first in (0, tiles)]
+
+    def added(*arrays):
+        total = arrays[0].astype(jnp.float32)
+        for array in arrays[1:]:
+            total = total + array.astype(jnp.float32)
+        return total.astype(jnp.bfloat16)
+
+    far = mixed(attend(last, part))
+    third_rows = attend(after(third, far), part)
+    mid = mixed(third_rows)
+    rest_rows = attend(after(place // 2, mid), 2 * part)
+    far_in, mid_in = [inward(a) for a in far], [inward(a) for a in mid]
+    outer_first = lax.rem(near, 2) * part
+    neighbour = mixed(lax.dynamic_slice_in_dim(rest_rows, outer_first, part, 0))
+    kept = mixed(lax.dynamic_slice_in_dim(rest_rows, part - outer_first, part, 0))
+    result = []
+    for i in (0, 1):
+        far_sum = across(added(far[i], far_in[i]))
+        mid_sum = across(added(mid[i], mid_in[i]))
+        near_sum = swap(added(neighbour[i], far_sum))
+        result.append(added(kept[i], near_sum, mid_sum))
+    return jnp.concatenate(result, axis=1)
 
 
 def solution(mesh):

time: 260 us -> 216 us (0.83)
  Pallas kernels: 77.2 us -> 52.8 us
  waiting for transfers between devices: 93.7 us -> 73.6 us
  local copies, waits for them, and re-layouts: 14.6 us -> 31.9 us
  starting transfers between devices: 64.4 us -> 49.6 us
  other arithmetic: 7.27 us -> 3.78 us
    ppermute x4 -> x3, waiting for transfers between devices: 54.3 us -> 19.9 us  [outward(): return lax.ppermute(array, 'tensor', [(1, 0), (2, 3)])]
    ppermute x5 -> x4, starting transfers between devices: 40.5 us -> 9.38 us  [inward(): return lax.ppermute(array, 'tensor', [(0, 1), (3, 2)])]
    pallas_call x3 -> x8, Pallas kernels: 37.2 us -> 16.5 us  [mix(): pl.pallas_call(mix_kernel, grid=(tiles,), in_specs=[whole(rows, depth), p...]
    ppermute x1 -> x3, starting transfers between devices: 3.02 us -> 21.9 us  [swap(): return lax.ppermute(array, 'tensor', [(0, 1), (1, 0), (2, 3), (3, 2)])]
    unnamed x67 -> x93, local copies, waits for them, and re-layouts: 11.1 us -> 29 us
    ppermute x5 -> x4, waiting for transfers between devices: 13.4 us -> 22.9 us  [inward(): return lax.ppermute(array, 'tensor', [(0, 1), (3, 2)])]
    pallas_call x3, Pallas kernels: 17.8 us -> 11 us  [attention(): pl.pallas_call(functools.partial(attention_kernel, n_parts, len(others),...]
    ppermute x1 -> x3, waiting for transfers between devices: 24.3 us -> 30.7 us  [swap(): return lax.ppermute(array, 'tensor', [(0, 1), (1, 0), (2, 3), (3, 2)])]
  transfers between devices with their start and end apart: 28 -> 24, of which waited for: 8 -> 8; matrix products, arithmetic and copies ran while one was open for 3% -> 3% of each run, Pallas kernels for 25% -> 21%
where the time goes in v3:
time: 216 us; the launch traced here: 213 us
  waiting for transfers between devices  73.6 us (34%)
  Pallas kernels  52.8 us (24%)
  starting transfers between devices  49.6 us (23%)
  local copies, waits for them, and re-layouts  31.9 us (15%)
  other arithmetic  3.78 us (2%)
    ppermute x3, waiting for transfers between devices, swap(): return lax.ppermute(array, 'tensor', [(0, 1), (1, 0), (2, 3), (3, 2)])  30.7 us
    unnamed x93, local copies, waits for them, and re-layouts  29 us
    ppermute x4, waiting for transfers between devices, inward(): return lax.ppermute(array, 'tensor', [(0, 1), (3, 2)])  22.9 us
    ppermute x3, starting transfers between devices, swap(): return lax.ppermute(array, 'tensor', [(0, 1), (1, 0), (2, 3), (3, 2)])  21.9 us
    ppermute x3, waiting for transfers between devices, outward(): return lax.ppermute(array, 'tensor', [(1, 0), (2, 3)])  19.9 us
    pallas_call x8, Pallas kernels, mix(): pl.pallas_call(mix_kernel, grid=(tiles,), in_specs=[whole(rows, depth), p...  16.5 us
    pallas_call x6, Pallas kernels, partial_projection(): pl.pallas_call(functools.partial(partial_kernel, [len(part) for part in p...  14.6 us
    pallas_call x3, Pallas kernels, attention(): pl.pallas_call(functools.partial(attention_kernel, n_parts, len(others),...  11 us
  transfers between devices with their start and end apart: 24, of which 8 were waited for; matrix products, arithmetic and copies ran while one was open for 3% of the time, Pallas kernels for 21%

profile of v3, /device:TPU:0, one launch (start us, length us, event | category | flops | bytes accessed | tf_op | source)
XLA Modules:
  0.0 213.2 jit_solution(6284714147290906863)
XLA Ops:
  0.0 3.0 %collective-permute-start = (bf16[512,1280]{1,0:T(8,128)(2,1)}, bf16[512,1280]{1,0:T(8,128)(2,1)}, u32[]{:S(2)}, u32[]{:S(2)}) collective-permute-start(bf16[512,1280]{1,0:T(8,128)(2,1)} %refs_0_.3), channel_id=1, source_target_pairs={{0,1},{1,0},{2,3},{3,2},{4,5},{5,4},{6,7},{7,6},{8,9},{9,8},{10,11... | collective-permute-start | bytes 3932168 | tf_op jit(solution)/shard_map/ppermute | solution.py:298
  3.0 1.8 collective-permute-start.1
  4.8 1.6 constant_dynamic-update-slice_fusion.1
  6.8 1.1 copy-done.14
  7.9 0.5 partial_projection.6.refs_2_
  8.5 4.0 %copy-done.2 = bf16[5120,1024]{1,0:T(8,128)(2,1)S(1)} copy-done((bf16[5120,1024]{1,0:T(8,128)(2,1)S(1)}, bf16[5120,1024]{1,0:T(8,128)(2,1)}, u32[]{:S(2)}) %copy-start.2) | copy-done | bytes 10485784
  12.4 2.0 partial_projection.7.refs_2_
  14.5 17.6 %collective-permute-done.refs_0_ = bf16[512,1280]{1,0:T(8,128)(2,1)} collective-permute-done((bf16[512,1280]{1,0:T(8,128)(2,1)}, bf16[512,1280]{1,0:T(8,128)(2,1)}, u32[]{:S(2)}, u32[]{:S(2)}) %collective-permute-start) | collective-permute-done | bytes 1310752 | tf_op jit(solution)/shard_map/ppermute | solution.py:298
  32.1 1.3 collective-permute-start.4
  33.4 2.4 %fusion.3 = (bf16[256,1280]{1,0:T(8,128)(2,1)}, bf16[256,1280]{1,0:T(8,128)(2,1)}) fusion(bf16[512,1280]{1,0:T(8,128)(2,1)} %collective-permute-done.refs_0_), kind=kLoop, calls=%fused_computation.20 | loop fusion | bytes 2621440 | tf_op jit(solution)/shard_map/slice | solution.py:332
  35.8 1.5 collective-permute-start.2
  37.3 1.5 collective-permute-start.5
  38.8 2.0 partial_projection.8.refs_3_
  40.8 0.8 copy-done.15
  41.6 4.0 %copy-done.3 = bf16[5120,1024]{1,0:T(8,128)(2,1)S(1)} copy-done((bf16[5120,1024]{1,0:T(8,128)(2,1)S(1)}, bf16[5120,1024]{1,0:T(8,128)(2,1)}, u32[]{:S(2)}) %copy-start.3) | copy-done | bytes 10485784
  45.6 3.3 %partial_projection.9.refs_3_ = f32[512,1024]{1,0:T(8,128)S(1)} custom-call(s32[1]{0:T(128)} %bitcast.2.block_ref, bf16[512,1280]{1,0:T(8,128)(2,1)} %collective-permute-done.refs_0_, bf16[5120,1024]{1,0:T(8,128)(2,1)S(1)} %copy-done.3, f32[512,1024]{1,0:T(8,128)S(1)} %copy-done.13), custom_call_target="tpu_custom_call" | custom-call | tf_op jit(solution)/shard_map/partial_projection/pallas_call | solution.py:77
  48.9 1.4 copy-done.10
  50.3 1.3 collective-permute-start.3
  51.6 1.5 collective-permute-start.6
  53.2 1.0 fusion.2
  54.4 13.7 %collective-permute-done.4.refs_1_ = bf16[512,1280]{1,0:T(8,128)(2,1)} collective-permute-done((bf16[512,1280]{1,0:T(8,128)(2,1)}, bf16[512,1280]{1,0:T(8,128)(2,1)}, u32[]{:S(2)}, u32[]{:S(2)}) %collective-permute-start.4) | collective-permute-done | bytes 1310752 | tf_op jit(solution)/shard_map/ppermute | solution.py:304
  68.2 4.0 %copy-done.4 = bf16[5120,1024]{1,0:T(8,128)(2,1)S(1)} copy-done((bf16[5120,1024]{1,0:T(8,128)(2,1)S(1)}, bf16[5120,1024]{1,0:T(8,128)(2,1)}, u32[]{:S(2)}) %copy-start.4) | copy-done | bytes 10485784
  72.1 3.7 %partial_projection.11.refs_3_ = f32[512,1024]{1,0:T(8,128)S(1)} custom-call(s32[1]{0:T(128)} %bitcast.3.block_ref, bf16[512,1280]{1,0:T(8,128)(2,1)} %collective-permute-done.1.refs_0_, bf16[512,1280]{1,0:T(8,128)(2,1)} %collective-permute-done.4.refs_1_, bf16[5120,1024]{1,0:T(8,128)(2,1)S(1)} %copy-done.4, f32[512,1024]{1,0:T(8,128)S(1)} %copy-done.11), custom_call_target="tpu_custom_call" | custom-call | tf_op jit(solution)/shard_map/partial_projection/pallas_call | solution.py:77
  75.9 3.0 %partial_projection.10.refs_3_.refs_5_ = f32[512,256]{1,0:T(8,128)S(1)} custom-call(s32[1]{0:T(128)} %bitcast.3.block_ref, bf16[512,1280]{1,0:T(8,128)(2,1)} %collective-permute-done.1.refs_0_, bf16[512,1280]{1,0:T(8,128)(2,1)} %collective-permute-done.4.refs_1_, bf16[5120,256]{1,0:T(8,128)(2,1)S(1)} %constant_dynamic-update-slice_fusion.refs_1_.refs_2_.refs_4_, ...), custom_call_target="tpu_custom_call" | custom-call | tf_op jit(solution)/shard_map/partial_projection/pallas_call | solution.py:77
  78.9 3.3 %collective-permute-done.3.refs_1_ = bf16[256,1280]{1,0:T(8,128)(2,1)} collective-permute-done((bf16[256,1280]{1,0:T(8,128)(2,1)}, bf16[256,1280]{1,0:T(8,128)(2,1)}, u32[]{:S(2)}, u32[]{:S(2)}) %collective-permute-start.3) | collective-permute-done | bytes 655392 | tf_op jit(solution)/shard_map/ppermute | solution.py:304
  82.2 4.0 %copy-done.5 = bf16[5120,1024]{1,0:T(8,128)(2,1)S(1)} copy-done((bf16[5120,1024]{1,0:T(8,128)(2,1)S(1)}, bf16[5120,1024]{1,0:T(8,128)(2,1)}, u32[]{:S(2)}) %copy-start.5) | copy-done | bytes 10485784
  86.2 3.2 %queries.2.refs_0_ = bf16[256,1024]{1,0:T(8,128)(2,1)S(1)} custom-call(s32[1]{0:T(128)} %bitcast.block_ref.place_ref, bf16[256,1280]{1,0:T(8,128)(2,1)} %collective-permute-done.2.refs_0_, bf16[256,1280]{1,0:T(8,128)(2,1)} %collective-permute-done.3.refs_1_, bf16[5120,1024]{1,0:T(8,128)(2,1)S(1)} %copy-done.5, f32[512,1024]{1,0:T(8,128)S(1)} %partial_projection.11.refs_3_, ...), custom_call_target="tpu_custom_call" | custom-call | tf_op jit(solution)/shard_map/queries/pallas_call | solution.py:166
  89.5 2.1 keys_values.2.refs_0_.refs_2_
  91.6 2.9 %collective-permute-done.6.refs_1_.refs_3_ = bf16[256,1280]{1,0:T(8,128)(2,1)} collective-permute-done((bf16[256,1280]{1,0:T(8,128)(2,1)}, bf16[256,1280]{1,0:T(8,128)(2,1)}, u32[]{:S(2)}, u32[]{:S(2)}) %collective-permute-start.6) | collective-permute-done | bytes 655392 | tf_op jit(solution)/shard_map/ppermute | solution.py:304
  94.5 2.2 %keys_values.3 = (bf16[256,256]{1,0:T(8,128)(2,1)S(1)}, bf16[128,256]{1,0:T(8,128)(2,1)S(1)}) custom-call(s32[1]{0:T(128)} %bitcast.block_ref.place_ref, bf16[256,256]{1,0:T(8,128)(2,1)S(1)} %keys_values.2.refs_0_.refs_2_, s32[128,1]{1,0:T(8,128)S(1)} %copy.10.refs_1_, bf16[256,1280]{1,0:T(8,128)(2,1)} %collective-permute-done.5.refs_0_.refs_2_, ...), custom_call_target="tpu_custom_call" | custom-call | tf_op jit(solution)/shard_map/keys_values/pallas_call | solution.py:137
  96.7 1.6 collective-permute-start.10
  98.3 1.4 collective-permute-start.12
  99.7 1.4 collective-permute-start.13
  101.3 1.5 collective-permute-start.8
  102.8 0.6 collective-permute-start.9
  104.1 3.2 %queries.3.refs_1_ = bf16[256,1024]{1,0:T(8,128)(2,1)S(1)} custom-call(s32[1]{0:T(128)} %bitcast.block_ref.place_ref, bf16[256,1280]{1,0:T(8,128)(2,1)} %collective-permute-done.5.refs_0_.refs_2_, bf16[256,1280]{1,0:T(8,128)(2,1)} %collective-permute-done.6.refs_1_.refs_3_, bf16[5120,1024]{1,0:T(8,128)(2,1)S(1)} %bitcast.14, f32[512,1024]{1,0:T(8,128)S(1)} %copy-done.9, ...), custom_call_target="tpu_custom_call" | custom-call | tf_op jit(solution)/shard_map/queries/pallas_call | solution.py:166
  107.5 3.0 %attention.3.own_ref = bf16[128,1024]{1,0:T(8,128)(2,1)S(1)} custom-call(s32[1]{0:T(128)} %bitcast.block_ref.place_ref, s32[1]{0:T(128)S(6)} %copy.12.length_ref, bf16[256,1024]{1,0:T(8,128)(2,1)S(1)} %queries.2.refs_0_, bf16[256,1024]{1,0:T(8,128)(2,1)S(1)} %queries.3.refs_1_, bf16[256,256]{1,0:T(8,128)(2,1)S(1)} %keys_values.2.refs_0_.refs_2_, ...), custom_call_target="tpu_custom_call" | custom-call | tf_op jit(solution)/shard_map/attention/pallas_call | solution.py:254
  110.5 2.1 mix.8
  112.7 5.4 %collective-permute-start.14 = (bf16[128,2560]{1,0:T(8,128)(2,1)S(1)}, bf16[128,2560]{1,0:T(8,128)(2,1)S(1)}, u32[]{:S(2)}, u32[]{:S(2)}) collective-permute-start(bf16[128,2560]{1,0:T(8,128)(2,1)S(1)} %mix.8), channel_id=1, source_target_pairs={{0,1},{3,2},{4,5},{7,6},{8,9},{11,10},{12,13},{15,14},{16,17},{19,... | collective-permute-start | bytes 1966088 | tf_op jit(solution)/shard_map/ppermute | solution.py:307
  118.1 4.0 %copy-done = bf16[1024,5120]{1,0:T(8,128)(2,1)S(1)} copy-done((bf16[1024,5120]{1,0:T(8,128)(2,1)S(1)}, bf16[1024,5120]{1,0:T(8,128)(2,1)}, u32[]{:S(2)}) %copy-start) | copy-done | bytes 10485784
  122.1 2.1 mix.9
  124.3 3.0 %attention.4.own_ref = bf16[128,1024]{1,0:T(8,128)(2,1)S(1)} custom-call(s32[1]{0:T(128)} %bitcast.7.place_ref, s32[1]{0:T(128)S(6)} %copy.12.length_ref, bf16[256,1024]{1,0:T(8,128)(2,1)S(1)} %queries.2.refs_0_, bf16[256,1024]{1,0:T(8,128)(2,1)S(1)} %queries.3.refs_1_, bf16[256,256]{1,0:T(8,128)(2,1)S(1)} %keys_values.2.refs_0_.refs_2_, ...), custom_call_target="tpu_custom_call" | custom-call | tf_op jit(solution)/shard_map/attention/pallas_call | solution.py:254
  127.3 4.0 %copy-done.1 = bf16[1024,5120]{1,0:T(8,128)(2,1)S(1)} copy-done((bf16[1024,5120]{1,0:T(8,128)(2,1)S(1)}, bf16[1024,5120]{1,0:T(8,128)(2,1)}, u32[]{:S(2)}) %copy-start.1) | copy-done | bytes 10485784
  131.3 2.0 mix.10
  133.3 2.1 mix.11
  135.4 1.3 collective-permute-start.17
  136.7 5.0 %attention.5 = bf16[256,1024]{1,0:T(8,128)(2,1)S(1)} custom-call(s32[1]{0:T(128)} %bitcast.8.place_ref, s32[1]{0:T(128)S(6)} %copy.12.length_ref, bf16[256,1024]{1,0:T(8,128)(2,1)S(1)} %queries.2.refs_0_, bf16[256,1024]{1,0:T(8,128)(2,1)S(1)} %queries.3.refs_1_, bf16[256,256]{1,0:T(8,128)(2,1)S(1)} %keys_values.2.refs_0_.refs_2_, ...), custom_call_target="tpu_custom_call" | custom-call | tf_op jit(solution)/shard_map/attention/pallas_call | solution.py:254
  141.8 2.1 mix.13
  143.9 2.1 mix.15
  146.0 1.3 collective-permute-start.19
  147.3 2.1 mix.12
  149.4 2.1 mix.14
  151.5 1.3 collective-permute-start.22
  153.0 0.7 collective-permute-start.15
  153.9 0.7 collective-permute-start.18
  154.6 9.7 %collective-permute-done.19 = bf16[128,2560]{1,0:T(8,128)(2,1)S(1)} collective-permute-done((bf16[128,2560]{1,0:T(8,128)(2,1)S(1)}, bf16[128,2560]{1,0:T(8,128)(2,1)S(1)}, u32[]{:S(2)}, u32[]{:S(2)}) %collective-permute-start.19) | collective-permute-done | bytes 655392 | tf_op jit(solution)/shard_map/ppermute | solution.py:307
  164.5 0.7 collective-permute-start.20
  165.2 13.2 %collective-permute-done.22 = bf16[128,2560]{1,0:T(8,128)(2,1)S(1)} collective-permute-done((bf16[128,2560]{1,0:T(8,128)(2,1)S(1)}, bf16[128,2560]{1,0:T(8,128)(2,1)S(1)}, u32[]{:S(2)}, u32[]{:S(2)}) %collective-permute-start.22) | collective-permute-done | bytes 655392 | tf_op jit(solution)/shard_map/ppermute | solution.py:307
  178.5 0.7 collective-permute-start.23
  179.4 5.2 %collective-permute-start.16 = (bf16[128,2560]{1,0:T(8,128)(2,1)S(1)}, bf16[128,2560]{1,0:T(8,128)(2,1)S(1)}, u32[]{:S(2)}, u32[]{:S(2)}) collective-permute-start(bf16[128,2560]{1,0:T(8,128)(2,1)S(1)} %add_convert_fusion.6), channel_id=1, source_target_pairs={{0,1},{1,0},{2,3},{3,2},{4,5},{5,4},{6,7},{7,6},{8,9},{9,8},{10,11... | collective-permute-start | bytes 1966088 | tf_op jit(solution)/shard_map/ppermute | solution.py:298
  184.8 13.7 %collective-permute-start.21 = (bf16[128,2560]{1,0:T(8,128)(2,1)S(1)}, bf16[128,2560]{1,0:T(8,128)(2,1)S(1)}, u32[]{:S(2)}, u32[]{:S(2)}) collective-permute-start(bf16[128,2560]{1,0:T(8,128)(2,1)S(1)} %add_convert_fusion.2), channel_id=1, source_target_pairs={{0,1},{1,0},{2,3},{3,2},{4,5},{5,4},{6,7},{7,6},{8,9},{9,8},{10,11... | collective-permute-start | bytes 1966088 | tf_op jit(solution)/shard_map/ppermute | solution.py:298
  198.5 1.1 collective-permute-done.16
  199.8 12.0 %collective-permute-done.21 = bf16[128,2560]{1,0:T(8,128)(2,1)S(1)} collective-permute-done((bf16[128,2560]{1,0:T(8,128)(2,1)S(1)}, bf16[128,2560]{1,0:T(8,128)(2,1)S(1)}, u32[]{:S(2)}, u32[]{:S(2)}) %collective-permute-start.21) | collective-permute-done | bytes 655392 | tf_op jit(solution)/shard_map/ppermute | solution.py:298
  212.1 1.2 pad_maximum_fusion
  (117 shorter events, 2.6 us)
Async XLA Ops:
  0.0 32.1 %collective-permute-start = (bf16[512,1280]{1,0:T(8,128)(2,1)}, bf16[512,1280]{1,0:T(8,128)(2,1)}, u32[]{:S(2)}, u32[]{:S(2)}) collective-permute-start(bf16[512,1280]{1,0:T(8,128)(2,1)} %refs_0_.3), channel_id=1, source_target_pairs={{0,1},{1,0},{2,3},{3,2},{4,5},{5,4},{6,7},{7,6},{8,9},{9,8},{10,11... | collective-permute-start | bytes 3932168 | tf_op jit(solution)/shard_map/ppermute | solution.py:298
  3.0 29.1 %collective-permute-start.1 = (bf16[512,1280]{1,0:T(8,128)(2,1)}, bf16[512,1280]{1,0:T(8,128)(2,1)}, u32[]{:S(2)}, u32[]{:S(2)}) collective-permute-start(bf16[512,1280]{1,0:T(8,128)(2,1)} %refs_0_.3), channel_id=1, source_target_pairs={{1,2},{2,1},{5,6},{6,5},{9,10},{10,9},{13,14},{14,13},{17,18},{18,... | collective-permute-start | bytes 3932168 | tf_op jit(solution)/shard_map/ppermute | solution.py:301
  6.8 69.1 %copy-start.6 = (bf16[5120,256]{1,0:T(8,128)(2,1)}, bf16[5120,256]{1,0:T(8,128)(2,1)S(1)}, u32[]{:S(2)}) copy-start(bf16[5120,256]{1,0:T(8,128)(2,1)S(1)} %constant_dynamic-update-slice_fusion.refs_1_.refs_2_.refs_4_) | copy-start | bytes 7864324
  8.5 4.0 %copy-start.2 = (bf16[5120,1024]{1,0:T(8,128)(2,1)S(1)}, bf16[5120,1024]{1,0:T(8,128)(2,1)}, u32[]{:S(2)}) copy-start(bf16[5120,1024]{1,0:T(8,128)(2,1)} %refs_2_.5) | copy-start | bytes 31457284
  14.5 21.4 %copy-start.12 = (f32[512,1024]{1,0:T(8,128)}, f32[512,1024]{1,0:T(8,128)S(1)}, u32[]{:S(2)}) copy-start(f32[512,1024]{1,0:T(8,128)S(1)} %partial_projection.7.refs_2_) | copy-start | bytes 6291460
  32.1 36.0 %collective-permute-start.4 = (bf16[512,1280]{1,0:T(8,128)(2,1)}, bf16[512,1280]{1,0:T(8,128)(2,1)}, u32[]{:S(2)}, u32[]{:S(2)}) collective-permute-start(bf16[512,1280]{1,0:T(8,128)(2,1)} %collective-permute-done.1.refs_0_), channel_id=1, source_target_pairs={{1,0},{2,3},{5,4},{6,7},{9,8},{10,11},{13,12},{14,15},{17,16},{18,... | collective-permute-start | bytes 3932168 | tf_op jit(solution)/shard_map/ppermute | solution.py:304
  35.8 14.5 %collective-permute-start.2 = (bf16[256,1280]{1,0:T(8,128)(2,1)}, bf16[256,1280]{1,0:T(8,128)(2,1)}, u32[]{:S(2)}, u32[]{:S(2)}) collective-permute-start(bf16[256,1280]{1,0:T(8,128)(2,1)} %get-tuple-element.34), channel_id=1, source_target_pairs={{1,2},{2,1},{5,6},{6,5},{9,10},{10,9},{13,14},{14,13},{17,18},{18,... | collective-permute-start | bytes 1966088 | tf_op jit(solution)/shard_map/ppermute | solution.py:301
  37.3 14.2 %collective-permute-start.5 = (bf16[256,1280]{1,0:T(8,128)(2,1)}, bf16[256,1280]{1,0:T(8,128)(2,1)}, u32[]{:S(2)}, u32[]{:S(2)}) collective-permute-start(bf16[256,1280]{1,0:T(8,128)(2,1)} %get-tuple-element.33), channel_id=1, source_target_pairs={{1,2},{2,1},{5,6},{6,5},{9,10},{10,9},{13,14},{14,13},{17,18},{18,... | collective-permute-start | bytes 1966088 | tf_op jit(solution)/shard_map/ppermute | solution.py:301
  38.8 2.8 %copy-start.13 = (f32[512,1024]{1,0:T(8,128)S(1)}, f32[512,1024]{1,0:T(8,128)}, u32[]{:S(2)}) copy-start(f32[512,1024]{1,0:T(8,128)} %copy-done.12) | copy-start | bytes 6291460
  41.6 4.0 %copy-start.3 = (bf16[5120,1024]{1,0:T(8,128)(2,1)S(1)}, bf16[5120,1024]{1,0:T(8,128)(2,1)}, u32[]{:S(2)}) copy-start(bf16[5120,1024]{1,0:T(8,128)(2,1)} %refs_2_.5) | copy-start | bytes 31457284
  45.6 7.5 %copy-start.36 = (s32[1,128]{1,0:T(1,128)S(1)}, s32[1,128]{1,0:T(1,128)}, u32[]{:S(2)}) copy-start(s32[1,128]{1,0:T(1,128)} %param.11) | copy-start | bytes 1540
  50.3 31.9 %collective-permute-start.3 = (bf16[256,1280]{1,0:T(8,128)(2,1)}, bf16[256,1280]{1,0:T(8,128)(2,1)}, u32[]{:S(2)}, u32[]{:S(2)}) collective-permute-start(bf16[256,1280]{1,0:T(8,128)(2,1)} %collective-permute-done.2.refs_0_), channel_id=1, source_target_pairs={{1,0},{2,3},{5,4},{6,7},{9,8},{10,11},{13,12},{14,15},{17,16},{18,... | collective-permute-start | bytes 1966088 | tf_op jit(solution)/shard_map/ppermute | solution.py:304
  51.6 42.9 %collective-permute-start.6 = (bf16[256,1280]{1,0:T(8,128)(2,1)}, bf16[256,1280]{1,0:T(8,128)(2,1)}, u32[]{:S(2)}, u32[]{:S(2)}) collective-permute-start(bf16[256,1280]{1,0:T(8,128)(2,1)} %collective-permute-done.5.refs_0_.refs_2_), channel_id=1, source_target_pairs={{1,0},{2,3},{5,4},{6,7},{9,8},{10,11},{13,12},{14,15},{17,16},{18,... | collective-permute-start | bytes 1966088 | tf_op jit(solution)/shard_map/ppermute | solution.py:304
  53.2 15.0 %copy-start.11 = (f32[512,1024]{1,0:T(8,128)S(1)}, f32[512,1024]{1,0:T(8,128)}, u32[]{:S(2)}) copy-start(f32[512,1024]{1,0:T(8,128)} %copy-done.10) | copy-start | bytes 6291460
  68.2 4.0 %copy-start.4 = (bf16[5120,1024]{1,0:T(8,128)(2,1)S(1)}, bf16[5120,1024]{1,0:T(8,128)(2,1)}, u32[]{:S(2)}) copy-start(bf16[5120,1024]{1,0:T(8,128)(2,1)} %refs_2_.5) | copy-start | bytes 31457284
  72.1 3.8 %copy-start.16 = (f32[512,256]{1,0:T(8,128)S(1)}, f32[512,256]{1,0:T(8,128)}, u32[]{:S(2)}) copy-start(f32[512,256]{1,0:T(8,128)} %copy-done.15) | copy-start | bytes 1572868
  75.9 6.3 %copy-start.8 = (f32[512,1024]{1,0:T(8,128)}, f32[512,1024]{1,0:T(8,128)S(1)}, u32[]{:S(2)}) copy-start(f32[512,1024]{1,0:T(8,128)S(1)} %partial_projection.11.refs_3_) | copy-start | bytes 6291460
  75.9 6.3 %copy-start.34 = (f32[128]{0:T(128)S(1)}, f32[128]{0:T(128)}, u32[]{:S(2)}) copy-start(f32[128]{0:T(128)} %param.16) | copy-start | bytes 1540
  82.2 4.0 %copy-start.5 = (bf16[5120,1024]{1,0:T(8,128)(2,1)S(1)}, bf16[5120,1024]{1,0:T(8,128)(2,1)}, u32[]{:S(2)}) copy-start(bf16[5120,1024]{1,0:T(8,128)(2,1)} %refs_2_.5) | copy-start | bytes 31457284
  86.2 3.3 %copy-start.7 = (bf16[5120,256]{1,0:T(8,128)(2,1)S(1)}, bf16[5120,256]{1,0:T(8,128)(2,1)}, u32[]{:S(2)}) copy-start(bf16[5120,256]{1,0:T(8,128)(2,1)} %copy-done.6) | copy-start | bytes 7864324
  86.2 3.3 %copy-start.33 = (f32[128]{0:T(128)S(1)}, f32[128]{0:T(128)}, u32[]{:S(2)}) copy-start(f32[128]{0:T(128)} %param.17) | copy-start | bytes 1540
  86.2 17.9 %slice-start.6 = ((s8[10485760]{0:T(1024)(128)(4,1)}), s8[4194304]{0:T(1024)(128)(4,1)S(1)}, s32[]{:S(2)}) async-start(s8[10485760]{0:T(1024)(128)(4,1)} %bitcast.13), calls=%async_computation.6 | async-start | bytes 8388608
  86.2 17.9 %slice-start.7 = ((s8[10485760]{0:T(1024)(128)(4,1)}), s8[4194304]{0:T(1024)(128)(4,1)S(1)}, s32[]{:S(2)}) async-start(s8[10485760]{0:T(1024)(128)(4,1)} %bitcast.13), calls=%async_computation.7 | async-start | bytes 8388608
  89.5 14.6 %slice-start.8 = ((s8[10485760]{0:T(1024)(128)(4,1)}), s8[2097152]{0:T(1024)(128)(4,1)S(1)}, s32[]{:S(2)}) async-start(s8[10485760]{0:T(1024)(128)(4,1)} %bitcast.13), calls=%async_computation.8 | async-start | bytes 4194304
  91.6 12.5 %copy-start.9 = (f32[512,1024]{1,0:T(8,128)S(1)}, f32[512,1024]{1,0:T(8,128)}, u32[]{:S(2)}) copy-start(f32[512,1024]{1,0:T(8,128)} %copy-done.8) | copy-start | bytes 6291460
  94.5 16.1 %slice-start = ((s8[10485760]{0:T(1024)(128)(4,1)}), s8[4194304]{0:T(1024)(128)(4,1)S(1)}, s32[]{:S(2)}) async-start(s8[10485760]{0:T(1024)(128)(4,1)} %bitcast.9), calls=%async_computation | async-start | bytes 8388608
  96.7 10.8 %copy-start.17 = (bf16[256,256]{1,0:T(8,128)(2,1)}, bf16[256,256]{1,0:T(8,128)(2,1)S(1)}, u32[]{:S(2)}) copy-start(bf16[256,256]{1,0:T(8,128)(2,1)S(1)} %get-tuple-element.29.refs_3_) | copy-start | bytes 393220
  96.7 4.6 %collective-permute-start.10 = (bf16[128,256]{1,0:T(8,128)(2,1)S(1)}, bf16[128,256]{1,0:T(8,128)(2,1)S(1)}, u32[]{:S(2)}, u32[]{:S(2)}) collective-permute-start(bf16[128,256]{1,0:T(8,128)(2,1)S(1)} %get-tuple-element.30), channel_id=1, source_target_pairs={{0,16},{4,20},{8,24},{12,28},{16,0},{20,4},{24,8},{28,12},{1,17},{... | collective-permute-start | bytes 196616 | tf_op jit(solution)/shard_map/ppermute | solution.py:310
  98.3 4.6 %collective-permute-start.11 = (bf16[128,256]{1,0:T(8,128)(2,1)S(1)}, bf16[128,256]{1,0:T(8,128)(2,1)S(1)}, u32[]{:S(2)}, u32[]{:S(2)}) collective-permute-start(bf16[128,256]{1,0:T(8,128)(2,1)S(1)} %get-tuple-element.30), channel_id=1, source_target_pairs={{0,20},{4,16},{8,28},{12,24},{16,4},{20,0},{24,12},{28,8},{1,21},{... | collective-permute-start | bytes 196616 | tf_op jit(solution)/shard_map/ppermute | solution.py:310
  98.3 9.1 %collective-permute-start.12 = (bf16[128,256]{1,0:T(8,128)(2,1)S(1)}, bf16[128,256]{1,0:T(8,128)(2,1)S(1)}, u32[]{:S(2)}, u32[]{:S(2)}) collective-permute-start(bf16[128,256]{1,0:T(8,128)(2,1)S(1)} %get-tuple-element.30), channel_id=1, source_target_pairs={{0,24},{4,28},{8,16},{12,20},{16,8},{20,12},{24,0},{28,4},{1,25},{... | collective-permute-start | bytes 196616 | tf_op jit(solution)/shard_map/ppermute | solution.py:310
  99.7 7.7 %collective-permute-start.13 = (bf16[128,256]{1,0:T(8,128)(2,1)S(1)}, bf16[128,256]{1,0:T(8,128)(2,1)S(1)}, u32[]{:S(2)}, u32[]{:S(2)}) collective-permute-start(bf16[128,256]{1,0:T(8,128)(2,1)S(1)} %get-tuple-element.30), channel_id=1, source_target_pairs={{0,28},{4,24},{8,20},{12,16},{16,12},{20,8},{24,4},{28,0},{1,29},{... | collective-permute-start | bytes 196616 | tf_op jit(solution)/shard_map/ppermute | solution.py:310
  101.1 6.3 %collective-permute-start.7 = (bf16[128,256]{1,0:T(8,128)(2,1)S(1)}, bf16[128,256]{1,0:T(8,128)(2,1)S(1)}, u32[]{:S(2)}, u32[]{:S(2)}) collective-permute-start(bf16[128,256]{1,0:T(8,128)(2,1)S(1)} %get-tuple-element.30), channel_id=1, source_target_pairs={{0,4},{4,0},{8,12},{12,8},{16,20},{20,16},{24,28},{28,24},{1,5},{5... | collective-permute-start | bytes 196616 | tf_op jit(solution)/shard_map/ppermute | solution.py:310
  101.3 6.2 %copy-start.19 = (bf16[128,256]{1,0:T(8,128)(2,1)}, bf16[128,256]{1,0:T(8,128)(2,1)S(1)}, u32[]{:S(2)}) copy-start(bf16[128,256]{1,0:T(8,128)(2,1)S(1)} %collective-permute-done.10.refs_7_) | copy-start | bytes 196612
  101.3 6.1 %collective-permute-start.8 = (bf16[128,256]{1,0:T(8,128)(2,1)S(1)}, bf16[128,256]{1,0:T(8,128)(2,1)S(1)}, u32[]{:S(2)}, u32[]{:S(2)}) collective-permute-start(bf16[128,256]{1,0:T(8,128)(2,1)S(1)} %get-tuple-element.30), channel_id=1, source_target_pairs={{0,8},{4,12},{8,0},{12,4},{16,24},{20,28},{24,16},{28,20},{1,9},{5... | collective-permute-start | bytes 196616 | tf_op jit(solution)/shard_map/ppermute | solution.py:310
  102.8 4.7 %copy-start.21 = (bf16[128,256]{1,0:T(8,128)(2,1)}, bf16[128,256]{1,0:T(8,128)(2,1)S(1)}, u32[]{:S(2)}) copy-start(bf16[128,256]{1,0:T(8,128)(2,1)S(1)} %collective-permute-done.11.refs_8_) | copy-start | bytes 196612
  102.8 4.6 %collective-permute-start.9 = (bf16[128,256]{1,0:T(8,128)(2,1)S(1)}, bf16[128,256]{1,0:T(8,128)(2,1)S(1)}, u32[]{:S(2)}, u32[]{:S(2)}) collective-permute-start(bf16[128,256]{1,0:T(8,128)(2,1)S(1)} %get-tuple-element.30), channel_id=1, source_target_pairs={{0,12},{4,8},{8,4},{12,0},{16,28},{20,24},{24,20},{28,16},{1,13},{... | collective-permute-start | bytes 196616 | tf_op jit(solution)/shard_map/ppermute | solution.py:310
  104.1 6.4 %slice-start.1 = ((s8[10485760]{0:T(1024)(128)(4,1)}), s8[4194304]{0:T(1024)(128)(4,1)S(1)}, s32[]{:S(2)}) async-start(s8[10485760]{0:T(1024)(128)(4,1)} %bitcast.9), calls=%async_computation.1 | async-start | bytes 8388608
  104.1 6.4 %slice-start.2 = ((s8[10485760]{0:T(1024)(128)(4,1)}), s8[2097152]{0:T(1024)(128)(4,1)S(1)}, s32[]{:S(2)}) async-start(s8[10485760]{0:T(1024)(128)(4,1)} %bitcast.9), calls=%async_computation.2 | async-start | bytes 4194304
  107.4 5.2 %copy-start.23 = (bf16[128,256]{1,0:T(8,128)(2,1)}, bf16[128,256]{1,0:T(8,128)(2,1)S(1)}, u32[]{:S(2)}) copy-start(bf16[128,256]{1,0:T(8,128)(2,1)S(1)} %collective-permute-done.12.refs_9_) | copy-start | bytes 196612
  107.4 5.2 %copy-start.25 = (bf16[128,256]{1,0:T(8,128)(2,1)}, bf16[128,256]{1,0:T(8,128)(2,1)S(1)}, u32[]{:S(2)}) copy-start(bf16[128,256]{1,0:T(8,128)(2,1)S(1)} %collective-permute-done.13.refs_10_) | copy-start | bytes 196612
  107.4 5.2 %copy-start.27 = (bf16[128,256]{1,0:T(8,128)(2,1)}, bf16[128,256]{1,0:T(8,128)(2,1)S(1)}, u32[]{:S(2)}) copy-start(bf16[128,256]{1,0:T(8,128)(2,1)S(1)} %collective-permute-done.7.refs_4_) | copy-start | bytes 196612
  107.4 5.2 %copy-start.29 = (bf16[128,256]{1,0:T(8,128)(2,1)}, bf16[128,256]{1,0:T(8,128)(2,1)S(1)}, u32[]{:S(2)}) copy-start(bf16[128,256]{1,0:T(8,128)(2,1)S(1)} %collective-permute-done.8.refs_5_) | copy-start | bytes 196612
  107.5 5.2 %copy-start.31 = (bf16[128,256]{1,0:T(8,128)(2,1)}, bf16[128,256]{1,0:T(8,128)(2,1)S(1)}, u32[]{:S(2)}) copy-start(bf16[128,256]{1,0:T(8,128)(2,1)S(1)} %collective-permute-done.9.refs_6_) | copy-start | bytes 196612
  112.7 40.2 %collective-permute-start.14 = (bf16[128,2560]{1,0:T(8,128)(2,1)S(1)}, bf16[128,2560]{1,0:T(8,128)(2,1)S(1)}, u32[]{:S(2)}, u32[]{:S(2)}) collective-permute-start(bf16[128,2560]{1,0:T(8,128)(2,1)S(1)} %mix.8), channel_id=1, source_target_pairs={{0,1},{3,2},{4,5},{7,6},{8,9},{11,10},{12,13},{15,14},{16,17},{19,... | collective-permute-start | bytes 1966088 | tf_op jit(solution)/shard_map/ppermute | solution.py:307
  118.1 4.0 %copy-start = (bf16[1024,5120]{1,0:T(8,128)(2,1)S(1)}, bf16[1024,5120]{1,0:T(8,128)(2,1)}, u32[]{:S(2)}) copy-start(bf16[1024,5120]{1,0:T(8,128)(2,1)} %w_ref.15) | copy-start | bytes 31457284
  122.1 2.2 %copy-start.22 = (bf16[128,256]{1,0:T(8,128)(2,1)S(1)}, bf16[128,256]{1,0:T(8,128)(2,1)}, u32[]{:S(2)}) copy-start(bf16[128,256]{1,0:T(8,128)(2,1)} %copy-done.21) | copy-start | bytes 196612
  122.1 2.2 %copy-start.24 = (bf16[128,256]{1,0:T(8,128)(2,1)S(1)}, bf16[128,256]{1,0:T(8,128)(2,1)}, u32[]{:S(2)}) copy-start(bf16[128,256]{1,0:T(8,128)(2,1)} %copy-done.23) | copy-start | bytes 196612
  122.1 2.2 %copy-start.26 = (bf16[128,256]{1,0:T(8,128)(2,1)S(1)}, bf16[128,256]{1,0:T(8,128)(2,1)}, u32[]{:S(2)}) copy-start(bf16[128,256]{1,0:T(8,128)(2,1)} %copy-done.25) | copy-start | bytes 196612
  122.1 2.2 %copy-start.28 = (bf16[128,256]{1,0:T(8,128)(2,1)S(1)}, bf16[128,256]{1,0:T(8,128)(2,1)}, u32[]{:S(2)}) copy-start(bf16[128,256]{1,0:T(8,128)(2,1)} %copy-done.27) | copy-start | bytes 196612
  122.1 2.2 %copy-start.30 = (bf16[128,256]{1,0:T(8,128)(2,1)S(1)}, bf16[128,256]{1,0:T(8,128)(2,1)}, u32[]{:S(2)}) copy-start(bf16[128,256]{1,0:T(8,128)(2,1)} %copy-done.29) | copy-start | bytes 196612
  122.1 2.2 %copy-start.32 = (bf16[128,256]{1,0:T(8,128)(2,1)S(1)}, bf16[128,256]{1,0:T(8,128)(2,1)}, u32[]{:S(2)}) copy-start(bf16[128,256]{1,0:T(8,128)(2,1)} %copy-done.31) | copy-start | bytes 196612
  127.3 4.0 %copy-start.1 = (bf16[1024,5120]{1,0:T(8,128)(2,1)S(1)}, bf16[1024,5120]{1,0:T(8,128)(2,1)}, u32[]{:S(2)}) copy-start(bf16[1024,5120]{1,0:T(8,128)(2,1)} %w_ref.15) | copy-start | bytes 31457284
  131.3 10.6 %slice-start.3 = ((s8[10485760]{0:T(1024)(128)(4,1)}), s8[4194304]{0:T(1024)(128)(4,1)S(1)}, s32[]{:S(2)}) async-start(s8[10485760]{0:T(1024)(128)(4,1)} %bitcast.11), calls=%async_computation.3 | async-start | bytes 8388608
  131.3 10.6 %slice-start.4 = ((s8[10485760]{0:T(1024)(128)(4,1)}), s8[4194304]{0:T(1024)(128)(4,1)S(1)}, s32[]{:S(2)}) async-start(s8[10485760]{0:T(1024)(128)(4,1)} %bitcast.11), calls=%async_computation.4 | async-start | bytes 8388608
  133.3 8.5 %slice-start.5 = ((s8[10485760]{0:T(1024)(128)(4,1)}), s8[2097152]{0:T(1024)(128)(4,1)S(1)}, s32[]{:S(2)}) async-start(s8[10485760]{0:T(1024)(128)(4,1)} %bitcast.11), calls=%async_computation.5 | async-start | bytes 4194304
  135.4 18.3 %collective-permute-start.17 = (bf16[128,2560]{1,0:T(8,128)(2,1)S(1)}, bf16[128,2560]{1,0:T(8,128)(2,1)S(1)}, u32[]{:S(2)}, u32[]{:S(2)}) collective-permute-start(bf16[128,2560]{1,0:T(8,128)(2,1)S(1)} %mix.10), channel_id=1, source_target_pairs={{0,1},{3,2},{4,5},{7,6},{8,9},{11,10},{12,13},{15,14},{16,17},{19,... | collective-permute-start | bytes 1966088 | tf_op jit(solution)/shard_map/ppermute | solution.py:307
  146.0 18.3 %collective-permute-start.19 = (bf16[128,2560]{1,0:T(8,128)(2,1)S(1)}, bf16[128,2560]{1,0:T(8,128)(2,1)S(1)}, u32[]{:S(2)}, u32[]{:S(2)}) collective-permute-start(bf16[128,2560]{1,0:T(8,128)(2,1)S(1)} %mix.9), channel_id=1, source_target_pairs={{0,1},{3,2},{4,5},{7,6},{8,9},{11,10},{12,13},{15,14},{16,17},{19,... | collective-permute-start | bytes 1966088 | tf_op jit(solution)/shard_map/ppermute | solution.py:307
  151.5 26.9 %collective-permute-start.22 = (bf16[128,2560]{1,0:T(8,128)(2,1)S(1)}, bf16[128,2560]{1,0:T(8,128)(2,1)S(1)}, u32[]{:S(2)}, u32[]{:S(2)}) collective-permute-start(bf16[128,2560]{1,0:T(8,128)(2,1)S(1)} %mix.11), channel_id=1, source_target_pairs={{0,1},{3,2},{4,5},{7,6},{8,9},{11,10},{12,13},{15,14},{16,17},{19,... | collective-permute-start | bytes 1966088 | tf_op jit(solution)/shard_map/ppermute | solution.py:307
  153.0 26.2 %collective-permute-start.15 = (bf16[128,2560]{1,0:T(8,128)(2,1)S(1)}, bf16[128,2560]{1,0:T(8,128)(2,1)S(1)}, u32[]{:S(2)}, u32[]{:S(2)}) collective-permute-start(bf16[128,2560]{1,0:T(8,128)(2,1)S(1)} %add_convert_fusion.7), channel_id=1, source_target_pairs={{1,2},{2,1},{5,6},{6,5},{9,10},{10,9},{13,14},{14,13},{17,18},{18,... | collective-permute-start | bytes 1966088 | tf_op jit(solution)/shard_map/ppermute | solution.py:301
  153.9 44.6 %collective-permute-start.18 = (bf16[128,2560]{1,0:T(8,128)(2,1)S(1)}, bf16[128,2560]{1,0:T(8,128)(2,1)S(1)}, u32[]{:S(2)}, u32[]{:S(2)}) collective-permute-start(bf16[128,2560]{1,0:T(8,128)(2,1)S(1)} %add_convert_fusion.5), channel_id=1, source_target_pairs={{1,2},{2,1},{5,6},{6,5},{9,10},{10,9},{13,14},{14,13},{17,18},{18,... | collective-permute-start | bytes 1966088 | tf_op jit(solution)/shard_map/ppermute | solution.py:301
  164.5 20.1 %collective-permute-start.20 = (bf16[128,2560]{1,0:T(8,128)(2,1)S(1)}, bf16[128,2560]{1,0:T(8,128)(2,1)S(1)}, u32[]{:S(2)}, u32[]{:S(2)}) collective-permute-start(bf16[128,2560]{1,0:T(8,128)(2,1)S(1)} %add_convert_fusion.3), channel_id=1, source_target_pairs={{1,2},{2,1},{5,6},{6,5},{9,10},{10,9},{13,14},{14,13},{17,18},{18,... | collective-permute-start | bytes 1966088 | tf_op jit(solution)/shard_map/ppermute | solution.py:301
  178.5 21.3 %collective-permute-start.23 = (bf16[128,2560]{1,0:T(8,128)(2,1)S(1)}, bf16[128,2560]{1,0:T(8,128)(2,1)S(1)}, u32[]{:S(2)}, u32[]{:S(2)}) collective-permute-start(bf16[128,2560]{1,0:T(8,128)(2,1)S(1)} %add_convert_fusion.1), channel_id=1, source_target_pairs={{1,2},{2,1},{5,6},{6,5},{9,10},{10,9},{13,14},{14,13},{17,18},{18,... | collective-permute-start | bytes 1966088 | tf_op jit(solution)/shard_map/ppermute | solution.py:301
  179.4 20.2 %collective-permute-start.16 = (bf16[128,2560]{1,0:T(8,128)(2,1)S(1)}, bf16[128,2560]{1,0:T(8,128)(2,1)S(1)}, u32[]{:S(2)}, u32[]{:S(2)}) collective-permute-start(bf16[128,2560]{1,0:T(8,128)(2,1)S(1)} %add_convert_fusion.6), channel_id=1, source_target_pairs={{0,1},{1,0},{2,3},{3,2},{4,5},{5,4},{6,7},{7,6},{8,9},{9,8},{10,11... | collective-permute-start | bytes 1966088 | tf_op jit(solution)/shard_map/ppermute | solution.py:298
  184.8 27.1 %collective-permute-start.21 = (bf16[128,2560]{1,0:T(8,128)(2,1)S(1)}, bf16[128,2560]{1,0:T(8,128)(2,1)S(1)}, u32[]{:S(2)}, u32[]{:S(2)}) collective-permute-start(bf16[128,2560]{1,0:T(8,128)(2,1)S(1)} %add_convert_fusion.2), channel_id=1, source_target_pairs={{0,1},{1,0},{2,3},{3,2},{4,5},{5,4},{6,7},{7,6},{8,9},{9,8},{10,11... | collective-permute-start | bytes 1966088 | tf_op jit(solution)/shard_map/ppermute | solution.py:298
  (6 other events, 9.6 us)

commit v4 on v3

v4 whole, which is shorter than its diff:
```python
import functools

import jax
import jax.numpy as jnp
import numpy as np
from jax import lax
from jax.experimental import pallas as pl
from jax.experimental.pallas import tpu as pltpu
from jax.sharding import PartitionSpec as P

MIB = 1024 * 1024
LOG2E = 1.4426950408889634
OWN, NEAR, THIRD, LAST = range(4)


def rope_tables(rows, width):
    half_width = width // 2
    frequency = (1000000.0 ** (-(np.arange(half_width) * 2.0 / width))).astype(np.float32)
    angle = np.arange(rows, dtype=np.float32)[:, None] * frequency[None, :]
    angle = angle.astype(np.float64)
    cosine, sine = np.cos(angle), np.sin(angle)
    return (
        jnp.asarray(np.concatenate([cosine, cosine], axis=1).astype(np.float32)),
        jnp.asarray(np.concatenate([-sine, sine], axis=1).astype(np.float32)),
    )


def norm_rope(vectors, gain, cosine, sine):
    scale = lax.rsqrt(jnp.mean(vectors * vectors, axis=-1, keepdims=True) + 1e-06)
    vectors = vectors * scale * gain
    return vectors * cosine + pltpu.roll(vectors, vectors.shape[-1] // 2, 1) * sine


def params(mebibytes):
    return pltpu.CompilerParams(vmem_limit_bytes=mebibytes * MIB)


def cost(flops):
    return pl.CostEstimate(flops=flops, bytes_accessed=1, transcendentals=0)


def after(array, cue):
    return lax.optimization_barrier((array, cue))[0]


def whole(*shape):
    return pl.BlockSpec(shape, lambda *_: (0,) * len(shape))


def summed(refs):
    total = refs[0][...]
    for ref in refs[1:]:
        total = total + ref[...]
    return total


def partial_kernel(counts, with_acc, places_ref, *refs):
    rows = []
    for count in counts:
        rows.append(summed(refs[:count]))
        refs = refs[count:]
    hidden = jnp.concatenate(rows, axis=0) if len(rows) > 1 else rows[0]
    weights, outs = refs[:3], refs[-3:]
    accs = refs[3:6] if with_acc else (None,) * 3
    step = pl.program_id(0)

    def add(w_ref, acc_ref, out_ref):
        product = jnp.dot(hidden, w_ref[...], preferred_element_type=jnp.float32)
        out_ref[...] = product if acc_ref is None else product + acc_ref[...]

    add(weights[0], accs[0], outs[0])

    @pl.when(step == 0)
    def _():
        add(weights[1], accs[1], outs[1])
        add(weights[2], accs[2], outs[2])


def partial_projection(places, slot, parts, weights, accs):
    features = parts[0][0].shape[1]
    rows = sum(part[0].shape[0] for part in parts)
    arrivals = [array for part in parts for array in part]
    widths = [weight.shape[1] for weight in weights]
    tile = 512
    column = lambda height: pl.BlockSpec((height, tile), lambda i, p: (0, i))
    per_array = lambda height: [column(height), whole(height, widths[1]), whole(height, widths[2])]
    block = lambda width: pl.BlockSpec((features, width), lambda i, p: (p[slot], 0))
    in_specs = [whole(*array.shape) for array in arrivals]
    in_specs.append(pl.BlockSpec((features, tile), lambda i, p: (p[slot], i)))
    in_specs += [block(widths[1]), block(widths[2])]
    operands = [*arrivals, *weights]
    if accs is not None:
        in_specs += per_array(rows)
        operands += accs
    return pl.pallas_call(
        functools.partial(partial_kernel, [len(part) for part in parts], accs is not None),
        grid_spec=pltpu.PrefetchScalarGridSpec(
            num_scalar_prefetch=1,
            grid=(widths[0] // tile,),
            in_specs=in_specs,
            out_specs=per_array(rows),
        ),
        out_shape=[jax.ShapeDtypeStruct((rows, width), jnp.float32) for width in widths],
        compiler_params=params(20),
        cost_estimate=cost(1),
        name="partial_projection",
    )(places, *operands)


def keys_values_kernel(count, n_before, places_ref, *refs):
    before, refs = refs[:n_before], refs[n_before:]
    hidden = summed(refs[:count])
    wk_ref, wv_ref, acck_ref, accv_ref, gain_ref, cos_ref, sin_ref = refs[count : count + 7]
    refs = refs[count + 7 :]
    head = gain_ref.shape[1]
    out_ref = refs[0] if n_before == 0 else refs[1]
    keys = acck_ref[...] + jnp.dot(hidden, wk_ref[...], preferred_element_type=jnp.float32)
    values = accv_ref[...] + jnp.dot(hidden, wv_ref[...], preferred_element_type=jnp.float32)
    keys = norm_rope(keys, gain_ref[...], cos_ref[...], sin_ref[...])
    out_ref[:, :head] = keys.astype(jnp.bfloat16)
    out_ref[:, head:] = values.astype(jnp.bfloat16)
    if n_before:
        pos_ref, summary_ref = refs[0], refs[2]
        picks = pos_ref.shape[1]
        picked, start = None, 0
        for ref in (*before, out_ref):
            rows = ref.shape[0]
            row = lax.broadcasted_iota(jnp.int32, (rows, picks), 0) + start
            chosen = jnp.where(row == pos_ref[...], 1.0, 0.0).astype(jnp.bfloat16)
            found = lax.dot_general(
                chosen, ref[...], (((0,), (0,)), ((), ())), preferred_element_type=jnp.float32
            )
            picked = found if picked is None else picked + found
            start += rows
        summary_ref[...] = picked.astype(jnp.bfloat16)


def keys_values(places, hidden, part, weights, accs, gain, cosine, sine, before=(), positions=None):
    rows, features = hidden[0].shape
    head = gain.shape[1]
    row_part = pl.BlockSpec((rows, head), lambda i, p: (part, 0))
    block = pl.BlockSpec((features, head), lambda i, p: (p[LAST], 0))
    in_specs = [whole(*array.shape) for array in (*before, *hidden)]
    in_specs += [block, block, row_part, row_part, whole(1, head), row_part, row_part]
    operands = [*before, *hidden, *weights, *accs, gain, cosine, sine]
    out_shape = [jax.ShapeDtypeStruct((rows, 2 * head), jnp.bfloat16)]
    if before:
        in_specs.append(whole(*positions.shape))
        operands.append(positions)
        out_shape.append(jax.ShapeDtypeStruct((positions.shape[1], 2 * head), jnp.bfloat16))
    return pl.pallas_call(
        functools.partial(keys_values_kernel, len(hidden), len(before)),
        grid_spec=pltpu.PrefetchScalarGridSpec(
            num_scalar_prefetch=1,
            grid=(1,),
            in_specs=in_specs,
            out_specs=[whole(*shape.shape) for shape in out_shape],
        ),
        out_shape=out_shape,
        compiler_params=params(12),
        cost_estimate=cost(1),
        name="keys_values",
    )(places, *operands)


def queries_kernel(count, places_ref, *refs):
    hidden = summed(refs[:count])
    w_ref, acc_ref, gain_ref, cos_ref, sin_ref, q_ref = refs[count:]
    head = gain_ref.shape[1]
    proj = acc_ref[...] + jnp.dot(hidden, w_ref[...], preferred_element_type=jnp.float32)
    for start in range(0, proj.shape[1], head):
        one = norm_rope(proj[:, start : start + head], gain_ref[...], cos_ref[...], sin_ref[...])
        q_ref[:, start : start + head] = one.astype(jnp.bfloat16)


def queries_of(places, hidden, part, weights, acc, gain, cosine, sine):
    rows, features = hidden[0].shape
    head = gain.shape[1]
    width = weights.shape[1]
    tile = 4 * head
    row_part = pl.BlockSpec((rows, head), lambda i, p: (part, 0))
    return pl.pallas_call(
        functools.partial(queries_kernel, len(hidden)),
        grid_spec=pltpu.PrefetchScalarGridSpec(
            num_scalar_prefetch=1,
            grid=(width // tile,),
            in_specs=[whole(rows, features) for _ in hidden]
            + [
                pl.BlockSpec((features, tile), lambda i, p: (p[LAST], i)),
                pl.BlockSpec((rows, tile), lambda i, p: (part, i)),
                whole(1, head),
                row_part,
                row_part,
            ],
            out_specs=pl.BlockSpec((rows, tile), lambda i, p: (0, i)),
        ),
        out_shape=jax.ShapeDtypeStruct((rows, width), jnp.bfloat16),
        compiler_params=params(12),
        cost_estimate=cost(1),
        name="queries",
    )(places, *hidden, weights, acc, gain, cosine, sine)


def attention_kernel(slots, n_parts, n_others, stack, places_ref, length_ref, *refs):
    q_parts, refs = refs[:n_parts], refs[n_parts:]
    own_parts, refs = refs[:n_parts], refs[n_parts:]
    others, refs = refs[:n_others], refs[n_others:]
    o_refs, (keys_all, values_all) = refs[:-2], refs[-2:]
    part_rows, width = own_parts[0].shape
    head = width // 2
    picks = others[0].shape[0]
    cross = n_others * picks
    rows = o_refs[0].shape[0]

    start = 0
    for ref in (*others, *own_parts):
        stop = start + ref.shape[0]
        keys_all[start:stop, :] = ref[:, :head]
        values_all[start:stop, :] = ref[:, head:]
        start = stop

    scale = head ** (-0.5) * LOG2E
    own_rows = n_parts * part_rows
    for slot, o_ref in zip(slots, o_refs):
        first = places_ref[slot] * rows
        offset = pl.multiple_of(lax.rem(first, part_rows), rows)
        row = lax.broadcasted_iota(jnp.int32, (rows, own_rows), 0) + first
        column = lax.broadcasted_iota(jnp.int32, (rows, own_rows), 1)
        allowed = jnp.concatenate([column <= row] * stack, axis=0)
        position = lax.broadcasted_iota(jnp.int32, (rows, head), 0) + first
        kept = jnp.concatenate([position < length_ref[0]] * stack, axis=0)
        for left in range(0, o_ref.shape[1], stack * head):
            lanes = [slice(left + i * head, left + (i + 1) * head) for i in range(stack)]
            queries = [q_parts[0][pl.ds(offset, rows), lane] for lane in lanes]
            for part in range(1, n_parts):
                here = first >= part * part_rows
                queries = [
                    jnp.where(here, q_parts[part][pl.ds(offset, rows), lane], query)
                    for lane, query in zip(lanes, queries)
                ]
            scores = lax.dot_general(
                jnp.concatenate(queries, axis=0),
                keys_all[...],
                (((1,), (1,)), ((), ())),
                preferred_element_type=jnp.float32,
            )
            own = jnp.where(allowed, scores[:, cross:], -1e30)
            free = scores[:, :cross]
            largest = jnp.maximum(
                jnp.max(free, axis=1, keepdims=True), jnp.max(own, axis=1, keepdims=True)
            )
            free = jnp.exp2((free - largest) * scale)
            own = jnp.exp2((own - largest) * scale)
            total = jnp.sum(free, axis=1, keepdims=True) + jnp.sum(own, axis=1, keepdims=True)
            mixed = jnp.dot(
                free.astype(jnp.bfloat16), values_all[:cross, :], preferred_element_type=jnp.float32
            ) + jnp.dot(
                own.astype(jnp.bfloat16), values_all[cross:, :], preferred_element_type=jnp.float32
            )
            mixed = jnp.where(kept, mixed / total, 0.0).astype(jnp.bfloat16)
            for index, lane in enumerate(lanes):
                o_ref[:, lane] = mixed[index * rows : (index + 1) * rows, :]


def attention(places, slots, rows, lengths, queries, own, others):
    n_parts = len(own)
    part_rows, width = queries[0].shape
    head = own[0].shape[1] // 2
    picks = others[0].shape[0]
    reach = n_parts * part_rows + len(others) * picks
    return pl.pallas_call(
        functools.partial(attention_kernel, slots, n_parts, len(others), 512 // rows),
        grid_spec=pltpu.PrefetchScalarGridSpec(
            num_scalar_prefetch=2,
            grid=(1,),
            in_specs=[whole(*array.shape) for array in (*queries, *own, *others)],
            out_specs=[whole(rows, width) for _ in slots],
            scratch_shapes=[
                pltpu.VMEM((reach, head), jnp.bfloat16),
                pltpu.VMEM((reach, head), jnp.bfloat16),
            ],
        ),
        out_shape=[jax.ShapeDtypeStruct((rows, width), jnp.bfloat16) for _ in slots],
        compiler_params=params(24 if reach <= 2048 else 56),
        cost_estimate=cost(1),
        name="attention",
    )(places, lengths, *queries, *own, *others)


def mix_kernel(rows_ref, w_ref, out_ref):
    total = jnp.dot(rows_ref[...], w_ref[...], preferred_element_type=jnp.float32)
    out_ref[...] = total.astype(out_ref.dtype)


def mix(attended, w_out, which):
    rows, depth = attended.shape
    width = w_out.shape[1] // 2
    tiles = 5
    tile = width // tiles
    return pl.pallas_call(
        mix_kernel,
        grid=(tiles,),
        in_specs=[
            whole(rows, depth),
            pl.BlockSpec((depth, tile), lambda i: (0, i + which * tiles)),
        ],
        out_specs=pl.BlockSpec((rows, tile), lambda i: (0, i)),
        out_shape=jax.ShapeDtypeStruct((rows, width), jnp.bfloat16),
        compiler_params=params(8),
        cost_estimate=cost(1),
        name="mix",
    )(attended, w_out)


def add_kernel(count, *refs):
    total = refs[0][...].astype(jnp.float32)
    for ref in refs[1:count]:
        total = total + ref[...].astype(jnp.float32)
    refs[-1][...] = total.astype(jnp.bfloat16)


def added(*arrays, half=None, into=None):
    rows, width = arrays[0].shape
    wide = 1 if half is None else 2
    at = half or 0
    operands = list(arrays)
    in_specs = [whole(rows, width) for _ in arrays]
    aliases = {}
    if into is not None:
        operands.append(into)
        in_specs.append(pl.BlockSpec(memory_space=pl.ANY))
        aliases = {len(arrays): 0}
    return pl.pallas_call(
        functools.partial(add_kernel, len(arrays)),
        grid=(1,),
        in_specs=in_specs,
        out_specs=pl.BlockSpec((rows, width), lambda i: (0, at)),
        out_shape=jax.ShapeDtypeStruct((rows, wide * width), jnp.bfloat16),
        input_output_aliases=aliases,
        compiler_params=params(8),
        cost_estimate=cost(1),
        name="added",
    )(*operands)


def shards(hidden_in, lengths, summary_pos, w_query, w_key, w_value, w_out, q_gain, k_gain):
    rows_here = hidden_in.shape[0]
    head_width = q_gain.shape[0]
    place = lax.axis_index("tensor")
    n_cand = lax.axis_size("cand")
    assert lax.axis_size("tensor") == 4 and w_key.shape[1] == head_width

    def swap(array):
        return lax.ppermute(array, "tensor", [(0, 1), (1, 0), (2, 3), (3, 2)])

    def across(array):
        return lax.ppermute(array, "tensor", [(1, 2), (2, 1)])

    def outward(array):
        return lax.ppermute(array, "tensor", [(1, 0), (2, 3)])

    def inward(array):
        return lax.ppermute(array, "tensor", [(0, 1), (3, 2)])

    def between(array, offset):
        return lax.ppermute(array, "cand", [(i, i ^ offset) for i in range(n_cand)])

    low = place < 2
    near = jnp.bitwise_xor(place, 1)
    places = jnp.stack([place, near, jnp.where(low, 2, 1), jnp.where(low, 3, 0)])
    places = places.astype(jnp.int32)
    tables = rope_tables(rows_here, head_width)
    k_gain, q_gain = k_gain[None], q_gain[None]
    weights = [w_query, w_key, w_value]
    half = rows_here // 2

    mine = [lax.slice_in_dim(hidden_in, i * half, (i + 1) * half) for i in (0, 1)]
    from_near, from_mid = [], []
    for array in mine:
        from_near.append(swap(array))
        from_mid.append(across(array))
    accs = partial_projection(places, OWN, [[hidden_in]], weights, None)
    to_inner = [across(array) for array in from_near]
    to_outer = [outward(array) for array in from_mid]
    from_near[1], accs = lax.optimization_barrier((from_near[1], accs))
    accs = partial_projection(places, NEAR, [[a] for a in from_near], weights, accs)
    to_inner[0], accs = lax.optimization_barrier((to_inner[0], accs))
    end = [outward(array) for array in to_inner]
    accs = partial_projection(
        places, THIRD, [[a, b] for a, b in zip(from_mid, to_outer)], weights, accs
    )

    final = [[a, b] for a, b in zip(to_inner, end)]
    (own_first,) = keys_values(places, final[0], 0, weights[1:], accs[1:], k_gain, *tables)
    first_queries = queries_of(places, final[0], 0, w_query, accs[0], q_gain, *tables)
    own_second, summary = keys_values(
        places,
        final[1],
        1,
        weights[1:],
        after(accs[1:], first_queries),
        k_gain,
        *tables,
        [own_first],
        summary_pos,
    )
    own = [own_first, own_second]
    others = [between(summary, offset) for offset in range(1, n_cand)]
    second_queries = queries_of(places, final[1], 1, w_query, accs[0], q_gain, *tables)
    queries = [first_queries, second_queries]

    def attend(slots):
        return attention(places, slots, rows_here // 4, lengths, queries, own, others)

    def mixed(rows):
        return [mix(rows, w_out, which) for which in (0, 1)]

    (far_rows,) = attend((LAST,))
    far = mixed(far_rows)
    places = after(places, far)
    third_rows, near_rows, own_rows = attend((THIRD, NEAR, OWN))
    mid = mixed(third_rows)
    far_in = [inward(array) for array in far]
    mid_in = [inward(array) for array in mid]
    far_sum = [added(far[0], after(far_in[0], mid))]
    near_part = mixed(after(near_rows, far_sum[0]))
    far_sum.append(added(far[1], after(far_in[1], near_part)))
    kept = mixed(after(own_rows, far_sum[1]))
    far_sum = [across(array) for array in far_sum]
    near_sum, mid_sum = [None, None], [None, None]
    cue = kept
    for i in (0, 1):
        near_sum[i] = added(near_part[i], after(far_sum[i], cue))
        mid_sum[i] = added(mid[i], after(mid_in[i], near_sum[i]))
        cue = mid_sum[i]
    near_sum = [swap(array) for array in near_sum]
    mid_sum = [across(array) for array in mid_sum]
    result = added(kept[0], near_sum[0], mid_sum[0], half=0)
    return added(kept[1], near_sum[1], mid_sum[1], half=1, into=result)


def solution(mesh):
    return jax.shard_map(
        shards,
        mesh=mesh,
        in_specs=(
            P("cand", "tensor"),
            P("cand"),
            P("cand", None),
            P(None, "tensor"),
            P(None, "tensor"),
            P(None, "tensor"),
            P("tensor", None),
            P(),
            P(),
        ),
        out_specs=P(("cand", "tensor"), None),
        check_vma=False,
    )
```

time: 216 us -> 212 us (0.981)
  waiting for transfers between devices: 73.6 us -> 106 us
  local copies, waits for them, and re-layouts: 31.9 us -> 7.93 us
  starting transfers between devices: 49.6 us -> 43.3 us
  other arithmetic: 3.78 us -> 0.08 us
    unnamed x93 -> x26, local copies, waits for them, and re-layouts: 29 us -> 5.35 us
    ppermute x3 -> x4, waiting for transfers between devices: 19.9 us -> 41.1 us  [outward(): return lax.ppermute(array, 'tensor', [(1, 0), (2, 3)])]
    ppermute x3 -> x4, waiting for transfers between devices: 30.7 us -> 45.3 us  [swap(): return lax.ppermute(array, 'tensor', [(0, 1), (1, 0), (2, 3), (3, 2)])]
    ppermute x3 -> x4, starting transfers between devices: 21.9 us -> 7.86 us  [swap(): return lax.ppermute(array, 'tensor', [(0, 1), (1, 0), (2, 3), (3, 2)])]
    ppermute x4, starting transfers between devices: 9.38 us -> 15.8 us  [inward(): return lax.ppermute(array, 'tensor', [(0, 1), (3, 2)])]
    ppermute x4, waiting for transfers between devices: 22.9 us -> 17.6 us  [inward(): return lax.ppermute(array, 'tensor', [(0, 1), (3, 2)])]
    pallas_call x7 -> x14, Pallas kernels: 21.8 us -> 23.7 us  [the longest x2 11.2 us: attention(): pl.pallas_call(functools.partial(attention_kernel, slots, n_parts, len(ot...]
    pallas_call x6 -> x3, Pallas kernels: 14.6 us -> 13 us  [partial_projection(): pl.pallas_call(functools.partial(partial_kernel, [len(part) for part in p...]
  transfers between devices with their start and end apart: 24 -> 27, of which waited for: 8 -> 12; matrix products, arithmetic and copies ran while one was open for 3% -> 0% of each run, Pallas kernels for 21% -> 21%
where the time goes in v4:
time: 212 us; the launch traced here: 211 us
  waiting for transfers between devices  106 us (50%)
  Pallas kernels  53.2 us (25%)
  starting transfers between devices  43.3 us (20%)
  local copies, waits for them, and re-layouts  7.93 us (4%)
    ppermute x4, waiting for transfers between devices, swap(): return lax.ppermute(array, 'tensor', [(0, 1), (1, 0), (2, 3), (3, 2)])  45.3 us
    ppermute x4, waiting for transfers between devices, outward(): return lax.ppermute(array, 'tensor', [(1, 0), (2, 3)])  41.1 us
    ppermute x4, waiting for transfers between devices, inward(): return lax.ppermute(array, 'tensor', [(0, 1), (3, 2)])  17.6 us
    pallas_call x8, Pallas kernels, mix(): pl.pallas_call(mix_kernel, grid=(tiles,), in_specs=[whole(rows, depth), p...  16.5 us
    ppermute x4, starting transfers between devices, inward(): return lax.ppermute(array, 'tensor', [(0, 1), (3, 2)])  15.8 us
    pallas_call x3, Pallas kernels, partial_projection(): pl.pallas_call(functools.partial(partial_kernel, [len(part) for part in p...  13 us
    pallas_call x2, Pallas kernels, attention(): pl.pallas_call(functools.partial(attention_kernel, slots, n_parts, len(ot...  11.2 us
    ppermute x8, starting transfers between devices, across(): return lax.ppermute(array, 'tensor', [(1, 2), (2, 1)])  8.02 us
  transfers between devices with their start and end apart: 27, of which 12 were waited for; matrix products, arithmetic and copies ran while one was open for 0% of the time, Pallas kernels for 21%

profile of v4, /device:TPU:0, one launch (start us, length us, event | category | flops | bytes accessed | tf_op | source)
XLA Modules:
  0.0 211.2 jit_solution(13775692886972679805)
XLA Ops:
  0.0 2.6 %fusion = (bf16[256,1280]{1,0:T(8,128)(2,1)}, bf16[256,1280]{1,0:T(8,128)(2,1)}) fusion(bf16[512,1280]{1,0:T(8,128)(2,1)} %refs_0_.1), kind=kLoop, calls=%fused_computation.1 | loop fusion | bytes 2621440 | tf_op jit(solution)/shard_map/slice | solution.py:377
  2.6 3.0 %collective-permute-start = (bf16[256,1280]{1,0:T(8,128)(2,1)}, bf16[256,1280]{1,0:T(8,128)(2,1)}, u32[]{:S(2)}, u32[]{:S(2)}) collective-permute-start(bf16[256,1280]{1,0:T(8,128)(2,1)} %get-tuple-element.72), channel_id=1, source_target_pairs={{0,1},{1,0},{2,3},{3,2},{4,5},{5,4},{6,7},{7,6},{8,9},{9,8},{10,11... | collective-permute-start | bytes 1966088 | tf_op jit(solution)/shard_map/ppermute | solution.py:354
  5.6 1.5 collective-permute-start.4
  7.1 1.5 collective-permute-start.6
  8.7 12.8 %collective-permute-done.refs_0_ = bf16[256,1280]{1,0:T(8,128)(2,1)} collective-permute-done((bf16[256,1280]{1,0:T(8,128)(2,1)}, bf16[256,1280]{1,0:T(8,128)(2,1)}, u32[]{:S(2)}, u32[]{:S(2)}) %collective-permute-start) | collective-permute-done | bytes 655392 | tf_op jit(solution)/shard_map/ppermute | solution.py:354
  21.5 1.5 collective-permute-start.1
  23.0 11.7 %collective-permute-done.2.refs_1_ = bf16[256,1280]{1,0:T(8,128)(2,1)} collective-permute-done((bf16[256,1280]{1,0:T(8,128)(2,1)}, bf16[256,1280]{1,0:T(8,128)(2,1)}, u32[]{:S(2)}, u32[]{:S(2)}) %collective-permute-start.2) | collective-permute-done | bytes 655392 | tf_op jit(solution)/shard_map/ppermute | solution.py:354
  34.7 0.7 collective-permute-start.8
  35.5 4.0 %copy-done = bf16[5120,1024]{1,0:T(8,128)(2,1)S(1)} copy-done((bf16[5120,1024]{1,0:T(8,128)(2,1)S(1)}, bf16[5120,1024]{1,0:T(8,128)(2,1)}, u32[]{:S(2)}) %copy-start) | copy-done | bytes 10485784
  39.5 1.3 copy-done.4
  40.8 3.4 %partial_projection.3 = (f32[512,1024]{1,0:T(8,128)S(1)}, f32[512,128]{1,0:T(8,128)S(1)}, f32[512,128]{1,0:T(8,128)S(1)}) custom-call(s32[4]{0:T(128)S(1)} %pad_add_fusion.places_ref, bf16[512,1280]{1,0:T(8,128)(2,1)S(1)} %copy-done.4, bf16[5120,1024]{1,0:T(8,128)(2,1)S(1)} %copy-done, bf16[5120,128]{1,0:T(8,128)(2,1)S(1)} %copy-done.2, ...), custom_call_target="tpu_custom_call" | custom-call | flops 1 | bytes 1 | tf_op jit(solution)/shard_map/partial_projection/pallas_call | solution.py:95
  44.3 1.3 collective-permute-start.5
  45.6 1.3 collective-permute-start.7
  46.9 4.7 %partial_projection.4 = (f32[512,1024]{1,0:T(8,128)S(1)}, f32[512,128]{1,0:T(8,128)S(1)}, f32[512,128]{1,0:T(8,128)S(1)}) custom-call(s32[4]{0:T(128)S(1)} %pad_add_fusion.places_ref, bf16[256,1280]{1,0:T(8,128)(2,1)} %collective-permute-done.refs_0_, bf16[256,1280]{1,0:T(8,128)(2,1)} %collective-permute-done.2.refs_1_, bf16[5120,1024]{1,0:T(8,128)(2,1)S(1)} %copy-done.1, ...), custom_call_target="tpu_custom_call" | custom-call | flops 1 | bytes 1 | tf_op jit(solution)/shard_map/partial_projection/pallas_call | solution.py:95
  51.7 1.4 collective-permute-start.3
  53.1 1.3 collective-permute-start.9
  54.4 11.5 %collective-permute-done.5.refs_1_ = bf16[256,1280]{1,0:T(8,128)(2,1)S(1)} collective-permute-done((bf16[256,1280]{1,0:T(8,128)(2,1)}, bf16[256,1280]{1,0:T(8,128)(2,1)S(1)}, u32[]{:S(2)}, u32[]{:S(2)}) %collective-permute-start.5) | collective-permute-done | bytes 655392 | tf_op jit(solution)/shard_map/ppermute | solution.py:360
  65.9 14.0 %collective-permute-done.7.refs_3_ = bf16[256,1280]{1,0:T(8,128)(2,1)S(1)} collective-permute-done((bf16[256,1280]{1,0:T(8,128)(2,1)}, bf16[256,1280]{1,0:T(8,128)(2,1)S(1)}, u32[]{:S(2)}, u32[]{:S(2)}) %collective-permute-start.7) | collective-permute-done | bytes 655392 | tf_op jit(solution)/shard_map/ppermute | solution.py:360
  80.0 4.8 %partial_projection.5 = (f32[512,1024]{1,0:T(8,128)S(1)}, f32[512,128]{1,0:T(8,128)S(1)}, f32[512,128]{1,0:T(8,128)S(1)}) custom-call(s32[4]{0:T(128)S(1)} %pad_add_fusion.places_ref, bf16[256,1280]{1,0:T(8,128)(2,1)} %collective-permute-done.4.refs_0_, bf16[256,1280]{1,0:T(8,128)(2,1)S(1)} %collective-permute-done.5.refs_1_, ...), custom_call_target="tpu_custom_call" | custom-call | flops 1 | bytes 1 | tf_op jit(solution)/shard_map/partial_projection/pallas_call | solution.py:95
  84.7 9.3 %collective-permute-done.3.refs_1_ = bf16[256,1280]{1,0:T(8,128)(2,1)S(1)} collective-permute-done((bf16[256,1280]{1,0:T(8,128)(2,1)}, bf16[256,1280]{1,0:T(8,128)(2,1)S(1)}, u32[]{:S(2)}, u32[]{:S(2)}) %collective-permute-start.3) | collective-permute-done | bytes 655392 | tf_op jit(solution)/shard_map/ppermute | solution.py:360
  94.0 3.4 %queries.2.refs_0_ = bf16[256,1024]{1,0:T(8,128)(2,1)S(1)} custom-call(s32[4]{0:T(128)S(1)} %pad_add_fusion.places_ref, bf16[256,1280]{1,0:T(8,128)(2,1)} %collective-permute-done.1.refs_0_, bf16[256,1280]{1,0:T(8,128)(2,1)S(1)} %collective-permute-done.3.refs_1_, bf16[5120,1024]{1,0:T(8,128)(2,1)S(1)} %copy-done.1, ...), custom_call_target="tpu_custom_call" | custom-call | flops 1 | bytes 1 | tf_op jit(solution)/shard_map/queries/pallas_call | solution.py:182
  97.5 2.2 %keys_values.2.refs_0_.refs_2_ = bf16[256,256]{1,0:T(8,128)(2,1)S(1)} custom-call(s32[4]{0:T(128)S(1)} %pad_add_fusion.places_ref, bf16[256,1280]{1,0:T(8,128)(2,1)} %collective-permute-done.1.refs_0_, bf16[256,1280]{1,0:T(8,128)(2,1)S(1)} %collective-permute-done.3.refs_1_, bf16[5120,128]{1,0:T(8,128)(2,1)S(1)} %copy-done.2, ...), custom_call_target="tpu_custom_call" | custom-call | flops 1 | bytes 1 | tf_op jit(solution)/shard_map/keys_values/pallas_call | solution.py:151
  99.7 6.3 %collective-permute-done.9.refs_1_.refs_2_ = bf16[256,1280]{1,0:T(8,128)(2,1)S(1)} collective-permute-done((bf16[256,1280]{1,0:T(8,128)(2,1)S(1)}, bf16[256,1280]{1,0:T(8,128)(2,1)S(1)}, u32[]{:S(2)}, u32[]{:S(2)}) %collective-permute-start.9) | collective-permute-done | bytes 655392 | tf_op jit(solution)/shard_map/ppermute | solution.py:360
  106.0 1.3 keys_values.3
  107.4 1.6 collective-permute-start.11
  108.9 0.3 collective-permute-start.12
  109.2 1.5 collective-permute-start.13
  110.7 0.2 collective-permute-start.14
  110.9 2.4 %collective-permute-start.15 = (bf16[128,256]{1,0:T(8,128)(2,1)S(1)}, bf16[128,256]{1,0:T(8,128)(2,1)S(1)}, u32[]{:S(2)}, u32[]{:S(2)}) collective-permute-start(bf16[128,256]{1,0:T(8,128)(2,1)S(1)} %get-tuple-element.58), channel_id=1, source_target_pairs={{0,24},{4,28},{8,16},{12,20},{16,8},{20,12},{24,0},{28,4},{1,25},{... | collective-permute-start | bytes 196616 | tf_op jit(solution)/shard_map/ppermute | solution.py:366
  113.4 0.3 collective-permute-start.16
  114.3 2.5 %queries.3.refs_1_ = bf16[256,1024]{1,0:T(8,128)(2,1)S(1)} custom-call(s32[4]{0:T(128)S(1)} %pad_add_fusion.places_ref, bf16[256,1280]{1,0:T(8,128)(2,1)S(1)} %collective-permute-done.8.refs_0_.refs_1_, bf16[256,1280]{1,0:T(8,128)(2,1)S(1)} %collective-permute-done.9.refs_1_.refs_2_, bf16[5120,1024]{1,0:T(8,128)(2,1)S(1)} %copy-done.1, ...), custom_call_target="tpu_custom_call" | custom-call | flops 1 | bytes 1 | tf_op jit(solution)/shard_map/queries/pallas_call | solution.py:182
  116.9 1.5 collective-permute-done.16.refs_10_
  118.3 3.6 %attention.2.rows_ref = bf16[128,1024]{1,0:T(8,128)(2,1)S(1)} custom-call(s32[4]{0:T(128)S(1)} %pad_add_fusion.places_ref, s32[1]{0:T(128)S(6)} %copy.14.length_ref, bf16[256,1024]{1,0:T(8,128)(2,1)S(1)} %queries.2.refs_0_, bf16[256,1024]{1,0:T(8,128)(2,1)S(1)} %queries.3.refs_1_, bf16[256,256]{1,0:T(8,128)(2,1)S(1)} %keys_values.2.refs_0_.refs_2_, ...), custom_call_target="tpu_custom_call" | custom-call | flops 1 | bytes 1 | tf_op jit(solution)/shard_map/attention/pallas_call | solution.py:271
  121.9 2.1 mix.8.refs_0_
  124.0 1.5 collective-permute-start.18
  125.5 2.1 mix.9.refs_0_
  127.6 1.5 collective-permute-start.17
  129.1 7.6 %attention.3 = (bf16[128,1024]{1,0:T(8,128)(2,1)S(1)}, bf16[128,1024]{1,0:T(8,128)(2,1)S(1)}, bf16[128,1024]{1,0:T(8,128)(2,1)S(1)}) custom-call(s32[4]{0:T(128)S(1)} %pad_add_fusion.places_ref, s32[1]{0:T(128)S(6)} %copy.14.length_ref, bf16[256,1024]{1,0:T(8,128)(2,1)S(1)} %queries.2.refs_0_, bf16[256,1024]{1,0:T(8,128)(2,1)S(1)} %queries.3.refs_1_, ...), custom_call_target="tpu_custom_call" | custom-call | flops 1 | bytes 1 | tf_op jit(solution)/shard_map/attention/pallas_call | solution.py:271
  136.8 2.1 mix.10.refs_0_
  138.8 2.1 mix.11.refs_0_
  140.9 0.2 added.8
  141.1 0.7 collective-permute-start.21
  141.8 6.2 %collective-permute-start.20 = (bf16[128,2560]{1,0:T(8,128)(2,1)S(1)}, bf16[128,2560]{1,0:T(8,128)(2,1)S(1)}, u32[]{:S(2)}, u32[]{:S(2)}) collective-permute-start(bf16[128,2560]{1,0:T(8,128)(2,1)S(1)} %mix.10.refs_0_), channel_id=1, source_target_pairs={{0,1},{3,2},{4,5},{7,6},{8,9},{11,10},{12,13},{15,14},{16,17},{19,... | collective-permute-start | bytes 1966088 | tf_op jit(solution)/shard_map/ppermute | solution.py:363
  148.0 2.1 mix.12.refs_0_
  150.1 2.1 mix.13.refs_0_
  152.1 2.4 %collective-permute-done.17.refs_1_ = bf16[128,2560]{1,0:T(8,128)(2,1)S(1)} collective-permute-done((bf16[128,2560]{1,0:T(8,128)(2,1)S(1)}, bf16[128,2560]{1,0:T(8,128)(2,1)S(1)}, u32[]{:S(2)}, u32[]{:S(2)}) %collective-permute-start.17) | collective-permute-done | bytes 655392 | tf_op jit(solution)/shard_map/ppermute | solution.py:363
  154.6 0.2 added.9
  154.7 0.7 collective-permute-start.19
  155.4 6.6 %collective-permute-start.23 = (bf16[128,2560]{1,0:T(8,128)(2,1)S(1)}, bf16[128,2560]{1,0:T(8,128)(2,1)S(1)}, u32[]{:S(2)}, u32[]{:S(2)}) collective-permute-start(bf16[128,2560]{1,0:T(8,128)(2,1)S(1)} %mix.11.refs_0_), channel_id=1, source_target_pairs={{0,1},{3,2},{4,5},{7,6},{8,9},{11,10},{12,13},{15,14},{16,17},{19,... | collective-permute-start | bytes 1966088 | tf_op jit(solution)/shard_map/ppermute | solution.py:363
  162.0 2.1 mix.14.refs_0_
  164.1 2.1 mix.15.refs_0_
  166.2 0.2 added.10
  166.4 2.2 %collective-permute-done.20.refs_1_ = bf16[128,2560]{1,0:T(8,128)(2,1)S(1)} collective-permute-done((bf16[128,2560]{1,0:T(8,128)(2,1)S(1)}, bf16[128,2560]{1,0:T(8,128)(2,1)S(1)}, u32[]{:S(2)}, u32[]{:S(2)}) %collective-permute-start.20) | collective-permute-done | bytes 655392 | tf_op jit(solution)/shard_map/ppermute | solution.py:363
  168.6 0.2 added.11
  168.8 0.7 collective-permute-start.26
  169.5 0.2 added.12
  169.6 13.0 %collective-permute-done.23.refs_1_ = bf16[128,2560]{1,0:T(8,128)(2,1)S(1)} collective-permute-done((bf16[128,2560]{1,0:T(8,128)(2,1)S(1)}, bf16[128,2560]{1,0:T(8,128)(2,1)S(1)}, u32[]{:S(2)}, u32[]{:S(2)}) %collective-permute-start.23) | collective-permute-done | bytes 655392 | tf_op jit(solution)/shard_map/ppermute | solution.py:363
  182.6 0.2 added.13
  182.8 0.7 collective-permute-start.24
  183.5 4.7 %collective-permute-start.22 = (bf16[128,2560]{1,0:T(8,128)(2,1)S(1)}, bf16[128,2560]{1,0:T(8,128)(2,1)S(1)}, u32[]{:S(2)}, u32[]{:S(2)}) collective-permute-start(bf16[128,2560]{1,0:T(8,128)(2,1)S(1)} %added.12), channel_id=1, source_target_pairs={{0,1},{1,0},{2,3},{3,2},{4,5},{5,4},{6,7},{7,6},{8,9},{9,8},{10,11... | collective-permute-start | bytes 1966088 | tf_op jit(solution)/shard_map/ppermute | solution.py:354
  188.2 8.4 %collective-permute-done.25.refs_1_ = bf16[128,2560]{1,0:T(8,128)(2,1)S(1)} collective-permute-done((bf16[128,2560]{1,0:T(8,128)(2,1)S(1)}, bf16[128,2560]{1,0:T(8,128)(2,1)S(1)}, u32[]{:S(2)}, u32[]{:S(2)}) %collective-permute-start.25) | collective-permute-done | bytes 655392 | tf_op jit(solution)/shard_map/ppermute | solution.py:354
  196.7 1.1 added.14.refs_3_
  197.8 12.3 %collective-permute-done.22.refs_1_ = bf16[128,2560]{1,0:T(8,128)(2,1)S(1)} collective-permute-done((bf16[128,2560]{1,0:T(8,128)(2,1)S(1)}, bf16[128,2560]{1,0:T(8,128)(2,1)S(1)}, u32[]{:S(2)}, u32[]{:S(2)}) %collective-permute-start.22) | collective-permute-done | bytes 655392 | tf_op jit(solution)/shard_map/ppermute | solution.py:354
  210.1 1.1 added.15
  (44 shorter events, 0.4 us)
Async XLA Ops:
  0.0 35.5 %copy-start.2 = (bf16[5120,128]{1,0:T(8,128)(2,1)S(1)}, bf16[5120,128]{1,0:T(8,128)(2,1)}, u32[]{:S(2)}) copy-start(bf16[5120,128]{1,0:T(8,128)(2,1)} %refs_3_.7) | copy-start | bytes 3932164
  0.0 35.5 %copy-start.3 = (bf16[5120,128]{1,0:T(8,128)(2,1)S(1)}, bf16[5120,128]{1,0:T(8,128)(2,1)}, u32[]{:S(2)}) copy-start(bf16[5120,128]{1,0:T(8,128)(2,1)} %refs_4_.5) | copy-start | bytes 3932164
  2.6 18.9 %collective-permute-start = (bf16[256,1280]{1,0:T(8,128)(2,1)}, bf16[256,1280]{1,0:T(8,128)(2,1)}, u32[]{:S(2)}, u32[]{:S(2)}) collective-permute-start(bf16[256,1280]{1,0:T(8,128)(2,1)} %get-tuple-element.72), channel_id=1, source_target_pairs={{0,1},{1,0},{2,3},{3,2},{4,5},{5,4},{6,7},{7,6},{8,9},{9,8},{10,11... | collective-permute-start | bytes 1966088 | tf_op jit(solution)/shard_map/ppermute | solution.py:354
  5.6 29.1 %collective-permute-start.2 = (bf16[256,1280]{1,0:T(8,128)(2,1)}, bf16[256,1280]{1,0:T(8,128)(2,1)}, u32[]{:S(2)}, u32[]{:S(2)}) collective-permute-start(bf16[256,1280]{1,0:T(8,128)(2,1)} %get-tuple-element.71), channel_id=1, source_target_pairs={{0,1},{1,0},{2,3},{3,2},{4,5},{5,4},{6,7},{7,6},{8,9},{9,8},{10,11... | collective-permute-start | bytes 1966088 | tf_op jit(solution)/shard_map/ppermute | solution.py:354
  5.6 38.6 %collective-permute-start.4 = (bf16[256,1280]{1,0:T(8,128)(2,1)}, bf16[256,1280]{1,0:T(8,128)(2,1)}, u32[]{:S(2)}, u32[]{:S(2)}) collective-permute-start(bf16[256,1280]{1,0:T(8,128)(2,1)} %get-tuple-element.72), channel_id=1, source_target_pairs={{1,2},{2,1},{5,6},{6,5},{9,10},{10,9},{13,14},{14,13},{17,18},{18,... | collective-permute-start | bytes 1966088 | tf_op jit(solution)/shard_map/ppermute | solution.py:357
  7.1 38.4 %collective-permute-start.6 = (bf16[256,1280]{1,0:T(8,128)(2,1)}, bf16[256,1280]{1,0:T(8,128)(2,1)}, u32[]{:S(2)}, u32[]{:S(2)}) collective-permute-start(bf16[256,1280]{1,0:T(8,128)(2,1)} %get-tuple-element.71), channel_id=1, source_target_pairs={{1,2},{2,1},{5,6},{6,5},{9,10},{10,9},{13,14},{14,13},{17,18},{18,... | collective-permute-start | bytes 1966088 | tf_op jit(solution)/shard_map/ppermute | solution.py:357
  21.5 30.1 %collective-permute-start.1 = (bf16[256,1280]{1,0:T(8,128)(2,1)}, bf16[256,1280]{1,0:T(8,128)(2,1)}, u32[]{:S(2)}, u32[]{:S(2)}) collective-permute-start(bf16[256,1280]{1,0:T(8,128)(2,1)} %collective-permute-done.refs_0_), channel_id=1, source_target_pairs={{1,2},{2,1},{5,6},{6,5},{9,10},{10,9},{13,14},{14,13},{17,18},{18,... | collective-permute-start | bytes 1966088 | tf_op jit(solution)/shard_map/ppermute | solution.py:357
  34.7 18.4 %collective-permute-start.8 = (bf16[256,1280]{1,0:T(8,128)(2,1)}, bf16[256,1280]{1,0:T(8,128)(2,1)S(1)}, u32[]{:S(2)}, u32[]{:S(2)}) collective-permute-start(bf16[256,1280]{1,0:T(8,128)(2,1)} %collective-permute-done.2.refs_1_), channel_id=1, source_target_pairs={{1,2},{2,1},{5,6},{6,5},{9,10},{10,9},{13,14},{14,13},{17,18},{18,... | collective-permute-start | bytes 1966088 | tf_op jit(solution)/shard_map/ppermute | solution.py:357
  35.5 4.0 %copy-start = (bf16[5120,1024]{1,0:T(8,128)(2,1)S(1)}, bf16[5120,1024]{1,0:T(8,128)(2,1)}, u32[]{:S(2)}) copy-start(bf16[5120,1024]{1,0:T(8,128)(2,1)} %refs_2_.8) | copy-start | bytes 31457284
  39.5 1.3 copy-start.4
  40.8 6.1 %copy-start.1 = (bf16[5120,1024]{1,0:T(8,128)(2,1)S(1)}, bf16[5120,1024]{1,0:T(8,128)(2,1)}, u32[]{:S(2)}) copy-start(bf16[5120,1024]{1,0:T(8,128)(2,1)} %refs_2_.8) | copy-start | bytes 31457284
  44.3 21.7 %collective-permute-start.5 = (bf16[256,1280]{1,0:T(8,128)(2,1)}, bf16[256,1280]{1,0:T(8,128)(2,1)S(1)}, u32[]{:S(2)}, u32[]{:S(2)}) collective-permute-start(bf16[256,1280]{1,0:T(8,128)(2,1)} %collective-permute-done.4.refs_0_), channel_id=1, source_target_pairs={{1,0},{2,3},{5,4},{6,7},{9,8},{10,11},{13,12},{14,15},{17,16},{18,... | collective-permute-start | bytes 1966088 | tf_op jit(solution)/shard_map/ppermute | solution.py:360
  45.6 34.4 %collective-permute-start.7 = (bf16[256,1280]{1,0:T(8,128)(2,1)}, bf16[256,1280]{1,0:T(8,128)(2,1)S(1)}, u32[]{:S(2)}, u32[]{:S(2)}) collective-permute-start(bf16[256,1280]{1,0:T(8,128)(2,1)} %collective-permute-done.6.refs_2_), channel_id=1, source_target_pairs={{1,0},{2,3},{5,4},{6,7},{9,8},{10,11},{13,12},{14,15},{17,16},{18,... | collective-permute-start | bytes 1966088 | tf_op jit(solution)/shard_map/ppermute | solution.py:360
  51.6 42.4 %copy-start.5 = (f32[512,128]{1,0:T(8,128)S(1)}, f32[512,128]{1,0:T(8,128)}, u32[]{:S(2)}) copy-start(f32[512,128]{1,0:T(8,128)} %constant.16.clone.refs_5_.refs_7_.refs_8_) | copy-start | bytes 786436
  51.6 42.4 %copy-start.6 = (f32[512,128]{1,0:T(8,128)S(1)}, f32[512,128]{1,0:T(8,128)}, u32[]{:S(2)}) copy-start(f32[512,128]{1,0:T(8,128)} %constant.17.clone.refs_6_.refs_8_.refs_9_) | copy-start | bytes 786436
  51.7 42.3 %copy-start.8 = (f32[128]{0:T(128)S(1)}, f32[128]{0:T(128)}, u32[]{:S(2)}) copy-start(f32[128]{0:T(128)} %param.18) | copy-start | bytes 1540
  51.7 42.3 %collective-permute-start.3 = (bf16[256,1280]{1,0:T(8,128)(2,1)}, bf16[256,1280]{1,0:T(8,128)(2,1)S(1)}, u32[]{:S(2)}, u32[]{:S(2)}) collective-permute-start(bf16[256,1280]{1,0:T(8,128)(2,1)} %collective-permute-done.1.refs_0_), channel_id=1, source_target_pairs={{1,0},{2,3},{5,4},{6,7},{9,8},{10,11},{13,12},{14,15},{17,16},{18,... | collective-permute-start | bytes 1966088 | tf_op jit(solution)/shard_map/ppermute | solution.py:360
  53.1 52.9 %collective-permute-start.9 = (bf16[256,1280]{1,0:T(8,128)(2,1)S(1)}, bf16[256,1280]{1,0:T(8,128)(2,1)S(1)}, u32[]{:S(2)}, u32[]{:S(2)}) collective-permute-start(bf16[256,1280]{1,0:T(8,128)(2,1)S(1)} %collective-permute-done.8.refs_0_.refs_1_), channel_id=1, source_target_pairs={{1,0},{2,3},{5,4},{6,7},{9,8},{10,11},{13,12},{14,15},{17,16},{18,... | collective-permute-start | bytes 1966088 | tf_op jit(solution)/shard_map/ppermute | solution.py:360
  94.0 3.5 %copy-start.7 = (f32[128]{0:T(128)S(1)}, f32[128]{0:T(128)}, u32[]{:S(2)}) copy-start(f32[128]{0:T(128)} %param.19) | copy-start | bytes 1540
  97.5 8.5 %copy-start.9 = (s32[1,128]{1,0:T(1,128)S(1)}, s32[1,128]{1,0:T(1,128)}, u32[]{:S(2)}) copy-start(s32[1,128]{1,0:T(1,128)} %refs_10_.1) | copy-start | bytes 1540
  106.0 15.9 %slice-start = ((s8[10485760]{0:T(1024)(128)(4,1)}), s8[4194304]{0:T(1024)(128)(4,1)S(1)}, s32[]{:S(2)}) async-start(s8[10485760]{0:T(1024)(128)(4,1)} %bitcast.6), calls=%async_computation | async-start | bytes 8388608
  107.3 3.6 %collective-permute-start.10 = (bf16[128,256]{1,0:T(8,128)(2,1)S(1)}, bf16[128,256]{1,0:T(8,128)(2,1)S(1)}, u32[]{:S(2)}, u32[]{:S(2)}) collective-permute-start(bf16[128,256]{1,0:T(8,128)(2,1)S(1)} %get-tuple-element.58), channel_id=1, source_target_pairs={{0,4},{4,0},{8,12},{12,8},{16,20},{20,16},{24,28},{28,24},{1,5},{5... | collective-permute-start | bytes 196616 | tf_op jit(solution)/shard_map/ppermute | solution.py:366
  107.4 6.0 %collective-permute-start.11 = (bf16[128,256]{1,0:T(8,128)(2,1)S(1)}, bf16[128,256]{1,0:T(8,128)(2,1)S(1)}, u32[]{:S(2)}, u32[]{:S(2)}) collective-permute-start(bf16[128,256]{1,0:T(8,128)(2,1)S(1)} %get-tuple-element.58), channel_id=1, source_target_pairs={{0,8},{4,12},{8,0},{12,4},{16,24},{20,28},{24,16},{28,20},{1,9},{5... | collective-permute-start | bytes 196616 | tf_op jit(solution)/shard_map/ppermute | solution.py:366
  108.9 7.9 %collective-permute-start.12 = (bf16[128,256]{1,0:T(8,128)(2,1)S(1)}, bf16[128,256]{1,0:T(8,128)(2,1)S(1)}, u32[]{:S(2)}, u32[]{:S(2)}) collective-permute-start(bf16[128,256]{1,0:T(8,128)(2,1)S(1)} %get-tuple-element.58), channel_id=1, source_target_pairs={{0,12},{4,8},{8,4},{12,0},{16,28},{20,24},{24,20},{28,16},{1,13},{... | collective-permute-start | bytes 196616 | tf_op jit(solution)/shard_map/ppermute | solution.py:366
  109.2 7.6 %collective-permute-start.13 = (bf16[128,256]{1,0:T(8,128)(2,1)S(1)}, bf16[128,256]{1,0:T(8,128)(2,1)S(1)}, u32[]{:S(2)}, u32[]{:S(2)}) collective-permute-start(bf16[128,256]{1,0:T(8,128)(2,1)S(1)} %get-tuple-element.58), channel_id=1, source_target_pairs={{0,16},{4,20},{8,24},{12,28},{16,0},{20,4},{24,8},{28,12},{1,17},{... | collective-permute-start | bytes 196616 | tf_op jit(solution)/shard_map/ppermute | solution.py:366
  110.7 6.1 %collective-permute-start.14 = (bf16[128,256]{1,0:T(8,128)(2,1)S(1)}, bf16[128,256]{1,0:T(8,128)(2,1)S(1)}, u32[]{:S(2)}, u32[]{:S(2)}) collective-permute-start(bf16[128,256]{1,0:T(8,128)(2,1)S(1)} %get-tuple-element.58), channel_id=1, source_target_pairs={{0,20},{4,16},{8,28},{12,24},{16,4},{20,0},{24,12},{28,8},{1,21},{... | collective-permute-start | bytes 196616 | tf_op jit(solution)/shard_map/ppermute | solution.py:366
  110.9 5.9 %collective-permute-start.15 = (bf16[128,256]{1,0:T(8,128)(2,1)S(1)}, bf16[128,256]{1,0:T(8,128)(2,1)S(1)}, u32[]{:S(2)}, u32[]{:S(2)}) collective-permute-start(bf16[128,256]{1,0:T(8,128)(2,1)S(1)} %get-tuple-element.58), channel_id=1, source_target_pairs={{0,24},{4,28},{8,16},{12,20},{16,8},{20,12},{24,0},{28,4},{1,25},{... | collective-permute-start | bytes 196616 | tf_op jit(solution)/shard_map/ppermute | solution.py:366
  113.4 4.9 %collective-permute-start.16 = (bf16[128,256]{1,0:T(8,128)(2,1)S(1)}, bf16[128,256]{1,0:T(8,128)(2,1)S(1)}, u32[]{:S(2)}, u32[]{:S(2)}) collective-permute-start(bf16[128,256]{1,0:T(8,128)(2,1)S(1)} %get-tuple-element.58), channel_id=1, source_target_pairs={{0,28},{4,24},{8,20},{12,16},{16,12},{20,8},{24,4},{28,0},{1,29},{... | collective-permute-start | bytes 196616 | tf_op jit(solution)/shard_map/ppermute | solution.py:366
  114.3 7.6 %slice-start.1 = ((s8[10485760]{0:T(1024)(128)(4,1)}), s8[4194304]{0:T(1024)(128)(4,1)S(1)}, s32[]{:S(2)}) async-start(s8[10485760]{0:T(1024)(128)(4,1)} %bitcast.6), calls=%async_computation.1 | async-start | bytes 8388608
  114.3 7.6 %slice-start.2 = ((s8[10485760]{0:T(1024)(128)(4,1)}), s8[2097152]{0:T(1024)(128)(4,1)S(1)}, s32[]{:S(2)}) async-start(s8[10485760]{0:T(1024)(128)(4,1)} %bitcast.6), calls=%async_computation.2 | async-start | bytes 4194304
  124.0 16.9 %collective-permute-start.18 = (bf16[128,2560]{1,0:T(8,128)(2,1)S(1)}, bf16[128,2560]{1,0:T(8,128)(2,1)S(1)}, u32[]{:S(2)}, u32[]{:S(2)}) collective-permute-start(bf16[128,2560]{1,0:T(8,128)(2,1)S(1)} %mix.8.refs_0_), channel_id=1, source_target_pairs={{0,1},{3,2},{4,5},{7,6},{8,9},{11,10},{12,13},{15,14},{16,17},{19,... | collective-permute-start | bytes 1966088 | tf_op jit(solution)/shard_map/ppermute | solution.py:363
  127.6 27.0 %collective-permute-start.17 = (bf16[128,2560]{1,0:T(8,128)(2,1)S(1)}, bf16[128,2560]{1,0:T(8,128)(2,1)S(1)}, u32[]{:S(2)}, u32[]{:S(2)}) collective-permute-start(bf16[128,2560]{1,0:T(8,128)(2,1)S(1)} %mix.9.refs_0_), channel_id=1, source_target_pairs={{0,1},{3,2},{4,5},{7,6},{8,9},{11,10},{12,13},{15,14},{16,17},{19,... | collective-permute-start | bytes 1966088 | tf_op jit(solution)/shard_map/ppermute | solution.py:363
  141.1 25.1 %collective-permute-start.21 = (bf16[128,2560]{1,0:T(8,128)(2,1)S(1)}, bf16[128,2560]{1,0:T(8,128)(2,1)S(1)}, u32[]{:S(2)}, u32[]{:S(2)}) collective-permute-start(bf16[128,2560]{1,0:T(8,128)(2,1)S(1)} %added.8), channel_id=1, source_target_pairs={{1,2},{2,1},{5,6},{6,5},{9,10},{10,9},{13,14},{14,13},{17,18},{18,... | collective-permute-start | bytes 1966088 | tf_op jit(solution)/shard_map/ppermute | solution.py:357
  141.8 26.8 %collective-permute-start.20 = (bf16[128,2560]{1,0:T(8,128)(2,1)S(1)}, bf16[128,2560]{1,0:T(8,128)(2,1)S(1)}, u32[]{:S(2)}, u32[]{:S(2)}) collective-permute-start(bf16[128,2560]{1,0:T(8,128)(2,1)S(1)} %mix.10.refs_0_), channel_id=1, source_target_pairs={{0,1},{3,2},{4,5},{7,6},{8,9},{11,10},{12,13},{15,14},{16,17},{19,... | collective-permute-start | bytes 1966088 | tf_op jit(solution)/shard_map/ppermute | solution.py:363
  154.7 14.8 %collective-permute-start.19 = (bf16[128,2560]{1,0:T(8,128)(2,1)S(1)}, bf16[128,2560]{1,0:T(8,128)(2,1)S(1)}, u32[]{:S(2)}, u32[]{:S(2)}) collective-permute-start(bf16[128,2560]{1,0:T(8,128)(2,1)S(1)} %added.9), channel_id=1, source_target_pairs={{1,2},{2,1},{5,6},{6,5},{9,10},{10,9},{13,14},{14,13},{17,18},{18,... | collective-permute-start | bytes 1966088 | tf_op jit(solution)/shard_map/ppermute | solution.py:357
  155.4 27.2 %collective-permute-start.23 = (bf16[128,2560]{1,0:T(8,128)(2,1)S(1)}, bf16[128,2560]{1,0:T(8,128)(2,1)S(1)}, u32[]{:S(2)}, u32[]{:S(2)}) collective-permute-start(bf16[128,2560]{1,0:T(8,128)(2,1)S(1)} %mix.11.refs_0_), channel_id=1, source_target_pairs={{0,1},{3,2},{4,5},{7,6},{8,9},{11,10},{12,13},{15,14},{16,17},{19,... | collective-permute-start | bytes 1966088 | tf_op jit(solution)/shard_map/ppermute | solution.py:363
  166.4 30.3 %collective-permute-start.25 = (bf16[128,2560]{1,0:T(8,128)(2,1)S(1)}, bf16[128,2560]{1,0:T(8,128)(2,1)S(1)}, u32[]{:S(2)}, u32[]{:S(2)}) collective-permute-start(bf16[128,2560]{1,0:T(8,128)(2,1)S(1)} %added.10), channel_id=1, source_target_pairs={{0,1},{1,0},{2,3},{3,2},{4,5},{5,4},{6,7},{7,6},{8,9},{9,8},{10,11... | collective-permute-start | bytes 1966088 | tf_op jit(solution)/shard_map/ppermute | solution.py:354
  168.8 19.5 %collective-permute-start.26 = (bf16[128,2560]{1,0:T(8,128)(2,1)S(1)}, bf16[128,2560]{1,0:T(8,128)(2,1)S(1)}, u32[]{:S(2)}, u32[]{:S(2)}) collective-permute-start(bf16[128,2560]{1,0:T(8,128)(2,1)S(1)} %added.11), channel_id=1, source_target_pairs={{1,2},{2,1},{5,6},{6,5},{9,10},{10,9},{13,14},{14,13},{17,18},{18,... | collective-permute-start | bytes 1966088 | tf_op jit(solution)/shard_map/ppermute | solution.py:357
  182.8 15.0 %collective-permute-start.24 = (bf16[128,2560]{1,0:T(8,128)(2,1)S(1)}, bf16[128,2560]{1,0:T(8,128)(2,1)S(1)}, u32[]{:S(2)}, u32[]{:S(2)}) collective-permute-start(bf16[128,2560]{1,0:T(8,128)(2,1)S(1)} %added.13), channel_id=1, source_target_pairs={{1,2},{2,1},{5,6},{6,5},{9,10},{10,9},{13,14},{14,13},{17,18},{18,... | collective-permute-start | bytes 1966088 | tf_op jit(solution)/shard_map/ppermute | solution.py:357
  183.5 26.6 %collective-permute-start.22 = (bf16[128,2560]{1,0:T(8,128)(2,1)S(1)}, bf16[128,2560]{1,0:T(8,128)(2,1)S(1)}, u32[]{:S(2)}, u32[]{:S(2)}) collective-permute-start(bf16[128,2560]{1,0:T(8,128)(2,1)S(1)} %added.12), channel_id=1, source_target_pairs={{0,1},{1,0},{2,3},{3,2},{4,5},{5,4},{6,7},{7,6},{8,9},{9,8},{10,11... | collective-permute-start | bytes 1966088 | tf_op jit(solution)/shard_map/ppermute | solution.py:354

commit v5 on v4

--- a/solution.py
+++ b/solution.py
@@ -379,15 +379,20 @@
     for array in mine:
         from_near.append(swap(array))
         from_mid.append(across(array))
-    accs = partial_projection(places, OWN, [[hidden_in]], weights, None)
+    cue = (from_near[0], from_mid[0])
+    accs = partial_projection(after(places, cue), OWN, [[hidden_in]], weights, None)
+    from_near[1], from_mid[1], accs = lax.optimization_barrier((from_near[1], from_mid[1], accs))
     to_inner = [across(array) for array in from_near]
     to_outer = [outward(array) for array in from_mid]
-    from_near[1], accs = lax.optimization_barrier((from_near[1], accs))
-    accs = partial_projection(places, NEAR, [[a] for a in from_near], weights, accs)
-    to_inner[0], accs = lax.optimization_barrier((to_inner[0], accs))
+    cue = (from_near[1], from_mid[1])
+    accs = partial_projection(
+        after(places, cue), NEAR, [[a] for a in from_near], weights, accs
+    )
+    to_inner[1], accs = lax.optimization_barrier((to_inner[1], accs))
     end = [outward(array) for array in to_inner]
+    cue = tuple(to_inner)
     accs = partial_projection(
-        places, THIRD, [[a, b] for a, b in zip(from_mid, to_outer)], weights, accs
+        after(places, cue), THIRD, [[a, b] for a, b in zip(from_mid, to_outer)], weights, accs
     )
 
     final = [[a, b] for a, b in zip(to_inner, end)]

time: 212 us -> 206 us (0.972)
  waiting for transfers between devices: 106 us -> 100 us
  Pallas kernels: 53.2 us -> 50.9 us
    ppermute x4, waiting for transfers between devices: 45.3 us -> 34 us  [swap(): return lax.ppermute(array, 'tensor', [(0, 1), (1, 0), (2, 3), (3, 2)])]
    ppermute x4, waiting for transfers between devices: 41.1 us -> 46.2 us  [outward(): return lax.ppermute(array, 'tensor', [(1, 0), (2, 3)])]
    ppermute x4, starting transfers between devices: 7.86 us -> 11.1 us  [swap(): return lax.ppermute(array, 'tensor', [(0, 1), (1, 0), (2, 3), (3, 2)])]
where the time goes in v5:
time: 206 us; the launch traced here: 205 us
  waiting for transfers between devices  100 us (49%)
  Pallas kernels  50.9 us (25%)
  starting transfers between devices  45 us (22%)
  local copies, waits for them, and re-layouts  7.95 us (4%)
    ppermute x4, waiting for transfers between devices, outward(): return lax.ppermute(array, 'tensor', [(1, 0), (2, 3)])  46.2 us
    ppermute x4, waiting for transfers between devices, swap(): return lax.ppermute(array, 'tensor', [(0, 1), (1, 0), (2, 3), (3, 2)])  34 us
    ppermute x4, waiting for transfers between devices, inward(): return lax.ppermute(array, 'tensor', [(0, 1), (3, 2)])  18.3 us
    pallas_call x8, Pallas kernels, mix(): pl.pallas_call(mix_kernel, grid=(tiles,), in_specs=[whole(rows, depth), p...  16.5 us
    ppermute x4, starting transfers between devices, inward(): return lax.ppermute(array, 'tensor', [(0, 1), (3, 2)])  15.1 us
    pallas_call x3, Pallas kernels, partial_projection(): pl.pallas_call(functools.partial(partial_kernel, [len(part) for part in p...  12.7 us
    pallas_call x2, Pallas kernels, attention(): pl.pallas_call(functools.partial(attention_kernel, slots, n_parts, len(ot...  11.2 us
    ppermute x4, starting transfers between devices, swap(): return lax.ppermute(array, 'tensor', [(0, 1), (1, 0), (2, 3), (3, 2)])  11.1 us
  transfers between devices with their start and end apart: 27, of which 12 were waited for; matrix products, arithmetic and copies ran while one was open for 0% of the time, Pallas kernels for 21%

profile of v5, /device:TPU:0, one launch (start us, length us, event | category | flops | bytes accessed | tf_op | source)
XLA Modules:
  0.0 205.2 jit_solution(7992348260689531755)
XLA Ops:
  0.0 2.6 %fusion = (bf16[256,1280]{1,0:T(8,128)(2,1)}, bf16[256,1280]{1,0:T(8,128)(2,1)}) fusion(bf16[512,1280]{1,0:T(8,128)(2,1)} %refs_0_.1), kind=kLoop, calls=%fused_computation.1 | loop fusion | bytes 2621440 | tf_op jit(solution)/shard_map/slice | solution.py:377
  2.6 3.0 %collective-permute-start = (bf16[256,1280]{1,0:T(8,128)(2,1)}, bf16[256,1280]{1,0:T(8,128)(2,1)S(1)}, u32[]{:S(2)}, u32[]{:S(2)}) collective-permute-start(bf16[256,1280]{1,0:T(8,128)(2,1)} %get-tuple-element.80), channel_id=1, source_target_pairs={{0,1},{1,0},{2,3},{3,2},{4,5},{5,4},{6,7},{7,6},{8,9},{9,8},{10,11... | collective-permute-start | bytes 1966088 | tf_op jit(solution)/shard_map/ppermute | solution.py:354
  5.6 1.5 collective-permute-start.5
  7.1 3.6 %collective-permute-start.3 = (bf16[256,1280]{1,0:T(8,128)(2,1)}, bf16[256,1280]{1,0:T(8,128)(2,1)}, u32[]{:S(2)}, u32[]{:S(2)}) collective-permute-start(bf16[256,1280]{1,0:T(8,128)(2,1)} %get-tuple-element.79), channel_id=1, source_target_pairs={{0,1},{1,0},{2,3},{3,2},{4,5},{5,4},{6,7},{7,6},{8,9},{9,8},{10,11... | collective-permute-start | bytes 1966088 | tf_op jit(solution)/shard_map/ppermute | solution.py:354
  10.8 1.5 collective-permute-start.4
  12.3 9.1 %collective-permute-done.refs_0_ = bf16[256,1280]{1,0:T(8,128)(2,1)S(1)} collective-permute-done((bf16[256,1280]{1,0:T(8,128)(2,1)}, bf16[256,1280]{1,0:T(8,128)(2,1)S(1)}, u32[]{:S(2)}, u32[]{:S(2)}) %collective-permute-start) | collective-permute-done | bytes 655392 | tf_op jit(solution)/shard_map/ppermute | solution.py:354
  21.4 4.0 %copy-done = bf16[5120,1024]{1,0:T(8,128)(2,1)S(1)} copy-done((bf16[5120,1024]{1,0:T(8,128)(2,1)S(1)}, bf16[5120,1024]{1,0:T(8,128)(2,1)}, u32[]{:S(2)}) %copy-start) | copy-done | bytes 10485784
  25.4 1.3 copy-done.4
  26.7 3.4 %partial_projection.3 = (f32[512,1024]{1,0:T(8,128)S(1)}, f32[512,128]{1,0:T(8,128)S(1)}, f32[512,128]{1,0:T(8,128)S(1)}) custom-call(s32[4]{0:T(128)S(1)} %pad_add_fusion.places_ref, bf16[512,1280]{1,0:T(8,128)(2,1)S(1)} %copy-done.4, bf16[5120,1024]{1,0:T(8,128)(2,1)S(1)} %copy-done, bf16[5120,128]{1,0:T(8,128)(2,1)S(1)} %copy-done.2, ...), custom_call_target="tpu_custom_call" | custom-call | flops 1 | bytes 1 | tf_op jit(solution)/shard_map/partial_projection/pallas_call | solution.py:95
  30.2 0.7 collective-permute-start.1
  30.9 3.9 %collective-permute-done.3.refs_1_ = bf16[256,1280]{1,0:T(8,128)(2,1)} collective-permute-done((bf16[256,1280]{1,0:T(8,128)(2,1)}, bf16[256,1280]{1,0:T(8,128)(2,1)}, u32[]{:S(2)}, u32[]{:S(2)}) %collective-permute-start.3) | collective-permute-done | bytes 655392 | tf_op jit(solution)/shard_map/ppermute | solution.py:354
  34.7 0.7 collective-permute-start.6
  35.4 1.3 collective-permute-start.8
  36.7 1.3 collective-permute-start.7
  38.0 1.3 collective-permute-start.2
  39.3 4.5 %partial_projection.4 = (f32[512,1024]{1,0:T(8,128)S(1)}, f32[512,128]{1,0:T(8,128)S(1)}, f32[512,128]{1,0:T(8,128)S(1)}) custom-call(s32[4]{0:T(128)S(1)} %pad_add_fusion.places_ref, bf16[256,1280]{1,0:T(8,128)(2,1)S(1)} %collective-permute-done.refs_0_, bf16[256,1280]{1,0:T(8,128)(2,1)} %collective-permute-done.3.refs_1_, ...), custom_call_target="tpu_custom_call" | custom-call | flops 1 | bytes 1 | tf_op jit(solution)/shard_map/partial_projection/pallas_call | solution.py:95
  43.9 1.4 collective-permute-start.9
  45.4 16.3 %collective-permute-done.8.refs_3_ = bf16[256,1280]{1,0:T(8,128)(2,1)S(1)} collective-permute-done((bf16[256,1280]{1,0:T(8,128)(2,1)}, bf16[256,1280]{1,0:T(8,128)(2,1)S(1)}, u32[]{:S(2)}, u32[]{:S(2)}) %collective-permute-start.8) | collective-permute-done | bytes 655392 | tf_op jit(solution)/shard_map/ppermute | solution.py:360
  61.7 14.0 %collective-permute-done.7.refs_1_ = bf16[256,1280]{1,0:T(8,128)(2,1)S(1)} collective-permute-done((bf16[256,1280]{1,0:T(8,128)(2,1)}, bf16[256,1280]{1,0:T(8,128)(2,1)S(1)}, u32[]{:S(2)}, u32[]{:S(2)}) %collective-permute-start.7) | collective-permute-done | bytes 655392 | tf_op jit(solution)/shard_map/ppermute | solution.py:360
  75.8 4.8 %partial_projection.5 = (f32[512,1024]{1,0:T(8,128)S(1)}, f32[512,128]{1,0:T(8,128)S(1)}, f32[512,128]{1,0:T(8,128)S(1)}) custom-call(s32[4]{0:T(128)S(1)} %pad_add_fusion.places_ref, bf16[256,1280]{1,0:T(8,128)(2,1)} %collective-permute-done.5.refs_0_, bf16[256,1280]{1,0:T(8,128)(2,1)S(1)} %collective-permute-done.7.refs_1_, ...), custom_call_target="tpu_custom_call" | custom-call | flops 1 | bytes 1 | tf_op jit(solution)/shard_map/partial_projection/pallas_call | solution.py:95
  80.5 9.3 %collective-permute-done.2.refs_1_ = bf16[256,1280]{1,0:T(8,128)(2,1)S(1)} collective-permute-done((bf16[256,1280]{1,0:T(8,128)(2,1)S(1)}, bf16[256,1280]{1,0:T(8,128)(2,1)S(1)}, u32[]{:S(2)}, u32[]{:S(2)}) %collective-permute-start.2) | collective-permute-done | bytes 655392 | tf_op jit(solution)/shard_map/ppermute | solution.py:360
  89.8 2.5 %queries.2.refs_0_ = bf16[256,1024]{1,0:T(8,128)(2,1)S(1)} custom-call(s32[4]{0:T(128)S(1)} %pad_add_fusion.places_ref, bf16[256,1280]{1,0:T(8,128)(2,1)S(1)} %collective-permute-done.1.refs_0_, bf16[256,1280]{1,0:T(8,128)(2,1)S(1)} %collective-permute-done.2.refs_1_, bf16[5120,1024]{1,0:T(8,128)(2,1)S(1)} %copy-done.1, ...), custom_call_target="tpu_custom_call" | custom-call | flops 1 | bytes 1 | tf_op jit(solution)/shard_map/queries/pallas_call | solution.py:182
  92.4 1.1 keys_values.2.refs_0_.refs_2_
  93.4 6.6 %collective-permute-done.9.refs_1_.refs_2_ = bf16[256,1280]{1,0:T(8,128)(2,1)S(1)} collective-permute-done((bf16[256,1280]{1,0:T(8,128)(2,1)S(1)}, bf16[256,1280]{1,0:T(8,128)(2,1)S(1)}, u32[]{:S(2)}, u32[]{:S(2)}) %collective-permute-start.9) | collective-permute-done | bytes 655392 | tf_op jit(solution)/shard_map/ppermute | solution.py:360
  100.0 1.3 keys_values.3
  101.4 1.6 collective-permute-start.11
  102.9 0.3 collective-permute-start.12
  103.3 1.5 collective-permute-start.13
  104.8 0.2 collective-permute-start.14
  105.0 2.4 %collective-permute-start.15 = (bf16[128,256]{1,0:T(8,128)(2,1)S(1)}, bf16[128,256]{1,0:T(8,128)(2,1)S(1)}, u32[]{:S(2)}, u32[]{:S(2)}) collective-permute-start(bf16[128,256]{1,0:T(8,128)(2,1)S(1)} %get-tuple-element.66), channel_id=1, source_target_pairs={{0,24},{4,28},{8,16},{12,20},{16,8},{20,12},{24,0},{28,4},{1,25},{... | collective-permute-start | bytes 196616 | tf_op jit(solution)/shard_map/ppermute | solution.py:366
  107.4 0.2 collective-permute-start.16
  108.3 2.5 %queries.3.refs_1_ = bf16[256,1024]{1,0:T(8,128)(2,1)S(1)} custom-call(s32[4]{0:T(128)S(1)} %pad_add_fusion.places_ref, bf16[256,1280]{1,0:T(8,128)(2,1)S(1)} %collective-permute-done.6.refs_0_.refs_1_, bf16[256,1280]{1,0:T(8,128)(2,1)S(1)} %collective-permute-done.9.refs_1_.refs_2_, bf16[5120,1024]{1,0:T(8,128)(2,1)S(1)} %copy-done.1, ...), custom_call_target="tpu_custom_call" | custom-call | flops 1 | bytes 1 | tf_op jit(solution)/shard_map/queries/pallas_call | solution.py:182
  110.9 1.5 collective-permute-done.16.refs_10_
  112.3 3.6 %attention.2.rows_ref = bf16[128,1024]{1,0:T(8,128)(2,1)S(1)} custom-call(s32[4]{0:T(128)S(1)} %pad_add_fusion.places_ref, s32[1]{0:T(128)S(6)} %copy.14.length_ref, bf16[256,1024]{1,0:T(8,128)(2,1)S(1)} %queries.2.refs_0_, bf16[256,1024]{1,0:T(8,128)(2,1)S(1)} %queries.3.refs_1_, bf16[256,256]{1,0:T(8,128)(2,1)S(1)} %keys_values.2.refs_0_.refs_2_, ...), custom_call_target="tpu_custom_call" | custom-call | flops 1 | bytes 1 | tf_op jit(solution)/shard_map/attention/pallas_call | solution.py:271
  116.0 2.1 %mix.8.refs_0_ = bf16[128,2560]{1,0:T(8,128)(2,1)S(1)} custom-call(bf16[128,1024]{1,0:T(8,128)(2,1)S(1)} %attention.2.rows_ref, bf16[1024,5120]{1,0:T(8,128)(2,1)S(1)} %bitcast.7), custom_call_target="tpu_custom_call" | custom-call | flops 1 | bytes 1 | tf_op jit(solution)/shard_map/mix/pallas_call | solution.py:300
  118.0 1.5 collective-permute-start.18
  119.5 2.1 %mix.9.refs_0_ = bf16[128,2560]{1,0:T(8,128)(2,1)S(1)} custom-call(bf16[128,1024]{1,0:T(8,128)(2,1)S(1)} %attention.2.rows_ref, bf16[1024,5120]{1,0:T(8,128)(2,1)S(1)} %bitcast.7), custom_call_target="tpu_custom_call" | custom-call | flops 1 | bytes 1 | tf_op jit(solution)/shard_map/mix/pallas_call | solution.py:300
  121.6 1.5 collective-permute-start.17
  123.1 7.7 %attention.3 = (bf16[128,1024]{1,0:T(8,128)(2,1)S(1)}, bf16[128,1024]{1,0:T(8,128)(2,1)S(1)}, bf16[128,1024]{1,0:T(8,128)(2,1)S(1)}) custom-call(s32[4]{0:T(128)S(1)} %pad_add_fusion.places_ref, s32[1]{0:T(128)S(6)} %copy.14.length_ref, bf16[256,1024]{1,0:T(8,128)(2,1)S(1)} %queries.2.refs_0_, bf16[256,1024]{1,0:T(8,128)(2,1)S(1)} %queries.3.refs_1_, ...), custom_call_target="tpu_custom_call" | custom-call | flops 1 | bytes 1 | tf_op jit(solution)/shard_map/attention/pallas_call | solution.py:271
  130.8 2.1 %mix.10.refs_0_ = bf16[128,2560]{1,0:T(8,128)(2,1)S(1)} custom-call(bf16[128,1024]{1,0:T(8,128)(2,1)S(1)} %get-tuple-element.70.rows_ref, bf16[1024,5120]{1,0:T(8,128)(2,1)S(1)} %bitcast.7), custom_call_target="tpu_custom_call" | custom-call | flops 1 | bytes 1 | tf_op jit(solution)/shard_map/mix/pallas_call | solution.py:300
  132.9 2.1 %mix.11.refs_0_ = bf16[128,2560]{1,0:T(8,128)(2,1)S(1)} custom-call(bf16[128,1024]{1,0:T(8,128)(2,1)S(1)} %get-tuple-element.70.rows_ref, bf16[1024,5120]{1,0:T(8,128)(2,1)S(1)} %bitcast.7), custom_call_target="tpu_custom_call" | custom-call | flops 1 | bytes 1 | tf_op jit(solution)/shard_map/mix/pallas_call | solution.py:300
  134.9 0.2 added.8
  135.1 0.7 collective-permute-start.21
  135.8 5.8 %collective-permute-start.20 = (bf16[128,2560]{1,0:T(8,128)(2,1)S(1)}, bf16[128,2560]{1,0:T(8,128)(2,1)S(1)}, u32[]{:S(2)}, u32[]{:S(2)}) collective-permute-start(bf16[128,2560]{1,0:T(8,128)(2,1)S(1)} %mix.10.refs_0_), channel_id=1, source_target_pairs={{0,1},{3,2},{4,5},{7,6},{8,9},{11,10},{12,13},{15,14},{16,17},{19,... | collective-permute-start | bytes 1966088 | tf_op jit(solution)/shard_map/ppermute | solution.py:363
  141.7 2.1 %mix.12.refs_0_ = bf16[128,2560]{1,0:T(8,128)(2,1)S(1)} custom-call(bf16[128,1024]{1,0:T(8,128)(2,1)S(1)} %get-tuple-element.72.rows_ref, bf16[1024,5120]{1,0:T(8,128)(2,1)S(1)} %bitcast.7), custom_call_target="tpu_custom_call" | custom-call | flops 1 | bytes 1 | tf_op jit(solution)/shard_map/mix/pallas_call | solution.py:300
  143.7 2.1 %mix.13.refs_0_ = bf16[128,2560]{1,0:T(8,128)(2,1)S(1)} custom-call(bf16[128,1024]{1,0:T(8,128)(2,1)S(1)} %get-tuple-element.72.rows_ref, bf16[1024,5120]{1,0:T(8,128)(2,1)S(1)} %bitcast.7), custom_call_target="tpu_custom_call" | custom-call | flops 1 | bytes 1 | tf_op jit(solution)/shard_map/mix/pallas_call | solution.py:300
  145.8 2.8 %collective-permute-done.17.refs_1_ = bf16[128,2560]{1,0:T(8,128)(2,1)S(1)} collective-permute-done((bf16[128,2560]{1,0:T(8,128)(2,1)S(1)}, bf16[128,2560]{1,0:T(8,128)(2,1)S(1)}, u32[]{:S(2)}, u32[]{:S(2)}) %collective-permute-start.17) | collective-permute-done | bytes 655392 | tf_op jit(solution)/shard_map/ppermute | solution.py:363
  148.6 0.2 added.9
  148.7 0.7 collective-permute-start.19
  149.5 6.2 %collective-permute-start.23 = (bf16[128,2560]{1,0:T(8,128)(2,1)S(1)}, bf16[128,2560]{1,0:T(8,128)(2,1)S(1)}, u32[]{:S(2)}, u32[]{:S(2)}) collective-permute-start(bf16[128,2560]{1,0:T(8,128)(2,1)S(1)} %mix.11.refs_0_), channel_id=1, source_target_pairs={{0,1},{3,2},{4,5},{7,6},{8,9},{11,10},{12,13},{15,14},{16,17},{19,... | collective-permute-start | bytes 1966088 | tf_op jit(solution)/shard_map/ppermute | solution.py:363
  155.7 2.1 %mix.14.refs_0_ = bf16[128,2560]{1,0:T(8,128)(2,1)S(1)} custom-call(bf16[128,1024]{1,0:T(8,128)(2,1)S(1)} %get-tuple-element.74.rows_ref, bf16[1024,5120]{1,0:T(8,128)(2,1)S(1)} %bitcast.7), custom_call_target="tpu_custom_call" | custom-call | flops 1 | bytes 1 | tf_op jit(solution)/shard_map/mix/pallas_call | solution.py:300
  157.8 2.1 %mix.15.refs_0_ = bf16[128,2560]{1,0:T(8,128)(2,1)S(1)} custom-call(bf16[128,1024]{1,0:T(8,128)(2,1)S(1)} %get-tuple-element.74.rows_ref, bf16[1024,5120]{1,0:T(8,128)(2,1)S(1)} %bitcast.7), custom_call_target="tpu_custom_call" | custom-call | flops 1 | bytes 1 | tf_op jit(solution)/shard_map/mix/pallas_call | solution.py:300
  159.9 0.2 added.10
  160.1 2.5 %collective-permute-done.20.refs_1_ = bf16[128,2560]{1,0:T(8,128)(2,1)S(1)} collective-permute-done((bf16[128,2560]{1,0:T(8,128)(2,1)S(1)}, bf16[128,2560]{1,0:T(8,128)(2,1)S(1)}, u32[]{:S(2)}, u32[]{:S(2)}) %collective-permute-start.20) | collective-permute-done | bytes 655392 | tf_op jit(solution)/shard_map/ppermute | solution.py:363
  162.6 0.2 added.11
  162.8 0.7 collective-permute-start.26
  163.5 0.2 added.12
  163.7 13.0 %collective-permute-done.23.refs_1_ = bf16[128,2560]{1,0:T(8,128)(2,1)S(1)} collective-permute-done((bf16[128,2560]{1,0:T(8,128)(2,1)S(1)}, bf16[128,2560]{1,0:T(8,128)(2,1)S(1)}, u32[]{:S(2)}, u32[]{:S(2)}) %collective-permute-start.23) | collective-permute-done | bytes 655392 | tf_op jit(solution)/shard_map/ppermute | solution.py:363
  176.8 0.7 collective-permute-start.24
  177.5 4.4 %collective-permute-start.22 = (bf16[128,2560]{1,0:T(8,128)(2,1)S(1)}, bf16[128,2560]{1,0:T(8,128)(2,1)S(1)}, u32[]{:S(2)}, u32[]{:S(2)}) collective-permute-start(bf16[128,2560]{1,0:T(8,128)(2,1)S(1)} %added.12), channel_id=1, source_target_pairs={{0,1},{1,0},{2,3},{3,2},{4,5},{5,4},{6,7},{7,6},{8,9},{9,8},{10,11... | collective-permute-start | bytes 1966088 | tf_op jit(solution)/shard_map/ppermute | solution.py:354
  181.9 8.8 %collective-permute-done.25.refs_1_ = bf16[128,2560]{1,0:T(8,128)(2,1)S(1)} collective-permute-done((bf16[128,2560]{1,0:T(8,128)(2,1)S(1)}, bf16[128,2560]{1,0:T(8,128)(2,1)S(1)}, u32[]{:S(2)}, u32[]{:S(2)}) %collective-permute-start.25) | collective-permute-done | bytes 655392 | tf_op jit(solution)/shard_map/ppermute | solution.py:354
  190.7 1.1 added.14.refs_3_
  191.8 12.3 %collective-permute-done.22.refs_1_ = bf16[128,2560]{1,0:T(8,128)(2,1)S(1)} collective-permute-done((bf16[128,2560]{1,0:T(8,128)(2,1)S(1)}, bf16[128,2560]{1,0:T(8,128)(2,1)S(1)}, u32[]{:S(2)}, u32[]{:S(2)}) %collective-permute-start.22) | collective-permute-done | bytes 655392 | tf_op jit(solution)/shard_map/ppermute | solution.py:354
  204.1 1.1 added.15
  (44 shorter events, 0.5 us)
Async XLA Ops:
  0.0 21.4 %copy-start.2 = (bf16[5120,128]{1,0:T(8,128)(2,1)S(1)}, bf16[5120,128]{1,0:T(8,128)(2,1)}, u32[]{:S(2)}) copy-start(bf16[5120,128]{1,0:T(8,128)(2,1)} %refs_3_.7) | copy-start | bytes 3932164
  0.0 21.4 %copy-start.3 = (bf16[5120,128]{1,0:T(8,128)(2,1)S(1)}, bf16[5120,128]{1,0:T(8,128)(2,1)}, u32[]{:S(2)}) copy-start(bf16[5120,128]{1,0:T(8,128)(2,1)} %refs_4_.5) | copy-start | bytes 3932164
  2.6 18.8 %collective-permute-start = (bf16[256,1280]{1,0:T(8,128)(2,1)}, bf16[256,1280]{1,0:T(8,128)(2,1)S(1)}, u32[]{:S(2)}, u32[]{:S(2)}) collective-permute-start(bf16[256,1280]{1,0:T(8,128)(2,1)} %get-tuple-element.80), channel_id=1, source_target_pairs={{0,1},{1,0},{2,3},{3,2},{4,5},{5,4},{6,7},{7,6},{8,9},{9,8},{10,11... | collective-permute-start | bytes 1966088 | tf_op jit(solution)/shard_map/ppermute | solution.py:354
  5.6 15.8 %collective-permute-start.5 = (bf16[256,1280]{1,0:T(8,128)(2,1)}, bf16[256,1280]{1,0:T(8,128)(2,1)}, u32[]{:S(2)}, u32[]{:S(2)}) collective-permute-start(bf16[256,1280]{1,0:T(8,128)(2,1)} %get-tuple-element.80), channel_id=1, source_target_pairs={{1,2},{2,1},{5,6},{6,5},{9,10},{10,9},{13,14},{14,13},{17,18},{18,... | collective-permute-start | bytes 1966088 | tf_op jit(solution)/shard_map/ppermute | solution.py:357
  7.1 27.6 %collective-permute-start.3 = (bf16[256,1280]{1,0:T(8,128)(2,1)}, bf16[256,1280]{1,0:T(8,128)(2,1)}, u32[]{:S(2)}, u32[]{:S(2)}) collective-permute-start(bf16[256,1280]{1,0:T(8,128)(2,1)} %get-tuple-element.79), channel_id=1, source_target_pairs={{0,1},{1,0},{2,3},{3,2},{4,5},{5,4},{6,7},{7,6},{8,9},{9,8},{10,11... | collective-permute-start | bytes 1966088 | tf_op jit(solution)/shard_map/ppermute | solution.py:354
  10.8 24.0 %collective-permute-start.4 = (bf16[256,1280]{1,0:T(8,128)(2,1)}, bf16[256,1280]{1,0:T(8,128)(2,1)}, u32[]{:S(2)}, u32[]{:S(2)}) collective-permute-start(bf16[256,1280]{1,0:T(8,128)(2,1)} %get-tuple-element.79), channel_id=1, source_target_pairs={{1,2},{2,1},{5,6},{6,5},{9,10},{10,9},{13,14},{14,13},{17,18},{18,... | collective-permute-start | bytes 1966088 | tf_op jit(solution)/shard_map/ppermute | solution.py:357
  21.4 4.0 %copy-start = (bf16[5120,1024]{1,0:T(8,128)(2,1)S(1)}, bf16[5120,1024]{1,0:T(8,128)(2,1)}, u32[]{:S(2)}) copy-start(bf16[5120,1024]{1,0:T(8,128)(2,1)} %refs_2_.8) | copy-start | bytes 31457284
  25.4 1.3 copy-start.4
  26.7 12.6 %copy-start.1 = (bf16[5120,1024]{1,0:T(8,128)(2,1)S(1)}, bf16[5120,1024]{1,0:T(8,128)(2,1)}, u32[]{:S(2)}) copy-start(bf16[5120,1024]{1,0:T(8,128)(2,1)} %refs_2_.8) | copy-start | bytes 31457284
  30.2 7.9 %collective-permute-start.1 = (bf16[256,1280]{1,0:T(8,128)(2,1)S(1)}, bf16[256,1280]{1,0:T(8,128)(2,1)S(1)}, u32[]{:S(2)}, u32[]{:S(2)}) collective-permute-start(bf16[256,1280]{1,0:T(8,128)(2,1)S(1)} %collective-permute-done.refs_0_), channel_id=1, source_target_pairs={{1,2},{2,1},{5,6},{6,5},{9,10},{10,9},{13,14},{14,13},{17,18},{18,... | collective-permute-start | bytes 1966088 | tf_op jit(solution)/shard_map/ppermute | solution.py:357
  34.7 9.2 %collective-permute-start.6 = (bf16[256,1280]{1,0:T(8,128)(2,1)}, bf16[256,1280]{1,0:T(8,128)(2,1)S(1)}, u32[]{:S(2)}, u32[]{:S(2)}) collective-permute-start(bf16[256,1280]{1,0:T(8,128)(2,1)} %collective-permute-done.3.refs_1_), channel_id=1, source_target_pairs={{1,2},{2,1},{5,6},{6,5},{9,10},{10,9},{13,14},{14,13},{17,18},{18,... | collective-permute-start | bytes 1966088 | tf_op jit(solution)/shard_map/ppermute | solution.py:357
  35.4 26.3 %collective-permute-start.8 = (bf16[256,1280]{1,0:T(8,128)(2,1)}, bf16[256,1280]{1,0:T(8,128)(2,1)S(1)}, u32[]{:S(2)}, u32[]{:S(2)}) collective-permute-start(bf16[256,1280]{1,0:T(8,128)(2,1)} %collective-permute-done.4.refs_2_), channel_id=1, source_target_pairs={{1,0},{2,3},{5,4},{6,7},{9,8},{10,11},{13,12},{14,15},{17,16},{18,... | collective-permute-start | bytes 1966088 | tf_op jit(solution)/shard_map/ppermute | solution.py:360
  36.7 39.0 %collective-permute-start.7 = (bf16[256,1280]{1,0:T(8,128)(2,1)}, bf16[256,1280]{1,0:T(8,128)(2,1)S(1)}, u32[]{:S(2)}, u32[]{:S(2)}) collective-permute-start(bf16[256,1280]{1,0:T(8,128)(2,1)} %collective-permute-done.5.refs_0_), channel_id=1, source_target_pairs={{1,0},{2,3},{5,4},{6,7},{9,8},{10,11},{13,12},{14,15},{17,16},{18,... | collective-permute-start | bytes 1966088 | tf_op jit(solution)/shard_map/ppermute | solution.py:360
  38.0 51.8 %collective-permute-start.2 = (bf16[256,1280]{1,0:T(8,128)(2,1)S(1)}, bf16[256,1280]{1,0:T(8,128)(2,1)S(1)}, u32[]{:S(2)}, u32[]{:S(2)}) collective-permute-start(bf16[256,1280]{1,0:T(8,128)(2,1)S(1)} %collective-permute-done.1.refs_0_), channel_id=1, source_target_pairs={{1,0},{2,3},{5,4},{6,7},{9,8},{10,11},{13,12},{14,15},{17,16},{18,... | collective-permute-start | bytes 1966088 | tf_op jit(solution)/shard_map/ppermute | solution.py:360
  43.9 45.9 %copy-start.5 = (f32[512,128]{1,0:T(8,128)S(1)}, f32[512,128]{1,0:T(8,128)}, u32[]{:S(2)}) copy-start(f32[512,128]{1,0:T(8,128)} %constant.16.clone.refs_5_.refs_7_.refs_8_) | copy-start | bytes 786436
  43.9 45.9 %copy-start.6 = (f32[512,128]{1,0:T(8,128)S(1)}, f32[512,128]{1,0:T(8,128)}, u32[]{:S(2)}) copy-start(f32[512,128]{1,0:T(8,128)} %constant.17.clone.refs_6_.refs_8_.refs_9_) | copy-start | bytes 786436
  43.9 45.9 %copy-start.8 = (f32[128]{0:T(128)S(1)}, f32[128]{0:T(128)}, u32[]{:S(2)}) copy-start(f32[128]{0:T(128)} %param.18) | copy-start | bytes 1540
  43.9 56.1 %collective-permute-start.9 = (bf16[256,1280]{1,0:T(8,128)(2,1)S(1)}, bf16[256,1280]{1,0:T(8,128)(2,1)S(1)}, u32[]{:S(2)}, u32[]{:S(2)}) collective-permute-start(bf16[256,1280]{1,0:T(8,128)(2,1)S(1)} %collective-permute-done.6.refs_0_.refs_1_), channel_id=1, source_target_pairs={{1,0},{2,3},{5,4},{6,7},{9,8},{10,11},{13,12},{14,15},{17,16},{18,... | collective-permute-start | bytes 1966088 | tf_op jit(solution)/shard_map/ppermute | solution.py:360
  89.8 2.5 %copy-start.7 = (f32[128]{0:T(128)S(1)}, f32[128]{0:T(128)}, u32[]{:S(2)}) copy-start(f32[128]{0:T(128)} %param.19) | copy-start | bytes 1540
  92.3 7.7 %copy-start.9 = (s32[1,128]{1,0:T(1,128)S(1)}, s32[1,128]{1,0:T(1,128)}, u32[]{:S(2)}) copy-start(s32[1,128]{1,0:T(1,128)} %refs_10_.1) | copy-start | bytes 1540
  100.0 15.9 %slice-start = ((s8[10485760]{0:T(1024)(128)(4,1)}), s8[4194304]{0:T(1024)(128)(4,1)S(1)}, s32[]{:S(2)}) async-start(s8[10485760]{0:T(1024)(128)(4,1)} %bitcast.6), calls=%async_computation | async-start | bytes 8388608
  101.3 3.6 %collective-permute-start.10 = (bf16[128,256]{1,0:T(8,128)(2,1)S(1)}, bf16[128,256]{1,0:T(8,128)(2,1)S(1)}, u32[]{:S(2)}, u32[]{:S(2)}) collective-permute-start(bf16[128,256]{1,0:T(8,128)(2,1)S(1)} %get-tuple-element.66), channel_id=1, source_target_pairs={{0,4},{4,0},{8,12},{12,8},{16,20},{20,16},{24,28},{28,24},{1,5},{5... | collective-permute-start | bytes 196616 | tf_op jit(solution)/shard_map/ppermute | solution.py:366
  101.4 6.0 %collective-permute-start.11 = (bf16[128,256]{1,0:T(8,128)(2,1)S(1)}, bf16[128,256]{1,0:T(8,128)(2,1)S(1)}, u32[]{:S(2)}, u32[]{:S(2)}) collective-permute-start(bf16[128,256]{1,0:T(8,128)(2,1)S(1)} %get-tuple-element.66), channel_id=1, source_target_pairs={{0,8},{4,12},{8,0},{12,4},{16,24},{20,28},{24,16},{28,20},{1,9},{5... | collective-permute-start | bytes 196616 | tf_op jit(solution)/shard_map/ppermute | solution.py:366
  102.9 7.9 %collective-permute-start.12 = (bf16[128,256]{1,0:T(8,128)(2,1)S(1)}, bf16[128,256]{1,0:T(8,128)(2,1)S(1)}, u32[]{:S(2)}, u32[]{:S(2)}) collective-permute-start(bf16[128,256]{1,0:T(8,128)(2,1)S(1)} %get-tuple-element.66), channel_id=1, source_target_pairs={{0,12},{4,8},{8,4},{12,0},{16,28},{20,24},{24,20},{28,16},{1,13},{... | collective-permute-start | bytes 196616 | tf_op jit(solution)/shard_map/ppermute | solution.py:366
  103.3 7.6 %collective-permute-start.13 = (bf16[128,256]{1,0:T(8,128)(2,1)S(1)}, bf16[128,256]{1,0:T(8,128)(2,1)S(1)}, u32[]{:S(2)}, u32[]{:S(2)}) collective-permute-start(bf16[128,256]{1,0:T(8,128)(2,1)S(1)} %get-tuple-element.66), channel_id=1, source_target_pairs={{0,16},{4,20},{8,24},{12,28},{16,0},{20,4},{24,8},{28,12},{1,17},{... | collective-permute-start | bytes 196616 | tf_op jit(solution)/shard_map/ppermute | solution.py:366
  104.8 6.1 %collective-permute-start.14 = (bf16[128,256]{1,0:T(8,128)(2,1)S(1)}, bf16[128,256]{1,0:T(8,128)(2,1)S(1)}, u32[]{:S(2)}, u32[]{:S(2)}) collective-permute-start(bf16[128,256]{1,0:T(8,128)(2,1)S(1)} %get-tuple-element.66), channel_id=1, source_target_pairs={{0,20},{4,16},{8,28},{12,24},{16,4},{20,0},{24,12},{28,8},{1,21},{... | collective-permute-start | bytes 196616 | tf_op jit(solution)/shard_map/ppermute | solution.py:366
  105.0 5.9 %collective-permute-start.15 = (bf16[128,256]{1,0:T(8,128)(2,1)S(1)}, bf16[128,256]{1,0:T(8,128)(2,1)S(1)}, u32[]{:S(2)}, u32[]{:S(2)}) collective-permute-start(bf16[128,256]{1,0:T(8,128)(2,1)S(1)} %get-tuple-element.66), channel_id=1, source_target_pairs={{0,24},{4,28},{8,16},{12,20},{16,8},{20,12},{24,0},{28,4},{1,25},{... | collective-permute-start | bytes 196616 | tf_op jit(solution)/shard_map/ppermute | solution.py:366
  107.4 4.9 %collective-permute-start.16 = (bf16[128,256]{1,0:T(8,128)(2,1)S(1)}, bf16[128,256]{1,0:T(8,128)(2,1)S(1)}, u32[]{:S(2)}, u32[]{:S(2)}) collective-permute-start(bf16[128,256]{1,0:T(8,128)(2,1)S(1)} %get-tuple-element.66), channel_id=1, source_target_pairs={{0,28},{4,24},{8,20},{12,16},{16,12},{20,8},{24,4},{28,0},{1,29},{... | collective-permute-start | bytes 196616 | tf_op jit(solution)/shard_map/ppermute | solution.py:366
  108.3 7.6 %slice-start.1 = ((s8[10485760]{0:T(1024)(128)(4,1)}), s8[4194304]{0:T(1024)(128)(4,1)S(1)}, s32[]{:S(2)}) async-start(s8[10485760]{0:T(1024)(128)(4,1)} %bitcast.6), calls=%async_computation.1 | async-start | bytes 8388608
  108.3 7.6 %slice-start.2 = ((s8[10485760]{0:T(1024)(128)(4,1)}), s8[2097152]{0:T(1024)(128)(4,1)S(1)}, s32[]{:S(2)}) async-start(s8[10485760]{0:T(1024)(128)(4,1)} %bitcast.6), calls=%async_computation.2 | async-start | bytes 4194304
  118.0 16.9 %collective-permute-start.18 = (bf16[128,2560]{1,0:T(8,128)(2,1)S(1)}, bf16[128,2560]{1,0:T(8,128)(2,1)S(1)}, u32[]{:S(2)}, u32[]{:S(2)}) collective-permute-start(bf16[128,2560]{1,0:T(8,128)(2,1)S(1)} %mix.8.refs_0_), channel_id=1, source_target_pairs={{0,1},{3,2},{4,5},{7,6},{8,9},{11,10},{12,13},{15,14},{16,17},{19,... | collective-permute-start | bytes 1966088 | tf_op jit(solution)/shard_map/ppermute | solution.py:363
  121.6 27.0 %collective-permute-start.17 = (bf16[128,2560]{1,0:T(8,128)(2,1)S(1)}, bf16[128,2560]{1,0:T(8,128)(2,1)S(1)}, u32[]{:S(2)}, u32[]{:S(2)}) collective-permute-start(bf16[128,2560]{1,0:T(8,128)(2,1)S(1)} %mix.9.refs_0_), channel_id=1, source_target_pairs={{0,1},{3,2},{4,5},{7,6},{8,9},{11,10},{12,13},{15,14},{16,17},{19,... | collective-permute-start | bytes 1966088 | tf_op jit(solution)/shard_map/ppermute | solution.py:363
  135.1 24.8 %collective-permute-start.21 = (bf16[128,2560]{1,0:T(8,128)(2,1)S(1)}, bf16[128,2560]{1,0:T(8,128)(2,1)S(1)}, u32[]{:S(2)}, u32[]{:S(2)}) collective-permute-start(bf16[128,2560]{1,0:T(8,128)(2,1)S(1)} %added.8), channel_id=1, source_target_pairs={{1,2},{2,1},{5,6},{6,5},{9,10},{10,9},{13,14},{14,13},{17,18},{18,... | collective-permute-start | bytes 1966088 | tf_op jit(solution)/shard_map/ppermute | solution.py:357
  135.8 26.8 %collective-permute-start.20 = (bf16[128,2560]{1,0:T(8,128)(2,1)S(1)}, bf16[128,2560]{1,0:T(8,128)(2,1)S(1)}, u32[]{:S(2)}, u32[]{:S(2)}) collective-permute-start(bf16[128,2560]{1,0:T(8,128)(2,1)S(1)} %mix.10.refs_0_), channel_id=1, source_target_pairs={{0,1},{3,2},{4,5},{7,6},{8,9},{11,10},{12,13},{15,14},{16,17},{19,... | collective-permute-start | bytes 1966088 | tf_op jit(solution)/shard_map/ppermute | solution.py:363
  148.7 14.8 %collective-permute-start.19 = (bf16[128,2560]{1,0:T(8,128)(2,1)S(1)}, bf16[128,2560]{1,0:T(8,128)(2,1)S(1)}, u32[]{:S(2)}, u32[]{:S(2)}) collective-permute-start(bf16[128,2560]{1,0:T(8,128)(2,1)S(1)} %added.9), channel_id=1, source_target_pairs={{1,2},{2,1},{5,6},{6,5},{9,10},{10,9},{13,14},{14,13},{17,18},{18,... | collective-permute-start | bytes 1966088 | tf_op jit(solution)/shard_map/ppermute | solution.py:357
  149.5 27.2 %collective-permute-start.23 = (bf16[128,2560]{1,0:T(8,128)(2,1)S(1)}, bf16[128,2560]{1,0:T(8,128)(2,1)S(1)}, u32[]{:S(2)}, u32[]{:S(2)}) collective-permute-start(bf16[128,2560]{1,0:T(8,128)(2,1)S(1)} %mix.11.refs_0_), channel_id=1, source_target_pairs={{0,1},{3,2},{4,5},{7,6},{8,9},{11,10},{12,13},{15,14},{16,17},{19,... | collective-permute-start | bytes 1966088 | tf_op jit(solution)/shard_map/ppermute | solution.py:363
  160.0 30.7 %collective-permute-start.25 = (bf16[128,2560]{1,0:T(8,128)(2,1)S(1)}, bf16[128,2560]{1,0:T(8,128)(2,1)S(1)}, u32[]{:S(2)}, u32[]{:S(2)}) collective-permute-start(bf16[128,2560]{1,0:T(8,128)(2,1)S(1)} %added.10), channel_id=1, source_target_pairs={{0,1},{1,0},{2,3},{3,2},{4,5},{5,4},{6,7},{7,6},{8,9},{9,8},{10,11... | collective-permute-start | bytes 1966088 | tf_op jit(solution)/shard_map/ppermute | solution.py:354
  162.8 19.1 %collective-permute-start.26 = (bf16[128,2560]{1,0:T(8,128)(2,1)S(1)}, bf16[128,2560]{1,0:T(8,128)(2,1)S(1)}, u32[]{:S(2)}, u32[]{:S(2)}) collective-permute-start(bf16[128,2560]{1,0:T(8,128)(2,1)S(1)} %added.11), channel_id=1, source_target_pairs={{1,2},{2,1},{5,6},{6,5},{9,10},{10,9},{13,14},{14,13},{17,18},{18,... | collective-permute-start | bytes 1966088 | tf_op jit(solution)/shard_map/ppermute | solution.py:357
  176.8 15.0 %collective-permute-start.24 = (bf16[128,2560]{1,0:T(8,128)(2,1)S(1)}, bf16[128,2560]{1,0:T(8,128)(2,1)S(1)}, u32[]{:S(2)}, u32[]{:S(2)}) collective-permute-start(bf16[128,2560]{1,0:T(8,128)(2,1)S(1)} %added.13), channel_id=1, source_target_pairs={{1,2},{2,1},{5,6},{6,5},{9,10},{10,9},{13,14},{14,13},{17,18},{18,... | collective-permute-start | bytes 1966088 | tf_op jit(solution)/shard_map/ppermute | solution.py:357
  177.5 26.6 %collective-permute-start.22 = (bf16[128,2560]{1,0:T(8,128)(2,1)S(1)}, bf16[128,2560]{1,0:T(8,128)(2,1)S(1)}, u32[]{:S(2)}, u32[]{:S(2)}) collective-permute-start(bf16[128,2560]{1,0:T(8,128)(2,1)S(1)} %added.12), channel_id=1, source_target_pairs={{0,1},{1,0},{2,3},{3,2},{4,5},{5,4},{6,7},{7,6},{8,9},{9,8},{10,11... | collective-permute-start | bytes 1966088 | tf_op jit(solution)/shard_map/ppermute | solution.py:354

commit v6 on v5

--- a/solution.py
+++ b/solution.py
@@ -10,7 +10,8 @@
 
 MIB = 1024 * 1024
 LOG2E = 1.4426950408889634
-OWN, NEAR, THIRD, LAST = range(4)
+OWN, NEAR, THIRD, LAST, EIGHTHS = range(5)
+OFFSETS = (0, 6, 2, 4, 1, 7, 3, 5)
 
 
 def rope_tables(rows, width):
@@ -312,6 +313,62 @@
     )(attended, w_out)
 
 
+def eighths_kernel(places_ref, w_ref, out_ref):
+    out_ref[...] = w_ref[...]
+
+
+def eighths(places, w_out, share):
+    width = w_out.shape[1] // 2
+    return pl.pallas_call(
+        eighths_kernel,
+        grid_spec=pltpu.PrefetchScalarGridSpec(
+            num_scalar_prefetch=1,
+            grid=(2,),
+            in_specs=[pl.BlockSpec((share, width), lambda i, p: (p[EIGHTHS + i], 1))],
+            out_specs=pl.BlockSpec((share, width), lambda i, p: (i, 0)),
+        ),
+        out_shape=jax.ShapeDtypeStruct((2 * share, width), w_out.dtype),
+        compiler_params=params(8),
+        cost_estimate=cost(1),
+        name="eighths",
+    )(places, w_out)
+
+
+def mix_sent_kernel(places_ref, rows_ref, *refs):
+    pieces, out_ref = refs[:-1], refs[-1]
+    share = rows_ref.shape[1] // len(OFFSETS)
+    rows = []
+    for index in range(len(OFFSETS)):
+        start = pl.multiple_of(places_ref[EIGHTHS + index] * share, share)
+        rows.append(rows_ref[:, pl.ds(start, share)])
+    total = jnp.dot(
+        jnp.concatenate(rows, axis=1),
+        jnp.concatenate([piece[...] for piece in pieces], axis=0),
+        preferred_element_type=jnp.float32,
+    )
+    out_ref[...] = total.astype(out_ref.dtype)
+
+
+def mix_sent(places, attended, pieces):
+    rows, depth = attended.shape
+    width = pieces[0].shape[1]
+    tile = width // 5
+    column = lambda height: pl.BlockSpec((height, tile), lambda i, p: (0, i))
+    return pl.pallas_call(
+        mix_sent_kernel,
+        grid_spec=pltpu.PrefetchScalarGridSpec(
+            num_scalar_prefetch=1,
+            grid=(width // tile,),
+            in_specs=[whole(rows, depth)] + [column(piece.shape[0]) for piece in pieces],
+            out_specs=column(rows),
+        ),
+        out_shape=jax.ShapeDtypeStruct((rows, width), jnp.bfloat16),
+        compiler_params=params(8),
+        cost_estimate=cost(1),
+        name="mix_sent",
+    )(places, attended, *pieces)
+
+
 def add_kernel(count, *refs):
     total = refs[0][...].astype(jnp.float32)
     for ref in refs[1:count]:
@@ -367,8 +424,11 @@
 
     low = place < 2
     near = jnp.bitwise_xor(place, 1)
-    places = jnp.stack([place, near, jnp.where(low, 2, 1), jnp.where(low, 3, 0)])
-    places = places.astype(jnp.int32)
+    places = [place, near, jnp.where(low, 2, 1), jnp.where(low, 3, 0)]
+    places += [jnp.bitwise_xor(lax.axis_index("cand"), offset) for offset in OFFSETS]
+    places = jnp.stack(places).astype(jnp.int32)
+    share = w_out.shape[0] // n_cand
+    spread = n_cand == len(OFFSETS) and share % 128 == 0
     tables = rope_tables(rows_here, head_width)
     k_gain, q_gain = k_gain[None], q_gain[None]
     weights = [w_query, w_key, w_value]
@@ -379,18 +439,23 @@
     for array in mine:
         from_near.append(swap(array))
         from_mid.append(across(array))
+    to_outer = [outward(array) for array in from_mid]
+    to_inner = [across(from_near[0])]
     cue = (from_near[0], from_mid[0])
     accs = partial_projection(after(places, cue), OWN, [[hidden_in]], weights, None)
-    from_near[1], from_mid[1], accs = lax.optimization_barrier((from_near[1], from_mid[1], accs))
-    to_inner = [across(array) for array in from_near]
-    to_outer = [outward(array) for array in from_mid]
+    pieces = []
+    if spread:
+        pieces.append(inward(after(eighths(places, w_out, share), from_near[0])))
+    from_near[1], accs = lax.optimization_barrier((from_near[1], accs))
+    to_inner.append(across(after(from_near[1], to_outer[0])))
     cue = (from_near[1], from_mid[1])
     accs = partial_projection(
         after(places, cue), NEAR, [[a] for a in from_near], weights, accs
     )
-    to_inner[1], accs = lax.optimization_barrier((to_inner[1], accs))
-    end = [outward(array) for array in to_inner]
-    cue = tuple(to_inner)
+    end = [outward(to_inner[0]), outward(after(to_inner[1], (to_outer[1], accs)))]
+    if spread:
+        pieces.append(between(pieces[0], OFFSETS[2]))
+    cue = (to_inner, accs)
     accs = partial_projection(
         after(places, cue), THIRD, [[a, b] for a, b in zip(from_mid, to_outer)], weights, accs
     )
@@ -420,6 +485,7 @@
     def mixed(rows):
         return [mix(rows, w_out, which) for which in (0, 1)]
 
+    places, pieces = lax.optimization_barrier((places, pieces))
     (far_rows,) = attend((LAST,))
     far = mixed(far_rows)
     places = after(places, far)
@@ -427,9 +493,10 @@
     mid = mixed(third_rows)
     far_in = [inward(array) for array in far]
     mid_in = [inward(array) for array in mid]
-    far_sum = [added(far[0], after(far_in[0], mid))]
-    near_part = mixed(after(near_rows, far_sum[0]))
-    far_sum.append(added(far[1], after(far_in[1], near_part)))
+
+    far_sum = added(far[0], after(far_in[0], mid))
+    near_part = mixed(after(near_rows, far_sum))
+    far_sum = [far_sum, added(far[1], after(far_in[1], near_part))]
     kept = mixed(after(own_rows, far_sum[1]))
     far_sum = [across(array) for array in far_sum]
     near_sum, mid_sum = [None, None], [None, None]
@@ -438,9 +505,18 @@
         near_sum[i] = added(near_part[i], after(far_sum[i], cue))
         mid_sum[i] = added(mid[i], after(mid_in[i], near_sum[i]))
         cue = mid_sum[i]
-    near_sum = [swap(array) for array in near_sum]
     mid_sum = [across(array) for array in mid_sum]
-    result = added(kept[0], near_sum[0], mid_sum[0], half=0)
+    if spread:
+        kept[0] = added(kept[0], mid_sum[0])
+        near_in = inward(near_rows)
+        pieces += [between(after(piece, cue), 1) for piece in pieces]
+        near_in, near_sum[0], _ = lax.optimization_barrier((near_in, near_sum[0], (cue, kept[0])))
+        near_sum = [swap(near_sum[0]), outward(near_sum[1])]
+        kept[1] = added(kept[1], mix_sent(places, near_in, pieces))
+        result = added(kept[0], near_sum[0], half=0)
+    else:
+        near_sum = [swap(array) for array in near_sum]
+        result = added(kept[0], near_sum[0], mid_sum[0], half=0)
     return added(kept[1], near_sum[1], mid_sum[1], half=1, into=result)
 
 

time: 206 us -> 233 us (1.13)
  waiting for transfers between devices: 100 us -> 125 us
  Pallas kernels: 50.9 us -> 53.3 us
    ppermute x4 -> x3, waiting for transfers between devices: 34 us -> 55.1 us  [swap(): return lax.ppermute(array, 'tensor', [(0, 1), (1, 0), (2, 3), (3, 2)])]
    ppermute x4 -> x6, waiting for transfers between devices: 18.3 us -> 26.8 us  [inward(): return lax.ppermute(array, 'tensor', [(0, 1), (3, 2)])]
    ppermute x4 -> x3, starting transfers between devices: 11.1 us -> 5.58 us  [swap(): return lax.ppermute(array, 'tensor', [(0, 1), (1, 0), (2, 3), (3, 2)])]
    ppermute x4 -> x5, waiting for transfers between devices: 46.2 us -> 40.8 us  [outward(): return lax.ppermute(array, 'tensor', [(1, 0), (2, 3)])]
    pallas_call x0 -> x2, Pallas kernels: none -> 3.45 us  [the longest x1 2.66 us: mix_sent(): pl.pallas_call(mix_sent_kernel, grid_spec=pltpu.PrefetchScalarGridSpec(nu...]
    ppermute x4 -> x6, starting transfers between devices: 15.1 us -> 18.5 us  [inward(): return lax.ppermute(array, 'tensor', [(0, 1), (3, 2)])]
    ppermute x7 -> x10, starting transfers between devices: 6.32 us -> 8.65 us  [between(): return lax.ppermute(array, 'cand', [(i, i ^ offset) for i in range(n_cand)])]
    ppermute x4 -> x5, starting transfers between devices: 5.3 us -> 6.58 us  [outward(): return lax.ppermute(array, 'tensor', [(1, 0), (2, 3)])]
  transfers between devices with their start and end apart: 27 -> 32, of which waited for: 12 -> 13; matrix products, arithmetic and copies ran while one was open for 0% -> 0% of each run, Pallas kernels for 21% -> 20%
where the time goes in v6:
time: 233 us; the launch traced here: 232 us
  waiting for transfers between devices  125 us (54%)
  Pallas kernels  53.3 us (23%)
  starting transfers between devices  45.7 us (20%)
  local copies, waits for them, and re-layouts  6.71 us (3%)
    ppermute x3, waiting for transfers between devices, swap(): return lax.ppermute(array, 'tensor', [(0, 1), (1, 0), (2, 3), (3, 2)])  55.1 us
    ppermute x5, waiting for transfers between devices, outward(): return lax.ppermute(array, 'tensor', [(1, 0), (2, 3)])  40.8 us
    ppermute x6, waiting for transfers between devices, inward(): return lax.ppermute(array, 'tensor', [(0, 1), (3, 2)])  26.8 us
    ppermute x6, starting transfers between devices, inward(): return lax.ppermute(array, 'tensor', [(0, 1), (3, 2)])  18.5 us
    pallas_call x8, Pallas kernels, mix(): pl.pallas_call(mix_kernel, grid=(tiles,), in_specs=[whole(rows, depth), p...  16.5 us
    pallas_call x3, Pallas kernels, partial_projection(): pl.pallas_call(functools.partial(partial_kernel, [len(part) for part in p...  11.6 us
    pallas_call x2, Pallas kernels, attention(): pl.pallas_call(functools.partial(attention_kernel, slots, n_parts, len(ot...  11.2 us
    ppermute x10, starting transfers between devices, between(): return lax.ppermute(array, 'cand', [(i, i ^ offset) for i in range(n_cand)])  8.65 us
  transfers between devices with their start and end apart: 32, of which 13 were waited for; matrix products, arithmetic and copies ran while one was open for 0% of the time, Pallas kernels for 20%

profile of v6, /device:TPU:0, one launch (start us, length us, event | category | flops | bytes accessed | tf_op | source)
XLA Modules:
  0.0 232.0 jit_solution(9802636816253365178)
XLA Ops:
  0.0 2.6 %fusion = (bf16[256,1280]{1,0:T(8,128)(2,1)}, bf16[256,1280]{1,0:T(8,128)(2,1)}) fusion(bf16[512,1280]{1,0:T(8,128)(2,1)} %refs_0_.1), kind=kLoop, calls=%fused_computation | loop fusion | bytes 2621440 | tf_op jit(solution)/shard_map/slice | solution.py:437
  2.6 3.0 %collective-permute-start = (bf16[256,1280]{1,0:T(8,128)(2,1)}, bf16[256,1280]{1,0:T(8,128)(2,1)S(1)}, u32[]{:S(2)}, u32[]{:S(2)}) collective-permute-start(bf16[256,1280]{1,0:T(8,128)(2,1)} %get-tuple-element.90), channel_id=1, source_target_pairs={{0,1},{1,0},{2,3},{3,2},{4,5},{5,4},{6,7},{7,6},{8,9},{9,8},{10,11... | collective-permute-start | bytes 1966088 | tf_op jit(solution)/shard_map/ppermute | solution.py:411
  5.6 1.5 collective-permute-start.6
  7.2 4.0 %copy-done = bf16[1024,5120]{1,0:T(8,128)(2,1)S(1)} copy-done((bf16[1024,5120]{1,0:T(8,128)(2,1)S(1)}, bf16[1024,5120]{1,0:T(8,128)(2,1)}, u32[]{:S(2)}) %copy-start) | copy-done | bytes 10485784
  11.2 0.8 eighths.1
  12.0 8.6 %collective-permute-done.refs_0_ = bf16[256,1280]{1,0:T(8,128)(2,1)S(1)} collective-permute-done((bf16[256,1280]{1,0:T(8,128)(2,1)}, bf16[256,1280]{1,0:T(8,128)(2,1)S(1)}, u32[]{:S(2)}, u32[]{:S(2)}) %collective-permute-start) | collective-permute-done | bytes 655392 | tf_op jit(solution)/shard_map/ppermute | solution.py:411
  20.6 3.7 %collective-permute-start.1 = (bf16[256,2560]{1,0:T(8,128)(2,1)S(1)}, bf16[256,2560]{1,0:T(8,128)(2,1)S(1)}, u32[]{:S(2)}, u32[]{:S(2)}) collective-permute-start(bf16[256,2560]{1,0:T(8,128)(2,1)S(1)} %eighths.1), channel_id=1, source_target_pairs={{0,1},{3,2},{4,5},{7,6},{8,9},{11,10},{12,13},{15,14},{16,17},{19,... | collective-permute-start | bytes 3932168 | tf_op jit(solution)/shard_map/ppermute | solution.py:420
  24.4 0.7 collective-permute-start.9
  25.1 1.3 collective-permute-start.7
  26.4 3.4 %partial_projection.3 = (f32[512,1024]{1,0:T(8,128)S(1)}, f32[512,128]{1,0:T(8,128)S(1)}, f32[512,128]{1,0:T(8,128)S(1)}) custom-call(s32[12]{0:T(128)S(1)} %stack.51.places_ref, bf16[512,1280]{1,0:T(8,128)(2,1)S(1)} %copy-done.4, bf16[5120,1024]{1,0:T(8,128)(2,1)S(1)} %copy-done.1, bf16[5120,128]{1,0:T(8,128)(2,1)S(1)} %copy-done.2, ...), custom_call_target="tpu_custom_call" | custom-call | flops 1 | bytes 1 | tf_op jit(solution)/shard_map/partial_projection/pallas_call | solution.py:96
  29.9 35.7 %collective-permute-done.5.refs_1_ = bf16[256,1280]{1,0:T(8,128)(2,1)S(1)} collective-permute-done((bf16[256,1280]{1,0:T(8,128)(2,1)}, bf16[256,1280]{1,0:T(8,128)(2,1)S(1)}, u32[]{:S(2)}, u32[]{:S(2)}) %collective-permute-start.5) | collective-permute-done | bytes 655392 | tf_op jit(solution)/shard_map/ppermute | solution.py:411
  65.6 0.7 collective-permute-start.3
  66.3 1.3 collective-permute-start.10
  67.6 0.7 collective-permute-start.8
  68.3 1.6 collective-permute-start.2
  69.9 1.3 collective-permute-start.4
  71.2 3.6 %partial_projection.4 = (f32[512,1024]{1,0:T(8,128)S(1)}, f32[512,128]{1,0:T(8,128)S(1)}, f32[512,128]{1,0:T(8,128)S(1)}) custom-call(s32[12]{0:T(128)S(1)} %stack.51.places_ref, bf16[256,1280]{1,0:T(8,128)(2,1)S(1)} %collective-permute-done.refs_0_, bf16[256,1280]{1,0:T(8,128)(2,1)S(1)} %collective-permute-done.5.refs_1_, bf16[5120,1024]{1,0:T(8,128)(2,1)S(1)} %copy-done.1, ...), custom_call_target="tpu_custom_call" | custom-call | flops 1 | bytes 1 | tf_op jit(solution)/shard_map/partial_projection/pallas_call | solution.py:96
  74.8 12.1 %collective-permute-done.10.refs_3_ = bf16[256,1280]{1,0:T(8,128)(2,1)S(1)} collective-permute-done((bf16[256,1280]{1,0:T(8,128)(2,1)S(1)}, bf16[256,1280]{1,0:T(8,128)(2,1)S(1)}, u32[]{:S(2)}, u32[]{:S(2)}) %collective-permute-start.10) | collective-permute-done | bytes 655392 | tf_op jit(solution)/shard_map/ppermute | solution.py:417
  87.0 1.4 collective-permute-start.11
  88.4 4.5 %partial_projection.5 = (f32[512,1024]{1,0:T(8,128)S(1)}, f32[512,128]{1,0:T(8,128)S(1)}, f32[512,128]{1,0:T(8,128)S(1)}) custom-call(s32[12]{0:T(128)S(1)} %stack.51.places_ref, bf16[256,1280]{1,0:T(8,128)(2,1)} %collective-permute-done.6.refs_0_, bf16[256,1280]{1,0:T(8,128)(2,1)S(1)} %collective-permute-done.7.refs_1_, ...), custom_call_target="tpu_custom_call" | custom-call | flops 1 | bytes 1 | tf_op jit(solution)/shard_map/partial_projection/pallas_call | solution.py:96
  93.0 7.9 %collective-permute-done.4.refs_1_ = bf16[256,1280]{1,0:T(8,128)(2,1)S(1)} collective-permute-done((bf16[256,1280]{1,0:T(8,128)(2,1)S(1)}, bf16[256,1280]{1,0:T(8,128)(2,1)S(1)}, u32[]{:S(2)}, u32[]{:S(2)}) %collective-permute-start.4) | collective-permute-done | bytes 655392 | tf_op jit(solution)/shard_map/ppermute | solution.py:417
  100.9 2.5 %queries.2.refs_0_ = bf16[256,1024]{1,0:T(8,128)(2,1)S(1)} custom-call(s32[12]{0:T(128)S(1)} %stack.51.places_ref, bf16[256,1280]{1,0:T(8,128)(2,1)S(1)} %collective-permute-done.3.refs_0_, bf16[256,1280]{1,0:T(8,128)(2,1)S(1)} %collective-permute-done.4.refs_1_, bf16[5120,1024]{1,0:T(8,128)(2,1)S(1)} %copy-done.1, ...), custom_call_target="tpu_custom_call" | custom-call | flops 1 | bytes 1 | tf_op jit(solution)/shard_map/queries/pallas_call | solution.py:183
  103.4 1.1 keys_values.2.refs_0_.refs_2_
  104.4 9.2 %collective-permute-done.11.refs_1_.refs_2_ = bf16[256,1280]{1,0:T(8,128)(2,1)S(1)} collective-permute-done((bf16[256,1280]{1,0:T(8,128)(2,1)S(1)}, bf16[256,1280]{1,0:T(8,128)(2,1)S(1)}, u32[]{:S(2)}, u32[]{:S(2)}) %collective-permute-start.11) | collective-permute-done | bytes 655392 | tf_op jit(solution)/shard_map/ppermute | solution.py:417
  113.6 1.3 keys_values.3
  115.0 1.6 collective-permute-start.13
  116.5 0.3 collective-permute-start.14
  116.8 1.5 collective-permute-start.15
  118.4 0.2 collective-permute-start.16
  118.5 0.9 collective-permute-done.13.refs_5_
  119.5 2.9 %collective-permute-start.17 = (bf16[128,256]{1,0:T(8,128)(2,1)S(1)}, bf16[128,256]{1,0:T(8,128)(2,1)S(1)}, u32[]{:S(2)}, u32[]{:S(2)}) collective-permute-start(bf16[128,256]{1,0:T(8,128)(2,1)S(1)} %get-tuple-element.70), channel_id=1, source_target_pairs={{0,24},{4,28},{8,16},{12,20},{16,8},{20,12},{24,0},{28,4},{1,25},{... | collective-permute-start | bytes 196616 | tf_op jit(solution)/shard_map/ppermute | solution.py:423
  123.1 2.5 %queries.3.refs_1_ = bf16[256,1024]{1,0:T(8,128)(2,1)S(1)} custom-call(s32[12]{0:T(128)S(1)} %stack.51.places_ref, bf16[256,1280]{1,0:T(8,128)(2,1)S(1)} %collective-permute-done.8.refs_0_.refs_1_, bf16[256,1280]{1,0:T(8,128)(2,1)S(1)} %collective-permute-done.11.refs_1_.refs_2_, bf16[5120,1024]{1,0:T(8,128)(2,1)S(1)} %copy-done.1, ...), custom_call_target="tpu_custom_call" | custom-call | flops 1 | bytes 1 | tf_op jit(solution)/shard_map/queries/pallas_call | solution.py:183
  125.6 1.4 collective-permute-done.18.refs_10_
  127.0 3.5 %attention.2.rows_ref = bf16[128,1024]{1,0:T(8,128)(2,1)S(1)} custom-call(s32[12]{0:T(128)S(1)} %stack.51.places_ref, s32[1]{0:T(128)S(6)} %copy.14.length_ref, bf16[256,1024]{1,0:T(8,128)(2,1)S(1)} %queries.2.refs_0_, bf16[256,1024]{1,0:T(8,128)(2,1)S(1)} %queries.3.refs_1_, bf16[256,256]{1,0:T(8,128)(2,1)S(1)} %keys_values.2.refs_0_.refs_2_, ...), custom_call_target="tpu_custom_call" | custom-call | flops 1 | bytes 1 | tf_op jit(solution)/shard_map/attention/pallas_call | solution.py:272
  130.6 2.1 mix.8.refs_0_
  132.6 1.7 collective-permute-start.20
  134.3 2.1 mix.9.refs_0_
  136.4 1.3 collective-permute-start.19
  137.7 7.6 %attention.3 = (bf16[128,1024]{1,0:T(8,128)(2,1)S(1)}, bf16[128,1024]{1,0:T(8,128)(2,1)S(1)}, bf16[128,1024]{1,0:T(8,128)(2,1)S(1)}) custom-call(s32[12]{0:T(128)S(1)} %stack.51.places_ref, s32[1]{0:T(128)S(6)} %copy.14.length_ref, bf16[256,1024]{1,0:T(8,128)(2,1)S(1)} %queries.2.refs_0_, bf16[256,1024]{1,0:T(8,128)(2,1)S(1)} %queries.3.refs_1_, ...), custom_call_target="tpu_custom_call" | custom-call | flops 1 | bytes 1 | tf_op jit(solution)/shard_map/attention/pallas_call | solution.py:272
  145.4 2.1 mix.10.refs_0_
  147.4 2.1 mix.11.refs_0_
  149.5 1.3 collective-permute-start.25
  151.0 0.7 collective-permute-start.22
  151.7 2.1 mix.12.refs_0_
  153.8 2.1 mix.13.refs_0_
  155.9 7.4 %collective-permute-done.19.refs_1_ = bf16[128,2560]{1,0:T(8,128)(2,1)S(1)} collective-permute-done((bf16[128,2560]{1,0:T(8,128)(2,1)S(1)}, bf16[128,2560]{1,0:T(8,128)(2,1)S(1)}, u32[]{:S(2)}, u32[]{:S(2)}) %collective-permute-start.19) | collective-permute-done | bytes 655392 | tf_op jit(solution)/shard_map/ppermute | solution.py:420
  163.5 0.7 collective-permute-start.24
  164.2 6.1 %collective-permute-start.23 = (bf16[128,2560]{1,0:T(8,128)(2,1)S(1)}, bf16[128,2560]{1,0:T(8,128)(2,1)S(1)}, u32[]{:S(2)}, u32[]{:S(2)}) collective-permute-start(bf16[128,2560]{1,0:T(8,128)(2,1)S(1)} %mix.11.refs_0_), channel_id=1, source_target_pairs={{0,1},{3,2},{4,5},{7,6},{8,9},{11,10},{12,13},{15,14},{16,17},{19,... | collective-permute-start | bytes 1966088 | tf_op jit(solution)/shard_map/ppermute | solution.py:420
  170.3 2.1 mix.14.refs_0_
  172.3 2.1 mix.15.refs_0_
  174.6 2.8 %collective-permute-done.25.refs_1_ = bf16[128,2560]{1,0:T(8,128)(2,1)S(1)} collective-permute-done((bf16[128,2560]{1,0:T(8,128)(2,1)S(1)}, bf16[128,2560]{1,0:T(8,128)(2,1)S(1)}, u32[]{:S(2)}, u32[]{:S(2)}) %collective-permute-start.25) | collective-permute-done | bytes 655392 | tf_op jit(solution)/shard_map/ppermute | solution.py:420
  177.5 0.7 collective-permute-start.26
  178.4 11.0 %collective-permute-done.23.refs_1_ = bf16[128,2560]{1,0:T(8,128)(2,1)S(1)} collective-permute-done((bf16[128,2560]{1,0:T(8,128)(2,1)S(1)}, bf16[128,2560]{1,0:T(8,128)(2,1)S(1)}, u32[]{:S(2)}, u32[]{:S(2)}) %collective-permute-start.23) | collective-permute-done | bytes 655392 | tf_op jit(solution)/shard_map/ppermute | solution.py:420
  189.6 0.5 collective-permute-start.27
  190.1 4.4 %collective-permute-start.21 = (bf16[128,1024]{1,0:T(8,128)(2,1)S(1)}, bf16[128,1024]{1,0:T(8,128)(2,1)S(1)}, u32[]{:S(2)}, u32[]{:S(2)}) collective-permute-start(bf16[128,1024]{1,0:T(8,128)(2,1)S(1)} %get-tuple-element.76.rows_ref), channel_id=1, source_target_pairs={{0,1},{3,2},{4,5},{7,6},{8,9},{11,10},{12,13},{15,14},{16,17},{19,... | collective-permute-start | bytes 786440 | tf_op jit(solution)/shard_map/ppermute | solution.py:420
  194.7 5.6 %collective-permute-done.21.rows_ref = bf16[128,1024]{1,0:T(8,128)(2,1)S(1)} collective-permute-done((bf16[128,1024]{1,0:T(8,128)(2,1)S(1)}, bf16[128,1024]{1,0:T(8,128)(2,1)S(1)}, u32[]{:S(2)}, u32[]{:S(2)}) %collective-permute-start.21) | collective-permute-done | bytes 262176 | tf_op jit(solution)/shard_map/ppermute | solution.py:420
  200.3 2.5 %collective-permute-start.31 = (bf16[128,2560]{1,0:T(8,128)(2,1)S(1)}, bf16[128,2560]{1,0:T(8,128)(2,1)S(1)}, u32[]{:S(2)}, u32[]{:S(2)}) collective-permute-start(bf16[128,2560]{1,0:T(8,128)(2,1)S(1)} %added.12), channel_id=1, source_target_pairs={{0,1},{1,0},{2,3},{3,2},{4,5},{5,4},{6,7},{7,6},{8,9},{9,8},{10,11... | collective-permute-start | bytes 1966088 | tf_op jit(solution)/shard_map/ppermute | solution.py:411
  202.8 0.7 collective-permute-start.30
  203.5 1.3 collective-permute-start.29
  204.8 2.7 %mix_sent.1.refs_1_ = bf16[128,2560]{1,0:T(8,128)(2,1)S(1)} custom-call(s32[12]{0:T(128)S(1)} %stack.51.places_ref, bf16[128,1024]{1,0:T(8,128)(2,1)S(1)} %collective-permute-done.21.rows_ref, bf16[256,2560]{1,0:T(8,128)(2,1)S(1)} %collective-permute-done.1.refs_0_, bf16[256,2560]{1,0:T(8,128)(2,1)S(1)} %collective-permute-done.2.refs_1_, ...), custom_call_target="tpu_custom_call" | custom-call | flops 1 | bytes 1 | tf_op jit(solution)/shard_map/mix_sent/pallas_call | solution.py:357
  207.6 10.8 %collective-permute-done.31.refs_1_ = bf16[128,2560]{1,0:T(8,128)(2,1)S(1)} collective-permute-done((bf16[128,2560]{1,0:T(8,128)(2,1)S(1)}, bf16[128,2560]{1,0:T(8,128)(2,1)S(1)}, u32[]{:S(2)}, u32[]{:S(2)}) %collective-permute-start.31) | collective-permute-done | bytes 655392 | tf_op jit(solution)/shard_map/ppermute | solution.py:411
  218.4 1.0 added.18.refs_3_
  219.4 11.5 %collective-permute-done.29.refs_1_ = bf16[128,2560]{1,0:T(8,128)(2,1)S(1)} collective-permute-done((bf16[128,2560]{1,0:T(8,128)(2,1)S(1)}, bf16[128,2560]{1,0:T(8,128)(2,1)S(1)}, u32[]{:S(2)}, u32[]{:S(2)}) %collective-permute-start.29) | collective-permute-done | bytes 655392 | tf_op jit(solution)/shard_map/ppermute | solution.py:417
  231.0 1.1 added.19
  (58 shorter events, 1.6 us)
Async XLA Ops:
  0.0 26.4 %copy-start.3 = (bf16[5120,128]{1,0:T(8,128)(2,1)S(1)}, bf16[5120,128]{1,0:T(8,128)(2,1)}, u32[]{:S(2)}) copy-start(bf16[5120,128]{1,0:T(8,128)(2,1)} %refs_4_.5) | copy-start | bytes 3932164
  0.0 26.4 %copy-start.4 = (bf16[512,1280]{1,0:T(8,128)(2,1)S(1)}, bf16[512,1280]{1,0:T(8,128)(2,1)}, u32[]{:S(2)}) copy-start(bf16[512,1280]{1,0:T(8,128)(2,1)} %refs_0_.1) | copy-start | bytes 3932164
  2.6 18.0 %collective-permute-start = (bf16[256,1280]{1,0:T(8,128)(2,1)}, bf16[256,1280]{1,0:T(8,128)(2,1)S(1)}, u32[]{:S(2)}, u32[]{:S(2)}) collective-permute-start(bf16[256,1280]{1,0:T(8,128)(2,1)} %get-tuple-element.90), channel_id=1, source_target_pairs={{0,1},{1,0},{2,3},{3,2},{4,5},{5,4},{6,7},{7,6},{8,9},{9,8},{10,11... | collective-permute-start | bytes 1966088 | tf_op jit(solution)/shard_map/ppermute | solution.py:411
  5.6 19.5 %collective-permute-start.6 = (bf16[256,1280]{1,0:T(8,128)(2,1)}, bf16[256,1280]{1,0:T(8,128)(2,1)}, u32[]{:S(2)}, u32[]{:S(2)}) collective-permute-start(bf16[256,1280]{1,0:T(8,128)(2,1)} %get-tuple-element.90), channel_id=1, source_target_pairs={{1,2},{2,1},{5,6},{6,5},{9,10},{10,9},{13,14},{14,13},{17,18},{18,... | collective-permute-start | bytes 1966088 | tf_op jit(solution)/shard_map/ppermute | solution.py:414
  7.2 4.0 %copy-start = (bf16[1024,5120]{1,0:T(8,128)(2,1)S(1)}, bf16[1024,5120]{1,0:T(8,128)(2,1)}, u32[]{:S(2)}) copy-start(bf16[1024,5120]{1,0:T(8,128)(2,1)} %w_ref.17) | copy-start | bytes 31457284
  11.2 15.2 %copy-start.1 = (bf16[5120,1024]{1,0:T(8,128)(2,1)S(1)}, bf16[5120,1024]{1,0:T(8,128)(2,1)}, u32[]{:S(2)}) copy-start(bf16[5120,1024]{1,0:T(8,128)(2,1)} %refs_2_.8) | copy-start | bytes 31457284
  11.2 15.2 %copy-start.2 = (bf16[5120,128]{1,0:T(8,128)(2,1)S(1)}, bf16[5120,128]{1,0:T(8,128)(2,1)}, u32[]{:S(2)}) copy-start(bf16[5120,128]{1,0:T(8,128)(2,1)} %refs_3_.7) | copy-start | bytes 3932164
  20.6 47.8 %collective-permute-start.1 = (bf16[256,2560]{1,0:T(8,128)(2,1)S(1)}, bf16[256,2560]{1,0:T(8,128)(2,1)S(1)}, u32[]{:S(2)}, u32[]{:S(2)}) collective-permute-start(bf16[256,2560]{1,0:T(8,128)(2,1)S(1)} %eighths.1), channel_id=1, source_target_pairs={{0,1},{3,2},{4,5},{7,6},{8,9},{11,10},{12,13},{15,14},{16,17},{19,... | collective-permute-start | bytes 3932168 | tf_op jit(solution)/shard_map/ppermute | solution.py:420
  24.3 41.3 %collective-permute-start.5 = (bf16[256,1280]{1,0:T(8,128)(2,1)}, bf16[256,1280]{1,0:T(8,128)(2,1)S(1)}, u32[]{:S(2)}, u32[]{:S(2)}) collective-permute-start(bf16[256,1280]{1,0:T(8,128)(2,1)} %get-tuple-element.89), channel_id=1, source_target_pairs={{0,1},{1,0},{2,3},{3,2},{4,5},{5,4},{6,7},{7,6},{8,9},{9,8},{10,11... | collective-permute-start | bytes 1966088 | tf_op jit(solution)/shard_map/ppermute | solution.py:411
  24.4 41.9 %collective-permute-start.9 = (bf16[256,1280]{1,0:T(8,128)(2,1)}, bf16[256,1280]{1,0:T(8,128)(2,1)S(1)}, u32[]{:S(2)}, u32[]{:S(2)}) collective-permute-start(bf16[256,1280]{1,0:T(8,128)(2,1)} %get-tuple-element.89), channel_id=1, source_target_pairs={{1,2},{2,1},{5,6},{6,5},{9,10},{10,9},{13,14},{14,13},{17,18},{18,... | collective-permute-start | bytes 1966088 | tf_op jit(solution)/shard_map/ppermute | solution.py:414
  25.1 42.5 %collective-permute-start.7 = (bf16[256,1280]{1,0:T(8,128)(2,1)}, bf16[256,1280]{1,0:T(8,128)(2,1)S(1)}, u32[]{:S(2)}, u32[]{:S(2)}) collective-permute-start(bf16[256,1280]{1,0:T(8,128)(2,1)} %collective-permute-done.6.refs_0_), channel_id=1, source_target_pairs={{1,0},{2,3},{5,4},{6,7},{9,8},{10,11},{13,12},{14,15},{17,16},{18,... | collective-permute-start | bytes 1966088 | tf_op jit(solution)/shard_map/ppermute | solution.py:417
  65.6 4.3 %collective-permute-start.3 = (bf16[256,1280]{1,0:T(8,128)(2,1)S(1)}, bf16[256,1280]{1,0:T(8,128)(2,1)S(1)}, u32[]{:S(2)}, u32[]{:S(2)}) collective-permute-start(bf16[256,1280]{1,0:T(8,128)(2,1)S(1)} %collective-permute-done.refs_0_), channel_id=1, source_target_pairs={{1,2},{2,1},{5,6},{6,5},{9,10},{10,9},{13,14},{14,13},{17,18},{18,... | collective-permute-start | bytes 1966088 | tf_op jit(solution)/shard_map/ppermute | solution.py:414
  66.3 20.6 %collective-permute-start.10 = (bf16[256,1280]{1,0:T(8,128)(2,1)S(1)}, bf16[256,1280]{1,0:T(8,128)(2,1)S(1)}, u32[]{:S(2)}, u32[]{:S(2)}) collective-permute-start(bf16[256,1280]{1,0:T(8,128)(2,1)S(1)} %collective-permute-done.9.refs_2_), channel_id=1, source_target_pairs={{1,0},{2,3},{5,4},{6,7},{9,8},{10,11},{13,12},{14,15},{17,16},{18,... | collective-permute-start | bytes 1966088 | tf_op jit(solution)/shard_map/ppermute | solution.py:417
  67.6 19.3 %collective-permute-start.8 = (bf16[256,1280]{1,0:T(8,128)(2,1)S(1)}, bf16[256,1280]{1,0:T(8,128)(2,1)S(1)}, u32[]{:S(2)}, u32[]{:S(2)}) collective-permute-start(bf16[256,1280]{1,0:T(8,128)(2,1)S(1)} %collective-permute-done.5.refs_1_), channel_id=1, source_target_pairs={{1,2},{2,1},{5,6},{6,5},{9,10},{10,9},{13,14},{14,13},{17,18},{18,... | collective-permute-start | bytes 1966088 | tf_op jit(solution)/shard_map/ppermute | solution.py:414
  68.3 54.0 %collective-permute-start.2 = (bf16[256,2560]{1,0:T(8,128)(2,1)S(1)}, bf16[256,2560]{1,0:T(8,128)(2,1)S(1)}, u32[]{:S(2)}, u32[]{:S(2)}) collective-permute-start(bf16[256,2560]{1,0:T(8,128)(2,1)S(1)} %collective-permute-done.1.refs_0_), channel_id=1, source_target_pairs={{0,8},{4,12},{8,0},{12,4},{16,24},{20,28},{24,16},{28,20},{1,9},{5... | collective-permute-start | bytes 3932168 | tf_op jit(solution)/shard_map/ppermute | solution.py:423
  69.9 31.0 %collective-permute-start.4 = (bf16[256,1280]{1,0:T(8,128)(2,1)S(1)}, bf16[256,1280]{1,0:T(8,128)(2,1)S(1)}, u32[]{:S(2)}, u32[]{:S(2)}) collective-permute-start(bf16[256,1280]{1,0:T(8,128)(2,1)S(1)} %collective-permute-done.3.refs_0_), channel_id=1, source_target_pairs={{1,0},{2,3},{5,4},{6,7},{9,8},{10,11},{13,12},{14,15},{17,16},{18,... | collective-permute-start | bytes 1966088 | tf_op jit(solution)/shard_map/ppermute | solution.py:417
  87.0 13.9 %copy-start.5 = (f32[512,128]{1,0:T(8,128)S(1)}, f32[512,128]{1,0:T(8,128)}, u32[]{:S(2)}) copy-start(f32[512,128]{1,0:T(8,128)} %constant.29.clone.refs_5_.refs_7_.refs_8_) | copy-start | bytes 786436
  87.0 13.9 %copy-start.6 = (f32[512,128]{1,0:T(8,128)S(1)}, f32[512,128]{1,0:T(8,128)}, u32[]{:S(2)}) copy-start(f32[512,128]{1,0:T(8,128)} %constant.30.clone.refs_6_.refs_8_.refs_9_) | copy-start | bytes 786436
  87.0 13.9 %copy-start.8 = (f32[128]{0:T(128)S(1)}, f32[128]{0:T(128)}, u32[]{:S(2)}) copy-start(f32[128]{0:T(128)} %param.18) | copy-start | bytes 1540
  87.0 26.6 %collective-permute-start.11 = (bf16[256,1280]{1,0:T(8,128)(2,1)S(1)}, bf16[256,1280]{1,0:T(8,128)(2,1)S(1)}, u32[]{:S(2)}, u32[]{:S(2)}) collective-permute-start(bf16[256,1280]{1,0:T(8,128)(2,1)S(1)} %collective-permute-done.8.refs_0_.refs_1_), channel_id=1, source_target_pairs={{1,0},{2,3},{5,4},{6,7},{9,8},{10,11},{13,12},{14,15},{17,16},{18,... | collective-permute-start | bytes 1966088 | tf_op jit(solution)/shard_map/ppermute | solution.py:417
  100.9 2.5 %copy-start.7 = (f32[128]{0:T(128)S(1)}, f32[128]{0:T(128)}, u32[]{:S(2)}) copy-start(f32[128]{0:T(128)} %param.19) | copy-start | bytes 1540
  103.4 10.2 %copy-start.9 = (s32[1,128]{1,0:T(1,128)S(1)}, s32[1,128]{1,0:T(1,128)}, u32[]{:S(2)}) copy-start(s32[1,128]{1,0:T(1,128)} %refs_10_.1) | copy-start | bytes 1540
  113.6 16.9 %slice-start = ((s8[10485760]{0:T(1024)(128)(4,1)}), s8[4194304]{0:T(1024)(128)(4,1)S(1)}, s32[]{:S(2)}) async-start(s8[10485760]{0:T(1024)(128)(4,1)} %bitcast.14), calls=%async_computation | async-start | bytes 8388608
  114.9 3.5 %collective-permute-start.12 = (bf16[128,256]{1,0:T(8,128)(2,1)S(1)}, bf16[128,256]{1,0:T(8,128)(2,1)S(1)}, u32[]{:S(2)}, u32[]{:S(2)}) collective-permute-start(bf16[128,256]{1,0:T(8,128)(2,1)S(1)} %get-tuple-element.70), channel_id=1, source_target_pairs={{0,4},{4,0},{8,12},{12,8},{16,20},{20,16},{24,28},{28,24},{1,5},{5... | collective-permute-start | bytes 196616 | tf_op jit(solution)/shard_map/ppermute | solution.py:423
  115.0 4.5 %collective-permute-start.13 = (bf16[128,256]{1,0:T(8,128)(2,1)S(1)}, bf16[128,256]{1,0:T(8,128)(2,1)S(1)}, u32[]{:S(2)}, u32[]{:S(2)}) collective-permute-start(bf16[128,256]{1,0:T(8,128)(2,1)S(1)} %get-tuple-element.70), channel_id=1, source_target_pairs={{0,8},{4,12},{8,0},{12,4},{16,24},{20,28},{24,16},{28,20},{1,9},{5... | collective-permute-start | bytes 196616 | tf_op jit(solution)/shard_map/ppermute | solution.py:423
  116.5 9.0 %collective-permute-start.14 = (bf16[128,256]{1,0:T(8,128)(2,1)S(1)}, bf16[128,256]{1,0:T(8,128)(2,1)S(1)}, u32[]{:S(2)}, u32[]{:S(2)}) collective-permute-start(bf16[128,256]{1,0:T(8,128)(2,1)S(1)} %get-tuple-element.70), channel_id=1, source_target_pairs={{0,12},{4,8},{8,4},{12,0},{16,28},{20,24},{24,20},{28,16},{1,13},{... | collective-permute-start | bytes 196616 | tf_op jit(solution)/shard_map/ppermute | solution.py:423
  116.8 8.7 %collective-permute-start.15 = (bf16[128,256]{1,0:T(8,128)(2,1)S(1)}, bf16[128,256]{1,0:T(8,128)(2,1)S(1)}, u32[]{:S(2)}, u32[]{:S(2)}) collective-permute-start(bf16[128,256]{1,0:T(8,128)(2,1)S(1)} %get-tuple-element.70), channel_id=1, source_target_pairs={{0,16},{4,20},{8,24},{12,28},{16,0},{20,4},{24,8},{28,12},{1,17},{... | collective-permute-start | bytes 196616 | tf_op jit(solution)/shard_map/ppermute | solution.py:423
  118.4 7.2 %collective-permute-start.16 = (bf16[128,256]{1,0:T(8,128)(2,1)S(1)}, bf16[128,256]{1,0:T(8,128)(2,1)S(1)}, u32[]{:S(2)}, u32[]{:S(2)}) collective-permute-start(bf16[128,256]{1,0:T(8,128)(2,1)S(1)} %get-tuple-element.70), channel_id=1, source_target_pairs={{0,20},{4,16},{8,28},{12,24},{16,4},{20,0},{24,12},{28,8},{1,21},{... | collective-permute-start | bytes 196616 | tf_op jit(solution)/shard_map/ppermute | solution.py:423
  119.5 6.1 %collective-permute-start.17 = (bf16[128,256]{1,0:T(8,128)(2,1)S(1)}, bf16[128,256]{1,0:T(8,128)(2,1)S(1)}, u32[]{:S(2)}, u32[]{:S(2)}) collective-permute-start(bf16[128,256]{1,0:T(8,128)(2,1)S(1)} %get-tuple-element.70), channel_id=1, source_target_pairs={{0,24},{4,28},{8,16},{12,20},{16,8},{20,12},{24,0},{28,4},{1,25},{... | collective-permute-start | bytes 196616 | tf_op jit(solution)/shard_map/ppermute | solution.py:423
  122.4 4.6 %collective-permute-start.18 = (bf16[128,256]{1,0:T(8,128)(2,1)S(1)}, bf16[128,256]{1,0:T(8,128)(2,1)S(1)}, u32[]{:S(2)}, u32[]{:S(2)}) collective-permute-start(bf16[128,256]{1,0:T(8,128)(2,1)S(1)} %get-tuple-element.70), channel_id=1, source_target_pairs={{0,28},{4,24},{8,20},{12,16},{16,12},{20,8},{24,4},{28,0},{1,29},{... | collective-permute-start | bytes 196616 | tf_op jit(solution)/shard_map/ppermute | solution.py:423
  123.0 7.5 %slice-start.1 = ((s8[10485760]{0:T(1024)(128)(4,1)}), s8[4194304]{0:T(1024)(128)(4,1)S(1)}, s32[]{:S(2)}) async-start(s8[10485760]{0:T(1024)(128)(4,1)} %bitcast.14), calls=%async_computation.1 | async-start | bytes 8388608
  123.1 7.5 %slice-start.2 = ((s8[10485760]{0:T(1024)(128)(4,1)}), s8[2097152]{0:T(1024)(128)(4,1)S(1)}, s32[]{:S(2)}) async-start(s8[10485760]{0:T(1024)(128)(4,1)} %bitcast.14), calls=%async_computation.2 | async-start | bytes 4194304
  132.6 18.2 %collective-permute-start.20 = (bf16[128,2560]{1,0:T(8,128)(2,1)S(1)}, bf16[128,2560]{1,0:T(8,128)(2,1)S(1)}, u32[]{:S(2)}, u32[]{:S(2)}) collective-permute-start(bf16[128,2560]{1,0:T(8,128)(2,1)S(1)} %mix.8.refs_0_), channel_id=1, source_target_pairs={{0,1},{3,2},{4,5},{7,6},{8,9},{11,10},{12,13},{15,14},{16,17},{19,... | collective-permute-start | bytes 1966088 | tf_op jit(solution)/shard_map/ppermute | solution.py:420
  136.4 26.9 %collective-permute-start.19 = (bf16[128,2560]{1,0:T(8,128)(2,1)S(1)}, bf16[128,2560]{1,0:T(8,128)(2,1)S(1)}, u32[]{:S(2)}, u32[]{:S(2)}) collective-permute-start(bf16[128,2560]{1,0:T(8,128)(2,1)S(1)} %mix.9.refs_0_), channel_id=1, source_target_pairs={{0,1},{3,2},{4,5},{7,6},{8,9},{11,10},{12,13},{15,14},{16,17},{19,... | collective-permute-start | bytes 1966088 | tf_op jit(solution)/shard_map/ppermute | solution.py:420
  149.5 27.9 %collective-permute-start.25 = (bf16[128,2560]{1,0:T(8,128)(2,1)S(1)}, bf16[128,2560]{1,0:T(8,128)(2,1)S(1)}, u32[]{:S(2)}, u32[]{:S(2)}) collective-permute-start(bf16[128,2560]{1,0:T(8,128)(2,1)S(1)} %mix.10.refs_0_), channel_id=1, source_target_pairs={{0,1},{3,2},{4,5},{7,6},{8,9},{11,10},{12,13},{15,14},{16,17},{19,... | collective-permute-start | bytes 1966088 | tf_op jit(solution)/shard_map/ppermute | solution.py:420
  151.0 23.4 %collective-permute-start.22 = (bf16[128,2560]{1,0:T(8,128)(2,1)S(1)}, bf16[128,2560]{1,0:T(8,128)(2,1)S(1)}, u32[]{:S(2)}, u32[]{:S(2)}) collective-permute-start(bf16[128,2560]{1,0:T(8,128)(2,1)S(1)} %added.10), channel_id=1, source_target_pairs={{1,2},{2,1},{5,6},{6,5},{9,10},{10,9},{13,14},{14,13},{17,18},{18,... | collective-permute-start | bytes 1966088 | tf_op jit(solution)/shard_map/ppermute | solution.py:414
  163.5 14.8 %collective-permute-start.24 = (bf16[128,2560]{1,0:T(8,128)(2,1)S(1)}, bf16[128,2560]{1,0:T(8,128)(2,1)S(1)}, u32[]{:S(2)}, u32[]{:S(2)}) collective-permute-start(bf16[128,2560]{1,0:T(8,128)(2,1)S(1)} %added.11), channel_id=1, source_target_pairs={{1,2},{2,1},{5,6},{6,5},{9,10},{10,9},{13,14},{14,13},{17,18},{18,... | collective-permute-start | bytes 1966088 | tf_op jit(solution)/shard_map/ppermute | solution.py:414
  164.2 25.2 %collective-permute-start.23 = (bf16[128,2560]{1,0:T(8,128)(2,1)S(1)}, bf16[128,2560]{1,0:T(8,128)(2,1)S(1)}, u32[]{:S(2)}, u32[]{:S(2)}) collective-permute-start(bf16[128,2560]{1,0:T(8,128)(2,1)S(1)} %mix.11.refs_0_), channel_id=1, source_target_pairs={{0,1},{3,2},{4,5},{7,6},{8,9},{11,10},{12,13},{15,14},{16,17},{19,... | collective-permute-start | bytes 1966088 | tf_op jit(solution)/shard_map/ppermute | solution.py:420
  177.5 17.0 %collective-permute-start.26 = (bf16[128,2560]{1,0:T(8,128)(2,1)S(1)}, bf16[128,2560]{1,0:T(8,128)(2,1)S(1)}, u32[]{:S(2)}, u32[]{:S(2)}) collective-permute-start(bf16[128,2560]{1,0:T(8,128)(2,1)S(1)} %added.13), channel_id=1, source_target_pairs={{1,2},{2,1},{5,6},{6,5},{9,10},{10,9},{13,14},{14,13},{17,18},{18,... | collective-permute-start | bytes 1966088 | tf_op jit(solution)/shard_map/ppermute | solution.py:414
  189.6 15.2 %collective-permute-start.28 = (bf16[256,2560]{1,0:T(8,128)(2,1)S(1)}, bf16[256,2560]{1,0:T(8,128)(2,1)S(1)}, u32[]{:S(2)}, u32[]{:S(2)}) collective-permute-start(bf16[256,2560]{1,0:T(8,128)(2,1)S(1)} %collective-permute-done.2.refs_1_), channel_id=1, source_target_pairs={{0,4},{4,0},{8,12},{12,8},{16,20},{20,16},{24,28},{28,24},{1,5},{5... | collective-permute-start | bytes 3932168 | tf_op jit(solution)/shard_map/ppermute | solution.py:423
  189.6 15.2 %collective-permute-start.27 = (bf16[256,2560]{1,0:T(8,128)(2,1)S(1)}, bf16[256,2560]{1,0:T(8,128)(2,1)S(1)}, u32[]{:S(2)}, u32[]{:S(2)}) collective-permute-start(bf16[256,2560]{1,0:T(8,128)(2,1)S(1)} %collective-permute-done.1.refs_0_), channel_id=1, source_target_pairs={{0,4},{4,0},{8,12},{12,8},{16,20},{20,16},{24,28},{28,24},{1,5},{5... | collective-permute-start | bytes 3932168 | tf_op jit(solution)/shard_map/ppermute | solution.py:423
  190.1 10.2 %collective-permute-start.21 = (bf16[128,1024]{1,0:T(8,128)(2,1)S(1)}, bf16[128,1024]{1,0:T(8,128)(2,1)S(1)}, u32[]{:S(2)}, u32[]{:S(2)}) collective-permute-start(bf16[128,1024]{1,0:T(8,128)(2,1)S(1)} %get-tuple-element.76.rows_ref), channel_id=1, source_target_pairs={{0,1},{3,2},{4,5},{7,6},{8,9},{11,10},{12,13},{15,14},{16,17},{19,... | collective-permute-start | bytes 786440 | tf_op jit(solution)/shard_map/ppermute | solution.py:420
  200.3 18.1 %collective-permute-start.31 = (bf16[128,2560]{1,0:T(8,128)(2,1)S(1)}, bf16[128,2560]{1,0:T(8,128)(2,1)S(1)}, u32[]{:S(2)}, u32[]{:S(2)}) collective-permute-start(bf16[128,2560]{1,0:T(8,128)(2,1)S(1)} %added.12), channel_id=1, source_target_pairs={{0,1},{1,0},{2,3},{3,2},{4,5},{5,4},{6,7},{7,6},{8,9},{9,8},{10,11... | collective-permute-start | bytes 1966088 | tf_op jit(solution)/shard_map/ppermute | solution.py:411
  202.8 16.6 %collective-permute-start.30 = (bf16[128,2560]{1,0:T(8,128)(2,1)S(1)}, bf16[128,2560]{1,0:T(8,128)(2,1)S(1)}, u32[]{:S(2)}, u32[]{:S(2)}) collective-permute-start(bf16[128,2560]{1,0:T(8,128)(2,1)S(1)} %added.15), channel_id=1, source_target_pairs={{1,2},{2,1},{5,6},{6,5},{9,10},{10,9},{13,14},{14,13},{17,18},{18,... | collective-permute-start | bytes 1966088 | tf_op jit(solution)/shard_map/ppermute | solution.py:414
  203.5 27.5 %collective-permute-start.29 = (bf16[128,2560]{1,0:T(8,128)(2,1)S(1)}, bf16[128,2560]{1,0:T(8,128)(2,1)S(1)}, u32[]{:S(2)}, u32[]{:S(2)}) collective-permute-start(bf16[128,2560]{1,0:T(8,128)(2,1)S(1)} %added.14), channel_id=1, source_target_pairs={{1,0},{2,3},{5,4},{6,7},{9,8},{10,11},{13,12},{14,15},{17,16},{18,... | collective-permute-start | bytes 1966088 | tf_op jit(solution)/shard_map/ppermute | solution.py:417

commit v7 on v6

--- a/solution.py
+++ b/solution.py
@@ -439,22 +439,22 @@
     for array in mine:
         from_near.append(swap(array))
         from_mid.append(across(array))
+    accs = partial_projection(places, OWN, [[hidden_in]], weights, None)
+    from_near[0], from_mid[0], accs = lax.optimization_barrier((from_near[0], from_mid[0], accs))
     to_outer = [outward(array) for array in from_mid]
     to_inner = [across(from_near[0])]
-    cue = (from_near[0], from_mid[0])
-    accs = partial_projection(after(places, cue), OWN, [[hidden_in]], weights, None)
+    to_inner.append(across(after(from_near[1], (to_outer[0], from_mid[1]))))
     pieces = []
     if spread:
-        pieces.append(inward(after(eighths(places, w_out, share), from_near[0])))
-    from_near[1], accs = lax.optimization_barrier((from_near[1], accs))
-    to_inner.append(across(after(from_near[1], to_outer[0])))
+        pieces.append(inward(after(eighths(places, w_out, share), from_near)))
     cue = (from_near[1], from_mid[1])
     accs = partial_projection(
         after(places, cue), NEAR, [[a] for a in from_near], weights, accs
     )
     end = [outward(to_inner[0]), outward(after(to_inner[1], (to_outer[1], accs)))]
     if spread:
-        pieces.append(between(pieces[0], OFFSETS[2]))
+        pieces.append(between(after(pieces[0], to_inner[1]), OFFSETS[2]))
+        pieces.append(between(after(pieces[0], end[0]), 1))
     cue = (to_inner, accs)
     accs = partial_projection(
         after(places, cue), THIRD, [[a, b] for a, b in zip(from_mid, to_outer)], weights, accs
@@ -468,7 +468,7 @@
         final[1],
         1,
         weights[1:],
-        after(accs[1:], first_queries),
+        after(accs[1:], (first_queries, pieces)),
         k_gain,
         *tables,
         [own_first],
@@ -485,10 +485,11 @@
     def mixed(rows):
         return [mix(rows, w_out, which) for which in (0, 1)]
 
-    places, pieces = lax.optimization_barrier((places, pieces))
+    if spread:
+        pieces.append(between(after(pieces[1], others), 1))
     (far_rows,) = attend((LAST,))
     far = mixed(far_rows)
-    places = after(places, far)
+    places = after(places, (far, pieces))
     third_rows, near_rows, own_rows = attend((THIRD, NEAR, OWN))
     mid = mixed(third_rows)
     far_in = [inward(array) for array in far]
@@ -499,25 +500,25 @@
     far_sum = [far_sum, added(far[1], after(far_in[1], near_part))]
     kept = mixed(after(own_rows, far_sum[1]))
     far_sum = [across(array) for array in far_sum]
-    near_sum, mid_sum = [None, None], [None, None]
-    cue = kept
-    for i in (0, 1):
-        near_sum[i] = added(near_part[i], after(far_sum[i], cue))
-        mid_sum[i] = added(mid[i], after(mid_in[i], near_sum[i]))
-        cue = mid_sum[i]
+    out_sum, mid_sum = [None, None], [None, None]
+    out_sum[0] = added(near_part[0], after(far_sum[0], kept))
+    mid_sum[0] = added(mid[0], after(mid_in[0], out_sum[0]))
+    out_sum[1] = added(near_part[1], after(far_sum[1], mid_sum[0]))
+    from_inner = [outward(array) for array in out_sum]
+    kept[0] = added(kept[0], after(from_inner[0], out_sum[1]))
+    mid_sum[1] = added(mid[1], after(mid_in[1], kept[0]))
+    cue = mid_sum[1]
     mid_sum = [across(array) for array in mid_sum]
     if spread:
-        kept[0] = added(kept[0], mid_sum[0])
-        near_in = inward(near_rows)
-        pieces += [between(after(piece, cue), 1) for piece in pieces]
-        near_in, near_sum[0], _ = lax.optimization_barrier((near_in, near_sum[0], (cue, kept[0])))
-        near_sum = [swap(near_sum[0]), outward(near_sum[1])]
-        kept[1] = added(kept[1], mix_sent(places, near_in, pieces))
-        result = added(kept[0], near_sum[0], half=0)
+        near_in = inward(after(near_rows, out_sum[0]))
+        sent = mix_sent(places, after(near_in, cue), pieces)
     else:
-        near_sum = [swap(array) for array in near_sum]
-        result = added(kept[0], near_sum[0], mid_sum[0], half=0)
-    return added(kept[1], near_sum[1], mid_sum[1], half=1, into=result)
+        sent = inward(near_part[1])
+    near_in = inward(after(near_part[0], near_in if spread else out_sum[1]))
+    kept[1] = added(kept[1], from_inner[1], sent)
+    kept[0] = added(kept[0], after(mid_sum[0], kept[1]))
+    result = added(kept[1], after(mid_sum[1], kept[0]), half=1)
+    return added(kept[0], near_in, half=0, into=result)
 
 
 def solution(mesh):

time: 233 us -> 206 us (0.88)
  waiting for transfers between devices: 125 us -> 82.8 us
  starting transfers between devices: 45.7 us -> 56.5 us
  local copies, waits for them, and re-layouts: 6.71 us -> 10.2 us
    ppermute x3 -> x2, waiting for transfers between devices: 55.1 us -> 14.7 us  [swap(): return lax.ppermute(array, 'tensor', [(0, 1), (1, 0), (2, 3), (3, 2)])]
    ppermute x6 -> x7, waiting for transfers between devices: 26.8 us -> 17.2 us  [inward(): return lax.ppermute(array, 'tensor', [(0, 1), (3, 2)])]
    ppermute x6 -> x7, starting transfers between devices: 18.5 us -> 28.1 us  [inward(): return lax.ppermute(array, 'tensor', [(0, 1), (3, 2)])]
    ppermute x10, waiting for transfers between devices: 2.38 us -> 9.23 us  [between(): return lax.ppermute(array, 'cand', [(i, i ^ offset) for i in range(n_cand)])]
    unnamed x26, local copies, waits for them, and re-layouts: 4.03 us -> 7.5 us
    ppermute x5 -> x6, starting transfers between devices: 6.58 us -> 7.86 us  [outward(): return lax.ppermute(array, 'tensor', [(1, 0), (2, 3)])]
    ppermute x5 -> x6, waiting for transfers between devices: 40.8 us -> 41.7 us  [outward(): return lax.ppermute(array, 'tensor', [(1, 0), (2, 3)])]
    ppermute x3 -> x2, starting transfers between devices: 5.58 us -> 5.14 us  [swap(): return lax.ppermute(array, 'tensor', [(0, 1), (1, 0), (2, 3), (3, 2)])]
  transfers between devices with their start and end apart: 32 -> 33, of which waited for: 13 -> 16; matrix products, arithmetic and copies ran while one was open for 0% -> 0% of each run, Pallas kernels for 20% -> 25%
where the time goes in v7:
time: 206 us; the launch traced here: 205 us
  waiting for transfers between devices  82.8 us (40%)
  starting transfers between devices  56.5 us (27%)
  Pallas kernels  54.7 us (27%)
  local copies, waits for them, and re-layouts  10.2 us (5%)
    ppermute x6, waiting for transfers between devices, outward(): return lax.ppermute(array, 'tensor', [(1, 0), (2, 3)])  41.7 us
    ppermute x7, starting transfers between devices, inward(): return lax.ppermute(array, 'tensor', [(0, 1), (3, 2)])  28.1 us
    ppermute x7, waiting for transfers between devices, inward(): return lax.ppermute(array, 'tensor', [(0, 1), (3, 2)])  17.2 us
    pallas_call x8, Pallas kernels, mix(): pl.pallas_call(mix_kernel, grid=(tiles,), in_specs=[whole(rows, depth), p...  16.5 us
    ppermute x2, waiting for transfers between devices, swap(): return lax.ppermute(array, 'tensor', [(0, 1), (1, 0), (2, 3), (3, 2)])  14.7 us
    pallas_call x3, Pallas kernels, partial_projection(): pl.pallas_call(functools.partial(partial_kernel, [len(part) for part in p...  12.7 us
    pallas_call x2, Pallas kernels, attention(): pl.pallas_call(functools.partial(attention_kernel, slots, n_parts, len(ot...  11.2 us
    ppermute x10, waiting for transfers between devices, between(): return lax.ppermute(array, 'cand', [(i, i ^ offset) for i in range(n_cand)])  9.23 us
  transfers between devices with their start and end apart: 33, of which 16 were waited for; matrix products, arithmetic and copies ran while one was open for 0% of the time, Pallas kernels for 25%

profile of v7, /device:TPU:0, one launch (start us, length us, event | category | flops | bytes accessed | tf_op | source)
XLA Modules:
  0.0 205.4 jit_solution(10459202618518706822)
XLA Ops:
  0.0 2.6 %fusion = (bf16[256,1280]{1,0:T(8,128)(2,1)}, bf16[256,1280]{1,0:T(8,128)(2,1)}) fusion(bf16[512,1280]{1,0:T(8,128)(2,1)} %refs_0_.1), kind=kLoop, calls=%fused_computation | loop fusion | bytes 2621440 | tf_op jit(solution)/shard_map/slice | solution.py:437
  2.6 1.5 collective-permute-start.1
  4.1 5.1 %collective-permute-start = (bf16[256,1280]{1,0:T(8,128)(2,1)}, bf16[256,1280]{1,0:T(8,128)(2,1)S(1)}, u32[]{:S(2)}, u32[]{:S(2)}) collective-permute-start(bf16[256,1280]{1,0:T(8,128)(2,1)} %get-tuple-element.94), channel_id=1, source_target_pairs={{0,1},{1,0},{2,3},{3,2},{4,5},{5,4},{6,7},{7,6},{8,9},{9,8},{10,11... | collective-permute-start | bytes 1966088 | tf_op jit(solution)/shard_map/ppermute | solution.py:411
  9.2 1.5 collective-permute-start.6
  10.9 4.0 %copy-done = bf16[1024,5120]{1,0:T(8,128)(2,1)S(1)} copy-done((bf16[1024,5120]{1,0:T(8,128)(2,1)S(1)}, bf16[1024,5120]{1,0:T(8,128)(2,1)}, u32[]{:S(2)}) %copy-start) | copy-done | bytes 10485784
  14.8 0.8 eighths.1
  15.7 3.2 %copy-done.1 = bf16[5120,1024]{1,0:T(8,128)(2,1)S(1)} copy-done((bf16[5120,1024]{1,0:T(8,128)(2,1)S(1)}, bf16[5120,1024]{1,0:T(8,128)(2,1)}, u32[]{:S(2)}) %copy-start.1) | copy-done | bytes 10485784
  19.1 3.4 %partial_projection.3 = (f32[512,1024]{1,0:T(8,128)S(1)}, f32[512,128]{1,0:T(8,128)S(1)}, f32[512,128]{1,0:T(8,128)S(1)}) custom-call(s32[12]{0:T(128)S(1)} %stack.51.places_ref, bf16[512,1280]{1,0:T(8,128)(2,1)S(1)} %copy-done.4, bf16[5120,1024]{1,0:T(8,128)(2,1)S(1)} %copy-done.1, bf16[5120,128]{1,0:T(8,128)(2,1)S(1)} %copy-done.2, ...), custom_call_target="tpu_custom_call" | custom-call | flops 1 | bytes 1 | tf_op jit(solution)/shard_map/partial_projection/pallas_call | solution.py:96
  22.6 2.4 %collective-permute-done.refs_0_ = bf16[256,1280]{1,0:T(8,128)(2,1)S(1)} collective-permute-done((bf16[256,1280]{1,0:T(8,128)(2,1)}, bf16[256,1280]{1,0:T(8,128)(2,1)S(1)}, u32[]{:S(2)}, u32[]{:S(2)}) %collective-permute-start) | collective-permute-done | bytes 655392 | tf_op jit(solution)/shard_map/ppermute | solution.py:411
  25.0 0.7 collective-permute-start.2
  25.7 12.3 %collective-permute-done.4.refs_1_ = bf16[256,1280]{1,0:T(8,128)(2,1)} collective-permute-done((bf16[256,1280]{1,0:T(8,128)(2,1)}, bf16[256,1280]{1,0:T(8,128)(2,1)}, u32[]{:S(2)}, u32[]{:S(2)}) %collective-permute-start.4) | collective-permute-done | bytes 655392 | tf_op jit(solution)/shard_map/ppermute | solution.py:411
  38.0 1.3 collective-permute-start.5
  39.3 4.7 %collective-permute-start.10 = (bf16[256,2560]{1,0:T(8,128)(2,1)S(1)}, bf16[256,2560]{1,0:T(8,128)(2,1)S(1)}, u32[]{:S(2)}, u32[]{:S(2)}) collective-permute-start(bf16[256,2560]{1,0:T(8,128)(2,1)S(1)} %eighths.1), channel_id=1, source_target_pairs={{0,1},{3,2},{4,5},{7,6},{8,9},{11,10},{12,13},{15,14},{16,17},{19,... | collective-permute-start | bytes 3932168 | tf_op jit(solution)/shard_map/ppermute | solution.py:420
  44.0 1.3 collective-permute-start.3
  45.3 12.5 %collective-permute-done.5.refs_1_ = bf16[256,1280]{1,0:T(8,128)(2,1)S(1)} collective-permute-done((bf16[256,1280]{1,0:T(8,128)(2,1)}, bf16[256,1280]{1,0:T(8,128)(2,1)S(1)}, u32[]{:S(2)}, u32[]{:S(2)}) %collective-permute-start.5) | collective-permute-done | bytes 655392 | tf_op jit(solution)/shard_map/ppermute | solution.py:417
  58.4 1.3 collective-permute-start.8
  59.7 12.0 %collective-permute-done.3.refs_1_ = bf16[256,1280]{1,0:T(8,128)(2,1)S(1)} collective-permute-done((bf16[256,1280]{1,0:T(8,128)(2,1)S(1)}, bf16[256,1280]{1,0:T(8,128)(2,1)S(1)}, u32[]{:S(2)}, u32[]{:S(2)}) %collective-permute-start.3) | collective-permute-done | bytes 655392 | tf_op jit(solution)/shard_map/ppermute | solution.py:417
  71.8 1.5 collective-permute-start.11
  73.3 4.5 %partial_projection.4 = (f32[512,1024]{1,0:T(8,128)S(1)}, f32[512,128]{1,0:T(8,128)S(1)}, f32[512,128]{1,0:T(8,128)S(1)}) custom-call(s32[12]{0:T(128)S(1)} %stack.51.places_ref, bf16[256,1280]{1,0:T(8,128)(2,1)S(1)} %collective-permute-done.refs_0_, bf16[256,1280]{1,0:T(8,128)(2,1)} %collective-permute-done.4.refs_1_, bf16[5120,1024]{1,0:T(8,128)(2,1)S(1)} %copy-done.1, ...), custom_call_target="tpu_custom_call" | custom-call | flops 1 | bytes 1 | tf_op jit(solution)/shard_map/partial_projection/pallas_call | solution.py:96
  77.8 5.9 %collective-permute-done.8.refs_3_ = bf16[256,1280]{1,0:T(8,128)(2,1)S(1)} collective-permute-done((bf16[256,1280]{1,0:T(8,128)(2,1)}, bf16[256,1280]{1,0:T(8,128)(2,1)S(1)}, u32[]{:S(2)}, u32[]{:S(2)}) %collective-permute-start.8) | collective-permute-done | bytes 655392 | tf_op jit(solution)/shard_map/ppermute | solution.py:417
  83.8 1.4 collective-permute-start.9
  85.2 4.7 %partial_projection.5 = (f32[512,1024]{1,0:T(8,128)S(1)}, f32[512,128]{1,0:T(8,128)S(1)}, f32[512,128]{1,0:T(8,128)S(1)}) custom-call(s32[12]{0:T(128)S(1)} %stack.51.places_ref, bf16[256,1280]{1,0:T(8,128)(2,1)} %collective-permute-done.1.refs_0_, bf16[256,1280]{1,0:T(8,128)(2,1)S(1)} %collective-permute-done.5.refs_1_, ...), custom_call_target="tpu_custom_call" | custom-call | flops 1 | bytes 1 | tf_op jit(solution)/shard_map/partial_projection/pallas_call | solution.py:96
  90.0 2.5 %queries.2.refs_0_ = bf16[256,1024]{1,0:T(8,128)(2,1)S(1)} custom-call(s32[12]{0:T(128)S(1)} %stack.51.places_ref, bf16[256,1280]{1,0:T(8,128)(2,1)S(1)} %collective-permute-done.2.refs_0_, bf16[256,1280]{1,0:T(8,128)(2,1)S(1)} %collective-permute-done.3.refs_1_, bf16[5120,1024]{1,0:T(8,128)(2,1)S(1)} %copy-done.1, ...), custom_call_target="tpu_custom_call" | custom-call | flops 1 | bytes 1 | tf_op jit(solution)/shard_map/queries/pallas_call | solution.py:183
  92.5 1.1 keys_values.2.refs_0_.refs_2_
  93.6 5.6 %collective-permute-done.11.refs_1_ = bf16[256,2560]{1,0:T(8,128)(2,1)S(1)} collective-permute-done((bf16[256,2560]{1,0:T(8,128)(2,1)S(1)}, bf16[256,2560]{1,0:T(8,128)(2,1)S(1)}, u32[]{:S(2)}, u32[]{:S(2)}) %collective-permute-start.11) | collective-permute-done | bytes 1310752 | tf_op jit(solution)/shard_map/ppermute | solution.py:423
  99.2 1.3 collective-permute-done.9.refs_1_.refs_2_
  100.5 1.3 keys_values.3
  101.8 2.5 %collective-permute-start.18 = (bf16[128,256]{1,0:T(8,128)(2,1)S(1)}, bf16[128,256]{1,0:T(8,128)(2,1)S(1)}, u32[]{:S(2)}, u32[]{:S(2)}) collective-permute-start(bf16[128,256]{1,0:T(8,128)(2,1)S(1)} %get-tuple-element.73), channel_id=1, source_target_pairs={{0,24},{4,28},{8,16},{12,20},{16,8},{20,12},{24,0},{28,4},{1,25},{... | collective-permute-start | bytes 196616 | tf_op jit(solution)/shard_map/ppermute | solution.py:423
  104.4 1.4 collective-permute-start.17
  106.2 0.7 collective-permute-start.15
  107.0 1.0 collective-permute-start.14
  108.5 1.4 collective-permute-done.17.refs_8_
  109.9 1.4 collective-permute-done.16.refs_7_
  112.7 2.5 %queries.3.refs_1_ = bf16[256,1024]{1,0:T(8,128)(2,1)S(1)} custom-call(s32[12]{0:T(128)S(1)} %stack.51.places_ref, bf16[256,1280]{1,0:T(8,128)(2,1)S(1)} %collective-permute-done.7.refs_0_.refs_1_, bf16[256,1280]{1,0:T(8,128)(2,1)S(1)} %collective-permute-done.9.refs_1_.refs_2_, bf16[5120,1024]{1,0:T(8,128)(2,1)S(1)} %copy-done.1, ...), custom_call_target="tpu_custom_call" | custom-call | flops 1 | bytes 1 | tf_op jit(solution)/shard_map/queries/pallas_call | solution.py:183
  115.2 3.6 %attention.2.rows_ref = bf16[128,1024]{1,0:T(8,128)(2,1)S(1)} custom-call(s32[12]{0:T(128)S(1)} %stack.51.places_ref, s32[1]{0:T(128)S(6)} %copy.14.length_ref, bf16[256,1024]{1,0:T(8,128)(2,1)S(1)} %queries.2.refs_0_, bf16[256,1024]{1,0:T(8,128)(2,1)S(1)} %queries.3.refs_1_, bf16[256,256]{1,0:T(8,128)(2,1)S(1)} %keys_values.2.refs_0_.refs_2_, ...), custom_call_target="tpu_custom_call" | custom-call | flops 1 | bytes 1 | tf_op jit(solution)/shard_map/attention/pallas_call | solution.py:272
  118.8 2.1 %mix.8.refs_0_ = bf16[128,2560]{1,0:T(8,128)(2,1)S(1)} custom-call(bf16[128,1024]{1,0:T(8,128)(2,1)S(1)} %attention.2.rows_ref, bf16[1024,5120]{1,0:T(8,128)(2,1)S(1)} %bitcast.15), custom_call_target="tpu_custom_call" | custom-call | flops 1 | bytes 1 | tf_op jit(solution)/shard_map/mix/pallas_call | solution.py:301
  120.9 3.3 %collective-permute-start.22 = (bf16[128,2560]{1,0:T(8,128)(2,1)S(1)}, bf16[128,2560]{1,0:T(8,128)(2,1)S(1)}, u32[]{:S(2)}, u32[]{:S(2)}) collective-permute-start(bf16[128,2560]{1,0:T(8,128)(2,1)S(1)} %mix.8.refs_0_), channel_id=1, source_target_pairs={{0,1},{3,2},{4,5},{7,6},{8,9},{11,10},{12,13},{15,14},{16,17},{19,... | collective-permute-start | bytes 1966088 | tf_op jit(solution)/shard_map/ppermute | solution.py:420
  124.2 2.1 %mix.9.refs_0_ = bf16[128,2560]{1,0:T(8,128)(2,1)S(1)} custom-call(bf16[128,1024]{1,0:T(8,128)(2,1)S(1)} %attention.2.rows_ref, bf16[1024,5120]{1,0:T(8,128)(2,1)S(1)} %bitcast.15), custom_call_target="tpu_custom_call" | custom-call | flops 1 | bytes 1 | tf_op jit(solution)/shard_map/mix/pallas_call | solution.py:301
  126.3 1.3 collective-permute-start.21
  127.7 7.6 %attention.3 = (bf16[128,1024]{1,0:T(8,128)(2,1)S(1)}, bf16[128,1024]{1,0:T(8,128)(2,1)S(1)}, bf16[128,1024]{1,0:T(8,128)(2,1)S(1)}) custom-call(s32[12]{0:T(128)S(1)} %stack.51.places_ref, s32[1]{0:T(128)S(6)} %copy.14.length_ref, bf16[256,1024]{1,0:T(8,128)(2,1)S(1)} %queries.2.refs_0_, bf16[256,1024]{1,0:T(8,128)(2,1)S(1)} %queries.3.refs_1_, ...), custom_call_target="tpu_custom_call" | custom-call | flops 1 | bytes 1 | tf_op jit(solution)/shard_map/attention/pallas_call | solution.py:272
  135.3 2.1 %mix.11.refs_0_ = bf16[128,2560]{1,0:T(8,128)(2,1)S(1)} custom-call(bf16[128,1024]{1,0:T(8,128)(2,1)S(1)} %get-tuple-element.78.rows_ref, bf16[1024,5120]{1,0:T(8,128)(2,1)S(1)} %bitcast.15), custom_call_target="tpu_custom_call" | custom-call | flops 1 | bytes 1 | tf_op jit(solution)/shard_map/mix/pallas_call | solution.py:301
  137.4 2.1 %mix.10.refs_0_ = bf16[128,2560]{1,0:T(8,128)(2,1)S(1)} custom-call(bf16[128,1024]{1,0:T(8,128)(2,1)S(1)} %get-tuple-element.78.rows_ref, bf16[1024,5120]{1,0:T(8,128)(2,1)S(1)} %bitcast.15), custom_call_target="tpu_custom_call" | custom-call | flops 1 | bytes 1 | tf_op jit(solution)/shard_map/mix/pallas_call | solution.py:301
  139.6 0.7 collective-permute-start.23
  140.4 2.1 %mix.12.refs_0_ = bf16[128,2560]{1,0:T(8,128)(2,1)S(1)} custom-call(bf16[128,1024]{1,0:T(8,128)(2,1)S(1)} %get-tuple-element.87.rows_ref, bf16[1024,5120]{1,0:T(8,128)(2,1)S(1)} %bitcast.15), custom_call_target="tpu_custom_call" | custom-call | flops 1 | bytes 1 | tf_op jit(solution)/shard_map/mix/pallas_call | solution.py:301
  142.4 2.1 %mix.13.refs_0_ = bf16[128,2560]{1,0:T(8,128)(2,1)S(1)} custom-call(bf16[128,1024]{1,0:T(8,128)(2,1)S(1)} %get-tuple-element.87.rows_ref, bf16[1024,5120]{1,0:T(8,128)(2,1)S(1)} %bitcast.15), custom_call_target="tpu_custom_call" | custom-call | flops 1 | bytes 1 | tf_op jit(solution)/shard_map/mix/pallas_call | solution.py:301
  144.5 6.3 %collective-permute-start.26 = (bf16[128,2560]{1,0:T(8,128)(2,1)S(1)}, bf16[128,2560]{1,0:T(8,128)(2,1)S(1)}, u32[]{:S(2)}, u32[]{:S(2)}) collective-permute-start(bf16[128,2560]{1,0:T(8,128)(2,1)S(1)} %mix.10.refs_0_), channel_id=1, source_target_pairs={{0,1},{3,2},{4,5},{7,6},{8,9},{11,10},{12,13},{15,14},{16,17},{19,... | collective-permute-start | bytes 1966088 | tf_op jit(solution)/shard_map/ppermute | solution.py:420
  150.8 2.3 %collective-permute-done.21.refs_1_ = bf16[128,2560]{1,0:T(8,128)(2,1)S(1)} collective-permute-done((bf16[128,2560]{1,0:T(8,128)(2,1)S(1)}, bf16[128,2560]{1,0:T(8,128)(2,1)S(1)}, u32[]{:S(2)}, u32[]{:S(2)}) %collective-permute-start.21) | collective-permute-done | bytes 655392 | tf_op jit(solution)/shard_map/ppermute | solution.py:420
  153.2 0.7 collective-permute-start.25
  154.0 2.1 %mix.15.refs_0_ = bf16[128,2560]{1,0:T(8,128)(2,1)S(1)} custom-call(bf16[128,1024]{1,0:T(8,128)(2,1)S(1)} %get-tuple-element.82.rows_ref, bf16[1024,5120]{1,0:T(8,128)(2,1)S(1)} %bitcast.15), custom_call_target="tpu_custom_call" | custom-call | flops 1 | bytes 1 | tf_op jit(solution)/shard_map/mix/pallas_call | solution.py:301
  156.0 2.1 %mix.14.refs_0_ = bf16[128,2560]{1,0:T(8,128)(2,1)S(1)} custom-call(bf16[128,1024]{1,0:T(8,128)(2,1)S(1)} %get-tuple-element.82.rows_ref, bf16[1024,5120]{1,0:T(8,128)(2,1)S(1)} %bitcast.15), custom_call_target="tpu_custom_call" | custom-call | flops 1 | bytes 1 | tf_op jit(solution)/shard_map/mix/pallas_call | solution.py:301
  158.3 1.3 collective-permute-start.24
  159.6 6.8 %collective-permute-start.30 = (bf16[128,2560]{1,0:T(8,128)(2,1)S(1)}, bf16[128,2560]{1,0:T(8,128)(2,1)S(1)}, u32[]{:S(2)}, u32[]{:S(2)}) collective-permute-start(bf16[128,2560]{1,0:T(8,128)(2,1)S(1)} %mix.11.refs_0_), channel_id=1, source_target_pairs={{0,1},{3,2},{4,5},{7,6},{8,9},{11,10},{12,13},{15,14},{16,17},{19,... | collective-permute-start | bytes 1966088 | tf_op jit(solution)/shard_map/ppermute | solution.py:420
  166.4 1.3 collective-permute-start.29
  167.8 0.7 collective-permute-start.27
  168.7 1.3 collective-permute-start.28
  170.0 10.0 %collective-permute-done.24.refs_1_ = bf16[128,2560]{1,0:T(8,128)(2,1)S(1)} collective-permute-done((bf16[128,2560]{1,0:T(8,128)(2,1)S(1)}, bf16[128,2560]{1,0:T(8,128)(2,1)S(1)}, u32[]{:S(2)}, u32[]{:S(2)}) %collective-permute-start.24) | collective-permute-done | bytes 655392 | tf_op jit(solution)/shard_map/ppermute | solution.py:417
  180.1 1.3 collective-permute-done.30.refs_1_
  181.6 0.7 collective-permute-start.32
  182.4 4.1 %collective-permute-done.29.rows_ref = bf16[128,1024]{1,0:T(8,128)(2,1)S(1)} collective-permute-done((bf16[128,1024]{1,0:T(8,128)(2,1)S(1)}, bf16[128,1024]{1,0:T(8,128)(2,1)S(1)}, u32[]{:S(2)}, u32[]{:S(2)}) %collective-permute-start.29) | collective-permute-done | bytes 262176 | tf_op jit(solution)/shard_map/ppermute | solution.py:420
  186.4 4.4 %collective-permute-start.31 = (bf16[128,2560]{1,0:T(8,128)(2,1)S(1)}, bf16[128,2560]{1,0:T(8,128)(2,1)S(1)}, u32[]{:S(2)}, u32[]{:S(2)}) collective-permute-start(bf16[128,2560]{1,0:T(8,128)(2,1)S(1)} %mix.12.refs_0_), channel_id=1, source_target_pairs={{0,1},{3,2},{4,5},{7,6},{8,9},{11,10},{12,13},{15,14},{16,17},{19,... | collective-permute-start | bytes 1966088 | tf_op jit(solution)/shard_map/ppermute | solution.py:420
  190.8 2.6 %mix_sent.1.refs_2_ = bf16[128,2560]{1,0:T(8,128)(2,1)S(1)} custom-call(s32[12]{0:T(128)S(1)} %stack.51.places_ref, bf16[128,1024]{1,0:T(8,128)(2,1)S(1)} %collective-permute-done.29.rows_ref, bf16[256,2560]{1,0:T(8,128)(2,1)S(1)} %collective-permute-done.10.refs_0_, bf16[256,2560]{1,0:T(8,128)(2,1)S(1)} %collective-permute-done.11.refs_1_, ...), custom_call_target="tpu_custom_call" | custom-call | flops 1 | bytes 1 | tf_op jit(solution)/shard_map/mix_sent/pallas_call | solution.py:357
  193.9 1.0 added.20.refs_2_
  194.9 9.5 %collective-permute-done.31.refs_1_ = bf16[128,2560]{1,0:T(8,128)(2,1)S(1)} collective-permute-done((bf16[128,2560]{1,0:T(8,128)(2,1)S(1)}, bf16[128,2560]{1,0:T(8,128)(2,1)S(1)}, u32[]{:S(2)}, u32[]{:S(2)}) %collective-permute-start.31) | collective-permute-done | bytes 655392 | tf_op jit(solution)/shard_map/ppermute | solution.py:420
  204.4 1.0 added.21
  (61 shorter events, 4.5 us)
Async XLA Ops:
  0.0 15.6 %copy-start.3 = (bf16[5120,128]{1,0:T(8,128)(2,1)S(1)}, bf16[5120,128]{1,0:T(8,128)(2,1)}, u32[]{:S(2)}) copy-start(bf16[5120,128]{1,0:T(8,128)(2,1)} %refs_4_.5) | copy-start | bytes 3932164
  0.0 15.6 %copy-start.4 = (bf16[512,1280]{1,0:T(8,128)(2,1)S(1)}, bf16[512,1280]{1,0:T(8,128)(2,1)}, u32[]{:S(2)}) copy-start(bf16[512,1280]{1,0:T(8,128)(2,1)} %refs_0_.1) | copy-start | bytes 3932164
  2.6 20.0 %collective-permute-start.1 = (bf16[256,1280]{1,0:T(8,128)(2,1)}, bf16[256,1280]{1,0:T(8,128)(2,1)}, u32[]{:S(2)}, u32[]{:S(2)}) collective-permute-start(bf16[256,1280]{1,0:T(8,128)(2,1)} %get-tuple-element.94), channel_id=1, source_target_pairs={{1,2},{2,1},{5,6},{6,5},{9,10},{10,9},{13,14},{14,13},{17,18},{18,... | collective-permute-start | bytes 1966088 | tf_op jit(solution)/shard_map/ppermute | solution.py:414
  4.1 20.9 %collective-permute-start = (bf16[256,1280]{1,0:T(8,128)(2,1)}, bf16[256,1280]{1,0:T(8,128)(2,1)S(1)}, u32[]{:S(2)}, u32[]{:S(2)}) collective-permute-start(bf16[256,1280]{1,0:T(8,128)(2,1)} %get-tuple-element.94), channel_id=1, source_target_pairs={{0,1},{1,0},{2,3},{3,2},{4,5},{5,4},{6,7},{7,6},{8,9},{9,8},{10,11... | collective-permute-start | bytes 1966088 | tf_op jit(solution)/shard_map/ppermute | solution.py:411
  9.2 28.8 %collective-permute-start.4 = (bf16[256,1280]{1,0:T(8,128)(2,1)}, bf16[256,1280]{1,0:T(8,128)(2,1)}, u32[]{:S(2)}, u32[]{:S(2)}) collective-permute-start(bf16[256,1280]{1,0:T(8,128)(2,1)} %get-tuple-element.93), channel_id=1, source_target_pairs={{0,1},{1,0},{2,3},{3,2},{4,5},{5,4},{6,7},{7,6},{8,9},{9,8},{10,11... | collective-permute-start | bytes 1966088 | tf_op jit(solution)/shard_map/ppermute | solution.py:411
  9.2 36.0 %collective-permute-start.6 = (bf16[256,1280]{1,0:T(8,128)(2,1)}, bf16[256,1280]{1,0:T(8,128)(2,1)}, u32[]{:S(2)}, u32[]{:S(2)}) collective-permute-start(bf16[256,1280]{1,0:T(8,128)(2,1)} %get-tuple-element.93), channel_id=1, source_target_pairs={{1,2},{2,1},{5,6},{6,5},{9,10},{10,9},{13,14},{14,13},{17,18},{18,... | collective-permute-start | bytes 1966088 | tf_op jit(solution)/shard_map/ppermute | solution.py:414
  10.8 4.0 %copy-start = (bf16[1024,5120]{1,0:T(8,128)(2,1)S(1)}, bf16[1024,5120]{1,0:T(8,128)(2,1)}, u32[]{:S(2)}) copy-start(bf16[1024,5120]{1,0:T(8,128)(2,1)} %w_ref.17) | copy-start | bytes 31457284
  14.8 4.0 %copy-start.1 = (bf16[5120,1024]{1,0:T(8,128)(2,1)S(1)}, bf16[5120,1024]{1,0:T(8,128)(2,1)}, u32[]{:S(2)}) copy-start(bf16[5120,1024]{1,0:T(8,128)(2,1)} %refs_2_.8) | copy-start | bytes 31457284
  14.8 4.3 %copy-start.2 = (bf16[5120,128]{1,0:T(8,128)(2,1)S(1)}, bf16[5120,128]{1,0:T(8,128)(2,1)}, u32[]{:S(2)}) copy-start(bf16[5120,128]{1,0:T(8,128)(2,1)} %refs_3_.7) | copy-start | bytes 3932164
  25.0 19.0 %collective-permute-start.2 = (bf16[256,1280]{1,0:T(8,128)(2,1)S(1)}, bf16[256,1280]{1,0:T(8,128)(2,1)S(1)}, u32[]{:S(2)}, u32[]{:S(2)}) collective-permute-start(bf16[256,1280]{1,0:T(8,128)(2,1)S(1)} %collective-permute-done.refs_0_), channel_id=1, source_target_pairs={{1,2},{2,1},{5,6},{6,5},{9,10},{10,9},{13,14},{14,13},{17,18},{18,... | collective-permute-start | bytes 1966088 | tf_op jit(solution)/shard_map/ppermute | solution.py:414
  38.0 19.8 %collective-permute-start.5 = (bf16[256,1280]{1,0:T(8,128)(2,1)}, bf16[256,1280]{1,0:T(8,128)(2,1)S(1)}, u32[]{:S(2)}, u32[]{:S(2)}) collective-permute-start(bf16[256,1280]{1,0:T(8,128)(2,1)} %collective-permute-done.1.refs_0_), channel_id=1, source_target_pairs={{1,0},{2,3},{5,4},{6,7},{9,8},{10,11},{13,12},{14,15},{17,16},{18,... | collective-permute-start | bytes 1966088 | tf_op jit(solution)/shard_map/ppermute | solution.py:417
  39.3 32.5 %collective-permute-start.10 = (bf16[256,2560]{1,0:T(8,128)(2,1)S(1)}, bf16[256,2560]{1,0:T(8,128)(2,1)S(1)}, u32[]{:S(2)}, u32[]{:S(2)}) collective-permute-start(bf16[256,2560]{1,0:T(8,128)(2,1)S(1)} %eighths.1), channel_id=1, source_target_pairs={{0,1},{3,2},{4,5},{7,6},{8,9},{11,10},{12,13},{15,14},{16,17},{19,... | collective-permute-start | bytes 3932168 | tf_op jit(solution)/shard_map/ppermute | solution.py:420
  44.0 27.8 %collective-permute-start.3 = (bf16[256,1280]{1,0:T(8,128)(2,1)S(1)}, bf16[256,1280]{1,0:T(8,128)(2,1)S(1)}, u32[]{:S(2)}, u32[]{:S(2)}) collective-permute-start(bf16[256,1280]{1,0:T(8,128)(2,1)S(1)} %collective-permute-done.2.refs_0_), channel_id=1, source_target_pairs={{1,0},{2,3},{5,4},{6,7},{9,8},{10,11},{13,12},{14,15},{17,16},{18,... | collective-permute-start | bytes 1966088 | tf_op jit(solution)/shard_map/ppermute | solution.py:417
  57.7 14.1 %collective-permute-start.7 = (bf16[256,1280]{1,0:T(8,128)(2,1)}, bf16[256,1280]{1,0:T(8,128)(2,1)S(1)}, u32[]{:S(2)}, u32[]{:S(2)}) collective-permute-start(bf16[256,1280]{1,0:T(8,128)(2,1)} %collective-permute-done.4.refs_1_), channel_id=1, source_target_pairs={{1,2},{2,1},{5,6},{6,5},{9,10},{10,9},{13,14},{14,13},{17,18},{18,... | collective-permute-start | bytes 1966088 | tf_op jit(solution)/shard_map/ppermute | solution.py:414
  58.4 25.3 %collective-permute-start.8 = (bf16[256,1280]{1,0:T(8,128)(2,1)}, bf16[256,1280]{1,0:T(8,128)(2,1)S(1)}, u32[]{:S(2)}, u32[]{:S(2)}) collective-permute-start(bf16[256,1280]{1,0:T(8,128)(2,1)} %collective-permute-done.6.refs_2_), channel_id=1, source_target_pairs={{1,0},{2,3},{5,4},{6,7},{9,8},{10,11},{13,12},{14,15},{17,16},{18,... | collective-permute-start | bytes 1966088 | tf_op jit(solution)/shard_map/ppermute | solution.py:417
  71.8 27.4 %collective-permute-start.11 = (bf16[256,2560]{1,0:T(8,128)(2,1)S(1)}, bf16[256,2560]{1,0:T(8,128)(2,1)S(1)}, u32[]{:S(2)}, u32[]{:S(2)}) collective-permute-start(bf16[256,2560]{1,0:T(8,128)(2,1)S(1)} %collective-permute-done.10.refs_0_), channel_id=1, source_target_pairs={{0,8},{4,12},{8,0},{12,4},{16,24},{20,28},{24,16},{28,20},{1,9},{5... | collective-permute-start | bytes 3932168 | tf_op jit(solution)/shard_map/ppermute | solution.py:423
  73.3 25.9 %collective-permute-start.12 = (bf16[256,2560]{1,0:T(8,128)(2,1)S(1)}, bf16[256,2560]{1,0:T(8,128)(2,1)S(1)}, u32[]{:S(2)}, u32[]{:S(2)}) collective-permute-start(bf16[256,2560]{1,0:T(8,128)(2,1)S(1)} %collective-permute-done.10.refs_0_), channel_id=1, source_target_pairs={{0,4},{4,0},{8,12},{12,8},{16,20},{20,16},{24,28},{28,24},{1,5},{5... | collective-permute-start | bytes 3932168 | tf_op jit(solution)/shard_map/ppermute | solution.py:423
  83.8 6.2 %copy-start.5 = (f32[512,128]{1,0:T(8,128)S(1)}, f32[512,128]{1,0:T(8,128)}, u32[]{:S(2)}) copy-start(f32[512,128]{1,0:T(8,128)} %constant.30.clone.refs_6_.refs_8_.refs_9_) | copy-start | bytes 786436
  83.8 6.2 %copy-start.6 = (f32[512,128]{1,0:T(8,128)S(1)}, f32[512,128]{1,0:T(8,128)}, u32[]{:S(2)}) copy-start(f32[512,128]{1,0:T(8,128)} %constant.29.clone.refs_5_.refs_7_.refs_8_) | copy-start | bytes 786436
  83.8 6.2 %copy-start.8 = (f32[128]{0:T(128)S(1)}, f32[128]{0:T(128)}, u32[]{:S(2)}) copy-start(f32[128]{0:T(128)} %param.18) | copy-start | bytes 1540
  83.8 16.7 %collective-permute-start.9 = (bf16[256,1280]{1,0:T(8,128)(2,1)S(1)}, bf16[256,1280]{1,0:T(8,128)(2,1)S(1)}, u32[]{:S(2)}, u32[]{:S(2)}) collective-permute-start(bf16[256,1280]{1,0:T(8,128)(2,1)S(1)} %collective-permute-done.7.refs_0_.refs_1_), channel_id=1, source_target_pairs={{1,0},{2,3},{5,4},{6,7},{9,8},{10,11},{13,12},{14,15},{17,16},{18,... | collective-permute-start | bytes 1966088 | tf_op jit(solution)/shard_map/ppermute | solution.py:417
  90.0 2.5 %copy-start.7 = (f32[128]{0:T(128)S(1)}, f32[128]{0:T(128)}, u32[]{:S(2)}) copy-start(f32[128]{0:T(128)} %param.19) | copy-start | bytes 1540
  92.5 8.0 %copy-start.9 = (s32[1,128]{1,0:T(1,128)S(1)}, s32[1,128]{1,0:T(1,128)}, u32[]{:S(2)}) copy-start(s32[1,128]{1,0:T(1,128)} %refs_10_.1) | copy-start | bytes 1540
  100.5 18.3 %slice-start = ((s8[10485760]{0:T(1024)(128)(4,1)}), s8[4194304]{0:T(1024)(128)(4,1)S(1)}, s32[]{:S(2)}) async-start(s8[10485760]{0:T(1024)(128)(4,1)} %bitcast.14), calls=%async_computation | async-start | bytes 8388608
  101.8 5.3 %collective-permute-start.19 = (bf16[128,256]{1,0:T(8,128)(2,1)S(1)}, bf16[128,256]{1,0:T(8,128)(2,1)S(1)}, u32[]{:S(2)}, u32[]{:S(2)}) collective-permute-start(bf16[128,256]{1,0:T(8,128)(2,1)S(1)} %get-tuple-element.73), channel_id=1, source_target_pairs={{0,28},{4,24},{8,20},{12,16},{16,12},{20,8},{24,4},{28,0},{1,29},{... | collective-permute-start | bytes 196616 | tf_op jit(solution)/shard_map/ppermute | solution.py:423
  101.8 6.2 %collective-permute-start.18 = (bf16[128,256]{1,0:T(8,128)(2,1)S(1)}, bf16[128,256]{1,0:T(8,128)(2,1)S(1)}, u32[]{:S(2)}, u32[]{:S(2)}) collective-permute-start(bf16[128,256]{1,0:T(8,128)(2,1)S(1)} %get-tuple-element.73), channel_id=1, source_target_pairs={{0,24},{4,28},{8,16},{12,20},{16,8},{20,12},{24,0},{28,4},{1,25},{... | collective-permute-start | bytes 196616 | tf_op jit(solution)/shard_map/ppermute | solution.py:423
  104.4 5.5 %collective-permute-start.17 = (bf16[128,256]{1,0:T(8,128)(2,1)S(1)}, bf16[128,256]{1,0:T(8,128)(2,1)S(1)}, u32[]{:S(2)}, u32[]{:S(2)}) collective-permute-start(bf16[128,256]{1,0:T(8,128)(2,1)S(1)} %get-tuple-element.73), channel_id=1, source_target_pairs={{0,20},{4,16},{8,28},{12,24},{16,4},{20,0},{24,12},{28,8},{1,21},{... | collective-permute-start | bytes 196616 | tf_op jit(solution)/shard_map/ppermute | solution.py:423
  105.7 5.6 %collective-permute-start.16 = (bf16[128,256]{1,0:T(8,128)(2,1)S(1)}, bf16[128,256]{1,0:T(8,128)(2,1)S(1)}, u32[]{:S(2)}, u32[]{:S(2)}) collective-permute-start(bf16[128,256]{1,0:T(8,128)(2,1)S(1)} %get-tuple-element.73), channel_id=1, source_target_pairs={{0,16},{4,20},{8,24},{12,28},{16,0},{20,4},{24,8},{28,12},{1,17},{... | collective-permute-start | bytes 196616 | tf_op jit(solution)/shard_map/ppermute | solution.py:423
  106.2 5.1 %collective-permute-start.15 = (bf16[128,256]{1,0:T(8,128)(2,1)S(1)}, bf16[128,256]{1,0:T(8,128)(2,1)S(1)}, u32[]{:S(2)}, u32[]{:S(2)}) collective-permute-start(bf16[128,256]{1,0:T(8,128)(2,1)S(1)} %get-tuple-element.73), channel_id=1, source_target_pairs={{0,12},{4,8},{8,4},{12,0},{16,28},{20,24},{24,20},{28,16},{1,13},{... | collective-permute-start | bytes 196616 | tf_op jit(solution)/shard_map/ppermute | solution.py:423
  107.0 5.0 %collective-permute-start.14 = (bf16[128,256]{1,0:T(8,128)(2,1)S(1)}, bf16[128,256]{1,0:T(8,128)(2,1)S(1)}, u32[]{:S(2)}, u32[]{:S(2)}) collective-permute-start(bf16[128,256]{1,0:T(8,128)(2,1)S(1)} %get-tuple-element.73), channel_id=1, source_target_pairs={{0,8},{4,12},{8,0},{12,4},{16,24},{20,28},{24,16},{28,20},{1,9},{5... | collective-permute-start | bytes 196616 | tf_op jit(solution)/shard_map/ppermute | solution.py:423
  108.0 4.0 %collective-permute-start.13 = (bf16[128,256]{1,0:T(8,128)(2,1)S(1)}, bf16[128,256]{1,0:T(8,128)(2,1)S(1)}, u32[]{:S(2)}, u32[]{:S(2)}) collective-permute-start(bf16[128,256]{1,0:T(8,128)(2,1)S(1)} %get-tuple-element.73), channel_id=1, source_target_pairs={{0,4},{4,0},{8,12},{12,8},{16,20},{20,16},{24,28},{28,24},{1,5},{5... | collective-permute-start | bytes 196616 | tf_op jit(solution)/shard_map/ppermute | solution.py:423
  112.0 15.6 %collective-permute-start.20 = (bf16[256,2560]{1,0:T(8,128)(2,1)S(1)}, bf16[256,2560]{1,0:T(8,128)(2,1)S(1)}, u32[]{:S(2)}, u32[]{:S(2)}) collective-permute-start(bf16[256,2560]{1,0:T(8,128)(2,1)S(1)} %collective-permute-done.11.refs_1_), channel_id=1, source_target_pairs={{0,4},{4,0},{8,12},{12,8},{16,20},{20,16},{24,28},{28,24},{1,5},{5... | collective-permute-start | bytes 3932168 | tf_op jit(solution)/shard_map/ppermute | solution.py:423
  112.7 6.1 %slice-start.1 = ((s8[10485760]{0:T(1024)(128)(4,1)}), s8[4194304]{0:T(1024)(128)(4,1)S(1)}, s32[]{:S(2)}) async-start(s8[10485760]{0:T(1024)(128)(4,1)} %bitcast.14), calls=%async_computation.1 | async-start | bytes 8388608
  112.7 6.1 %slice-start.2 = ((s8[10485760]{0:T(1024)(128)(4,1)}), s8[2097152]{0:T(1024)(128)(4,1)S(1)}, s32[]{:S(2)}) async-start(s8[10485760]{0:T(1024)(128)(4,1)} %bitcast.14), calls=%async_computation.2 | async-start | bytes 4194304
  120.9 18.6 %collective-permute-start.22 = (bf16[128,2560]{1,0:T(8,128)(2,1)S(1)}, bf16[128,2560]{1,0:T(8,128)(2,1)S(1)}, u32[]{:S(2)}, u32[]{:S(2)}) collective-permute-start(bf16[128,2560]{1,0:T(8,128)(2,1)S(1)} %mix.8.refs_0_), channel_id=1, source_target_pairs={{0,1},{3,2},{4,5},{7,6},{8,9},{11,10},{12,13},{15,14},{16,17},{19,... | collective-permute-start | bytes 1966088 | tf_op jit(solution)/shard_map/ppermute | solution.py:420
  126.3 26.8 %collective-permute-start.21 = (bf16[128,2560]{1,0:T(8,128)(2,1)S(1)}, bf16[128,2560]{1,0:T(8,128)(2,1)S(1)}, u32[]{:S(2)}, u32[]{:S(2)}) collective-permute-start(bf16[128,2560]{1,0:T(8,128)(2,1)S(1)} %mix.9.refs_0_), channel_id=1, source_target_pairs={{0,1},{3,2},{4,5},{7,6},{8,9},{11,10},{12,13},{15,14},{16,17},{19,... | collective-permute-start | bytes 1966088 | tf_op jit(solution)/shard_map/ppermute | solution.py:420
  139.6 18.5 %collective-permute-start.23 = (bf16[128,2560]{1,0:T(8,128)(2,1)S(1)}, bf16[128,2560]{1,0:T(8,128)(2,1)S(1)}, u32[]{:S(2)}, u32[]{:S(2)}) collective-permute-start(bf16[128,2560]{1,0:T(8,128)(2,1)S(1)} %added.11), channel_id=1, source_target_pairs={{1,2},{2,1},{5,6},{6,5},{9,10},{10,9},{13,14},{14,13},{17,18},{18,... | collective-permute-start | bytes 1966088 | tf_op jit(solution)/shard_map/ppermute | solution.py:414
  144.5 23.2 %collective-permute-start.26 = (bf16[128,2560]{1,0:T(8,128)(2,1)S(1)}, bf16[128,2560]{1,0:T(8,128)(2,1)S(1)}, u32[]{:S(2)}, u32[]{:S(2)}) collective-permute-start(bf16[128,2560]{1,0:T(8,128)(2,1)S(1)} %mix.10.refs_0_), channel_id=1, source_target_pairs={{0,1},{3,2},{4,5},{7,6},{8,9},{11,10},{12,13},{15,14},{16,17},{19,... | collective-permute-start | bytes 1966088 | tf_op jit(solution)/shard_map/ppermute | solution.py:420
  153.2 15.3 %collective-permute-start.25 = (bf16[128,2560]{1,0:T(8,128)(2,1)S(1)}, bf16[128,2560]{1,0:T(8,128)(2,1)S(1)}, u32[]{:S(2)}, u32[]{:S(2)}) collective-permute-start(bf16[128,2560]{1,0:T(8,128)(2,1)S(1)} %added.12), channel_id=1, source_target_pairs={{1,2},{2,1},{5,6},{6,5},{9,10},{10,9},{13,14},{14,13},{17,18},{18,... | collective-permute-start | bytes 1966088 | tf_op jit(solution)/shard_map/ppermute | solution.py:414
  158.3 21.7 %collective-permute-start.24 = (bf16[128,2560]{1,0:T(8,128)(2,1)S(1)}, bf16[128,2560]{1,0:T(8,128)(2,1)S(1)}, u32[]{:S(2)}, u32[]{:S(2)}) collective-permute-start(bf16[128,2560]{1,0:T(8,128)(2,1)S(1)} %added.13), channel_id=1, source_target_pairs={{1,0},{2,3},{5,4},{6,7},{9,8},{10,11},{13,12},{14,15},{17,16},{18,... | collective-permute-start | bytes 1966088 | tf_op jit(solution)/shard_map/ppermute | solution.py:417
  159.6 21.9 %collective-permute-start.30 = (bf16[128,2560]{1,0:T(8,128)(2,1)S(1)}, bf16[128,2560]{1,0:T(8,128)(2,1)S(1)}, u32[]{:S(2)}, u32[]{:S(2)}) collective-permute-start(bf16[128,2560]{1,0:T(8,128)(2,1)S(1)} %mix.11.refs_0_), channel_id=1, source_target_pairs={{0,1},{3,2},{4,5},{7,6},{8,9},{11,10},{12,13},{15,14},{16,17},{19,... | collective-permute-start | bytes 1966088 | tf_op jit(solution)/shard_map/ppermute | solution.py:420
  166.4 20.1 %collective-permute-start.29 = (bf16[128,1024]{1,0:T(8,128)(2,1)S(1)}, bf16[128,1024]{1,0:T(8,128)(2,1)S(1)}, u32[]{:S(2)}, u32[]{:S(2)}) collective-permute-start(bf16[128,1024]{1,0:T(8,128)(2,1)S(1)} %get-tuple-element.87.rows_ref), channel_id=1, source_target_pairs={{0,1},{3,2},{4,5},{7,6},{8,9},{11,10},{12,13},{15,14},{16,17},{19,... | collective-permute-start | bytes 786440 | tf_op jit(solution)/shard_map/ppermute | solution.py:420
  167.8 25.9 %collective-permute-start.27 = (bf16[128,2560]{1,0:T(8,128)(2,1)S(1)}, bf16[128,2560]{1,0:T(8,128)(2,1)S(1)}, u32[]{:S(2)}, u32[]{:S(2)}) collective-permute-start(bf16[128,2560]{1,0:T(8,128)(2,1)S(1)} %added.14), channel_id=1, source_target_pairs={{1,2},{2,1},{5,6},{6,5},{9,10},{10,9},{13,14},{14,13},{17,18},{18,... | collective-permute-start | bytes 1966088 | tf_op jit(solution)/shard_map/ppermute | solution.py:414
  168.7 24.7 %collective-permute-start.28 = (bf16[128,2560]{1,0:T(8,128)(2,1)S(1)}, bf16[128,2560]{1,0:T(8,128)(2,1)S(1)}, u32[]{:S(2)}, u32[]{:S(2)}) collective-permute-start(bf16[128,2560]{1,0:T(8,128)(2,1)S(1)} %added.15), channel_id=1, source_target_pairs={{1,0},{2,3},{5,4},{6,7},{9,8},{10,11},{13,12},{14,15},{17,16},{18,... | collective-permute-start | bytes 1966088 | tf_op jit(solution)/shard_map/ppermute | solution.py:417
  181.6 12.2 %collective-permute-start.32 = (bf16[128,2560]{1,0:T(8,128)(2,1)S(1)}, bf16[128,2560]{1,0:T(8,128)(2,1)S(1)}, u32[]{:S(2)}, u32[]{:S(2)}) collective-permute-start(bf16[128,2560]{1,0:T(8,128)(2,1)S(1)} %added.17), channel_id=1, source_target_pairs={{1,2},{2,1},{5,6},{6,5},{9,10},{10,9},{13,14},{14,13},{17,18},{18,... | collective-permute-start | bytes 1966088 | tf_op jit(solution)/shard_map/ppermute | solution.py:414
  186.4 17.9 %collective-permute-start.31 = (bf16[128,2560]{1,0:T(8,128)(2,1)S(1)}, bf16[128,2560]{1,0:T(8,128)(2,1)S(1)}, u32[]{:S(2)}, u32[]{:S(2)}) collective-permute-start(bf16[128,2560]{1,0:T(8,128)(2,1)S(1)} %mix.12.refs_0_), channel_id=1, source_target_pairs={{0,1},{3,2},{4,5},{7,6},{8,9},{11,10},{12,13},{15,14},{16,17},{19,... | collective-permute-start | bytes 1966088 | tf_op jit(solution)/shard_map/ppermute | solution.py:420

commit v8 on v7

--- a/solution.py
+++ b/solution.py
@@ -313,24 +313,24 @@
     )(attended, w_out)
 
 
-def eighths_kernel(places_ref, w_ref, out_ref):
+def eighth_kernel(places_ref, w_ref, out_ref):
     out_ref[...] = w_ref[...]
 
 
-def eighths(places, w_out, share):
+def eighth(places, which, w_out, share):
     width = w_out.shape[1] // 2
     return pl.pallas_call(
-        eighths_kernel,
+        eighth_kernel,
         grid_spec=pltpu.PrefetchScalarGridSpec(
             num_scalar_prefetch=1,
-            grid=(2,),
-            in_specs=[pl.BlockSpec((share, width), lambda i, p: (p[EIGHTHS + i], 1))],
-            out_specs=pl.BlockSpec((share, width), lambda i, p: (i, 0)),
-        ),
-        out_shape=jax.ShapeDtypeStruct((2 * share, width), w_out.dtype),
+            grid=(1,),
+            in_specs=[pl.BlockSpec((share, width), lambda i, p: (p[EIGHTHS + which], 1))],
+            out_specs=whole(share, width),
+        ),
+        out_shape=jax.ShapeDtypeStruct((share, width), w_out.dtype),
         compiler_params=params(8),
         cost_estimate=cost(1),
-        name="eighths",
+        name="eighth",
     )(places, w_out)
 
 
@@ -442,19 +442,21 @@
     accs = partial_projection(places, OWN, [[hidden_in]], weights, None)
     from_near[0], from_mid[0], accs = lax.optimization_barrier((from_near[0], from_mid[0], accs))
     to_outer = [outward(array) for array in from_mid]
-    to_inner = [across(from_near[0])]
-    to_inner.append(across(after(from_near[1], (to_outer[0], from_mid[1]))))
-    pieces = []
-    if spread:
-        pieces.append(inward(after(eighths(places, w_out, share), from_near)))
     cue = (from_near[1], from_mid[1])
     accs = partial_projection(
         after(places, cue), NEAR, [[a] for a in from_near], weights, accs
     )
-    end = [outward(to_inner[0]), outward(after(to_inner[1], (to_outer[1], accs)))]
+    to_inner = [across(from_near[0])]
+    to_inner.append(across(after(from_near[1], (to_outer[0], accs))))
+    end = [outward(array) for array in to_inner]
+    pieces = {}
     if spread:
-        pieces.append(between(after(pieces[0], to_inner[1]), OFFSETS[2]))
-        pieces.append(between(after(pieces[0], end[0]), 1))
+        first, second = (eighth(places, i, w_out, share) for i in (0, 1))
+        pieces[0] = inward(after(first, to_outer[0]))
+        cue = (to_inner[1], to_outer[1])
+        pieces[6] = inward(after(second, cue))
+        first = after(pieces[0], cue)
+        pieces[2], pieces[4] = between(first, 2), between(first, 4)
     cue = (to_inner, accs)
     accs = partial_projection(
         after(places, cue), THIRD, [[a, b] for a, b in zip(from_mid, to_outer)], weights, accs
@@ -479,46 +481,57 @@
     second_queries = queries_of(places, final[1], 1, w_query, accs[0], q_gain, *tables)
     queries = [first_queries, second_queries]
 
+    if spread:
+        cue = (others, second_queries)
+        for offset in (0, 6, 2, 4):
+            pieces[offset ^ 1] = between(after(pieces[offset], cue), 1)
+
     def attend(slots):
         return attention(places, slots, rows_here // 4, lengths, queries, own, others)
 
+    def send(rows, part):
+        return inward(rows if spread else part)
+
+    def share_of(arrived):
+        if not spread:
+            return arrived
+        return mix_sent(places, arrived, [pieces[offset] for offset in OFFSETS])
+
     def mixed(rows):
         return [mix(rows, w_out, which) for which in (0, 1)]
 
-    if spread:
-        pieces.append(between(after(pieces[1], others), 1))
     (far_rows,) = attend((LAST,))
     far = mixed(far_rows)
-    places = after(places, (far, pieces))
-    third_rows, near_rows, own_rows = attend((THIRD, NEAR, OWN))
-    mid = mixed(third_rows)
-    far_in = [inward(array) for array in far]
-    mid_in = [inward(array) for array in mid]
-
-    far_sum = added(far[0], after(far_in[0], mid))
-    near_part = mixed(after(near_rows, far_sum))
-    far_sum = [far_sum, added(far[1], after(far_in[1], near_part))]
-    kept = mixed(after(own_rows, far_sum[1]))
-    far_sum = [across(array) for array in far_sum]
-    out_sum, mid_sum = [None, None], [None, None]
-    out_sum[0] = added(near_part[0], after(far_sum[0], kept))
-    mid_sum[0] = added(mid[0], after(mid_in[0], out_sum[0]))
-    out_sum[1] = added(near_part[1], after(far_sum[1], mid_sum[0]))
-    from_inner = [outward(array) for array in out_sum]
-    kept[0] = added(kept[0], after(from_inner[0], out_sum[1]))
-    mid_sum[1] = added(mid[1], after(mid_in[1], kept[0]))
-    cue = mid_sum[1]
-    mid_sum = [across(array) for array in mid_sum]
-    if spread:
-        near_in = inward(after(near_rows, out_sum[0]))
-        sent = mix_sent(places, after(near_in, cue), pieces)
-    else:
-        sent = inward(near_part[1])
-    near_in = inward(after(near_part[0], near_in if spread else out_sum[1]))
-    kept[1] = added(kept[1], from_inner[1], sent)
-    kept[0] = added(kept[0], after(mid_sum[0], kept[1]))
-    result = added(kept[1], after(mid_sum[1], kept[0]), half=1)
-    return added(kept[0], near_in, half=0, into=result)
+    far_sent = send(far_rows, far[1])
+    places = after(places, far)
+    (third_rows,) = attend((THIRD,))
+    far_sent = after(far_sent, third_rows)
+    far_in = inward(after(far[0], far_sent))
+    far_right = added(far[1], share_of(far_sent))
+    third = mixed(after(third_rows, far_right))
+    third_sent = send(third_rows, third[1])
+    far_right = across(far_right)
+    places = after(places, third)
+    near_rows, own_rows = attend((NEAR, OWN))
+    far_left = added(far[0], after(far_in, near_rows))
+    third_sent = after(third_sent, far_left)
+    far_left = across(far_left)
+    third_in = inward(after(third[0], third_sent))
+    third_right = added(third[1], share_of(third_sent))
+    near = mixed(after(near_rows, third_right))
+    near_sent = send(near_rows, near[1])
+    third_right = across(third_right)
+    out_right = added(near[1], after(far_right, near))
+    kept = mixed(after(own_rows, (out_right, far_left)))
+    near_sent = after(near_sent, kept)
+    near_in = inward(after(near[0], near_sent))
+    near_sent = share_of(near_sent)
+    third_left = added(third[0], after(third_in, near_sent))
+    arrived = after((outward(out_right), third_right), third_left)
+    result = added(kept[1], near_sent, *arrived, half=1)
+    third_left = across(third_left)
+    out_left = outward(added(near[0], after(far_left, result)))
+    return added(kept[0], near_in, out_left, third_left, half=0, into=result)
 
 
 def solution(mesh):

time: 206 us -> 197 us (0.956)
  waiting for transfers between devices: 82.8 us -> 47.2 us
  Pallas kernels: 54.7 us -> 67 us
  starting transfers between devices: 56.5 us -> 64.5 us
  local copies, waits for them, and re-layouts: 10.2 us -> 15.4 us
    ppermute x6, waiting for transfers between devices: 41.7 us -> 16.9 us  [outward(): return lax.ppermute(array, 'tensor', [(1, 0), (2, 3)])]
    ppermute x10 -> x13, waiting for transfers between devices: 9.23 us -> 0.36 us  [between(): return lax.ppermute(array, 'cand', [(i, i ^ offset) for i in range(n_cand)])]
    pallas_call x1 -> x3, Pallas kernels: 2.61 us -> 7.96 us  [mix_sent(): pl.pallas_call(mix_sent_kernel, grid_spec=pltpu.PrefetchScalarGridSpec(nu...]
    unnamed x26 -> x50, local copies, waits for them, and re-layouts: 7.5 us -> 12.7 us
    ppermute x7 -> x8, waiting for transfers between devices: 17.2 us -> 13.4 us  [inward(): return lax.ppermute(array, 'tensor', [(0, 1), (3, 2)])]
    ppermute x7 -> x8, starting transfers between devices: 28.1 us -> 31.3 us  [inward(): return lax.ppermute(array, 'tensor', [(0, 1), (3, 2)])]
    ppermute x10 -> x13, starting transfers between devices: 8.11 us -> 10.7 us  [between(): return lax.ppermute(array, 'cand', [(i, i ^ offset) for i in range(n_cand)])]
    pallas_call x2, Pallas kernels: 2.36 us -> 4.71 us  [keys_values(): pl.pallas_call(functools.partial(keys_values_kernel, len(hidden), len(bef...]
  transfers between devices with their start and end apart: 33 -> 37, of which waited for: 16 -> 10; matrix products, arithmetic and copies ran while one was open for 0% -> 0% of each run, Pallas kernels for 25% -> 32%
where the time goes in v8:
time: 197 us; the launch traced here: 196 us
  Pallas kernels  67 us (34%)
  starting transfers between devices  64.5 us (33%)
  waiting for transfers between devices  47.2 us (24%)
  local copies, waits for them, and re-layouts  15.4 us (8%)
    ppermute x8, starting transfers between devices, inward(): return lax.ppermute(array, 'tensor', [(0, 1), (3, 2)])  31.3 us
    ppermute x6, waiting for transfers between devices, outward(): return lax.ppermute(array, 'tensor', [(1, 0), (2, 3)])  16.9 us
    pallas_call x8, Pallas kernels, mix(): pl.pallas_call(mix_kernel, grid=(tiles,), in_specs=[whole(rows, depth), p...  16.5 us
    ppermute x2, waiting for transfers between devices, swap(): return lax.ppermute(array, 'tensor', [(0, 1), (1, 0), (2, 3), (3, 2)])  16.5 us
    ppermute x8, waiting for transfers between devices, inward(): return lax.ppermute(array, 'tensor', [(0, 1), (3, 2)])  13.4 us
    pallas_call x3, Pallas kernels, partial_projection(): pl.pallas_call(functools.partial(partial_kernel, [len(part) for part in p...  12.7 us
    pallas_call x3, Pallas kernels, attention(): pl.pallas_call(functools.partial(attention_kernel, slots, n_parts, len(ot...  12.7 us
    unnamed x50, local copies, waits for them, and re-layouts  12.7 us
  transfers between devices with their start and end apart: 37, of which 10 were waited for; matrix products, arithmetic and copies ran while one was open for 0% of the time, Pallas kernels for 32%

profile of v8, /device:TPU:0, one launch (start us, length us, event | category | flops | bytes accessed | tf_op | source)
XLA Modules:
  0.0 195.6 jit_solution(955560207610333727)
XLA Ops:
  0.0 2.6 %fusion = (bf16[256,1280]{1,0:T(8,128)(2,1)}, bf16[256,1280]{1,0:T(8,128)(2,1)}) fusion(bf16[512,1280]{1,0:T(8,128)(2,1)} %refs_0_.1), kind=kLoop, calls=%fused_computation | loop fusion | bytes 2621440 | tf_op jit(solution)/shard_map/slice | solution.py:437
  2.6 1.5 collective-permute-start.1
  4.1 5.1 %collective-permute-start = (bf16[256,1280]{1,0:T(8,128)(2,1)}, bf16[256,1280]{1,0:T(8,128)(2,1)}, u32[]{:S(2)}, u32[]{:S(2)}) collective-permute-start(bf16[256,1280]{1,0:T(8,128)(2,1)} %get-tuple-element.100), channel_id=1, source_target_pairs={{0,1},{1,0},{2,3},{3,2},{4,5},{5,4},{6,7},{7,6},{8,9},{9,8},{10,11... | collective-permute-start | bytes 1966088 | tf_op jit(solution)/shard_map/ppermute | solution.py:411
  9.2 1.5 collective-permute-start.6
  10.7 1.6 collective-permute-start.4
  12.4 4.0 %copy-done = bf16[5120,1024]{1,0:T(8,128)(2,1)S(1)} copy-done((bf16[5120,1024]{1,0:T(8,128)(2,1)S(1)}, bf16[5120,1024]{1,0:T(8,128)(2,1)}, u32[]{:S(2)}) %copy-start) | copy-done | bytes 10485784
  16.3 1.3 copy-done.4
  17.7 3.4 %partial_projection.3 = (f32[512,1024]{1,0:T(8,128)S(1)}, f32[512,128]{1,0:T(8,128)S(1)}, f32[512,128]{1,0:T(8,128)S(1)}) custom-call(s32[12]{0:T(128)S(1)} %stack.51.places_ref, bf16[512,1280]{1,0:T(8,128)(2,1)S(1)} %copy-done.4, bf16[5120,1024]{1,0:T(8,128)(2,1)S(1)} %copy-done, bf16[5120,128]{1,0:T(8,128)(2,1)S(1)} %copy-done.2, ...), custom_call_target="tpu_custom_call" | custom-call | flops 1 | bytes 1 | tf_op jit(solution)/shard_map/partial_projection/pallas_call | solution.py:96
  21.1 4.0 %collective-permute-done.refs_0_ = bf16[256,1280]{1,0:T(8,128)(2,1)} collective-permute-done((bf16[256,1280]{1,0:T(8,128)(2,1)}, bf16[256,1280]{1,0:T(8,128)(2,1)}, u32[]{:S(2)}, u32[]{:S(2)}) %collective-permute-start) | collective-permute-done | bytes 655392 | tf_op jit(solution)/shard_map/ppermute | solution.py:411
  25.1 1.4 collective-permute-start.5
  26.5 12.5 %collective-permute-done.4.refs_1_ = bf16[256,1280]{1,0:T(8,128)(2,1)S(1)} collective-permute-done((bf16[256,1280]{1,0:T(8,128)(2,1)}, bf16[256,1280]{1,0:T(8,128)(2,1)S(1)}, u32[]{:S(2)}, u32[]{:S(2)}) %collective-permute-start.4) | collective-permute-done | bytes 655392 | tf_op jit(solution)/shard_map/ppermute | solution.py:411
  39.0 1.5 collective-permute-start.2
  40.6 1.3 collective-permute-start.8
  41.9 4.0 %copy-done.1 = bf16[5120,1024]{1,0:T(8,128)(2,1)S(1)} copy-done((bf16[5120,1024]{1,0:T(8,128)(2,1)S(1)}, bf16[5120,1024]{1,0:T(8,128)(2,1)}, u32[]{:S(2)}) %copy-start.1) | copy-done | bytes 10485784
  45.8 4.5 %partial_projection.4 = (f32[512,1024]{1,0:T(8,128)S(1)}, f32[512,128]{1,0:T(8,128)S(1)}, f32[512,128]{1,0:T(8,128)S(1)}) custom-call(s32[12]{0:T(128)S(1)} %stack.51.places_ref, bf16[256,1280]{1,0:T(8,128)(2,1)} %collective-permute-done.refs_0_, bf16[256,1280]{1,0:T(8,128)(2,1)S(1)} %collective-permute-done.4.refs_1_, bf16[5120,1024]{1,0:T(8,128)(2,1)S(1)} %copy-done.1, ...), custom_call_target="tpu_custom_call" | custom-call | flops 1 | bytes 1 | tf_op jit(solution)/shard_map/partial_projection/pallas_call | solution.py:96
  51.1 2.0 %collective-permute-done.5.refs_1_ = bf16[256,1280]{1,0:T(8,128)(2,1)S(1)} collective-permute-done((bf16[256,1280]{1,0:T(8,128)(2,1)}, bf16[256,1280]{1,0:T(8,128)(2,1)S(1)}, u32[]{:S(2)}, u32[]{:S(2)}) %collective-permute-start.5) | collective-permute-done | bytes 655392 | tf_op jit(solution)/shard_map/ppermute | solution.py:417
  54.4 5.1 %collective-permute-start.10 = (bf16[128,2560]{1,0:T(8,128)(2,1)S(1)}, bf16[128,2560]{1,0:T(8,128)(2,1)S(1)}, u32[]{:S(2)}, u32[]{:S(2)}) collective-permute-start(bf16[128,2560]{1,0:T(8,128)(2,1)S(1)} %eighth.2), channel_id=1, source_target_pairs={{0,1},{3,2},{4,5},{7,6},{8,9},{11,10},{12,13},{15,14},{16,17},{19,... | collective-permute-start | bytes 1966088 | tf_op jit(solution)/shard_map/ppermute | solution.py:420
  59.5 1.3 collective-permute-start.3
  60.9 1.4 eighth.3
  62.3 4.8 %collective-permute-done.8.refs_3_ = bf16[256,1280]{1,0:T(8,128)(2,1)S(1)} collective-permute-done((bf16[256,1280]{1,0:T(8,128)(2,1)}, bf16[256,1280]{1,0:T(8,128)(2,1)S(1)}, u32[]{:S(2)}, u32[]{:S(2)}) %collective-permute-start.8) | collective-permute-done | bytes 655392 | tf_op jit(solution)/shard_map/ppermute | solution.py:417
  67.1 0.8 copy-done.12
  68.0 5.1 %collective-permute-start.13 = (bf16[128,2560]{1,0:T(8,128)(2,1)}, bf16[128,2560]{1,0:T(8,128)(2,1)S(1)}, u32[]{:S(2)}, u32[]{:S(2)}) collective-permute-start(bf16[128,2560]{1,0:T(8,128)(2,1)} %eighth.3), channel_id=1, source_target_pairs={{0,1},{3,2},{4,5},{7,6},{8,9},{11,10},{12,13},{15,14},{16,17},{19,... | collective-permute-start | bytes 1966088 | tf_op jit(solution)/shard_map/ppermute | solution.py:420
  73.1 1.6 collective-permute-start.12
  74.7 1.5 collective-permute-start.11
  76.2 1.3 collective-permute-start.9
  77.5 1.1 copy-done.13
  78.6 4.8 %partial_projection.5 = (f32[512,1024]{1,0:T(8,128)S(1)}, f32[512,128]{1,0:T(8,128)S(1)}, f32[512,128]{1,0:T(8,128)S(1)}) custom-call(s32[12]{0:T(128)S(1)} %stack.51.places_ref, bf16[256,1280]{1,0:T(8,128)(2,1)} %collective-permute-done.1.refs_0_, bf16[256,1280]{1,0:T(8,128)(2,1)S(1)} %collective-permute-done.5.refs_1_, ...), custom_call_target="tpu_custom_call" | custom-call | flops 1 | bytes 1 | tf_op jit(solution)/shard_map/partial_projection/pallas_call | solution.py:96
  84.2 3.6 %queries.2.refs_0_ = bf16[256,1024]{1,0:T(8,128)(2,1)S(1)} custom-call(s32[12]{0:T(128)S(1)} %stack.51.places_ref, bf16[256,1280]{1,0:T(8,128)(2,1)} %collective-permute-done.2.refs_0_, bf16[256,1280]{1,0:T(8,128)(2,1)} %collective-permute-done.3.refs_1_, bf16[5120,1024]{1,0:T(8,128)(2,1)S(1)} %bitcast.17, f32[512,1024]{1,0:T(8,128)S(1)} %get-tuple-element.66.refs_3_, ...), custom_call_target="tpu_custom_call" | custom-call | flops 1 | bytes 1 | tf_op jit(solution)/shard_map/queries/pallas_call | solution.py:183
  87.8 2.3 %keys_values.2.refs_0_.refs_2_ = bf16[256,256]{1,0:T(8,128)(2,1)S(1)} custom-call(s32[12]{0:T(128)S(1)} %stack.51.places_ref, bf16[256,1280]{1,0:T(8,128)(2,1)} %collective-permute-done.2.refs_0_, bf16[256,1280]{1,0:T(8,128)(2,1)} %collective-permute-done.3.refs_1_, bf16[5120,128]{1,0:T(8,128)(2,1)S(1)} %copy-done.2, bf16[5120,128]{1,0:T(8,128)(2,1)S(1)} %copy-done.3, ...), custom_call_target="tpu_custom_call" | custom-call | flops 1 | bytes 1 | tf_op jit(solution)/shard_map/keys_values/pallas_call | solution.py:152
  90.2 4.0 %collective-permute-done.9.refs_1_.refs_2_ = bf16[256,1280]{1,0:T(8,128)(2,1)} collective-permute-done((bf16[256,1280]{1,0:T(8,128)(2,1)S(1)}, bf16[256,1280]{1,0:T(8,128)(2,1)}, u32[]{:S(2)}, u32[]{:S(2)}) %collective-permute-start.9) | collective-permute-done | bytes 655392 | tf_op jit(solution)/shard_map/ppermute | solution.py:417
  94.2 2.4 %keys_values.3 = (bf16[256,256]{1,0:T(8,128)(2,1)S(1)}, bf16[128,256]{1,0:T(8,128)(2,1)S(1)}) custom-call(s32[12]{0:T(128)S(1)} %stack.51.places_ref, bf16[256,256]{1,0:T(8,128)(2,1)S(1)} %keys_values.2.refs_0_.refs_2_, bf16[256,1280]{1,0:T(8,128)(2,1)S(1)} %collective-permute-done.7.refs_0_.refs_1_, ...), custom_call_target="tpu_custom_call" | custom-call | flops 1 | bytes 1 | tf_op jit(solution)/shard_map/keys_values/pallas_call | solution.py:152
  96.6 1.1 collective-permute-start.20
  97.6 1.5 collective-permute-start.19
  99.2 1.4 collective-permute-start.18
  101.8 1.0 collective-permute-start.15
  103.4 3.4 %queries.3.refs_1_ = bf16[256,1024]{1,0:T(8,128)(2,1)S(1)} custom-call(s32[12]{0:T(128)S(1)} %stack.51.places_ref, bf16[256,1280]{1,0:T(8,128)(2,1)S(1)} %collective-permute-done.7.refs_0_.refs_1_, bf16[256,1280]{1,0:T(8,128)(2,1)} %collective-permute-done.9.refs_1_.refs_2_, bf16[5120,1024]{1,0:T(8,128)(2,1)S(1)} %bitcast.17, ...), custom_call_target="tpu_custom_call" | custom-call | flops 1 | bytes 1 | tf_op jit(solution)/shard_map/queries/pallas_call | solution.py:183
  108.7 3.6 %attention.3.rows_ref = bf16[128,1024]{1,0:T(8,128)(2,1)S(1)} custom-call(s32[12]{0:T(128)S(1)} %stack.51.places_ref, s32[1]{0:T(128)S(6)} %copy.14.length_ref, bf16[256,1024]{1,0:T(8,128)(2,1)S(1)} %queries.2.refs_0_, bf16[256,1024]{1,0:T(8,128)(2,1)S(1)} %queries.3.refs_1_, bf16[256,256]{1,0:T(8,128)(2,1)S(1)} %keys_values.2.refs_0_.refs_2_, ...), custom_call_target="tpu_custom_call" | custom-call | flops 1 | bytes 1 | tf_op jit(solution)/shard_map/attention/pallas_call | solution.py:272
  112.3 1.5 collective-permute-start.21
  113.8 2.1 %mix.8.refs_0_ = bf16[128,2560]{1,0:T(8,128)(2,1)S(1)} custom-call(bf16[128,1024]{1,0:T(8,128)(2,1)S(1)} %attention.3.rows_ref, bf16[1024,5120]{1,0:T(8,128)(2,1)S(1)} %bitcast.15), custom_call_target="tpu_custom_call" | custom-call | flops 1 | bytes 1 | tf_op jit(solution)/shard_map/mix/pallas_call | solution.py:301
  115.9 2.1 %mix.9.refs_0_ = bf16[128,2560]{1,0:T(8,128)(2,1)S(1)} custom-call(bf16[128,1024]{1,0:T(8,128)(2,1)S(1)} %attention.3.rows_ref, bf16[1024,5120]{1,0:T(8,128)(2,1)S(1)} %bitcast.15), custom_call_target="tpu_custom_call" | custom-call | flops 1 | bytes 1 | tf_op jit(solution)/shard_map/mix/pallas_call | solution.py:301
  117.9 3.6 %attention.4.rows_ref = bf16[128,1024]{1,0:T(8,128)(2,1)S(1)} custom-call(s32[12]{0:T(128)S(1)} %stack.51.places_ref, s32[1]{0:T(128)S(6)} %copy.14.length_ref, bf16[256,1024]{1,0:T(8,128)(2,1)S(1)} %queries.2.refs_0_, bf16[256,1024]{1,0:T(8,128)(2,1)S(1)} %queries.3.refs_1_, bf16[256,256]{1,0:T(8,128)(2,1)S(1)} %keys_values.2.refs_0_.refs_2_, ...), custom_call_target="tpu_custom_call" | custom-call | flops 1 | bytes 1 | tf_op jit(solution)/shard_map/attention/pallas_call | solution.py:272
  121.5 2.6 %collective-permute-start.27 = (bf16[128,2560]{1,0:T(8,128)(2,1)S(1)}, bf16[128,2560]{1,0:T(8,128)(2,1)S(1)}, u32[]{:S(2)}, u32[]{:S(2)}) collective-permute-start(bf16[128,2560]{1,0:T(8,128)(2,1)S(1)} %mix.8.refs_0_), channel_id=1, source_target_pairs={{0,1},{3,2},{4,5},{7,6},{8,9},{11,10},{12,13},{15,14},{16,17},{19,... | collective-permute-start | bytes 1966088 | tf_op jit(solution)/shard_map/ppermute | solution.py:420
  124.2 2.7 %mix_sent.3.refs_1_ = bf16[128,2560]{1,0:T(8,128)(2,1)S(1)} custom-call(s32[12]{0:T(128)S(1)} %stack.51.places_ref, bf16[128,1024]{1,0:T(8,128)(2,1)S(1)} %collective-permute-done.21.rows_ref, bf16[128,2560]{1,0:T(8,128)(2,1)S(1)} %collective-permute-done.10.refs_0_, bf16[128,2560]{1,0:T(8,128)(2,1)S(1)} %collective-permute-done.13.refs_1_, ...), custom_call_target="tpu_custom_call" | custom-call | flops 1 | bytes 1 | tf_op jit(solution)/shard_map/mix_sent/pallas_call | solution.py:357
  127.7 3.6 %collective-permute-start.26 = (bf16[128,1024]{1,0:T(8,128)(2,1)S(1)}, bf16[128,1024]{1,0:T(8,128)(2,1)S(1)}, u32[]{:S(2)}, u32[]{:S(2)}) collective-permute-start(bf16[128,1024]{1,0:T(8,128)(2,1)S(1)} %attention.4.rows_ref), channel_id=1, source_target_pairs={{0,1},{3,2},{4,5},{7,6},{8,9},{11,10},{12,13},{15,14},{16,17},{19,... | collective-permute-start | bytes 786440 | tf_op jit(solution)/shard_map/ppermute | solution.py:420
  131.3 2.1 %mix.10.refs_0_ = bf16[128,2560]{1,0:T(8,128)(2,1)S(1)} custom-call(bf16[128,1024]{1,0:T(8,128)(2,1)S(1)} %attention.4.rows_ref, bf16[1024,5120]{1,0:T(8,128)(2,1)S(1)} %bitcast.15), custom_call_target="tpu_custom_call" | custom-call | flops 1 | bytes 1 | tf_op jit(solution)/shard_map/mix/pallas_call | solution.py:301
  133.4 2.1 %mix.11.refs_0_ = bf16[128,2560]{1,0:T(8,128)(2,1)S(1)} custom-call(bf16[128,1024]{1,0:T(8,128)(2,1)S(1)} %attention.4.rows_ref, bf16[1024,5120]{1,0:T(8,128)(2,1)S(1)} %bitcast.15), custom_call_target="tpu_custom_call" | custom-call | flops 1 | bytes 1 | tf_op jit(solution)/shard_map/mix/pallas_call | solution.py:301
  135.4 5.6 %attention.5 = (bf16[128,1024]{1,0:T(8,128)(2,1)S(1)}, bf16[128,1024]{1,0:T(8,128)(2,1)S(1)}) custom-call(s32[12]{0:T(128)S(1)} %stack.51.places_ref, s32[1]{0:T(128)S(6)} %copy.14.length_ref, bf16[256,1024]{1,0:T(8,128)(2,1)S(1)} %queries.2.refs_0_, bf16[256,1024]{1,0:T(8,128)(2,1)S(1)} %queries.3.refs_1_, bf16[256,256]{1,0:T(8,128)(2,1)S(1)} %keys_values.2.refs_0_.refs_2_, ...), custom_call_target="tpu_custom_call" | custom-call | flops 1 | bytes 1 | tf_op jit(solution)/shard_map/attention/pallas_call | solution.py:272
  141.9 1.5 collective-permute-done.26.rows_ref
  143.5 2.7 %mix_sent.4.refs_1_ = bf16[128,2560]{1,0:T(8,128)(2,1)S(1)} custom-call(s32[12]{0:T(128)S(1)} %stack.51.places_ref, bf16[128,1024]{1,0:T(8,128)(2,1)S(1)} %collective-permute-done.26.rows_ref, bf16[128,2560]{1,0:T(8,128)(2,1)S(1)} %collective-permute-done.10.refs_0_, bf16[128,2560]{1,0:T(8,128)(2,1)S(1)} %collective-permute-done.13.refs_1_, ...), custom_call_target="tpu_custom_call" | custom-call | flops 1 | bytes 1 | tf_op jit(solution)/shard_map/mix_sent/pallas_call | solution.py:357
  146.3 4.4 %collective-permute-start.34 = (bf16[128,2560]{1,0:T(8,128)(2,1)S(1)}, bf16[128,2560]{1,0:T(8,128)(2,1)S(1)}, u32[]{:S(2)}, u32[]{:S(2)}) collective-permute-start(bf16[128,2560]{1,0:T(8,128)(2,1)S(1)} %mix.10.refs_0_), channel_id=1, source_target_pairs={{0,1},{3,2},{4,5},{7,6},{8,9},{11,10},{12,13},{15,14},{16,17},{19,... | collective-permute-start | bytes 1966088 | tf_op jit(solution)/shard_map/ppermute | solution.py:420
  150.7 2.1 %mix.13.refs_0_ = bf16[128,2560]{1,0:T(8,128)(2,1)S(1)} custom-call(bf16[128,1024]{1,0:T(8,128)(2,1)S(1)} %get-tuple-element.89.rows_ref, bf16[1024,5120]{1,0:T(8,128)(2,1)S(1)} %bitcast.15), custom_call_target="tpu_custom_call" | custom-call | flops 1 | bytes 1 | tf_op jit(solution)/shard_map/mix/pallas_call | solution.py:301
  152.8 2.1 %mix.12.refs_0_ = bf16[128,2560]{1,0:T(8,128)(2,1)S(1)} custom-call(bf16[128,1024]{1,0:T(8,128)(2,1)S(1)} %get-tuple-element.89.rows_ref, bf16[1024,5120]{1,0:T(8,128)(2,1)S(1)} %bitcast.15), custom_call_target="tpu_custom_call" | custom-call | flops 1 | bytes 1 | tf_op jit(solution)/shard_map/mix/pallas_call | solution.py:301
  155.7 1.3 collective-permute-start.32
  157.0 4.6 %collective-permute-start.30 = (bf16[128,1024]{1,0:T(8,128)(2,1)S(1)}, bf16[128,1024]{1,0:T(8,128)(2,1)S(1)}, u32[]{:S(2)}, u32[]{:S(2)}) collective-permute-start(bf16[128,1024]{1,0:T(8,128)(2,1)S(1)} %get-tuple-element.89.rows_ref), channel_id=1, source_target_pairs={{0,1},{3,2},{4,5},{7,6},{8,9},{11,10},{12,13},{15,14},{16,17},{19,... | collective-permute-start | bytes 786440 | tf_op jit(solution)/shard_map/ppermute | solution.py:420
  161.7 2.1 %mix.15.refs_0_ = bf16[128,2560]{1,0:T(8,128)(2,1)S(1)} custom-call(bf16[128,1024]{1,0:T(8,128)(2,1)S(1)} %get-tuple-element.91.rows_ref, bf16[1024,5120]{1,0:T(8,128)(2,1)S(1)} %bitcast.15), custom_call_target="tpu_custom_call" | custom-call | flops 1 | bytes 1 | tf_op jit(solution)/shard_map/mix/pallas_call | solution.py:301
  163.7 2.1 %mix.14.refs_0_ = bf16[128,2560]{1,0:T(8,128)(2,1)S(1)} custom-call(bf16[128,1024]{1,0:T(8,128)(2,1)S(1)} %get-tuple-element.91.rows_ref, bf16[1024,5120]{1,0:T(8,128)(2,1)S(1)} %bitcast.15), custom_call_target="tpu_custom_call" | custom-call | flops 1 | bytes 1 | tf_op jit(solution)/shard_map/mix/pallas_call | solution.py:301
  165.8 3.3 %collective-permute-done.30.rows_ref = bf16[128,1024]{1,0:T(8,128)(2,1)S(1)} collective-permute-done((bf16[128,1024]{1,0:T(8,128)(2,1)S(1)}, bf16[128,1024]{1,0:T(8,128)(2,1)S(1)}, u32[]{:S(2)}, u32[]{:S(2)}) %collective-permute-start.30) | collective-permute-done | bytes 262176 | tf_op jit(solution)/shard_map/ppermute | solution.py:420
  169.1 2.7 %mix_sent.5.refs_1_ = bf16[128,2560]{1,0:T(8,128)(2,1)S(1)} custom-call(s32[12]{0:T(128)S(1)} %stack.51.places_ref, bf16[128,1024]{1,0:T(8,128)(2,1)S(1)} %collective-permute-done.30.rows_ref, bf16[128,2560]{1,0:T(8,128)(2,1)S(1)} %collective-permute-done.10.refs_0_, bf16[128,2560]{1,0:T(8,128)(2,1)S(1)} %collective-permute-done.13.refs_1_, ...), custom_call_target="tpu_custom_call" | custom-call | flops 1 | bytes 1 | tf_op jit(solution)/shard_map/mix_sent/pallas_call | solution.py:357
  172.0 4.4 %collective-permute-start.31 = (bf16[128,2560]{1,0:T(8,128)(2,1)S(1)}, bf16[128,2560]{1,0:T(8,128)(2,1)S(1)}, u32[]{:S(2)}, u32[]{:S(2)}) collective-permute-start(bf16[128,2560]{1,0:T(8,128)(2,1)S(1)} %mix.13.refs_0_), channel_id=1, source_target_pairs={{0,1},{3,2},{4,5},{7,6},{8,9},{11,10},{12,13},{15,14},{16,17},{19,... | collective-permute-start | bytes 1966088 | tf_op jit(solution)/shard_map/ppermute | solution.py:420
  177.1 1.2 added.13.refs_4_
  178.4 1.3 collective-permute-start.35
  179.7 8.5 %collective-permute-done.31.refs_1_ = bf16[128,2560]{1,0:T(8,128)(2,1)S(1)} collective-permute-done((bf16[128,2560]{1,0:T(8,128)(2,1)S(1)}, bf16[128,2560]{1,0:T(8,128)(2,1)S(1)}, u32[]{:S(2)}, u32[]{:S(2)}) %collective-permute-start.31) | collective-permute-done | bytes 655392 | tf_op jit(solution)/shard_map/ppermute | solution.py:420
  188.3 6.2 %collective-permute-done.35.refs_2_ = bf16[128,2560]{1,0:T(8,128)(2,1)S(1)} collective-permute-done((bf16[128,2560]{1,0:T(8,128)(2,1)S(1)}, bf16[128,2560]{1,0:T(8,128)(2,1)S(1)}, u32[]{:S(2)}, u32[]{:S(2)}) %collective-permute-start.35) | collective-permute-done | bytes 655392 | tf_op jit(solution)/shard_map/ppermute | solution.py:417
  194.5 1.2 added.15
  (95 shorter events, 9.7 us)
Async XLA Ops:
  0.0 12.3 %copy-start.3 = (bf16[5120,128]{1,0:T(8,128)(2,1)S(1)}, bf16[5120,128]{1,0:T(8,128)(2,1)}, u32[]{:S(2)}) copy-start(bf16[5120,128]{1,0:T(8,128)(2,1)} %refs_4_.5) | copy-start | bytes 3932164
  0.0 12.3 %copy-start.2 = (bf16[5120,128]{1,0:T(8,128)(2,1)S(1)}, bf16[5120,128]{1,0:T(8,128)(2,1)}, u32[]{:S(2)}) copy-start(bf16[5120,128]{1,0:T(8,128)(2,1)} %refs_3_.7) | copy-start | bytes 3932164
  2.6 18.5 %collective-permute-start.1 = (bf16[256,1280]{1,0:T(8,128)(2,1)}, bf16[256,1280]{1,0:T(8,128)(2,1)}, u32[]{:S(2)}, u32[]{:S(2)}) collective-permute-start(bf16[256,1280]{1,0:T(8,128)(2,1)} %get-tuple-element.100), channel_id=1, source_target_pairs={{1,2},{2,1},{5,6},{6,5},{9,10},{10,9},{13,14},{14,13},{17,18},{18,... | collective-permute-start | bytes 1966088 | tf_op jit(solution)/shard_map/ppermute | solution.py:414
  4.1 21.0 %collective-permute-start = (bf16[256,1280]{1,0:T(8,128)(2,1)}, bf16[256,1280]{1,0:T(8,128)(2,1)}, u32[]{:S(2)}, u32[]{:S(2)}) collective-permute-start(bf16[256,1280]{1,0:T(8,128)(2,1)} %get-tuple-element.100), channel_id=1, source_target_pairs={{0,1},{1,0},{2,3},{3,2},{4,5},{5,4},{6,7},{7,6},{8,9},{9,8},{10,11... | collective-permute-start | bytes 1966088 | tf_op jit(solution)/shard_map/ppermute | solution.py:411
  9.2 17.3 %collective-permute-start.6 = (bf16[256,1280]{1,0:T(8,128)(2,1)}, bf16[256,1280]{1,0:T(8,128)(2,1)}, u32[]{:S(2)}, u32[]{:S(2)}) collective-permute-start(bf16[256,1280]{1,0:T(8,128)(2,1)} %get-tuple-element.99), channel_id=1, source_target_pairs={{1,2},{2,1},{5,6},{6,5},{9,10},{10,9},{13,14},{14,13},{17,18},{18,... | collective-permute-start | bytes 1966088 | tf_op jit(solution)/shard_map/ppermute | solution.py:414
  10.7 28.4 %collective-permute-start.4 = (bf16[256,1280]{1,0:T(8,128)(2,1)}, bf16[256,1280]{1,0:T(8,128)(2,1)S(1)}, u32[]{:S(2)}, u32[]{:S(2)}) collective-permute-start(bf16[256,1280]{1,0:T(8,128)(2,1)} %get-tuple-element.99), channel_id=1, source_target_pairs={{0,1},{1,0},{2,3},{3,2},{4,5},{5,4},{6,7},{7,6},{8,9},{9,8},{10,11... | collective-permute-start | bytes 1966088 | tf_op jit(solution)/shard_map/ppermute | solution.py:411
  12.4 4.0 %copy-start = (bf16[5120,1024]{1,0:T(8,128)(2,1)S(1)}, bf16[5120,1024]{1,0:T(8,128)(2,1)}, u32[]{:S(2)}) copy-start(bf16[5120,1024]{1,0:T(8,128)(2,1)} %refs_2_.8) | copy-start | bytes 31457284
  16.3 1.3 copy-start.4
  17.7 36.1 %slice-start = ((s8[10485760]{0:T(1024)(128)(4,1)}), s8[4194304]{0:T(1024)(128)(4,1)S(1)}, s32[]{:S(2)}) async-start(s8[10485760]{0:T(1024)(128)(4,1)} %bitcast.14), calls=%async_computation | async-start | bytes 8388608
  17.7 36.1 %slice-start.1 = ((s8[10485760]{0:T(1024)(128)(4,1)}), s8[4194304]{0:T(1024)(128)(4,1)S(1)}, s32[]{:S(2)}) async-start(s8[10485760]{0:T(1024)(128)(4,1)} %bitcast.14), calls=%async_computation.1 | async-start | bytes 8388608
  25.1 28.7 %slice-start.2 = ((s8[10485760]{0:T(1024)(128)(4,1)}), s8[2097152]{0:T(1024)(128)(4,1)S(1)}, s32[]{:S(2)}) async-start(s8[10485760]{0:T(1024)(128)(4,1)} %bitcast.14), calls=%async_computation.2 | async-start | bytes 4194304
  25.1 28.0 %collective-permute-start.5 = (bf16[256,1280]{1,0:T(8,128)(2,1)}, bf16[256,1280]{1,0:T(8,128)(2,1)S(1)}, u32[]{:S(2)}, u32[]{:S(2)}) collective-permute-start(bf16[256,1280]{1,0:T(8,128)(2,1)} %collective-permute-done.1.refs_0_), channel_id=1, source_target_pairs={{1,0},{2,3},{5,4},{6,7},{9,8},{10,11},{13,12},{14,15},{17,16},{18,... | collective-permute-start | bytes 1966088 | tf_op jit(solution)/shard_map/ppermute | solution.py:417
  39.0 11.3 %copy-start.11 = (bf16[256,1280]{1,0:T(8,128)(2,1)}, bf16[256,1280]{1,0:T(8,128)(2,1)S(1)}, u32[]{:S(2)}) copy-start(bf16[256,1280]{1,0:T(8,128)(2,1)S(1)} %collective-permute-done.4.refs_1_) | copy-start | bytes 1966084
  39.0 20.5 %collective-permute-start.2 = (bf16[256,1280]{1,0:T(8,128)(2,1)}, bf16[256,1280]{1,0:T(8,128)(2,1)}, u32[]{:S(2)}, u32[]{:S(2)}) collective-permute-start(bf16[256,1280]{1,0:T(8,128)(2,1)} %collective-permute-done.refs_0_), channel_id=1, source_target_pairs={{1,2},{2,1},{5,6},{6,5},{9,10},{10,9},{13,14},{14,13},{17,18},{18,... | collective-permute-start | bytes 1966088 | tf_op jit(solution)/shard_map/ppermute | solution.py:414
  40.6 26.6 %collective-permute-start.8 = (bf16[256,1280]{1,0:T(8,128)(2,1)}, bf16[256,1280]{1,0:T(8,128)(2,1)S(1)}, u32[]{:S(2)}, u32[]{:S(2)}) collective-permute-start(bf16[256,1280]{1,0:T(8,128)(2,1)} %collective-permute-done.6.refs_2_), channel_id=1, source_target_pairs={{1,0},{2,3},{5,4},{6,7},{9,8},{10,11},{13,12},{14,15},{17,16},{18,... | collective-permute-start | bytes 1966088 | tf_op jit(solution)/shard_map/ppermute | solution.py:417
  41.9 4.0 %copy-start.1 = (bf16[5120,1024]{1,0:T(8,128)(2,1)S(1)}, bf16[5120,1024]{1,0:T(8,128)(2,1)}, u32[]{:S(2)}) copy-start(bf16[5120,1024]{1,0:T(8,128)(2,1)} %refs_2_.8) | copy-start | bytes 31457284
  50.4 0.7 copy-start.14
  51.1 3.3 %copy-start.7 = (f32[512,1024]{1,0:T(8,128)}, f32[512,1024]{1,0:T(8,128)S(1)}, u32[]{:S(2)}) copy-start(f32[512,1024]{1,0:T(8,128)S(1)} %get-tuple-element.61.refs_7_) | copy-start | bytes 6291460
  53.1 14.9 %collective-permute-start.7 = (bf16[256,1280]{1,0:T(8,128)(2,1)}, bf16[256,1280]{1,0:T(8,128)(2,1)S(1)}, u32[]{:S(2)}, u32[]{:S(2)}) collective-permute-start(bf16[256,1280]{1,0:T(8,128)(2,1)} %copy-done.11), channel_id=1, source_target_pairs={{1,2},{2,1},{5,6},{6,5},{9,10},{10,9},{13,14},{14,13},{17,18},{18,... | collective-permute-start | bytes 1966088 | tf_op jit(solution)/shard_map/ppermute | solution.py:414
  54.4 23.1 %copy-start.15 = (f32[512,128]{1,0:T(8,128)S(1)}, f32[512,128]{1,0:T(8,128)}, u32[]{:S(2)}) copy-start(f32[512,128]{1,0:T(8,128)} %copy-done.14) | copy-start | bytes 786436
  54.4 18.7 %collective-permute-start.10 = (bf16[128,2560]{1,0:T(8,128)(2,1)S(1)}, bf16[128,2560]{1,0:T(8,128)(2,1)S(1)}, u32[]{:S(2)}, u32[]{:S(2)}) collective-permute-start(bf16[128,2560]{1,0:T(8,128)(2,1)S(1)} %eighth.2), channel_id=1, source_target_pairs={{0,1},{3,2},{4,5},{7,6},{8,9},{11,10},{12,13},{15,14},{16,17},{19,... | collective-permute-start | bytes 1966088 | tf_op jit(solution)/shard_map/ppermute | solution.py:420
  59.5 24.5 %collective-permute-start.3 = (bf16[256,1280]{1,0:T(8,128)(2,1)}, bf16[256,1280]{1,0:T(8,128)(2,1)}, u32[]{:S(2)}, u32[]{:S(2)}) collective-permute-start(bf16[256,1280]{1,0:T(8,128)(2,1)} %collective-permute-done.2.refs_0_), channel_id=1, source_target_pairs={{1,0},{2,3},{5,4},{6,7},{9,8},{10,11},{13,12},{14,15},{17,16},{18,... | collective-permute-start | bytes 1966088 | tf_op jit(solution)/shard_map/ppermute | solution.py:417
  60.8 16.7 %copy-start.8 = (f32[512,1024]{1,0:T(8,128)S(1)}, f32[512,1024]{1,0:T(8,128)}, u32[]{:S(2)}) copy-start(f32[512,1024]{1,0:T(8,128)} %copy-done.7) | copy-start | bytes 6291460
  60.8 23.2 %slice-start.3 = ((s8[10485760]{0:T(1024)(128)(4,1)}), s8[4194304]{0:T(1024)(128)(4,1)S(1)}, s32[]{:S(2)}) async-start(s8[10485760]{0:T(1024)(128)(4,1)} %bitcast.16), calls=%async_computation.3 | async-start | bytes 8388608
  60.9 23.2 %slice-start.4 = ((s8[10485760]{0:T(1024)(128)(4,1)}), s8[4194304]{0:T(1024)(128)(4,1)S(1)}, s32[]{:S(2)}) async-start(s8[10485760]{0:T(1024)(128)(4,1)} %bitcast.16), calls=%async_computation.4 | async-start | bytes 8388608
  60.9 23.2 %copy-start.17 = (f32[128]{0:T(128)S(1)}, f32[128]{0:T(128)}, u32[]{:S(2)}) copy-start(f32[128]{0:T(128)} %param.18) | copy-start | bytes 1540
  62.3 21.8 %slice-start.5 = ((s8[10485760]{0:T(1024)(128)(4,1)}), s8[2097152]{0:T(1024)(128)(4,1)S(1)}, s32[]{:S(2)}) async-start(s8[10485760]{0:T(1024)(128)(4,1)} %bitcast.16), calls=%async_computation.5 | async-start | bytes 4194304
  62.3 21.8 %copy-start.5 = (f32[512,128]{1,0:T(8,128)S(1)}, f32[512,128]{1,0:T(8,128)}, u32[]{:S(2)}) copy-start(f32[512,128]{1,0:T(8,128)} %constant.30.clone.refs_6_.refs_8_.refs_9_) | copy-start | bytes 786436
  62.3 21.8 %copy-start.6 = (f32[512,128]{1,0:T(8,128)S(1)}, f32[512,128]{1,0:T(8,128)}, u32[]{:S(2)}) copy-start(f32[512,128]{1,0:T(8,128)} %constant.29.clone.refs_5_.refs_7_.refs_8_) | copy-start | bytes 786436
  67.1 0.8 copy-start.12
  68.0 22.2 %collective-permute-start.13 = (bf16[128,2560]{1,0:T(8,128)(2,1)}, bf16[128,2560]{1,0:T(8,128)(2,1)S(1)}, u32[]{:S(2)}, u32[]{:S(2)}) collective-permute-start(bf16[128,2560]{1,0:T(8,128)(2,1)} %eighth.3), channel_id=1, source_target_pairs={{0,1},{3,2},{4,5},{7,6},{8,9},{11,10},{12,13},{15,14},{16,17},{19,... | collective-permute-start | bytes 1966088 | tf_op jit(solution)/shard_map/ppermute | solution.py:420
  73.1 17.1 %collective-permute-start.12 = (bf16[128,2560]{1,0:T(8,128)(2,1)S(1)}, bf16[128,2560]{1,0:T(8,128)(2,1)S(1)}, u32[]{:S(2)}, u32[]{:S(2)}) collective-permute-start(bf16[128,2560]{1,0:T(8,128)(2,1)S(1)} %collective-permute-done.10.refs_0_), channel_id=1, source_target_pairs={{0,16},{4,20},{8,24},{12,28},{16,0},{20,4},{24,8},{28,12},{1,17},{... | collective-permute-start | bytes 1966088 | tf_op jit(solution)/shard_map/ppermute | solution.py:423
  74.7 15.5 %collective-permute-start.11 = (bf16[128,2560]{1,0:T(8,128)(2,1)S(1)}, bf16[128,2560]{1,0:T(8,128)(2,1)S(1)}, u32[]{:S(2)}, u32[]{:S(2)}) collective-permute-start(bf16[128,2560]{1,0:T(8,128)(2,1)S(1)} %collective-permute-done.10.refs_0_), channel_id=1, source_target_pairs={{0,8},{4,12},{8,0},{12,4},{16,24},{20,28},{24,16},{28,20},{1,9},{5... | collective-permute-start | bytes 1966088 | tf_op jit(solution)/shard_map/ppermute | solution.py:423
  76.2 18.0 %collective-permute-start.9 = (bf16[256,1280]{1,0:T(8,128)(2,1)S(1)}, bf16[256,1280]{1,0:T(8,128)(2,1)}, u32[]{:S(2)}, u32[]{:S(2)}) collective-permute-start(bf16[256,1280]{1,0:T(8,128)(2,1)S(1)} %collective-permute-done.7.refs_0_.refs_1_), channel_id=1, source_target_pairs={{1,0},{2,3},{5,4},{6,7},{9,8},{10,11},{13,12},{14,15},{17,16},{18,... | collective-permute-start | bytes 1966088 | tf_op jit(solution)/shard_map/ppermute | solution.py:417
  77.5 1.1 copy-start.13
  83.4 0.7 copy-start.9
  84.1 3.7 %copy-start.10 = (f32[512,128]{1,0:T(8,128)S(1)}, f32[512,128]{1,0:T(8,128)}, u32[]{:S(2)}) copy-start(f32[512,128]{1,0:T(8,128)} %copy-done.9) | copy-start | bytes 786436
  84.1 3.7 %copy-start.16 = (f32[128]{0:T(128)S(1)}, f32[128]{0:T(128)}, u32[]{:S(2)}) copy-start(f32[128]{0:T(128)} %param.19) | copy-start | bytes 1540
  87.8 6.4 %copy-start.18 = (s32[1,128]{1,0:T(1,128)S(1)}, s32[1,128]{1,0:T(1,128)}, u32[]{:S(2)}) copy-start(s32[1,128]{1,0:T(1,128)} %refs_10_.1) | copy-start | bytes 1540
  96.6 5.2 %collective-permute-start.20 = (bf16[128,256]{1,0:T(8,128)(2,1)S(1)}, bf16[128,256]{1,0:T(8,128)(2,1)S(1)}, u32[]{:S(2)}, u32[]{:S(2)}) collective-permute-start(bf16[128,256]{1,0:T(8,128)(2,1)S(1)} %get-tuple-element.75), channel_id=1, source_target_pairs={{0,28},{4,24},{8,20},{12,16},{16,12},{20,8},{24,4},{28,0},{1,29},{... | collective-permute-start | bytes 196616 | tf_op jit(solution)/shard_map/ppermute | solution.py:423
  97.6 5.5 %collective-permute-start.19 = (bf16[128,256]{1,0:T(8,128)(2,1)S(1)}, bf16[128,256]{1,0:T(8,128)(2,1)S(1)}, u32[]{:S(2)}, u32[]{:S(2)}) collective-permute-start(bf16[128,256]{1,0:T(8,128)(2,1)S(1)} %get-tuple-element.75), channel_id=1, source_target_pairs={{0,24},{4,28},{8,16},{12,20},{16,8},{20,12},{24,0},{28,4},{1,25},{... | collective-permute-start | bytes 196616 | tf_op jit(solution)/shard_map/ppermute | solution.py:423
  99.2 7.7 %collective-permute-start.18 = (bf16[128,256]{1,0:T(8,128)(2,1)S(1)}, bf16[128,256]{1,0:T(8,128)(2,1)S(1)}, u32[]{:S(2)}, u32[]{:S(2)}) collective-permute-start(bf16[128,256]{1,0:T(8,128)(2,1)S(1)} %get-tuple-element.75), channel_id=1, source_target_pairs={{0,20},{4,16},{8,28},{12,24},{16,4},{20,0},{24,12},{28,8},{1,21},{... | collective-permute-start | bytes 196616 | tf_op jit(solution)/shard_map/ppermute | solution.py:423
  100.5 6.4 %collective-permute-start.17 = (bf16[128,256]{1,0:T(8,128)(2,1)S(1)}, bf16[128,256]{1,0:T(8,128)(2,1)S(1)}, u32[]{:S(2)}, u32[]{:S(2)}) collective-permute-start(bf16[128,256]{1,0:T(8,128)(2,1)S(1)} %get-tuple-element.75), channel_id=1, source_target_pairs={{0,16},{4,20},{8,24},{12,28},{16,0},{20,4},{24,8},{28,12},{1,17},{... | collective-permute-start | bytes 196616 | tf_op jit(solution)/shard_map/ppermute | solution.py:423
  101.0 5.9 %collective-permute-start.16 = (bf16[128,256]{1,0:T(8,128)(2,1)S(1)}, bf16[128,256]{1,0:T(8,128)(2,1)S(1)}, u32[]{:S(2)}, u32[]{:S(2)}) collective-permute-start(bf16[128,256]{1,0:T(8,128)(2,1)S(1)} %get-tuple-element.75), channel_id=1, source_target_pairs={{0,12},{4,8},{8,4},{12,0},{16,28},{20,24},{24,20},{28,16},{1,13},{... | collective-permute-start | bytes 196616 | tf_op jit(solution)/shard_map/ppermute | solution.py:423
  101.8 5.1 %collective-permute-start.15 = (bf16[128,256]{1,0:T(8,128)(2,1)S(1)}, bf16[128,256]{1,0:T(8,128)(2,1)S(1)}, u32[]{:S(2)}, u32[]{:S(2)}) collective-permute-start(bf16[128,256]{1,0:T(8,128)(2,1)S(1)} %get-tuple-element.75), channel_id=1, source_target_pairs={{0,8},{4,12},{8,0},{12,4},{16,24},{20,28},{24,16},{28,20},{1,9},{5... | collective-permute-start | bytes 196616 | tf_op jit(solution)/shard_map/ppermute | solution.py:423
  103.1 3.8 %collective-permute-start.14 = (bf16[128,256]{1,0:T(8,128)(2,1)S(1)}, bf16[128,256]{1,0:T(8,128)(2,1)S(1)}, u32[]{:S(2)}, u32[]{:S(2)}) collective-permute-start(bf16[128,256]{1,0:T(8,128)(2,1)S(1)} %get-tuple-element.75), channel_id=1, source_target_pairs={{0,4},{4,0},{8,12},{12,8},{16,20},{20,16},{24,28},{28,24},{1,5},{5... | collective-permute-start | bytes 196616 | tf_op jit(solution)/shard_map/ppermute | solution.py:423
  106.9 17.2 %collective-permute-start.22 = (bf16[128,2560]{1,0:T(8,128)(2,1)S(1)}, bf16[128,2560]{1,0:T(8,128)(2,1)S(1)}, u32[]{:S(2)}, u32[]{:S(2)}) collective-permute-start(bf16[128,2560]{1,0:T(8,128)(2,1)S(1)} %collective-permute-done.10.refs_0_), channel_id=1, source_target_pairs={{0,4},{4,0},{8,12},{12,8},{16,20},{20,16},{24,28},{28,24},{1,5},{5... | collective-permute-start | bytes 1966088 | tf_op jit(solution)/shard_map/ppermute | solution.py:423
  107.2 17.0 %collective-permute-start.23 = (bf16[128,2560]{1,0:T(8,128)(2,1)S(1)}, bf16[128,2560]{1,0:T(8,128)(2,1)S(1)}, u32[]{:S(2)}, u32[]{:S(2)}) collective-permute-start(bf16[128,2560]{1,0:T(8,128)(2,1)S(1)} %collective-permute-done.13.refs_1_), channel_id=1, source_target_pairs={{0,4},{4,0},{8,12},{12,8},{16,20},{20,16},{24,28},{28,24},{1,5},{5... | collective-permute-start | bytes 1966088 | tf_op jit(solution)/shard_map/ppermute | solution.py:423
  107.5 16.6 %collective-permute-start.24 = (bf16[128,2560]{1,0:T(8,128)(2,1)S(1)}, bf16[128,2560]{1,0:T(8,128)(2,1)S(1)}, u32[]{:S(2)}, u32[]{:S(2)}) collective-permute-start(bf16[128,2560]{1,0:T(8,128)(2,1)S(1)} %collective-permute-done.11.refs_2_), channel_id=1, source_target_pairs={{0,4},{4,0},{8,12},{12,8},{16,20},{20,16},{24,28},{28,24},{1,5},{5... | collective-permute-start | bytes 1966088 | tf_op jit(solution)/shard_map/ppermute | solution.py:423
  107.7 16.5 %collective-permute-start.25 = (bf16[128,2560]{1,0:T(8,128)(2,1)S(1)}, bf16[128,2560]{1,0:T(8,128)(2,1)S(1)}, u32[]{:S(2)}, u32[]{:S(2)}) collective-permute-start(bf16[128,2560]{1,0:T(8,128)(2,1)S(1)} %collective-permute-done.12.refs_3_), channel_id=1, source_target_pairs={{0,4},{4,0},{8,12},{12,8},{16,20},{20,16},{24,28},{28,24},{1,5},{5... | collective-permute-start | bytes 1966088 | tf_op jit(solution)/shard_map/ppermute | solution.py:423
  112.3 9.3 %collective-permute-start.21 = (bf16[128,1024]{1,0:T(8,128)(2,1)S(1)}, bf16[128,1024]{1,0:T(8,128)(2,1)S(1)}, u32[]{:S(2)}, u32[]{:S(2)}) collective-permute-start(bf16[128,1024]{1,0:T(8,128)(2,1)S(1)} %attention.3.rows_ref), channel_id=1, source_target_pairs={{0,1},{3,2},{4,5},{7,6},{8,9},{11,10},{12,13},{15,14},{16,17},{19,... | collective-permute-start | bytes 786440 | tf_op jit(solution)/shard_map/ppermute | solution.py:420
  121.5 19.5 %collective-permute-start.27 = (bf16[128,2560]{1,0:T(8,128)(2,1)S(1)}, bf16[128,2560]{1,0:T(8,128)(2,1)S(1)}, u32[]{:S(2)}, u32[]{:S(2)}) collective-permute-start(bf16[128,2560]{1,0:T(8,128)(2,1)S(1)} %mix.8.refs_0_), channel_id=1, source_target_pairs={{0,1},{3,2},{4,5},{7,6},{8,9},{11,10},{12,13},{15,14},{16,17},{19,... | collective-permute-start | bytes 1966088 | tf_op jit(solution)/shard_map/ppermute | solution.py:420
  127.0 28.6 %collective-permute-start.28 = (bf16[128,2560]{1,0:T(8,128)(2,1)S(1)}, bf16[128,2560]{1,0:T(8,128)(2,1)S(1)}, u32[]{:S(2)}, u32[]{:S(2)}) collective-permute-start(bf16[128,2560]{1,0:T(8,128)(2,1)S(1)} %added.8), channel_id=1, source_target_pairs={{1,2},{2,1},{5,6},{6,5},{9,10},{10,9},{13,14},{14,13},{17,18},{18,... | collective-permute-start | bytes 1966088 | tf_op jit(solution)/shard_map/ppermute | solution.py:414
  127.7 15.7 %collective-permute-start.26 = (bf16[128,1024]{1,0:T(8,128)(2,1)S(1)}, bf16[128,1024]{1,0:T(8,128)(2,1)S(1)}, u32[]{:S(2)}, u32[]{:S(2)}) collective-permute-start(bf16[128,1024]{1,0:T(8,128)(2,1)S(1)} %attention.4.rows_ref), channel_id=1, source_target_pairs={{0,1},{3,2},{4,5},{7,6},{8,9},{11,10},{12,13},{15,14},{16,17},{19,... | collective-permute-start | bytes 786440 | tf_op jit(solution)/shard_map/ppermute | solution.py:420
  141.2 20.4 %collective-permute-start.29 = (bf16[128,2560]{1,0:T(8,128)(2,1)S(1)}, bf16[128,2560]{1,0:T(8,128)(2,1)S(1)}, u32[]{:S(2)}, u32[]{:S(2)}) collective-permute-start(bf16[128,2560]{1,0:T(8,128)(2,1)S(1)} %added.9), channel_id=1, source_target_pairs={{1,2},{2,1},{5,6},{6,5},{9,10},{10,9},{13,14},{14,13},{17,18},{18,... | collective-permute-start | bytes 1966088 | tf_op jit(solution)/shard_map/ppermute | solution.py:414
  146.3 25.5 %collective-permute-start.34 = (bf16[128,2560]{1,0:T(8,128)(2,1)S(1)}, bf16[128,2560]{1,0:T(8,128)(2,1)S(1)}, u32[]{:S(2)}, u32[]{:S(2)}) collective-permute-start(bf16[128,2560]{1,0:T(8,128)(2,1)S(1)} %mix.10.refs_0_), channel_id=1, source_target_pairs={{0,1},{3,2},{4,5},{7,6},{8,9},{11,10},{12,13},{15,14},{16,17},{19,... | collective-permute-start | bytes 1966088 | tf_op jit(solution)/shard_map/ppermute | solution.py:420
  154.9 22.2 %collective-permute-start.33 = (bf16[128,2560]{1,0:T(8,128)(2,1)S(1)}, bf16[128,2560]{1,0:T(8,128)(2,1)S(1)}, u32[]{:S(2)}, u32[]{:S(2)}) collective-permute-start(bf16[128,2560]{1,0:T(8,128)(2,1)S(1)} %added.10), channel_id=1, source_target_pairs={{1,2},{2,1},{5,6},{6,5},{9,10},{10,9},{13,14},{14,13},{17,18},{18,... | collective-permute-start | bytes 1966088 | tf_op jit(solution)/shard_map/ppermute | solution.py:414
  155.7 21.4 %collective-permute-start.32 = (bf16[128,2560]{1,0:T(8,128)(2,1)S(1)}, bf16[128,2560]{1,0:T(8,128)(2,1)S(1)}, u32[]{:S(2)}, u32[]{:S(2)}) collective-permute-start(bf16[128,2560]{1,0:T(8,128)(2,1)S(1)} %added.11), channel_id=1, source_target_pairs={{1,0},{2,3},{5,4},{6,7},{9,8},{10,11},{13,12},{14,15},{17,16},{18,... | collective-permute-start | bytes 1966088 | tf_op jit(solution)/shard_map/ppermute | solution.py:417
  157.0 12.1 %collective-permute-start.30 = (bf16[128,1024]{1,0:T(8,128)(2,1)S(1)}, bf16[128,1024]{1,0:T(8,128)(2,1)S(1)}, u32[]{:S(2)}, u32[]{:S(2)}) collective-permute-start(bf16[128,1024]{1,0:T(8,128)(2,1)S(1)} %get-tuple-element.89.rows_ref), channel_id=1, source_target_pairs={{0,1},{3,2},{4,5},{7,6},{8,9},{11,10},{12,13},{15,14},{16,17},{19,... | collective-permute-start | bytes 786440 | tf_op jit(solution)/shard_map/ppermute | solution.py:420
  172.0 16.3 %collective-permute-start.31 = (bf16[128,2560]{1,0:T(8,128)(2,1)S(1)}, bf16[128,2560]{1,0:T(8,128)(2,1)S(1)}, u32[]{:S(2)}, u32[]{:S(2)}) collective-permute-start(bf16[128,2560]{1,0:T(8,128)(2,1)S(1)} %mix.13.refs_0_), channel_id=1, source_target_pairs={{0,1},{3,2},{4,5},{7,6},{8,9},{11,10},{12,13},{15,14},{16,17},{19,... | collective-permute-start | bytes 1966088 | tf_op jit(solution)/shard_map/ppermute | solution.py:420
  176.4 11.9 %collective-permute-start.36 = (bf16[128,2560]{1,0:T(8,128)(2,1)S(1)}, bf16[128,2560]{1,0:T(8,128)(2,1)S(1)}, u32[]{:S(2)}, u32[]{:S(2)}) collective-permute-start(bf16[128,2560]{1,0:T(8,128)(2,1)S(1)} %added.12), channel_id=1, source_target_pairs={{1,2},{2,1},{5,6},{6,5},{9,10},{10,9},{13,14},{14,13},{17,18},{18,... | collective-permute-start | bytes 1966088 | tf_op jit(solution)/shard_map/ppermute | solution.py:414
  178.4 16.0 %collective-permute-start.35 = (bf16[128,2560]{1,0:T(8,128)(2,1)S(1)}, bf16[128,2560]{1,0:T(8,128)(2,1)S(1)}, u32[]{:S(2)}, u32[]{:S(2)}) collective-permute-start(bf16[128,2560]{1,0:T(8,128)(2,1)S(1)} %added.14), channel_id=1, source_target_pairs={{1,0},{2,3},{5,4},{6,7},{9,8},{10,11},{13,12},{14,15},{17,16},{18,... | collective-permute-start | bytes 1966088 | tf_op jit(solution)/shard_map/ppermute | solution.py:417

commit v9 on v8

--- a/solution.py
+++ b/solution.py
@@ -369,6 +369,27 @@
     )(places, attended, *pieces)
 
 
+def halves_kernel(ref, first_ref, second_ref):
+    half = first_ref.shape[0]
+    first_ref[...] = ref[:half, :]
+    second_ref[...] = ref[half:, :]
+
+
+def halves(array):
+    rows, width = array.shape
+    half = jax.ShapeDtypeStruct((rows // 2, width), array.dtype)
+    return pl.pallas_call(
+        halves_kernel,
+        grid=(1,),
+        in_specs=[whole(rows, width)],
+        out_specs=[whole(rows // 2, width)] * 2,
+        out_shape=[half, half],
+        compiler_params=params(8),
+        cost_estimate=cost(1),
+        name="halves",
+    )(array)
+
+
 def add_kernel(count, *refs):
     total = refs[0][...].astype(jnp.float32)
     for ref in refs[1:count]:
@@ -434,18 +455,13 @@
     weights = [w_query, w_key, w_value]
     half = rows_here // 2
 
-    mine = [lax.slice_in_dim(hidden_in, i * half, (i + 1) * half) for i in (0, 1)]
-    from_near, from_mid = [], []
-    for array in mine:
-        from_near.append(swap(array))
-        from_mid.append(across(array))
+    from_near = swap(hidden_in)
+    from_mid = [across(array) for array in halves(hidden_in)]
     accs = partial_projection(places, OWN, [[hidden_in]], weights, None)
-    from_near[0], from_mid[0], accs = lax.optimization_barrier((from_near[0], from_mid[0], accs))
+    from_mid[0], accs = lax.optimization_barrier((from_mid[0], accs))
     to_outer = [outward(array) for array in from_mid]
-    cue = (from_near[1], from_mid[1])
-    accs = partial_projection(
-        after(places, cue), NEAR, [[a] for a in from_near], weights, accs
-    )
+    accs = partial_projection(after(places, from_mid[1]), NEAR, [[from_near]], weights, accs)
+    from_near = halves(from_near)
     to_inner = [across(from_near[0])]
     to_inner.append(across(after(from_near[1], (to_outer[0], accs))))
     end = [outward(array) for array in to_inner]
@@ -516,21 +532,19 @@
     far_left = added(far[0], after(far_in, near_rows))
     third_sent = after(third_sent, far_left)
     far_left = across(far_left)
-    third_in = inward(after(third[0], third_sent))
+    third_in = inward(third[0])
     third_right = added(third[1], share_of(third_sent))
     near = mixed(after(near_rows, third_right))
     near_sent = send(near_rows, near[1])
     third_right = across(third_right)
     out_right = added(near[1], after(far_right, near))
     kept = mixed(after(own_rows, (out_right, far_left)))
-    near_sent = after(near_sent, kept)
-    near_in = inward(after(near[0], near_sent))
-    near_sent = share_of(near_sent)
-    third_left = added(third[0], after(third_in, near_sent))
-    arrived = after((outward(out_right), third_right), third_left)
-    result = added(kept[1], near_sent, *arrived, half=1)
-    third_left = across(third_left)
-    out_left = outward(added(near[0], after(far_left, result)))
+    out_left = added(near[0], after(far_left, kept))
+    third_left = added(third[0], after(third_in, out_left))
+    near_sent = share_of(after(near_sent, third_left))
+    result = added(kept[1], near_sent, outward(out_right), third_right, half=1)
+    near_in = inward(after(near[0], third_left))
+    out_left, third_left = outward(out_left), across(third_left)
     return added(kept[0], near_in, out_left, third_left, half=0, into=result)
 
 

time: 197 us -> 204 us (1.036)
  waiting for transfers between devices: 47.2 us -> 67.3 us
  Pallas kernels: 67 us -> 61.8 us
  local copies, waits for them, and re-layouts: 15.4 us -> 11.1 us
  starting transfers between devices: 64.5 us -> 61.3 us
    ppermute x6, waiting for transfers between devices: 16.9 us -> 29.9 us  [outward(): return lax.ppermute(array, 'tensor', [(1, 0), (2, 3)])]
    ppermute x8, waiting for transfers between devices: 13.4 us -> 24.5 us  [inward(): return lax.ppermute(array, 'tensor', [(0, 1), (3, 2)])]
    ppermute x2 -> x1, waiting for transfers between devices: 16.5 us -> 11.1 us  [swap(): return lax.ppermute(array, 'tensor', [(0, 1), (1, 0), (2, 3), (3, 2)])]
    ppermute x2 -> x1, starting transfers between devices: 6.67 us -> 3.02 us  [swap(): return lax.ppermute(array, 'tensor', [(0, 1), (1, 0), (2, 3), (3, 2)])]
    slice x1 -> x0, local copies, waits for them, and re-layouts: 2.61 us -> none  [shards(): lax.slice_in_dim(hidden_in, i * half, (i + 1) * half)]
    ppermute x8, starting transfers between devices: 31.3 us -> 33.7 us  [inward(): return lax.ppermute(array, 'tensor', [(0, 1), (3, 2)])]
    pallas_call x2, Pallas kernels: 4.71 us -> 2.38 us  [keys_values(): pl.pallas_call(functools.partial(keys_values_kernel, len(hidden), len(bef...]
    pallas_call x2, Pallas kernels: 7.08 us -> 4.96 us  [queries_of(): pl.pallas_call(functools.partial(queries_kernel, len(hidden)), grid_spec=...]
  transfers between devices with their start and end apart: 37 -> 36, of which waited for: 10 -> 12; matrix products, arithmetic and copies ran while one was open for 0% -> 0% of each run, Pallas kernels for 32% -> 27%
where the time goes in v9:
time: 204 us; the launch traced here: 203 us
  waiting for transfers between devices  67.3 us (33%)
  Pallas kernels  61.8 us (30%)
  starting transfers between devices  61.3 us (30%)
  local copies, waits for them, and re-layouts  11.1 us (5%)
    ppermute x8, starting transfers between devices, inward(): return lax.ppermute(array, 'tensor', [(0, 1), (3, 2)])  33.7 us
    ppermute x6, waiting for transfers between devices, outward(): return lax.ppermute(array, 'tensor', [(1, 0), (2, 3)])  29.9 us
    ppermute x8, waiting for transfers between devices, inward(): return lax.ppermute(array, 'tensor', [(0, 1), (3, 2)])  24.5 us
    pallas_call x8, Pallas kernels, mix(): pl.pallas_call(mix_kernel, grid=(tiles,), in_specs=[whole(rows, depth), p...  16.5 us
    pallas_call x3, Pallas kernels, attention(): pl.pallas_call(functools.partial(attention_kernel, slots, n_parts, len(ot...  12.7 us
    pallas_call x3, Pallas kernels, partial_projection(): pl.pallas_call(functools.partial(partial_kernel, [len(part) for part in p...  11.8 us
    ppermute x1, waiting for transfers between devices, swap(): return lax.ppermute(array, 'tensor', [(0, 1), (1, 0), (2, 3), (3, 2)])  11.1 us
    unnamed x36, local copies, waits for them, and re-layouts  11 us
  transfers between devices with their start and end apart: 36, of which 12 were waited for; matrix products, arithmetic and copies ran while one was open for 0% of the time, Pallas kernels for 27%

profile of v9, /device:TPU:0, one launch (start us, length us, event | category | flops | bytes accessed | tf_op | source)
XLA Modules:
  0.0 202.8 jit_solution(15602948844308254661)
XLA Ops:
  0.0 3.0 %collective-permute-start = (bf16[512,1280]{1,0:T(8,128)(2,1)}, bf16[512,1280]{1,0:T(8,128)(2,1)S(1)}, u32[]{:S(2)}, u32[]{:S(2)}) collective-permute-start(bf16[512,1280]{1,0:T(8,128)(2,1)} %refs_0_.1), channel_id=1, source_target_pairs={{0,1},{1,0},{2,3},{3,2},{4,5},{5,4},{6,7},{7,6},{8,9},{9,8},{10,11... | collective-permute-start | bytes 3932168 | tf_op jit(solution)/shard_map/ppermute | solution.py:432
  3.0 1.3 copy-done.4
  4.4 0.9 halves.3
  5.3 1.5 collective-permute-start.3
  6.8 1.5 collective-permute-start.5
  8.4 4.0 %copy-done.1 = bf16[5120,1024]{1,0:T(8,128)(2,1)S(1)} copy-done((bf16[5120,1024]{1,0:T(8,128)(2,1)S(1)}, bf16[5120,1024]{1,0:T(8,128)(2,1)}, u32[]{:S(2)}) %copy-start.1) | copy-done | bytes 10485784
  12.4 1.3 copy-done.3
  13.7 1.3 copy-done.5
  15.0 3.4 %partial_projection.3 = (f32[512,1024]{1,0:T(8,128)S(1)}, f32[512,128]{1,0:T(8,128)S(1)}, f32[512,128]{1,0:T(8,128)S(1)}) custom-call(s32[12]{0:T(128)S(1)} %stack.51.places_ref, bf16[512,1280]{1,0:T(8,128)(2,1)S(1)} %copy-done.5, bf16[5120,1024]{1,0:T(8,128)(2,1)S(1)} %copy-done.1, bf16[5120,128]{1,0:T(8,128)(2,1)S(1)} %copy-done.2, ...), custom_call_target="tpu_custom_call" | custom-call | flops 1 | bytes 1 | tf_op jit(solution)/shard_map/partial_projection/pallas_call | solution.py:96
  18.5 1.3 collective-permute-start.4
  20.4 1.3 collective-permute-start.7
  21.7 11.1 %collective-permute-done.ref.refs_0_ = bf16[512,1280]{1,0:T(8,128)(2,1)S(1)} collective-permute-done((bf16[512,1280]{1,0:T(8,128)(2,1)}, bf16[512,1280]{1,0:T(8,128)(2,1)S(1)}, u32[]{:S(2)}, u32[]{:S(2)}) %collective-permute-start) | collective-permute-done | bytes 1310752 | tf_op jit(solution)/shard_map/ppermute | solution.py:432
  33.7 3.6 %partial_projection.4 = (f32[512,1024]{1,0:T(8,128)S(1)}, f32[512,128]{1,0:T(8,128)S(1)}, f32[512,128]{1,0:T(8,128)S(1)}) custom-call(s32[12]{0:T(128)S(1)} %stack.51.places_ref, bf16[512,1280]{1,0:T(8,128)(2,1)S(1)} %collective-permute-done.ref.refs_0_, bf16[5120,1024]{1,0:T(8,128)(2,1)S(1)} %copy-done.1, bf16[5120,128]{1,0:T(8,128)(2,1)S(1)} %copy-done.2, ...), custom_call_target="tpu_custom_call" | custom-call | flops 1 | bytes 1 | tf_op jit(solution)/shard_map/partial_projection/pallas_call | solution.py:96
  37.3 9.6 %collective-permute-done.4.refs_1_ = bf16[256,1280]{1,0:T(8,128)(2,1)S(1)} collective-permute-done((bf16[256,1280]{1,0:T(8,128)(2,1)}, bf16[256,1280]{1,0:T(8,128)(2,1)S(1)}, u32[]{:S(2)}, u32[]{:S(2)}) %collective-permute-start.4) | collective-permute-done | bytes 655392 | tf_op jit(solution)/shard_map/ppermute | solution.py:438
  47.7 6.1 %collective-permute-start.9 = (bf16[128,2560]{1,0:T(8,128)(2,1)S(1)}, bf16[128,2560]{1,0:T(8,128)(2,1)S(1)}, u32[]{:S(2)}, u32[]{:S(2)}) collective-permute-start(bf16[128,2560]{1,0:T(8,128)(2,1)S(1)} %eighth.2), channel_id=1, source_target_pairs={{0,1},{3,2},{4,5},{7,6},{8,9},{11,10},{12,13},{15,14},{16,17},{19,... | collective-permute-start | bytes 1966088 | tf_op jit(solution)/shard_map/ppermute | solution.py:441
  53.9 1.3 collective-permute-start.2
  55.8 5.1 %collective-permute-done.7.refs_3_ = bf16[256,1280]{1,0:T(8,128)(2,1)S(1)} collective-permute-done((bf16[256,1280]{1,0:T(8,128)(2,1)}, bf16[256,1280]{1,0:T(8,128)(2,1)S(1)}, u32[]{:S(2)}, u32[]{:S(2)}) %collective-permute-start.7) | collective-permute-done | bytes 655392 | tf_op jit(solution)/shard_map/ppermute | solution.py:438
  61.8 3.7 %collective-permute-done.9.refs_0_ = bf16[128,2560]{1,0:T(8,128)(2,1)S(1)} collective-permute-done((bf16[128,2560]{1,0:T(8,128)(2,1)S(1)}, bf16[128,2560]{1,0:T(8,128)(2,1)S(1)}, u32[]{:S(2)}, u32[]{:S(2)}) %collective-permute-start.9) | collective-permute-done | bytes 655392 | tf_op jit(solution)/shard_map/ppermute | solution.py:441
  65.5 1.5 collective-permute-start.10
  67.0 1.5 collective-permute-start.11
  68.5 8.6 %collective-permute-start.12 = (bf16[128,2560]{1,0:T(8,128)(2,1)S(1)}, bf16[128,2560]{1,0:T(8,128)(2,1)S(1)}, u32[]{:S(2)}, u32[]{:S(2)}) collective-permute-start(bf16[128,2560]{1,0:T(8,128)(2,1)S(1)} %eighth.3), channel_id=1, source_target_pairs={{0,1},{3,2},{4,5},{7,6},{8,9},{11,10},{12,13},{15,14},{16,17},{19,... | collective-permute-start | bytes 1966088 | tf_op jit(solution)/shard_map/ppermute | solution.py:441
  77.1 1.3 collective-permute-start.8
  78.4 1.1 copy-done.9
  79.5 1.1 copy-done.11
  80.6 4.8 %partial_projection.5 = (f32[512,1024]{1,0:T(8,128)S(1)}, f32[512,128]{1,0:T(8,128)S(1)}, f32[512,128]{1,0:T(8,128)S(1)}) custom-call(s32[12]{0:T(128)S(1)} %stack.51.places_ref, bf16[256,1280]{1,0:T(8,128)(2,1)} %collective-permute-done.3.refs_0_, bf16[256,1280]{1,0:T(8,128)(2,1)S(1)} %copy-done.9, bf16[256,1280]{1,0:T(8,128)(2,1)} %collective-permute-done.5.refs_2_, ...), custom_call_target="tpu_custom_call" | custom-call | flops 1 | bytes 1 | tf_op jit(solution)/shard_map/partial_projection/pallas_call | solution.py:96
  85.4 2.5 %queries.2.refs_0_ = bf16[256,1024]{1,0:T(8,128)(2,1)S(1)} custom-call(s32[12]{0:T(128)S(1)} %stack.51.places_ref, bf16[256,1280]{1,0:T(8,128)(2,1)S(1)} %collective-permute-done.1.refs_0_, bf16[256,1280]{1,0:T(8,128)(2,1)S(1)} %collective-permute-done.2.refs_1_, bf16[5120,1024]{1,0:T(8,128)(2,1)S(1)} %bitcast.15, ...), custom_call_target="tpu_custom_call" | custom-call | flops 1 | bytes 1 | tf_op jit(solution)/shard_map/queries/pallas_call | solution.py:183
  87.9 1.1 keys_values.2.refs_0_.refs_2_
  89.0 3.8 %collective-permute-done.8.refs_1_.refs_2_ = bf16[256,1280]{1,0:T(8,128)(2,1)S(1)} collective-permute-done((bf16[256,1280]{1,0:T(8,128)(2,1)S(1)}, bf16[256,1280]{1,0:T(8,128)(2,1)S(1)}, u32[]{:S(2)}, u32[]{:S(2)}) %collective-permute-start.8) | collective-permute-done | bytes 655392 | tf_op jit(solution)/shard_map/ppermute | solution.py:438
  92.8 1.3 keys_values.3
  94.8 1.3 collective-permute-start.15
  96.6 1.2 collective-permute-start.17
  98.2 0.9 collective-permute-done.14.refs_5_
  99.2 1.3 collective-permute-start.19
  101.1 2.5 %queries.3.refs_1_ = bf16[256,1024]{1,0:T(8,128)(2,1)S(1)} custom-call(s32[12]{0:T(128)S(1)} %stack.51.places_ref, bf16[256,1280]{1,0:T(8,128)(2,1)S(1)} %collective-permute-done.6.refs_0_.refs_1_, bf16[256,1280]{1,0:T(8,128)(2,1)S(1)} %collective-permute-done.8.refs_1_.refs_2_, bf16[5120,1024]{1,0:T(8,128)(2,1)S(1)} %bitcast.15, ...), custom_call_target="tpu_custom_call" | custom-call | flops 1 | bytes 1 | tf_op jit(solution)/shard_map/queries/pallas_call | solution.py:183
  103.7 0.8 collective-permute-done.19.refs_10_
  104.5 3.6 %attention.3.rows_ref = bf16[128,1024]{1,0:T(8,128)(2,1)S(1)} custom-call(s32[12]{0:T(128)S(1)} %stack.51.places_ref, s32[1]{0:T(128)S(6)} %copy.14.length_ref, bf16[256,1024]{1,0:T(8,128)(2,1)S(1)} %queries.2.refs_0_, bf16[256,1024]{1,0:T(8,128)(2,1)S(1)} %queries.3.refs_1_, bf16[256,256]{1,0:T(8,128)(2,1)S(1)} %keys_values.2.refs_0_.refs_2_, ...), custom_call_target="tpu_custom_call" | custom-call | flops 1 | bytes 1 | tf_op jit(solution)/shard_map/attention/pallas_call | solution.py:272
  108.1 1.6 collective-permute-start.20
  110.8 2.1 %mix.8.refs_0_ = bf16[128,2560]{1,0:T(8,128)(2,1)S(1)} custom-call(bf16[128,1024]{1,0:T(8,128)(2,1)S(1)} %attention.3.rows_ref, bf16[1024,5120]{1,0:T(8,128)(2,1)S(1)} %copy-done), custom_call_target="tpu_custom_call" | custom-call | flops 1 | bytes 1 | tf_op jit(solution)/shard_map/mix/pallas_call | solution.py:301
  112.9 2.1 %mix.9.refs_0_ = bf16[128,2560]{1,0:T(8,128)(2,1)S(1)} custom-call(bf16[128,1024]{1,0:T(8,128)(2,1)S(1)} %attention.3.rows_ref, bf16[1024,5120]{1,0:T(8,128)(2,1)S(1)} %copy-done), custom_call_target="tpu_custom_call" | custom-call | flops 1 | bytes 1 | tf_op jit(solution)/shard_map/mix/pallas_call | solution.py:301
  114.9 3.6 %attention.4.rows_ref = bf16[128,1024]{1,0:T(8,128)(2,1)S(1)} custom-call(s32[12]{0:T(128)S(1)} %stack.51.places_ref, s32[1]{0:T(128)S(6)} %copy.14.length_ref, bf16[256,1024]{1,0:T(8,128)(2,1)S(1)} %queries.2.refs_0_, bf16[256,1024]{1,0:T(8,128)(2,1)S(1)} %queries.3.refs_1_, bf16[256,256]{1,0:T(8,128)(2,1)S(1)} %keys_values.2.refs_0_.refs_2_, ...), custom_call_target="tpu_custom_call" | custom-call | flops 1 | bytes 1 | tf_op jit(solution)/shard_map/attention/pallas_call | solution.py:272
  118.5 1.3 collective-permute-start.26
  119.9 2.7 %mix_sent.3.refs_1_ = bf16[128,2560]{1,0:T(8,128)(2,1)S(1)} custom-call(s32[12]{0:T(128)S(1)} %stack.51.places_ref, bf16[128,1024]{1,0:T(8,128)(2,1)S(1)} %collective-permute-done.20.rows_ref, bf16[128,2560]{1,0:T(8,128)(2,1)S(1)} %collective-permute-done.9.refs_0_, bf16[128,2560]{1,0:T(8,128)(2,1)S(1)} %collective-permute-done.12.refs_1_, ...), custom_call_target="tpu_custom_call" | custom-call | flops 1 | bytes 1 | tf_op jit(solution)/shard_map/mix_sent/pallas_call | solution.py:357
  122.7 2.1 %mix.10.refs_0_ = bf16[128,2560]{1,0:T(8,128)(2,1)S(1)} custom-call(bf16[128,1024]{1,0:T(8,128)(2,1)S(1)} %attention.4.rows_ref, bf16[1024,5120]{1,0:T(8,128)(2,1)S(1)} %copy-done), custom_call_target="tpu_custom_call" | custom-call | flops 1 | bytes 1 | tf_op jit(solution)/shard_map/mix/pallas_call | solution.py:301
  124.8 2.1 %mix.11.refs_0_ = bf16[128,2560]{1,0:T(8,128)(2,1)S(1)} custom-call(bf16[128,1024]{1,0:T(8,128)(2,1)S(1)} %attention.4.rows_ref, bf16[1024,5120]{1,0:T(8,128)(2,1)S(1)} %copy-done), custom_call_target="tpu_custom_call" | custom-call | flops 1 | bytes 1 | tf_op jit(solution)/shard_map/mix/pallas_call | solution.py:301
  127.6 5.6 %attention.5 = (bf16[128,1024]{1,0:T(8,128)(2,1)S(1)}, bf16[128,1024]{1,0:T(8,128)(2,1)S(1)}) custom-call(s32[12]{0:T(128)S(1)} %stack.51.places_ref, s32[1]{0:T(128)S(6)} %copy.14.length_ref, bf16[256,1024]{1,0:T(8,128)(2,1)S(1)} %queries.2.refs_0_, bf16[256,1024]{1,0:T(8,128)(2,1)S(1)} %queries.3.refs_1_, bf16[256,256]{1,0:T(8,128)(2,1)S(1)} %keys_values.2.refs_0_.refs_2_, ...), custom_call_target="tpu_custom_call" | custom-call | flops 1 | bytes 1 | tf_op jit(solution)/shard_map/attention/pallas_call | solution.py:272
  133.2 1.1 collective-permute-done.26.refs_1_
  135.2 6.7 %collective-permute-start.29 = (bf16[128,2560]{1,0:T(8,128)(2,1)S(1)}, bf16[128,2560]{1,0:T(8,128)(2,1)S(1)}, u32[]{:S(2)}, u32[]{:S(2)}) collective-permute-start(bf16[128,2560]{1,0:T(8,128)(2,1)S(1)} %mix.10.refs_0_), channel_id=1, source_target_pairs={{0,1},{3,2},{4,5},{7,6},{8,9},{11,10},{12,13},{15,14},{16,17},{19,... | collective-permute-start | bytes 1966088 | tf_op jit(solution)/shard_map/ppermute | solution.py:441
  141.9 1.3 collective-permute-start.25
  143.2 1.3 collective-permute-start.33
  144.5 18.1 %collective-permute-done.25.rows_ref = bf16[128,1024]{1,0:T(8,128)(2,1)S(1)} collective-permute-done((bf16[128,1024]{1,0:T(8,128)(2,1)S(1)}, bf16[128,1024]{1,0:T(8,128)(2,1)S(1)}, u32[]{:S(2)}, u32[]{:S(2)}) %collective-permute-start.25) | collective-permute-done | bytes 262176 | tf_op jit(solution)/shard_map/ppermute | solution.py:441
  162.7 2.7 %mix_sent.4.refs_1_ = bf16[128,2560]{1,0:T(8,128)(2,1)S(1)} custom-call(s32[12]{0:T(128)S(1)} %stack.51.places_ref, bf16[128,1024]{1,0:T(8,128)(2,1)S(1)} %collective-permute-done.25.rows_ref, bf16[128,2560]{1,0:T(8,128)(2,1)S(1)} %collective-permute-done.9.refs_0_, bf16[128,2560]{1,0:T(8,128)(2,1)S(1)} %collective-permute-done.12.refs_1_, ...), custom_call_target="tpu_custom_call" | custom-call | flops 1 | bytes 1 | tf_op jit(solution)/shard_map/mix_sent/pallas_call | solution.py:357
  165.5 2.1 %mix.12.refs_0_ = bf16[128,2560]{1,0:T(8,128)(2,1)S(1)} custom-call(bf16[128,1024]{1,0:T(8,128)(2,1)S(1)} %get-tuple-element.92.rows_ref, bf16[1024,5120]{1,0:T(8,128)(2,1)S(1)} %copy-done), custom_call_target="tpu_custom_call" | custom-call | flops 1 | bytes 1 | tf_op jit(solution)/shard_map/mix/pallas_call | solution.py:301
  167.6 2.1 %mix.13.refs_0_ = bf16[128,2560]{1,0:T(8,128)(2,1)S(1)} custom-call(bf16[128,1024]{1,0:T(8,128)(2,1)S(1)} %get-tuple-element.92.rows_ref, bf16[1024,5120]{1,0:T(8,128)(2,1)S(1)} %copy-done), custom_call_target="tpu_custom_call" | custom-call | flops 1 | bytes 1 | tf_op jit(solution)/shard_map/mix/pallas_call | solution.py:301
  170.5 1.3 collective-permute-start.34
  171.8 2.1 %mix.14.refs_0_ = bf16[128,2560]{1,0:T(8,128)(2,1)S(1)} custom-call(bf16[128,1024]{1,0:T(8,128)(2,1)S(1)} %get-tuple-element.94.rows_ref, bf16[1024,5120]{1,0:T(8,128)(2,1)S(1)} %copy-done), custom_call_target="tpu_custom_call" | custom-call | flops 1 | bytes 1 | tf_op jit(solution)/shard_map/mix/pallas_call | solution.py:301
  173.9 2.1 %mix.15.refs_0_ = bf16[128,2560]{1,0:T(8,128)(2,1)S(1)} custom-call(bf16[128,1024]{1,0:T(8,128)(2,1)S(1)} %get-tuple-element.94.rows_ref, bf16[1024,5120]{1,0:T(8,128)(2,1)S(1)} %copy-done), custom_call_target="tpu_custom_call" | custom-call | flops 1 | bytes 1 | tf_op jit(solution)/shard_map/mix/pallas_call | solution.py:301
  176.1 1.3 collective-permute-start.31
  177.6 6.7 %collective-permute-start.30 = (bf16[128,2560]{1,0:T(8,128)(2,1)S(1)}, bf16[128,2560]{1,0:T(8,128)(2,1)S(1)}, u32[]{:S(2)}, u32[]{:S(2)}) collective-permute-start(bf16[128,2560]{1,0:T(8,128)(2,1)S(1)} %mix.13.refs_0_), channel_id=1, source_target_pairs={{0,1},{3,2},{4,5},{7,6},{8,9},{11,10},{12,13},{15,14},{16,17},{19,... | collective-permute-start | bytes 1966088 | tf_op jit(solution)/shard_map/ppermute | solution.py:441
  185.0 2.7 %mix_sent.5.refs_1_ = bf16[128,2560]{1,0:T(8,128)(2,1)S(1)} custom-call(s32[12]{0:T(128)S(1)} %stack.51.places_ref, bf16[128,1024]{1,0:T(8,128)(2,1)S(1)} %collective-permute-done.33.rows_ref, bf16[128,2560]{1,0:T(8,128)(2,1)S(1)} %collective-permute-done.9.refs_0_, bf16[128,2560]{1,0:T(8,128)(2,1)S(1)} %collective-permute-done.12.refs_1_, ...), custom_call_target="tpu_custom_call" | custom-call | flops 1 | bytes 1 | tf_op jit(solution)/shard_map/mix_sent/pallas_call | solution.py:357
  187.7 4.4 %collective-permute-done.34.refs_2_ = bf16[128,2560]{1,0:T(8,128)(2,1)S(1)} collective-permute-done((bf16[128,2560]{1,0:T(8,128)(2,1)S(1)}, bf16[128,2560]{1,0:T(8,128)(2,1)S(1)}, u32[]{:S(2)}, u32[]{:S(2)}) %collective-permute-start.34) | collective-permute-done | bytes 655392 | tf_op jit(solution)/shard_map/ppermute | solution.py:438
  192.0 1.2 added.14.refs_4_
  193.2 1.5 collective-permute-done.30.refs_1_
  194.7 7.0 %collective-permute-done.31.refs_2_ = bf16[128,2560]{1,0:T(8,128)(2,1)S(1)} collective-permute-done((bf16[128,2560]{1,0:T(8,128)(2,1)S(1)}, bf16[128,2560]{1,0:T(8,128)(2,1)S(1)}, u32[]{:S(2)}, u32[]{:S(2)}) %collective-permute-start.31) | collective-permute-done | bytes 655392 | tf_op jit(solution)/shard_map/ppermute | solution.py:438
  201.7 1.2 added.15
  (79 shorter events, 10.3 us)
Async XLA Ops:
  0.0 8.4 %copy-start.2 = (bf16[5120,128]{1,0:T(8,128)(2,1)S(1)}, bf16[5120,128]{1,0:T(8,128)(2,1)}, u32[]{:S(2)}) copy-start(bf16[5120,128]{1,0:T(8,128)(2,1)} %refs_3_.7) | copy-start | bytes 3932164
  0.0 32.8 %collective-permute-start = (bf16[512,1280]{1,0:T(8,128)(2,1)}, bf16[512,1280]{1,0:T(8,128)(2,1)S(1)}, u32[]{:S(2)}, u32[]{:S(2)}) collective-permute-start(bf16[512,1280]{1,0:T(8,128)(2,1)} %refs_0_.1), channel_id=1, source_target_pairs={{0,1},{1,0},{2,3},{3,2},{4,5},{5,4},{6,7},{7,6},{8,9},{9,8},{10,11... | collective-permute-start | bytes 3932168 | tf_op jit(solution)/shard_map/ppermute | solution.py:432
  3.0 1.4 copy-start.4
  5.3 13.2 %collective-permute-start.3 = (bf16[256,1280]{1,0:T(8,128)(2,1)}, bf16[256,1280]{1,0:T(8,128)(2,1)}, u32[]{:S(2)}, u32[]{:S(2)}) collective-permute-start(bf16[256,1280]{1,0:T(8,128)(2,1)} %get-tuple-element.54), channel_id=1, source_target_pairs={{1,2},{2,1},{5,6},{6,5},{9,10},{10,9},{13,14},{14,13},{17,18},{18,... | collective-permute-start | bytes 1966088 | tf_op jit(solution)/shard_map/ppermute | solution.py:435
  6.8 13.6 %collective-permute-start.5 = (bf16[256,1280]{1,0:T(8,128)(2,1)S(1)}, bf16[256,1280]{1,0:T(8,128)(2,1)}, u32[]{:S(2)}, u32[]{:S(2)}) collective-permute-start(bf16[256,1280]{1,0:T(8,128)(2,1)S(1)} %get-tuple-element.59), channel_id=1, source_target_pairs={{1,2},{2,1},{5,6},{6,5},{9,10},{10,9},{13,14},{14,13},{17,18},{18,... | collective-permute-start | bytes 1966088 | tf_op jit(solution)/shard_map/ppermute | solution.py:435
  8.4 4.0 %copy-start.1 = (bf16[5120,1024]{1,0:T(8,128)(2,1)S(1)}, bf16[5120,1024]{1,0:T(8,128)(2,1)}, u32[]{:S(2)}) copy-start(bf16[5120,1024]{1,0:T(8,128)(2,1)} %refs_2_.8) | copy-start | bytes 31457284
  12.4 1.3 copy-start.3
  13.7 1.3 copy-start.5
  15.0 4.8 %copy-start = (bf16[1024,5120]{1,0:T(8,128)(2,1)S(1)}, bf16[1024,5120]{1,0:T(8,128)(2,1)}, u32[]{:S(2)}) copy-start(bf16[1024,5120]{1,0:T(8,128)(2,1)} %w_ref.19) | copy-start | bytes 31457284
  18.5 28.4 %collective-permute-start.4 = (bf16[256,1280]{1,0:T(8,128)(2,1)}, bf16[256,1280]{1,0:T(8,128)(2,1)S(1)}, u32[]{:S(2)}, u32[]{:S(2)}) collective-permute-start(bf16[256,1280]{1,0:T(8,128)(2,1)} %collective-permute-done.3.refs_0_), channel_id=1, source_target_pairs={{1,0},{2,3},{5,4},{6,7},{9,8},{10,11},{13,12},{14,15},{17,16},{18,... | collective-permute-start | bytes 1966088 | tf_op jit(solution)/shard_map/ppermute | solution.py:438
  20.4 40.5 %collective-permute-start.7 = (bf16[256,1280]{1,0:T(8,128)(2,1)}, bf16[256,1280]{1,0:T(8,128)(2,1)S(1)}, u32[]{:S(2)}, u32[]{:S(2)}) collective-permute-start(bf16[256,1280]{1,0:T(8,128)(2,1)} %collective-permute-done.5.refs_2_), channel_id=1, source_target_pairs={{1,0},{2,3},{5,4},{6,7},{9,8},{10,11},{13,12},{14,15},{17,16},{18,... | collective-permute-start | bytes 1966088 | tf_op jit(solution)/shard_map/ppermute | solution.py:438
  32.9 20.9 %collective-permute-start.1 = (bf16[256,1280]{1,0:T(8,128)(2,1)S(1)}, bf16[256,1280]{1,0:T(8,128)(2,1)S(1)}, u32[]{:S(2)}, u32[]{:S(2)}) collective-permute-start(bf16[256,1280]{1,0:T(8,128)(2,1)S(1)} %get-tuple-element.52), channel_id=1, source_target_pairs={{1,2},{2,1},{5,6},{6,5},{9,10},{10,9},{13,14},{14,13},{17,18},{18,... | collective-permute-start | bytes 1966088 | tf_op jit(solution)/shard_map/ppermute | solution.py:435
  33.6 44.7 %slice-start = ((s8[10485760]{0:T(1024)(128)(4,1)}), s8[4194304]{0:T(1024)(128)(4,1)S(1)}, s32[]{:S(2)}) async-start(s8[10485760]{0:T(1024)(128)(4,1)} %bitcast.14), calls=%async_computation | async-start | bytes 8388608
  33.7 44.7 %slice-start.1 = ((s8[10485760]{0:T(1024)(128)(4,1)}), s8[4194304]{0:T(1024)(128)(4,1)S(1)}, s32[]{:S(2)}) async-start(s8[10485760]{0:T(1024)(128)(4,1)} %bitcast.14), calls=%async_computation.1 | async-start | bytes 8388608
  46.9 8.9 %copy-start.8 = (bf16[256,1280]{1,0:T(8,128)(2,1)}, bf16[256,1280]{1,0:T(8,128)(2,1)S(1)}, u32[]{:S(2)}) copy-start(bf16[256,1280]{1,0:T(8,128)(2,1)S(1)} %collective-permute-done.4.refs_1_) | copy-start | bytes 1966084
  46.9 31.5 %slice-start.2 = ((s8[10485760]{0:T(1024)(128)(4,1)}), s8[2097152]{0:T(1024)(128)(4,1)S(1)}, s32[]{:S(2)}) async-start(s8[10485760]{0:T(1024)(128)(4,1)} %bitcast.14), calls=%async_computation.2 | async-start | bytes 4194304
  46.9 14.9 %collective-permute-start.6 = (bf16[256,1280]{1,0:T(8,128)(2,1)S(1)}, bf16[256,1280]{1,0:T(8,128)(2,1)S(1)}, u32[]{:S(2)}, u32[]{:S(2)}) collective-permute-start(bf16[256,1280]{1,0:T(8,128)(2,1)S(1)} %get-tuple-element.67), channel_id=1, source_target_pairs={{1,2},{2,1},{5,6},{6,5},{9,10},{10,9},{13,14},{14,13},{17,18},{18,... | collective-permute-start | bytes 1966088 | tf_op jit(solution)/shard_map/ppermute | solution.py:435
  47.7 17.8 %collective-permute-start.9 = (bf16[128,2560]{1,0:T(8,128)(2,1)S(1)}, bf16[128,2560]{1,0:T(8,128)(2,1)S(1)}, u32[]{:S(2)}, u32[]{:S(2)}) collective-permute-start(bf16[128,2560]{1,0:T(8,128)(2,1)S(1)} %eighth.2), channel_id=1, source_target_pairs={{0,1},{3,2},{4,5},{7,6},{8,9},{11,10},{12,13},{15,14},{16,17},{19,... | collective-permute-start | bytes 1966088 | tf_op jit(solution)/shard_map/ppermute | solution.py:441
  53.9 31.5 %collective-permute-start.2 = (bf16[256,1280]{1,0:T(8,128)(2,1)S(1)}, bf16[256,1280]{1,0:T(8,128)(2,1)S(1)}, u32[]{:S(2)}, u32[]{:S(2)}) collective-permute-start(bf16[256,1280]{1,0:T(8,128)(2,1)S(1)} %collective-permute-done.1.refs_0_), channel_id=1, source_target_pairs={{1,0},{2,3},{5,4},{6,7},{9,8},{10,11},{13,12},{14,15},{17,16},{18,... | collective-permute-start | bytes 1966088 | tf_op jit(solution)/shard_map/ppermute | solution.py:438
  55.2 30.2 %copy-start.13 = (f32[128]{0:T(128)S(1)}, f32[128]{0:T(128)}, u32[]{:S(2)}) copy-start(f32[128]{0:T(128)} %param.18) | copy-start | bytes 1540
  55.8 29.6 %copy-start.6 = (f32[512,128]{1,0:T(8,128)S(1)}, f32[512,128]{1,0:T(8,128)}, u32[]{:S(2)}) copy-start(f32[512,128]{1,0:T(8,128)} %constant.29.clone.refs_5_.refs_7_.refs_8_) | copy-start | bytes 786436
  55.8 29.6 %copy-start.7 = (f32[512,128]{1,0:T(8,128)S(1)}, f32[512,128]{1,0:T(8,128)}, u32[]{:S(2)}) copy-start(f32[512,128]{1,0:T(8,128)} %constant.30.clone.refs_6_.refs_8_.refs_9_) | copy-start | bytes 786436
  60.9 0.8 copy-start.10
  65.5 23.5 %collective-permute-start.10 = (bf16[128,2560]{1,0:T(8,128)(2,1)S(1)}, bf16[128,2560]{1,0:T(8,128)(2,1)S(1)}, u32[]{:S(2)}, u32[]{:S(2)}) collective-permute-start(bf16[128,2560]{1,0:T(8,128)(2,1)S(1)} %collective-permute-done.9.refs_0_), channel_id=1, source_target_pairs={{0,8},{4,12},{8,0},{12,4},{16,24},{20,28},{24,16},{28,20},{1,9},{5... | collective-permute-start | bytes 1966088 | tf_op jit(solution)/shard_map/ppermute | solution.py:444
  67.0 22.0 %collective-permute-start.11 = (bf16[128,2560]{1,0:T(8,128)(2,1)S(1)}, bf16[128,2560]{1,0:T(8,128)(2,1)S(1)}, u32[]{:S(2)}, u32[]{:S(2)}) collective-permute-start(bf16[128,2560]{1,0:T(8,128)(2,1)S(1)} %collective-permute-done.9.refs_0_), channel_id=1, source_target_pairs={{0,16},{4,20},{8,24},{12,28},{16,0},{20,4},{24,8},{28,12},{1,17},{... | collective-permute-start | bytes 1966088 | tf_op jit(solution)/shard_map/ppermute | solution.py:444
  68.5 20.5 %collective-permute-start.12 = (bf16[128,2560]{1,0:T(8,128)(2,1)S(1)}, bf16[128,2560]{1,0:T(8,128)(2,1)S(1)}, u32[]{:S(2)}, u32[]{:S(2)}) collective-permute-start(bf16[128,2560]{1,0:T(8,128)(2,1)S(1)} %eighth.3), channel_id=1, source_target_pairs={{0,1},{3,2},{4,5},{7,6},{8,9},{11,10},{12,13},{15,14},{16,17},{19,... | collective-permute-start | bytes 1966088 | tf_op jit(solution)/shard_map/ppermute | solution.py:441
  77.1 15.7 %collective-permute-start.8 = (bf16[256,1280]{1,0:T(8,128)(2,1)S(1)}, bf16[256,1280]{1,0:T(8,128)(2,1)S(1)}, u32[]{:S(2)}, u32[]{:S(2)}) collective-permute-start(bf16[256,1280]{1,0:T(8,128)(2,1)S(1)} %collective-permute-done.6.refs_0_.refs_1_), channel_id=1, source_target_pairs={{1,0},{2,3},{5,4},{6,7},{9,8},{10,11},{13,12},{14,15},{17,16},{18,... | collective-permute-start | bytes 1966088 | tf_op jit(solution)/shard_map/ppermute | solution.py:438
  78.4 1.1 copy-start.9
  79.5 1.1 copy-start.11
  85.4 2.5 %copy-start.12 = (f32[128]{0:T(128)S(1)}, f32[128]{0:T(128)}, u32[]{:S(2)}) copy-start(f32[128]{0:T(128)} %param.19) | copy-start | bytes 1540
  87.9 4.9 %copy-start.14 = (s32[1,128]{1,0:T(1,128)S(1)}, s32[1,128]{1,0:T(1,128)}, u32[]{:S(2)}) copy-start(s32[1,128]{1,0:T(1,128)} %refs_10_.1) | copy-start | bytes 1540
  94.1 3.6 %collective-permute-start.13 = (bf16[128,256]{1,0:T(8,128)(2,1)S(1)}, bf16[128,256]{1,0:T(8,128)(2,1)S(1)}, u32[]{:S(2)}, u32[]{:S(2)}) collective-permute-start(bf16[128,256]{1,0:T(8,128)(2,1)S(1)} %get-tuple-element.78), channel_id=1, source_target_pairs={{0,4},{4,0},{8,12},{12,8},{16,20},{20,16},{24,28},{28,24},{1,5},{5... | collective-permute-start | bytes 196616 | tf_op jit(solution)/shard_map/ppermute | solution.py:444
  94.2 5.0 %collective-permute-start.14 = (bf16[128,256]{1,0:T(8,128)(2,1)S(1)}, bf16[128,256]{1,0:T(8,128)(2,1)S(1)}, u32[]{:S(2)}, u32[]{:S(2)}) collective-permute-start(bf16[128,256]{1,0:T(8,128)(2,1)S(1)} %get-tuple-element.78), channel_id=1, source_target_pairs={{0,8},{4,12},{8,0},{12,4},{16,24},{20,28},{24,16},{28,20},{1,9},{5... | collective-permute-start | bytes 196616 | tf_op jit(solution)/shard_map/ppermute | solution.py:444
  94.8 8.8 %collective-permute-start.15 = (bf16[128,256]{1,0:T(8,128)(2,1)S(1)}, bf16[128,256]{1,0:T(8,128)(2,1)S(1)}, u32[]{:S(2)}, u32[]{:S(2)}) collective-permute-start(bf16[128,256]{1,0:T(8,128)(2,1)S(1)} %get-tuple-element.78), channel_id=1, source_target_pairs={{0,12},{4,8},{8,4},{12,0},{16,28},{20,24},{24,20},{28,16},{1,13},{... | collective-permute-start | bytes 196616 | tf_op jit(solution)/shard_map/ppermute | solution.py:444
  96.1 7.6 %collective-permute-start.16 = (bf16[128,256]{1,0:T(8,128)(2,1)S(1)}, bf16[128,256]{1,0:T(8,128)(2,1)S(1)}, u32[]{:S(2)}, u32[]{:S(2)}) collective-permute-start(bf16[128,256]{1,0:T(8,128)(2,1)S(1)} %get-tuple-element.78), channel_id=1, source_target_pairs={{0,16},{4,20},{8,24},{12,28},{16,0},{20,4},{24,8},{28,12},{1,17},{... | collective-permute-start | bytes 196616 | tf_op jit(solution)/shard_map/ppermute | solution.py:444
  96.6 7.1 %collective-permute-start.17 = (bf16[128,256]{1,0:T(8,128)(2,1)S(1)}, bf16[128,256]{1,0:T(8,128)(2,1)S(1)}, u32[]{:S(2)}, u32[]{:S(2)}) collective-permute-start(bf16[128,256]{1,0:T(8,128)(2,1)S(1)} %get-tuple-element.78), channel_id=1, source_target_pairs={{0,20},{4,16},{8,28},{12,24},{16,4},{20,0},{24,12},{28,8},{1,21},{... | collective-permute-start | bytes 196616 | tf_op jit(solution)/shard_map/ppermute | solution.py:444
  97.8 5.9 %collective-permute-start.18 = (bf16[128,256]{1,0:T(8,128)(2,1)S(1)}, bf16[128,256]{1,0:T(8,128)(2,1)S(1)}, u32[]{:S(2)}, u32[]{:S(2)}) collective-permute-start(bf16[128,256]{1,0:T(8,128)(2,1)S(1)} %get-tuple-element.78), channel_id=1, source_target_pairs={{0,24},{4,28},{8,16},{12,20},{16,8},{20,12},{24,0},{28,4},{1,25},{... | collective-permute-start | bytes 196616 | tf_op jit(solution)/shard_map/ppermute | solution.py:444
  99.2 5.3 %collective-permute-start.19 = (bf16[128,256]{1,0:T(8,128)(2,1)S(1)}, bf16[128,256]{1,0:T(8,128)(2,1)S(1)}, u32[]{:S(2)}, u32[]{:S(2)}) collective-permute-start(bf16[128,256]{1,0:T(8,128)(2,1)S(1)} %get-tuple-element.78), channel_id=1, source_target_pairs={{0,28},{4,24},{8,20},{12,16},{16,12},{20,8},{24,4},{28,0},{1,29},{... | collective-permute-start | bytes 196616 | tf_op jit(solution)/shard_map/ppermute | solution.py:444
  108.1 10.5 %collective-permute-start.20 = (bf16[128,1024]{1,0:T(8,128)(2,1)S(1)}, bf16[128,1024]{1,0:T(8,128)(2,1)S(1)}, u32[]{:S(2)}, u32[]{:S(2)}) collective-permute-start(bf16[128,1024]{1,0:T(8,128)(2,1)S(1)} %attention.3.rows_ref), channel_id=1, source_target_pairs={{0,1},{3,2},{4,5},{7,6},{8,9},{11,10},{12,13},{15,14},{16,17},{19,... | collective-permute-start | bytes 786440 | tf_op jit(solution)/shard_map/ppermute | solution.py:441
  109.7 10.2 %collective-permute-start.21 = (bf16[128,2560]{1,0:T(8,128)(2,1)S(1)}, bf16[128,2560]{1,0:T(8,128)(2,1)S(1)}, u32[]{:S(2)}, u32[]{:S(2)}) collective-permute-start(bf16[128,2560]{1,0:T(8,128)(2,1)S(1)} %collective-permute-done.9.refs_0_), channel_id=1, source_target_pairs={{0,4},{4,0},{8,12},{12,8},{16,20},{20,16},{24,28},{28,24},{1,5},{5... | collective-permute-start | bytes 1966088 | tf_op jit(solution)/shard_map/ppermute | solution.py:444
  109.8 10.1 %collective-permute-start.22 = (bf16[128,2560]{1,0:T(8,128)(2,1)S(1)}, bf16[128,2560]{1,0:T(8,128)(2,1)S(1)}, u32[]{:S(2)}, u32[]{:S(2)}) collective-permute-start(bf16[128,2560]{1,0:T(8,128)(2,1)S(1)} %collective-permute-done.12.refs_1_), channel_id=1, source_target_pairs={{0,4},{4,0},{8,12},{12,8},{16,20},{20,16},{24,28},{28,24},{1,5},{5... | collective-permute-start | bytes 1966088 | tf_op jit(solution)/shard_map/ppermute | solution.py:444
  110.3 9.6 %collective-permute-start.23 = (bf16[128,2560]{1,0:T(8,128)(2,1)S(1)}, bf16[128,2560]{1,0:T(8,128)(2,1)S(1)}, u32[]{:S(2)}, u32[]{:S(2)}) collective-permute-start(bf16[128,2560]{1,0:T(8,128)(2,1)S(1)} %collective-permute-done.10.refs_2_), channel_id=1, source_target_pairs={{0,4},{4,0},{8,12},{12,8},{16,20},{20,16},{24,28},{28,24},{1,5},{5... | collective-permute-start | bytes 1966088 | tf_op jit(solution)/shard_map/ppermute | solution.py:444
  110.4 9.5 %collective-permute-start.24 = (bf16[128,2560]{1,0:T(8,128)(2,1)S(1)}, bf16[128,2560]{1,0:T(8,128)(2,1)S(1)}, u32[]{:S(2)}, u32[]{:S(2)}) collective-permute-start(bf16[128,2560]{1,0:T(8,128)(2,1)S(1)} %collective-permute-done.11.refs_3_), channel_id=1, source_target_pairs={{0,4},{4,0},{8,12},{12,8},{16,20},{20,16},{24,28},{28,24},{1,5},{5... | collective-permute-start | bytes 1966088 | tf_op jit(solution)/shard_map/ppermute | solution.py:444
  118.5 15.8 %collective-permute-start.26 = (bf16[128,2560]{1,0:T(8,128)(2,1)S(1)}, bf16[128,2560]{1,0:T(8,128)(2,1)S(1)}, u32[]{:S(2)}, u32[]{:S(2)}) collective-permute-start(bf16[128,2560]{1,0:T(8,128)(2,1)S(1)} %mix.8.refs_0_), channel_id=1, source_target_pairs={{0,1},{3,2},{4,5},{7,6},{8,9},{11,10},{12,13},{15,14},{16,17},{19,... | collective-permute-start | bytes 1966088 | tf_op jit(solution)/shard_map/ppermute | solution.py:441
  126.9 43.5 %collective-permute-start.27 = (bf16[128,2560]{1,0:T(8,128)(2,1)S(1)}, bf16[128,2560]{1,0:T(8,128)(2,1)S(1)}, u32[]{:S(2)}, u32[]{:S(2)}) collective-permute-start(bf16[128,2560]{1,0:T(8,128)(2,1)S(1)} %added.8), channel_id=1, source_target_pairs={{1,2},{2,1},{5,6},{6,5},{9,10},{10,9},{13,14},{14,13},{17,18},{18,... | collective-permute-start | bytes 1966088 | tf_op jit(solution)/shard_map/ppermute | solution.py:435
  134.5 37.3 %collective-permute-start.28 = (bf16[128,2560]{1,0:T(8,128)(2,1)S(1)}, bf16[128,2560]{1,0:T(8,128)(2,1)S(1)}, u32[]{:S(2)}, u32[]{:S(2)}) collective-permute-start(bf16[128,2560]{1,0:T(8,128)(2,1)S(1)} %added.9), channel_id=1, source_target_pairs={{1,2},{2,1},{5,6},{6,5},{9,10},{10,9},{13,14},{14,13},{17,18},{18,... | collective-permute-start | bytes 1966088 | tf_op jit(solution)/shard_map/ppermute | solution.py:435
  135.2 42.2 %collective-permute-start.29 = (bf16[128,2560]{1,0:T(8,128)(2,1)S(1)}, bf16[128,2560]{1,0:T(8,128)(2,1)S(1)}, u32[]{:S(2)}, u32[]{:S(2)}) collective-permute-start(bf16[128,2560]{1,0:T(8,128)(2,1)S(1)} %mix.10.refs_0_), channel_id=1, source_target_pairs={{0,1},{3,2},{4,5},{7,6},{8,9},{11,10},{12,13},{15,14},{16,17},{19,... | collective-permute-start | bytes 1966088 | tf_op jit(solution)/shard_map/ppermute | solution.py:441
  141.9 20.7 %collective-permute-start.25 = (bf16[128,1024]{1,0:T(8,128)(2,1)S(1)}, bf16[128,1024]{1,0:T(8,128)(2,1)S(1)}, u32[]{:S(2)}, u32[]{:S(2)}) collective-permute-start(bf16[128,1024]{1,0:T(8,128)(2,1)S(1)} %attention.4.rows_ref), channel_id=1, source_target_pairs={{0,1},{3,2},{4,5},{7,6},{8,9},{11,10},{12,13},{15,14},{16,17},{19,... | collective-permute-start | bytes 786440 | tf_op jit(solution)/shard_map/ppermute | solution.py:441
  143.2 41.0 %collective-permute-start.33 = (bf16[128,1024]{1,0:T(8,128)(2,1)S(1)}, bf16[128,1024]{1,0:T(8,128)(2,1)S(1)}, u32[]{:S(2)}, u32[]{:S(2)}) collective-permute-start(bf16[128,1024]{1,0:T(8,128)(2,1)S(1)} %get-tuple-element.92.rows_ref), channel_id=1, source_target_pairs={{0,1},{3,2},{4,5},{7,6},{8,9},{11,10},{12,13},{15,14},{16,17},{19,... | collective-permute-start | bytes 786440 | tf_op jit(solution)/shard_map/ppermute | solution.py:441
  169.6 18.0 %collective-permute-start.35 = (bf16[128,2560]{1,0:T(8,128)(2,1)S(1)}, bf16[128,2560]{1,0:T(8,128)(2,1)S(1)}, u32[]{:S(2)}, u32[]{:S(2)}) collective-permute-start(bf16[128,2560]{1,0:T(8,128)(2,1)S(1)} %added.10), channel_id=1, source_target_pairs={{1,2},{2,1},{5,6},{6,5},{9,10},{10,9},{13,14},{14,13},{17,18},{18,... | collective-permute-start | bytes 1966088 | tf_op jit(solution)/shard_map/ppermute | solution.py:435
  170.5 21.5 %collective-permute-start.34 = (bf16[128,2560]{1,0:T(8,128)(2,1)S(1)}, bf16[128,2560]{1,0:T(8,128)(2,1)S(1)}, u32[]{:S(2)}, u32[]{:S(2)}) collective-permute-start(bf16[128,2560]{1,0:T(8,128)(2,1)S(1)} %added.11), channel_id=1, source_target_pairs={{1,0},{2,3},{5,4},{6,7},{9,8},{10,11},{13,12},{14,15},{17,16},{18,... | collective-permute-start | bytes 1966088 | tf_op jit(solution)/shard_map/ppermute | solution.py:438
  176.1 25.5 %collective-permute-start.31 = (bf16[128,2560]{1,0:T(8,128)(2,1)S(1)}, bf16[128,2560]{1,0:T(8,128)(2,1)S(1)}, u32[]{:S(2)}, u32[]{:S(2)}) collective-permute-start(bf16[128,2560]{1,0:T(8,128)(2,1)S(1)} %added.12), channel_id=1, source_target_pairs={{1,0},{2,3},{5,4},{6,7},{9,8},{10,11},{13,12},{14,15},{17,16},{18,... | collective-permute-start | bytes 1966088 | tf_op jit(solution)/shard_map/ppermute | solution.py:438
  177.6 17.1 %collective-permute-start.30 = (bf16[128,2560]{1,0:T(8,128)(2,1)S(1)}, bf16[128,2560]{1,0:T(8,128)(2,1)S(1)}, u32[]{:S(2)}, u32[]{:S(2)}) collective-permute-start(bf16[128,2560]{1,0:T(8,128)(2,1)S(1)} %mix.13.refs_0_), channel_id=1, source_target_pairs={{0,1},{3,2},{4,5},{7,6},{8,9},{11,10},{12,13},{15,14},{16,17},{19,... | collective-permute-start | bytes 1966088 | tf_op jit(solution)/shard_map/ppermute | solution.py:441
  184.3 17.4 %collective-permute-start.32 = (bf16[128,2560]{1,0:T(8,128)(2,1)S(1)}, bf16[128,2560]{1,0:T(8,128)(2,1)S(1)}, u32[]{:S(2)}, u32[]{:S(2)}) collective-permute-start(bf16[128,2560]{1,0:T(8,128)(2,1)S(1)} %added.13), channel_id=1, source_target_pairs={{1,2},{2,1},{5,6},{6,5},{9,10},{10,9},{13,14},{14,13},{17,18},{18,... | collective-permute-start | bytes 1966088 | tf_op jit(solution)/shard_map/ppermute | solution.py:435

commit v10 on v9

--- a/solution.py
+++ b/solution.py
@@ -524,17 +524,17 @@
     far_sent = after(far_sent, third_rows)
     far_in = inward(after(far[0], far_sent))
     far_right = added(far[1], share_of(far_sent))
-    third = mixed(after(third_rows, far_right))
+    places = after(places, far_right)
+    near_rows, own_rows = attend((NEAR, OWN))
+    third = mixed(after(third_rows, near_rows))
     third_sent = send(third_rows, third[1])
     far_right = across(far_right)
-    places = after(places, third)
-    near_rows, own_rows = attend((NEAR, OWN))
-    far_left = added(far[0], after(far_in, near_rows))
+    far_left = added(far[0], after(far_in, third))
     third_sent = after(third_sent, far_left)
     far_left = across(far_left)
-    third_in = inward(third[0])
+    third_in = inward(after(third[0], third_sent))
     third_right = added(third[1], share_of(third_sent))
-    near = mixed(after(near_rows, third_right))
+    near = mixed(after(near_rows, (third_right, far_right)))
     near_sent = send(near_rows, near[1])
     third_right = across(third_right)
     out_right = added(near[1], after(far_right, near))

time: 204 us -> 187 us (0.917)
  waiting for transfers between devices: 67.3 us -> 55.3 us
  starting transfers between devices: 61.3 us -> 57 us
    ppermute x8, waiting for transfers between devices: 24.5 us -> 12.4 us  [inward(): return lax.ppermute(array, 'tensor', [(0, 1), (3, 2)])]
    ppermute x8, starting transfers between devices: 33.7 us -> 29.4 us  [inward(): return lax.ppermute(array, 'tensor', [(0, 1), (3, 2)])]
  transfers between devices with their start and end apart: 36 -> 36, of which waited for: 12 -> 12; matrix products, arithmetic and copies ran while one was open for 0% -> 0% of each run, Pallas kernels for 27% -> 30%
where the time goes in v10:
time: 187 us
  Pallas kernels  61.8 us (33%)
  starting transfers between devices  57 us (30%)
  waiting for transfers between devices  55.3 us (30%)
  local copies, waits for them, and re-layouts  11.1 us (6%)
    ppermute x6, waiting for transfers between devices, outward(): return lax.ppermute(array, 'tensor', [(1, 0), (2, 3)])  29.9 us
    ppermute x8, starting transfers between devices, inward(): return lax.ppermute(array, 'tensor', [(0, 1), (3, 2)])  29.4 us
    pallas_call x8, Pallas kernels, mix(): pl.pallas_call(mix_kernel, grid=(tiles,), in_specs=[whole(rows, depth), p...  16.5 us
    pallas_call x3, Pallas kernels, attention(): pl.pallas_call(functools.partial(attention_kernel, slots, n_parts, len(ot...  12.7 us
    ppermute x8, waiting for transfers between devices, inward(): return lax.ppermute(array, 'tensor', [(0, 1), (3, 2)])  12.4 us
    pallas_call x3, Pallas kernels, partial_projection(): pl.pallas_call(functools.partial(partial_kernel, [len(part) for part in p...  11.8 us
    ppermute x1, waiting for transfers between devices, swap(): return lax.ppermute(array, 'tensor', [(0, 1), (1, 0), (2, 3), (3, 2)])  11.1 us
    unnamed x36, local copies, waits for them, and re-layouts  11 us
  transfers between devices with their start and end apart: 36, of which 12 were waited for; matrix products, arithmetic and copies ran while one was open for 0% of the time, Pallas kernels for 30%

profile of v10, /device:TPU:0, one launch (start us, length us, event | category | flops | bytes accessed | tf_op | source)
XLA Modules:
  0.0 186.6 jit_solution(18094846706248478834)
XLA Ops:
  0.0 3.0 %collective-permute-start = (bf16[512,1280]{1,0:T(8,128)(2,1)}, bf16[512,1280]{1,0:T(8,128)(2,1)S(1)}, u32[]{:S(2)}, u32[]{:S(2)}) collective-permute-start(bf16[512,1280]{1,0:T(8,128)(2,1)} %refs_0_.1), channel_id=1, source_target_pairs={{0,1},{1,0},{2,3},{3,2},{4,5},{5,4},{6,7},{7,6},{8,9},{9,8},{10,11... | collective-permute-start | bytes 3932168 | tf_op jit(solution)/shard_map/ppermute | solution.py:432
  3.0 1.3 copy-done.4
  4.4 0.9 halves.3
  5.3 1.5 collective-permute-start.3
  6.8 1.5 collective-permute-start.5
  8.4 4.0 %copy-done.1 = bf16[5120,1024]{1,0:T(8,128)(2,1)S(1)} copy-done((bf16[5120,1024]{1,0:T(8,128)(2,1)S(1)}, bf16[5120,1024]{1,0:T(8,128)(2,1)}, u32[]{:S(2)}) %copy-start.1) | copy-done | bytes 10485784
  12.4 1.3 copy-done.3
  13.7 1.3 copy-done.5
  15.0 3.4 %partial_projection.3 = (f32[512,1024]{1,0:T(8,128)S(1)}, f32[512,128]{1,0:T(8,128)S(1)}, f32[512,128]{1,0:T(8,128)S(1)}) custom-call(s32[12]{0:T(128)S(1)} %stack.51.places_ref, bf16[512,1280]{1,0:T(8,128)(2,1)S(1)} %copy-done.5, bf16[5120,1024]{1,0:T(8,128)(2,1)S(1)} %copy-done.1, bf16[5120,128]{1,0:T(8,128)(2,1)S(1)} %copy-done.2, ...), custom_call_target="tpu_custom_call" | custom-call | flops 1 | bytes 1 | tf_op jit(solution)/shard_map/partial_projection/pallas_call | solution.py:96
  18.5 1.3 collective-permute-start.4
  20.4 1.3 collective-permute-start.7
  21.7 11.1 %collective-permute-done.ref.refs_0_ = bf16[512,1280]{1,0:T(8,128)(2,1)S(1)} collective-permute-done((bf16[512,1280]{1,0:T(8,128)(2,1)}, bf16[512,1280]{1,0:T(8,128)(2,1)S(1)}, u32[]{:S(2)}, u32[]{:S(2)}) %collective-permute-start) | collective-permute-done | bytes 1310752 | tf_op jit(solution)/shard_map/ppermute | solution.py:432
  33.7 3.6 %partial_projection.4 = (f32[512,1024]{1,0:T(8,128)S(1)}, f32[512,128]{1,0:T(8,128)S(1)}, f32[512,128]{1,0:T(8,128)S(1)}) custom-call(s32[12]{0:T(128)S(1)} %stack.51.places_ref, bf16[512,1280]{1,0:T(8,128)(2,1)S(1)} %collective-permute-done.ref.refs_0_, bf16[5120,1024]{1,0:T(8,128)(2,1)S(1)} %copy-done.1, bf16[5120,128]{1,0:T(8,128)(2,1)S(1)} %copy-done.2, ...), custom_call_target="tpu_custom_call" | custom-call | flops 1 | bytes 1 | tf_op jit(solution)/shard_map/partial_projection/pallas_call | solution.py:96
  37.3 9.6 %collective-permute-done.4.refs_1_ = bf16[256,1280]{1,0:T(8,128)(2,1)S(1)} collective-permute-done((bf16[256,1280]{1,0:T(8,128)(2,1)}, bf16[256,1280]{1,0:T(8,128)(2,1)S(1)}, u32[]{:S(2)}, u32[]{:S(2)}) %collective-permute-start.4) | collective-permute-done | bytes 655392 | tf_op jit(solution)/shard_map/ppermute | solution.py:438
  47.7 6.1 %collective-permute-start.9 = (bf16[128,2560]{1,0:T(8,128)(2,1)S(1)}, bf16[128,2560]{1,0:T(8,128)(2,1)S(1)}, u32[]{:S(2)}, u32[]{:S(2)}) collective-permute-start(bf16[128,2560]{1,0:T(8,128)(2,1)S(1)} %eighth.2), channel_id=1, source_target_pairs={{0,1},{3,2},{4,5},{7,6},{8,9},{11,10},{12,13},{15,14},{16,17},{19,... | collective-permute-start | bytes 1966088 | tf_op jit(solution)/shard_map/ppermute | solution.py:441
  53.9 1.3 collective-permute-start.2
  55.8 5.1 %collective-permute-done.7.refs_3_ = bf16[256,1280]{1,0:T(8,128)(2,1)S(1)} collective-permute-done((bf16[256,1280]{1,0:T(8,128)(2,1)}, bf16[256,1280]{1,0:T(8,128)(2,1)S(1)}, u32[]{:S(2)}, u32[]{:S(2)}) %collective-permute-start.7) | collective-permute-done | bytes 655392 | tf_op jit(solution)/shard_map/ppermute | solution.py:438
  60.9 0.8 copy-done.10
  61.8 3.7 %collective-permute-done.9.refs_0_ = bf16[128,2560]{1,0:T(8,128)(2,1)S(1)} collective-permute-done((bf16[128,2560]{1,0:T(8,128)(2,1)S(1)}, bf16[128,2560]{1,0:T(8,128)(2,1)S(1)}, u32[]{:S(2)}, u32[]{:S(2)}) %collective-permute-start.9) | collective-permute-done | bytes 655392 | tf_op jit(solution)/shard_map/ppermute | solution.py:441
  65.5 1.5 collective-permute-start.10
  67.0 1.5 collective-permute-start.11
  68.5 8.6 %collective-permute-start.12 = (bf16[128,2560]{1,0:T(8,128)(2,1)S(1)}, bf16[128,2560]{1,0:T(8,128)(2,1)S(1)}, u32[]{:S(2)}, u32[]{:S(2)}) collective-permute-start(bf16[128,2560]{1,0:T(8,128)(2,1)S(1)} %eighth.3), channel_id=1, source_target_pairs={{0,1},{3,2},{4,5},{7,6},{8,9},{11,10},{12,13},{15,14},{16,17},{19,... | collective-permute-start | bytes 1966088 | tf_op jit(solution)/shard_map/ppermute | solution.py:441
  77.1 1.3 collective-permute-start.8
  78.4 1.1 copy-done.9
  79.5 1.1 copy-done.11
  80.6 4.8 %partial_projection.5 = (f32[512,1024]{1,0:T(8,128)S(1)}, f32[512,128]{1,0:T(8,128)S(1)}, f32[512,128]{1,0:T(8,128)S(1)}) custom-call(s32[12]{0:T(128)S(1)} %stack.51.places_ref, bf16[256,1280]{1,0:T(8,128)(2,1)} %collective-permute-done.3.refs_0_, bf16[256,1280]{1,0:T(8,128)(2,1)S(1)} %copy-done.9, bf16[256,1280]{1,0:T(8,128)(2,1)} %collective-permute-done.5.refs_2_, ...), custom_call_target="tpu_custom_call" | custom-call | flops 1 | bytes 1 | tf_op jit(solution)/shard_map/partial_projection/pallas_call | solution.py:96
  85.4 2.5 %queries.2.refs_0_ = bf16[256,1024]{1,0:T(8,128)(2,1)S(1)} custom-call(s32[12]{0:T(128)S(1)} %stack.51.places_ref, bf16[256,1280]{1,0:T(8,128)(2,1)S(1)} %collective-permute-done.1.refs_0_, bf16[256,1280]{1,0:T(8,128)(2,1)S(1)} %collective-permute-done.2.refs_1_, bf16[5120,1024]{1,0:T(8,128)(2,1)S(1)} %bitcast.15, ...), custom_call_target="tpu_custom_call" | custom-call | flops 1 | bytes 1 | tf_op jit(solution)/shard_map/queries/pallas_call | solution.py:183
  87.9 1.1 keys_values.2.refs_0_.refs_2_
  89.0 3.8 %collective-permute-done.8.refs_1_.refs_2_ = bf16[256,1280]{1,0:T(8,128)(2,1)S(1)} collective-permute-done((bf16[256,1280]{1,0:T(8,128)(2,1)S(1)}, bf16[256,1280]{1,0:T(8,128)(2,1)S(1)}, u32[]{:S(2)}, u32[]{:S(2)}) %collective-permute-start.8) | collective-permute-done | bytes 655392 | tf_op jit(solution)/shard_map/ppermute | solution.py:438
  92.8 1.3 keys_values.3
  94.8 1.3 collective-permute-start.15
  96.6 1.2 collective-permute-start.17
  98.2 0.9 collective-permute-done.14.refs_5_
  99.2 1.3 collective-permute-start.19
  101.1 2.5 %queries.3.refs_1_ = bf16[256,1024]{1,0:T(8,128)(2,1)S(1)} custom-call(s32[12]{0:T(128)S(1)} %stack.51.places_ref, bf16[256,1280]{1,0:T(8,128)(2,1)S(1)} %collective-permute-done.6.refs_0_.refs_1_, bf16[256,1280]{1,0:T(8,128)(2,1)S(1)} %collective-permute-done.8.refs_1_.refs_2_, bf16[5120,1024]{1,0:T(8,128)(2,1)S(1)} %bitcast.15, ...), custom_call_target="tpu_custom_call" | custom-call | flops 1 | bytes 1 | tf_op jit(solution)/shard_map/queries/pallas_call | solution.py:183
  103.7 0.8 collective-permute-done.19.refs_10_
  104.5 3.6 %attention.3.rows_ref = bf16[128,1024]{1,0:T(8,128)(2,1)S(1)} custom-call(s32[12]{0:T(128)S(1)} %stack.51.places_ref, s32[1]{0:T(128)S(6)} %copy.14.length_ref, bf16[256,1024]{1,0:T(8,128)(2,1)S(1)} %queries.2.refs_0_, bf16[256,1024]{1,0:T(8,128)(2,1)S(1)} %queries.3.refs_1_, bf16[256,256]{1,0:T(8,128)(2,1)S(1)} %keys_values.2.refs_0_.refs_2_, ...), custom_call_target="tpu_custom_call" | custom-call | flops 1 | bytes 1 | tf_op jit(solution)/shard_map/attention/pallas_call | solution.py:272
  108.1 1.6 collective-permute-start.20
  110.8 2.1 %mix.8.refs_0_ = bf16[128,2560]{1,0:T(8,128)(2,1)S(1)} custom-call(bf16[128,1024]{1,0:T(8,128)(2,1)S(1)} %attention.3.rows_ref, bf16[1024,5120]{1,0:T(8,128)(2,1)S(1)} %copy-done), custom_call_target="tpu_custom_call" | custom-call | flops 1 | bytes 1 | tf_op jit(solution)/shard_map/mix/pallas_call | solution.py:301
  112.9 2.1 %mix.9.refs_0_ = bf16[128,2560]{1,0:T(8,128)(2,1)S(1)} custom-call(bf16[128,1024]{1,0:T(8,128)(2,1)S(1)} %attention.3.rows_ref, bf16[1024,5120]{1,0:T(8,128)(2,1)S(1)} %copy-done), custom_call_target="tpu_custom_call" | custom-call | flops 1 | bytes 1 | tf_op jit(solution)/shard_map/mix/pallas_call | solution.py:301
  114.9 3.6 %attention.4.rows_ref = bf16[128,1024]{1,0:T(8,128)(2,1)S(1)} custom-call(s32[12]{0:T(128)S(1)} %stack.51.places_ref, s32[1]{0:T(128)S(6)} %copy.14.length_ref, bf16[256,1024]{1,0:T(8,128)(2,1)S(1)} %queries.2.refs_0_, bf16[256,1024]{1,0:T(8,128)(2,1)S(1)} %queries.3.refs_1_, bf16[256,256]{1,0:T(8,128)(2,1)S(1)} %keys_values.2.refs_0_.refs_2_, ...), custom_call_target="tpu_custom_call" | custom-call | flops 1 | bytes 1 | tf_op jit(solution)/shard_map/attention/pallas_call | solution.py:272
  118.5 1.3 collective-permute-start.26
  119.9 1.3 collective-permute-start.25
  121.2 2.7 %mix_sent.3.refs_1_ = bf16[128,2560]{1,0:T(8,128)(2,1)S(1)} custom-call(s32[12]{0:T(128)S(1)} %stack.51.places_ref, bf16[128,1024]{1,0:T(8,128)(2,1)S(1)} %collective-permute-done.20.rows_ref, bf16[128,2560]{1,0:T(8,128)(2,1)S(1)} %collective-permute-done.9.refs_0_, bf16[128,2560]{1,0:T(8,128)(2,1)S(1)} %collective-permute-done.12.refs_1_, ...), custom_call_target="tpu_custom_call" | custom-call | flops 1 | bytes 1 | tf_op jit(solution)/shard_map/mix_sent/pallas_call | solution.py:357
  124.8 5.6 %attention.5 = (bf16[128,1024]{1,0:T(8,128)(2,1)S(1)}, bf16[128,1024]{1,0:T(8,128)(2,1)S(1)}) custom-call(s32[12]{0:T(128)S(1)} %stack.51.places_ref, s32[1]{0:T(128)S(6)} %copy.14.length_ref, bf16[256,1024]{1,0:T(8,128)(2,1)S(1)} %queries.2.refs_0_, bf16[256,1024]{1,0:T(8,128)(2,1)S(1)} %queries.3.refs_1_, bf16[256,256]{1,0:T(8,128)(2,1)S(1)} %keys_values.2.refs_0_.refs_2_, ...), custom_call_target="tpu_custom_call" | custom-call | flops 1 | bytes 1 | tf_op jit(solution)/shard_map/attention/pallas_call | solution.py:272
  130.4 2.1 %mix.10.refs_0_ = bf16[128,2560]{1,0:T(8,128)(2,1)S(1)} custom-call(bf16[128,1024]{1,0:T(8,128)(2,1)S(1)} %attention.4.rows_ref, bf16[1024,5120]{1,0:T(8,128)(2,1)S(1)} %copy-done), custom_call_target="tpu_custom_call" | custom-call | flops 1 | bytes 1 | tf_op jit(solution)/shard_map/mix/pallas_call | solution.py:301
  132.4 2.1 %mix.11.refs_0_ = bf16[128,2560]{1,0:T(8,128)(2,1)S(1)} custom-call(bf16[128,1024]{1,0:T(8,128)(2,1)S(1)} %attention.4.rows_ref, bf16[1024,5120]{1,0:T(8,128)(2,1)S(1)} %copy-done), custom_call_target="tpu_custom_call" | custom-call | flops 1 | bytes 1 | tf_op jit(solution)/shard_map/mix/pallas_call | solution.py:301
  135.7 4.2 %collective-permute-done.25.rows_ref = bf16[128,1024]{1,0:T(8,128)(2,1)S(1)} collective-permute-done((bf16[128,1024]{1,0:T(8,128)(2,1)S(1)}, bf16[128,1024]{1,0:T(8,128)(2,1)S(1)}, u32[]{:S(2)}, u32[]{:S(2)}) %collective-permute-start.25) | collective-permute-done | bytes 262176 | tf_op jit(solution)/shard_map/ppermute | solution.py:441
  139.9 4.4 %collective-permute-start.29 = (bf16[128,2560]{1,0:T(8,128)(2,1)S(1)}, bf16[128,2560]{1,0:T(8,128)(2,1)S(1)}, u32[]{:S(2)}, u32[]{:S(2)}) collective-permute-start(bf16[128,2560]{1,0:T(8,128)(2,1)S(1)} %mix.11.refs_0_), channel_id=1, source_target_pairs={{0,1},{3,2},{4,5},{7,6},{8,9},{11,10},{12,13},{15,14},{16,17},{19,... | collective-permute-start | bytes 1966088 | tf_op jit(solution)/shard_map/ppermute | solution.py:441
  144.4 1.3 collective-permute-start.33
  145.7 2.7 %mix_sent.4.refs_1_ = bf16[128,2560]{1,0:T(8,128)(2,1)S(1)} custom-call(s32[12]{0:T(128)S(1)} %stack.51.places_ref, bf16[128,1024]{1,0:T(8,128)(2,1)S(1)} %collective-permute-done.25.rows_ref, bf16[128,2560]{1,0:T(8,128)(2,1)S(1)} %collective-permute-done.9.refs_0_, bf16[128,2560]{1,0:T(8,128)(2,1)S(1)} %collective-permute-done.12.refs_1_, ...), custom_call_target="tpu_custom_call" | custom-call | flops 1 | bytes 1 | tf_op jit(solution)/shard_map/mix_sent/pallas_call | solution.py:357
  149.2 2.1 %mix.12.refs_0_ = bf16[128,2560]{1,0:T(8,128)(2,1)S(1)} custom-call(bf16[128,1024]{1,0:T(8,128)(2,1)S(1)} %get-tuple-element.93.rows_ref, bf16[1024,5120]{1,0:T(8,128)(2,1)S(1)} %copy-done), custom_call_target="tpu_custom_call" | custom-call | flops 1 | bytes 1 | tf_op jit(solution)/shard_map/mix/pallas_call | solution.py:301
  151.3 2.1 %mix.13.refs_0_ = bf16[128,2560]{1,0:T(8,128)(2,1)S(1)} custom-call(bf16[128,1024]{1,0:T(8,128)(2,1)S(1)} %get-tuple-element.93.rows_ref, bf16[1024,5120]{1,0:T(8,128)(2,1)S(1)} %copy-done), custom_call_target="tpu_custom_call" | custom-call | flops 1 | bytes 1 | tf_op jit(solution)/shard_map/mix/pallas_call | solution.py:301
  153.5 1.3 collective-permute-start.34
  154.8 2.1 %mix.14.refs_0_ = bf16[128,2560]{1,0:T(8,128)(2,1)S(1)} custom-call(bf16[128,1024]{1,0:T(8,128)(2,1)S(1)} %get-tuple-element.95.rows_ref, bf16[1024,5120]{1,0:T(8,128)(2,1)S(1)} %copy-done), custom_call_target="tpu_custom_call" | custom-call | flops 1 | bytes 1 | tf_op jit(solution)/shard_map/mix/pallas_call | solution.py:301
  156.9 2.1 %mix.15.refs_0_ = bf16[128,2560]{1,0:T(8,128)(2,1)S(1)} custom-call(bf16[128,1024]{1,0:T(8,128)(2,1)S(1)} %get-tuple-element.95.rows_ref, bf16[1024,5120]{1,0:T(8,128)(2,1)S(1)} %copy-done), custom_call_target="tpu_custom_call" | custom-call | flops 1 | bytes 1 | tf_op jit(solution)/shard_map/mix/pallas_call | solution.py:301
  159.1 1.3 collective-permute-start.31
  160.6 4.7 %collective-permute-start.30 = (bf16[128,2560]{1,0:T(8,128)(2,1)S(1)}, bf16[128,2560]{1,0:T(8,128)(2,1)S(1)}, u32[]{:S(2)}, u32[]{:S(2)}) collective-permute-start(bf16[128,2560]{1,0:T(8,128)(2,1)S(1)} %mix.13.refs_0_), channel_id=1, source_target_pairs={{0,1},{3,2},{4,5},{7,6},{8,9},{11,10},{12,13},{15,14},{16,17},{19,... | collective-permute-start | bytes 1966088 | tf_op jit(solution)/shard_map/ppermute | solution.py:441
  166.0 2.7 %mix_sent.5.refs_1_ = bf16[128,2560]{1,0:T(8,128)(2,1)S(1)} custom-call(s32[12]{0:T(128)S(1)} %stack.51.places_ref, bf16[128,1024]{1,0:T(8,128)(2,1)S(1)} %collective-permute-done.33.rows_ref, bf16[128,2560]{1,0:T(8,128)(2,1)S(1)} %collective-permute-done.9.refs_0_, bf16[128,2560]{1,0:T(8,128)(2,1)S(1)} %collective-permute-done.12.refs_1_, ...), custom_call_target="tpu_custom_call" | custom-call | flops 1 | bytes 1 | tf_op jit(solution)/shard_map/mix_sent/pallas_call | solution.py:357
  168.7 4.4 %collective-permute-done.34.refs_2_ = bf16[128,2560]{1,0:T(8,128)(2,1)S(1)} collective-permute-done((bf16[128,2560]{1,0:T(8,128)(2,1)S(1)}, bf16[128,2560]{1,0:T(8,128)(2,1)S(1)}, u32[]{:S(2)}, u32[]{:S(2)}) %collective-permute-start.34) | collective-permute-done | bytes 655392 | tf_op jit(solution)/shard_map/ppermute | solution.py:438
  173.1 1.2 added.14.refs_4_
  174.3 4.1 %collective-permute-done.30.refs_1_ = bf16[128,2560]{1,0:T(8,128)(2,1)S(1)} collective-permute-done((bf16[128,2560]{1,0:T(8,128)(2,1)S(1)}, bf16[128,2560]{1,0:T(8,128)(2,1)S(1)}, u32[]{:S(2)}, u32[]{:S(2)}) %collective-permute-start.30) | collective-permute-done | bytes 655392 | tf_op jit(solution)/shard_map/ppermute | solution.py:441
  178.4 7.0 %collective-permute-done.31.refs_2_ = bf16[128,2560]{1,0:T(8,128)(2,1)S(1)} collective-permute-done((bf16[128,2560]{1,0:T(8,128)(2,1)S(1)}, bf16[128,2560]{1,0:T(8,128)(2,1)S(1)}, u32[]{:S(2)}, u32[]{:S(2)}) %collective-permute-start.31) | collective-permute-done | bytes 655392 | tf_op jit(solution)/shard_map/ppermute | solution.py:438
  185.4 1.2 added.15
  (79 shorter events, 9.8 us)
Async XLA Ops:
  0.0 8.4 %copy-start.2 = (bf16[5120,128]{1,0:T(8,128)(2,1)S(1)}, bf16[5120,128]{1,0:T(8,128)(2,1)}, u32[]{:S(2)}) copy-start(bf16[5120,128]{1,0:T(8,128)(2,1)} %refs_3_.7) | copy-start | bytes 3932164
  0.0 32.8 %collective-permute-start = (bf16[512,1280]{1,0:T(8,128)(2,1)}, bf16[512,1280]{1,0:T(8,128)(2,1)S(1)}, u32[]{:S(2)}, u32[]{:S(2)}) collective-permute-start(bf16[512,1280]{1,0:T(8,128)(2,1)} %refs_0_.1), channel_id=1, source_target_pairs={{0,1},{1,0},{2,3},{3,2},{4,5},{5,4},{6,7},{7,6},{8,9},{9,8},{10,11... | collective-permute-start | bytes 3932168 | tf_op jit(solution)/shard_map/ppermute | solution.py:432
  3.0 1.4 copy-start.4
  5.3 13.2 %collective-permute-start.3 = (bf16[256,1280]{1,0:T(8,128)(2,1)}, bf16[256,1280]{1,0:T(8,128)(2,1)}, u32[]{:S(2)}, u32[]{:S(2)}) collective-permute-start(bf16[256,1280]{1,0:T(8,128)(2,1)} %get-tuple-element.55), channel_id=1, source_target_pairs={{1,2},{2,1},{5,6},{6,5},{9,10},{10,9},{13,14},{14,13},{17,18},{18,... | collective-permute-start | bytes 1966088 | tf_op jit(solution)/shard_map/ppermute | solution.py:435
  6.8 13.6 %collective-permute-start.5 = (bf16[256,1280]{1,0:T(8,128)(2,1)S(1)}, bf16[256,1280]{1,0:T(8,128)(2,1)}, u32[]{:S(2)}, u32[]{:S(2)}) collective-permute-start(bf16[256,1280]{1,0:T(8,128)(2,1)S(1)} %get-tuple-element.60), channel_id=1, source_target_pairs={{1,2},{2,1},{5,6},{6,5},{9,10},{10,9},{13,14},{14,13},{17,18},{18,... | collective-permute-start | bytes 1966088 | tf_op jit(solution)/shard_map/ppermute | solution.py:435
  8.4 4.0 %copy-start.1 = (bf16[5120,1024]{1,0:T(8,128)(2,1)S(1)}, bf16[5120,1024]{1,0:T(8,128)(2,1)}, u32[]{:S(2)}) copy-start(bf16[5120,1024]{1,0:T(8,128)(2,1)} %refs_2_.8) | copy-start | bytes 31457284
  12.4 1.3 copy-start.3
  13.7 1.3 copy-start.5
  15.0 4.8 %copy-start = (bf16[1024,5120]{1,0:T(8,128)(2,1)S(1)}, bf16[1024,5120]{1,0:T(8,128)(2,1)}, u32[]{:S(2)}) copy-start(bf16[1024,5120]{1,0:T(8,128)(2,1)} %w_ref.19) | copy-start | bytes 31457284
  18.5 28.4 %collective-permute-start.4 = (bf16[256,1280]{1,0:T(8,128)(2,1)}, bf16[256,1280]{1,0:T(8,128)(2,1)S(1)}, u32[]{:S(2)}, u32[]{:S(2)}) collective-permute-start(bf16[256,1280]{1,0:T(8,128)(2,1)} %collective-permute-done.3.refs_0_), channel_id=1, source_target_pairs={{1,0},{2,3},{5,4},{6,7},{9,8},{10,11},{13,12},{14,15},{17,16},{18,... | collective-permute-start | bytes 1966088 | tf_op jit(solution)/shard_map/ppermute | solution.py:438
  20.4 40.5 %collective-permute-start.7 = (bf16[256,1280]{1,0:T(8,128)(2,1)}, bf16[256,1280]{1,0:T(8,128)(2,1)S(1)}, u32[]{:S(2)}, u32[]{:S(2)}) collective-permute-start(bf16[256,1280]{1,0:T(8,128)(2,1)} %collective-permute-done.5.refs_2_), channel_id=1, source_target_pairs={{1,0},{2,3},{5,4},{6,7},{9,8},{10,11},{13,12},{14,15},{17,16},{18,... | collective-permute-start | bytes 1966088 | tf_op jit(solution)/shard_map/ppermute | solution.py:438
  32.9 20.9 %collective-permute-start.1 = (bf16[256,1280]{1,0:T(8,128)(2,1)S(1)}, bf16[256,1280]{1,0:T(8,128)(2,1)S(1)}, u32[]{:S(2)}, u32[]{:S(2)}) collective-permute-start(bf16[256,1280]{1,0:T(8,128)(2,1)S(1)} %get-tuple-element.53), channel_id=1, source_target_pairs={{1,2},{2,1},{5,6},{6,5},{9,10},{10,9},{13,14},{14,13},{17,18},{18,... | collective-permute-start | bytes 1966088 | tf_op jit(solution)/shard_map/ppermute | solution.py:435
  33.6 44.7 %slice-start = ((s8[10485760]{0:T(1024)(128)(4,1)}), s8[4194304]{0:T(1024)(128)(4,1)S(1)}, s32[]{:S(2)}) async-start(s8[10485760]{0:T(1024)(128)(4,1)} %bitcast.14), calls=%async_computation | async-start | bytes 8388608
  33.7 44.7 %slice-start.1 = ((s8[10485760]{0:T(1024)(128)(4,1)}), s8[4194304]{0:T(1024)(128)(4,1)S(1)}, s32[]{:S(2)}) async-start(s8[10485760]{0:T(1024)(128)(4,1)} %bitcast.14), calls=%async_computation.1 | async-start | bytes 8388608
  46.9 8.9 %copy-start.8 = (bf16[256,1280]{1,0:T(8,128)(2,1)}, bf16[256,1280]{1,0:T(8,128)(2,1)S(1)}, u32[]{:S(2)}) copy-start(bf16[256,1280]{1,0:T(8,128)(2,1)S(1)} %collective-permute-done.4.refs_1_) | copy-start | bytes 1966084
  46.9 31.5 %slice-start.2 = ((s8[10485760]{0:T(1024)(128)(4,1)}), s8[2097152]{0:T(1024)(128)(4,1)S(1)}, s32[]{:S(2)}) async-start(s8[10485760]{0:T(1024)(128)(4,1)} %bitcast.14), calls=%async_computation.2 | async-start | bytes 4194304
  46.9 14.9 %collective-permute-start.6 = (bf16[256,1280]{1,0:T(8,128)(2,1)S(1)}, bf16[256,1280]{1,0:T(8,128)(2,1)S(1)}, u32[]{:S(2)}, u32[]{:S(2)}) collective-permute-start(bf16[256,1280]{1,0:T(8,128)(2,1)S(1)} %get-tuple-element.68), channel_id=1, source_target_pairs={{1,2},{2,1},{5,6},{6,5},{9,10},{10,9},{13,14},{14,13},{17,18},{18,... | collective-permute-start | bytes 1966088 | tf_op jit(solution)/shard_map/ppermute | solution.py:435
  47.7 17.8 %collective-permute-start.9 = (bf16[128,2560]{1,0:T(8,128)(2,1)S(1)}, bf16[128,2560]{1,0:T(8,128)(2,1)S(1)}, u32[]{:S(2)}, u32[]{:S(2)}) collective-permute-start(bf16[128,2560]{1,0:T(8,128)(2,1)S(1)} %eighth.2), channel_id=1, source_target_pairs={{0,1},{3,2},{4,5},{7,6},{8,9},{11,10},{12,13},{15,14},{16,17},{19,... | collective-permute-start | bytes 1966088 | tf_op jit(solution)/shard_map/ppermute | solution.py:441
  53.9 31.5 %collective-permute-start.2 = (bf16[256,1280]{1,0:T(8,128)(2,1)S(1)}, bf16[256,1280]{1,0:T(8,128)(2,1)S(1)}, u32[]{:S(2)}, u32[]{:S(2)}) collective-permute-start(bf16[256,1280]{1,0:T(8,128)(2,1)S(1)} %collective-permute-done.1.refs_0_), channel_id=1, source_target_pairs={{1,0},{2,3},{5,4},{6,7},{9,8},{10,11},{13,12},{14,15},{17,16},{18,... | collective-permute-start | bytes 1966088 | tf_op jit(solution)/shard_map/ppermute | solution.py:438
  55.2 30.2 %copy-start.13 = (f32[128]{0:T(128)S(1)}, f32[128]{0:T(128)}, u32[]{:S(2)}) copy-start(f32[128]{0:T(128)} %param.18) | copy-start | bytes 1540
  55.8 29.6 %copy-start.6 = (f32[512,128]{1,0:T(8,128)S(1)}, f32[512,128]{1,0:T(8,128)}, u32[]{:S(2)}) copy-start(f32[512,128]{1,0:T(8,128)} %constant.29.clone.refs_5_.refs_7_.refs_8_) | copy-start | bytes 786436
  55.8 29.6 %copy-start.7 = (f32[512,128]{1,0:T(8,128)S(1)}, f32[512,128]{1,0:T(8,128)}, u32[]{:S(2)}) copy-start(f32[512,128]{1,0:T(8,128)} %constant.30.clone.refs_6_.refs_8_.refs_9_) | copy-start | bytes 786436
  60.9 0.8 copy-start.10
  65.5 23.5 %collective-permute-start.10 = (bf16[128,2560]{1,0:T(8,128)(2,1)S(1)}, bf16[128,2560]{1,0:T(8,128)(2,1)S(1)}, u32[]{:S(2)}, u32[]{:S(2)}) collective-permute-start(bf16[128,2560]{1,0:T(8,128)(2,1)S(1)} %collective-permute-done.9.refs_0_), channel_id=1, source_target_pairs={{0,8},{4,12},{8,0},{12,4},{16,24},{20,28},{24,16},{28,20},{1,9},{5... | collective-permute-start | bytes 1966088 | tf_op jit(solution)/shard_map/ppermute | solution.py:444
  67.0 22.0 %collective-permute-start.11 = (bf16[128,2560]{1,0:T(8,128)(2,1)S(1)}, bf16[128,2560]{1,0:T(8,128)(2,1)S(1)}, u32[]{:S(2)}, u32[]{:S(2)}) collective-permute-start(bf16[128,2560]{1,0:T(8,128)(2,1)S(1)} %collective-permute-done.9.refs_0_), channel_id=1, source_target_pairs={{0,16},{4,20},{8,24},{12,28},{16,0},{20,4},{24,8},{28,12},{1,17},{... | collective-permute-start | bytes 1966088 | tf_op jit(solution)/shard_map/ppermute | solution.py:444
  68.5 20.5 %collective-permute-start.12 = (bf16[128,2560]{1,0:T(8,128)(2,1)S(1)}, bf16[128,2560]{1,0:T(8,128)(2,1)S(1)}, u32[]{:S(2)}, u32[]{:S(2)}) collective-permute-start(bf16[128,2560]{1,0:T(8,128)(2,1)S(1)} %eighth.3), channel_id=1, source_target_pairs={{0,1},{3,2},{4,5},{7,6},{8,9},{11,10},{12,13},{15,14},{16,17},{19,... | collective-permute-start | bytes 1966088 | tf_op jit(solution)/shard_map/ppermute | solution.py:441
  77.1 15.7 %collective-permute-start.8 = (bf16[256,1280]{1,0:T(8,128)(2,1)S(1)}, bf16[256,1280]{1,0:T(8,128)(2,1)S(1)}, u32[]{:S(2)}, u32[]{:S(2)}) collective-permute-start(bf16[256,1280]{1,0:T(8,128)(2,1)S(1)} %collective-permute-done.6.refs_0_.refs_1_), channel_id=1, source_target_pairs={{1,0},{2,3},{5,4},{6,7},{9,8},{10,11},{13,12},{14,15},{17,16},{18,... | collective-permute-start | bytes 1966088 | tf_op jit(solution)/shard_map/ppermute | solution.py:438
  78.4 1.1 copy-start.9
  79.5 1.1 copy-start.11
  85.4 2.5 %copy-start.12 = (f32[128]{0:T(128)S(1)}, f32[128]{0:T(128)}, u32[]{:S(2)}) copy-start(f32[128]{0:T(128)} %param.19) | copy-start | bytes 1540
  87.9 4.9 %copy-start.14 = (s32[1,128]{1,0:T(1,128)S(1)}, s32[1,128]{1,0:T(1,128)}, u32[]{:S(2)}) copy-start(s32[1,128]{1,0:T(1,128)} %refs_10_.1) | copy-start | bytes 1540
  94.1 3.6 %collective-permute-start.13 = (bf16[128,256]{1,0:T(8,128)(2,1)S(1)}, bf16[128,256]{1,0:T(8,128)(2,1)S(1)}, u32[]{:S(2)}, u32[]{:S(2)}) collective-permute-start(bf16[128,256]{1,0:T(8,128)(2,1)S(1)} %get-tuple-element.79), channel_id=1, source_target_pairs={{0,4},{4,0},{8,12},{12,8},{16,20},{20,16},{24,28},{28,24},{1,5},{5... | collective-permute-start | bytes 196616 | tf_op jit(solution)/shard_map/ppermute | solution.py:444
  94.2 5.0 %collective-permute-start.14 = (bf16[128,256]{1,0:T(8,128)(2,1)S(1)}, bf16[128,256]{1,0:T(8,128)(2,1)S(1)}, u32[]{:S(2)}, u32[]{:S(2)}) collective-permute-start(bf16[128,256]{1,0:T(8,128)(2,1)S(1)} %get-tuple-element.79), channel_id=1, source_target_pairs={{0,8},{4,12},{8,0},{12,4},{16,24},{20,28},{24,16},{28,20},{1,9},{5... | collective-permute-start | bytes 196616 | tf_op jit(solution)/shard_map/ppermute | solution.py:444
  94.8 8.8 %collective-permute-start.15 = (bf16[128,256]{1,0:T(8,128)(2,1)S(1)}, bf16[128,256]{1,0:T(8,128)(2,1)S(1)}, u32[]{:S(2)}, u32[]{:S(2)}) collective-permute-start(bf16[128,256]{1,0:T(8,128)(2,1)S(1)} %get-tuple-element.79), channel_id=1, source_target_pairs={{0,12},{4,8},{8,4},{12,0},{16,28},{20,24},{24,20},{28,16},{1,13},{... | collective-permute-start | bytes 196616 | tf_op jit(solution)/shard_map/ppermute | solution.py:444
  96.1 7.6 %collective-permute-start.16 = (bf16[128,256]{1,0:T(8,128)(2,1)S(1)}, bf16[128,256]{1,0:T(8,128)(2,1)S(1)}, u32[]{:S(2)}, u32[]{:S(2)}) collective-permute-start(bf16[128,256]{1,0:T(8,128)(2,1)S(1)} %get-tuple-element.79), channel_id=1, source_target_pairs={{0,16},{4,20},{8,24},{12,28},{16,0},{20,4},{24,8},{28,12},{1,17},{... | collective-permute-start | bytes 196616 | tf_op jit(solution)/shard_map/ppermute | solution.py:444
  96.6 7.1 %collective-permute-start.17 = (bf16[128,256]{1,0:T(8,128)(2,1)S(1)}, bf16[128,256]{1,0:T(8,128)(2,1)S(1)}, u32[]{:S(2)}, u32[]{:S(2)}) collective-permute-start(bf16[128,256]{1,0:T(8,128)(2,1)S(1)} %get-tuple-element.79), channel_id=1, source_target_pairs={{0,20},{4,16},{8,28},{12,24},{16,4},{20,0},{24,12},{28,8},{1,21},{... | collective-permute-start | bytes 196616 | tf_op jit(solution)/shard_map/ppermute | solution.py:444
  97.8 5.9 %collective-permute-start.18 = (bf16[128,256]{1,0:T(8,128)(2,1)S(1)}, bf16[128,256]{1,0:T(8,128)(2,1)S(1)}, u32[]{:S(2)}, u32[]{:S(2)}) collective-permute-start(bf16[128,256]{1,0:T(8,128)(2,1)S(1)} %get-tuple-element.79), channel_id=1, source_target_pairs={{0,24},{4,28},{8,16},{12,20},{16,8},{20,12},{24,0},{28,4},{1,25},{... | collective-permute-start | bytes 196616 | tf_op jit(solution)/shard_map/ppermute | solution.py:444
  99.2 5.3 %collective-permute-start.19 = (bf16[128,256]{1,0:T(8,128)(2,1)S(1)}, bf16[128,256]{1,0:T(8,128)(2,1)S(1)}, u32[]{:S(2)}, u32[]{:S(2)}) collective-permute-start(bf16[128,256]{1,0:T(8,128)(2,1)S(1)} %get-tuple-element.79), channel_id=1, source_target_pairs={{0,28},{4,24},{8,20},{12,16},{16,12},{20,8},{24,4},{28,0},{1,29},{... | collective-permute-start | bytes 196616 | tf_op jit(solution)/shard_map/ppermute | solution.py:444
  108.1 10.5 %collective-permute-start.20 = (bf16[128,1024]{1,0:T(8,128)(2,1)S(1)}, bf16[128,1024]{1,0:T(8,128)(2,1)S(1)}, u32[]{:S(2)}, u32[]{:S(2)}) collective-permute-start(bf16[128,1024]{1,0:T(8,128)(2,1)S(1)} %attention.3.rows_ref), channel_id=1, source_target_pairs={{0,1},{3,2},{4,5},{7,6},{8,9},{11,10},{12,13},{15,14},{16,17},{19,... | collective-permute-start | bytes 786440 | tf_op jit(solution)/shard_map/ppermute | solution.py:441
  109.7 10.2 %collective-permute-start.21 = (bf16[128,2560]{1,0:T(8,128)(2,1)S(1)}, bf16[128,2560]{1,0:T(8,128)(2,1)S(1)}, u32[]{:S(2)}, u32[]{:S(2)}) collective-permute-start(bf16[128,2560]{1,0:T(8,128)(2,1)S(1)} %collective-permute-done.9.refs_0_), channel_id=1, source_target_pairs={{0,4},{4,0},{8,12},{12,8},{16,20},{20,16},{24,28},{28,24},{1,5},{5... | collective-permute-start | bytes 1966088 | tf_op jit(solution)/shard_map/ppermute | solution.py:444
  109.8 11.4 %collective-permute-start.22 = (bf16[128,2560]{1,0:T(8,128)(2,1)S(1)}, bf16[128,2560]{1,0:T(8,128)(2,1)S(1)}, u32[]{:S(2)}, u32[]{:S(2)}) collective-permute-start(bf16[128,2560]{1,0:T(8,128)(2,1)S(1)} %collective-permute-done.12.refs_1_), channel_id=1, source_target_pairs={{0,4},{4,0},{8,12},{12,8},{16,20},{20,16},{24,28},{28,24},{1,5},{5... | collective-permute-start | bytes 1966088 | tf_op jit(solution)/shard_map/ppermute | solution.py:444
  110.3 10.9 %collective-permute-start.23 = (bf16[128,2560]{1,0:T(8,128)(2,1)S(1)}, bf16[128,2560]{1,0:T(8,128)(2,1)S(1)}, u32[]{:S(2)}, u32[]{:S(2)}) collective-permute-start(bf16[128,2560]{1,0:T(8,128)(2,1)S(1)} %collective-permute-done.10.refs_2_), channel_id=1, source_target_pairs={{0,4},{4,0},{8,12},{12,8},{16,20},{20,16},{24,28},{28,24},{1,5},{5... | collective-permute-start | bytes 1966088 | tf_op jit(solution)/shard_map/ppermute | solution.py:444
  110.4 10.8 %collective-permute-start.24 = (bf16[128,2560]{1,0:T(8,128)(2,1)S(1)}, bf16[128,2560]{1,0:T(8,128)(2,1)S(1)}, u32[]{:S(2)}, u32[]{:S(2)}) collective-permute-start(bf16[128,2560]{1,0:T(8,128)(2,1)S(1)} %collective-permute-done.11.refs_3_), channel_id=1, source_target_pairs={{0,4},{4,0},{8,12},{12,8},{16,20},{20,16},{24,28},{28,24},{1,5},{5... | collective-permute-start | bytes 1966088 | tf_op jit(solution)/shard_map/ppermute | solution.py:444
  118.5 16.4 %collective-permute-start.26 = (bf16[128,2560]{1,0:T(8,128)(2,1)S(1)}, bf16[128,2560]{1,0:T(8,128)(2,1)S(1)}, u32[]{:S(2)}, u32[]{:S(2)}) collective-permute-start(bf16[128,2560]{1,0:T(8,128)(2,1)S(1)} %mix.8.refs_0_), channel_id=1, source_target_pairs={{0,1},{3,2},{4,5},{7,6},{8,9},{11,10},{12,13},{15,14},{16,17},{19,... | collective-permute-start | bytes 1966088 | tf_op jit(solution)/shard_map/ppermute | solution.py:441
  119.9 20.1 %collective-permute-start.25 = (bf16[128,1024]{1,0:T(8,128)(2,1)S(1)}, bf16[128,1024]{1,0:T(8,128)(2,1)S(1)}, u32[]{:S(2)}, u32[]{:S(2)}) collective-permute-start(bf16[128,1024]{1,0:T(8,128)(2,1)S(1)} %attention.4.rows_ref), channel_id=1, source_target_pairs={{0,1},{3,2},{4,5},{7,6},{8,9},{11,10},{12,13},{15,14},{16,17},{19,... | collective-permute-start | bytes 786440 | tf_op jit(solution)/shard_map/ppermute | solution.py:441
  124.0 25.2 %collective-permute-start.27 = (bf16[128,2560]{1,0:T(8,128)(2,1)S(1)}, bf16[128,2560]{1,0:T(8,128)(2,1)S(1)}, u32[]{:S(2)}, u32[]{:S(2)}) collective-permute-start(bf16[128,2560]{1,0:T(8,128)(2,1)S(1)} %added.8), channel_id=1, source_target_pairs={{1,2},{2,1},{5,6},{6,5},{9,10},{10,9},{13,14},{14,13},{17,18},{18,... | collective-permute-start | bytes 1966088 | tf_op jit(solution)/shard_map/ppermute | solution.py:435
  135.0 19.8 %collective-permute-start.28 = (bf16[128,2560]{1,0:T(8,128)(2,1)S(1)}, bf16[128,2560]{1,0:T(8,128)(2,1)S(1)}, u32[]{:S(2)}, u32[]{:S(2)}) collective-permute-start(bf16[128,2560]{1,0:T(8,128)(2,1)S(1)} %added.9), channel_id=1, source_target_pairs={{1,2},{2,1},{5,6},{6,5},{9,10},{10,9},{13,14},{14,13},{17,18},{18,... | collective-permute-start | bytes 1966088 | tf_op jit(solution)/shard_map/ppermute | solution.py:435
  139.9 20.5 %collective-permute-start.29 = (bf16[128,2560]{1,0:T(8,128)(2,1)S(1)}, bf16[128,2560]{1,0:T(8,128)(2,1)S(1)}, u32[]{:S(2)}, u32[]{:S(2)}) collective-permute-start(bf16[128,2560]{1,0:T(8,128)(2,1)S(1)} %mix.11.refs_0_), channel_id=1, source_target_pairs={{0,1},{3,2},{4,5},{7,6},{8,9},{11,10},{12,13},{15,14},{16,17},{19,... | collective-permute-start | bytes 1966088 | tf_op jit(solution)/shard_map/ppermute | solution.py:441
  144.4 21.0 %collective-permute-start.33 = (bf16[128,1024]{1,0:T(8,128)(2,1)S(1)}, bf16[128,1024]{1,0:T(8,128)(2,1)S(1)}, u32[]{:S(2)}, u32[]{:S(2)}) collective-permute-start(bf16[128,1024]{1,0:T(8,128)(2,1)S(1)} %get-tuple-element.93.rows_ref), channel_id=1, source_target_pairs={{0,1},{3,2},{4,5},{7,6},{8,9},{11,10},{12,13},{15,14},{16,17},{19,... | collective-permute-start | bytes 786440 | tf_op jit(solution)/shard_map/ppermute | solution.py:441
  148.5 20.2 %collective-permute-start.35 = (bf16[128,2560]{1,0:T(8,128)(2,1)S(1)}, bf16[128,2560]{1,0:T(8,128)(2,1)S(1)}, u32[]{:S(2)}, u32[]{:S(2)}) collective-permute-start(bf16[128,2560]{1,0:T(8,128)(2,1)S(1)} %added.10), channel_id=1, source_target_pairs={{1,2},{2,1},{5,6},{6,5},{9,10},{10,9},{13,14},{14,13},{17,18},{18,... | collective-permute-start | bytes 1966088 | tf_op jit(solution)/shard_map/ppermute | solution.py:435
  153.5 19.6 %collective-permute-start.34 = (bf16[128,2560]{1,0:T(8,128)(2,1)S(1)}, bf16[128,2560]{1,0:T(8,128)(2,1)S(1)}, u32[]{:S(2)}, u32[]{:S(2)}) collective-permute-start(bf16[128,2560]{1,0:T(8,128)(2,1)S(1)} %added.11), channel_id=1, source_target_pairs={{1,0},{2,3},{5,4},{6,7},{9,8},{10,11},{13,12},{14,15},{17,16},{18,... | collective-permute-start | bytes 1966088 | tf_op jit(solution)/shard_map/ppermute | solution.py:438
  159.1 26.2 %collective-permute-start.31 = (bf16[128,2560]{1,0:T(8,128)(2,1)S(1)}, bf16[128,2560]{1,0:T(8,128)(2,1)S(1)}, u32[]{:S(2)}, u32[]{:S(2)}) collective-permute-start(bf16[128,2560]{1,0:T(8,128)(2,1)S(1)} %added.12), channel_id=1, source_target_pairs={{1,0},{2,3},{5,4},{6,7},{9,8},{10,11},{13,12},{14,15},{17,16},{18,... | collective-permute-start | bytes 1966088 | tf_op jit(solution)/shard_map/ppermute | solution.py:438
  160.6 17.8 %collective-permute-start.30 = (bf16[128,2560]{1,0:T(8,128)(2,1)S(1)}, bf16[128,2560]{1,0:T(8,128)(2,1)S(1)}, u32[]{:S(2)}, u32[]{:S(2)}) collective-permute-start(bf16[128,2560]{1,0:T(8,128)(2,1)S(1)} %mix.13.refs_0_), channel_id=1, source_target_pairs={{0,1},{3,2},{4,5},{7,6},{8,9},{11,10},{12,13},{15,14},{16,17},{19,... | collective-permute-start | bytes 1966088 | tf_op jit(solution)/shard_map/ppermute | solution.py:441
  165.3 20.1 %collective-permute-start.32 = (bf16[128,2560]{1,0:T(8,128)(2,1)S(1)}, bf16[128,2560]{1,0:T(8,128)(2,1)S(1)}, u32[]{:S(2)}, u32[]{:S(2)}) collective-permute-start(bf16[128,2560]{1,0:T(8,128)(2,1)S(1)} %added.13), channel_id=1, source_target_pairs={{1,2},{2,1},{5,6},{6,5},{9,10},{10,9},{13,14},{14,13},{17,18},{18,... | collective-permute-start | bytes 1966088 | tf_op jit(solution)/shard_map/ppermute | solution.py:435

commit v11 on v10

--- a/solution.py
+++ b/solution.py
@@ -518,33 +518,37 @@
 
     (far_rows,) = attend((LAST,))
     far = mixed(far_rows)
-    far_sent = send(far_rows, far[1])
-    places = after(places, far)
-    (third_rows,) = attend((THIRD,))
-    far_sent = after(far_sent, third_rows)
+    far_sent = after(send(far_rows, far[1]), far)
     far_in = inward(after(far[0], far_sent))
     far_right = added(far[1], share_of(far_sent))
     places = after(places, far_right)
-    near_rows, own_rows = attend((NEAR, OWN))
-    third = mixed(after(third_rows, near_rows))
+    (third_rows,) = attend((THIRD,))
+    third = mixed(third_rows)
     third_sent = send(third_rows, third[1])
     far_right = across(far_right)
     far_left = added(far[0], after(far_in, third))
-    third_sent = after(third_sent, far_left)
+    places = after(places, far_left)
+    near_rows, own_rows = attend((NEAR, OWN))
     far_left = across(far_left)
+    third_sent = after(third_sent, near_rows)
     third_in = inward(after(third[0], third_sent))
+    near = [None, mix(near_rows, w_out, 1)]
+    near_sent = send(near_rows, near[1])
+    out_right = added(near[1], far_right)
+    third_sent = after(third_sent, out_right)
+    out_right = outward(out_right)
     third_right = added(third[1], share_of(third_sent))
-    near = mixed(after(near_rows, (third_right, far_right)))
-    near_sent = send(near_rows, near[1])
+    near[0] = mix(after(near_rows, third_right), w_out, 0)
     third_right = across(third_right)
-    out_right = added(near[1], after(far_right, near))
-    kept = mixed(after(own_rows, (out_right, far_left)))
-    out_left = added(near[0], after(far_left, kept))
+    out_left = added(near[0], far_left)
     third_left = added(third[0], after(third_in, out_left))
-    near_sent = share_of(after(near_sent, third_left))
-    result = added(kept[1], near_sent, outward(out_right), third_right, half=1)
-    near_in = inward(after(near[0], third_left))
-    out_left, third_left = outward(out_left), across(third_left)
+    out_left = outward(out_left)
+    near_sent = after(near_sent, third_left)
+    kept = mixed(after(own_rows, near_sent))
+    near_in = inward(after(near[0], (out_right, near_sent)))
+    near_sent = share_of(near_sent)
+    result = added(kept[1], near_sent, out_right, third_right, half=1)
+    third_left = across(third_left)
     return added(kept[0], near_in, out_left, third_left, half=0, into=result)
 
 

time: 187 us -> 188 us (level)
  the two profiles are of different devices: /device:TPU:0 before, /device:TPU:8 now
where the time goes in v11:
time: 188 us; the launch traced here: 187 us
  starting transfers between devices  61.8 us (33%)
  Pallas kernels  61.8 us (33%)
  waiting for transfers between devices  50.7 us (27%)
  local copies, waits for them, and re-layouts  11.2 us (6%)
    ppermute x8, waiting for transfers between devices, across(): return lax.ppermute(array, 'tensor', [(1, 2), (2, 1)])  39.5 us
    ppermute x8, starting transfers between devices, across(): return lax.ppermute(array, 'tensor', [(1, 2), (2, 1)])  26.2 us
    pallas_call x8, Pallas kernels, mix(): pl.pallas_call(mix_kernel, grid=(tiles,), in_specs=[whole(rows, depth), p...  16.5 us
    ppermute x6, starting transfers between devices, outward(): return lax.ppermute(array, 'tensor', [(1, 0), (2, 3)])  15.7 us
    pallas_call x3, Pallas kernels, attention(): pl.pallas_call(functools.partial(attention_kernel, slots, n_parts, len(ot...  12.7 us
    pallas_call x3, Pallas kernels, partial_projection(): pl.pallas_call(functools.partial(partial_kernel, [len(part) for part in p...  11.8 us
    unnamed x36, local copies, waits for them, and re-layouts  11.1 us
    ppermute x8, starting transfers between devices, inward(): return lax.ppermute(array, 'tensor', [(0, 1), (3, 2)])  10.5 us
  transfers between devices with their start and end apart: 36, of which 12 were waited for; matrix products, arithmetic and copies ran while one was open for 0% of the time, Pallas kernels for 32%

profile of v11, /device:TPU:8, one launch (start us, length us, event | category | flops | bytes accessed | tf_op | source)
XLA Modules:
  0.0 186.9 jit_solution(18230537817219218010)
XLA Ops:
  0.0 1.4 copy-done.4
  2.3 5.0 %collective-permute-start.3 = (bf16[256,1280]{1,0:T(8,128)(2,1)}, bf16[256,1280]{1,0:T(8,128)(2,1)}, u32[]{:S(2)}, u32[]{:S(2)}) collective-permute-start(bf16[256,1280]{1,0:T(8,128)(2,1)} %get-tuple-element.53), channel_id=1, source_target_pairs={{1,2},{2,1},{5,6},{6,5},{9,10},{10,9},{13,14},{14,13},{17,18},{18,... | collective-permute-start | bytes 1966088 | tf_op jit(solution)/shard_map/ppermute | solution.py:435
  7.3 1.9 %collective-permute-start.5 = (bf16[256,1280]{1,0:T(8,128)(2,1)S(1)}, bf16[256,1280]{1,0:T(8,128)(2,1)}, u32[]{:S(2)}, u32[]{:S(2)}) collective-permute-start(bf16[256,1280]{1,0:T(8,128)(2,1)S(1)} %get-tuple-element.58), channel_id=1, source_target_pairs={{1,2},{2,1},{5,6},{6,5},{9,10},{10,9},{13,14},{14,13},{17,18},{18,... | collective-permute-start | bytes 1966088 | tf_op jit(solution)/shard_map/ppermute | solution.py:435
  9.4 4.0 %copy-done.1 = bf16[5120,1024]{1,0:T(8,128)(2,1)S(1)} copy-done((bf16[5120,1024]{1,0:T(8,128)(2,1)S(1)}, bf16[5120,1024]{1,0:T(8,128)(2,1)}, u32[]{:S(2)}) %copy-start.1) | copy-done | bytes 10485784
  13.4 1.3 copy-done.3
  14.7 1.3 copy-done.5
  16.0 3.4 %partial_projection.3 = (f32[512,1024]{1,0:T(8,128)S(1)}, f32[512,128]{1,0:T(8,128)S(1)}, f32[512,128]{1,0:T(8,128)S(1)}) custom-call(s32[12]{0:T(128)S(1)} %stack.51.places_ref, bf16[512,1280]{1,0:T(8,128)(2,1)S(1)} %copy-done.5, bf16[5120,1024]{1,0:T(8,128)(2,1)S(1)} %copy-done.1, bf16[5120,128]{1,0:T(8,128)(2,1)S(1)} %copy-done.2, ...), custom_call_target="tpu_custom_call" | custom-call | flops 1 | bytes 1 | tf_op jit(solution)/shard_map/partial_projection/pallas_call | solution.py:96
  19.4 3.8 %collective-permute-done.3.refs_0_ = bf16[256,1280]{1,0:T(8,128)(2,1)} collective-permute-done((bf16[256,1280]{1,0:T(8,128)(2,1)}, bf16[256,1280]{1,0:T(8,128)(2,1)}, u32[]{:S(2)}, u32[]{:S(2)}) %collective-permute-start.3) | collective-permute-done | bytes 655392 | tf_op jit(solution)/shard_map/ppermute | solution.py:435
  23.2 1.3 collective-permute-start.4
  25.2 11.0 %collective-permute-done.5.refs_2_ = bf16[256,1280]{1,0:T(8,128)(2,1)} collective-permute-done((bf16[256,1280]{1,0:T(8,128)(2,1)S(1)}, bf16[256,1280]{1,0:T(8,128)(2,1)}, u32[]{:S(2)}, u32[]{:S(2)}) %collective-permute-start.5) | collective-permute-done | bytes 655392 | tf_op jit(solution)/shard_map/ppermute | solution.py:435
  36.1 1.3 collective-permute-start.7
  37.6 3.6 %collective-permute-start.1 = (bf16[256,1280]{1,0:T(8,128)(2,1)S(1)}, bf16[256,1280]{1,0:T(8,128)(2,1)S(1)}, u32[]{:S(2)}, u32[]{:S(2)}) collective-permute-start(bf16[256,1280]{1,0:T(8,128)(2,1)S(1)} %get-tuple-element.51), channel_id=1, source_target_pairs={{1,2},{2,1},{5,6},{6,5},{9,10},{10,9},{13,14},{14,13},{17,18},{18,... | collective-permute-start | bytes 1966088 | tf_op jit(solution)/shard_map/ppermute | solution.py:435
  41.2 3.6 %partial_projection.4 = (f32[512,1024]{1,0:T(8,128)S(1)}, f32[512,128]{1,0:T(8,128)S(1)}, f32[512,128]{1,0:T(8,128)S(1)}) custom-call(s32[12]{0:T(128)S(1)} %stack.51.places_ref, bf16[512,1280]{1,0:T(8,128)(2,1)S(1)} %collective-permute-done.ref.refs_0_, bf16[5120,1024]{1,0:T(8,128)(2,1)S(1)} %copy-done.1, bf16[5120,128]{1,0:T(8,128)(2,1)S(1)} %copy-done.2, ...), custom_call_target="tpu_custom_call" | custom-call | flops 1 | bytes 1 | tf_op jit(solution)/shard_map/partial_projection/pallas_call | solution.py:96
  44.9 4.0 %collective-permute-start.6 = (bf16[256,1280]{1,0:T(8,128)(2,1)S(1)}, bf16[256,1280]{1,0:T(8,128)(2,1)S(1)}, u32[]{:S(2)}, u32[]{:S(2)}) collective-permute-start(bf16[256,1280]{1,0:T(8,128)(2,1)S(1)} %get-tuple-element.66), channel_id=1, source_target_pairs={{1,2},{2,1},{5,6},{6,5},{9,10},{10,9},{13,14},{14,13},{17,18},{18,... | collective-permute-start | bytes 1966088 | tf_op jit(solution)/shard_map/ppermute | solution.py:435
  48.9 1.3 collective-permute-start.9
  50.2 7.0 %collective-permute-done.1.refs_0_ = bf16[256,1280]{1,0:T(8,128)(2,1)S(1)} collective-permute-done((bf16[256,1280]{1,0:T(8,128)(2,1)S(1)}, bf16[256,1280]{1,0:T(8,128)(2,1)S(1)}, u32[]{:S(2)}, u32[]{:S(2)}) %collective-permute-start.1) | collective-permute-done | bytes 655392 | tf_op jit(solution)/shard_map/ppermute | solution.py:435
  57.1 1.3 collective-permute-start.2
  59.9 9.2 %collective-permute-done.6.refs_0_.refs_1_ = bf16[256,1280]{1,0:T(8,128)(2,1)S(1)} collective-permute-done((bf16[256,1280]{1,0:T(8,128)(2,1)S(1)}, bf16[256,1280]{1,0:T(8,128)(2,1)S(1)}, u32[]{:S(2)}, u32[]{:S(2)}) %collective-permute-start.6) | collective-permute-done | bytes 655392 | tf_op jit(solution)/shard_map/ppermute | solution.py:435
  69.1 1.5 collective-permute-start.10
  70.6 1.5 collective-permute-start.11
  72.1 1.3 collective-permute-start.12
  73.4 4.6 %collective-permute-start.8 = (bf16[256,1280]{1,0:T(8,128)(2,1)S(1)}, bf16[256,1280]{1,0:T(8,128)(2,1)S(1)}, u32[]{:S(2)}, u32[]{:S(2)}) collective-permute-start(bf16[256,1280]{1,0:T(8,128)(2,1)S(1)} %collective-permute-done.6.refs_0_.refs_1_), channel_id=1, source_target_pairs={{1,0},{2,3},{5,4},{6,7},{9,8},{10,11},{13,12},{14,15},{17,16},{18,... | collective-permute-start | bytes 1966088 | tf_op jit(solution)/shard_map/ppermute | solution.py:438
  78.1 1.1 copy-done.9
  79.2 1.1 copy-done.11
  80.2 4.8 %partial_projection.5 = (f32[512,1024]{1,0:T(8,128)S(1)}, f32[512,128]{1,0:T(8,128)S(1)}, f32[512,128]{1,0:T(8,128)S(1)}) custom-call(s32[12]{0:T(128)S(1)} %stack.51.places_ref, bf16[256,1280]{1,0:T(8,128)(2,1)} %collective-permute-done.3.refs_0_, bf16[256,1280]{1,0:T(8,128)(2,1)S(1)} %copy-done.9, bf16[256,1280]{1,0:T(8,128)(2,1)} %collective-permute-done.5.refs_2_, ...), custom_call_target="tpu_custom_call" | custom-call | flops 1 | bytes 1 | tf_op jit(solution)/shard_map/partial_projection/pallas_call | solution.py:96
  85.1 2.5 %queries.2.refs_0_ = bf16[256,1024]{1,0:T(8,128)(2,1)S(1)} custom-call(s32[12]{0:T(128)S(1)} %stack.51.places_ref, bf16[256,1280]{1,0:T(8,128)(2,1)S(1)} %collective-permute-done.1.refs_0_, bf16[256,1280]{1,0:T(8,128)(2,1)S(1)} %collective-permute-done.2.refs_1_, bf16[5120,1024]{1,0:T(8,128)(2,1)S(1)} %bitcast.15, ...), custom_call_target="tpu_custom_call" | custom-call | flops 1 | bytes 1 | tf_op jit(solution)/shard_map/queries/pallas_call | solution.py:183
  87.6 1.1 keys_values.2.refs_0_.refs_2_
  89.3 1.3 keys_values.3
  91.3 1.3 collective-permute-start.15
  93.1 1.2 collective-permute-start.17
  95.7 1.3 collective-permute-start.19
  97.0 2.5 %queries.3.refs_1_ = bf16[256,1024]{1,0:T(8,128)(2,1)S(1)} custom-call(s32[12]{0:T(128)S(1)} %stack.51.places_ref, bf16[256,1280]{1,0:T(8,128)(2,1)S(1)} %collective-permute-done.6.refs_0_.refs_1_, bf16[256,1280]{1,0:T(8,128)(2,1)S(1)} %collective-permute-done.8.refs_1_.refs_2_, bf16[5120,1024]{1,0:T(8,128)(2,1)S(1)} %bitcast.15, ...), custom_call_target="tpu_custom_call" | custom-call | flops 1 | bytes 1 | tf_op jit(solution)/shard_map/queries/pallas_call | solution.py:183
  99.9 1.1 collective-permute-done.19.refs_10_
  102.7 3.6 %attention.3.rows_ref = bf16[128,1024]{1,0:T(8,128)(2,1)S(1)} custom-call(s32[12]{0:T(128)S(1)} %stack.51.places_ref, s32[1]{0:T(128)S(6)} %copy.14.length_ref, bf16[256,1024]{1,0:T(8,128)(2,1)S(1)} %queries.2.refs_0_, bf16[256,1024]{1,0:T(8,128)(2,1)S(1)} %queries.3.refs_1_, bf16[256,256]{1,0:T(8,128)(2,1)S(1)} %keys_values.2.refs_0_.refs_2_, ...), custom_call_target="tpu_custom_call" | custom-call | flops 1 | bytes 1 | tf_op jit(solution)/shard_map/attention/pallas_call | solution.py:272
  106.3 1.5 collective-permute-start.20
  107.7 2.1 %mix.8.refs_0_ = bf16[128,2560]{1,0:T(8,128)(2,1)S(1)} custom-call(bf16[128,1024]{1,0:T(8,128)(2,1)S(1)} %attention.3.rows_ref, bf16[1024,5120]{1,0:T(8,128)(2,1)S(1)} %copy-done), custom_call_target="tpu_custom_call" | custom-call | flops 1 | bytes 1 | tf_op jit(solution)/shard_map/mix/pallas_call | solution.py:301
  109.8 2.1 %mix.9.refs_0_ = bf16[128,2560]{1,0:T(8,128)(2,1)S(1)} custom-call(bf16[128,1024]{1,0:T(8,128)(2,1)S(1)} %attention.3.rows_ref, bf16[1024,5120]{1,0:T(8,128)(2,1)S(1)} %copy-done), custom_call_target="tpu_custom_call" | custom-call | flops 1 | bytes 1 | tf_op jit(solution)/shard_map/mix/pallas_call | solution.py:301
  111.9 4.7 %collective-permute-done.20.rows_ref = bf16[128,1024]{1,0:T(8,128)(2,1)S(1)} collective-permute-done((bf16[128,1024]{1,0:T(8,128)(2,1)S(1)}, bf16[128,1024]{1,0:T(8,128)(2,1)S(1)}, u32[]{:S(2)}, u32[]{:S(2)}) %collective-permute-start.20) | collective-permute-done | bytes 262176 | tf_op jit(solution)/shard_map/ppermute | solution.py:441
  116.5 1.3 collective-permute-start.25
  117.9 2.7 %mix_sent.3.refs_1_ = bf16[128,2560]{1,0:T(8,128)(2,1)S(1)} custom-call(s32[12]{0:T(128)S(1)} %stack.51.places_ref, bf16[128,1024]{1,0:T(8,128)(2,1)S(1)} %collective-permute-done.20.rows_ref, bf16[128,2560]{1,0:T(8,128)(2,1)S(1)} %collective-permute-done.9.refs_0_, bf16[128,2560]{1,0:T(8,128)(2,1)S(1)} %collective-permute-done.12.refs_1_, ...), custom_call_target="tpu_custom_call" | custom-call | flops 1 | bytes 1 | tf_op jit(solution)/shard_map/mix_sent/pallas_call | solution.py:357
  120.7 3.0 %collective-permute-start.29 = (bf16[128,2560]{1,0:T(8,128)(2,1)S(1)}, bf16[128,2560]{1,0:T(8,128)(2,1)S(1)}, u32[]{:S(2)}, u32[]{:S(2)}) collective-permute-start(bf16[128,2560]{1,0:T(8,128)(2,1)S(1)} %added.8), channel_id=1, source_target_pairs={{1,2},{2,1},{5,6},{6,5},{9,10},{10,9},{13,14},{14,13},{17,18},{18,... | collective-permute-start | bytes 1966088 | tf_op jit(solution)/shard_map/ppermute | solution.py:435
  123.7 3.6 %attention.4.rows_ref = bf16[128,1024]{1,0:T(8,128)(2,1)S(1)} custom-call(s32[12]{0:T(128)S(1)} %stack.51.places_ref, s32[1]{0:T(128)S(6)} %copy.14.length_ref, bf16[256,1024]{1,0:T(8,128)(2,1)S(1)} %queries.2.refs_0_, bf16[256,1024]{1,0:T(8,128)(2,1)S(1)} %queries.3.refs_1_, bf16[256,256]{1,0:T(8,128)(2,1)S(1)} %keys_values.2.refs_0_.refs_2_, ...), custom_call_target="tpu_custom_call" | custom-call | flops 1 | bytes 1 | tf_op jit(solution)/shard_map/attention/pallas_call | solution.py:272
  127.3 1.3 collective-permute-start.27
  128.6 2.1 %mix.10.refs_0_ = bf16[128,2560]{1,0:T(8,128)(2,1)S(1)} custom-call(bf16[128,1024]{1,0:T(8,128)(2,1)S(1)} %attention.4.rows_ref, bf16[1024,5120]{1,0:T(8,128)(2,1)S(1)} %copy-done), custom_call_target="tpu_custom_call" | custom-call | flops 1 | bytes 1 | tf_op jit(solution)/shard_map/mix/pallas_call | solution.py:301
  130.7 2.1 %mix.11.refs_0_ = bf16[128,2560]{1,0:T(8,128)(2,1)S(1)} custom-call(bf16[128,1024]{1,0:T(8,128)(2,1)S(1)} %attention.4.rows_ref, bf16[1024,5120]{1,0:T(8,128)(2,1)S(1)} %copy-done), custom_call_target="tpu_custom_call" | custom-call | flops 1 | bytes 1 | tf_op jit(solution)/shard_map/mix/pallas_call | solution.py:301
  132.7 3.4 %collective-permute-done.25.refs_1_ = bf16[128,2560]{1,0:T(8,128)(2,1)S(1)} collective-permute-done((bf16[128,2560]{1,0:T(8,128)(2,1)S(1)}, bf16[128,2560]{1,0:T(8,128)(2,1)S(1)}, u32[]{:S(2)}, u32[]{:S(2)}) %collective-permute-start.25) | collective-permute-done | bytes 655392 | tf_op jit(solution)/shard_map/ppermute | solution.py:441
  136.3 3.0 %collective-permute-start.30 = (bf16[128,2560]{1,0:T(8,128)(2,1)S(1)}, bf16[128,2560]{1,0:T(8,128)(2,1)S(1)}, u32[]{:S(2)}, u32[]{:S(2)}) collective-permute-start(bf16[128,2560]{1,0:T(8,128)(2,1)S(1)} %added.9), channel_id=1, source_target_pairs={{1,2},{2,1},{5,6},{6,5},{9,10},{10,9},{13,14},{14,13},{17,18},{18,... | collective-permute-start | bytes 1966088 | tf_op jit(solution)/shard_map/ppermute | solution.py:435
  139.3 5.6 %attention.5 = (bf16[128,1024]{1,0:T(8,128)(2,1)S(1)}, bf16[128,1024]{1,0:T(8,128)(2,1)S(1)}) custom-call(s32[12]{0:T(128)S(1)} %stack.51.places_ref, s32[1]{0:T(128)S(6)} %copy.14.length_ref, bf16[256,1024]{1,0:T(8,128)(2,1)S(1)} %queries.2.refs_0_, bf16[256,1024]{1,0:T(8,128)(2,1)S(1)} %queries.3.refs_1_, bf16[256,256]{1,0:T(8,128)(2,1)S(1)} %keys_values.2.refs_0_.refs_2_, ...), custom_call_target="tpu_custom_call" | custom-call | flops 1 | bytes 1 | tf_op jit(solution)/shard_map/attention/pallas_call | solution.py:272
  144.9 1.3 collective-permute-start.28
  146.2 2.1 %mix.12.refs_0_ = bf16[128,2560]{1,0:T(8,128)(2,1)S(1)} custom-call(bf16[128,1024]{1,0:T(8,128)(2,1)S(1)} %get-tuple-element.92.rows_ref, bf16[1024,5120]{1,0:T(8,128)(2,1)S(1)} %copy-done), custom_call_target="tpu_custom_call" | custom-call | flops 1 | bytes 1 | tf_op jit(solution)/shard_map/mix/pallas_call | solution.py:301
  148.4 4.6 %collective-permute-start.31 = (bf16[128,2560]{1,0:T(8,128)(2,1)S(1)}, bf16[128,2560]{1,0:T(8,128)(2,1)S(1)}, u32[]{:S(2)}, u32[]{:S(2)}) collective-permute-start(bf16[128,2560]{1,0:T(8,128)(2,1)S(1)} %added.10), channel_id=1, source_target_pairs={{1,0},{2,3},{5,4},{6,7},{9,8},{10,11},{13,12},{14,15},{17,16},{18,... | collective-permute-start | bytes 1966088 | tf_op jit(solution)/shard_map/ppermute | solution.py:438
  153.1 1.3 collective-permute-start.26
  154.4 2.7 %mix_sent.4.refs_1_ = bf16[128,2560]{1,0:T(8,128)(2,1)S(1)} custom-call(s32[12]{0:T(128)S(1)} %stack.51.places_ref, bf16[128,1024]{1,0:T(8,128)(2,1)S(1)} %collective-permute-done.27.rows_ref, bf16[128,2560]{1,0:T(8,128)(2,1)S(1)} %collective-permute-done.9.refs_0_, bf16[128,2560]{1,0:T(8,128)(2,1)S(1)} %collective-permute-done.12.refs_1_, ...), custom_call_target="tpu_custom_call" | custom-call | flops 1 | bytes 1 | tf_op jit(solution)/shard_map/mix_sent/pallas_call | solution.py:357
  157.2 2.8 %collective-permute-start.35 = (bf16[128,2560]{1,0:T(8,128)(2,1)S(1)}, bf16[128,2560]{1,0:T(8,128)(2,1)S(1)}, u32[]{:S(2)}, u32[]{:S(2)}) collective-permute-start(bf16[128,2560]{1,0:T(8,128)(2,1)S(1)} %added.11), channel_id=1, source_target_pairs={{1,2},{2,1},{5,6},{6,5},{9,10},{10,9},{13,14},{14,13},{17,18},{18,... | collective-permute-start | bytes 1966088 | tf_op jit(solution)/shard_map/ppermute | solution.py:435
  160.0 2.1 %mix.13.refs_0_ = bf16[128,2560]{1,0:T(8,128)(2,1)S(1)} custom-call(bf16[128,1024]{1,0:T(8,128)(2,1)S(1)} %get-tuple-element.92.rows_ref, bf16[1024,5120]{1,0:T(8,128)(2,1)S(1)} %copy-done), custom_call_target="tpu_custom_call" | custom-call | flops 1 | bytes 1 | tf_op jit(solution)/shard_map/mix/pallas_call | solution.py:301
  162.3 2.5 %collective-permute-start.33 = (bf16[128,2560]{1,0:T(8,128)(2,1)S(1)}, bf16[128,2560]{1,0:T(8,128)(2,1)S(1)}, u32[]{:S(2)}, u32[]{:S(2)}) collective-permute-start(bf16[128,2560]{1,0:T(8,128)(2,1)S(1)} %added.12), channel_id=1, source_target_pairs={{1,0},{2,3},{5,4},{6,7},{9,8},{10,11},{13,12},{14,15},{17,16},{18,... | collective-permute-start | bytes 1966088 | tf_op jit(solution)/shard_map/ppermute | solution.py:438
  164.9 2.8 %collective-permute-start.34 = (bf16[128,2560]{1,0:T(8,128)(2,1)S(1)}, bf16[128,2560]{1,0:T(8,128)(2,1)S(1)}, u32[]{:S(2)}, u32[]{:S(2)}) collective-permute-start(bf16[128,2560]{1,0:T(8,128)(2,1)S(1)} %added.13), channel_id=1, source_target_pairs={{1,2},{2,1},{5,6},{6,5},{9,10},{10,9},{13,14},{14,13},{17,18},{18,... | collective-permute-start | bytes 1966088 | tf_op jit(solution)/shard_map/ppermute | solution.py:435
  167.8 1.3 collective-permute-start.32
  169.1 2.1 %mix.14.refs_0_ = bf16[128,2560]{1,0:T(8,128)(2,1)S(1)} custom-call(bf16[128,1024]{1,0:T(8,128)(2,1)S(1)} %get-tuple-element.95.rows_ref, bf16[1024,5120]{1,0:T(8,128)(2,1)S(1)} %copy-done), custom_call_target="tpu_custom_call" | custom-call | flops 1 | bytes 1 | tf_op jit(solution)/shard_map/mix/pallas_call | solution.py:301
  171.1 2.1 %mix.15.refs_0_ = bf16[128,2560]{1,0:T(8,128)(2,1)S(1)} custom-call(bf16[128,1024]{1,0:T(8,128)(2,1)S(1)} %get-tuple-element.95.rows_ref, bf16[1024,5120]{1,0:T(8,128)(2,1)S(1)} %copy-done), custom_call_target="tpu_custom_call" | custom-call | flops 1 | bytes 1 | tf_op jit(solution)/shard_map/mix/pallas_call | solution.py:301
  173.2 2.7 %mix_sent.5.refs_1_ = bf16[128,2560]{1,0:T(8,128)(2,1)S(1)} custom-call(s32[12]{0:T(128)S(1)} %stack.51.places_ref, bf16[128,1024]{1,0:T(8,128)(2,1)S(1)} %collective-permute-done.26.rows_ref, bf16[128,2560]{1,0:T(8,128)(2,1)S(1)} %collective-permute-done.9.refs_0_, bf16[128,2560]{1,0:T(8,128)(2,1)S(1)} %collective-permute-done.12.refs_1_, ...), custom_call_target="tpu_custom_call" | custom-call | flops 1 | bytes 1 | tf_op jit(solution)/shard_map/mix_sent/pallas_call | solution.py:357
  176.8 1.2 added.14.refs_4_
  177.9 7.8 %collective-permute-done.34.refs_3_ = bf16[128,2560]{1,0:T(8,128)(2,1)S(1)} collective-permute-done((bf16[128,2560]{1,0:T(8,128)(2,1)S(1)}, bf16[128,2560]{1,0:T(8,128)(2,1)S(1)}, u32[]{:S(2)}, u32[]{:S(2)}) %collective-permute-start.34) | collective-permute-done | bytes 655392 | tf_op jit(solution)/shard_map/ppermute | solution.py:435
  185.7 1.2 added.15
  (79 shorter events, 9.6 us)
Async XLA Ops:
  0.0 9.4 %copy-start.2 = (bf16[5120,128]{1,0:T(8,128)(2,1)S(1)}, bf16[5120,128]{1,0:T(8,128)(2,1)}, u32[]{:S(2)}) copy-start(bf16[5120,128]{1,0:T(8,128)(2,1)} %refs_3_.7) | copy-start | bytes 3932164
  0.0 37.5 %collective-permute-start = (bf16[512,1280]{1,0:T(8,128)(2,1)}, bf16[512,1280]{1,0:T(8,128)(2,1)S(1)}, u32[]{:S(2)}, u32[]{:S(2)}) collective-permute-start(bf16[512,1280]{1,0:T(8,128)(2,1)} %refs_0_.1), channel_id=1, source_target_pairs={{0,1},{1,0},{2,3},{3,2},{4,5},{5,4},{6,7},{7,6},{8,9},{9,8},{10,11... | collective-permute-start | bytes 3932168 | tf_op jit(solution)/shard_map/ppermute | solution.py:432
  0.0 1.4 copy-start.4
  2.3 20.9 %collective-permute-start.3 = (bf16[256,1280]{1,0:T(8,128)(2,1)}, bf16[256,1280]{1,0:T(8,128)(2,1)}, u32[]{:S(2)}, u32[]{:S(2)}) collective-permute-start(bf16[256,1280]{1,0:T(8,128)(2,1)} %get-tuple-element.53), channel_id=1, source_target_pairs={{1,2},{2,1},{5,6},{6,5},{9,10},{10,9},{13,14},{14,13},{17,18},{18,... | collective-permute-start | bytes 1966088 | tf_op jit(solution)/shard_map/ppermute | solution.py:435
  7.3 28.8 %collective-permute-start.5 = (bf16[256,1280]{1,0:T(8,128)(2,1)S(1)}, bf16[256,1280]{1,0:T(8,128)(2,1)}, u32[]{:S(2)}, u32[]{:S(2)}) collective-permute-start(bf16[256,1280]{1,0:T(8,128)(2,1)S(1)} %get-tuple-element.58), channel_id=1, source_target_pairs={{1,2},{2,1},{5,6},{6,5},{9,10},{10,9},{13,14},{14,13},{17,18},{18,... | collective-permute-start | bytes 1966088 | tf_op jit(solution)/shard_map/ppermute | solution.py:435
  9.4 4.0 %copy-start.1 = (bf16[5120,1024]{1,0:T(8,128)(2,1)S(1)}, bf16[5120,1024]{1,0:T(8,128)(2,1)}, u32[]{:S(2)}) copy-start(bf16[5120,1024]{1,0:T(8,128)(2,1)} %refs_2_.8) | copy-start | bytes 31457284
  13.4 1.3 copy-start.3
  14.7 1.3 copy-start.5
  16.0 8.6 %copy-start = (bf16[1024,5120]{1,0:T(8,128)(2,1)S(1)}, bf16[1024,5120]{1,0:T(8,128)(2,1)}, u32[]{:S(2)}) copy-start(bf16[1024,5120]{1,0:T(8,128)(2,1)} %w_ref.19) | copy-start | bytes 31457284
  23.2 21.6 %collective-permute-start.4 = (bf16[256,1280]{1,0:T(8,128)(2,1)}, bf16[256,1280]{1,0:T(8,128)(2,1)S(1)}, u32[]{:S(2)}, u32[]{:S(2)}) collective-permute-start(bf16[256,1280]{1,0:T(8,128)(2,1)} %collective-permute-done.3.refs_0_), channel_id=1, source_target_pairs={{1,0},{2,3},{5,4},{6,7},{9,8},{10,11},{13,12},{14,15},{17,16},{18,... | collective-permute-start | bytes 1966088 | tf_op jit(solution)/shard_map/ppermute | solution.py:438
  36.1 23.0 %collective-permute-start.7 = (bf16[256,1280]{1,0:T(8,128)(2,1)}, bf16[256,1280]{1,0:T(8,128)(2,1)S(1)}, u32[]{:S(2)}, u32[]{:S(2)}) collective-permute-start(bf16[256,1280]{1,0:T(8,128)(2,1)} %collective-permute-done.5.refs_2_), channel_id=1, source_target_pairs={{1,0},{2,3},{5,4},{6,7},{9,8},{10,11},{13,12},{14,15},{17,16},{18,... | collective-permute-start | bytes 1966088 | tf_op jit(solution)/shard_map/ppermute | solution.py:438
  37.6 19.6 %collective-permute-start.1 = (bf16[256,1280]{1,0:T(8,128)(2,1)S(1)}, bf16[256,1280]{1,0:T(8,128)(2,1)S(1)}, u32[]{:S(2)}, u32[]{:S(2)}) collective-permute-start(bf16[256,1280]{1,0:T(8,128)(2,1)S(1)} %get-tuple-element.51), channel_id=1, source_target_pairs={{1,2},{2,1},{5,6},{6,5},{9,10},{10,9},{13,14},{14,13},{17,18},{18,... | collective-permute-start | bytes 1966088 | tf_op jit(solution)/shard_map/ppermute | solution.py:435
  41.2 36.8 %slice-start = ((s8[10485760]{0:T(1024)(128)(4,1)}), s8[4194304]{0:T(1024)(128)(4,1)S(1)}, s32[]{:S(2)}) async-start(s8[10485760]{0:T(1024)(128)(4,1)} %bitcast.14), calls=%async_computation | async-start | bytes 8388608
  41.2 36.8 %slice-start.1 = ((s8[10485760]{0:T(1024)(128)(4,1)}), s8[4194304]{0:T(1024)(128)(4,1)S(1)}, s32[]{:S(2)}) async-start(s8[10485760]{0:T(1024)(128)(4,1)} %bitcast.14), calls=%async_computation.1 | async-start | bytes 8388608
  44.9 14.2 %copy-start.8 = (bf16[256,1280]{1,0:T(8,128)(2,1)}, bf16[256,1280]{1,0:T(8,128)(2,1)S(1)}, u32[]{:S(2)}) copy-start(bf16[256,1280]{1,0:T(8,128)(2,1)S(1)} %collective-permute-done.4.refs_1_) | copy-start | bytes 1966084
  44.9 33.2 %slice-start.2 = ((s8[10485760]{0:T(1024)(128)(4,1)}), s8[2097152]{0:T(1024)(128)(4,1)S(1)}, s32[]{:S(2)}) async-start(s8[10485760]{0:T(1024)(128)(4,1)} %bitcast.14), calls=%async_computation.2 | async-start | bytes 4194304
  44.9 24.2 %collective-permute-start.6 = (bf16[256,1280]{1,0:T(8,128)(2,1)S(1)}, bf16[256,1280]{1,0:T(8,128)(2,1)S(1)}, u32[]{:S(2)}, u32[]{:S(2)}) collective-permute-start(bf16[256,1280]{1,0:T(8,128)(2,1)S(1)} %get-tuple-element.66), channel_id=1, source_target_pairs={{1,2},{2,1},{5,6},{6,5},{9,10},{10,9},{13,14},{14,13},{17,18},{18,... | collective-permute-start | bytes 1966088 | tf_op jit(solution)/shard_map/ppermute | solution.py:435
  48.9 20.2 %collective-permute-start.9 = (bf16[128,2560]{1,0:T(8,128)(2,1)S(1)}, bf16[128,2560]{1,0:T(8,128)(2,1)S(1)}, u32[]{:S(2)}, u32[]{:S(2)}) collective-permute-start(bf16[128,2560]{1,0:T(8,128)(2,1)S(1)} %eighth.2), channel_id=1, source_target_pairs={{0,1},{3,2},{4,5},{7,6},{8,9},{11,10},{12,13},{15,14},{16,17},{19,... | collective-permute-start | bytes 1966088 | tf_op jit(solution)/shard_map/ppermute | solution.py:441
  57.1 27.9 %collective-permute-start.2 = (bf16[256,1280]{1,0:T(8,128)(2,1)S(1)}, bf16[256,1280]{1,0:T(8,128)(2,1)S(1)}, u32[]{:S(2)}, u32[]{:S(2)}) collective-permute-start(bf16[256,1280]{1,0:T(8,128)(2,1)S(1)} %collective-permute-done.1.refs_0_), channel_id=1, source_target_pairs={{1,0},{2,3},{5,4},{6,7},{9,8},{10,11},{13,12},{14,15},{17,16},{18,... | collective-permute-start | bytes 1966088 | tf_op jit(solution)/shard_map/ppermute | solution.py:438
  58.5 26.6 %copy-start.13 = (f32[128]{0:T(128)S(1)}, f32[128]{0:T(128)}, u32[]{:S(2)}) copy-start(f32[128]{0:T(128)} %param.18) | copy-start | bytes 1540
  59.1 26.0 %copy-start.6 = (f32[512,128]{1,0:T(8,128)S(1)}, f32[512,128]{1,0:T(8,128)}, u32[]{:S(2)}) copy-start(f32[512,128]{1,0:T(8,128)} %constant.29.clone.refs_5_.refs_7_.refs_8_) | copy-start | bytes 786436
  59.1 26.0 %copy-start.7 = (f32[512,128]{1,0:T(8,128)S(1)}, f32[512,128]{1,0:T(8,128)}, u32[]{:S(2)}) copy-start(f32[512,128]{1,0:T(8,128)} %constant.30.clone.refs_6_.refs_8_.refs_9_) | copy-start | bytes 786436
  59.1 0.8 copy-start.10
  69.1 19.6 %collective-permute-start.10 = (bf16[128,2560]{1,0:T(8,128)(2,1)S(1)}, bf16[128,2560]{1,0:T(8,128)(2,1)S(1)}, u32[]{:S(2)}, u32[]{:S(2)}) collective-permute-start(bf16[128,2560]{1,0:T(8,128)(2,1)S(1)} %collective-permute-done.9.refs_0_), channel_id=1, source_target_pairs={{0,8},{4,12},{8,0},{12,4},{16,24},{20,28},{24,16},{28,20},{1,9},{5... | collective-permute-start | bytes 1966088 | tf_op jit(solution)/shard_map/ppermute | solution.py:444
  70.6 18.1 %collective-permute-start.11 = (bf16[128,2560]{1,0:T(8,128)(2,1)S(1)}, bf16[128,2560]{1,0:T(8,128)(2,1)S(1)}, u32[]{:S(2)}, u32[]{:S(2)}) collective-permute-start(bf16[128,2560]{1,0:T(8,128)(2,1)S(1)} %collective-permute-done.9.refs_0_), channel_id=1, source_target_pairs={{0,16},{4,20},{8,24},{12,28},{16,0},{20,4},{24,8},{28,12},{1,17},{... | collective-permute-start | bytes 1966088 | tf_op jit(solution)/shard_map/ppermute | solution.py:444
  72.1 16.6 %collective-permute-start.12 = (bf16[128,2560]{1,0:T(8,128)(2,1)S(1)}, bf16[128,2560]{1,0:T(8,128)(2,1)S(1)}, u32[]{:S(2)}, u32[]{:S(2)}) collective-permute-start(bf16[128,2560]{1,0:T(8,128)(2,1)S(1)} %eighth.3), channel_id=1, source_target_pairs={{0,1},{3,2},{4,5},{7,6},{8,9},{11,10},{12,13},{15,14},{16,17},{19,... | collective-permute-start | bytes 1966088 | tf_op jit(solution)/shard_map/ppermute | solution.py:441
  73.4 15.9 %collective-permute-start.8 = (bf16[256,1280]{1,0:T(8,128)(2,1)S(1)}, bf16[256,1280]{1,0:T(8,128)(2,1)S(1)}, u32[]{:S(2)}, u32[]{:S(2)}) collective-permute-start(bf16[256,1280]{1,0:T(8,128)(2,1)S(1)} %collective-permute-done.6.refs_0_.refs_1_), channel_id=1, source_target_pairs={{1,0},{2,3},{5,4},{6,7},{9,8},{10,11},{13,12},{14,15},{17,16},{18,... | collective-permute-start | bytes 1966088 | tf_op jit(solution)/shard_map/ppermute | solution.py:438
  78.1 1.1 copy-start.9
  79.2 1.1 copy-start.11
  85.1 2.5 %copy-start.12 = (f32[128]{0:T(128)S(1)}, f32[128]{0:T(128)}, u32[]{:S(2)}) copy-start(f32[128]{0:T(128)} %param.19) | copy-start | bytes 1540
  87.6 1.8 copy-start.14
  90.6 3.6 %collective-permute-start.13 = (bf16[128,256]{1,0:T(8,128)(2,1)S(1)}, bf16[128,256]{1,0:T(8,128)(2,1)S(1)}, u32[]{:S(2)}, u32[]{:S(2)}) collective-permute-start(bf16[128,256]{1,0:T(8,128)(2,1)S(1)} %get-tuple-element.77), channel_id=1, source_target_pairs={{0,4},{4,0},{8,12},{12,8},{16,20},{20,16},{24,28},{28,24},{1,5},{5... | collective-permute-start | bytes 196616 | tf_op jit(solution)/shard_map/ppermute | solution.py:444
  90.7 5.0 %collective-permute-start.14 = (bf16[128,256]{1,0:T(8,128)(2,1)S(1)}, bf16[128,256]{1,0:T(8,128)(2,1)S(1)}, u32[]{:S(2)}, u32[]{:S(2)}) collective-permute-start(bf16[128,256]{1,0:T(8,128)(2,1)S(1)} %get-tuple-element.77), channel_id=1, source_target_pairs={{0,8},{4,12},{8,0},{12,4},{16,24},{20,28},{24,16},{28,20},{1,9},{5... | collective-permute-start | bytes 196616 | tf_op jit(solution)/shard_map/ppermute | solution.py:444
  91.3 8.2 %collective-permute-start.15 = (bf16[128,256]{1,0:T(8,128)(2,1)S(1)}, bf16[128,256]{1,0:T(8,128)(2,1)S(1)}, u32[]{:S(2)}, u32[]{:S(2)}) collective-permute-start(bf16[128,256]{1,0:T(8,128)(2,1)S(1)} %get-tuple-element.77), channel_id=1, source_target_pairs={{0,12},{4,8},{8,4},{12,0},{16,28},{20,24},{24,20},{28,16},{1,13},{... | collective-permute-start | bytes 196616 | tf_op jit(solution)/shard_map/ppermute | solution.py:444
  92.6 6.9 %collective-permute-start.16 = (bf16[128,256]{1,0:T(8,128)(2,1)S(1)}, bf16[128,256]{1,0:T(8,128)(2,1)S(1)}, u32[]{:S(2)}, u32[]{:S(2)}) collective-permute-start(bf16[128,256]{1,0:T(8,128)(2,1)S(1)} %get-tuple-element.77), channel_id=1, source_target_pairs={{0,16},{4,20},{8,24},{12,28},{16,0},{20,4},{24,8},{28,12},{1,17},{... | collective-permute-start | bytes 196616 | tf_op jit(solution)/shard_map/ppermute | solution.py:444
  93.1 6.4 %collective-permute-start.17 = (bf16[128,256]{1,0:T(8,128)(2,1)S(1)}, bf16[128,256]{1,0:T(8,128)(2,1)S(1)}, u32[]{:S(2)}, u32[]{:S(2)}) collective-permute-start(bf16[128,256]{1,0:T(8,128)(2,1)S(1)} %get-tuple-element.77), channel_id=1, source_target_pairs={{0,20},{4,16},{8,28},{12,24},{16,4},{20,0},{24,12},{28,8},{1,21},{... | collective-permute-start | bytes 196616 | tf_op jit(solution)/shard_map/ppermute | solution.py:444
  94.3 5.6 %collective-permute-start.18 = (bf16[128,256]{1,0:T(8,128)(2,1)S(1)}, bf16[128,256]{1,0:T(8,128)(2,1)S(1)}, u32[]{:S(2)}, u32[]{:S(2)}) collective-permute-start(bf16[128,256]{1,0:T(8,128)(2,1)S(1)} %get-tuple-element.77), channel_id=1, source_target_pairs={{0,24},{4,28},{8,16},{12,20},{16,8},{20,12},{24,0},{28,4},{1,25},{... | collective-permute-start | bytes 196616 | tf_op jit(solution)/shard_map/ppermute | solution.py:444
  95.7 5.3 %collective-permute-start.19 = (bf16[128,256]{1,0:T(8,128)(2,1)S(1)}, bf16[128,256]{1,0:T(8,128)(2,1)S(1)}, u32[]{:S(2)}, u32[]{:S(2)}) collective-permute-start(bf16[128,256]{1,0:T(8,128)(2,1)S(1)} %get-tuple-element.77), channel_id=1, source_target_pairs={{0,28},{4,24},{8,20},{12,16},{16,12},{20,8},{24,4},{28,0},{1,29},{... | collective-permute-start | bytes 196616 | tf_op jit(solution)/shard_map/ppermute | solution.py:444
  101.0 16.8 %collective-permute-start.21 = (bf16[128,2560]{1,0:T(8,128)(2,1)S(1)}, bf16[128,2560]{1,0:T(8,128)(2,1)S(1)}, u32[]{:S(2)}, u32[]{:S(2)}) collective-permute-start(bf16[128,2560]{1,0:T(8,128)(2,1)S(1)} %collective-permute-done.9.refs_0_), channel_id=1, source_target_pairs={{0,4},{4,0},{8,12},{12,8},{16,20},{20,16},{24,28},{28,24},{1,5},{5... | collective-permute-start | bytes 1966088 | tf_op jit(solution)/shard_map/ppermute | solution.py:444
  101.1 16.8 %collective-permute-start.22 = (bf16[128,2560]{1,0:T(8,128)(2,1)S(1)}, bf16[128,2560]{1,0:T(8,128)(2,1)S(1)}, u32[]{:S(2)}, u32[]{:S(2)}) collective-permute-start(bf16[128,2560]{1,0:T(8,128)(2,1)S(1)} %collective-permute-done.12.refs_1_), channel_id=1, source_target_pairs={{0,4},{4,0},{8,12},{12,8},{16,20},{20,16},{24,28},{28,24},{1,5},{5... | collective-permute-start | bytes 1966088 | tf_op jit(solution)/shard_map/ppermute | solution.py:444
  101.5 16.3 %collective-permute-start.23 = (bf16[128,2560]{1,0:T(8,128)(2,1)S(1)}, bf16[128,2560]{1,0:T(8,128)(2,1)S(1)}, u32[]{:S(2)}, u32[]{:S(2)}) collective-permute-start(bf16[128,2560]{1,0:T(8,128)(2,1)S(1)} %collective-permute-done.10.refs_2_), channel_id=1, source_target_pairs={{0,4},{4,0},{8,12},{12,8},{16,20},{20,16},{24,28},{28,24},{1,5},{5... | collective-permute-start | bytes 1966088 | tf_op jit(solution)/shard_map/ppermute | solution.py:444
  101.6 16.3 %collective-permute-start.24 = (bf16[128,2560]{1,0:T(8,128)(2,1)S(1)}, bf16[128,2560]{1,0:T(8,128)(2,1)S(1)}, u32[]{:S(2)}, u32[]{:S(2)}) collective-permute-start(bf16[128,2560]{1,0:T(8,128)(2,1)S(1)} %collective-permute-done.11.refs_3_), channel_id=1, source_target_pairs={{0,4},{4,0},{8,12},{12,8},{16,20},{20,16},{24,28},{28,24},{1,5},{5... | collective-permute-start | bytes 1966088 | tf_op jit(solution)/shard_map/ppermute | solution.py:444
  106.3 10.3 %collective-permute-start.20 = (bf16[128,1024]{1,0:T(8,128)(2,1)S(1)}, bf16[128,1024]{1,0:T(8,128)(2,1)S(1)}, u32[]{:S(2)}, u32[]{:S(2)}) collective-permute-start(bf16[128,1024]{1,0:T(8,128)(2,1)S(1)} %attention.3.rows_ref), channel_id=1, source_target_pairs={{0,1},{3,2},{4,5},{7,6},{8,9},{11,10},{12,13},{15,14},{16,17},{19,... | collective-permute-start | bytes 786440 | tf_op jit(solution)/shard_map/ppermute | solution.py:441
  116.5 19.6 %collective-permute-start.25 = (bf16[128,2560]{1,0:T(8,128)(2,1)S(1)}, bf16[128,2560]{1,0:T(8,128)(2,1)S(1)}, u32[]{:S(2)}, u32[]{:S(2)}) collective-permute-start(bf16[128,2560]{1,0:T(8,128)(2,1)S(1)} %mix.9.refs_0_), channel_id=1, source_target_pairs={{0,1},{3,2},{4,5},{7,6},{8,9},{11,10},{12,13},{15,14},{16,17},{19,... | collective-permute-start | bytes 1966088 | tf_op jit(solution)/shard_map/ppermute | solution.py:441
  120.7 27.6 %collective-permute-start.29 = (bf16[128,2560]{1,0:T(8,128)(2,1)S(1)}, bf16[128,2560]{1,0:T(8,128)(2,1)S(1)}, u32[]{:S(2)}, u32[]{:S(2)}) collective-permute-start(bf16[128,2560]{1,0:T(8,128)(2,1)S(1)} %added.8), channel_id=1, source_target_pairs={{1,2},{2,1},{5,6},{6,5},{9,10},{10,9},{13,14},{14,13},{17,18},{18,... | collective-permute-start | bytes 1966088 | tf_op jit(solution)/shard_map/ppermute | solution.py:435
  127.3 17.6 %collective-permute-start.27 = (bf16[128,1024]{1,0:T(8,128)(2,1)S(1)}, bf16[128,1024]{1,0:T(8,128)(2,1)S(1)}, u32[]{:S(2)}, u32[]{:S(2)}) collective-permute-start(bf16[128,1024]{1,0:T(8,128)(2,1)S(1)} %attention.4.rows_ref), channel_id=1, source_target_pairs={{0,1},{3,2},{4,5},{7,6},{8,9},{11,10},{12,13},{15,14},{16,17},{19,... | collective-permute-start | bytes 786440 | tf_op jit(solution)/shard_map/ppermute | solution.py:441
  136.3 25.9 %collective-permute-start.30 = (bf16[128,2560]{1,0:T(8,128)(2,1)S(1)}, bf16[128,2560]{1,0:T(8,128)(2,1)S(1)}, u32[]{:S(2)}, u32[]{:S(2)}) collective-permute-start(bf16[128,2560]{1,0:T(8,128)(2,1)S(1)} %added.9), channel_id=1, source_target_pairs={{1,2},{2,1},{5,6},{6,5},{9,10},{10,9},{13,14},{14,13},{17,18},{18,... | collective-permute-start | bytes 1966088 | tf_op jit(solution)/shard_map/ppermute | solution.py:435
  144.9 19.9 %collective-permute-start.28 = (bf16[128,2560]{1,0:T(8,128)(2,1)S(1)}, bf16[128,2560]{1,0:T(8,128)(2,1)S(1)}, u32[]{:S(2)}, u32[]{:S(2)}) collective-permute-start(bf16[128,2560]{1,0:T(8,128)(2,1)S(1)} %mix.10.refs_0_), channel_id=1, source_target_pairs={{0,1},{3,2},{4,5},{7,6},{8,9},{11,10},{12,13},{15,14},{16,17},{19,... | collective-permute-start | bytes 1966088 | tf_op jit(solution)/shard_map/ppermute | solution.py:441
  148.4 19.3 %collective-permute-start.31 = (bf16[128,2560]{1,0:T(8,128)(2,1)S(1)}, bf16[128,2560]{1,0:T(8,128)(2,1)S(1)}, u32[]{:S(2)}, u32[]{:S(2)}) collective-permute-start(bf16[128,2560]{1,0:T(8,128)(2,1)S(1)} %added.10), channel_id=1, source_target_pairs={{1,0},{2,3},{5,4},{6,7},{9,8},{10,11},{13,12},{14,15},{17,16},{18,... | collective-permute-start | bytes 1966088 | tf_op jit(solution)/shard_map/ppermute | solution.py:438
  153.1 14.7 %collective-permute-start.26 = (bf16[128,1024]{1,0:T(8,128)(2,1)S(1)}, bf16[128,1024]{1,0:T(8,128)(2,1)S(1)}, u32[]{:S(2)}, u32[]{:S(2)}) collective-permute-start(bf16[128,1024]{1,0:T(8,128)(2,1)S(1)} %get-tuple-element.92.rows_ref), channel_id=1, source_target_pairs={{0,1},{3,2},{4,5},{7,6},{8,9},{11,10},{12,13},{15,14},{16,17},{19,... | collective-permute-start | bytes 786440 | tf_op jit(solution)/shard_map/ppermute | solution.py:441
  157.2 19.6 %collective-permute-start.35 = (bf16[128,2560]{1,0:T(8,128)(2,1)S(1)}, bf16[128,2560]{1,0:T(8,128)(2,1)S(1)}, u32[]{:S(2)}, u32[]{:S(2)}) collective-permute-start(bf16[128,2560]{1,0:T(8,128)(2,1)S(1)} %added.11), channel_id=1, source_target_pairs={{1,2},{2,1},{5,6},{6,5},{9,10},{10,9},{13,14},{14,13},{17,18},{18,... | collective-permute-start | bytes 1966088 | tf_op jit(solution)/shard_map/ppermute | solution.py:435
  162.3 15.6 %collective-permute-start.33 = (bf16[128,2560]{1,0:T(8,128)(2,1)S(1)}, bf16[128,2560]{1,0:T(8,128)(2,1)S(1)}, u32[]{:S(2)}, u32[]{:S(2)}) collective-permute-start(bf16[128,2560]{1,0:T(8,128)(2,1)S(1)} %added.12), channel_id=1, source_target_pairs={{1,0},{2,3},{5,4},{6,7},{9,8},{10,11},{13,12},{14,15},{17,16},{18,... | collective-permute-start | bytes 1966088 | tf_op jit(solution)/shard_map/ppermute | solution.py:438
  164.9 20.8 %collective-permute-start.34 = (bf16[128,2560]{1,0:T(8,128)(2,1)S(1)}, bf16[128,2560]{1,0:T(8,128)(2,1)S(1)}, u32[]{:S(2)}, u32[]{:S(2)}) collective-permute-start(bf16[128,2560]{1,0:T(8,128)(2,1)S(1)} %added.13), channel_id=1, source_target_pairs={{1,2},{2,1},{5,6},{6,5},{9,10},{10,9},{13,14},{14,13},{17,18},{18,... | collective-permute-start | bytes 1966088 | tf_op jit(solution)/shard_map/ppermute | solution.py:435
  167.8 17.9 %collective-permute-start.32 = (bf16[128,2560]{1,0:T(8,128)(2,1)S(1)}, bf16[128,2560]{1,0:T(8,128)(2,1)S(1)}, u32[]{:S(2)}, u32[]{:S(2)}) collective-permute-start(bf16[128,2560]{1,0:T(8,128)(2,1)S(1)} %mix.13.refs_0_), channel_id=1, source_target_pairs={{0,1},{3,2},{4,5},{7,6},{8,9},{11,10},{12,13},{15,14},{16,17},{19,... | collective-permute-start | bytes 1966088 | tf_op jit(solution)/shard_map/ppermute | solution.py:441

commit v12 on v10

--- a/solution.py
+++ b/solution.py
@@ -459,9 +459,10 @@
     from_mid = [across(array) for array in halves(hidden_in)]
     accs = partial_projection(places, OWN, [[hidden_in]], weights, None)
     from_mid[0], accs = lax.optimization_barrier((from_mid[0], accs))
-    to_outer = [outward(array) for array in from_mid]
+    to_outer = [outward(from_mid[0])]
     accs = partial_projection(after(places, from_mid[1]), NEAR, [[from_near]], weights, accs)
     from_near = halves(from_near)
+    to_outer.append(outward(after(from_mid[1], from_near)))
     to_inner = [across(from_near[0])]
     to_inner.append(across(after(from_near[1], (to_outer[0], accs))))
     end = [outward(array) for array in to_inner]
@@ -469,7 +470,7 @@
     if spread:
         first, second = (eighth(places, i, w_out, share) for i in (0, 1))
         pieces[0] = inward(after(first, to_outer[0]))
-        cue = (to_inner[1], to_outer[1])
+        cue = to_outer[1]
         pieces[6] = inward(after(second, cue))
         first = after(pieces[0], cue)
         pieces[2], pieces[4] = between(first, 2), between(first, 4)

time: 187 us -> 184 us (0.984)
  starting transfers between devices: 57 us -> 48.5 us
  waiting for transfers between devices: 55.3 us -> 61.8 us
    ppermute x8, starting transfers between devices: 29.4 us -> 20 us  [inward(): return lax.ppermute(array, 'tensor', [(0, 1), (3, 2)])]
    ppermute x6, waiting for transfers between devices: 29.9 us -> 38.4 us  [outward(): return lax.ppermute(array, 'tensor', [(1, 0), (2, 3)])]
    ppermute x8, waiting for transfers between devices: 12.4 us -> 8.81 us  [inward(): return lax.ppermute(array, 'tensor', [(0, 1), (3, 2)])]
    unnamed x36 -> x40, local copies, waits for them, and re-layouts: 11 us -> 9.95 us
  transfers between devices with their start and end apart: 36 -> 36, of which waited for: 12 -> 11; matrix products, arithmetic and copies ran while one was open for 0% -> 0% of each run, Pallas kernels for 30% -> 30%
where the time goes in v12:
time: 184 us
  Pallas kernels  61.8 us (34%)
  waiting for transfers between devices  61.8 us (34%)
  starting transfers between devices  48.5 us (26%)
  local copies, waits for them, and re-layouts  10 us (5%)
    ppermute x6, waiting for transfers between devices, outward(): return lax.ppermute(array, 'tensor', [(1, 0), (2, 3)])  38.4 us
    ppermute x8, starting transfers between devices, inward(): return lax.ppermute(array, 'tensor', [(0, 1), (3, 2)])  20 us
    pallas_call x8, Pallas kernels, mix(): pl.pallas_call(mix_kernel, grid=(tiles,), in_specs=[whole(rows, depth), p...  16.5 us
    ppermute x1, waiting for transfers between devices, swap(): return lax.ppermute(array, 'tensor', [(0, 1), (1, 0), (2, 3), (3, 2)])  13 us
    pallas_call x3, Pallas kernels, attention(): pl.pallas_call(functools.partial(attention_kernel, slots, n_parts, len(ot...  12.7 us
    pallas_call x3, Pallas kernels, partial_projection(): pl.pallas_call(functools.partial(partial_kernel, [len(part) for part in p...  11.6 us
    ppermute x13, starting transfers between devices, between(): return lax.ppermute(array, 'cand', [(i, i ^ offset) for i in range(n_cand)])  11 us
    unnamed x40, local copies, waits for them, and re-layouts  9.95 us
  transfers between devices with their start and end apart: 36, of which 11 were waited for; matrix products, arithmetic and copies ran while one was open for 0% of the time, Pallas kernels for 30%

profile of v12, /device:TPU:0, one launch (start us, length us, event | category | flops | bytes accessed | tf_op | source)
XLA Modules:
  0.0 183.5 jit_solution(7313539493860683426)
XLA Ops:
  0.0 3.0 %collective-permute-start = (bf16[512,1280]{1,0:T(8,128)(2,1)}, bf16[512,1280]{1,0:T(8,128)(2,1)S(1)}, u32[]{:S(2)}, u32[]{:S(2)}) collective-permute-start(bf16[512,1280]{1,0:T(8,128)(2,1)} %refs_0_.1), channel_id=1, source_target_pairs={{0,1},{1,0},{2,3},{3,2},{4,5},{5,4},{6,7},{7,6},{8,9},{9,8},{10,11... | collective-permute-start | bytes 3932168 | tf_op jit(solution)/shard_map/ppermute | solution.py:432
  3.0 1.3 copy-done.4
  4.4 1.2 halves.3
  5.5 1.5 collective-permute-start.3
  7.9 4.0 %copy-done.1 = bf16[5120,1024]{1,0:T(8,128)(2,1)S(1)} copy-done((bf16[5120,1024]{1,0:T(8,128)(2,1)S(1)}, bf16[5120,1024]{1,0:T(8,128)(2,1)}, u32[]{:S(2)}) %copy-start.1) | copy-done | bytes 10485784
  11.9 1.3 copy-done.3
  13.2 1.3 copy-done.5
  14.5 3.4 %partial_projection.3 = (f32[512,1024]{1,0:T(8,128)S(1)}, f32[512,128]{1,0:T(8,128)S(1)}, f32[512,128]{1,0:T(8,128)S(1)}) custom-call(s32[12]{0:T(128)S(1)} %stack.51.places_ref, bf16[512,1280]{1,0:T(8,128)(2,1)S(1)} %copy-done.5, bf16[5120,1024]{1,0:T(8,128)(2,1)S(1)} %copy-done.1, bf16[5120,128]{1,0:T(8,128)(2,1)S(1)} %copy-done.2, ...), custom_call_target="tpu_custom_call" | custom-call | flops 1 | bytes 1 | tf_op jit(solution)/shard_map/partial_projection/pallas_call | solution.py:96
  17.9 1.3 collective-permute-start.4
  19.9 13.0 %collective-permute-done.ref.refs_0_ = bf16[512,1280]{1,0:T(8,128)(2,1)S(1)} collective-permute-done((bf16[512,1280]{1,0:T(8,128)(2,1)}, bf16[512,1280]{1,0:T(8,128)(2,1)S(1)}, u32[]{:S(2)}, u32[]{:S(2)}) %collective-permute-start) | collective-permute-done | bytes 1310752 | tf_op jit(solution)/shard_map/ppermute | solution.py:432
  32.9 0.7 collective-permute-start.1
  33.6 1.3 collective-permute-start.7
  34.9 11.9 %collective-permute-done.4.refs_1_ = bf16[256,1280]{1,0:T(8,128)(2,1)S(1)} collective-permute-done((bf16[256,1280]{1,0:T(8,128)(2,1)}, bf16[256,1280]{1,0:T(8,128)(2,1)S(1)}, u32[]{:S(2)}, u32[]{:S(2)}) %collective-permute-start.4) | collective-permute-done | bytes 655392 | tf_op jit(solution)/shard_map/ppermute | solution.py:438
  46.9 1.6 collective-permute-start.9
  48.5 3.6 %partial_projection.4 = (f32[512,1024]{1,0:T(8,128)S(1)}, f32[512,128]{1,0:T(8,128)S(1)}, f32[512,128]{1,0:T(8,128)S(1)}) custom-call(s32[12]{0:T(128)S(1)} %stack.51.places_ref, bf16[512,1280]{1,0:T(8,128)(2,1)S(1)} %collective-permute-done.ref.refs_0_, bf16[5120,1024]{1,0:T(8,128)(2,1)S(1)} %copy-done.1, bf16[5120,128]{1,0:T(8,128)(2,1)S(1)} %copy-done.2, ...), custom_call_target="tpu_custom_call" | custom-call | flops 1 | bytes 1 | tf_op jit(solution)/shard_map/partial_projection/pallas_call | solution.py:96
  52.2 0.8 collective-permute-start.6
  53.0 1.4 collective-permute-start.2
  55.1 5.9 %collective-permute-done.7.refs_3_ = bf16[256,1280]{1,0:T(8,128)(2,1)S(1)} collective-permute-done((bf16[256,1280]{1,0:T(8,128)(2,1)}, bf16[256,1280]{1,0:T(8,128)(2,1)S(1)}, u32[]{:S(2)}, u32[]{:S(2)}) %collective-permute-start.7) | collective-permute-done | bytes 655392 | tf_op jit(solution)/shard_map/ppermute | solution.py:438
  60.9 0.8 copy-done.12
  61.8 2.0 %collective-permute-start.10 = (bf16[128,2560]{1,0:T(8,128)(2,1)S(1)}, bf16[128,2560]{1,0:T(8,128)(2,1)S(1)}, u32[]{:S(2)}, u32[]{:S(2)}) collective-permute-start(bf16[128,2560]{1,0:T(8,128)(2,1)S(1)} %collective-permute-done.9.refs_0_), channel_id=1, source_target_pairs={{0,8},{4,12},{8,0},{12,4},{16,24},{20,28},{24,16},{28,20},{1,9},{5... | collective-permute-start | bytes 1966088 | tf_op jit(solution)/shard_map/ppermute | solution.py:444
  63.7 1.5 collective-permute-start.11
  65.3 3.1 %collective-permute-start.12 = (bf16[128,2560]{1,0:T(8,128)(2,1)S(1)}, bf16[128,2560]{1,0:T(8,128)(2,1)S(1)}, u32[]{:S(2)}, u32[]{:S(2)}) collective-permute-start(bf16[128,2560]{1,0:T(8,128)(2,1)S(1)} %eighth.3), channel_id=1, source_target_pairs={{0,1},{3,2},{4,5},{7,6},{8,9},{11,10},{12,13},{15,14},{16,17},{19,... | collective-permute-start | bytes 1966088 | tf_op jit(solution)/shard_map/ppermute | solution.py:441
  68.3 1.3 collective-permute-start.8
  69.7 1.1 copy-done.13
  70.8 4.6 %partial_projection.5 = (f32[512,1024]{1,0:T(8,128)S(1)}, f32[512,128]{1,0:T(8,128)S(1)}, f32[512,128]{1,0:T(8,128)S(1)}) custom-call(s32[12]{0:T(128)S(1)} %stack.51.places_ref, bf16[256,1280]{1,0:T(8,128)(2,1)} %collective-permute-done.3.refs_0_, bf16[256,1280]{1,0:T(8,128)(2,1)S(1)} %copy-done.11, bf16[256,1280]{1,0:T(8,128)(2,1)S(1)} %copy-done.9, ...), custom_call_target="tpu_custom_call" | custom-call | flops 1 | bytes 1 | tf_op jit(solution)/shard_map/partial_projection/pallas_call | solution.py:96
  75.3 1.0 collective-permute-done.2.refs_1_
  76.4 2.5 %queries.2.refs_0_ = bf16[256,1024]{1,0:T(8,128)(2,1)S(1)} custom-call(s32[12]{0:T(128)S(1)} %stack.51.places_ref, bf16[256,1280]{1,0:T(8,128)(2,1)S(1)} %collective-permute-done.1.refs_0_, bf16[256,1280]{1,0:T(8,128)(2,1)S(1)} %collective-permute-done.2.refs_1_, bf16[5120,1024]{1,0:T(8,128)(2,1)S(1)} %bitcast.15, ...), custom_call_target="tpu_custom_call" | custom-call | flops 1 | bytes 1 | tf_op jit(solution)/shard_map/queries/pallas_call | solution.py:183
  78.9 1.1 keys_values.2.refs_0_.refs_2_
  80.0 8.2 %collective-permute-done.8.refs_1_.refs_2_ = bf16[256,1280]{1,0:T(8,128)(2,1)S(1)} collective-permute-done((bf16[256,1280]{1,0:T(8,128)(2,1)S(1)}, bf16[256,1280]{1,0:T(8,128)(2,1)S(1)}, u32[]{:S(2)}, u32[]{:S(2)}) %collective-permute-start.8) | collective-permute-done | bytes 655392 | tf_op jit(solution)/shard_map/ppermute | solution.py:438
  88.2 1.3 keys_values.3
  89.6 1.7 collective-permute-start.14
  91.4 1.7 collective-permute-start.16
  93.2 2.6 %collective-permute-start.18 = (bf16[128,256]{1,0:T(8,128)(2,1)S(1)}, bf16[128,256]{1,0:T(8,128)(2,1)S(1)}, u32[]{:S(2)}, u32[]{:S(2)}) collective-permute-start(bf16[128,256]{1,0:T(8,128)(2,1)S(1)} %get-tuple-element.81), channel_id=1, source_target_pairs={{0,24},{4,28},{8,16},{12,20},{16,8},{20,12},{24,0},{28,4},{1,25},{... | collective-permute-start | bytes 196616 | tf_op jit(solution)/shard_map/ppermute | solution.py:444
  96.6 2.5 %queries.3.refs_1_ = bf16[256,1024]{1,0:T(8,128)(2,1)S(1)} custom-call(s32[12]{0:T(128)S(1)} %stack.51.places_ref, bf16[256,1280]{1,0:T(8,128)(2,1)S(1)} %collective-permute-done.6.refs_0_.refs_1_, bf16[256,1280]{1,0:T(8,128)(2,1)S(1)} %collective-permute-done.8.refs_1_.refs_2_, bf16[5120,1024]{1,0:T(8,128)(2,1)S(1)} %bitcast.15, ...), custom_call_target="tpu_custom_call" | custom-call | flops 1 | bytes 1 | tf_op jit(solution)/shard_map/queries/pallas_call | solution.py:183
  99.1 1.6 collective-permute-done.19.refs_10_
  100.7 3.6 %attention.3.rows_ref = bf16[128,1024]{1,0:T(8,128)(2,1)S(1)} custom-call(s32[12]{0:T(128)S(1)} %stack.51.places_ref, s32[1]{0:T(128)S(6)} %copy.14.length_ref, bf16[256,1024]{1,0:T(8,128)(2,1)S(1)} %queries.2.refs_0_, bf16[256,1024]{1,0:T(8,128)(2,1)S(1)} %queries.3.refs_1_, bf16[256,256]{1,0:T(8,128)(2,1)S(1)} %keys_values.2.refs_0_.refs_2_, ...), custom_call_target="tpu_custom_call" | custom-call | flops 1 | bytes 1 | tf_op jit(solution)/shard_map/attention/pallas_call | solution.py:272
  104.3 1.6 collective-permute-start.20
  107.0 2.1 %mix.8.refs_0_ = bf16[128,2560]{1,0:T(8,128)(2,1)S(1)} custom-call(bf16[128,1024]{1,0:T(8,128)(2,1)S(1)} %attention.3.rows_ref, bf16[1024,5120]{1,0:T(8,128)(2,1)S(1)} %copy-done), custom_call_target="tpu_custom_call" | custom-call | flops 1 | bytes 1 | tf_op jit(solution)/shard_map/mix/pallas_call | solution.py:301
  109.1 2.1 %mix.9.refs_0_ = bf16[128,2560]{1,0:T(8,128)(2,1)S(1)} custom-call(bf16[128,1024]{1,0:T(8,128)(2,1)S(1)} %attention.3.rows_ref, bf16[1024,5120]{1,0:T(8,128)(2,1)S(1)} %copy-done), custom_call_target="tpu_custom_call" | custom-call | flops 1 | bytes 1 | tf_op jit(solution)/shard_map/mix/pallas_call | solution.py:301
  111.2 3.6 %attention.4.rows_ref = bf16[128,1024]{1,0:T(8,128)(2,1)S(1)} custom-call(s32[12]{0:T(128)S(1)} %stack.51.places_ref, s32[1]{0:T(128)S(6)} %copy.14.length_ref, bf16[256,1024]{1,0:T(8,128)(2,1)S(1)} %queries.2.refs_0_, bf16[256,1024]{1,0:T(8,128)(2,1)S(1)} %queries.3.refs_1_, bf16[256,256]{1,0:T(8,128)(2,1)S(1)} %keys_values.2.refs_0_.refs_2_, ...), custom_call_target="tpu_custom_call" | custom-call | flops 1 | bytes 1 | tf_op jit(solution)/shard_map/attention/pallas_call | solution.py:272
  114.7 1.4 collective-permute-start.26
  116.2 1.3 collective-permute-start.25
  117.5 2.7 %mix_sent.3.refs_1_ = bf16[128,2560]{1,0:T(8,128)(2,1)S(1)} custom-call(s32[12]{0:T(128)S(1)} %stack.51.places_ref, bf16[128,1024]{1,0:T(8,128)(2,1)S(1)} %collective-permute-done.20.rows_ref, bf16[128,2560]{1,0:T(8,128)(2,1)S(1)} %collective-permute-done.9.refs_0_, bf16[128,2560]{1,0:T(8,128)(2,1)S(1)} %collective-permute-done.12.refs_1_, ...), custom_call_target="tpu_custom_call" | custom-call | flops 1 | bytes 1 | tf_op jit(solution)/shard_map/mix_sent/pallas_call | solution.py:357
  120.3 0.7 collective-permute-start.27
  121.1 5.6 %attention.5 = (bf16[128,1024]{1,0:T(8,128)(2,1)S(1)}, bf16[128,1024]{1,0:T(8,128)(2,1)S(1)}) custom-call(s32[12]{0:T(128)S(1)} %stack.51.places_ref, s32[1]{0:T(128)S(6)} %copy.14.length_ref, bf16[256,1024]{1,0:T(8,128)(2,1)S(1)} %queries.2.refs_0_, bf16[256,1024]{1,0:T(8,128)(2,1)S(1)} %queries.3.refs_1_, bf16[256,256]{1,0:T(8,128)(2,1)S(1)} %keys_values.2.refs_0_.refs_2_, ...), custom_call_target="tpu_custom_call" | custom-call | flops 1 | bytes 1 | tf_op jit(solution)/shard_map/attention/pallas_call | solution.py:272
  126.6 2.1 %mix.10.refs_0_ = bf16[128,2560]{1,0:T(8,128)(2,1)S(1)} custom-call(bf16[128,1024]{1,0:T(8,128)(2,1)S(1)} %attention.4.rows_ref, bf16[1024,5120]{1,0:T(8,128)(2,1)S(1)} %copy-done), custom_call_target="tpu_custom_call" | custom-call | flops 1 | bytes 1 | tf_op jit(solution)/shard_map/mix/pallas_call | solution.py:301
  128.7 2.1 %mix.11.refs_0_ = bf16[128,2560]{1,0:T(8,128)(2,1)S(1)} custom-call(bf16[128,1024]{1,0:T(8,128)(2,1)S(1)} %attention.4.rows_ref, bf16[1024,5120]{1,0:T(8,128)(2,1)S(1)} %copy-done), custom_call_target="tpu_custom_call" | custom-call | flops 1 | bytes 1 | tf_op jit(solution)/shard_map/mix/pallas_call | solution.py:301
  132.0 4.1 %collective-permute-done.25.rows_ref = bf16[128,1024]{1,0:T(8,128)(2,1)S(1)} collective-permute-done((bf16[128,1024]{1,0:T(8,128)(2,1)S(1)}, bf16[128,1024]{1,0:T(8,128)(2,1)S(1)}, u32[]{:S(2)}, u32[]{:S(2)}) %collective-permute-start.25) | collective-permute-done | bytes 262176 | tf_op jit(solution)/shard_map/ppermute | solution.py:441
  136.2 4.4 %collective-permute-start.29 = (bf16[128,2560]{1,0:T(8,128)(2,1)S(1)}, bf16[128,2560]{1,0:T(8,128)(2,1)S(1)}, u32[]{:S(2)}, u32[]{:S(2)}) collective-permute-start(bf16[128,2560]{1,0:T(8,128)(2,1)S(1)} %mix.11.refs_0_), channel_id=1, source_target_pairs={{0,1},{3,2},{4,5},{7,6},{8,9},{11,10},{12,13},{15,14},{16,17},{19,... | collective-permute-start | bytes 1966088 | tf_op jit(solution)/shard_map/ppermute | solution.py:441
  140.6 1.3 collective-permute-start.33
  141.9 2.7 %mix_sent.4.refs_1_ = bf16[128,2560]{1,0:T(8,128)(2,1)S(1)} custom-call(s32[12]{0:T(128)S(1)} %stack.51.places_ref, bf16[128,1024]{1,0:T(8,128)(2,1)S(1)} %collective-permute-done.25.rows_ref, bf16[128,2560]{1,0:T(8,128)(2,1)S(1)} %collective-permute-done.9.refs_0_, bf16[128,2560]{1,0:T(8,128)(2,1)S(1)} %collective-permute-done.12.refs_1_, ...), custom_call_target="tpu_custom_call" | custom-call | flops 1 | bytes 1 | tf_op jit(solution)/shard_map/mix_sent/pallas_call | solution.py:357
  145.4 2.1 %mix.12.refs_0_ = bf16[128,2560]{1,0:T(8,128)(2,1)S(1)} custom-call(bf16[128,1024]{1,0:T(8,128)(2,1)S(1)} %get-tuple-element.95.rows_ref, bf16[1024,5120]{1,0:T(8,128)(2,1)S(1)} %copy-done), custom_call_target="tpu_custom_call" | custom-call | flops 1 | bytes 1 | tf_op jit(solution)/shard_map/mix/pallas_call | solution.py:301
  147.5 2.1 %mix.13.refs_0_ = bf16[128,2560]{1,0:T(8,128)(2,1)S(1)} custom-call(bf16[128,1024]{1,0:T(8,128)(2,1)S(1)} %get-tuple-element.95.rows_ref, bf16[1024,5120]{1,0:T(8,128)(2,1)S(1)} %copy-done), custom_call_target="tpu_custom_call" | custom-call | flops 1 | bytes 1 | tf_op jit(solution)/shard_map/mix/pallas_call | solution.py:301
  149.8 1.3 collective-permute-start.34
  151.1 2.1 %mix.14.refs_0_ = bf16[128,2560]{1,0:T(8,128)(2,1)S(1)} custom-call(bf16[128,1024]{1,0:T(8,128)(2,1)S(1)} %get-tuple-element.97.rows_ref, bf16[1024,5120]{1,0:T(8,128)(2,1)S(1)} %copy-done), custom_call_target="tpu_custom_call" | custom-call | flops 1 | bytes 1 | tf_op jit(solution)/shard_map/mix/pallas_call | solution.py:301
  153.1 2.1 %mix.15.refs_0_ = bf16[128,2560]{1,0:T(8,128)(2,1)S(1)} custom-call(bf16[128,1024]{1,0:T(8,128)(2,1)S(1)} %get-tuple-element.97.rows_ref, bf16[1024,5120]{1,0:T(8,128)(2,1)S(1)} %copy-done), custom_call_target="tpu_custom_call" | custom-call | flops 1 | bytes 1 | tf_op jit(solution)/shard_map/mix/pallas_call | solution.py:301
  155.4 1.3 collective-permute-start.31
  156.8 5.3 %collective-permute-start.30 = (bf16[128,2560]{1,0:T(8,128)(2,1)S(1)}, bf16[128,2560]{1,0:T(8,128)(2,1)S(1)}, u32[]{:S(2)}, u32[]{:S(2)}) collective-permute-start(bf16[128,2560]{1,0:T(8,128)(2,1)S(1)} %mix.13.refs_0_), channel_id=1, source_target_pairs={{0,1},{3,2},{4,5},{7,6},{8,9},{11,10},{12,13},{15,14},{16,17},{19,... | collective-permute-start | bytes 1966088 | tf_op jit(solution)/shard_map/ppermute | solution.py:441
  162.8 2.7 %mix_sent.5.refs_1_ = bf16[128,2560]{1,0:T(8,128)(2,1)S(1)} custom-call(s32[12]{0:T(128)S(1)} %stack.51.places_ref, bf16[128,1024]{1,0:T(8,128)(2,1)S(1)} %collective-permute-done.33.rows_ref, bf16[128,2560]{1,0:T(8,128)(2,1)S(1)} %collective-permute-done.9.refs_0_, bf16[128,2560]{1,0:T(8,128)(2,1)S(1)} %collective-permute-done.12.refs_1_, ...), custom_call_target="tpu_custom_call" | custom-call | flops 1 | bytes 1 | tf_op jit(solution)/shard_map/mix_sent/pallas_call | solution.py:357
  165.5 4.4 %collective-permute-done.34.refs_2_ = bf16[128,2560]{1,0:T(8,128)(2,1)S(1)} collective-permute-done((bf16[128,2560]{1,0:T(8,128)(2,1)S(1)}, bf16[128,2560]{1,0:T(8,128)(2,1)S(1)}, u32[]{:S(2)}, u32[]{:S(2)}) %collective-permute-start.34) | collective-permute-done | bytes 655392 | tf_op jit(solution)/shard_map/ppermute | solution.py:438
  169.9 1.2 added.14.refs_4_
  171.1 4.3 %collective-permute-done.30.refs_1_ = bf16[128,2560]{1,0:T(8,128)(2,1)S(1)} collective-permute-done((bf16[128,2560]{1,0:T(8,128)(2,1)S(1)}, bf16[128,2560]{1,0:T(8,128)(2,1)S(1)}, u32[]{:S(2)}, u32[]{:S(2)}) %collective-permute-start.30) | collective-permute-done | bytes 655392 | tf_op jit(solution)/shard_map/ppermute | solution.py:441
  175.4 7.0 %collective-permute-done.31.refs_2_ = bf16[128,2560]{1,0:T(8,128)(2,1)S(1)} collective-permute-done((bf16[128,2560]{1,0:T(8,128)(2,1)S(1)}, bf16[128,2560]{1,0:T(8,128)(2,1)S(1)}, u32[]{:S(2)}, u32[]{:S(2)}) %collective-permute-start.31) | collective-permute-done | bytes 655392 | tf_op jit(solution)/shard_map/ppermute | solution.py:438
  182.4 1.2 added.15
  (83 shorter events, 7.1 us)
Async XLA Ops:
  0.0 7.9 %copy-start.2 = (bf16[5120,128]{1,0:T(8,128)(2,1)S(1)}, bf16[5120,128]{1,0:T(8,128)(2,1)}, u32[]{:S(2)}) copy-start(bf16[5120,128]{1,0:T(8,128)(2,1)} %refs_3_.7) | copy-start | bytes 3932164
  0.0 32.8 %collective-permute-start = (bf16[512,1280]{1,0:T(8,128)(2,1)}, bf16[512,1280]{1,0:T(8,128)(2,1)S(1)}, u32[]{:S(2)}, u32[]{:S(2)}) collective-permute-start(bf16[512,1280]{1,0:T(8,128)(2,1)} %refs_0_.1), channel_id=1, source_target_pairs={{0,1},{1,0},{2,3},{3,2},{4,5},{5,4},{6,7},{7,6},{8,9},{9,8},{10,11... | collective-permute-start | bytes 3932168 | tf_op jit(solution)/shard_map/ppermute | solution.py:432
  3.0 1.4 copy-start.4
  5.5 12.4 %collective-permute-start.3 = (bf16[256,1280]{1,0:T(8,128)(2,1)}, bf16[256,1280]{1,0:T(8,128)(2,1)}, u32[]{:S(2)}, u32[]{:S(2)}) collective-permute-start(bf16[256,1280]{1,0:T(8,128)(2,1)} %get-tuple-element.56), channel_id=1, source_target_pairs={{1,2},{2,1},{5,6},{6,5},{9,10},{10,9},{13,14},{14,13},{17,18},{18,... | collective-permute-start | bytes 1966088 | tf_op jit(solution)/shard_map/ppermute | solution.py:435
  7.1 12.8 %collective-permute-start.5 = (bf16[256,1280]{1,0:T(8,128)(2,1)}, bf16[256,1280]{1,0:T(8,128)(2,1)S(1)}, u32[]{:S(2)}, u32[]{:S(2)}) collective-permute-start(bf16[256,1280]{1,0:T(8,128)(2,1)} %get-tuple-element.61), channel_id=1, source_target_pairs={{1,2},{2,1},{5,6},{6,5},{9,10},{10,9},{13,14},{14,13},{17,18},{18,... | collective-permute-start | bytes 1966088 | tf_op jit(solution)/shard_map/ppermute | solution.py:435
  7.9 4.0 %copy-start.1 = (bf16[5120,1024]{1,0:T(8,128)(2,1)S(1)}, bf16[5120,1024]{1,0:T(8,128)(2,1)}, u32[]{:S(2)}) copy-start(bf16[5120,1024]{1,0:T(8,128)(2,1)} %refs_2_.8) | copy-start | bytes 31457284
  11.9 1.3 copy-start.3
  13.2 1.3 copy-start.5
  14.5 4.8 %copy-start = (bf16[1024,5120]{1,0:T(8,128)(2,1)S(1)}, bf16[1024,5120]{1,0:T(8,128)(2,1)}, u32[]{:S(2)}) copy-start(bf16[1024,5120]{1,0:T(8,128)(2,1)} %w_ref.19) | copy-start | bytes 31457284
  17.9 28.9 %collective-permute-start.4 = (bf16[256,1280]{1,0:T(8,128)(2,1)}, bf16[256,1280]{1,0:T(8,128)(2,1)S(1)}, u32[]{:S(2)}, u32[]{:S(2)}) collective-permute-start(bf16[256,1280]{1,0:T(8,128)(2,1)} %collective-permute-done.3.refs_0_), channel_id=1, source_target_pairs={{1,0},{2,3},{5,4},{6,7},{9,8},{10,11},{13,12},{14,15},{17,16},{18,... | collective-permute-start | bytes 1966088 | tf_op jit(solution)/shard_map/ppermute | solution.py:438
  19.9 13.1 %copy-start.8 = (bf16[256,1280]{1,0:T(8,128)(2,1)}, bf16[256,1280]{1,0:T(8,128)(2,1)S(1)}, u32[]{:S(2)}) copy-start(bf16[256,1280]{1,0:T(8,128)(2,1)S(1)} %collective-permute-done.5.refs_2_) | copy-start | bytes 1966084
  32.9 20.1 %collective-permute-start.1 = (bf16[256,1280]{1,0:T(8,128)(2,1)S(1)}, bf16[256,1280]{1,0:T(8,128)(2,1)S(1)}, u32[]{:S(2)}, u32[]{:S(2)}) collective-permute-start(bf16[256,1280]{1,0:T(8,128)(2,1)S(1)} %get-tuple-element.54), channel_id=1, source_target_pairs={{1,2},{2,1},{5,6},{6,5},{9,10},{10,9},{13,14},{14,13},{17,18},{18,... | collective-permute-start | bytes 1966088 | tf_op jit(solution)/shard_map/ppermute | solution.py:435
  33.6 27.3 %collective-permute-start.7 = (bf16[256,1280]{1,0:T(8,128)(2,1)}, bf16[256,1280]{1,0:T(8,128)(2,1)S(1)}, u32[]{:S(2)}, u32[]{:S(2)}) collective-permute-start(bf16[256,1280]{1,0:T(8,128)(2,1)} %copy-done.8), channel_id=1, source_target_pairs={{1,0},{2,3},{5,4},{6,7},{9,8},{10,11},{13,12},{14,15},{17,16},{18,... | collective-permute-start | bytes 1966088 | tf_op jit(solution)/shard_map/ppermute | solution.py:438
  46.9 5.2 %copy-start.10 = (bf16[256,1280]{1,0:T(8,128)(2,1)}, bf16[256,1280]{1,0:T(8,128)(2,1)S(1)}, u32[]{:S(2)}) copy-start(bf16[256,1280]{1,0:T(8,128)(2,1)S(1)} %collective-permute-done.4.refs_1_) | copy-start | bytes 1966084
  46.9 14.9 %collective-permute-start.9 = (bf16[128,2560]{1,0:T(8,128)(2,1)S(1)}, bf16[128,2560]{1,0:T(8,128)(2,1)S(1)}, u32[]{:S(2)}, u32[]{:S(2)}) collective-permute-start(bf16[128,2560]{1,0:T(8,128)(2,1)S(1)} %eighth.2), channel_id=1, source_target_pairs={{0,1},{3,2},{4,5},{7,6},{8,9},{11,10},{12,13},{15,14},{16,17},{19,... | collective-permute-start | bytes 1966088 | tf_op jit(solution)/shard_map/ppermute | solution.py:441
  48.5 21.2 %slice-start = ((s8[10485760]{0:T(1024)(128)(4,1)}), s8[4194304]{0:T(1024)(128)(4,1)S(1)}, s32[]{:S(2)}) async-start(s8[10485760]{0:T(1024)(128)(4,1)} %bitcast.14), calls=%async_computation | async-start | bytes 8388608
  48.5 21.2 %slice-start.1 = ((s8[10485760]{0:T(1024)(128)(4,1)}), s8[4194304]{0:T(1024)(128)(4,1)S(1)}, s32[]{:S(2)}) async-start(s8[10485760]{0:T(1024)(128)(4,1)} %bitcast.14), calls=%async_computation.1 | async-start | bytes 8388608
  52.1 17.5 %slice-start.2 = ((s8[10485760]{0:T(1024)(128)(4,1)}), s8[2097152]{0:T(1024)(128)(4,1)S(1)}, s32[]{:S(2)}) async-start(s8[10485760]{0:T(1024)(128)(4,1)} %bitcast.14), calls=%async_computation.2 | async-start | bytes 4194304
  52.1 17.5 %copy-start.9 = (bf16[256,1280]{1,0:T(8,128)(2,1)S(1)}, bf16[256,1280]{1,0:T(8,128)(2,1)}, u32[]{:S(2)}) copy-start(bf16[256,1280]{1,0:T(8,128)(2,1)} %copy-done.8) | copy-start | bytes 1966084
  52.1 17.5 %copy-start.11 = (bf16[256,1280]{1,0:T(8,128)(2,1)S(1)}, bf16[256,1280]{1,0:T(8,128)(2,1)}, u32[]{:S(2)}) copy-start(bf16[256,1280]{1,0:T(8,128)(2,1)} %copy-done.10) | copy-start | bytes 1966084
  52.2 16.2 %collective-permute-start.6 = (bf16[256,1280]{1,0:T(8,128)(2,1)S(1)}, bf16[256,1280]{1,0:T(8,128)(2,1)S(1)}, u32[]{:S(2)}, u32[]{:S(2)}) collective-permute-start(bf16[256,1280]{1,0:T(8,128)(2,1)S(1)} %get-tuple-element.69), channel_id=1, source_target_pairs={{1,2},{2,1},{5,6},{6,5},{9,10},{10,9},{13,14},{14,13},{17,18},{18,... | collective-permute-start | bytes 1966088 | tf_op jit(solution)/shard_map/ppermute | solution.py:435
  53.0 23.4 %collective-permute-start.2 = (bf16[256,1280]{1,0:T(8,128)(2,1)S(1)}, bf16[256,1280]{1,0:T(8,128)(2,1)S(1)}, u32[]{:S(2)}, u32[]{:S(2)}) collective-permute-start(bf16[256,1280]{1,0:T(8,128)(2,1)S(1)} %collective-permute-done.1.refs_0_), channel_id=1, source_target_pairs={{1,0},{2,3},{5,4},{6,7},{9,8},{10,11},{13,12},{14,15},{17,16},{18,... | collective-permute-start | bytes 1966088 | tf_op jit(solution)/shard_map/ppermute | solution.py:438
  54.4 22.0 %copy-start.15 = (f32[128]{0:T(128)S(1)}, f32[128]{0:T(128)}, u32[]{:S(2)}) copy-start(f32[128]{0:T(128)} %param.18) | copy-start | bytes 1540
  55.0 21.3 %copy-start.6 = (f32[512,128]{1,0:T(8,128)S(1)}, f32[512,128]{1,0:T(8,128)}, u32[]{:S(2)}) copy-start(f32[512,128]{1,0:T(8,128)} %constant.29.clone.refs_5_.refs_7_.refs_8_) | copy-start | bytes 786436
  55.1 21.3 %copy-start.7 = (f32[512,128]{1,0:T(8,128)S(1)}, f32[512,128]{1,0:T(8,128)}, u32[]{:S(2)}) copy-start(f32[512,128]{1,0:T(8,128)} %constant.30.clone.refs_6_.refs_8_.refs_9_) | copy-start | bytes 786436
  60.9 0.8 copy-start.12
  61.8 18.2 %collective-permute-start.10 = (bf16[128,2560]{1,0:T(8,128)(2,1)S(1)}, bf16[128,2560]{1,0:T(8,128)(2,1)S(1)}, u32[]{:S(2)}, u32[]{:S(2)}) collective-permute-start(bf16[128,2560]{1,0:T(8,128)(2,1)S(1)} %collective-permute-done.9.refs_0_), channel_id=1, source_target_pairs={{0,8},{4,12},{8,0},{12,4},{16,24},{20,28},{24,16},{28,20},{1,9},{5... | collective-permute-start | bytes 1966088 | tf_op jit(solution)/shard_map/ppermute | solution.py:444
  63.7 16.3 %collective-permute-start.11 = (bf16[128,2560]{1,0:T(8,128)(2,1)S(1)}, bf16[128,2560]{1,0:T(8,128)(2,1)S(1)}, u32[]{:S(2)}, u32[]{:S(2)}) collective-permute-start(bf16[128,2560]{1,0:T(8,128)(2,1)S(1)} %collective-permute-done.9.refs_0_), channel_id=1, source_target_pairs={{0,16},{4,20},{8,24},{12,28},{16,0},{20,4},{24,8},{28,12},{1,17},{... | collective-permute-start | bytes 1966088 | tf_op jit(solution)/shard_map/ppermute | solution.py:444
  65.3 14.8 %collective-permute-start.12 = (bf16[128,2560]{1,0:T(8,128)(2,1)S(1)}, bf16[128,2560]{1,0:T(8,128)(2,1)S(1)}, u32[]{:S(2)}, u32[]{:S(2)}) collective-permute-start(bf16[128,2560]{1,0:T(8,128)(2,1)S(1)} %eighth.3), channel_id=1, source_target_pairs={{0,1},{3,2},{4,5},{7,6},{8,9},{11,10},{12,13},{15,14},{16,17},{19,... | collective-permute-start | bytes 1966088 | tf_op jit(solution)/shard_map/ppermute | solution.py:441
  68.3 19.9 %collective-permute-start.8 = (bf16[256,1280]{1,0:T(8,128)(2,1)S(1)}, bf16[256,1280]{1,0:T(8,128)(2,1)S(1)}, u32[]{:S(2)}, u32[]{:S(2)}) collective-permute-start(bf16[256,1280]{1,0:T(8,128)(2,1)S(1)} %collective-permute-done.6.refs_0_.refs_1_), channel_id=1, source_target_pairs={{1,0},{2,3},{5,4},{6,7},{9,8},{10,11},{13,12},{14,15},{17,16},{18,... | collective-permute-start | bytes 1966088 | tf_op jit(solution)/shard_map/ppermute | solution.py:438
  69.7 1.1 copy-start.13
  76.4 2.5 %copy-start.14 = (f32[128]{0:T(128)S(1)}, f32[128]{0:T(128)}, u32[]{:S(2)}) copy-start(f32[128]{0:T(128)} %param.19) | copy-start | bytes 1540
  78.9 9.3 %copy-start.16 = (s32[1,128]{1,0:T(1,128)S(1)}, s32[1,128]{1,0:T(1,128)}, u32[]{:S(2)}) copy-start(s32[1,128]{1,0:T(1,128)} %refs_10_.1) | copy-start | bytes 1540
  89.5 3.7 %collective-permute-start.13 = (bf16[128,256]{1,0:T(8,128)(2,1)S(1)}, bf16[128,256]{1,0:T(8,128)(2,1)S(1)}, u32[]{:S(2)}, u32[]{:S(2)}) collective-permute-start(bf16[128,256]{1,0:T(8,128)(2,1)S(1)} %get-tuple-element.81), channel_id=1, source_target_pairs={{0,4},{4,0},{8,12},{12,8},{16,20},{20,16},{24,28},{28,24},{1,5},{5... | collective-permute-start | bytes 196616 | tf_op jit(solution)/shard_map/ppermute | solution.py:444
  89.6 6.2 %collective-permute-start.14 = (bf16[128,256]{1,0:T(8,128)(2,1)S(1)}, bf16[128,256]{1,0:T(8,128)(2,1)S(1)}, u32[]{:S(2)}, u32[]{:S(2)}) collective-permute-start(bf16[128,256]{1,0:T(8,128)(2,1)S(1)} %get-tuple-element.81), channel_id=1, source_target_pairs={{0,8},{4,12},{8,0},{12,4},{16,24},{20,28},{24,16},{28,20},{1,9},{5... | collective-permute-start | bytes 196616 | tf_op jit(solution)/shard_map/ppermute | solution.py:444
  91.3 7.8 %collective-permute-start.15 = (bf16[128,256]{1,0:T(8,128)(2,1)S(1)}, bf16[128,256]{1,0:T(8,128)(2,1)S(1)}, u32[]{:S(2)}, u32[]{:S(2)}) collective-permute-start(bf16[128,256]{1,0:T(8,128)(2,1)S(1)} %get-tuple-element.81), channel_id=1, source_target_pairs={{0,12},{4,8},{8,4},{12,0},{16,28},{20,24},{24,20},{28,16},{1,13},{... | collective-permute-start | bytes 196616 | tf_op jit(solution)/shard_map/ppermute | solution.py:444
  91.4 7.7 %collective-permute-start.16 = (bf16[128,256]{1,0:T(8,128)(2,1)S(1)}, bf16[128,256]{1,0:T(8,128)(2,1)S(1)}, u32[]{:S(2)}, u32[]{:S(2)}) collective-permute-start(bf16[128,256]{1,0:T(8,128)(2,1)S(1)} %get-tuple-element.81), channel_id=1, source_target_pairs={{0,16},{4,20},{8,24},{12,28},{16,0},{20,4},{24,8},{28,12},{1,17},{... | collective-permute-start | bytes 196616 | tf_op jit(solution)/shard_map/ppermute | solution.py:444
  93.1 6.0 %collective-permute-start.17 = (bf16[128,256]{1,0:T(8,128)(2,1)S(1)}, bf16[128,256]{1,0:T(8,128)(2,1)S(1)}, u32[]{:S(2)}, u32[]{:S(2)}) collective-permute-start(bf16[128,256]{1,0:T(8,128)(2,1)S(1)} %get-tuple-element.81), channel_id=1, source_target_pairs={{0,20},{4,16},{8,28},{12,24},{16,4},{20,0},{24,12},{28,8},{1,21},{... | collective-permute-start | bytes 196616 | tf_op jit(solution)/shard_map/ppermute | solution.py:444
  93.2 6.0 %collective-permute-start.18 = (bf16[128,256]{1,0:T(8,128)(2,1)S(1)}, bf16[128,256]{1,0:T(8,128)(2,1)S(1)}, u32[]{:S(2)}, u32[]{:S(2)}) collective-permute-start(bf16[128,256]{1,0:T(8,128)(2,1)S(1)} %get-tuple-element.81), channel_id=1, source_target_pairs={{0,24},{4,28},{8,16},{12,20},{16,8},{20,12},{24,0},{28,4},{1,25},{... | collective-permute-start | bytes 196616 | tf_op jit(solution)/shard_map/ppermute | solution.py:444
  95.8 4.9 %collective-permute-start.19 = (bf16[128,256]{1,0:T(8,128)(2,1)S(1)}, bf16[128,256]{1,0:T(8,128)(2,1)S(1)}, u32[]{:S(2)}, u32[]{:S(2)}) collective-permute-start(bf16[128,256]{1,0:T(8,128)(2,1)S(1)} %get-tuple-element.81), channel_id=1, source_target_pairs={{0,28},{4,24},{8,20},{12,16},{16,12},{20,8},{24,4},{28,0},{1,29},{... | collective-permute-start | bytes 196616 | tf_op jit(solution)/shard_map/ppermute | solution.py:444
  104.3 10.5 %collective-permute-start.20 = (bf16[128,1024]{1,0:T(8,128)(2,1)S(1)}, bf16[128,1024]{1,0:T(8,128)(2,1)S(1)}, u32[]{:S(2)}, u32[]{:S(2)}) collective-permute-start(bf16[128,1024]{1,0:T(8,128)(2,1)S(1)} %attention.3.rows_ref), channel_id=1, source_target_pairs={{0,1},{3,2},{4,5},{7,6},{8,9},{11,10},{12,13},{15,14},{16,17},{19,... | collective-permute-start | bytes 786440 | tf_op jit(solution)/shard_map/ppermute | solution.py:441
  105.9 10.2 %collective-permute-start.21 = (bf16[128,2560]{1,0:T(8,128)(2,1)S(1)}, bf16[128,2560]{1,0:T(8,128)(2,1)S(1)}, u32[]{:S(2)}, u32[]{:S(2)}) collective-permute-start(bf16[128,2560]{1,0:T(8,128)(2,1)S(1)} %collective-permute-done.9.refs_0_), channel_id=1, source_target_pairs={{0,4},{4,0},{8,12},{12,8},{16,20},{20,16},{24,28},{28,24},{1,5},{5... | collective-permute-start | bytes 1966088 | tf_op jit(solution)/shard_map/ppermute | solution.py:444
  106.0 11.5 %collective-permute-start.22 = (bf16[128,2560]{1,0:T(8,128)(2,1)S(1)}, bf16[128,2560]{1,0:T(8,128)(2,1)S(1)}, u32[]{:S(2)}, u32[]{:S(2)}) collective-permute-start(bf16[128,2560]{1,0:T(8,128)(2,1)S(1)} %collective-permute-done.12.refs_1_), channel_id=1, source_target_pairs={{0,4},{4,0},{8,12},{12,8},{16,20},{20,16},{24,28},{28,24},{1,5},{5... | collective-permute-start | bytes 1966088 | tf_op jit(solution)/shard_map/ppermute | solution.py:444
  106.5 11.0 %collective-permute-start.23 = (bf16[128,2560]{1,0:T(8,128)(2,1)S(1)}, bf16[128,2560]{1,0:T(8,128)(2,1)S(1)}, u32[]{:S(2)}, u32[]{:S(2)}) collective-permute-start(bf16[128,2560]{1,0:T(8,128)(2,1)S(1)} %collective-permute-done.10.refs_2_), channel_id=1, source_target_pairs={{0,4},{4,0},{8,12},{12,8},{16,20},{20,16},{24,28},{28,24},{1,5},{5... | collective-permute-start | bytes 1966088 | tf_op jit(solution)/shard_map/ppermute | solution.py:444
  106.6 10.9 %collective-permute-start.24 = (bf16[128,2560]{1,0:T(8,128)(2,1)S(1)}, bf16[128,2560]{1,0:T(8,128)(2,1)S(1)}, u32[]{:S(2)}, u32[]{:S(2)}) collective-permute-start(bf16[128,2560]{1,0:T(8,128)(2,1)S(1)} %collective-permute-done.11.refs_3_), channel_id=1, source_target_pairs={{0,4},{4,0},{8,12},{12,8},{16,20},{20,16},{24,28},{28,24},{1,5},{5... | collective-permute-start | bytes 1966088 | tf_op jit(solution)/shard_map/ppermute | solution.py:444
  114.7 16.4 %collective-permute-start.26 = (bf16[128,2560]{1,0:T(8,128)(2,1)S(1)}, bf16[128,2560]{1,0:T(8,128)(2,1)S(1)}, u32[]{:S(2)}, u32[]{:S(2)}) collective-permute-start(bf16[128,2560]{1,0:T(8,128)(2,1)S(1)} %mix.8.refs_0_), channel_id=1, source_target_pairs={{0,1},{3,2},{4,5},{7,6},{8,9},{11,10},{12,13},{15,14},{16,17},{19,... | collective-permute-start | bytes 1966088 | tf_op jit(solution)/shard_map/ppermute | solution.py:441
  116.2 20.0 %collective-permute-start.25 = (bf16[128,1024]{1,0:T(8,128)(2,1)S(1)}, bf16[128,1024]{1,0:T(8,128)(2,1)S(1)}, u32[]{:S(2)}, u32[]{:S(2)}) collective-permute-start(bf16[128,1024]{1,0:T(8,128)(2,1)S(1)} %attention.4.rows_ref), channel_id=1, source_target_pairs={{0,1},{3,2},{4,5},{7,6},{8,9},{11,10},{12,13},{15,14},{16,17},{19,... | collective-permute-start | bytes 786440 | tf_op jit(solution)/shard_map/ppermute | solution.py:441
  120.3 25.1 %collective-permute-start.27 = (bf16[128,2560]{1,0:T(8,128)(2,1)S(1)}, bf16[128,2560]{1,0:T(8,128)(2,1)S(1)}, u32[]{:S(2)}, u32[]{:S(2)}) collective-permute-start(bf16[128,2560]{1,0:T(8,128)(2,1)S(1)} %added.8), channel_id=1, source_target_pairs={{1,2},{2,1},{5,6},{6,5},{9,10},{10,9},{13,14},{14,13},{17,18},{18,... | collective-permute-start | bytes 1966088 | tf_op jit(solution)/shard_map/ppermute | solution.py:435
  131.3 19.7 %collective-permute-start.28 = (bf16[128,2560]{1,0:T(8,128)(2,1)S(1)}, bf16[128,2560]{1,0:T(8,128)(2,1)S(1)}, u32[]{:S(2)}, u32[]{:S(2)}) collective-permute-start(bf16[128,2560]{1,0:T(8,128)(2,1)S(1)} %added.9), channel_id=1, source_target_pairs={{1,2},{2,1},{5,6},{6,5},{9,10},{10,9},{13,14},{14,13},{17,18},{18,... | collective-permute-start | bytes 1966088 | tf_op jit(solution)/shard_map/ppermute | solution.py:435
  136.2 20.5 %collective-permute-start.29 = (bf16[128,2560]{1,0:T(8,128)(2,1)S(1)}, bf16[128,2560]{1,0:T(8,128)(2,1)S(1)}, u32[]{:S(2)}, u32[]{:S(2)}) collective-permute-start(bf16[128,2560]{1,0:T(8,128)(2,1)S(1)} %mix.11.refs_0_), channel_id=1, source_target_pairs={{0,1},{3,2},{4,5},{7,6},{8,9},{11,10},{12,13},{15,14},{16,17},{19,... | collective-permute-start | bytes 1966088 | tf_op jit(solution)/shard_map/ppermute | solution.py:441
  140.6 21.5 %collective-permute-start.33 = (bf16[128,1024]{1,0:T(8,128)(2,1)S(1)}, bf16[128,1024]{1,0:T(8,128)(2,1)S(1)}, u32[]{:S(2)}, u32[]{:S(2)}) collective-permute-start(bf16[128,1024]{1,0:T(8,128)(2,1)S(1)} %get-tuple-element.95.rows_ref), channel_id=1, source_target_pairs={{0,1},{3,2},{4,5},{7,6},{8,9},{11,10},{12,13},{15,14},{16,17},{19,... | collective-permute-start | bytes 786440 | tf_op jit(solution)/shard_map/ppermute | solution.py:441
  144.7 20.8 %collective-permute-start.35 = (bf16[128,2560]{1,0:T(8,128)(2,1)S(1)}, bf16[128,2560]{1,0:T(8,128)(2,1)S(1)}, u32[]{:S(2)}, u32[]{:S(2)}) collective-permute-start(bf16[128,2560]{1,0:T(8,128)(2,1)S(1)} %added.10), channel_id=1, source_target_pairs={{1,2},{2,1},{5,6},{6,5},{9,10},{10,9},{13,14},{14,13},{17,18},{18,... | collective-permute-start | bytes 1966088 | tf_op jit(solution)/shard_map/ppermute | solution.py:435
  149.8 20.2 %collective-permute-start.34 = (bf16[128,2560]{1,0:T(8,128)(2,1)S(1)}, bf16[128,2560]{1,0:T(8,128)(2,1)S(1)}, u32[]{:S(2)}, u32[]{:S(2)}) collective-permute-start(bf16[128,2560]{1,0:T(8,128)(2,1)S(1)} %added.11), channel_id=1, source_target_pairs={{1,0},{2,3},{5,4},{6,7},{9,8},{10,11},{13,12},{14,15},{17,16},{18,... | collective-permute-start | bytes 1966088 | tf_op jit(solution)/shard_map/ppermute | solution.py:438
  155.4 27.0 %collective-permute-start.31 = (bf16[128,2560]{1,0:T(8,128)(2,1)S(1)}, bf16[128,2560]{1,0:T(8,128)(2,1)S(1)}, u32[]{:S(2)}, u32[]{:S(2)}) collective-permute-start(bf16[128,2560]{1,0:T(8,128)(2,1)S(1)} %added.12), channel_id=1, source_target_pairs={{1,0},{2,3},{5,4},{6,7},{9,8},{10,11},{13,12},{14,15},{17,16},{18,... | collective-permute-start | bytes 1966088 | tf_op jit(solution)/shard_map/ppermute | solution.py:438
  156.8 18.5 %collective-permute-start.30 = (bf16[128,2560]{1,0:T(8,128)(2,1)S(1)}, bf16[128,2560]{1,0:T(8,128)(2,1)S(1)}, u32[]{:S(2)}, u32[]{:S(2)}) collective-permute-start(bf16[128,2560]{1,0:T(8,128)(2,1)S(1)} %mix.13.refs_0_), channel_id=1, source_target_pairs={{0,1},{3,2},{4,5},{7,6},{8,9},{11,10},{12,13},{15,14},{16,17},{19,... | collective-permute-start | bytes 1966088 | tf_op jit(solution)/shard_map/ppermute | solution.py:441
  162.1 20.3 %collective-permute-start.32 = (bf16[128,2560]{1,0:T(8,128)(2,1)S(1)}, bf16[128,2560]{1,0:T(8,128)(2,1)S(1)}, u32[]{:S(2)}, u32[]{:S(2)}) collective-permute-start(bf16[128,2560]{1,0:T(8,128)(2,1)S(1)} %added.13), channel_id=1, source_target_pairs={{1,2},{2,1},{5,6},{6,5},{9,10},{10,9},{13,14},{14,13},{17,18},{18,... | collective-permute-start | bytes 1966088 | tf_op jit(solution)/shard_map/ppermute | solution.py:435

commit v13 on v12

--- a/solution.py
+++ b/solution.py
@@ -46,6 +46,10 @@
 
 def whole(*shape):
     return pl.BlockSpec(shape, lambda *_: (0,) * len(shape))
+
+
+def resident(count):
+    return [pl.BlockSpec(memory_space=pltpu.VMEM)] * count
 
 
 def summed(refs):
@@ -274,8 +278,8 @@
         grid_spec=pltpu.PrefetchScalarGridSpec(
             num_scalar_prefetch=2,
             grid=(1,),
-            in_specs=[whole(*array.shape) for array in (*queries, *own, *others)],
-            out_specs=[whole(rows, width) for _ in slots],
+            in_specs=resident(len(queries) + len(own) + len(others)),
+            out_specs=resident(len(slots)),
             scratch_shapes=[
                 pltpu.VMEM((reach, head), jnp.bfloat16),
                 pltpu.VMEM((reach, head), jnp.bfloat16),
@@ -288,24 +292,24 @@
     )(places, lengths, *queries, *own, *others)
 
 
-def mix_kernel(rows_ref, w_ref, out_ref):
-    total = jnp.dot(rows_ref[...], w_ref[...], preferred_element_type=jnp.float32)
-    out_ref[...] = total.astype(out_ref.dtype)
+def mix_kernel(which, tiles, rows_ref, w_ref, out_ref):
+    width = out_ref.shape[1]
+    tile = width // tiles
+    for start in range(0, width, tile):
+        left = which * width + start
+        total = jnp.dot(
+            rows_ref[...], w_ref[:, left : left + tile], preferred_element_type=jnp.float32
+        )
+        out_ref[:, start : start + tile] = total.astype(out_ref.dtype)
 
 
 def mix(attended, w_out, which):
-    rows, depth = attended.shape
+    rows = attended.shape[0]
     width = w_out.shape[1] // 2
-    tiles = 5
-    tile = width // tiles
-    return pl.pallas_call(
-        mix_kernel,
-        grid=(tiles,),
-        in_specs=[
-            whole(rows, depth),
-            pl.BlockSpec((depth, tile), lambda i: (0, i + which * tiles)),
-        ],
-        out_specs=pl.BlockSpec((rows, tile), lambda i: (0, i)),
+    return pl.pallas_call(
+        functools.partial(mix_kernel, which, 5),
+        in_specs=resident(2),
+        out_specs=resident(1)[0],
         out_shape=jax.ShapeDtypeStruct((rows, width), jnp.bfloat16),
         compiler_params=params(8),
         cost_estimate=cost(1),
@@ -334,36 +338,35 @@
     )(places, w_out)
 
 
-def mix_sent_kernel(places_ref, rows_ref, *refs):
+def mix_sent_kernel(tiles, places_ref, rows_ref, *refs):
     pieces, out_ref = refs[:-1], refs[-1]
     share = rows_ref.shape[1] // len(OFFSETS)
     rows = []
     for index in range(len(OFFSETS)):
         start = pl.multiple_of(places_ref[EIGHTHS + index] * share, share)
         rows.append(rows_ref[:, pl.ds(start, share)])
-    total = jnp.dot(
-        jnp.concatenate(rows, axis=1),
-        jnp.concatenate([piece[...] for piece in pieces], axis=0),
-        preferred_element_type=jnp.float32,
-    )
-    out_ref[...] = total.astype(out_ref.dtype)
+    rows = jnp.concatenate(rows, axis=1)
+    tile = out_ref.shape[1] // tiles
+    for start in range(0, out_ref.shape[1], tile):
+        columns = slice(start, start + tile)
+        weights = jnp.concatenate([piece[:, columns] for piece in pieces], axis=0)
+        total = jnp.dot(rows, weights, preferred_element_type=jnp.float32)
+        out_ref[:, columns] = total.astype(out_ref.dtype)
 
 
 def mix_sent(places, attended, pieces):
-    rows, depth = attended.shape
+    rows = attended.shape[0]
     width = pieces[0].shape[1]
-    tile = width // 5
-    column = lambda height: pl.BlockSpec((height, tile), lambda i, p: (0, i))
-    return pl.pallas_call(
-        mix_sent_kernel,
+    return pl.pallas_call(
+        functools.partial(mix_sent_kernel, 5),
         grid_spec=pltpu.PrefetchScalarGridSpec(
             num_scalar_prefetch=1,
-            grid=(width // tile,),
-            in_specs=[whole(rows, depth)] + [column(piece.shape[0]) for piece in pieces],
-            out_specs=column(rows),
+            grid=(1,),
+            in_specs=resident(1 + len(pieces)),
+            out_specs=resident(1)[0],
         ),
         out_shape=jax.ShapeDtypeStruct((rows, width), jnp.bfloat16),
-        compiler_params=params(8),
+        compiler_params=params(12),
         cost_estimate=cost(1),
         name="mix_sent",
     )(places, attended, *pieces)
@@ -402,7 +405,7 @@
     wide = 1 if half is None else 2
     at = half or 0
     operands = list(arrays)
-    in_specs = [whole(rows, width) for _ in arrays]
+    in_specs = resident(len(arrays))
     aliases = {}
     if into is not None:
         operands.append(into)
@@ -535,13 +538,14 @@
     far_left = across(far_left)
     third_in = inward(after(third[0], third_sent))
     third_right = added(third[1], share_of(third_sent))
-    near = mixed(after(near_rows, (third_right, far_right)))
+    near = [None, mix(after(near_rows, (third_right, far_right)), w_out, 1)]
     near_sent = send(near_rows, near[1])
     third_right = across(third_right)
-    out_right = added(near[1], after(far_right, near))
-    kept = mixed(after(own_rows, (out_right, far_left)))
-    out_left = added(near[0], after(far_left, kept))
+    out_right = added(near[1], far_right)
+    near[0] = mix(after(near_rows, out_right), w_out, 0)
+    out_left = added(near[0], far_left)
     third_left = added(third[0], after(third_in, out_left))
+    kept = mixed(after(own_rows, third_left))
     near_sent = share_of(after(near_sent, third_left))
     result = added(kept[1], near_sent, outward(out_right), third_right, half=1)
     near_in = inward(after(near[0], third_left))

time: 184 us -> 179 us (0.973)
  Pallas kernels: 61.8 us -> 48.4 us
  starting transfers between devices: 48.5 us -> 51.7 us
  waiting for transfers between devices: 61.8 us -> 64.9 us
    pallas_call x11, Pallas kernels: 24.5 us -> 11.1 us  [the longest x8 6.91 us: mix(): pl.pallas_call(functools.partial(mix_kernel, which, 5), in_specs=resident...]
    ppermute x8, waiting for transfers between devices: 8.81 us -> 20.9 us  [inward(): return lax.ppermute(array, 'tensor', [(0, 1), (3, 2)])]
    ppermute x6, waiting for transfers between devices: 38.4 us -> 29.4 us  [outward(): return lax.ppermute(array, 'tensor', [(1, 0), (2, 3)])]
    ppermute x8, starting transfers between devices: 20 us -> 23.1 us  [inward(): return lax.ppermute(array, 'tensor', [(0, 1), (3, 2)])]
  transfers between devices with their start and end apart: 36 -> 36, of which waited for: 11 -> 12; matrix products, arithmetic and copies ran while one was open for 0% -> 0% of each run, Pallas kernels for 30% -> 24%
where the time goes in v13:
time: 179 us; the launch traced here: 177 us
  waiting for transfers between devices  64.9 us (36%)
  starting transfers between devices  51.7 us (29%)
  Pallas kernels  48.4 us (27%)
  local copies, waits for them, and re-layouts  10.9 us (6%)
    ppermute x6, waiting for transfers between devices, outward(): return lax.ppermute(array, 'tensor', [(1, 0), (2, 3)])  29.4 us
    ppermute x8, starting transfers between devices, inward(): return lax.ppermute(array, 'tensor', [(0, 1), (3, 2)])  23.1 us
    ppermute x8, waiting for transfers between devices, inward(): return lax.ppermute(array, 'tensor', [(0, 1), (3, 2)])  20.9 us
    ppermute x1, waiting for transfers between devices, swap(): return lax.ppermute(array, 'tensor', [(0, 1), (1, 0), (2, 3), (3, 2)])  13 us
    pallas_call x3, Pallas kernels, attention(): pl.pallas_call(functools.partial(attention_kernel, slots, n_parts, len(ot...  12.7 us
    pallas_call x3, Pallas kernels, partial_projection(): pl.pallas_call(functools.partial(partial_kernel, [len(part) for part in p...  11.6 us
    ppermute x13, starting transfers between devices, between(): return lax.ppermute(array, 'cand', [(i, i ^ offset) for i in range(n_cand)])  10.9 us
    unnamed x40, local copies, waits for them, and re-layouts  10.8 us
  transfers between devices with their start and end apart: 36, of which 12 were waited for; matrix products, arithmetic and copies ran while one was open for 0% of the time, Pallas kernels for 24%

profile of v13, /device:TPU:0, one launch (start us, length us, event | category | flops | bytes accessed | tf_op | source)
XLA Modules:
  0.0 177.3 jit_solution(13273818428887502525)
XLA Ops:
  0.0 3.0 %collective-permute-start = (bf16[512,1280]{1,0:T(8,128)(2,1)}, bf16[512,1280]{1,0:T(8,128)(2,1)S(1)}, u32[]{:S(2)}, u32[]{:S(2)}) collective-permute-start(bf16[512,1280]{1,0:T(8,128)(2,1)} %refs_0_.1), channel_id=1, source_target_pairs={{0,1},{1,0},{2,3},{3,2},{4,5},{5,4},{6,7},{7,6},{8,9},{9,8},{10,11... | collective-permute-start | bytes 3932168 | tf_op jit(solution)/shard_map/ppermute | solution.py:435
  3.0 1.3 copy-done.4
  4.4 1.2 halves.3
  5.5 1.5 collective-permute-start.3
  7.9 4.0 %copy-done.1 = bf16[5120,1024]{1,0:T(8,128)(2,1)S(1)} copy-done((bf16[5120,1024]{1,0:T(8,128)(2,1)S(1)}, bf16[5120,1024]{1,0:T(8,128)(2,1)}, u32[]{:S(2)}) %copy-start.1) | copy-done | bytes 10485784
  11.9 1.3 copy-done.3
  13.2 1.3 copy-done.5
  14.5 3.4 %partial_projection.3 = (f32[512,1024]{1,0:T(8,128)S(1)}, f32[512,128]{1,0:T(8,128)S(1)}, f32[512,128]{1,0:T(8,128)S(1)}) custom-call(s32[12]{0:T(128)S(1)} %stack.51.places_ref, bf16[512,1280]{1,0:T(8,128)(2,1)S(1)} %copy-done.5, bf16[5120,1024]{1,0:T(8,128)(2,1)S(1)} %copy-done.1, bf16[5120,128]{1,0:T(8,128)(2,1)S(1)} %copy-done.2, ...), custom_call_target="tpu_custom_call" | custom-call | flops 1 | bytes 1 | tf_op jit(solution)/shard_map/partial_projection/pallas_call | solution.py:100
  17.9 1.3 collective-permute-start.4
  19.9 13.0 %collective-permute-done.ref.refs_0_ = bf16[512,1280]{1,0:T(8,128)(2,1)S(1)} collective-permute-done((bf16[512,1280]{1,0:T(8,128)(2,1)}, bf16[512,1280]{1,0:T(8,128)(2,1)S(1)}, u32[]{:S(2)}, u32[]{:S(2)}) %collective-permute-start) | collective-permute-done | bytes 1310752 | tf_op jit(solution)/shard_map/ppermute | solution.py:435
  33.6 1.3 collective-permute-start.7
  34.9 11.9 %collective-permute-done.4.refs_1_ = bf16[256,1280]{1,0:T(8,128)(2,1)S(1)} collective-permute-done((bf16[256,1280]{1,0:T(8,128)(2,1)}, bf16[256,1280]{1,0:T(8,128)(2,1)S(1)}, u32[]{:S(2)}, u32[]{:S(2)}) %collective-permute-start.4) | collective-permute-done | bytes 655392 | tf_op jit(solution)/shard_map/ppermute | solution.py:441
  46.9 0.8 copy-done.10
  47.7 1.6 collective-permute-start.9
  49.3 3.6 %partial_projection.4 = (f32[512,1024]{1,0:T(8,128)S(1)}, f32[512,128]{1,0:T(8,128)S(1)}, f32[512,128]{1,0:T(8,128)S(1)}) custom-call(s32[12]{0:T(128)S(1)} %stack.51.places_ref, bf16[512,1280]{1,0:T(8,128)(2,1)S(1)} %collective-permute-done.ref.refs_0_, bf16[5120,1024]{1,0:T(8,128)(2,1)S(1)} %copy-done.1, bf16[5120,128]{1,0:T(8,128)(2,1)S(1)} %copy-done.2, ...), custom_call_target="tpu_custom_call" | custom-call | flops 1 | bytes 1 | tf_op jit(solution)/shard_map/partial_projection/pallas_call | solution.py:100
  53.0 0.8 collective-permute-start.6
  53.8 1.4 collective-permute-start.2
  55.9 5.0 %collective-permute-done.7.refs_3_ = bf16[256,1280]{1,0:T(8,128)(2,1)S(1)} collective-permute-done((bf16[256,1280]{1,0:T(8,128)(2,1)}, bf16[256,1280]{1,0:T(8,128)(2,1)S(1)}, u32[]{:S(2)}, u32[]{:S(2)}) %collective-permute-start.7) | collective-permute-done | bytes 655392 | tf_op jit(solution)/shard_map/ppermute | solution.py:441
  61.9 1.9 %collective-permute-start.10 = (bf16[128,2560]{1,0:T(8,128)(2,1)S(1)}, bf16[128,2560]{1,0:T(8,128)(2,1)S(1)}, u32[]{:S(2)}, u32[]{:S(2)}) collective-permute-start(bf16[128,2560]{1,0:T(8,128)(2,1)S(1)} %collective-permute-done.9.refs_0_), channel_id=1, source_target_pairs={{0,8},{4,12},{8,0},{12,4},{16,24},{20,28},{24,16},{28,20},{1,9},{5... | collective-permute-start | bytes 1966088 | tf_op jit(solution)/shard_map/ppermute | solution.py:447
  63.7 1.5 collective-permute-start.11
  65.3 3.9 %collective-permute-start.12 = (bf16[128,2560]{1,0:T(8,128)(2,1)S(1)}, bf16[128,2560]{1,0:T(8,128)(2,1)S(1)}, u32[]{:S(2)}, u32[]{:S(2)}) collective-permute-start(bf16[128,2560]{1,0:T(8,128)(2,1)S(1)} %eighth.3), channel_id=1, source_target_pairs={{0,1},{3,2},{4,5},{7,6},{8,9},{11,10},{12,13},{15,14},{16,17},{19,... | collective-permute-start | bytes 1966088 | tf_op jit(solution)/shard_map/ppermute | solution.py:444
  69.2 1.3 collective-permute-start.8
  70.5 1.1 copy-done.13
  71.6 4.6 %partial_projection.5 = (f32[512,1024]{1,0:T(8,128)S(1)}, f32[512,128]{1,0:T(8,128)S(1)}, f32[512,128]{1,0:T(8,128)S(1)}) custom-call(s32[12]{0:T(128)S(1)} %stack.51.places_ref, bf16[256,1280]{1,0:T(8,128)(2,1)} %collective-permute-done.3.refs_0_, bf16[256,1280]{1,0:T(8,128)(2,1)S(1)} %copy-done.11, bf16[256,1280]{1,0:T(8,128)(2,1)S(1)} %copy-done.9, ...), custom_call_target="tpu_custom_call" | custom-call | flops 1 | bytes 1 | tf_op jit(solution)/shard_map/partial_projection/pallas_call | solution.py:100
  76.2 2.5 %queries.2.refs_0_ = bf16[256,1024]{1,0:T(8,128)(2,1)S(1)} custom-call(s32[12]{0:T(128)S(1)} %stack.51.places_ref, bf16[256,1280]{1,0:T(8,128)(2,1)S(1)} %collective-permute-done.1.refs_0_, bf16[256,1280]{1,0:T(8,128)(2,1)S(1)} %collective-permute-done.2.refs_1_, bf16[5120,1024]{1,0:T(8,128)(2,1)S(1)} %bitcast.15, ...), custom_call_target="tpu_custom_call" | custom-call | flops 1 | bytes 1 | tf_op jit(solution)/shard_map/queries/pallas_call | solution.py:187
  78.7 1.1 keys_values.2.refs_0_.refs_2_
  79.8 8.3 %collective-permute-done.8.refs_1_.refs_2_ = bf16[256,1280]{1,0:T(8,128)(2,1)S(1)} collective-permute-done((bf16[256,1280]{1,0:T(8,128)(2,1)S(1)}, bf16[256,1280]{1,0:T(8,128)(2,1)S(1)}, u32[]{:S(2)}, u32[]{:S(2)}) %collective-permute-start.8) | collective-permute-done | bytes 655392 | tf_op jit(solution)/shard_map/ppermute | solution.py:441
  88.2 1.3 keys_values.3
  89.6 1.7 collective-permute-start.14
  91.4 1.7 collective-permute-start.16
  93.2 2.6 %collective-permute-start.18 = (bf16[128,256]{1,0:T(8,128)(2,1)S(1)}, bf16[128,256]{1,0:T(8,128)(2,1)S(1)}, u32[]{:S(2)}, u32[]{:S(2)}) collective-permute-start(bf16[128,256]{1,0:T(8,128)(2,1)S(1)} %get-tuple-element.80), channel_id=1, source_target_pairs={{0,24},{4,28},{8,16},{12,20},{16,8},{20,12},{24,0},{28,4},{1,25},{... | collective-permute-start | bytes 196616 | tf_op jit(solution)/shard_map/ppermute | solution.py:447
  96.6 2.5 %queries.3.refs_1_ = bf16[256,1024]{1,0:T(8,128)(2,1)S(1)} custom-call(s32[12]{0:T(128)S(1)} %stack.51.places_ref, bf16[256,1280]{1,0:T(8,128)(2,1)S(1)} %collective-permute-done.6.refs_0_.refs_1_, bf16[256,1280]{1,0:T(8,128)(2,1)S(1)} %collective-permute-done.8.refs_1_.refs_2_, bf16[5120,1024]{1,0:T(8,128)(2,1)S(1)} %bitcast.15, ...), custom_call_target="tpu_custom_call" | custom-call | flops 1 | bytes 1 | tf_op jit(solution)/shard_map/queries/pallas_call | solution.py:187
  99.1 1.6 collective-permute-done.19.refs_10_
  100.7 3.6 %attention.3.rows_ref = bf16[128,1024]{1,0:T(8,128)(2,1)S(1)} custom-call(s32[12]{0:T(128)S(1)} %stack.51.places_ref, s32[1]{0:T(128)S(6)} %copy.14.length_ref, bf16[256,1024]{1,0:T(8,128)(2,1)S(1)} %queries.2.refs_0_, bf16[256,1024]{1,0:T(8,128)(2,1)S(1)} %queries.3.refs_1_, bf16[256,256]{1,0:T(8,128)(2,1)S(1)} %keys_values.2.refs_0_.refs_2_, ...), custom_call_target="tpu_custom_call" | custom-call | flops 1 | bytes 1 | tf_op jit(solution)/shard_map/attention/pallas_call | solution.py:276
  104.3 1.6 collective-permute-start.20
  107.0 0.9 mix.8.refs_0_
  107.9 0.9 mix.9.refs_0_
  108.8 3.6 %attention.4.rows_ref = bf16[128,1024]{1,0:T(8,128)(2,1)S(1)} custom-call(s32[12]{0:T(128)S(1)} %stack.51.places_ref, s32[1]{0:T(128)S(6)} %copy.14.length_ref, bf16[256,1024]{1,0:T(8,128)(2,1)S(1)} %queries.2.refs_0_, bf16[256,1024]{1,0:T(8,128)(2,1)S(1)} %queries.3.refs_1_, bf16[256,256]{1,0:T(8,128)(2,1)S(1)} %keys_values.2.refs_0_.refs_2_, ...), custom_call_target="tpu_custom_call" | custom-call | flops 1 | bytes 1 | tf_op jit(solution)/shard_map/attention/pallas_call | solution.py:276
  112.3 3.8 %collective-permute-start.26 = (bf16[128,2560]{1,0:T(8,128)(2,1)S(1)}, bf16[128,2560]{1,0:T(8,128)(2,1)S(1)}, u32[]{:S(2)}, u32[]{:S(2)}) collective-permute-start(bf16[128,2560]{1,0:T(8,128)(2,1)S(1)} %mix.8.refs_0_), channel_id=1, source_target_pairs={{0,1},{3,2},{4,5},{7,6},{8,9},{11,10},{12,13},{15,14},{16,17},{19,... | collective-permute-start | bytes 1966088 | tf_op jit(solution)/shard_map/ppermute | solution.py:444
  116.2 1.3 collective-permute-start.25
  117.5 1.4 mix_sent.3.refs_1_
  119.8 5.6 %attention.5 = (bf16[128,1024]{1,0:T(8,128)(2,1)S(1)}, bf16[128,1024]{1,0:T(8,128)(2,1)S(1)}) custom-call(s32[12]{0:T(128)S(1)} %stack.51.places_ref, s32[1]{0:T(128)S(6)} %copy.14.length_ref, bf16[256,1024]{1,0:T(8,128)(2,1)S(1)} %queries.2.refs_0_, bf16[256,1024]{1,0:T(8,128)(2,1)S(1)} %queries.3.refs_1_, bf16[256,256]{1,0:T(8,128)(2,1)S(1)} %keys_values.2.refs_0_.refs_2_, ...), custom_call_target="tpu_custom_call" | custom-call | flops 1 | bytes 1 | tf_op jit(solution)/shard_map/attention/pallas_call | solution.py:276
  125.4 0.9 mix.10.refs_0_
  126.3 0.9 mix.11.refs_0_
  127.1 4.2 %collective-permute-done.26.refs_1_ = bf16[128,2560]{1,0:T(8,128)(2,1)S(1)} collective-permute-done((bf16[128,2560]{1,0:T(8,128)(2,1)S(1)}, bf16[128,2560]{1,0:T(8,128)(2,1)S(1)}, u32[]{:S(2)}, u32[]{:S(2)}) %collective-permute-start.26) | collective-permute-done | bytes 655392 | tf_op jit(solution)/shard_map/ppermute | solution.py:444
  132.1 3.2 %collective-permute-done.25.rows_ref = bf16[128,1024]{1,0:T(8,128)(2,1)S(1)} collective-permute-done((bf16[128,1024]{1,0:T(8,128)(2,1)S(1)}, bf16[128,1024]{1,0:T(8,128)(2,1)S(1)}, u32[]{:S(2)}, u32[]{:S(2)}) %collective-permute-start.25) | collective-permute-done | bytes 262176 | tf_op jit(solution)/shard_map/ppermute | solution.py:444
  135.3 5.2 %collective-permute-start.27 = (bf16[128,2560]{1,0:T(8,128)(2,1)S(1)}, bf16[128,2560]{1,0:T(8,128)(2,1)S(1)}, u32[]{:S(2)}, u32[]{:S(2)}) collective-permute-start(bf16[128,2560]{1,0:T(8,128)(2,1)S(1)} %mix.10.refs_0_), channel_id=1, source_target_pairs={{0,1},{3,2},{4,5},{7,6},{8,9},{11,10},{12,13},{15,14},{16,17},{19,... | collective-permute-start | bytes 1966088 | tf_op jit(solution)/shard_map/ppermute | solution.py:444
  140.5 1.3 collective-permute-start.33
  141.8 1.4 mix_sent.4.refs_1_
  143.4 0.9 mix.12.refs_0_
  145.1 1.3 collective-permute-start.34
  146.4 0.9 mix.13.refs_0_
  147.5 1.3 collective-permute-start.31
  148.8 6.8 %collective-permute-done.27.refs_1_ = bf16[128,2560]{1,0:T(8,128)(2,1)S(1)} collective-permute-done((bf16[128,2560]{1,0:T(8,128)(2,1)S(1)}, bf16[128,2560]{1,0:T(8,128)(2,1)S(1)}, u32[]{:S(2)}, u32[]{:S(2)}) %collective-permute-start.27) | collective-permute-done | bytes 655392 | tf_op jit(solution)/shard_map/ppermute | solution.py:444
  155.8 4.4 %collective-permute-start.30 = (bf16[128,2560]{1,0:T(8,128)(2,1)S(1)}, bf16[128,2560]{1,0:T(8,128)(2,1)S(1)}, u32[]{:S(2)}, u32[]{:S(2)}) collective-permute-start(bf16[128,2560]{1,0:T(8,128)(2,1)S(1)} %mix.13.refs_0_), channel_id=1, source_target_pairs={{0,1},{3,2},{4,5},{7,6},{8,9},{11,10},{12,13},{15,14},{16,17},{19,... | collective-permute-start | bytes 1966088 | tf_op jit(solution)/shard_map/ppermute | solution.py:444
  160.2 1.0 collective-permute-done.33.rows_ref
  161.3 0.9 collective-permute-start.32
  162.2 0.9 mix.14.refs_0_
  163.0 0.9 mix.15.refs_0_
  163.9 1.4 mix_sent.5.refs_1_
  165.4 1.2 added.14.refs_4_
  166.5 5.6 %collective-permute-done.30.refs_1_ = bf16[128,2560]{1,0:T(8,128)(2,1)S(1)} collective-permute-done((bf16[128,2560]{1,0:T(8,128)(2,1)S(1)}, bf16[128,2560]{1,0:T(8,128)(2,1)S(1)}, u32[]{:S(2)}, u32[]{:S(2)}) %collective-permute-start.30) | collective-permute-done | bytes 655392 | tf_op jit(solution)/shard_map/ppermute | solution.py:444
  172.1 4.1 %collective-permute-done.31.refs_2_ = bf16[128,2560]{1,0:T(8,128)(2,1)S(1)} collective-permute-done((bf16[128,2560]{1,0:T(8,128)(2,1)S(1)}, bf16[128,2560]{1,0:T(8,128)(2,1)S(1)}, u32[]{:S(2)}, u32[]{:S(2)}) %collective-permute-start.31) | collective-permute-done | bytes 655392 | tf_op jit(solution)/shard_map/ppermute | solution.py:441
  176.1 1.2 added.15
  (83 shorter events, 8.4 us)
Async XLA Ops:
  0.0 7.9 %copy-start.2 = (bf16[5120,128]{1,0:T(8,128)(2,1)S(1)}, bf16[5120,128]{1,0:T(8,128)(2,1)}, u32[]{:S(2)}) copy-start(bf16[5120,128]{1,0:T(8,128)(2,1)} %refs_3_.7) | copy-start | bytes 3932164
  0.0 32.8 %collective-permute-start = (bf16[512,1280]{1,0:T(8,128)(2,1)}, bf16[512,1280]{1,0:T(8,128)(2,1)S(1)}, u32[]{:S(2)}, u32[]{:S(2)}) collective-permute-start(bf16[512,1280]{1,0:T(8,128)(2,1)} %refs_0_.1), channel_id=1, source_target_pairs={{0,1},{1,0},{2,3},{3,2},{4,5},{5,4},{6,7},{7,6},{8,9},{9,8},{10,11... | collective-permute-start | bytes 3932168 | tf_op jit(solution)/shard_map/ppermute | solution.py:435
  3.0 1.4 copy-start.4
  5.5 12.4 %collective-permute-start.3 = (bf16[256,1280]{1,0:T(8,128)(2,1)}, bf16[256,1280]{1,0:T(8,128)(2,1)}, u32[]{:S(2)}, u32[]{:S(2)}) collective-permute-start(bf16[256,1280]{1,0:T(8,128)(2,1)} %get-tuple-element.55), channel_id=1, source_target_pairs={{1,2},{2,1},{5,6},{6,5},{9,10},{10,9},{13,14},{14,13},{17,18},{18,... | collective-permute-start | bytes 1966088 | tf_op jit(solution)/shard_map/ppermute | solution.py:438
  7.1 12.8 %collective-permute-start.5 = (bf16[256,1280]{1,0:T(8,128)(2,1)}, bf16[256,1280]{1,0:T(8,128)(2,1)S(1)}, u32[]{:S(2)}, u32[]{:S(2)}) collective-permute-start(bf16[256,1280]{1,0:T(8,128)(2,1)} %get-tuple-element.60), channel_id=1, source_target_pairs={{1,2},{2,1},{5,6},{6,5},{9,10},{10,9},{13,14},{14,13},{17,18},{18,... | collective-permute-start | bytes 1966088 | tf_op jit(solution)/shard_map/ppermute | solution.py:438
  7.9 4.0 %copy-start.1 = (bf16[5120,1024]{1,0:T(8,128)(2,1)S(1)}, bf16[5120,1024]{1,0:T(8,128)(2,1)}, u32[]{:S(2)}) copy-start(bf16[5120,1024]{1,0:T(8,128)(2,1)} %refs_2_.8) | copy-start | bytes 31457284
  11.9 1.3 copy-start.3
  13.2 1.3 copy-start.5
  14.5 4.8 %copy-start = (bf16[1024,5120]{1,0:T(8,128)(2,1)S(1)}, bf16[1024,5120]{1,0:T(8,128)(2,1)}, u32[]{:S(2)}) copy-start(bf16[1024,5120]{1,0:T(8,128)(2,1)} %w_ref.19) | copy-start | bytes 31457284
  17.9 28.9 %collective-permute-start.4 = (bf16[256,1280]{1,0:T(8,128)(2,1)}, bf16[256,1280]{1,0:T(8,128)(2,1)S(1)}, u32[]{:S(2)}, u32[]{:S(2)}) collective-permute-start(bf16[256,1280]{1,0:T(8,128)(2,1)} %collective-permute-done.3.refs_0_), channel_id=1, source_target_pairs={{1,0},{2,3},{5,4},{6,7},{9,8},{10,11},{13,12},{14,15},{17,16},{18,... | collective-permute-start | bytes 1966088 | tf_op jit(solution)/shard_map/ppermute | solution.py:441
  19.9 13.1 %copy-start.8 = (bf16[256,1280]{1,0:T(8,128)(2,1)}, bf16[256,1280]{1,0:T(8,128)(2,1)S(1)}, u32[]{:S(2)}) copy-start(bf16[256,1280]{1,0:T(8,128)(2,1)S(1)} %collective-permute-done.5.refs_2_) | copy-start | bytes 1966084
  32.9 20.9 %collective-permute-start.1 = (bf16[256,1280]{1,0:T(8,128)(2,1)S(1)}, bf16[256,1280]{1,0:T(8,128)(2,1)S(1)}, u32[]{:S(2)}, u32[]{:S(2)}) collective-permute-start(bf16[256,1280]{1,0:T(8,128)(2,1)S(1)} %get-tuple-element.53), channel_id=1, source_target_pairs={{1,2},{2,1},{5,6},{6,5},{9,10},{10,9},{13,14},{14,13},{17,18},{18,... | collective-permute-start | bytes 1966088 | tf_op jit(solution)/shard_map/ppermute | solution.py:438
  33.6 27.3 %collective-permute-start.7 = (bf16[256,1280]{1,0:T(8,128)(2,1)}, bf16[256,1280]{1,0:T(8,128)(2,1)S(1)}, u32[]{:S(2)}, u32[]{:S(2)}) collective-permute-start(bf16[256,1280]{1,0:T(8,128)(2,1)} %copy-done.8), channel_id=1, source_target_pairs={{1,0},{2,3},{5,4},{6,7},{9,8},{10,11},{13,12},{14,15},{17,16},{18,... | collective-permute-start | bytes 1966088 | tf_op jit(solution)/shard_map/ppermute | solution.py:441
  46.9 0.8 copy-start.10
  47.7 14.2 %collective-permute-start.9 = (bf16[128,2560]{1,0:T(8,128)(2,1)S(1)}, bf16[128,2560]{1,0:T(8,128)(2,1)S(1)}, u32[]{:S(2)}, u32[]{:S(2)}) collective-permute-start(bf16[128,2560]{1,0:T(8,128)(2,1)S(1)} %eighth.2), channel_id=1, source_target_pairs={{0,1},{3,2},{4,5},{7,6},{8,9},{11,10},{12,13},{15,14},{16,17},{19,... | collective-permute-start | bytes 1966088 | tf_op jit(solution)/shard_map/ppermute | solution.py:444
  49.3 21.2 %slice-start = ((s8[10485760]{0:T(1024)(128)(4,1)}), s8[4194304]{0:T(1024)(128)(4,1)S(1)}, s32[]{:S(2)}) async-start(s8[10485760]{0:T(1024)(128)(4,1)} %bitcast.14), calls=%async_computation | async-start | bytes 8388608
  49.3 21.2 %slice-start.1 = ((s8[10485760]{0:T(1024)(128)(4,1)}), s8[4194304]{0:T(1024)(128)(4,1)S(1)}, s32[]{:S(2)}) async-start(s8[10485760]{0:T(1024)(128)(4,1)} %bitcast.14), calls=%async_computation.1 | async-start | bytes 8388608
  52.9 17.6 %slice-start.2 = ((s8[10485760]{0:T(1024)(128)(4,1)}), s8[2097152]{0:T(1024)(128)(4,1)S(1)}, s32[]{:S(2)}) async-start(s8[10485760]{0:T(1024)(128)(4,1)} %bitcast.14), calls=%async_computation.2 | async-start | bytes 4194304
  53.0 17.6 %copy-start.9 = (bf16[256,1280]{1,0:T(8,128)(2,1)S(1)}, bf16[256,1280]{1,0:T(8,128)(2,1)}, u32[]{:S(2)}) copy-start(bf16[256,1280]{1,0:T(8,128)(2,1)} %copy-done.8) | copy-start | bytes 1966084
  53.0 17.6 %copy-start.11 = (bf16[256,1280]{1,0:T(8,128)(2,1)S(1)}, bf16[256,1280]{1,0:T(8,128)(2,1)}, u32[]{:S(2)}) copy-start(bf16[256,1280]{1,0:T(8,128)(2,1)} %copy-done.10) | copy-start | bytes 1966084
  53.0 16.2 %collective-permute-start.6 = (bf16[256,1280]{1,0:T(8,128)(2,1)S(1)}, bf16[256,1280]{1,0:T(8,128)(2,1)S(1)}, u32[]{:S(2)}, u32[]{:S(2)}) collective-permute-start(bf16[256,1280]{1,0:T(8,128)(2,1)S(1)} %get-tuple-element.68), channel_id=1, source_target_pairs={{1,2},{2,1},{5,6},{6,5},{9,10},{10,9},{13,14},{14,13},{17,18},{18,... | collective-permute-start | bytes 1966088 | tf_op jit(solution)/shard_map/ppermute | solution.py:438
  53.8 22.4 %collective-permute-start.2 = (bf16[256,1280]{1,0:T(8,128)(2,1)S(1)}, bf16[256,1280]{1,0:T(8,128)(2,1)S(1)}, u32[]{:S(2)}, u32[]{:S(2)}) collective-permute-start(bf16[256,1280]{1,0:T(8,128)(2,1)S(1)} %collective-permute-done.1.refs_0_), channel_id=1, source_target_pairs={{1,0},{2,3},{5,4},{6,7},{9,8},{10,11},{13,12},{14,15},{17,16},{18,... | collective-permute-start | bytes 1966088 | tf_op jit(solution)/shard_map/ppermute | solution.py:441
  55.3 20.9 %copy-start.15 = (f32[128]{0:T(128)S(1)}, f32[128]{0:T(128)}, u32[]{:S(2)}) copy-start(f32[128]{0:T(128)} %param.18) | copy-start | bytes 1540
  55.9 20.3 %copy-start.6 = (f32[512,128]{1,0:T(8,128)S(1)}, f32[512,128]{1,0:T(8,128)}, u32[]{:S(2)}) copy-start(f32[512,128]{1,0:T(8,128)} %constant.29.clone.refs_5_.refs_7_.refs_8_) | copy-start | bytes 786436
  55.9 20.3 %copy-start.7 = (f32[512,128]{1,0:T(8,128)S(1)}, f32[512,128]{1,0:T(8,128)}, u32[]{:S(2)}) copy-start(f32[512,128]{1,0:T(8,128)} %constant.30.clone.refs_6_.refs_8_.refs_9_) | copy-start | bytes 786436
  60.9 0.8 copy-start.12
  61.9 17.9 %collective-permute-start.10 = (bf16[128,2560]{1,0:T(8,128)(2,1)S(1)}, bf16[128,2560]{1,0:T(8,128)(2,1)S(1)}, u32[]{:S(2)}, u32[]{:S(2)}) collective-permute-start(bf16[128,2560]{1,0:T(8,128)(2,1)S(1)} %collective-permute-done.9.refs_0_), channel_id=1, source_target_pairs={{0,8},{4,12},{8,0},{12,4},{16,24},{20,28},{24,16},{28,20},{1,9},{5... | collective-permute-start | bytes 1966088 | tf_op jit(solution)/shard_map/ppermute | solution.py:447
  63.7 16.1 %collective-permute-start.11 = (bf16[128,2560]{1,0:T(8,128)(2,1)S(1)}, bf16[128,2560]{1,0:T(8,128)(2,1)S(1)}, u32[]{:S(2)}, u32[]{:S(2)}) collective-permute-start(bf16[128,2560]{1,0:T(8,128)(2,1)S(1)} %collective-permute-done.9.refs_0_), channel_id=1, source_target_pairs={{0,16},{4,20},{8,24},{12,28},{16,0},{20,4},{24,8},{28,12},{1,17},{... | collective-permute-start | bytes 1966088 | tf_op jit(solution)/shard_map/ppermute | solution.py:447
  65.3 14.6 %collective-permute-start.12 = (bf16[128,2560]{1,0:T(8,128)(2,1)S(1)}, bf16[128,2560]{1,0:T(8,128)(2,1)S(1)}, u32[]{:S(2)}, u32[]{:S(2)}) collective-permute-start(bf16[128,2560]{1,0:T(8,128)(2,1)S(1)} %eighth.3), channel_id=1, source_target_pairs={{0,1},{3,2},{4,5},{7,6},{8,9},{11,10},{12,13},{15,14},{16,17},{19,... | collective-permute-start | bytes 1966088 | tf_op jit(solution)/shard_map/ppermute | solution.py:444
  69.2 19.0 %collective-permute-start.8 = (bf16[256,1280]{1,0:T(8,128)(2,1)S(1)}, bf16[256,1280]{1,0:T(8,128)(2,1)S(1)}, u32[]{:S(2)}, u32[]{:S(2)}) collective-permute-start(bf16[256,1280]{1,0:T(8,128)(2,1)S(1)} %collective-permute-done.6.refs_0_.refs_1_), channel_id=1, source_target_pairs={{1,0},{2,3},{5,4},{6,7},{9,8},{10,11},{13,12},{14,15},{17,16},{18,... | collective-permute-start | bytes 1966088 | tf_op jit(solution)/shard_map/ppermute | solution.py:441
  70.5 1.1 copy-start.13
  76.2 2.5 %copy-start.14 = (f32[128]{0:T(128)S(1)}, f32[128]{0:T(128)}, u32[]{:S(2)}) copy-start(f32[128]{0:T(128)} %param.19) | copy-start | bytes 1540
  78.7 9.5 %copy-start.16 = (s32[1,128]{1,0:T(1,128)S(1)}, s32[1,128]{1,0:T(1,128)}, u32[]{:S(2)}) copy-start(s32[1,128]{1,0:T(1,128)} %refs_10_.1) | copy-start | bytes 1540
  89.5 3.7 %collective-permute-start.13 = (bf16[128,256]{1,0:T(8,128)(2,1)S(1)}, bf16[128,256]{1,0:T(8,128)(2,1)S(1)}, u32[]{:S(2)}, u32[]{:S(2)}) collective-permute-start(bf16[128,256]{1,0:T(8,128)(2,1)S(1)} %get-tuple-element.80), channel_id=1, source_target_pairs={{0,4},{4,0},{8,12},{12,8},{16,20},{20,16},{24,28},{28,24},{1,5},{5... | collective-permute-start | bytes 196616 | tf_op jit(solution)/shard_map/ppermute | solution.py:447
  89.6 6.2 %collective-permute-start.14 = (bf16[128,256]{1,0:T(8,128)(2,1)S(1)}, bf16[128,256]{1,0:T(8,128)(2,1)S(1)}, u32[]{:S(2)}, u32[]{:S(2)}) collective-permute-start(bf16[128,256]{1,0:T(8,128)(2,1)S(1)} %get-tuple-element.80), channel_id=1, source_target_pairs={{0,8},{4,12},{8,0},{12,4},{16,24},{20,28},{24,16},{28,20},{1,9},{5... | collective-permute-start | bytes 196616 | tf_op jit(solution)/shard_map/ppermute | solution.py:447
  91.3 7.8 %collective-permute-start.15 = (bf16[128,256]{1,0:T(8,128)(2,1)S(1)}, bf16[128,256]{1,0:T(8,128)(2,1)S(1)}, u32[]{:S(2)}, u32[]{:S(2)}) collective-permute-start(bf16[128,256]{1,0:T(8,128)(2,1)S(1)} %get-tuple-element.80), channel_id=1, source_target_pairs={{0,12},{4,8},{8,4},{12,0},{16,28},{20,24},{24,20},{28,16},{1,13},{... | collective-permute-start | bytes 196616 | tf_op jit(solution)/shard_map/ppermute | solution.py:447
  91.4 7.7 %collective-permute-start.16 = (bf16[128,256]{1,0:T(8,128)(2,1)S(1)}, bf16[128,256]{1,0:T(8,128)(2,1)S(1)}, u32[]{:S(2)}, u32[]{:S(2)}) collective-permute-start(bf16[128,256]{1,0:T(8,128)(2,1)S(1)} %get-tuple-element.80), channel_id=1, source_target_pairs={{0,16},{4,20},{8,24},{12,28},{16,0},{20,4},{24,8},{28,12},{1,17},{... | collective-permute-start | bytes 196616 | tf_op jit(solution)/shard_map/ppermute | solution.py:447
  93.1 6.0 %collective-permute-start.17 = (bf16[128,256]{1,0:T(8,128)(2,1)S(1)}, bf16[128,256]{1,0:T(8,128)(2,1)S(1)}, u32[]{:S(2)}, u32[]{:S(2)}) collective-permute-start(bf16[128,256]{1,0:T(8,128)(2,1)S(1)} %get-tuple-element.80), channel_id=1, source_target_pairs={{0,20},{4,16},{8,28},{12,24},{16,4},{20,0},{24,12},{28,8},{1,21},{... | collective-permute-start | bytes 196616 | tf_op jit(solution)/shard_map/ppermute | solution.py:447
  93.2 6.0 %collective-permute-start.18 = (bf16[128,256]{1,0:T(8,128)(2,1)S(1)}, bf16[128,256]{1,0:T(8,128)(2,1)S(1)}, u32[]{:S(2)}, u32[]{:S(2)}) collective-permute-start(bf16[128,256]{1,0:T(8,128)(2,1)S(1)} %get-tuple-element.80), channel_id=1, source_target_pairs={{0,24},{4,28},{8,16},{12,20},{16,8},{20,12},{24,0},{28,4},{1,25},{... | collective-permute-start | bytes 196616 | tf_op jit(solution)/shard_map/ppermute | solution.py:447
  95.8 4.9 %collective-permute-start.19 = (bf16[128,256]{1,0:T(8,128)(2,1)S(1)}, bf16[128,256]{1,0:T(8,128)(2,1)S(1)}, u32[]{:S(2)}, u32[]{:S(2)}) collective-permute-start(bf16[128,256]{1,0:T(8,128)(2,1)S(1)} %get-tuple-element.80), channel_id=1, source_target_pairs={{0,28},{4,24},{8,20},{12,16},{16,12},{20,8},{24,4},{28,0},{1,29},{... | collective-permute-start | bytes 196616 | tf_op jit(solution)/shard_map/ppermute | solution.py:447
  104.3 8.1 %collective-permute-start.20 = (bf16[128,1024]{1,0:T(8,128)(2,1)S(1)}, bf16[128,1024]{1,0:T(8,128)(2,1)S(1)}, u32[]{:S(2)}, u32[]{:S(2)}) collective-permute-start(bf16[128,1024]{1,0:T(8,128)(2,1)S(1)} %attention.3.rows_ref), channel_id=1, source_target_pairs={{0,1},{3,2},{4,5},{7,6},{8,9},{11,10},{12,13},{15,14},{16,17},{19,... | collective-permute-start | bytes 786440 | tf_op jit(solution)/shard_map/ppermute | solution.py:444
  105.9 10.2 %collective-permute-start.21 = (bf16[128,2560]{1,0:T(8,128)(2,1)S(1)}, bf16[128,2560]{1,0:T(8,128)(2,1)S(1)}, u32[]{:S(2)}, u32[]{:S(2)}) collective-permute-start(bf16[128,2560]{1,0:T(8,128)(2,1)S(1)} %collective-permute-done.9.refs_0_), channel_id=1, source_target_pairs={{0,4},{4,0},{8,12},{12,8},{16,20},{20,16},{24,28},{28,24},{1,5},{5... | collective-permute-start | bytes 1966088 | tf_op jit(solution)/shard_map/ppermute | solution.py:447
  106.0 11.5 %collective-permute-start.22 = (bf16[128,2560]{1,0:T(8,128)(2,1)S(1)}, bf16[128,2560]{1,0:T(8,128)(2,1)S(1)}, u32[]{:S(2)}, u32[]{:S(2)}) collective-permute-start(bf16[128,2560]{1,0:T(8,128)(2,1)S(1)} %collective-permute-done.12.refs_1_), channel_id=1, source_target_pairs={{0,4},{4,0},{8,12},{12,8},{16,20},{20,16},{24,28},{28,24},{1,5},{5... | collective-permute-start | bytes 1966088 | tf_op jit(solution)/shard_map/ppermute | solution.py:447
  106.5 11.0 %collective-permute-start.23 = (bf16[128,2560]{1,0:T(8,128)(2,1)S(1)}, bf16[128,2560]{1,0:T(8,128)(2,1)S(1)}, u32[]{:S(2)}, u32[]{:S(2)}) collective-permute-start(bf16[128,2560]{1,0:T(8,128)(2,1)S(1)} %collective-permute-done.10.refs_2_), channel_id=1, source_target_pairs={{0,4},{4,0},{8,12},{12,8},{16,20},{20,16},{24,28},{28,24},{1,5},{5... | collective-permute-start | bytes 1966088 | tf_op jit(solution)/shard_map/ppermute | solution.py:447
  106.6 10.9 %collective-permute-start.24 = (bf16[128,2560]{1,0:T(8,128)(2,1)S(1)}, bf16[128,2560]{1,0:T(8,128)(2,1)S(1)}, u32[]{:S(2)}, u32[]{:S(2)}) collective-permute-start(bf16[128,2560]{1,0:T(8,128)(2,1)S(1)} %collective-permute-done.11.refs_3_), channel_id=1, source_target_pairs={{0,4},{4,0},{8,12},{12,8},{16,20},{20,16},{24,28},{28,24},{1,5},{5... | collective-permute-start | bytes 1966088 | tf_op jit(solution)/shard_map/ppermute | solution.py:447
  112.3 18.9 %collective-permute-start.26 = (bf16[128,2560]{1,0:T(8,128)(2,1)S(1)}, bf16[128,2560]{1,0:T(8,128)(2,1)S(1)}, u32[]{:S(2)}, u32[]{:S(2)}) collective-permute-start(bf16[128,2560]{1,0:T(8,128)(2,1)S(1)} %mix.8.refs_0_), channel_id=1, source_target_pairs={{0,1},{3,2},{4,5},{7,6},{8,9},{11,10},{12,13},{15,14},{16,17},{19,... | collective-permute-start | bytes 1966088 | tf_op jit(solution)/shard_map/ppermute | solution.py:444
  116.2 19.2 %collective-permute-start.25 = (bf16[128,1024]{1,0:T(8,128)(2,1)S(1)}, bf16[128,1024]{1,0:T(8,128)(2,1)S(1)}, u32[]{:S(2)}, u32[]{:S(2)}) collective-permute-start(bf16[128,1024]{1,0:T(8,128)(2,1)S(1)} %attention.4.rows_ref), channel_id=1, source_target_pairs={{0,1},{3,2},{4,5},{7,6},{8,9},{11,10},{12,13},{15,14},{16,17},{19,... | collective-permute-start | bytes 786440 | tf_op jit(solution)/shard_map/ppermute | solution.py:444
  119.1 24.3 %collective-permute-start.28 = (bf16[128,2560]{1,0:T(8,128)(2,1)S(1)}, bf16[128,2560]{1,0:T(8,128)(2,1)S(1)}, u32[]{:S(2)}, u32[]{:S(2)}) collective-permute-start(bf16[128,2560]{1,0:T(8,128)(2,1)S(1)} %added.8), channel_id=1, source_target_pairs={{1,2},{2,1},{5,6},{6,5},{9,10},{10,9},{13,14},{14,13},{17,18},{18,... | collective-permute-start | bytes 1966088 | tf_op jit(solution)/shard_map/ppermute | solution.py:438
  131.4 15.9 %collective-permute-start.29 = (bf16[128,2560]{1,0:T(8,128)(2,1)S(1)}, bf16[128,2560]{1,0:T(8,128)(2,1)S(1)}, u32[]{:S(2)}, u32[]{:S(2)}) collective-permute-start(bf16[128,2560]{1,0:T(8,128)(2,1)S(1)} %added.9), channel_id=1, source_target_pairs={{1,2},{2,1},{5,6},{6,5},{9,10},{10,9},{13,14},{14,13},{17,18},{18,... | collective-permute-start | bytes 1966088 | tf_op jit(solution)/shard_map/ppermute | solution.py:438
  135.3 20.3 %collective-permute-start.27 = (bf16[128,2560]{1,0:T(8,128)(2,1)S(1)}, bf16[128,2560]{1,0:T(8,128)(2,1)S(1)}, u32[]{:S(2)}, u32[]{:S(2)}) collective-permute-start(bf16[128,2560]{1,0:T(8,128)(2,1)S(1)} %mix.10.refs_0_), channel_id=1, source_target_pairs={{0,1},{3,2},{4,5},{7,6},{8,9},{11,10},{12,13},{15,14},{16,17},{19,... | collective-permute-start | bytes 1966088 | tf_op jit(solution)/shard_map/ppermute | solution.py:444
  140.5 20.7 %collective-permute-start.33 = (bf16[128,1024]{1,0:T(8,128)(2,1)S(1)}, bf16[128,1024]{1,0:T(8,128)(2,1)S(1)}, u32[]{:S(2)}, u32[]{:S(2)}) collective-permute-start(bf16[128,1024]{1,0:T(8,128)(2,1)S(1)} %get-tuple-element.96.rows_ref), channel_id=1, source_target_pairs={{0,1},{3,2},{4,5},{7,6},{8,9},{11,10},{12,13},{15,14},{16,17},{19,... | collective-permute-start | bytes 786440 | tf_op jit(solution)/shard_map/ppermute | solution.py:444
  144.3 21.1 %collective-permute-start.35 = (bf16[128,2560]{1,0:T(8,128)(2,1)S(1)}, bf16[128,2560]{1,0:T(8,128)(2,1)S(1)}, u32[]{:S(2)}, u32[]{:S(2)}) collective-permute-start(bf16[128,2560]{1,0:T(8,128)(2,1)S(1)} %added.10), channel_id=1, source_target_pairs={{1,2},{2,1},{5,6},{6,5},{9,10},{10,9},{13,14},{14,13},{17,18},{18,... | collective-permute-start | bytes 1966088 | tf_op jit(solution)/shard_map/ppermute | solution.py:438
  145.1 20.2 %collective-permute-start.34 = (bf16[128,2560]{1,0:T(8,128)(2,1)S(1)}, bf16[128,2560]{1,0:T(8,128)(2,1)S(1)}, u32[]{:S(2)}, u32[]{:S(2)}) collective-permute-start(bf16[128,2560]{1,0:T(8,128)(2,1)S(1)} %added.11), channel_id=1, source_target_pairs={{1,0},{2,3},{5,4},{6,7},{9,8},{10,11},{13,12},{14,15},{17,16},{18,... | collective-permute-start | bytes 1966088 | tf_op jit(solution)/shard_map/ppermute | solution.py:441
  147.5 28.7 %collective-permute-start.31 = (bf16[128,2560]{1,0:T(8,128)(2,1)S(1)}, bf16[128,2560]{1,0:T(8,128)(2,1)S(1)}, u32[]{:S(2)}, u32[]{:S(2)}) collective-permute-start(bf16[128,2560]{1,0:T(8,128)(2,1)S(1)} %added.12), channel_id=1, source_target_pairs={{1,0},{2,3},{5,4},{6,7},{9,8},{10,11},{13,12},{14,15},{17,16},{18,... | collective-permute-start | bytes 1966088 | tf_op jit(solution)/shard_map/ppermute | solution.py:441
  155.8 16.3 %collective-permute-start.30 = (bf16[128,2560]{1,0:T(8,128)(2,1)S(1)}, bf16[128,2560]{1,0:T(8,128)(2,1)S(1)}, u32[]{:S(2)}, u32[]{:S(2)}) collective-permute-start(bf16[128,2560]{1,0:T(8,128)(2,1)S(1)} %mix.13.refs_0_), channel_id=1, source_target_pairs={{0,1},{3,2},{4,5},{7,6},{8,9},{11,10},{12,13},{15,14},{16,17},{19,... | collective-permute-start | bytes 1966088 | tf_op jit(solution)/shard_map/ppermute | solution.py:444
  161.3 14.9 %collective-permute-start.32 = (bf16[128,2560]{1,0:T(8,128)(2,1)S(1)}, bf16[128,2560]{1,0:T(8,128)(2,1)S(1)}, u32[]{:S(2)}, u32[]{:S(2)}) collective-permute-start(bf16[128,2560]{1,0:T(8,128)(2,1)S(1)} %added.13), channel_id=1, source_target_pairs={{1,2},{2,1},{5,6},{6,5},{9,10},{10,9},{13,14},{14,13},{17,18},{18,... | collective-permute-start | bytes 1966088 | tf_op jit(solution)/shard_map/ppermute | solution.py:438

commit v14 on v13

--- a/solution.py
+++ b/solution.py
@@ -210,12 +210,12 @@
     q_parts, refs = refs[:n_parts], refs[n_parts:]
     own_parts, refs = refs[:n_parts], refs[n_parts:]
     others, refs = refs[:n_others], refs[n_others:]
-    o_refs, (keys_all, values_all) = refs[:-2], refs[-2:]
+    o_ref, keys_all, values_all = refs
     part_rows, width = own_parts[0].shape
     head = width // 2
     picks = others[0].shape[0]
     cross = n_others * picks
-    rows = o_refs[0].shape[0]
+    rows = o_ref.shape[0] // len(slots)
 
     start = 0
     for ref in (*others, *own_parts):
@@ -226,7 +226,7 @@
 
     scale = head ** (-0.5) * LOG2E
     own_rows = n_parts * part_rows
-    for slot, o_ref in zip(slots, o_refs):
+    for block, slot in enumerate(slots):
         first = places_ref[slot] * rows
         offset = pl.multiple_of(lax.rem(first, part_rows), rows)
         row = lax.broadcasted_iota(jnp.int32, (rows, own_rows), 0) + first
@@ -264,7 +264,9 @@
             )
             mixed = jnp.where(kept, mixed / total, 0.0).astype(jnp.bfloat16)
             for index, lane in enumerate(lanes):
-                o_ref[:, lane] = mixed[index * rows : (index + 1) * rows, :]
+                o_ref[block * rows : (block + 1) * rows, lane] = mixed[
+                    index * rows : (index + 1) * rows, :
+                ]
 
 
 def attention(places, slots, rows, lengths, queries, own, others):
@@ -279,35 +281,33 @@
             num_scalar_prefetch=2,
             grid=(1,),
             in_specs=resident(len(queries) + len(own) + len(others)),
-            out_specs=resident(len(slots)),
+            out_specs=resident(1)[0],
             scratch_shapes=[
                 pltpu.VMEM((reach, head), jnp.bfloat16),
                 pltpu.VMEM((reach, head), jnp.bfloat16),
             ],
         ),
-        out_shape=[jax.ShapeDtypeStruct((rows, width), jnp.bfloat16) for _ in slots],
+        out_shape=jax.ShapeDtypeStruct((len(slots) * rows, width), jnp.bfloat16),
         compiler_params=params(24 if reach <= 2048 else 56),
         cost_estimate=cost(1),
         name="attention",
     )(places, lengths, *queries, *own, *others)
 
 
-def mix_kernel(which, tiles, rows_ref, w_ref, out_ref):
-    width = out_ref.shape[1]
+def mix_kernel(which, block, tiles, rows_ref, w_ref, out_ref):
+    height, width = out_ref.shape
+    rows = rows_ref[block * height : (block + 1) * height, :]
     tile = width // tiles
     for start in range(0, width, tile):
         left = which * width + start
-        total = jnp.dot(
-            rows_ref[...], w_ref[:, left : left + tile], preferred_element_type=jnp.float32
-        )
+        total = jnp.dot(rows, w_ref[:, left : left + tile], preferred_element_type=jnp.float32)
         out_ref[:, start : start + tile] = total.astype(out_ref.dtype)
 
 
-def mix(attended, w_out, which):
-    rows = attended.shape[0]
+def mix(attended, w_out, which, rows, block=0):
     width = w_out.shape[1] // 2
     return pl.pallas_call(
-        functools.partial(mix_kernel, which, 5),
+        functools.partial(mix_kernel, which, block, 5),
         in_specs=resident(2),
         out_specs=resident(1)[0],
         out_shape=jax.ShapeDtypeStruct((rows, width), jnp.bfloat16),
@@ -338,13 +338,14 @@
     )(places, w_out)
 
 
-def mix_sent_kernel(tiles, places_ref, rows_ref, *refs):
+def mix_sent_kernel(block, tiles, places_ref, rows_ref, *refs):
     pieces, out_ref = refs[:-1], refs[-1]
+    height = out_ref.shape[0]
     share = rows_ref.shape[1] // len(OFFSETS)
     rows = []
     for index in range(len(OFFSETS)):
         start = pl.multiple_of(places_ref[EIGHTHS + index] * share, share)
-        rows.append(rows_ref[:, pl.ds(start, share)])
+        rows.append(rows_ref[block * height : (block + 1) * height, pl.ds(start, share)])
     rows = jnp.concatenate(rows, axis=1)
     tile = out_ref.shape[1] // tiles
     for start in range(0, out_ref.shape[1], tile):
@@ -354,11 +355,10 @@
         out_ref[:, columns] = total.astype(out_ref.dtype)
 
 
-def mix_sent(places, attended, pieces):
-    rows = attended.shape[0]
+def mix_sent(places, attended, pieces, rows, block=0):
     width = pieces[0].shape[1]
     return pl.pallas_call(
-        functools.partial(mix_sent_kernel, 5),
+        functools.partial(mix_sent_kernel, block, 5),
         grid_spec=pltpu.PrefetchScalarGridSpec(
             num_scalar_prefetch=1,
             grid=(1,),
@@ -370,6 +370,27 @@
         cost_estimate=cost(1),
         name="mix_sent",
     )(places, attended, *pieces)
+
+
+def joined_kernel(*refs):
+    start = 0
+    for ref in refs[:-1]:
+        stop = start + ref.shape[0]
+        refs[-1][start:stop, :] = ref[...]
+        start = stop
+
+
+def joined(arrays):
+    rows = sum(array.shape[0] for array in arrays)
+    return pl.pallas_call(
+        joined_kernel,
+        in_specs=resident(len(arrays)),
+        out_specs=resident(1)[0],
+        out_shape=jax.ShapeDtypeStruct((rows, arrays[0].shape[1]), arrays[0].dtype),
+        compiler_params=params(8),
+        cost_estimate=cost(1),
+        name="joined",
+    )(*arrays)
 
 
 def halves_kernel(ref, first_ref, second_ref):
@@ -482,6 +503,7 @@
         after(places, cue), THIRD, [[a, b] for a, b in zip(from_mid, to_outer)], weights, accs
     )
 
+    pieces = [joined([pieces[offset] for offset in OFFSETS[:4]])] if spread else []
     final = [[a, b] for a, b in zip(to_inner, end)]
     (own_first,) = keys_values(places, final[0], 0, weights[1:], accs[1:], k_gain, *tables)
     first_queries = queries_of(places, final[0], 0, w_query, accs[0], q_gain, *tables)
@@ -502,53 +524,53 @@
     queries = [first_queries, second_queries]
 
     if spread:
-        cue = (others, second_queries)
-        for offset in (0, 6, 2, 4):
-            pieces[offset ^ 1] = between(after(pieces[offset], cue), 1)
-
-    def attend(slots):
-        return attention(places, slots, rows_here // 4, lengths, queries, own, others)
-
-    def send(rows, part):
-        return inward(rows if spread else part)
-
-    def share_of(arrived):
-        if not spread:
-            return arrived
-        return mix_sent(places, arrived, [pieces[offset] for offset in OFFSETS])
-
-    def mixed(rows):
-        return [mix(rows, w_out, which) for which in (0, 1)]
-
-    (far_rows,) = attend((LAST,))
-    far = mixed(far_rows)
-    far_sent = send(far_rows, far[1])
+        pieces.append(between(after(pieces[0], (others, second_queries)), 1))
+    part = rows_here // 4
+
+    def attend(*slots):
+        return attention(places, slots, part, lengths, queries, own, others)
+
+    def mixed(rows, which, block=0):
+        return mix(rows, w_out, which, part, block)
+
+    def share_of(arrived, block=0):
+        return mix_sent(places, arrived, pieces, part, block)
+
+    far_rows = attend(LAST)
+    far = [mixed(far_rows, which) for which in (0, 1)]
     places = after(places, far)
-    (third_rows,) = attend((THIRD,))
-    far_sent = after(far_sent, third_rows)
-    far_in = inward(after(far[0], far_sent))
-    far_right = added(far[1], share_of(far_sent))
-    places = after(places, far_right)
-    near_rows, own_rows = attend((NEAR, OWN))
-    third = mixed(after(third_rows, near_rows))
-    third_sent = send(third_rows, third[1])
+    rows = attend(THIRD, NEAR)
+    if spread:
+        far_sent = after(inward(far_rows), rows)
+        far_in = inward(after(far[0], far_sent))
+        far_share = share_of(far_sent)
+        rows_sent = inward(rows)
+    else:
+        far_in, far_share = inward(far[0]), inward(far[1])
+    far_right = added(far[1], far_share)
+    far_left = added(far[0], after(far_in, far_right))
+    third = [mixed(after(rows, far_left), which) for which in (0, 1)]
     far_right = across(far_right)
-    far_left = added(far[0], after(far_in, third))
-    third_sent = after(third_sent, far_left)
+    if spread:
+        rows_sent = after(rows_sent, third)
+        third_in = inward(after(third[0], rows_sent))
+        third_share = share_of(rows_sent)
+    else:
+        third_in, third_share = inward(third[0]), inward(third[1])
     far_left = across(far_left)
-    third_in = inward(after(third[0], third_sent))
-    third_right = added(third[1], share_of(third_sent))
-    near = [None, mix(after(near_rows, (third_right, far_right)), w_out, 1)]
-    near_sent = send(near_rows, near[1])
+    third_right = added(third[1], third_share)
+    near = [None, mixed(after(rows, (third_right, far_right)), 1, 1)]
     third_right = across(third_right)
     out_right = added(near[1], far_right)
-    near[0] = mix(after(near_rows, out_right), w_out, 0)
+    near[0] = mixed(after(rows, out_right), 0, 1)
     out_left = added(near[0], far_left)
     third_left = added(third[0], after(third_in, out_left))
-    kept = mixed(after(own_rows, third_left))
-    near_sent = share_of(after(near_sent, third_left))
-    result = added(kept[1], near_sent, outward(out_right), third_right, half=1)
     near_in = inward(after(near[0], third_left))
+    places = after(places, third_left)
+    own_rows = attend(OWN)
+    kept = [mixed(own_rows, which) for which in (0, 1)]
+    near_share = share_of(after(rows_sent, kept), 1) if spread else inward(near[1])
+    result = added(kept[1], near_share, outward(out_right), third_right, half=1)
     out_left, third_left = outward(out_left), across(third_left)
     return added(kept[0], near_in, out_left, third_left, half=0, into=result)
 

time: 179 us -> 184 us (1.028)
  waiting for transfers between devices: 64.9 us -> 77.5 us
  starting transfers between devices: 51.7 us -> 45.6 us
    ppermute x8 -> x7, waiting for transfers between devices: 20.9 us -> 27.8 us  [inward(): return lax.ppermute(array, 'tensor', [(0, 1), (3, 2)])]
    ppermute x8 -> x7, starting transfers between devices: 23.1 us -> 18 us  [inward(): return lax.ppermute(array, 'tensor', [(0, 1), (3, 2)])]
    ppermute x6, waiting for transfers between devices: 29.4 us -> 34.3 us  [outward(): return lax.ppermute(array, 'tensor', [(1, 0), (2, 3)])]
    unnamed x40 -> x32, local copies, waits for them, and re-layouts: 10.8 us -> 9.93 us
    ppermute x13 -> x10, starting transfers between devices: 10.9 us -> 10.1 us  [between(): return lax.ppermute(array, 'cand', [(i, i ^ offset) for i in range(n_cand)])]
    pallas_call x11 -> x12, Pallas kernels: 11.1 us -> 11.3 us  [the longest x8 6.93 us: mix(): pl.pallas_call(functools.partial(mix_kernel, which, block, 5), in_specs=r...]
  transfers between devices with their start and end apart: 36 -> 32, of which waited for: 12 -> 13; matrix products, arithmetic and copies ran while one was open for 0% -> 0% of each run, Pallas kernels for 24% -> 25%
where the time goes in v14:
time: 184 us; the launch traced here: 183 us
  waiting for transfers between devices  77.5 us (42%)
  Pallas kernels  48.7 us (26%)
  starting transfers between devices  45.6 us (25%)
  local copies, waits for them, and re-layouts  10 us (5%)
    ppermute x6, waiting for transfers between devices, outward(): return lax.ppermute(array, 'tensor', [(1, 0), (2, 3)])  34.3 us
    ppermute x7, waiting for transfers between devices, inward(): return lax.ppermute(array, 'tensor', [(0, 1), (3, 2)])  27.8 us
    ppermute x7, starting transfers between devices, inward(): return lax.ppermute(array, 'tensor', [(0, 1), (3, 2)])  18 us
    ppermute x1, waiting for transfers between devices, swap(): return lax.ppermute(array, 'tensor', [(0, 1), (1, 0), (2, 3), (3, 2)])  13 us
    pallas_call x3, Pallas kernels, attention(): pl.pallas_call(functools.partial(attention_kernel, slots, n_parts, len(ot...  12.7 us
    pallas_call x3, Pallas kernels, partial_projection(): pl.pallas_call(functools.partial(partial_kernel, [len(part) for part in p...  11.6 us
    ppermute x10, starting transfers between devices, between(): return lax.ppermute(array, 'cand', [(i, i ^ offset) for i in range(n_cand)])  10.1 us
    unnamed x32, local copies, waits for them, and re-layouts  9.93 us
  transfers between devices with their start and end apart: 32, of which 13 were waited for; matrix products, arithmetic and copies ran while one was open for 0% of the time, Pallas kernels for 25%

profile of v14, /device:TPU:0, one launch (start us, length us, event | category | flops | bytes accessed | tf_op | source)
XLA Modules:
  0.0 183.1 jit_solution(2378056064997354103)
XLA Ops:
  0.0 3.0 %collective-permute-start = (bf16[512,1280]{1,0:T(8,128)(2,1)}, bf16[512,1280]{1,0:T(8,128)(2,1)S(1)}, u32[]{:S(2)}, u32[]{:S(2)}) collective-permute-start(bf16[512,1280]{1,0:T(8,128)(2,1)} %refs_0_.1), channel_id=1, source_target_pairs={{0,1},{1,0},{2,3},{3,2},{4,5},{5,4},{6,7},{7,6},{8,9},{9,8},{10,11... | collective-permute-start | bytes 3932168 | tf_op jit(solution)/shard_map/ppermute | solution.py:456
  3.0 1.3 copy-done.4
  4.4 1.2 halves.3
  6.2 1.5 collective-permute-start.5
  7.9 4.0 %copy-done.1 = bf16[5120,1024]{1,0:T(8,128)(2,1)S(1)} copy-done((bf16[5120,1024]{1,0:T(8,128)(2,1)S(1)}, bf16[5120,1024]{1,0:T(8,128)(2,1)}, u32[]{:S(2)}) %copy-start.1) | copy-done | bytes 10485784
  11.8 1.3 copy-done.3
  13.2 1.3 copy-done.5
  14.5 3.4 %partial_projection.3 = (f32[512,1024]{1,0:T(8,128)S(1)}, f32[512,128]{1,0:T(8,128)S(1)}, f32[512,128]{1,0:T(8,128)S(1)}) custom-call(s32[12]{0:T(128)S(1)} %stack.51.places_ref, bf16[512,1280]{1,0:T(8,128)(2,1)S(1)} %copy-done.5, bf16[5120,1024]{1,0:T(8,128)(2,1)S(1)} %copy-done.1, bf16[5120,128]{1,0:T(8,128)(2,1)S(1)} %copy-done.2, ...), custom_call_target="tpu_custom_call" | custom-call | flops 1 | bytes 1 | tf_op jit(solution)/shard_map/partial_projection/pallas_call | solution.py:100
  17.9 1.3 collective-permute-start.4
  19.8 13.0 %collective-permute-done.ref.refs_0_ = bf16[512,1280]{1,0:T(8,128)(2,1)S(1)} collective-permute-done((bf16[512,1280]{1,0:T(8,128)(2,1)}, bf16[512,1280]{1,0:T(8,128)(2,1)S(1)}, u32[]{:S(2)}, u32[]{:S(2)}) %collective-permute-start) | collective-permute-done | bytes 1310752 | tf_op jit(solution)/shard_map/ppermute | solution.py:456
  33.6 1.3 collective-permute-start.7
  34.9 11.9 %collective-permute-done.4.refs_1_ = bf16[256,1280]{1,0:T(8,128)(2,1)S(1)} collective-permute-done((bf16[256,1280]{1,0:T(8,128)(2,1)S(1)}, bf16[256,1280]{1,0:T(8,128)(2,1)S(1)}, u32[]{:S(2)}, u32[]{:S(2)}) %collective-permute-start.4) | collective-permute-done | bytes 655392 | tf_op jit(solution)/shard_map/ppermute | solution.py:462
  46.9 1.5 collective-permute-start.9
  48.4 3.6 %partial_projection.4 = (f32[512,1024]{1,0:T(8,128)S(1)}, f32[512,128]{1,0:T(8,128)S(1)}, f32[512,128]{1,0:T(8,128)S(1)}) custom-call(s32[12]{0:T(128)S(1)} %stack.51.places_ref, bf16[512,1280]{1,0:T(8,128)(2,1)S(1)} %collective-permute-done.ref.refs_0_, bf16[5120,1024]{1,0:T(8,128)(2,1)S(1)} %copy-done.1, bf16[5120,128]{1,0:T(8,128)(2,1)S(1)} %copy-done.2, ...), custom_call_target="tpu_custom_call" | custom-call | flops 1 | bytes 1 | tf_op jit(solution)/shard_map/partial_projection/pallas_call | solution.py:100
  52.0 0.8 collective-permute-start.6
  52.9 1.3 collective-permute-start.2
  54.8 6.1 %collective-permute-done.7.refs_3_ = bf16[256,1280]{1,0:T(8,128)(2,1)S(1)} collective-permute-done((bf16[256,1280]{1,0:T(8,128)(2,1)}, bf16[256,1280]{1,0:T(8,128)(2,1)S(1)}, u32[]{:S(2)}, u32[]{:S(2)}) %collective-permute-start.7) | collective-permute-done | bytes 655392 | tf_op jit(solution)/shard_map/ppermute | solution.py:462
  60.9 0.8 copy-done.8
  61.8 1.6 collective-permute-start.10
  63.4 2.0 %collective-permute-start.11 = (bf16[128,2560]{1,0:T(8,128)(2,1)S(1)}, bf16[128,2560]{1,0:T(8,128)(2,1)S(1)}, u32[]{:S(2)}, u32[]{:S(2)}) collective-permute-start(bf16[128,2560]{1,0:T(8,128)(2,1)S(1)} %collective-permute-done.9.refs_0_), channel_id=1, source_target_pairs={{0,8},{4,12},{8,0},{12,4},{16,24},{20,28},{24,16},{28,20},{1,9},{5... | collective-permute-start | bytes 1966088 | tf_op jit(solution)/shard_map/ppermute | solution.py:468
  65.4 1.5 collective-permute-start.12
  66.9 1.3 collective-permute-start.8
  68.3 1.1 copy-done.9
  69.3 4.6 %partial_projection.5 = (f32[512,1024]{1,0:T(8,128)S(1)}, f32[512,128]{1,0:T(8,128)S(1)}, f32[512,128]{1,0:T(8,128)S(1)}) custom-call(s32[12]{0:T(128)S(1)} %stack.51.places_ref, bf16[256,1280]{1,0:T(8,128)(2,1)S(1)} %collective-permute-done.3.refs_0_, bf16[256,1280]{1,0:T(8,128)(2,1)S(1)} %collective-permute-done.4.refs_1_, ...), custom_call_target="tpu_custom_call" | custom-call | flops 1 | bytes 1 | tf_op jit(solution)/shard_map/partial_projection/pallas_call | solution.py:100
  73.9 1.6 collective-permute-done.2.refs_1_
  75.6 2.5 %queries.2.refs_0_ = bf16[256,1024]{1,0:T(8,128)(2,1)S(1)} custom-call(s32[12]{0:T(128)S(1)} %stack.51.places_ref, bf16[256,1280]{1,0:T(8,128)(2,1)S(1)} %collective-permute-done.1.refs_0_, bf16[256,1280]{1,0:T(8,128)(2,1)S(1)} %collective-permute-done.2.refs_1_, bf16[5120,1024]{1,0:T(8,128)(2,1)S(1)} %bitcast.15, ...), custom_call_target="tpu_custom_call" | custom-call | flops 1 | bytes 1 | tf_op jit(solution)/shard_map/queries/pallas_call | solution.py:187
  78.1 1.1 keys_values.2.refs_0_.refs_2_
  79.5 8.7 %collective-permute-done.8.refs_1_.refs_2_ = bf16[256,1280]{1,0:T(8,128)(2,1)S(1)} collective-permute-done((bf16[256,1280]{1,0:T(8,128)(2,1)S(1)}, bf16[256,1280]{1,0:T(8,128)(2,1)S(1)}, u32[]{:S(2)}, u32[]{:S(2)}) %collective-permute-start.8) | collective-permute-done | bytes 655392 | tf_op jit(solution)/shard_map/ppermute | solution.py:462
  88.2 1.3 keys_values.3
  89.6 1.7 collective-permute-start.14
  91.4 1.7 collective-permute-start.16
  93.2 2.6 %collective-permute-start.18 = (bf16[128,256]{1,0:T(8,128)(2,1)S(1)}, bf16[128,256]{1,0:T(8,128)(2,1)S(1)}, u32[]{:S(2)}, u32[]{:S(2)}) collective-permute-start(bf16[128,256]{1,0:T(8,128)(2,1)S(1)} %get-tuple-element.74), channel_id=1, source_target_pairs={{0,24},{4,28},{8,16},{12,20},{16,8},{20,12},{24,0},{28,4},{1,25},{... | collective-permute-start | bytes 196616 | tf_op jit(solution)/shard_map/ppermute | solution.py:468
  96.0 2.5 %queries.3.refs_1_ = bf16[256,1024]{1,0:T(8,128)(2,1)S(1)} custom-call(s32[12]{0:T(128)S(1)} %stack.51.places_ref, bf16[256,1280]{1,0:T(8,128)(2,1)S(1)} %collective-permute-done.6.refs_0_.refs_1_, bf16[256,1280]{1,0:T(8,128)(2,1)S(1)} %collective-permute-done.8.refs_1_.refs_2_, bf16[5120,1024]{1,0:T(8,128)(2,1)S(1)} %bitcast.15, ...), custom_call_target="tpu_custom_call" | custom-call | flops 1 | bytes 1 | tf_op jit(solution)/shard_map/queries/pallas_call | solution.py:187
  98.7 2.0 %collective-permute-done.19.refs_10_ = bf16[128,256]{1,0:T(8,128)(2,1)S(1)} collective-permute-done((bf16[128,256]{1,0:T(8,128)(2,1)S(1)}, bf16[128,256]{1,0:T(8,128)(2,1)S(1)}, u32[]{:S(2)}, u32[]{:S(2)}) %collective-permute-start.19) | collective-permute-done | bytes 65568 | tf_op jit(solution)/shard_map/ppermute | solution.py:468
  101.5 3.6 %attention.3.rows_ref = bf16[128,1024]{1,0:T(8,128)(2,1)S(1)} custom-call(s32[12]{0:T(128)S(1)} %stack.51.places_ref, s32[1]{0:T(128)S(6)} %copy.14.length_ref, bf16[256,1024]{1,0:T(8,128)(2,1)S(1)} %queries.2.refs_0_, bf16[256,1024]{1,0:T(8,128)(2,1)S(1)} %queries.3.refs_1_, bf16[256,256]{1,0:T(8,128)(2,1)S(1)} %keys_values.2.refs_0_.refs_2_, ...), custom_call_target="tpu_custom_call" | custom-call | flops 1 | bytes 1 | tf_op jit(solution)/shard_map/attention/pallas_call | solution.py:278
  105.1 1.6 collective-permute-start.20
  106.8 0.9 mix.8.refs_0_
  107.6 0.9 mix.9.refs_0_
  108.5 5.6 %attention.4.rows_ref = bf16[256,1024]{1,0:T(8,128)(2,1)S(1)} custom-call(s32[12]{0:T(128)S(1)} %stack.51.places_ref, s32[1]{0:T(128)S(6)} %copy.14.length_ref, bf16[256,1024]{1,0:T(8,128)(2,1)S(1)} %queries.2.refs_0_, bf16[256,1024]{1,0:T(8,128)(2,1)S(1)} %queries.3.refs_1_, bf16[256,256]{1,0:T(8,128)(2,1)S(1)} %keys_values.2.refs_0_.refs_2_, ...), custom_call_target="tpu_custom_call" | custom-call | flops 1 | bytes 1 | tf_op jit(solution)/shard_map/attention/pallas_call | solution.py:278
  114.1 3.0 %collective-permute-start.21 = (bf16[128,2560]{1,0:T(8,128)(2,1)S(1)}, bf16[128,2560]{1,0:T(8,128)(2,1)S(1)}, u32[]{:S(2)}, u32[]{:S(2)}) collective-permute-start(bf16[128,2560]{1,0:T(8,128)(2,1)S(1)} %mix.8.refs_0_), channel_id=1, source_target_pairs={{0,1},{3,2},{4,5},{7,6},{8,9},{11,10},{12,13},{15,14},{16,17},{19,... | collective-permute-start | bytes 1966088 | tf_op jit(solution)/shard_map/ppermute | solution.py:465
  117.2 1.3 collective-permute-start.23
  118.5 1.4 mix_sent.3.refs_1_
  120.1 0.7 collective-permute-start.25
  120.8 11.5 %collective-permute-done.21.refs_1_ = bf16[128,2560]{1,0:T(8,128)(2,1)S(1)} collective-permute-done((bf16[128,2560]{1,0:T(8,128)(2,1)S(1)}, bf16[128,2560]{1,0:T(8,128)(2,1)S(1)}, u32[]{:S(2)}, u32[]{:S(2)}) %collective-permute-start.21) | collective-permute-done | bytes 655392 | tf_op jit(solution)/shard_map/ppermute | solution.py:465
  132.4 0.9 mix.10.refs_0_
  133.3 0.9 mix.11.refs_0_
  134.2 0.7 collective-permute-start.26
  134.9 7.3 %collective-permute-done.23.rows_ref = bf16[256,1024]{1,0:T(8,128)(2,1)S(1)} collective-permute-done((bf16[256,1024]{1,0:T(8,128)(2,1)S(1)}, bf16[256,1024]{1,0:T(8,128)(2,1)S(1)}, u32[]{:S(2)}, u32[]{:S(2)}) %collective-permute-start.23) | collective-permute-done | bytes 524320 | tf_op jit(solution)/shard_map/ppermute | solution.py:465
  142.2 4.4 %collective-permute-start.24 = (bf16[128,2560]{1,0:T(8,128)(2,1)S(1)}, bf16[128,2560]{1,0:T(8,128)(2,1)S(1)}, u32[]{:S(2)}, u32[]{:S(2)}) collective-permute-start(bf16[128,2560]{1,0:T(8,128)(2,1)S(1)} %mix.10.refs_0_), channel_id=1, source_target_pairs={{0,1},{3,2},{4,5},{7,6},{8,9},{11,10},{12,13},{15,14},{16,17},{19,... | collective-permute-start | bytes 1966088 | tf_op jit(solution)/shard_map/ppermute | solution.py:465
  146.6 1.4 mix_sent.4.refs_1_
  148.2 0.9 mix.12.refs_0_
  149.9 1.5 collective-permute-start.30
  151.4 0.9 mix.13.refs_0_
  152.5 7.0 %collective-permute-done.24.refs_1_ = bf16[128,2560]{1,0:T(8,128)(2,1)S(1)} collective-permute-done((bf16[128,2560]{1,0:T(8,128)(2,1)S(1)}, bf16[128,2560]{1,0:T(8,128)(2,1)S(1)}, u32[]{:S(2)}, u32[]{:S(2)}) %collective-permute-start.24) | collective-permute-done | bytes 655392 | tf_op jit(solution)/shard_map/ppermute | solution.py:465
  159.6 4.4 %collective-permute-start.27 = (bf16[128,2560]{1,0:T(8,128)(2,1)S(1)}, bf16[128,2560]{1,0:T(8,128)(2,1)S(1)}, u32[]{:S(2)}, u32[]{:S(2)}) collective-permute-start(bf16[128,2560]{1,0:T(8,128)(2,1)S(1)} %mix.13.refs_0_), channel_id=1, source_target_pairs={{0,1},{3,2},{4,5},{7,6},{8,9},{11,10},{12,13},{15,14},{16,17},{19,... | collective-permute-start | bytes 1966088 | tf_op jit(solution)/shard_map/ppermute | solution.py:465
  164.1 1.3 collective-permute-start.28
  166.1 3.6 %attention.5.rows_ref = bf16[128,1024]{1,0:T(8,128)(2,1)S(1)} custom-call(s32[12]{0:T(128)S(1)} %stack.51.places_ref, s32[1]{0:T(128)S(6)} %copy.14.length_ref, bf16[256,1024]{1,0:T(8,128)(2,1)S(1)} %queries.2.refs_0_, bf16[256,1024]{1,0:T(8,128)(2,1)S(1)} %queries.3.refs_1_, bf16[256,256]{1,0:T(8,128)(2,1)S(1)} %keys_values.2.refs_0_.refs_2_, ...), custom_call_target="tpu_custom_call" | custom-call | flops 1 | bytes 1 | tf_op jit(solution)/shard_map/attention/pallas_call | solution.py:278
  169.7 0.9 mix.14.refs_0_
  170.5 0.9 mix.15.refs_0_
  171.4 1.4 mix_sent.5.refs_1_
  172.8 1.2 added.14.refs_4_
  174.0 2.0 %collective-permute-done.27.refs_1_ = bf16[128,2560]{1,0:T(8,128)(2,1)S(1)} collective-permute-done((bf16[128,2560]{1,0:T(8,128)(2,1)S(1)}, bf16[128,2560]{1,0:T(8,128)(2,1)S(1)}, u32[]{:S(2)}, u32[]{:S(2)}) %collective-permute-start.27) | collective-permute-done | bytes 655392 | tf_op jit(solution)/shard_map/ppermute | solution.py:465
  176.0 5.9 %collective-permute-done.28.refs_2_ = bf16[128,2560]{1,0:T(8,128)(2,1)S(1)} collective-permute-done((bf16[128,2560]{1,0:T(8,128)(2,1)S(1)}, bf16[128,2560]{1,0:T(8,128)(2,1)S(1)}, u32[]{:S(2)}, u32[]{:S(2)}) %collective-permute-start.28) | collective-permute-done | bytes 655392 | tf_op jit(solution)/shard_map/ppermute | solution.py:462
  181.9 1.2 added.15
  (68 shorter events, 6.3 us)
Async XLA Ops:
  0.0 7.8 %copy-start.2 = (bf16[5120,128]{1,0:T(8,128)(2,1)S(1)}, bf16[5120,128]{1,0:T(8,128)(2,1)}, u32[]{:S(2)}) copy-start(bf16[5120,128]{1,0:T(8,128)(2,1)} %refs_3_.7) | copy-start | bytes 3932164
  0.0 32.8 %collective-permute-start = (bf16[512,1280]{1,0:T(8,128)(2,1)}, bf16[512,1280]{1,0:T(8,128)(2,1)S(1)}, u32[]{:S(2)}, u32[]{:S(2)}) collective-permute-start(bf16[512,1280]{1,0:T(8,128)(2,1)} %refs_0_.1), channel_id=1, source_target_pairs={{0,1},{1,0},{2,3},{3,2},{4,5},{5,4},{6,7},{7,6},{8,9},{9,8},{10,11... | collective-permute-start | bytes 3932168 | tf_op jit(solution)/shard_map/ppermute | solution.py:456
  3.0 1.4 copy-start.4
  5.5 12.4 %collective-permute-start.3 = (bf16[256,1280]{1,0:T(8,128)(2,1)}, bf16[256,1280]{1,0:T(8,128)(2,1)S(1)}, u32[]{:S(2)}, u32[]{:S(2)}) collective-permute-start(bf16[256,1280]{1,0:T(8,128)(2,1)} %get-tuple-element.49), channel_id=1, source_target_pairs={{1,2},{2,1},{5,6},{6,5},{9,10},{10,9},{13,14},{14,13},{17,18},{18,... | collective-permute-start | bytes 1966088 | tf_op jit(solution)/shard_map/ppermute | solution.py:459
  6.2 13.6 %collective-permute-start.5 = (bf16[256,1280]{1,0:T(8,128)(2,1)}, bf16[256,1280]{1,0:T(8,128)(2,1)}, u32[]{:S(2)}, u32[]{:S(2)}) collective-permute-start(bf16[256,1280]{1,0:T(8,128)(2,1)} %get-tuple-element.54), channel_id=1, source_target_pairs={{1,2},{2,1},{5,6},{6,5},{9,10},{10,9},{13,14},{14,13},{17,18},{18,... | collective-permute-start | bytes 1966088 | tf_op jit(solution)/shard_map/ppermute | solution.py:459
  7.9 4.0 %copy-start.1 = (bf16[5120,1024]{1,0:T(8,128)(2,1)S(1)}, bf16[5120,1024]{1,0:T(8,128)(2,1)}, u32[]{:S(2)}) copy-start(bf16[5120,1024]{1,0:T(8,128)(2,1)} %refs_2_.8) | copy-start | bytes 31457284
  11.8 1.3 copy-start.3
  13.2 1.3 copy-start.5
  14.5 4.8 %copy-start = (bf16[1024,5120]{1,0:T(8,128)(2,1)S(1)}, bf16[1024,5120]{1,0:T(8,128)(2,1)}, u32[]{:S(2)}) copy-start(bf16[1024,5120]{1,0:T(8,128)(2,1)} %w_ref.19) | copy-start | bytes 31457284
  17.9 29.0 %collective-permute-start.4 = (bf16[256,1280]{1,0:T(8,128)(2,1)S(1)}, bf16[256,1280]{1,0:T(8,128)(2,1)S(1)}, u32[]{:S(2)}, u32[]{:S(2)}) collective-permute-start(bf16[256,1280]{1,0:T(8,128)(2,1)S(1)} %collective-permute-done.3.refs_0_), channel_id=1, source_target_pairs={{1,0},{2,3},{5,4},{6,7},{9,8},{10,11},{13,12},{14,15},{17,16},{18,... | collective-permute-start | bytes 1966088 | tf_op jit(solution)/shard_map/ppermute | solution.py:462
  32.9 19.9 %collective-permute-start.1 = (bf16[256,1280]{1,0:T(8,128)(2,1)S(1)}, bf16[256,1280]{1,0:T(8,128)(2,1)S(1)}, u32[]{:S(2)}, u32[]{:S(2)}) collective-permute-start(bf16[256,1280]{1,0:T(8,128)(2,1)S(1)} %get-tuple-element.47), channel_id=1, source_target_pairs={{1,2},{2,1},{5,6},{6,5},{9,10},{10,9},{13,14},{14,13},{17,18},{18,... | collective-permute-start | bytes 1966088 | tf_op jit(solution)/shard_map/ppermute | solution.py:459
  33.6 27.3 %collective-permute-start.7 = (bf16[256,1280]{1,0:T(8,128)(2,1)}, bf16[256,1280]{1,0:T(8,128)(2,1)S(1)}, u32[]{:S(2)}, u32[]{:S(2)}) collective-permute-start(bf16[256,1280]{1,0:T(8,128)(2,1)} %collective-permute-done.5.refs_2_), channel_id=1, source_target_pairs={{1,0},{2,3},{5,4},{6,7},{9,8},{10,11},{13,12},{14,15},{17,16},{18,... | collective-permute-start | bytes 1966088 | tf_op jit(solution)/shard_map/ppermute | solution.py:462
  46.9 16.5 %collective-permute-start.9 = (bf16[128,2560]{1,0:T(8,128)(2,1)S(1)}, bf16[128,2560]{1,0:T(8,128)(2,1)S(1)}, u32[]{:S(2)}, u32[]{:S(2)}) collective-permute-start(bf16[128,2560]{1,0:T(8,128)(2,1)S(1)} %eighth.2), channel_id=1, source_target_pairs={{0,1},{3,2},{4,5},{7,6},{8,9},{11,10},{12,13},{15,14},{16,17},{19,... | collective-permute-start | bytes 1966088 | tf_op jit(solution)/shard_map/ppermute | solution.py:465
  48.4 19.9 %slice-start = ((s8[10485760]{0:T(1024)(128)(4,1)}), s8[4194304]{0:T(1024)(128)(4,1)S(1)}, s32[]{:S(2)}) async-start(s8[10485760]{0:T(1024)(128)(4,1)} %bitcast.14), calls=%async_computation | async-start | bytes 8388608
  48.4 19.8 %slice-start.1 = ((s8[10485760]{0:T(1024)(128)(4,1)}), s8[4194304]{0:T(1024)(128)(4,1)S(1)}, s32[]{:S(2)}) async-start(s8[10485760]{0:T(1024)(128)(4,1)} %bitcast.14), calls=%async_computation.1 | async-start | bytes 8388608
  52.0 16.2 %slice-start.2 = ((s8[10485760]{0:T(1024)(128)(4,1)}), s8[2097152]{0:T(1024)(128)(4,1)S(1)}, s32[]{:S(2)}) async-start(s8[10485760]{0:T(1024)(128)(4,1)} %bitcast.14), calls=%async_computation.2 | async-start | bytes 4194304
  52.0 14.9 %collective-permute-start.6 = (bf16[256,1280]{1,0:T(8,128)(2,1)S(1)}, bf16[256,1280]{1,0:T(8,128)(2,1)S(1)}, u32[]{:S(2)}, u32[]{:S(2)}) collective-permute-start(bf16[256,1280]{1,0:T(8,128)(2,1)S(1)} %get-tuple-element.62), channel_id=1, source_target_pairs={{1,2},{2,1},{5,6},{6,5},{9,10},{10,9},{13,14},{14,13},{17,18},{18,... | collective-permute-start | bytes 1966088 | tf_op jit(solution)/shard_map/ppermute | solution.py:459
  52.9 22.7 %collective-permute-start.2 = (bf16[256,1280]{1,0:T(8,128)(2,1)S(1)}, bf16[256,1280]{1,0:T(8,128)(2,1)S(1)}, u32[]{:S(2)}, u32[]{:S(2)}) collective-permute-start(bf16[256,1280]{1,0:T(8,128)(2,1)S(1)} %collective-permute-done.1.refs_0_), channel_id=1, source_target_pairs={{1,0},{2,3},{5,4},{6,7},{9,8},{10,11},{13,12},{14,15},{17,16},{18,... | collective-permute-start | bytes 1966088 | tf_op jit(solution)/shard_map/ppermute | solution.py:462
  54.2 21.4 %copy-start.11 = (f32[128]{0:T(128)S(1)}, f32[128]{0:T(128)}, u32[]{:S(2)}) copy-start(f32[128]{0:T(128)} %param.18) | copy-start | bytes 1540
  54.8 20.8 %copy-start.6 = (f32[512,128]{1,0:T(8,128)S(1)}, f32[512,128]{1,0:T(8,128)}, u32[]{:S(2)}) copy-start(f32[512,128]{1,0:T(8,128)} %constant.29.clone.refs_5_.refs_7_.refs_8_) | copy-start | bytes 786436
  54.8 20.8 %copy-start.7 = (f32[512,128]{1,0:T(8,128)S(1)}, f32[512,128]{1,0:T(8,128)}, u32[]{:S(2)}) copy-start(f32[512,128]{1,0:T(8,128)} %constant.30.clone.refs_6_.refs_8_.refs_9_) | copy-start | bytes 786436
  60.9 0.8 copy-start.8
  61.8 17.4 %collective-permute-start.10 = (bf16[128,2560]{1,0:T(8,128)(2,1)S(1)}, bf16[128,2560]{1,0:T(8,128)(2,1)S(1)}, u32[]{:S(2)}, u32[]{:S(2)}) collective-permute-start(bf16[128,2560]{1,0:T(8,128)(2,1)S(1)} %eighth.3), channel_id=1, source_target_pairs={{0,1},{3,2},{4,5},{7,6},{8,9},{11,10},{12,13},{15,14},{16,17},{19,... | collective-permute-start | bytes 1966088 | tf_op jit(solution)/shard_map/ppermute | solution.py:465
  63.4 15.8 %collective-permute-start.11 = (bf16[128,2560]{1,0:T(8,128)(2,1)S(1)}, bf16[128,2560]{1,0:T(8,128)(2,1)S(1)}, u32[]{:S(2)}, u32[]{:S(2)}) collective-permute-start(bf16[128,2560]{1,0:T(8,128)(2,1)S(1)} %collective-permute-done.9.refs_0_), channel_id=1, source_target_pairs={{0,8},{4,12},{8,0},{12,4},{16,24},{20,28},{24,16},{28,20},{1,9},{5... | collective-permute-start | bytes 1966088 | tf_op jit(solution)/shard_map/ppermute | solution.py:468
  65.4 13.9 %collective-permute-start.12 = (bf16[128,2560]{1,0:T(8,128)(2,1)S(1)}, bf16[128,2560]{1,0:T(8,128)(2,1)S(1)}, u32[]{:S(2)}, u32[]{:S(2)}) collective-permute-start(bf16[128,2560]{1,0:T(8,128)(2,1)S(1)} %collective-permute-done.9.refs_0_), channel_id=1, source_target_pairs={{0,16},{4,20},{8,24},{12,28},{16,0},{20,4},{24,8},{28,12},{1,17},{... | collective-permute-start | bytes 1966088 | tf_op jit(solution)/shard_map/ppermute | solution.py:468
  66.9 21.3 %collective-permute-start.8 = (bf16[256,1280]{1,0:T(8,128)(2,1)S(1)}, bf16[256,1280]{1,0:T(8,128)(2,1)S(1)}, u32[]{:S(2)}, u32[]{:S(2)}) collective-permute-start(bf16[256,1280]{1,0:T(8,128)(2,1)S(1)} %collective-permute-done.6.refs_0_.refs_1_), channel_id=1, source_target_pairs={{1,0},{2,3},{5,4},{6,7},{9,8},{10,11},{13,12},{14,15},{17,16},{18,... | collective-permute-start | bytes 1966088 | tf_op jit(solution)/shard_map/ppermute | solution.py:462
  68.2 1.1 copy-start.9
  75.6 2.5 %copy-start.10 = (f32[128]{0:T(128)S(1)}, f32[128]{0:T(128)}, u32[]{:S(2)}) copy-start(f32[128]{0:T(128)} %param.19) | copy-start | bytes 1540
  79.2 9.0 %copy-start.12 = (s32[1,128]{1,0:T(1,128)S(1)}, s32[1,128]{1,0:T(1,128)}, u32[]{:S(2)}) copy-start(s32[1,128]{1,0:T(1,128)} %refs_10_.1) | copy-start | bytes 1540
  89.5 3.7 %collective-permute-start.13 = (bf16[128,256]{1,0:T(8,128)(2,1)S(1)}, bf16[128,256]{1,0:T(8,128)(2,1)S(1)}, u32[]{:S(2)}, u32[]{:S(2)}) collective-permute-start(bf16[128,256]{1,0:T(8,128)(2,1)S(1)} %get-tuple-element.74), channel_id=1, source_target_pairs={{0,4},{4,0},{8,12},{12,8},{16,20},{20,16},{24,28},{28,24},{1,5},{5... | collective-permute-start | bytes 196616 | tf_op jit(solution)/shard_map/ppermute | solution.py:468
  89.6 6.2 %collective-permute-start.14 = (bf16[128,256]{1,0:T(8,128)(2,1)S(1)}, bf16[128,256]{1,0:T(8,128)(2,1)S(1)}, u32[]{:S(2)}, u32[]{:S(2)}) collective-permute-start(bf16[128,256]{1,0:T(8,128)(2,1)S(1)} %get-tuple-element.74), channel_id=1, source_target_pairs={{0,8},{4,12},{8,0},{12,4},{16,24},{20,28},{24,16},{28,20},{1,9},{5... | collective-permute-start | bytes 196616 | tf_op jit(solution)/shard_map/ppermute | solution.py:468
  91.3 7.2 %collective-permute-start.15 = (bf16[128,256]{1,0:T(8,128)(2,1)S(1)}, bf16[128,256]{1,0:T(8,128)(2,1)S(1)}, u32[]{:S(2)}, u32[]{:S(2)}) collective-permute-start(bf16[128,256]{1,0:T(8,128)(2,1)S(1)} %get-tuple-element.74), channel_id=1, source_target_pairs={{0,12},{4,8},{8,4},{12,0},{16,28},{20,24},{24,20},{28,16},{1,13},{... | collective-permute-start | bytes 196616 | tf_op jit(solution)/shard_map/ppermute | solution.py:468
  91.4 7.0 %collective-permute-start.16 = (bf16[128,256]{1,0:T(8,128)(2,1)S(1)}, bf16[128,256]{1,0:T(8,128)(2,1)S(1)}, u32[]{:S(2)}, u32[]{:S(2)}) collective-permute-start(bf16[128,256]{1,0:T(8,128)(2,1)S(1)} %get-tuple-element.74), channel_id=1, source_target_pairs={{0,16},{4,20},{8,24},{12,28},{16,0},{20,4},{24,8},{28,12},{1,17},{... | collective-permute-start | bytes 196616 | tf_op jit(solution)/shard_map/ppermute | solution.py:468
  93.1 5.6 %collective-permute-start.17 = (bf16[128,256]{1,0:T(8,128)(2,1)S(1)}, bf16[128,256]{1,0:T(8,128)(2,1)S(1)}, u32[]{:S(2)}, u32[]{:S(2)}) collective-permute-start(bf16[128,256]{1,0:T(8,128)(2,1)S(1)} %get-tuple-element.74), channel_id=1, source_target_pairs={{0,20},{4,16},{8,28},{12,24},{16,4},{20,0},{24,12},{28,8},{1,21},{... | collective-permute-start | bytes 196616 | tf_op jit(solution)/shard_map/ppermute | solution.py:468
  93.2 5.5 %collective-permute-start.18 = (bf16[128,256]{1,0:T(8,128)(2,1)S(1)}, bf16[128,256]{1,0:T(8,128)(2,1)S(1)}, u32[]{:S(2)}, u32[]{:S(2)}) collective-permute-start(bf16[128,256]{1,0:T(8,128)(2,1)S(1)} %get-tuple-element.74), channel_id=1, source_target_pairs={{0,24},{4,28},{8,16},{12,20},{16,8},{20,12},{24,0},{28,4},{1,25},{... | collective-permute-start | bytes 196616 | tf_op jit(solution)/shard_map/ppermute | solution.py:468
  95.8 4.9 %collective-permute-start.19 = (bf16[128,256]{1,0:T(8,128)(2,1)S(1)}, bf16[128,256]{1,0:T(8,128)(2,1)S(1)}, u32[]{:S(2)}, u32[]{:S(2)}) collective-permute-start(bf16[128,256]{1,0:T(8,128)(2,1)S(1)} %get-tuple-element.74), channel_id=1, source_target_pairs={{0,28},{4,24},{8,20},{12,16},{16,12},{20,8},{24,4},{28,0},{1,29},{... | collective-permute-start | bytes 196616 | tf_op jit(solution)/shard_map/ppermute | solution.py:468
  100.7 17.8 %collective-permute-start.22 = (bf16[512,2560]{1,0:T(8,128)(2,1)S(1)}, bf16[512,2560]{1,0:T(8,128)(2,1)S(1)}, u32[]{:S(2)}, u32[]{:S(2)}) collective-permute-start(bf16[512,2560]{1,0:T(8,128)(2,1)S(1)} %joined.1.refs_0_), channel_id=1, source_target_pairs={{0,4},{4,0},{8,12},{12,8},{16,20},{20,16},{24,28},{28,24},{1,5},{5... | collective-permute-start | bytes 7864328 | tf_op jit(solution)/shard_map/ppermute | solution.py:468
  105.1 9.0 %collective-permute-start.20 = (bf16[128,1024]{1,0:T(8,128)(2,1)S(1)}, bf16[128,1024]{1,0:T(8,128)(2,1)S(1)}, u32[]{:S(2)}, u32[]{:S(2)}) collective-permute-start(bf16[128,1024]{1,0:T(8,128)(2,1)S(1)} %attention.3.rows_ref), channel_id=1, source_target_pairs={{0,1},{3,2},{4,5},{7,6},{8,9},{11,10},{12,13},{15,14},{16,17},{19,... | collective-permute-start | bytes 786440 | tf_op jit(solution)/shard_map/ppermute | solution.py:465
  114.1 18.2 %collective-permute-start.21 = (bf16[128,2560]{1,0:T(8,128)(2,1)S(1)}, bf16[128,2560]{1,0:T(8,128)(2,1)S(1)}, u32[]{:S(2)}, u32[]{:S(2)}) collective-permute-start(bf16[128,2560]{1,0:T(8,128)(2,1)S(1)} %mix.8.refs_0_), channel_id=1, source_target_pairs={{0,1},{3,2},{4,5},{7,6},{8,9},{11,10},{12,13},{15,14},{16,17},{19,... | collective-permute-start | bytes 1966088 | tf_op jit(solution)/shard_map/ppermute | solution.py:465
  117.2 25.0 %collective-permute-start.23 = (bf16[256,1024]{1,0:T(8,128)(2,1)S(1)}, bf16[256,1024]{1,0:T(8,128)(2,1)S(1)}, u32[]{:S(2)}, u32[]{:S(2)}) collective-permute-start(bf16[256,1024]{1,0:T(8,128)(2,1)S(1)} %attention.4.rows_ref), channel_id=1, source_target_pairs={{0,1},{3,2},{4,5},{7,6},{8,9},{11,10},{12,13},{15,14},{16,17},{19,... | collective-permute-start | bytes 1572872 | tf_op jit(solution)/shard_map/ppermute | solution.py:465
  120.1 28.1 %collective-permute-start.25 = (bf16[128,2560]{1,0:T(8,128)(2,1)S(1)}, bf16[128,2560]{1,0:T(8,128)(2,1)S(1)}, u32[]{:S(2)}, u32[]{:S(2)}) collective-permute-start(bf16[128,2560]{1,0:T(8,128)(2,1)S(1)} %added.8), channel_id=1, source_target_pairs={{1,2},{2,1},{5,6},{6,5},{9,10},{10,9},{13,14},{14,13},{17,18},{18,... | collective-permute-start | bytes 1966088 | tf_op jit(solution)/shard_map/ppermute | solution.py:459
  134.2 18.2 %collective-permute-start.26 = (bf16[128,2560]{1,0:T(8,128)(2,1)S(1)}, bf16[128,2560]{1,0:T(8,128)(2,1)S(1)}, u32[]{:S(2)}, u32[]{:S(2)}) collective-permute-start(bf16[128,2560]{1,0:T(8,128)(2,1)S(1)} %added.9), channel_id=1, source_target_pairs={{1,2},{2,1},{5,6},{6,5},{9,10},{10,9},{13,14},{14,13},{17,18},{18,... | collective-permute-start | bytes 1966088 | tf_op jit(solution)/shard_map/ppermute | solution.py:459
  142.2 17.3 %collective-permute-start.24 = (bf16[128,2560]{1,0:T(8,128)(2,1)S(1)}, bf16[128,2560]{1,0:T(8,128)(2,1)S(1)}, u32[]{:S(2)}, u32[]{:S(2)}) collective-permute-start(bf16[128,2560]{1,0:T(8,128)(2,1)S(1)} %mix.10.refs_0_), channel_id=1, source_target_pairs={{0,1},{3,2},{4,5},{7,6},{8,9},{11,10},{12,13},{15,14},{16,17},{19,... | collective-permute-start | bytes 1966088 | tf_op jit(solution)/shard_map/ppermute | solution.py:465
  149.1 23.8 %collective-permute-start.31 = (bf16[128,2560]{1,0:T(8,128)(2,1)S(1)}, bf16[128,2560]{1,0:T(8,128)(2,1)S(1)}, u32[]{:S(2)}, u32[]{:S(2)}) collective-permute-start(bf16[128,2560]{1,0:T(8,128)(2,1)S(1)} %added.10), channel_id=1, source_target_pairs={{1,2},{2,1},{5,6},{6,5},{9,10},{10,9},{13,14},{14,13},{17,18},{18,... | collective-permute-start | bytes 1966088 | tf_op jit(solution)/shard_map/ppermute | solution.py:459
  149.9 22.9 %collective-permute-start.30 = (bf16[128,2560]{1,0:T(8,128)(2,1)S(1)}, bf16[128,2560]{1,0:T(8,128)(2,1)S(1)}, u32[]{:S(2)}, u32[]{:S(2)}) collective-permute-start(bf16[128,2560]{1,0:T(8,128)(2,1)S(1)} %added.11), channel_id=1, source_target_pairs={{1,0},{2,3},{5,4},{6,7},{9,8},{10,11},{13,12},{14,15},{17,16},{18,... | collective-permute-start | bytes 1966088 | tf_op jit(solution)/shard_map/ppermute | solution.py:462
  159.6 16.4 %collective-permute-start.27 = (bf16[128,2560]{1,0:T(8,128)(2,1)S(1)}, bf16[128,2560]{1,0:T(8,128)(2,1)S(1)}, u32[]{:S(2)}, u32[]{:S(2)}) collective-permute-start(bf16[128,2560]{1,0:T(8,128)(2,1)S(1)} %mix.13.refs_0_), channel_id=1, source_target_pairs={{0,1},{3,2},{4,5},{7,6},{8,9},{11,10},{12,13},{15,14},{16,17},{19,... | collective-permute-start | bytes 1966088 | tf_op jit(solution)/shard_map/ppermute | solution.py:465
  164.1 17.8 %collective-permute-start.28 = (bf16[128,2560]{1,0:T(8,128)(2,1)S(1)}, bf16[128,2560]{1,0:T(8,128)(2,1)S(1)}, u32[]{:S(2)}, u32[]{:S(2)}) collective-permute-start(bf16[128,2560]{1,0:T(8,128)(2,1)S(1)} %added.12), channel_id=1, source_target_pairs={{1,0},{2,3},{5,4},{6,7},{9,8},{10,11},{13,12},{14,15},{17,16},{18,... | collective-permute-start | bytes 1966088 | tf_op jit(solution)/shard_map/ppermute | solution.py:462
  165.4 16.5 %collective-permute-start.29 = (bf16[128,2560]{1,0:T(8,128)(2,1)S(1)}, bf16[128,2560]{1,0:T(8,128)(2,1)S(1)}, u32[]{:S(2)}, u32[]{:S(2)}) collective-permute-start(bf16[128,2560]{1,0:T(8,128)(2,1)S(1)} %added.13), channel_id=1, source_target_pairs={{1,2},{2,1},{5,6},{6,5},{9,10},{10,9},{13,14},{14,13},{17,18},{18,... | collective-permute-start | bytes 1966088 | tf_op jit(solution)/shard_map/ppermute | solution.py:459

commit v15 on v13

--- a/solution.py
+++ b/solution.py
@@ -497,7 +497,7 @@
         summary_pos,
     )
     own = [own_first, own_second]
-    others = [between(summary, offset) for offset in range(1, n_cand)]
+    others = [between(summary, offset) for offset in reversed(range(1, n_cand))]
     second_queries = queries_of(places, final[1], 1, w_query, accs[0], q_gain, *tables)
     queries = [first_queries, second_queries]
 

time: 179 us -> 178 us (level)
  waiting for transfers between devices: 64.9 us -> 63 us
where the time goes in v15:
time: 178 us; the launch traced here: 176 us
  waiting for transfers between devices  63 us (35%)
  starting transfers between devices  52.2 us (29%)
  Pallas kernels  48.4 us (27%)
  local copies, waits for them, and re-layouts  10.9 us (6%)
    ppermute x6, waiting for transfers between devices, outward(): return lax.ppermute(array, 'tensor', [(1, 0), (2, 3)])  29.2 us
    ppermute x8, starting transfers between devices, inward(): return lax.ppermute(array, 'tensor', [(0, 1), (3, 2)])  23.2 us
    ppermute x8, waiting for transfers between devices, inward(): return lax.ppermute(array, 'tensor', [(0, 1), (3, 2)])  20.5 us
    ppermute x1, waiting for transfers between devices, swap(): return lax.ppermute(array, 'tensor', [(0, 1), (1, 0), (2, 3), (3, 2)])  13 us
    pallas_call x3, Pallas kernels, attention(): pl.pallas_call(functools.partial(attention_kernel, slots, n_parts, len(ot...  12.7 us
    pallas_call x3, Pallas kernels, partial_projection(): pl.pallas_call(functools.partial(partial_kernel, [len(part) for part in p...  11.6 us
    ppermute x13, starting transfers between devices, between(): return lax.ppermute(array, 'cand', [(i, i ^ offset) for i in range(n_cand)])  11.3 us
    unnamed x40, local copies, waits for them, and re-layouts  10.8 us
  transfers between devices with their start and end apart: 36, of which 12 were waited for; matrix products, arithmetic and copies ran while one was open for 0% of the time, Pallas kernels for 24%

profile of v15, /device:TPU:0, one launch (start us, length us, event | category | flops | bytes accessed | tf_op | source)
XLA Modules:
  0.0 175.8 jit_solution(18277805788875162322)
XLA Ops:
  0.0 3.0 %collective-permute-start = (bf16[512,1280]{1,0:T(8,128)(2,1)}, bf16[512,1280]{1,0:T(8,128)(2,1)S(1)}, u32[]{:S(2)}, u32[]{:S(2)}) collective-permute-start(bf16[512,1280]{1,0:T(8,128)(2,1)} %refs_0_.1), channel_id=1, source_target_pairs={{0,1},{1,0},{2,3},{3,2},{4,5},{5,4},{6,7},{7,6},{8,9},{9,8},{10,11... | collective-permute-start | bytes 3932168 | tf_op jit(solution)/shard_map/ppermute | solution.py:435
  3.0 1.3 copy-done.4
  4.4 1.2 halves.3
  5.5 1.5 collective-permute-start.3
  7.9 4.0 %copy-done.1 = bf16[5120,1024]{1,0:T(8,128)(2,1)S(1)} copy-done((bf16[5120,1024]{1,0:T(8,128)(2,1)S(1)}, bf16[5120,1024]{1,0:T(8,128)(2,1)}, u32[]{:S(2)}) %copy-start.1) | copy-done | bytes 10485784
  11.9 1.3 copy-done.3
  13.2 1.3 copy-done.5
  14.5 3.4 %partial_projection.3 = (f32[512,1024]{1,0:T(8,128)S(1)}, f32[512,128]{1,0:T(8,128)S(1)}, f32[512,128]{1,0:T(8,128)S(1)}) custom-call(s32[12]{0:T(128)S(1)} %stack.51.places_ref, bf16[512,1280]{1,0:T(8,128)(2,1)S(1)} %copy-done.5, bf16[5120,1024]{1,0:T(8,128)(2,1)S(1)} %copy-done.1, bf16[5120,128]{1,0:T(8,128)(2,1)S(1)} %copy-done.2, ...), custom_call_target="tpu_custom_call" | custom-call | flops 1 | bytes 1 | tf_op jit(solution)/shard_map/partial_projection/pallas_call | solution.py:100
  17.9 1.3 collective-permute-start.4
  19.9 13.0 %collective-permute-done.ref.refs_0_ = bf16[512,1280]{1,0:T(8,128)(2,1)S(1)} collective-permute-done((bf16[512,1280]{1,0:T(8,128)(2,1)}, bf16[512,1280]{1,0:T(8,128)(2,1)S(1)}, u32[]{:S(2)}, u32[]{:S(2)}) %collective-permute-start) | collective-permute-done | bytes 1310752 | tf_op jit(solution)/shard_map/ppermute | solution.py:435
  33.6 1.3 collective-permute-start.7
  34.9 11.9 %collective-permute-done.4.refs_1_ = bf16[256,1280]{1,0:T(8,128)(2,1)S(1)} collective-permute-done((bf16[256,1280]{1,0:T(8,128)(2,1)}, bf16[256,1280]{1,0:T(8,128)(2,1)S(1)}, u32[]{:S(2)}, u32[]{:S(2)}) %collective-permute-start.4) | collective-permute-done | bytes 655392 | tf_op jit(solution)/shard_map/ppermute | solution.py:441
  46.9 0.8 copy-done.10
  47.7 1.6 collective-permute-start.9
  49.3 3.6 %partial_projection.4 = (f32[512,1024]{1,0:T(8,128)S(1)}, f32[512,128]{1,0:T(8,128)S(1)}, f32[512,128]{1,0:T(8,128)S(1)}) custom-call(s32[12]{0:T(128)S(1)} %stack.51.places_ref, bf16[512,1280]{1,0:T(8,128)(2,1)S(1)} %collective-permute-done.ref.refs_0_, bf16[5120,1024]{1,0:T(8,128)(2,1)S(1)} %copy-done.1, bf16[5120,128]{1,0:T(8,128)(2,1)S(1)} %copy-done.2, ...), custom_call_target="tpu_custom_call" | custom-call | flops 1 | bytes 1 | tf_op jit(solution)/shard_map/partial_projection/pallas_call | solution.py:100
  53.8 1.4 collective-permute-start.2
  55.9 5.0 %collective-permute-done.7.refs_3_ = bf16[256,1280]{1,0:T(8,128)(2,1)S(1)} collective-permute-done((bf16[256,1280]{1,0:T(8,128)(2,1)}, bf16[256,1280]{1,0:T(8,128)(2,1)S(1)}, u32[]{:S(2)}, u32[]{:S(2)}) %collective-permute-start.7) | collective-permute-done | bytes 655392 | tf_op jit(solution)/shard_map/ppermute | solution.py:441
  61.9 1.9 %collective-permute-start.10 = (bf16[128,2560]{1,0:T(8,128)(2,1)S(1)}, bf16[128,2560]{1,0:T(8,128)(2,1)S(1)}, u32[]{:S(2)}, u32[]{:S(2)}) collective-permute-start(bf16[128,2560]{1,0:T(8,128)(2,1)S(1)} %collective-permute-done.9.refs_0_), channel_id=1, source_target_pairs={{0,8},{4,12},{8,0},{12,4},{16,24},{20,28},{24,16},{28,20},{1,9},{5... | collective-permute-start | bytes 1966088 | tf_op jit(solution)/shard_map/ppermute | solution.py:447
  63.7 1.5 collective-permute-start.11
  65.3 3.9 %collective-permute-start.12 = (bf16[128,2560]{1,0:T(8,128)(2,1)S(1)}, bf16[128,2560]{1,0:T(8,128)(2,1)S(1)}, u32[]{:S(2)}, u32[]{:S(2)}) collective-permute-start(bf16[128,2560]{1,0:T(8,128)(2,1)S(1)} %eighth.3), channel_id=1, source_target_pairs={{0,1},{3,2},{4,5},{7,6},{8,9},{11,10},{12,13},{15,14},{16,17},{19,... | collective-permute-start | bytes 1966088 | tf_op jit(solution)/shard_map/ppermute | solution.py:444
  69.2 1.3 collective-permute-start.8
  70.5 1.1 copy-done.13
  71.6 4.6 %partial_projection.5 = (f32[512,1024]{1,0:T(8,128)S(1)}, f32[512,128]{1,0:T(8,128)S(1)}, f32[512,128]{1,0:T(8,128)S(1)}) custom-call(s32[12]{0:T(128)S(1)} %stack.51.places_ref, bf16[256,1280]{1,0:T(8,128)(2,1)} %collective-permute-done.3.refs_0_, bf16[256,1280]{1,0:T(8,128)(2,1)S(1)} %copy-done.11, bf16[256,1280]{1,0:T(8,128)(2,1)S(1)} %copy-done.9, ...), custom_call_target="tpu_custom_call" | custom-call | flops 1 | bytes 1 | tf_op jit(solution)/shard_map/partial_projection/pallas_call | solution.py:100
  76.2 2.5 %queries.2.refs_0_ = bf16[256,1024]{1,0:T(8,128)(2,1)S(1)} custom-call(s32[12]{0:T(128)S(1)} %stack.51.places_ref, bf16[256,1280]{1,0:T(8,128)(2,1)S(1)} %collective-permute-done.1.refs_0_, bf16[256,1280]{1,0:T(8,128)(2,1)S(1)} %collective-permute-done.2.refs_1_, bf16[5120,1024]{1,0:T(8,128)(2,1)S(1)} %bitcast.15, ...), custom_call_target="tpu_custom_call" | custom-call | flops 1 | bytes 1 | tf_op jit(solution)/shard_map/queries/pallas_call | solution.py:187
  78.7 1.1 keys_values.2.refs_0_.refs_2_
  79.8 8.3 %collective-permute-done.8.refs_1_.refs_2_ = bf16[256,1280]{1,0:T(8,128)(2,1)S(1)} collective-permute-done((bf16[256,1280]{1,0:T(8,128)(2,1)S(1)}, bf16[256,1280]{1,0:T(8,128)(2,1)S(1)}, u32[]{:S(2)}, u32[]{:S(2)}) %collective-permute-start.8) | collective-permute-done | bytes 655392 | tf_op jit(solution)/shard_map/ppermute | solution.py:441
  88.2 1.3 keys_values.3
  89.5 0.9 collective-permute-start.13
  90.4 1.8 %collective-permute-start.14 = (bf16[128,256]{1,0:T(8,128)(2,1)S(1)}, bf16[128,256]{1,0:T(8,128)(2,1)S(1)}, u32[]{:S(2)}, u32[]{:S(2)}) collective-permute-start(bf16[128,256]{1,0:T(8,128)(2,1)S(1)} %get-tuple-element.80), channel_id=1, source_target_pairs={{0,24},{4,28},{8,16},{12,20},{16,8},{20,12},{24,0},{28,4},{1,25},{... | collective-permute-start | bytes 196616 | tf_op jit(solution)/shard_map/ppermute | solution.py:447
  92.3 1.4 collective-permute-start.15
  94.0 0.9 collective-permute-start.17
  94.9 1.0 collective-permute-start.18
  97.0 2.5 %queries.3.refs_1_ = bf16[256,1024]{1,0:T(8,128)(2,1)S(1)} custom-call(s32[12]{0:T(128)S(1)} %stack.51.places_ref, bf16[256,1280]{1,0:T(8,128)(2,1)S(1)} %collective-permute-done.6.refs_0_.refs_1_, bf16[256,1280]{1,0:T(8,128)(2,1)S(1)} %collective-permute-done.8.refs_1_.refs_2_, bf16[5120,1024]{1,0:T(8,128)(2,1)S(1)} %bitcast.15, ...), custom_call_target="tpu_custom_call" | custom-call | flops 1 | bytes 1 | tf_op jit(solution)/shard_map/queries/pallas_call | solution.py:187
  99.8 3.6 %attention.3.rows_ref = bf16[128,1024]{1,0:T(8,128)(2,1)S(1)} custom-call(s32[12]{0:T(128)S(1)} %stack.51.places_ref, s32[1]{0:T(128)S(6)} %copy.14.length_ref, bf16[256,1024]{1,0:T(8,128)(2,1)S(1)} %queries.2.refs_0_, bf16[256,1024]{1,0:T(8,128)(2,1)S(1)} %queries.3.refs_1_, bf16[256,256]{1,0:T(8,128)(2,1)S(1)} %keys_values.2.refs_0_.refs_2_, ...), custom_call_target="tpu_custom_call" | custom-call | flops 1 | bytes 1 | tf_op jit(solution)/shard_map/attention/pallas_call | solution.py:276
  103.3 1.6 collective-permute-start.20
  106.1 0.9 mix.8.refs_0_
  107.0 0.9 mix.9.refs_0_
  107.8 3.6 %attention.4.rows_ref = bf16[128,1024]{1,0:T(8,128)(2,1)S(1)} custom-call(s32[12]{0:T(128)S(1)} %stack.51.places_ref, s32[1]{0:T(128)S(6)} %copy.14.length_ref, bf16[256,1024]{1,0:T(8,128)(2,1)S(1)} %queries.2.refs_0_, bf16[256,1024]{1,0:T(8,128)(2,1)S(1)} %queries.3.refs_1_, bf16[256,256]{1,0:T(8,128)(2,1)S(1)} %keys_values.2.refs_0_.refs_2_, ...), custom_call_target="tpu_custom_call" | custom-call | flops 1 | bytes 1 | tf_op jit(solution)/shard_map/attention/pallas_call | solution.py:276
  111.4 3.7 %collective-permute-start.26 = (bf16[128,2560]{1,0:T(8,128)(2,1)S(1)}, bf16[128,2560]{1,0:T(8,128)(2,1)S(1)}, u32[]{:S(2)}, u32[]{:S(2)}) collective-permute-start(bf16[128,2560]{1,0:T(8,128)(2,1)S(1)} %mix.8.refs_0_), channel_id=1, source_target_pairs={{0,1},{3,2},{4,5},{7,6},{8,9},{11,10},{12,13},{15,14},{16,17},{19,... | collective-permute-start | bytes 1966088 | tf_op jit(solution)/shard_map/ppermute | solution.py:444
  115.1 1.3 collective-permute-start.25
  116.5 1.4 mix_sent.3.refs_1_
  118.7 5.6 %attention.5 = (bf16[128,1024]{1,0:T(8,128)(2,1)S(1)}, bf16[128,1024]{1,0:T(8,128)(2,1)S(1)}) custom-call(s32[12]{0:T(128)S(1)} %stack.51.places_ref, s32[1]{0:T(128)S(6)} %copy.14.length_ref, bf16[256,1024]{1,0:T(8,128)(2,1)S(1)} %queries.2.refs_0_, bf16[256,1024]{1,0:T(8,128)(2,1)S(1)} %queries.3.refs_1_, bf16[256,256]{1,0:T(8,128)(2,1)S(1)} %keys_values.2.refs_0_.refs_2_, ...), custom_call_target="tpu_custom_call" | custom-call | flops 1 | bytes 1 | tf_op jit(solution)/shard_map/attention/pallas_call | solution.py:276
  124.3 0.9 mix.10.refs_0_
  125.2 0.9 mix.11.refs_0_
  126.1 4.2 %collective-permute-done.26.refs_1_ = bf16[128,2560]{1,0:T(8,128)(2,1)S(1)} collective-permute-done((bf16[128,2560]{1,0:T(8,128)(2,1)S(1)}, bf16[128,2560]{1,0:T(8,128)(2,1)S(1)}, u32[]{:S(2)}, u32[]{:S(2)}) %collective-permute-start.26) | collective-permute-done | bytes 655392 | tf_op jit(solution)/shard_map/ppermute | solution.py:444
  131.1 3.1 %collective-permute-done.25.rows_ref = bf16[128,1024]{1,0:T(8,128)(2,1)S(1)} collective-permute-done((bf16[128,1024]{1,0:T(8,128)(2,1)S(1)}, bf16[128,1024]{1,0:T(8,128)(2,1)S(1)}, u32[]{:S(2)}, u32[]{:S(2)}) %collective-permute-start.25) | collective-permute-done | bytes 262176 | tf_op jit(solution)/shard_map/ppermute | solution.py:444
  134.2 5.3 %collective-permute-start.27 = (bf16[128,2560]{1,0:T(8,128)(2,1)S(1)}, bf16[128,2560]{1,0:T(8,128)(2,1)S(1)}, u32[]{:S(2)}, u32[]{:S(2)}) collective-permute-start(bf16[128,2560]{1,0:T(8,128)(2,1)S(1)} %mix.10.refs_0_), channel_id=1, source_target_pairs={{0,1},{3,2},{4,5},{7,6},{8,9},{11,10},{12,13},{15,14},{16,17},{19,... | collective-permute-start | bytes 1966088 | tf_op jit(solution)/shard_map/ppermute | solution.py:444
  139.5 1.3 collective-permute-start.33
  140.8 1.4 mix_sent.4.refs_1_
  142.4 0.9 mix.12.refs_0_
  144.2 1.3 collective-permute-start.34
  145.5 0.9 mix.13.refs_0_
  146.5 1.3 collective-permute-start.31
  147.8 6.9 %collective-permute-done.27.refs_1_ = bf16[128,2560]{1,0:T(8,128)(2,1)S(1)} collective-permute-done((bf16[128,2560]{1,0:T(8,128)(2,1)S(1)}, bf16[128,2560]{1,0:T(8,128)(2,1)S(1)}, u32[]{:S(2)}, u32[]{:S(2)}) %collective-permute-start.27) | collective-permute-done | bytes 655392 | tf_op jit(solution)/shard_map/ppermute | solution.py:444
  154.8 4.4 %collective-permute-start.30 = (bf16[128,2560]{1,0:T(8,128)(2,1)S(1)}, bf16[128,2560]{1,0:T(8,128)(2,1)S(1)}, u32[]{:S(2)}, u32[]{:S(2)}) collective-permute-start(bf16[128,2560]{1,0:T(8,128)(2,1)S(1)} %mix.13.refs_0_), channel_id=1, source_target_pairs={{0,1},{3,2},{4,5},{7,6},{8,9},{11,10},{12,13},{15,14},{16,17},{19,... | collective-permute-start | bytes 1966088 | tf_op jit(solution)/shard_map/ppermute | solution.py:444
  159.2 1.0 collective-permute-done.33.rows_ref
  160.3 0.9 collective-permute-start.32
  161.2 0.9 mix.14.refs_0_
  162.1 0.9 mix.15.refs_0_
  162.9 1.4 mix_sent.5.refs_1_
  164.4 1.2 added.14.refs_4_
  165.5 5.3 %collective-permute-done.30.refs_1_ = bf16[128,2560]{1,0:T(8,128)(2,1)S(1)} collective-permute-done((bf16[128,2560]{1,0:T(8,128)(2,1)S(1)}, bf16[128,2560]{1,0:T(8,128)(2,1)S(1)}, u32[]{:S(2)}, u32[]{:S(2)}) %collective-permute-start.30) | collective-permute-done | bytes 655392 | tf_op jit(solution)/shard_map/ppermute | solution.py:444
  170.8 3.9 %collective-permute-done.31.refs_2_ = bf16[128,2560]{1,0:T(8,128)(2,1)S(1)} collective-permute-done((bf16[128,2560]{1,0:T(8,128)(2,1)S(1)}, bf16[128,2560]{1,0:T(8,128)(2,1)S(1)}, u32[]{:S(2)}, u32[]{:S(2)}) %collective-permute-start.31) | collective-permute-done | bytes 655392 | tf_op jit(solution)/shard_map/ppermute | solution.py:441
  174.7 1.2 added.15
  (83 shorter events, 9.8 us)
Async XLA Ops:
  0.0 7.9 %copy-start.2 = (bf16[5120,128]{1,0:T(8,128)(2,1)S(1)}, bf16[5120,128]{1,0:T(8,128)(2,1)}, u32[]{:S(2)}) copy-start(bf16[5120,128]{1,0:T(8,128)(2,1)} %refs_3_.7) | copy-start | bytes 3932164
  0.0 32.8 %collective-permute-start = (bf16[512,1280]{1,0:T(8,128)(2,1)}, bf16[512,1280]{1,0:T(8,128)(2,1)S(1)}, u32[]{:S(2)}, u32[]{:S(2)}) collective-permute-start(bf16[512,1280]{1,0:T(8,128)(2,1)} %refs_0_.1), channel_id=1, source_target_pairs={{0,1},{1,0},{2,3},{3,2},{4,5},{5,4},{6,7},{7,6},{8,9},{9,8},{10,11... | collective-permute-start | bytes 3932168 | tf_op jit(solution)/shard_map/ppermute | solution.py:435
  3.0 1.4 copy-start.4
  5.5 12.4 %collective-permute-start.3 = (bf16[256,1280]{1,0:T(8,128)(2,1)}, bf16[256,1280]{1,0:T(8,128)(2,1)}, u32[]{:S(2)}, u32[]{:S(2)}) collective-permute-start(bf16[256,1280]{1,0:T(8,128)(2,1)} %get-tuple-element.55), channel_id=1, source_target_pairs={{1,2},{2,1},{5,6},{6,5},{9,10},{10,9},{13,14},{14,13},{17,18},{18,... | collective-permute-start | bytes 1966088 | tf_op jit(solution)/shard_map/ppermute | solution.py:438
  7.1 12.8 %collective-permute-start.5 = (bf16[256,1280]{1,0:T(8,128)(2,1)}, bf16[256,1280]{1,0:T(8,128)(2,1)S(1)}, u32[]{:S(2)}, u32[]{:S(2)}) collective-permute-start(bf16[256,1280]{1,0:T(8,128)(2,1)} %get-tuple-element.60), channel_id=1, source_target_pairs={{1,2},{2,1},{5,6},{6,5},{9,10},{10,9},{13,14},{14,13},{17,18},{18,... | collective-permute-start | bytes 1966088 | tf_op jit(solution)/shard_map/ppermute | solution.py:438
  7.9 4.0 %copy-start.1 = (bf16[5120,1024]{1,0:T(8,128)(2,1)S(1)}, bf16[5120,1024]{1,0:T(8,128)(2,1)}, u32[]{:S(2)}) copy-start(bf16[5120,1024]{1,0:T(8,128)(2,1)} %refs_2_.8) | copy-start | bytes 31457284
  11.9 1.3 copy-start.3
  13.2 1.3 copy-start.5
  14.5 4.8 %copy-start = (bf16[1024,5120]{1,0:T(8,128)(2,1)S(1)}, bf16[1024,5120]{1,0:T(8,128)(2,1)}, u32[]{:S(2)}) copy-start(bf16[1024,5120]{1,0:T(8,128)(2,1)} %w_ref.19) | copy-start | bytes 31457284
  17.9 28.9 %collective-permute-start.4 = (bf16[256,1280]{1,0:T(8,128)(2,1)}, bf16[256,1280]{1,0:T(8,128)(2,1)S(1)}, u32[]{:S(2)}, u32[]{:S(2)}) collective-permute-start(bf16[256,1280]{1,0:T(8,128)(2,1)} %collective-permute-done.3.refs_0_), channel_id=1, source_target_pairs={{1,0},{2,3},{5,4},{6,7},{9,8},{10,11},{13,12},{14,15},{17,16},{18,... | collective-permute-start | bytes 1966088 | tf_op jit(solution)/shard_map/ppermute | solution.py:441
  19.9 13.1 %copy-start.8 = (bf16[256,1280]{1,0:T(8,128)(2,1)}, bf16[256,1280]{1,0:T(8,128)(2,1)S(1)}, u32[]{:S(2)}) copy-start(bf16[256,1280]{1,0:T(8,128)(2,1)S(1)} %collective-permute-done.5.refs_2_) | copy-start | bytes 1966084
  32.9 20.9 %collective-permute-start.1 = (bf16[256,1280]{1,0:T(8,128)(2,1)S(1)}, bf16[256,1280]{1,0:T(8,128)(2,1)S(1)}, u32[]{:S(2)}, u32[]{:S(2)}) collective-permute-start(bf16[256,1280]{1,0:T(8,128)(2,1)S(1)} %get-tuple-element.53), channel_id=1, source_target_pairs={{1,2},{2,1},{5,6},{6,5},{9,10},{10,9},{13,14},{14,13},{17,18},{18,... | collective-permute-start | bytes 1966088 | tf_op jit(solution)/shard_map/ppermute | solution.py:438
  33.6 27.3 %collective-permute-start.7 = (bf16[256,1280]{1,0:T(8,128)(2,1)}, bf16[256,1280]{1,0:T(8,128)(2,1)S(1)}, u32[]{:S(2)}, u32[]{:S(2)}) collective-permute-start(bf16[256,1280]{1,0:T(8,128)(2,1)} %copy-done.8), channel_id=1, source_target_pairs={{1,0},{2,3},{5,4},{6,7},{9,8},{10,11},{13,12},{14,15},{17,16},{18,... | collective-permute-start | bytes 1966088 | tf_op jit(solution)/shard_map/ppermute | solution.py:441
  46.9 0.8 copy-start.10
  47.7 14.2 %collective-permute-start.9 = (bf16[128,2560]{1,0:T(8,128)(2,1)S(1)}, bf16[128,2560]{1,0:T(8,128)(2,1)S(1)}, u32[]{:S(2)}, u32[]{:S(2)}) collective-permute-start(bf16[128,2560]{1,0:T(8,128)(2,1)S(1)} %eighth.2), channel_id=1, source_target_pairs={{0,1},{3,2},{4,5},{7,6},{8,9},{11,10},{12,13},{15,14},{16,17},{19,... | collective-permute-start | bytes 1966088 | tf_op jit(solution)/shard_map/ppermute | solution.py:444
  49.3 21.2 %slice-start = ((s8[10485760]{0:T(1024)(128)(4,1)}), s8[4194304]{0:T(1024)(128)(4,1)S(1)}, s32[]{:S(2)}) async-start(s8[10485760]{0:T(1024)(128)(4,1)} %bitcast.14), calls=%async_computation | async-start | bytes 8388608
  49.3 21.2 %slice-start.1 = ((s8[10485760]{0:T(1024)(128)(4,1)}), s8[4194304]{0:T(1024)(128)(4,1)S(1)}, s32[]{:S(2)}) async-start(s8[10485760]{0:T(1024)(128)(4,1)} %bitcast.14), calls=%async_computation.1 | async-start | bytes 8388608
  52.9 17.6 %slice-start.2 = ((s8[10485760]{0:T(1024)(128)(4,1)}), s8[2097152]{0:T(1024)(128)(4,1)S(1)}, s32[]{:S(2)}) async-start(s8[10485760]{0:T(1024)(128)(4,1)} %bitcast.14), calls=%async_computation.2 | async-start | bytes 4194304
  53.0 17.6 %copy-start.9 = (bf16[256,1280]{1,0:T(8,128)(2,1)S(1)}, bf16[256,1280]{1,0:T(8,128)(2,1)}, u32[]{:S(2)}) copy-start(bf16[256,1280]{1,0:T(8,128)(2,1)} %copy-done.8) | copy-start | bytes 1966084
  53.0 17.6 %copy-start.11 = (bf16[256,1280]{1,0:T(8,128)(2,1)S(1)}, bf16[256,1280]{1,0:T(8,128)(2,1)}, u32[]{:S(2)}) copy-start(bf16[256,1280]{1,0:T(8,128)(2,1)} %copy-done.10) | copy-start | bytes 1966084
  53.0 16.2 %collective-permute-start.6 = (bf16[256,1280]{1,0:T(8,128)(2,1)S(1)}, bf16[256,1280]{1,0:T(8,128)(2,1)S(1)}, u32[]{:S(2)}, u32[]{:S(2)}) collective-permute-start(bf16[256,1280]{1,0:T(8,128)(2,1)S(1)} %get-tuple-element.68), channel_id=1, source_target_pairs={{1,2},{2,1},{5,6},{6,5},{9,10},{10,9},{13,14},{14,13},{17,18},{18,... | collective-permute-start | bytes 1966088 | tf_op jit(solution)/shard_map/ppermute | solution.py:438
  53.8 22.4 %collective-permute-start.2 = (bf16[256,1280]{1,0:T(8,128)(2,1)S(1)}, bf16[256,1280]{1,0:T(8,128)(2,1)S(1)}, u32[]{:S(2)}, u32[]{:S(2)}) collective-permute-start(bf16[256,1280]{1,0:T(8,128)(2,1)S(1)} %collective-permute-done.1.refs_0_), channel_id=1, source_target_pairs={{1,0},{2,3},{5,4},{6,7},{9,8},{10,11},{13,12},{14,15},{17,16},{18,... | collective-permute-start | bytes 1966088 | tf_op jit(solution)/shard_map/ppermute | solution.py:441
  55.3 20.9 %copy-start.15 = (f32[128]{0:T(128)S(1)}, f32[128]{0:T(128)}, u32[]{:S(2)}) copy-start(f32[128]{0:T(128)} %param.18) | copy-start | bytes 1540
  55.9 20.3 %copy-start.6 = (f32[512,128]{1,0:T(8,128)S(1)}, f32[512,128]{1,0:T(8,128)}, u32[]{:S(2)}) copy-start(f32[512,128]{1,0:T(8,128)} %constant.29.clone.refs_5_.refs_7_.refs_8_) | copy-start | bytes 786436
  55.9 20.3 %copy-start.7 = (f32[512,128]{1,0:T(8,128)S(1)}, f32[512,128]{1,0:T(8,128)}, u32[]{:S(2)}) copy-start(f32[512,128]{1,0:T(8,128)} %constant.30.clone.refs_6_.refs_8_.refs_9_) | copy-start | bytes 786436
  60.9 0.8 copy-start.12
  61.9 17.9 %collective-permute-start.10 = (bf16[128,2560]{1,0:T(8,128)(2,1)S(1)}, bf16[128,2560]{1,0:T(8,128)(2,1)S(1)}, u32[]{:S(2)}, u32[]{:S(2)}) collective-permute-start(bf16[128,2560]{1,0:T(8,128)(2,1)S(1)} %collective-permute-done.9.refs_0_), channel_id=1, source_target_pairs={{0,8},{4,12},{8,0},{12,4},{16,24},{20,28},{24,16},{28,20},{1,9},{5... | collective-permute-start | bytes 1966088 | tf_op jit(solution)/shard_map/ppermute | solution.py:447
  63.7 16.1 %collective-permute-start.11 = (bf16[128,2560]{1,0:T(8,128)(2,1)S(1)}, bf16[128,2560]{1,0:T(8,128)(2,1)S(1)}, u32[]{:S(2)}, u32[]{:S(2)}) collective-permute-start(bf16[128,2560]{1,0:T(8,128)(2,1)S(1)} %collective-permute-done.9.refs_0_), channel_id=1, source_target_pairs={{0,16},{4,20},{8,24},{12,28},{16,0},{20,4},{24,8},{28,12},{1,17},{... | collective-permute-start | bytes 1966088 | tf_op jit(solution)/shard_map/ppermute | solution.py:447
  65.3 14.6 %collective-permute-start.12 = (bf16[128,2560]{1,0:T(8,128)(2,1)S(1)}, bf16[128,2560]{1,0:T(8,128)(2,1)S(1)}, u32[]{:S(2)}, u32[]{:S(2)}) collective-permute-start(bf16[128,2560]{1,0:T(8,128)(2,1)S(1)} %eighth.3), channel_id=1, source_target_pairs={{0,1},{3,2},{4,5},{7,6},{8,9},{11,10},{12,13},{15,14},{16,17},{19,... | collective-permute-start | bytes 1966088 | tf_op jit(solution)/shard_map/ppermute | solution.py:444
  69.2 19.0 %collective-permute-start.8 = (bf16[256,1280]{1,0:T(8,128)(2,1)S(1)}, bf16[256,1280]{1,0:T(8,128)(2,1)S(1)}, u32[]{:S(2)}, u32[]{:S(2)}) collective-permute-start(bf16[256,1280]{1,0:T(8,128)(2,1)S(1)} %collective-permute-done.6.refs_0_.refs_1_), channel_id=1, source_target_pairs={{1,0},{2,3},{5,4},{6,7},{9,8},{10,11},{13,12},{14,15},{17,16},{18,... | collective-permute-start | bytes 1966088 | tf_op jit(solution)/shard_map/ppermute | solution.py:441
  70.5 1.1 copy-start.13
  76.2 2.5 %copy-start.14 = (f32[128]{0:T(128)S(1)}, f32[128]{0:T(128)}, u32[]{:S(2)}) copy-start(f32[128]{0:T(128)} %param.19) | copy-start | bytes 1540
  78.7 9.5 %copy-start.16 = (s32[1,128]{1,0:T(1,128)S(1)}, s32[1,128]{1,0:T(1,128)}, u32[]{:S(2)}) copy-start(s32[1,128]{1,0:T(1,128)} %refs_10_.1) | copy-start | bytes 1540
  89.5 5.4 %collective-permute-start.13 = (bf16[128,256]{1,0:T(8,128)(2,1)S(1)}, bf16[128,256]{1,0:T(8,128)(2,1)S(1)}, u32[]{:S(2)}, u32[]{:S(2)}) collective-permute-start(bf16[128,256]{1,0:T(8,128)(2,1)S(1)} %get-tuple-element.80), channel_id=1, source_target_pairs={{0,28},{4,24},{8,20},{12,16},{16,12},{20,8},{24,4},{28,0},{1,29},{... | collective-permute-start | bytes 196616 | tf_op jit(solution)/shard_map/ppermute | solution.py:447
  90.4 5.5 %collective-permute-start.14 = (bf16[128,256]{1,0:T(8,128)(2,1)S(1)}, bf16[128,256]{1,0:T(8,128)(2,1)S(1)}, u32[]{:S(2)}, u32[]{:S(2)}) collective-permute-start(bf16[128,256]{1,0:T(8,128)(2,1)S(1)} %get-tuple-element.80), channel_id=1, source_target_pairs={{0,24},{4,28},{8,16},{12,20},{16,8},{20,12},{24,0},{28,4},{1,25},{... | collective-permute-start | bytes 196616 | tf_op jit(solution)/shard_map/ppermute | solution.py:447
  92.3 7.3 %collective-permute-start.15 = (bf16[128,256]{1,0:T(8,128)(2,1)S(1)}, bf16[128,256]{1,0:T(8,128)(2,1)S(1)}, u32[]{:S(2)}, u32[]{:S(2)}) collective-permute-start(bf16[128,256]{1,0:T(8,128)(2,1)S(1)} %get-tuple-element.80), channel_id=1, source_target_pairs={{0,20},{4,16},{8,28},{12,24},{16,4},{20,0},{24,12},{28,8},{1,21},{... | collective-permute-start | bytes 196616 | tf_op jit(solution)/shard_map/ppermute | solution.py:447
  93.6 5.9 %collective-permute-start.16 = (bf16[128,256]{1,0:T(8,128)(2,1)S(1)}, bf16[128,256]{1,0:T(8,128)(2,1)S(1)}, u32[]{:S(2)}, u32[]{:S(2)}) collective-permute-start(bf16[128,256]{1,0:T(8,128)(2,1)S(1)} %get-tuple-element.80), channel_id=1, source_target_pairs={{0,16},{4,20},{8,24},{12,28},{16,0},{20,4},{24,8},{28,12},{1,17},{... | collective-permute-start | bytes 196616 | tf_op jit(solution)/shard_map/ppermute | solution.py:447
  94.0 5.6 %collective-permute-start.17 = (bf16[128,256]{1,0:T(8,128)(2,1)S(1)}, bf16[128,256]{1,0:T(8,128)(2,1)S(1)}, u32[]{:S(2)}, u32[]{:S(2)}) collective-permute-start(bf16[128,256]{1,0:T(8,128)(2,1)S(1)} %get-tuple-element.80), channel_id=1, source_target_pairs={{0,12},{4,8},{8,4},{12,0},{16,28},{20,24},{24,20},{28,16},{1,13},{... | collective-permute-start | bytes 196616 | tf_op jit(solution)/shard_map/ppermute | solution.py:447
  94.9 4.9 %collective-permute-start.18 = (bf16[128,256]{1,0:T(8,128)(2,1)S(1)}, bf16[128,256]{1,0:T(8,128)(2,1)S(1)}, u32[]{:S(2)}, u32[]{:S(2)}) collective-permute-start(bf16[128,256]{1,0:T(8,128)(2,1)S(1)} %get-tuple-element.80), channel_id=1, source_target_pairs={{0,8},{4,12},{8,0},{12,4},{16,24},{20,28},{24,16},{28,20},{1,9},{5... | collective-permute-start | bytes 196616 | tf_op jit(solution)/shard_map/ppermute | solution.py:447
  95.9 3.9 %collective-permute-start.19 = (bf16[128,256]{1,0:T(8,128)(2,1)S(1)}, bf16[128,256]{1,0:T(8,128)(2,1)S(1)}, u32[]{:S(2)}, u32[]{:S(2)}) collective-permute-start(bf16[128,256]{1,0:T(8,128)(2,1)S(1)} %get-tuple-element.80), channel_id=1, source_target_pairs={{0,4},{4,0},{8,12},{12,8},{16,20},{20,16},{24,28},{28,24},{1,5},{5... | collective-permute-start | bytes 196616 | tf_op jit(solution)/shard_map/ppermute | solution.py:447
  103.3 8.1 %collective-permute-start.20 = (bf16[128,1024]{1,0:T(8,128)(2,1)S(1)}, bf16[128,1024]{1,0:T(8,128)(2,1)S(1)}, u32[]{:S(2)}, u32[]{:S(2)}) collective-permute-start(bf16[128,1024]{1,0:T(8,128)(2,1)S(1)} %attention.3.rows_ref), channel_id=1, source_target_pairs={{0,1},{3,2},{4,5},{7,6},{8,9},{11,10},{12,13},{15,14},{16,17},{19,... | collective-permute-start | bytes 786440 | tf_op jit(solution)/shard_map/ppermute | solution.py:444
  105.0 10.1 %collective-permute-start.21 = (bf16[128,2560]{1,0:T(8,128)(2,1)S(1)}, bf16[128,2560]{1,0:T(8,128)(2,1)S(1)}, u32[]{:S(2)}, u32[]{:S(2)}) collective-permute-start(bf16[128,2560]{1,0:T(8,128)(2,1)S(1)} %collective-permute-done.9.refs_0_), channel_id=1, source_target_pairs={{0,4},{4,0},{8,12},{12,8},{16,20},{20,16},{24,28},{28,24},{1,5},{5... | collective-permute-start | bytes 1966088 | tf_op jit(solution)/shard_map/ppermute | solution.py:447
  105.1 11.4 %collective-permute-start.22 = (bf16[128,2560]{1,0:T(8,128)(2,1)S(1)}, bf16[128,2560]{1,0:T(8,128)(2,1)S(1)}, u32[]{:S(2)}, u32[]{:S(2)}) collective-permute-start(bf16[128,2560]{1,0:T(8,128)(2,1)S(1)} %collective-permute-done.12.refs_1_), channel_id=1, source_target_pairs={{0,4},{4,0},{8,12},{12,8},{16,20},{20,16},{24,28},{28,24},{1,5},{5... | collective-permute-start | bytes 1966088 | tf_op jit(solution)/shard_map/ppermute | solution.py:447
  105.6 10.9 %collective-permute-start.23 = (bf16[128,2560]{1,0:T(8,128)(2,1)S(1)}, bf16[128,2560]{1,0:T(8,128)(2,1)S(1)}, u32[]{:S(2)}, u32[]{:S(2)}) collective-permute-start(bf16[128,2560]{1,0:T(8,128)(2,1)S(1)} %collective-permute-done.10.refs_2_), channel_id=1, source_target_pairs={{0,4},{4,0},{8,12},{12,8},{16,20},{20,16},{24,28},{28,24},{1,5},{5... | collective-permute-start | bytes 1966088 | tf_op jit(solution)/shard_map/ppermute | solution.py:447
  105.7 10.8 %collective-permute-start.24 = (bf16[128,2560]{1,0:T(8,128)(2,1)S(1)}, bf16[128,2560]{1,0:T(8,128)(2,1)S(1)}, u32[]{:S(2)}, u32[]{:S(2)}) collective-permute-start(bf16[128,2560]{1,0:T(8,128)(2,1)S(1)} %collective-permute-done.11.refs_3_), channel_id=1, source_target_pairs={{0,4},{4,0},{8,12},{12,8},{16,20},{20,16},{24,28},{28,24},{1,5},{5... | collective-permute-start | bytes 1966088 | tf_op jit(solution)/shard_map/ppermute | solution.py:447
  111.4 18.8 %collective-permute-start.26 = (bf16[128,2560]{1,0:T(8,128)(2,1)S(1)}, bf16[128,2560]{1,0:T(8,128)(2,1)S(1)}, u32[]{:S(2)}, u32[]{:S(2)}) collective-permute-start(bf16[128,2560]{1,0:T(8,128)(2,1)S(1)} %mix.8.refs_0_), channel_id=1, source_target_pairs={{0,1},{3,2},{4,5},{7,6},{8,9},{11,10},{12,13},{15,14},{16,17},{19,... | collective-permute-start | bytes 1966088 | tf_op jit(solution)/shard_map/ppermute | solution.py:444
  115.1 19.1 %collective-permute-start.25 = (bf16[128,1024]{1,0:T(8,128)(2,1)S(1)}, bf16[128,1024]{1,0:T(8,128)(2,1)S(1)}, u32[]{:S(2)}, u32[]{:S(2)}) collective-permute-start(bf16[128,1024]{1,0:T(8,128)(2,1)S(1)} %attention.4.rows_ref), channel_id=1, source_target_pairs={{0,1},{3,2},{4,5},{7,6},{8,9},{11,10},{12,13},{15,14},{16,17},{19,... | collective-permute-start | bytes 786440 | tf_op jit(solution)/shard_map/ppermute | solution.py:444
  118.0 24.4 %collective-permute-start.28 = (bf16[128,2560]{1,0:T(8,128)(2,1)S(1)}, bf16[128,2560]{1,0:T(8,128)(2,1)S(1)}, u32[]{:S(2)}, u32[]{:S(2)}) collective-permute-start(bf16[128,2560]{1,0:T(8,128)(2,1)S(1)} %added.8), channel_id=1, source_target_pairs={{1,2},{2,1},{5,6},{6,5},{9,10},{10,9},{13,14},{14,13},{17,18},{18,... | collective-permute-start | bytes 1966088 | tf_op jit(solution)/shard_map/ppermute | solution.py:438
  130.4 15.9 %collective-permute-start.29 = (bf16[128,2560]{1,0:T(8,128)(2,1)S(1)}, bf16[128,2560]{1,0:T(8,128)(2,1)S(1)}, u32[]{:S(2)}, u32[]{:S(2)}) collective-permute-start(bf16[128,2560]{1,0:T(8,128)(2,1)S(1)} %added.9), channel_id=1, source_target_pairs={{1,2},{2,1},{5,6},{6,5},{9,10},{10,9},{13,14},{14,13},{17,18},{18,... | collective-permute-start | bytes 1966088 | tf_op jit(solution)/shard_map/ppermute | solution.py:438
  134.2 20.5 %collective-permute-start.27 = (bf16[128,2560]{1,0:T(8,128)(2,1)S(1)}, bf16[128,2560]{1,0:T(8,128)(2,1)S(1)}, u32[]{:S(2)}, u32[]{:S(2)}) collective-permute-start(bf16[128,2560]{1,0:T(8,128)(2,1)S(1)} %mix.10.refs_0_), channel_id=1, source_target_pairs={{0,1},{3,2},{4,5},{7,6},{8,9},{11,10},{12,13},{15,14},{16,17},{19,... | collective-permute-start | bytes 1966088 | tf_op jit(solution)/shard_map/ppermute | solution.py:444
  139.5 20.7 %collective-permute-start.33 = (bf16[128,1024]{1,0:T(8,128)(2,1)S(1)}, bf16[128,1024]{1,0:T(8,128)(2,1)S(1)}, u32[]{:S(2)}, u32[]{:S(2)}) collective-permute-start(bf16[128,1024]{1,0:T(8,128)(2,1)S(1)} %get-tuple-element.96.rows_ref), channel_id=1, source_target_pairs={{0,1},{3,2},{4,5},{7,6},{8,9},{11,10},{12,13},{15,14},{16,17},{19,... | collective-permute-start | bytes 786440 | tf_op jit(solution)/shard_map/ppermute | solution.py:444
  143.3 21.1 %collective-permute-start.35 = (bf16[128,2560]{1,0:T(8,128)(2,1)S(1)}, bf16[128,2560]{1,0:T(8,128)(2,1)S(1)}, u32[]{:S(2)}, u32[]{:S(2)}) collective-permute-start(bf16[128,2560]{1,0:T(8,128)(2,1)S(1)} %added.10), channel_id=1, source_target_pairs={{1,2},{2,1},{5,6},{6,5},{9,10},{10,9},{13,14},{14,13},{17,18},{18,... | collective-permute-start | bytes 1966088 | tf_op jit(solution)/shard_map/ppermute | solution.py:438
  144.2 20.2 %collective-permute-start.34 = (bf16[128,2560]{1,0:T(8,128)(2,1)S(1)}, bf16[128,2560]{1,0:T(8,128)(2,1)S(1)}, u32[]{:S(2)}, u32[]{:S(2)}) collective-permute-start(bf16[128,2560]{1,0:T(8,128)(2,1)S(1)} %added.11), channel_id=1, source_target_pairs={{1,0},{2,3},{5,4},{6,7},{9,8},{10,11},{13,12},{14,15},{17,16},{18,... | collective-permute-start | bytes 1966088 | tf_op jit(solution)/shard_map/ppermute | solution.py:441
  146.5 28.2 %collective-permute-start.31 = (bf16[128,2560]{1,0:T(8,128)(2,1)S(1)}, bf16[128,2560]{1,0:T(8,128)(2,1)S(1)}, u32[]{:S(2)}, u32[]{:S(2)}) collective-permute-start(bf16[128,2560]{1,0:T(8,128)(2,1)S(1)} %added.12), channel_id=1, source_target_pairs={{1,0},{2,3},{5,4},{6,7},{9,8},{10,11},{13,12},{14,15},{17,16},{18,... | collective-permute-start | bytes 1966088 | tf_op jit(solution)/shard_map/ppermute | solution.py:441
  154.8 16.0 %collective-permute-start.30 = (bf16[128,2560]{1,0:T(8,128)(2,1)S(1)}, bf16[128,2560]{1,0:T(8,128)(2,1)S(1)}, u32[]{:S(2)}, u32[]{:S(2)}) collective-permute-start(bf16[128,2560]{1,0:T(8,128)(2,1)S(1)} %mix.13.refs_0_), channel_id=1, source_target_pairs={{0,1},{3,2},{4,5},{7,6},{8,9},{11,10},{12,13},{15,14},{16,17},{19,... | collective-permute-start | bytes 1966088 | tf_op jit(solution)/shard_map/ppermute | solution.py:444
  160.3 14.4 %collective-permute-start.32 = (bf16[128,2560]{1,0:T(8,128)(2,1)S(1)}, bf16[128,2560]{1,0:T(8,128)(2,1)S(1)}, u32[]{:S(2)}, u32[]{:S(2)}) collective-permute-start(bf16[128,2560]{1,0:T(8,128)(2,1)S(1)} %added.13), channel_id=1, source_target_pairs={{1,2},{2,1},{5,6},{6,5},{9,10},{10,9},{13,14},{14,13},{17,18},{18,... | collective-permute-start | bytes 1966088 | tf_op jit(solution)/shard_map/ppermute | solution.py:438

commit v16 on v15

--- a/solution.py
+++ b/solution.py
@@ -372,6 +372,27 @@
     )(places, attended, *pieces)
 
 
+def joined_kernel(*refs):
+    start = 0
+    for ref in refs[:-1]:
+        stop = start + ref.shape[0]
+        refs[-1][start:stop, :] = ref[...]
+        start = stop
+
+
+def joined(arrays):
+    rows = sum(array.shape[0] for array in arrays)
+    return pl.pallas_call(
+        joined_kernel,
+        in_specs=resident(len(arrays)),
+        out_specs=resident(1)[0],
+        out_shape=jax.ShapeDtypeStruct((rows, arrays[0].shape[1]), arrays[0].dtype),
+        compiler_params=params(8),
+        cost_estimate=cost(1),
+        name="joined",
+    )(*arrays)
+
+
 def halves_kernel(ref, first_ref, second_ref):
     half = first_ref.shape[0]
     first_ref[...] = ref[:half, :]
@@ -482,6 +503,7 @@
         after(places, cue), THIRD, [[a, b] for a, b in zip(from_mid, to_outer)], weights, accs
     )
 
+    pieces = [joined([pieces[offset] for offset in OFFSETS[:4]])] if spread else []
     final = [[a, b] for a, b in zip(to_inner, end)]
     (own_first,) = keys_values(places, final[0], 0, weights[1:], accs[1:], k_gain, *tables)
     first_queries = queries_of(places, final[0], 0, w_query, accs[0], q_gain, *tables)
@@ -502,9 +524,7 @@
     queries = [first_queries, second_queries]
 
     if spread:
-        cue = (others, second_queries)
-        for offset in (0, 6, 2, 4):
-            pieces[offset ^ 1] = between(after(pieces[offset], cue), 1)
+        pieces.append(between(after(pieces[0], (others, second_queries)), 1))
 
     def attend(slots):
         return attention(places, slots, rows_here // 4, lengths, queries, own, others)
@@ -515,7 +535,7 @@
     def share_of(arrived):
         if not spread:
             return arrived
-        return mix_sent(places, arrived, [pieces[offset] for offset in OFFSETS])
+        return mix_sent(places, arrived, pieces)
 
     def mixed(rows):
         return [mix(rows, w_out, which) for which in (0, 1)]
@@ -525,9 +545,8 @@
     far_sent = send(far_rows, far[1])
     places = after(places, far)
     (third_rows,) = attend((THIRD,))
-    far_sent = after(far_sent, third_rows)
-    far_in = inward(after(far[0], far_sent))
-    far_right = added(far[1], share_of(far_sent))
+    far_in = inward(far[0])
+    far_right = added(far[1], share_of(after(far_sent, third_rows)))
     places = after(places, far_right)
     near_rows, own_rows = attend((NEAR, OWN))
     third = mixed(after(third_rows, near_rows))
@@ -536,7 +555,7 @@
     far_left = added(far[0], after(far_in, third))
     third_sent = after(third_sent, far_left)
     far_left = across(far_left)
-    third_in = inward(after(third[0], third_sent))
+    third_in = inward(after(third[0], (third_sent, far_right)))
     third_right = added(third[1], share_of(third_sent))
     near = [None, mix(after(near_rows, (third_right, far_right)), w_out, 1)]
     near_sent = send(near_rows, near[1])

time: 178 us -> 177 us (level)
  waiting for transfers between devices: 63 us -> 59.8 us
  starting transfers between devices: 52.2 us -> 54.8 us
    ppermute x8, waiting for transfers between devices: 20.5 us -> 7.94 us  [inward(): return lax.ppermute(array, 'tensor', [(0, 1), (3, 2)])]
    ppermute x6, waiting for transfers between devices: 29.2 us -> 37.8 us  [outward(): return lax.ppermute(array, 'tensor', [(1, 0), (2, 3)])]
    ppermute x8, starting transfers between devices: 23.2 us -> 26.9 us  [inward(): return lax.ppermute(array, 'tensor', [(0, 1), (3, 2)])]
    ppermute x13 -> x10, starting transfers between devices: 11.3 us -> 10.5 us  [between(): return lax.ppermute(array, 'cand', [(i, i ^ offset) for i in range(n_cand)])]
    unnamed x40 -> x32, local copies, waits for them, and re-layouts: 10.8 us -> 9.93 us
  transfers between devices with their start and end apart: 36 -> 33, of which waited for: 12 -> 13; matrix products, arithmetic and copies ran while one was open for 0% -> 0% of each run, Pallas kernels for 24% -> 27%
where the time goes in v16:
time: 177 us; the launch traced here: 175 us
  waiting for transfers between devices  59.8 us (34%)
  starting transfers between devices  54.8 us (31%)
  Pallas kernels  48.9 us (28%)
  local copies, waits for them, and re-layouts  10 us (6%)
    ppermute x6, waiting for transfers between devices, outward(): return lax.ppermute(array, 'tensor', [(1, 0), (2, 3)])  37.8 us
    ppermute x8, starting transfers between devices, inward(): return lax.ppermute(array, 'tensor', [(0, 1), (3, 2)])  26.9 us
    ppermute x1, waiting for transfers between devices, swap(): return lax.ppermute(array, 'tensor', [(0, 1), (1, 0), (2, 3), (3, 2)])  13 us
    pallas_call x3, Pallas kernels, attention(): pl.pallas_call(functools.partial(attention_kernel, slots, n_parts, len(ot...  12.7 us
    pallas_call x3, Pallas kernels, partial_projection(): pl.pallas_call(functools.partial(partial_kernel, [len(part) for part in p...  11.6 us
    ppermute x10, starting transfers between devices, between(): return lax.ppermute(array, 'cand', [(i, i ^ offset) for i in range(n_cand)])  10.5 us
    unnamed x32, local copies, waits for them, and re-layouts  9.93 us
    ppermute x8, waiting for transfers between devices, inward(): return lax.ppermute(array, 'tensor', [(0, 1), (3, 2)])  7.94 us
  transfers between devices with their start and end apart: 33, of which 13 were waited for; matrix products, arithmetic and copies ran while one was open for 0% of the time, Pallas kernels for 27%

profile of v16, /device:TPU:0, one launch (start us, length us, event | category | flops | bytes accessed | tf_op | source)
XLA Modules:
  0.0 174.8 jit_solution(3420065815088549669)
XLA Ops:
  0.0 3.0 %collective-permute-start = (bf16[512,1280]{1,0:T(8,128)(2,1)}, bf16[512,1280]{1,0:T(8,128)(2,1)S(1)}, u32[]{:S(2)}, u32[]{:S(2)}) collective-permute-start(bf16[512,1280]{1,0:T(8,128)(2,1)} %refs_0_.1), channel_id=1, source_target_pairs={{0,1},{1,0},{2,3},{3,2},{4,5},{5,4},{6,7},{7,6},{8,9},{9,8},{10,11... | collective-permute-start | bytes 3932168 | tf_op jit(solution)/shard_map/ppermute | solution.py:456
  3.0 1.3 copy-done.4
  4.4 1.2 halves.3
  6.2 1.5 collective-permute-start.5
  7.9 4.0 %copy-done.1 = bf16[5120,1024]{1,0:T(8,128)(2,1)S(1)} copy-done((bf16[5120,1024]{1,0:T(8,128)(2,1)S(1)}, bf16[5120,1024]{1,0:T(8,128)(2,1)}, u32[]{:S(2)}) %copy-start.1) | copy-done | bytes 10485784
  11.8 1.3 copy-done.3
  13.1 1.3 copy-done.5
  14.5 3.4 %partial_projection.3 = (f32[512,1024]{1,0:T(8,128)S(1)}, f32[512,128]{1,0:T(8,128)S(1)}, f32[512,128]{1,0:T(8,128)S(1)}) custom-call(s32[12]{0:T(128)S(1)} %stack.51.places_ref, bf16[512,1280]{1,0:T(8,128)(2,1)S(1)} %copy-done.5, bf16[5120,1024]{1,0:T(8,128)(2,1)S(1)} %copy-done.1, bf16[5120,128]{1,0:T(8,128)(2,1)S(1)} %copy-done.2, ...), custom_call_target="tpu_custom_call" | custom-call | flops 1 | bytes 1 | tf_op jit(solution)/shard_map/partial_projection/pallas_call | solution.py:100
  17.9 1.3 collective-permute-start.4
  19.8 13.0 %collective-permute-done.ref.refs_0_ = bf16[512,1280]{1,0:T(8,128)(2,1)S(1)} collective-permute-done((bf16[512,1280]{1,0:T(8,128)(2,1)}, bf16[512,1280]{1,0:T(8,128)(2,1)S(1)}, u32[]{:S(2)}, u32[]{:S(2)}) %collective-permute-start) | collective-permute-done | bytes 1310752 | tf_op jit(solution)/shard_map/ppermute | solution.py:456
  32.9 0.7 collective-permute-start.1
  33.6 1.3 collective-permute-start.7
  34.9 11.9 %collective-permute-done.4.refs_1_ = bf16[256,1280]{1,0:T(8,128)(2,1)S(1)} collective-permute-done((bf16[256,1280]{1,0:T(8,128)(2,1)S(1)}, bf16[256,1280]{1,0:T(8,128)(2,1)S(1)}, u32[]{:S(2)}, u32[]{:S(2)}) %collective-permute-start.4) | collective-permute-done | bytes 655392 | tf_op jit(solution)/shard_map/ppermute | solution.py:462
  46.9 1.5 collective-permute-start.9
  48.4 3.6 %partial_projection.4 = (f32[512,1024]{1,0:T(8,128)S(1)}, f32[512,128]{1,0:T(8,128)S(1)}, f32[512,128]{1,0:T(8,128)S(1)}) custom-call(s32[12]{0:T(128)S(1)} %stack.51.places_ref, bf16[512,1280]{1,0:T(8,128)(2,1)S(1)} %collective-permute-done.ref.refs_0_, bf16[5120,1024]{1,0:T(8,128)(2,1)S(1)} %copy-done.1, bf16[5120,128]{1,0:T(8,128)(2,1)S(1)} %copy-done.2, ...), custom_call_target="tpu_custom_call" | custom-call | flops 1 | bytes 1 | tf_op jit(solution)/shard_map/partial_projection/pallas_call | solution.py:100
  52.0 0.8 collective-permute-start.6
  52.9 1.3 collective-permute-start.2
  54.8 6.1 %collective-permute-done.7.refs_3_ = bf16[256,1280]{1,0:T(8,128)(2,1)S(1)} collective-permute-done((bf16[256,1280]{1,0:T(8,128)(2,1)}, bf16[256,1280]{1,0:T(8,128)(2,1)S(1)}, u32[]{:S(2)}, u32[]{:S(2)}) %collective-permute-start.7) | collective-permute-done | bytes 655392 | tf_op jit(solution)/shard_map/ppermute | solution.py:462
  60.9 0.8 copy-done.8
  61.8 1.6 collective-permute-start.10
  63.4 2.0 %collective-permute-start.11 = (bf16[128,2560]{1,0:T(8,128)(2,1)S(1)}, bf16[128,2560]{1,0:T(8,128)(2,1)S(1)}, u32[]{:S(2)}, u32[]{:S(2)}) collective-permute-start(bf16[128,2560]{1,0:T(8,128)(2,1)S(1)} %collective-permute-done.9.refs_0_), channel_id=1, source_target_pairs={{0,8},{4,12},{8,0},{12,4},{16,24},{20,28},{24,16},{28,20},{1,9},{5... | collective-permute-start | bytes 1966088 | tf_op jit(solution)/shard_map/ppermute | solution.py:468
  65.4 1.5 collective-permute-start.12
  66.9 1.3 collective-permute-start.8
  68.3 1.1 copy-done.9
  69.3 4.6 %partial_projection.5 = (f32[512,1024]{1,0:T(8,128)S(1)}, f32[512,128]{1,0:T(8,128)S(1)}, f32[512,128]{1,0:T(8,128)S(1)}) custom-call(s32[12]{0:T(128)S(1)} %stack.51.places_ref, bf16[256,1280]{1,0:T(8,128)(2,1)S(1)} %collective-permute-done.3.refs_0_, bf16[256,1280]{1,0:T(8,128)(2,1)S(1)} %collective-permute-done.4.refs_1_, ...), custom_call_target="tpu_custom_call" | custom-call | flops 1 | bytes 1 | tf_op jit(solution)/shard_map/partial_projection/pallas_call | solution.py:100
  73.9 1.6 collective-permute-done.2.refs_1_
  75.6 2.5 %queries.2.refs_0_ = bf16[256,1024]{1,0:T(8,128)(2,1)S(1)} custom-call(s32[12]{0:T(128)S(1)} %stack.51.places_ref, bf16[256,1280]{1,0:T(8,128)(2,1)S(1)} %collective-permute-done.1.refs_0_, bf16[256,1280]{1,0:T(8,128)(2,1)S(1)} %collective-permute-done.2.refs_1_, bf16[5120,1024]{1,0:T(8,128)(2,1)S(1)} %bitcast.15, ...), custom_call_target="tpu_custom_call" | custom-call | flops 1 | bytes 1 | tf_op jit(solution)/shard_map/queries/pallas_call | solution.py:187
  78.1 1.1 keys_values.2.refs_0_.refs_2_
  79.5 8.7 %collective-permute-done.8.refs_1_.refs_2_ = bf16[256,1280]{1,0:T(8,128)(2,1)S(1)} collective-permute-done((bf16[256,1280]{1,0:T(8,128)(2,1)S(1)}, bf16[256,1280]{1,0:T(8,128)(2,1)S(1)}, u32[]{:S(2)}, u32[]{:S(2)}) %collective-permute-start.8) | collective-permute-done | bytes 655392 | tf_op jit(solution)/shard_map/ppermute | solution.py:462
  88.2 1.3 keys_values.3
  89.5 1.2 collective-permute-start.13
  90.7 1.6 collective-permute-start.14
  92.3 1.4 collective-permute-start.15
  94.0 0.9 collective-permute-start.17
  94.9 1.0 collective-permute-start.18
  96.5 2.5 %queries.3.refs_1_ = bf16[256,1024]{1,0:T(8,128)(2,1)S(1)} custom-call(s32[12]{0:T(128)S(1)} %stack.51.places_ref, bf16[256,1280]{1,0:T(8,128)(2,1)S(1)} %collective-permute-done.6.refs_0_.refs_1_, bf16[256,1280]{1,0:T(8,128)(2,1)S(1)} %collective-permute-done.8.refs_1_.refs_2_, bf16[5120,1024]{1,0:T(8,128)(2,1)S(1)} %bitcast.15, ...), custom_call_target="tpu_custom_call" | custom-call | flops 1 | bytes 1 | tf_op jit(solution)/shard_map/queries/pallas_call | solution.py:187
  100.5 3.6 %attention.3.rows_ref = bf16[128,1024]{1,0:T(8,128)(2,1)S(1)} custom-call(s32[12]{0:T(128)S(1)} %stack.51.places_ref, s32[1]{0:T(128)S(6)} %copy.14.length_ref, bf16[256,1024]{1,0:T(8,128)(2,1)S(1)} %queries.2.refs_0_, bf16[256,1024]{1,0:T(8,128)(2,1)S(1)} %queries.3.refs_1_, bf16[256,256]{1,0:T(8,128)(2,1)S(1)} %keys_values.2.refs_0_.refs_2_, ...), custom_call_target="tpu_custom_call" | custom-call | flops 1 | bytes 1 | tf_op jit(solution)/shard_map/attention/pallas_call | solution.py:276
  104.1 1.6 collective-permute-start.20
  105.7 0.9 mix.8.refs_0_
  106.6 0.9 mix.9.refs_0_
  107.5 1.3 collective-permute-start.23
  108.8 3.6 %attention.4.rows_ref = bf16[128,1024]{1,0:T(8,128)(2,1)S(1)} custom-call(s32[12]{0:T(128)S(1)} %stack.51.places_ref, s32[1]{0:T(128)S(6)} %copy.14.length_ref, bf16[256,1024]{1,0:T(8,128)(2,1)S(1)} %queries.2.refs_0_, bf16[256,1024]{1,0:T(8,128)(2,1)S(1)} %queries.3.refs_1_, bf16[256,256]{1,0:T(8,128)(2,1)S(1)} %keys_values.2.refs_0_.refs_2_, ...), custom_call_target="tpu_custom_call" | custom-call | flops 1 | bytes 1 | tf_op jit(solution)/shard_map/attention/pallas_call | solution.py:276
  112.4 1.4 mix_sent.3.refs_1_
  114.7 8.2 %collective-permute-start.22 = (bf16[128,1024]{1,0:T(8,128)(2,1)S(1)}, bf16[128,1024]{1,0:T(8,128)(2,1)S(1)}, u32[]{:S(2)}, u32[]{:S(2)}) collective-permute-start(bf16[128,1024]{1,0:T(8,128)(2,1)S(1)} %attention.4.rows_ref), channel_id=1, source_target_pairs={{0,1},{3,2},{4,5},{7,6},{8,9},{11,10},{12,13},{15,14},{16,17},{19,... | collective-permute-start | bytes 786440 | tf_op jit(solution)/shard_map/ppermute | solution.py:465
  122.9 5.6 %attention.5 = (bf16[128,1024]{1,0:T(8,128)(2,1)S(1)}, bf16[128,1024]{1,0:T(8,128)(2,1)S(1)}) custom-call(s32[12]{0:T(128)S(1)} %stack.51.places_ref, s32[1]{0:T(128)S(6)} %copy.14.length_ref, bf16[256,1024]{1,0:T(8,128)(2,1)S(1)} %queries.2.refs_0_, bf16[256,1024]{1,0:T(8,128)(2,1)S(1)} %queries.3.refs_1_, bf16[256,256]{1,0:T(8,128)(2,1)S(1)} %keys_values.2.refs_0_.refs_2_, ...), custom_call_target="tpu_custom_call" | custom-call | flops 1 | bytes 1 | tf_op jit(solution)/shard_map/attention/pallas_call | solution.py:276
  128.5 0.9 mix.10.refs_0_
  129.4 0.9 mix.11.refs_0_
  130.5 0.9 collective-permute-start.26
  131.5 6.9 %collective-permute-start.25 = (bf16[128,2560]{1,0:T(8,128)(2,1)S(1)}, bf16[128,2560]{1,0:T(8,128)(2,1)S(1)}, u32[]{:S(2)}, u32[]{:S(2)}) collective-permute-start(bf16[128,2560]{1,0:T(8,128)(2,1)S(1)} %mix.10.refs_0_), channel_id=1, source_target_pairs={{0,1},{3,2},{4,5},{7,6},{8,9},{11,10},{12,13},{15,14},{16,17},{19,... | collective-permute-start | bytes 1966088 | tf_op jit(solution)/shard_map/ppermute | solution.py:465
  138.4 1.3 collective-permute-start.30
  139.7 1.4 mix_sent.4.refs_1_
  141.3 0.9 mix.12.refs_0_
  143.0 1.3 collective-permute-start.31
  144.3 0.9 mix.13.refs_0_
  145.4 1.3 collective-permute-start.28
  146.7 6.8 %collective-permute-done.25.refs_1_ = bf16[128,2560]{1,0:T(8,128)(2,1)S(1)} collective-permute-done((bf16[128,2560]{1,0:T(8,128)(2,1)S(1)}, bf16[128,2560]{1,0:T(8,128)(2,1)S(1)}, u32[]{:S(2)}, u32[]{:S(2)}) %collective-permute-start.25) | collective-permute-done | bytes 655392 | tf_op jit(solution)/shard_map/ppermute | solution.py:465
  153.7 4.4 %collective-permute-start.27 = (bf16[128,2560]{1,0:T(8,128)(2,1)S(1)}, bf16[128,2560]{1,0:T(8,128)(2,1)S(1)}, u32[]{:S(2)}, u32[]{:S(2)}) collective-permute-start(bf16[128,2560]{1,0:T(8,128)(2,1)S(1)} %mix.13.refs_0_), channel_id=1, source_target_pairs={{0,1},{3,2},{4,5},{7,6},{8,9},{11,10},{12,13},{15,14},{16,17},{19,... | collective-permute-start | bytes 1966088 | tf_op jit(solution)/shard_map/ppermute | solution.py:465
  158.1 1.0 collective-permute-done.30.rows_ref
  159.8 0.9 mix.14.refs_0_
  160.7 0.9 mix.15.refs_0_
  161.6 1.4 mix_sent.5.refs_1_
  163.0 1.2 added.14.refs_4_
  164.2 9.4 %collective-permute-done.28.refs_2_ = bf16[128,2560]{1,0:T(8,128)(2,1)S(1)} collective-permute-done((bf16[128,2560]{1,0:T(8,128)(2,1)S(1)}, bf16[128,2560]{1,0:T(8,128)(2,1)S(1)}, u32[]{:S(2)}, u32[]{:S(2)}) %collective-permute-start.28) | collective-permute-done | bytes 655392 | tf_op jit(solution)/shard_map/ppermute | solution.py:462
  173.6 1.2 added.15
  (70 shorter events, 7.3 us)
Async XLA Ops:
  0.0 7.8 %copy-start.2 = (bf16[5120,128]{1,0:T(8,128)(2,1)S(1)}, bf16[5120,128]{1,0:T(8,128)(2,1)}, u32[]{:S(2)}) copy-start(bf16[5120,128]{1,0:T(8,128)(2,1)} %refs_3_.7) | copy-start | bytes 3932164
  0.0 32.8 %collective-permute-start = (bf16[512,1280]{1,0:T(8,128)(2,1)}, bf16[512,1280]{1,0:T(8,128)(2,1)S(1)}, u32[]{:S(2)}, u32[]{:S(2)}) collective-permute-start(bf16[512,1280]{1,0:T(8,128)(2,1)} %refs_0_.1), channel_id=1, source_target_pairs={{0,1},{1,0},{2,3},{3,2},{4,5},{5,4},{6,7},{7,6},{8,9},{9,8},{10,11... | collective-permute-start | bytes 3932168 | tf_op jit(solution)/shard_map/ppermute | solution.py:456
  3.0 1.4 copy-start.4
  5.5 12.4 %collective-permute-start.3 = (bf16[256,1280]{1,0:T(8,128)(2,1)}, bf16[256,1280]{1,0:T(8,128)(2,1)S(1)}, u32[]{:S(2)}, u32[]{:S(2)}) collective-permute-start(bf16[256,1280]{1,0:T(8,128)(2,1)} %get-tuple-element.51), channel_id=1, source_target_pairs={{1,2},{2,1},{5,6},{6,5},{9,10},{10,9},{13,14},{14,13},{17,18},{18,... | collective-permute-start | bytes 1966088 | tf_op jit(solution)/shard_map/ppermute | solution.py:459
  6.2 13.6 %collective-permute-start.5 = (bf16[256,1280]{1,0:T(8,128)(2,1)}, bf16[256,1280]{1,0:T(8,128)(2,1)}, u32[]{:S(2)}, u32[]{:S(2)}) collective-permute-start(bf16[256,1280]{1,0:T(8,128)(2,1)} %get-tuple-element.56), channel_id=1, source_target_pairs={{1,2},{2,1},{5,6},{6,5},{9,10},{10,9},{13,14},{14,13},{17,18},{18,... | collective-permute-start | bytes 1966088 | tf_op jit(solution)/shard_map/ppermute | solution.py:459
  7.8 4.0 %copy-start.1 = (bf16[5120,1024]{1,0:T(8,128)(2,1)S(1)}, bf16[5120,1024]{1,0:T(8,128)(2,1)}, u32[]{:S(2)}) copy-start(bf16[5120,1024]{1,0:T(8,128)(2,1)} %refs_2_.8) | copy-start | bytes 31457284
  11.8 1.3 copy-start.3
  13.1 1.3 copy-start.5
  14.5 4.8 %copy-start = (bf16[1024,5120]{1,0:T(8,128)(2,1)S(1)}, bf16[1024,5120]{1,0:T(8,128)(2,1)}, u32[]{:S(2)}) copy-start(bf16[1024,5120]{1,0:T(8,128)(2,1)} %w_ref.19) | copy-start | bytes 31457284
  17.9 29.0 %collective-permute-start.4 = (bf16[256,1280]{1,0:T(8,128)(2,1)S(1)}, bf16[256,1280]{1,0:T(8,128)(2,1)S(1)}, u32[]{:S(2)}, u32[]{:S(2)}) collective-permute-start(bf16[256,1280]{1,0:T(8,128)(2,1)S(1)} %collective-permute-done.3.refs_0_), channel_id=1, source_target_pairs={{1,0},{2,3},{5,4},{6,7},{9,8},{10,11},{13,12},{14,15},{17,16},{18,... | collective-permute-start | bytes 1966088 | tf_op jit(solution)/shard_map/ppermute | solution.py:462
  32.9 19.9 %collective-permute-start.1 = (bf16[256,1280]{1,0:T(8,128)(2,1)S(1)}, bf16[256,1280]{1,0:T(8,128)(2,1)S(1)}, u32[]{:S(2)}, u32[]{:S(2)}) collective-permute-start(bf16[256,1280]{1,0:T(8,128)(2,1)S(1)} %get-tuple-element.49), channel_id=1, source_target_pairs={{1,2},{2,1},{5,6},{6,5},{9,10},{10,9},{13,14},{14,13},{17,18},{18,... | collective-permute-start | bytes 1966088 | tf_op jit(solution)/shard_map/ppermute | solution.py:459
  33.6 27.3 %collective-permute-start.7 = (bf16[256,1280]{1,0:T(8,128)(2,1)}, bf16[256,1280]{1,0:T(8,128)(2,1)S(1)}, u32[]{:S(2)}, u32[]{:S(2)}) collective-permute-start(bf16[256,1280]{1,0:T(8,128)(2,1)} %collective-permute-done.5.refs_2_), channel_id=1, source_target_pairs={{1,0},{2,3},{5,4},{6,7},{9,8},{10,11},{13,12},{14,15},{17,16},{18,... | collective-permute-start | bytes 1966088 | tf_op jit(solution)/shard_map/ppermute | solution.py:462
  46.9 16.5 %collective-permute-start.9 = (bf16[128,2560]{1,0:T(8,128)(2,1)S(1)}, bf16[128,2560]{1,0:T(8,128)(2,1)S(1)}, u32[]{:S(2)}, u32[]{:S(2)}) collective-permute-start(bf16[128,2560]{1,0:T(8,128)(2,1)S(1)} %eighth.2), channel_id=1, source_target_pairs={{0,1},{3,2},{4,5},{7,6},{8,9},{11,10},{12,13},{15,14},{16,17},{19,... | collective-permute-start | bytes 1966088 | tf_op jit(solution)/shard_map/ppermute | solution.py:465
  48.4 19.9 %slice-start = ((s8[10485760]{0:T(1024)(128)(4,1)}), s8[4194304]{0:T(1024)(128)(4,1)S(1)}, s32[]{:S(2)}) async-start(s8[10485760]{0:T(1024)(128)(4,1)} %bitcast.14), calls=%async_computation | async-start | bytes 8388608
  48.4 19.8 %slice-start.1 = ((s8[10485760]{0:T(1024)(128)(4,1)}), s8[4194304]{0:T(1024)(128)(4,1)S(1)}, s32[]{:S(2)}) async-start(s8[10485760]{0:T(1024)(128)(4,1)} %bitcast.14), calls=%async_computation.1 | async-start | bytes 8388608
  52.0 16.2 %slice-start.2 = ((s8[10485760]{0:T(1024)(128)(4,1)}), s8[2097152]{0:T(1024)(128)(4,1)S(1)}, s32[]{:S(2)}) async-start(s8[10485760]{0:T(1024)(128)(4,1)} %bitcast.14), calls=%async_computation.2 | async-start | bytes 4194304
  52.0 14.9 %collective-permute-start.6 = (bf16[256,1280]{1,0:T(8,128)(2,1)S(1)}, bf16[256,1280]{1,0:T(8,128)(2,1)S(1)}, u32[]{:S(2)}, u32[]{:S(2)}) collective-permute-start(bf16[256,1280]{1,0:T(8,128)(2,1)S(1)} %get-tuple-element.64), channel_id=1, source_target_pairs={{1,2},{2,1},{5,6},{6,5},{9,10},{10,9},{13,14},{14,13},{17,18},{18,... | collective-permute-start | bytes 1966088 | tf_op jit(solution)/shard_map/ppermute | solution.py:459
  52.9 22.7 %collective-permute-start.2 = (bf16[256,1280]{1,0:T(8,128)(2,1)S(1)}, bf16[256,1280]{1,0:T(8,128)(2,1)S(1)}, u32[]{:S(2)}, u32[]{:S(2)}) collective-permute-start(bf16[256,1280]{1,0:T(8,128)(2,1)S(1)} %collective-permute-done.1.refs_0_), channel_id=1, source_target_pairs={{1,0},{2,3},{5,4},{6,7},{9,8},{10,11},{13,12},{14,15},{17,16},{18,... | collective-permute-start | bytes 1966088 | tf_op jit(solution)/shard_map/ppermute | solution.py:462
  54.2 21.4 %copy-start.11 = (f32[128]{0:T(128)S(1)}, f32[128]{0:T(128)}, u32[]{:S(2)}) copy-start(f32[128]{0:T(128)} %param.18) | copy-start | bytes 1540
  54.8 20.8 %copy-start.6 = (f32[512,128]{1,0:T(8,128)S(1)}, f32[512,128]{1,0:T(8,128)}, u32[]{:S(2)}) copy-start(f32[512,128]{1,0:T(8,128)} %constant.29.clone.refs_5_.refs_7_.refs_8_) | copy-start | bytes 786436
  54.8 20.8 %copy-start.7 = (f32[512,128]{1,0:T(8,128)S(1)}, f32[512,128]{1,0:T(8,128)}, u32[]{:S(2)}) copy-start(f32[512,128]{1,0:T(8,128)} %constant.30.clone.refs_6_.refs_8_.refs_9_) | copy-start | bytes 786436
  60.9 0.8 copy-start.8
  61.8 17.4 %collective-permute-start.10 = (bf16[128,2560]{1,0:T(8,128)(2,1)S(1)}, bf16[128,2560]{1,0:T(8,128)(2,1)S(1)}, u32[]{:S(2)}, u32[]{:S(2)}) collective-permute-start(bf16[128,2560]{1,0:T(8,128)(2,1)S(1)} %eighth.3), channel_id=1, source_target_pairs={{0,1},{3,2},{4,5},{7,6},{8,9},{11,10},{12,13},{15,14},{16,17},{19,... | collective-permute-start | bytes 1966088 | tf_op jit(solution)/shard_map/ppermute | solution.py:465
  63.4 15.8 %collective-permute-start.11 = (bf16[128,2560]{1,0:T(8,128)(2,1)S(1)}, bf16[128,2560]{1,0:T(8,128)(2,1)S(1)}, u32[]{:S(2)}, u32[]{:S(2)}) collective-permute-start(bf16[128,2560]{1,0:T(8,128)(2,1)S(1)} %collective-permute-done.9.refs_0_), channel_id=1, source_target_pairs={{0,8},{4,12},{8,0},{12,4},{16,24},{20,28},{24,16},{28,20},{1,9},{5... | collective-permute-start | bytes 1966088 | tf_op jit(solution)/shard_map/ppermute | solution.py:468
  65.4 13.9 %collective-permute-start.12 = (bf16[128,2560]{1,0:T(8,128)(2,1)S(1)}, bf16[128,2560]{1,0:T(8,128)(2,1)S(1)}, u32[]{:S(2)}, u32[]{:S(2)}) collective-permute-start(bf16[128,2560]{1,0:T(8,128)(2,1)S(1)} %collective-permute-done.9.refs_0_), channel_id=1, source_target_pairs={{0,16},{4,20},{8,24},{12,28},{16,0},{20,4},{24,8},{28,12},{1,17},{... | collective-permute-start | bytes 1966088 | tf_op jit(solution)/shard_map/ppermute | solution.py:468
  66.9 21.3 %collective-permute-start.8 = (bf16[256,1280]{1,0:T(8,128)(2,1)S(1)}, bf16[256,1280]{1,0:T(8,128)(2,1)S(1)}, u32[]{:S(2)}, u32[]{:S(2)}) collective-permute-start(bf16[256,1280]{1,0:T(8,128)(2,1)S(1)} %collective-permute-done.6.refs_0_.refs_1_), channel_id=1, source_target_pairs={{1,0},{2,3},{5,4},{6,7},{9,8},{10,11},{13,12},{14,15},{17,16},{18,... | collective-permute-start | bytes 1966088 | tf_op jit(solution)/shard_map/ppermute | solution.py:462
  68.2 1.1 copy-start.9
  75.6 2.5 %copy-start.10 = (f32[128]{0:T(128)S(1)}, f32[128]{0:T(128)}, u32[]{:S(2)}) copy-start(f32[128]{0:T(128)} %param.19) | copy-start | bytes 1540
  79.2 9.0 %copy-start.12 = (s32[1,128]{1,0:T(1,128)S(1)}, s32[1,128]{1,0:T(1,128)}, u32[]{:S(2)}) copy-start(s32[1,128]{1,0:T(1,128)} %refs_10_.1) | copy-start | bytes 1540
  89.5 5.4 %collective-permute-start.13 = (bf16[128,256]{1,0:T(8,128)(2,1)S(1)}, bf16[128,256]{1,0:T(8,128)(2,1)S(1)}, u32[]{:S(2)}, u32[]{:S(2)}) collective-permute-start(bf16[128,256]{1,0:T(8,128)(2,1)S(1)} %get-tuple-element.76), channel_id=1, source_target_pairs={{0,28},{4,24},{8,20},{12,16},{16,12},{20,8},{24,4},{28,0},{1,29},{... | collective-permute-start | bytes 196616 | tf_op jit(solution)/shard_map/ppermute | solution.py:468
  90.7 5.3 %collective-permute-start.14 = (bf16[128,256]{1,0:T(8,128)(2,1)S(1)}, bf16[128,256]{1,0:T(8,128)(2,1)S(1)}, u32[]{:S(2)}, u32[]{:S(2)}) collective-permute-start(bf16[128,256]{1,0:T(8,128)(2,1)S(1)} %get-tuple-element.76), channel_id=1, source_target_pairs={{0,24},{4,28},{8,16},{12,20},{16,8},{20,12},{24,0},{28,4},{1,25},{... | collective-permute-start | bytes 196616 | tf_op jit(solution)/shard_map/ppermute | solution.py:468
  92.3 6.7 %collective-permute-start.15 = (bf16[128,256]{1,0:T(8,128)(2,1)S(1)}, bf16[128,256]{1,0:T(8,128)(2,1)S(1)}, u32[]{:S(2)}, u32[]{:S(2)}) collective-permute-start(bf16[128,256]{1,0:T(8,128)(2,1)S(1)} %get-tuple-element.76), channel_id=1, source_target_pairs={{0,20},{4,16},{8,28},{12,24},{16,4},{20,0},{24,12},{28,8},{1,21},{... | collective-permute-start | bytes 196616 | tf_op jit(solution)/shard_map/ppermute | solution.py:468
  93.6 5.7 %collective-permute-start.16 = (bf16[128,256]{1,0:T(8,128)(2,1)S(1)}, bf16[128,256]{1,0:T(8,128)(2,1)S(1)}, u32[]{:S(2)}, u32[]{:S(2)}) collective-permute-start(bf16[128,256]{1,0:T(8,128)(2,1)S(1)} %get-tuple-element.76), channel_id=1, source_target_pairs={{0,16},{4,20},{8,24},{12,28},{16,0},{20,4},{24,8},{28,12},{1,17},{... | collective-permute-start | bytes 196616 | tf_op jit(solution)/shard_map/ppermute | solution.py:468
  94.0 5.4 %collective-permute-start.17 = (bf16[128,256]{1,0:T(8,128)(2,1)S(1)}, bf16[128,256]{1,0:T(8,128)(2,1)S(1)}, u32[]{:S(2)}, u32[]{:S(2)}) collective-permute-start(bf16[128,256]{1,0:T(8,128)(2,1)S(1)} %get-tuple-element.76), channel_id=1, source_target_pairs={{0,12},{4,8},{8,4},{12,0},{16,28},{20,24},{24,20},{28,16},{1,13},{... | collective-permute-start | bytes 196616 | tf_op jit(solution)/shard_map/ppermute | solution.py:468
  94.9 4.9 %collective-permute-start.18 = (bf16[128,256]{1,0:T(8,128)(2,1)S(1)}, bf16[128,256]{1,0:T(8,128)(2,1)S(1)}, u32[]{:S(2)}, u32[]{:S(2)}) collective-permute-start(bf16[128,256]{1,0:T(8,128)(2,1)S(1)} %get-tuple-element.76), channel_id=1, source_target_pairs={{0,8},{4,12},{8,0},{12,4},{16,24},{20,28},{24,16},{28,20},{1,9},{5... | collective-permute-start | bytes 196616 | tf_op jit(solution)/shard_map/ppermute | solution.py:468
  96.0 3.8 %collective-permute-start.19 = (bf16[128,256]{1,0:T(8,128)(2,1)S(1)}, bf16[128,256]{1,0:T(8,128)(2,1)S(1)}, u32[]{:S(2)}, u32[]{:S(2)}) collective-permute-start(bf16[128,256]{1,0:T(8,128)(2,1)S(1)} %get-tuple-element.76), channel_id=1, source_target_pairs={{0,4},{4,0},{8,12},{12,8},{16,20},{20,16},{24,28},{28,24},{1,5},{5... | collective-permute-start | bytes 196616 | tf_op jit(solution)/shard_map/ppermute | solution.py:468
  99.8 12.7 %collective-permute-start.21 = (bf16[512,2560]{1,0:T(8,128)(2,1)S(1)}, bf16[512,2560]{1,0:T(8,128)(2,1)S(1)}, u32[]{:S(2)}, u32[]{:S(2)}) collective-permute-start(bf16[512,2560]{1,0:T(8,128)(2,1)S(1)} %joined.1.refs_0_), channel_id=1, source_target_pairs={{0,4},{4,0},{8,12},{12,8},{16,20},{20,16},{24,28},{28,24},{1,5},{5... | collective-permute-start | bytes 7864328 | tf_op jit(solution)/shard_map/ppermute | solution.py:468
  104.1 8.4 %collective-permute-start.20 = (bf16[128,1024]{1,0:T(8,128)(2,1)S(1)}, bf16[128,1024]{1,0:T(8,128)(2,1)S(1)}, u32[]{:S(2)}, u32[]{:S(2)}) collective-permute-start(bf16[128,1024]{1,0:T(8,128)(2,1)S(1)} %attention.3.rows_ref), channel_id=1, source_target_pairs={{0,1},{3,2},{4,5},{7,6},{8,9},{11,10},{12,13},{15,14},{16,17},{19,... | collective-permute-start | bytes 786440 | tf_op jit(solution)/shard_map/ppermute | solution.py:465
  107.5 22.8 %collective-permute-start.23 = (bf16[128,2560]{1,0:T(8,128)(2,1)S(1)}, bf16[128,2560]{1,0:T(8,128)(2,1)S(1)}, u32[]{:S(2)}, u32[]{:S(2)}) collective-permute-start(bf16[128,2560]{1,0:T(8,128)(2,1)S(1)} %mix.8.refs_0_), channel_id=1, source_target_pairs={{0,1},{3,2},{4,5},{7,6},{8,9},{11,10},{12,13},{15,14},{16,17},{19,... | collective-permute-start | bytes 1966088 | tf_op jit(solution)/shard_map/ppermute | solution.py:465
  114.0 17.5 %collective-permute-start.24 = (bf16[128,2560]{1,0:T(8,128)(2,1)S(1)}, bf16[128,2560]{1,0:T(8,128)(2,1)S(1)}, u32[]{:S(2)}, u32[]{:S(2)}) collective-permute-start(bf16[128,2560]{1,0:T(8,128)(2,1)S(1)} %added.8), channel_id=1, source_target_pairs={{1,2},{2,1},{5,6},{6,5},{9,10},{10,9},{13,14},{14,13},{17,18},{18,... | collective-permute-start | bytes 1966088 | tf_op jit(solution)/shard_map/ppermute | solution.py:459
  114.7 16.7 %collective-permute-start.22 = (bf16[128,1024]{1,0:T(8,128)(2,1)S(1)}, bf16[128,1024]{1,0:T(8,128)(2,1)S(1)}, u32[]{:S(2)}, u32[]{:S(2)}) collective-permute-start(bf16[128,1024]{1,0:T(8,128)(2,1)S(1)} %attention.4.rows_ref), channel_id=1, source_target_pairs={{0,1},{3,2},{4,5},{7,6},{8,9},{11,10},{12,13},{15,14},{16,17},{19,... | collective-permute-start | bytes 786440 | tf_op jit(solution)/shard_map/ppermute | solution.py:465
  130.5 14.8 %collective-permute-start.26 = (bf16[128,2560]{1,0:T(8,128)(2,1)S(1)}, bf16[128,2560]{1,0:T(8,128)(2,1)S(1)}, u32[]{:S(2)}, u32[]{:S(2)}) collective-permute-start(bf16[128,2560]{1,0:T(8,128)(2,1)S(1)} %added.9), channel_id=1, source_target_pairs={{1,2},{2,1},{5,6},{6,5},{9,10},{10,9},{13,14},{14,13},{17,18},{18,... | collective-permute-start | bytes 1966088 | tf_op jit(solution)/shard_map/ppermute | solution.py:459
  131.5 22.0 %collective-permute-start.25 = (bf16[128,2560]{1,0:T(8,128)(2,1)S(1)}, bf16[128,2560]{1,0:T(8,128)(2,1)S(1)}, u32[]{:S(2)}, u32[]{:S(2)}) collective-permute-start(bf16[128,2560]{1,0:T(8,128)(2,1)S(1)} %mix.10.refs_0_), channel_id=1, source_target_pairs={{0,1},{3,2},{4,5},{7,6},{8,9},{11,10},{12,13},{15,14},{16,17},{19,... | collective-permute-start | bytes 1966088 | tf_op jit(solution)/shard_map/ppermute | solution.py:465
  138.4 20.7 %collective-permute-start.30 = (bf16[128,1024]{1,0:T(8,128)(2,1)S(1)}, bf16[128,1024]{1,0:T(8,128)(2,1)S(1)}, u32[]{:S(2)}, u32[]{:S(2)}) collective-permute-start(bf16[128,1024]{1,0:T(8,128)(2,1)S(1)} %get-tuple-element.88.rows_ref), channel_id=1, source_target_pairs={{0,1},{3,2},{4,5},{7,6},{8,9},{11,10},{12,13},{15,14},{16,17},{19,... | collective-permute-start | bytes 786440 | tf_op jit(solution)/shard_map/ppermute | solution.py:465
  142.1 20.9 %collective-permute-start.32 = (bf16[128,2560]{1,0:T(8,128)(2,1)S(1)}, bf16[128,2560]{1,0:T(8,128)(2,1)S(1)}, u32[]{:S(2)}, u32[]{:S(2)}) collective-permute-start(bf16[128,2560]{1,0:T(8,128)(2,1)S(1)} %added.10), channel_id=1, source_target_pairs={{1,2},{2,1},{5,6},{6,5},{9,10},{10,9},{13,14},{14,13},{17,18},{18,... | collective-permute-start | bytes 1966088 | tf_op jit(solution)/shard_map/ppermute | solution.py:459
  143.0 20.0 %collective-permute-start.31 = (bf16[128,2560]{1,0:T(8,128)(2,1)S(1)}, bf16[128,2560]{1,0:T(8,128)(2,1)S(1)}, u32[]{:S(2)}, u32[]{:S(2)}) collective-permute-start(bf16[128,2560]{1,0:T(8,128)(2,1)S(1)} %added.11), channel_id=1, source_target_pairs={{1,0},{2,3},{5,4},{6,7},{9,8},{10,11},{13,12},{14,15},{17,16},{18,... | collective-permute-start | bytes 1966088 | tf_op jit(solution)/shard_map/ppermute | solution.py:462
  145.4 28.2 %collective-permute-start.28 = (bf16[128,2560]{1,0:T(8,128)(2,1)S(1)}, bf16[128,2560]{1,0:T(8,128)(2,1)S(1)}, u32[]{:S(2)}, u32[]{:S(2)}) collective-permute-start(bf16[128,2560]{1,0:T(8,128)(2,1)S(1)} %added.12), channel_id=1, source_target_pairs={{1,0},{2,3},{5,4},{6,7},{9,8},{10,11},{13,12},{14,15},{17,16},{18,... | collective-permute-start | bytes 1966088 | tf_op jit(solution)/shard_map/ppermute | solution.py:462
  153.7 20.0 %collective-permute-start.27 = (bf16[128,2560]{1,0:T(8,128)(2,1)S(1)}, bf16[128,2560]{1,0:T(8,128)(2,1)S(1)}, u32[]{:S(2)}, u32[]{:S(2)}) collective-permute-start(bf16[128,2560]{1,0:T(8,128)(2,1)S(1)} %mix.13.refs_0_), channel_id=1, source_target_pairs={{0,1},{3,2},{4,5},{7,6},{8,9},{11,10},{12,13},{15,14},{16,17},{19,... | collective-permute-start | bytes 1966088 | tf_op jit(solution)/shard_map/ppermute | solution.py:465
  159.1 14.5 %collective-permute-start.29 = (bf16[128,2560]{1,0:T(8,128)(2,1)S(1)}, bf16[128,2560]{1,0:T(8,128)(2,1)S(1)}, u32[]{:S(2)}, u32[]{:S(2)}) collective-permute-start(bf16[128,2560]{1,0:T(8,128)(2,1)S(1)} %added.13), channel_id=1, source_target_pairs={{1,2},{2,1},{5,6},{6,5},{9,10},{10,9},{13,14},{14,13},{17,18},{18,... | collective-permute-start | bytes 1966088 | tf_op jit(solution)/shard_map/ppermute | solution.py:459

commit v17 on v16

--- a/solution.py
+++ b/solution.py
@@ -555,18 +555,18 @@
     far_left = added(far[0], after(far_in, third))
     third_sent = after(third_sent, far_left)
     far_left = across(far_left)
-    third_in = inward(after(third[0], (third_sent, far_right)))
+    near_sent = inward(near_rows) if spread else ()
+    third_in = inward(after(third[0], (third_sent, far_right, near_sent)))
     third_right = added(third[1], share_of(third_sent))
     near = [None, mix(after(near_rows, (third_right, far_right)), w_out, 1)]
-    near_sent = send(near_rows, near[1])
     third_right = across(third_right)
     out_right = added(near[1], far_right)
     near[0] = mix(after(near_rows, out_right), w_out, 0)
     out_left = added(near[0], far_left)
     third_left = added(third[0], after(third_in, out_left))
     kept = mixed(after(own_rows, third_left))
-    near_sent = share_of(after(near_sent, third_left))
-    result = added(kept[1], near_sent, outward(out_right), third_right, half=1)
+    near_share = share_of(after(near_sent, third_left)) if spread else inward(near[1])
+    result = added(kept[1], near_share, outward(out_right), third_right, half=1)
     near_in = inward(after(near[0], third_left))
     out_left, third_left = outward(out_left), across(third_left)
     return added(kept[0], near_in, out_left, third_left, half=0, into=result)

time: 177 us -> 180 us (1.017)
  waiting for transfers between devices: 59.8 us -> 66.6 us
  starting transfers between devices: 54.8 us -> 52.4 us
    ppermute x6, waiting for transfers between devices: 37.8 us -> 41.2 us  [outward(): return lax.ppermute(array, 'tensor', [(1, 0), (2, 3)])]
    ppermute x8, waiting for transfers between devices: 7.94 us -> 11.3 us  [inward(): return lax.ppermute(array, 'tensor', [(0, 1), (3, 2)])]
    ppermute x8, starting transfers between devices: 26.9 us -> 24.6 us  [inward(): return lax.ppermute(array, 'tensor', [(0, 1), (3, 2)])]
  transfers between devices with their start and end apart: 33 -> 33, of which waited for: 13 -> 13; matrix products, arithmetic and copies ran while one was open for 0% -> 0% of each run, Pallas kernels for 27% -> 26%
where the time goes in v17:
time: 180 us; the launch traced here: 179 us
  waiting for transfers between devices  66.6 us (37%)
  starting transfers between devices  52.4 us (29%)
  Pallas kernels  48.9 us (27%)
  local copies, waits for them, and re-layouts  10 us (6%)
    ppermute x6, waiting for transfers between devices, outward(): return lax.ppermute(array, 'tensor', [(1, 0), (2, 3)])  41.2 us
    ppermute x8, starting transfers between devices, inward(): return lax.ppermute(array, 'tensor', [(0, 1), (3, 2)])  24.6 us
    ppermute x1, waiting for transfers between devices, swap(): return lax.ppermute(array, 'tensor', [(0, 1), (1, 0), (2, 3), (3, 2)])  13 us
    pallas_call x3, Pallas kernels, attention(): pl.pallas_call(functools.partial(attention_kernel, slots, n_parts, len(ot...  12.7 us
    pallas_call x3, Pallas kernels, partial_projection(): pl.pallas_call(functools.partial(partial_kernel, [len(part) for part in p...  11.6 us
    ppermute x8, waiting for transfers between devices, inward(): return lax.ppermute(array, 'tensor', [(0, 1), (3, 2)])  11.3 us
    ppermute x10, starting transfers between devices, between(): return lax.ppermute(array, 'cand', [(i, i ^ offset) for i in range(n_cand)])  10.5 us
    unnamed x32, local copies, waits for them, and re-layouts  9.93 us
  transfers between devices with their start and end apart: 33, of which 13 were waited for; matrix products, arithmetic and copies ran while one was open for 0% of the time, Pallas kernels for 26%

profile of v17, /device:TPU:0, one launch (start us, length us, event | category | flops | bytes accessed | tf_op | source)
XLA Modules:
  0.0 179.1 jit_solution(17707023128173090817)
XLA Ops:
  0.0 3.0 %collective-permute-start = (bf16[512,1280]{1,0:T(8,128)(2,1)}, bf16[512,1280]{1,0:T(8,128)(2,1)S(1)}, u32[]{:S(2)}, u32[]{:S(2)}) collective-permute-start(bf16[512,1280]{1,0:T(8,128)(2,1)} %refs_0_.1), channel_id=1, source_target_pairs={{0,1},{1,0},{2,3},{3,2},{4,5},{5,4},{6,7},{7,6},{8,9},{9,8},{10,11... | collective-permute-start | bytes 3932168 | tf_op jit(solution)/shard_map/ppermute | solution.py:456
  3.0 1.3 copy-done.4
  4.4 1.2 halves.3
  6.2 1.5 collective-permute-start.5
  7.9 4.0 %copy-done.1 = bf16[5120,1024]{1,0:T(8,128)(2,1)S(1)} copy-done((bf16[5120,1024]{1,0:T(8,128)(2,1)S(1)}, bf16[5120,1024]{1,0:T(8,128)(2,1)}, u32[]{:S(2)}) %copy-start.1) | copy-done | bytes 10485784
  11.8 1.3 copy-done.3
  13.1 1.3 copy-done.5
  14.5 3.4 %partial_projection.3 = (f32[512,1024]{1,0:T(8,128)S(1)}, f32[512,128]{1,0:T(8,128)S(1)}, f32[512,128]{1,0:T(8,128)S(1)}) custom-call(s32[12]{0:T(128)S(1)} %stack.51.places_ref, bf16[512,1280]{1,0:T(8,128)(2,1)S(1)} %copy-done.5, bf16[5120,1024]{1,0:T(8,128)(2,1)S(1)} %copy-done.1, bf16[5120,128]{1,0:T(8,128)(2,1)S(1)} %copy-done.2, ...), custom_call_target="tpu_custom_call" | custom-call | flops 1 | bytes 1 | tf_op jit(solution)/shard_map/partial_projection/pallas_call | solution.py:100
  17.9 1.3 collective-permute-start.4
  19.8 13.0 %collective-permute-done.ref.refs_0_ = bf16[512,1280]{1,0:T(8,128)(2,1)S(1)} collective-permute-done((bf16[512,1280]{1,0:T(8,128)(2,1)}, bf16[512,1280]{1,0:T(8,128)(2,1)S(1)}, u32[]{:S(2)}, u32[]{:S(2)}) %collective-permute-start) | collective-permute-done | bytes 1310752 | tf_op jit(solution)/shard_map/ppermute | solution.py:456
  32.9 0.7 collective-permute-start.1
  33.6 1.3 collective-permute-start.7
  34.9 11.9 %collective-permute-done.4.refs_1_ = bf16[256,1280]{1,0:T(8,128)(2,1)S(1)} collective-permute-done((bf16[256,1280]{1,0:T(8,128)(2,1)S(1)}, bf16[256,1280]{1,0:T(8,128)(2,1)S(1)}, u32[]{:S(2)}, u32[]{:S(2)}) %collective-permute-start.4) | collective-permute-done | bytes 655392 | tf_op jit(solution)/shard_map/ppermute | solution.py:462
  46.9 1.5 collective-permute-start.9
  48.4 3.6 %partial_projection.4 = (f32[512,1024]{1,0:T(8,128)S(1)}, f32[512,128]{1,0:T(8,128)S(1)}, f32[512,128]{1,0:T(8,128)S(1)}) custom-call(s32[12]{0:T(128)S(1)} %stack.51.places_ref, bf16[512,1280]{1,0:T(8,128)(2,1)S(1)} %collective-permute-done.ref.refs_0_, bf16[5120,1024]{1,0:T(8,128)(2,1)S(1)} %copy-done.1, bf16[5120,128]{1,0:T(8,128)(2,1)S(1)} %copy-done.2, ...), custom_call_target="tpu_custom_call" | custom-call | flops 1 | bytes 1 | tf_op jit(solution)/shard_map/partial_projection/pallas_call | solution.py:100
  52.0 0.8 collective-permute-start.6
  52.9 1.3 collective-permute-start.2
  54.8 6.1 %collective-permute-done.7.refs_3_ = bf16[256,1280]{1,0:T(8,128)(2,1)S(1)} collective-permute-done((bf16[256,1280]{1,0:T(8,128)(2,1)}, bf16[256,1280]{1,0:T(8,128)(2,1)S(1)}, u32[]{:S(2)}, u32[]{:S(2)}) %collective-permute-start.7) | collective-permute-done | bytes 655392 | tf_op jit(solution)/shard_map/ppermute | solution.py:462
  60.9 0.8 copy-done.8
  61.8 1.6 collective-permute-start.10
  63.4 2.0 %collective-permute-start.11 = (bf16[128,2560]{1,0:T(8,128)(2,1)S(1)}, bf16[128,2560]{1,0:T(8,128)(2,1)S(1)}, u32[]{:S(2)}, u32[]{:S(2)}) collective-permute-start(bf16[128,2560]{1,0:T(8,128)(2,1)S(1)} %collective-permute-done.9.refs_0_), channel_id=1, source_target_pairs={{0,8},{4,12},{8,0},{12,4},{16,24},{20,28},{24,16},{28,20},{1,9},{5... | collective-permute-start | bytes 1966088 | tf_op jit(solution)/shard_map/ppermute | solution.py:468
  65.4 1.5 collective-permute-start.12
  66.9 1.3 collective-permute-start.8
  68.3 1.1 copy-done.9
  69.3 4.6 %partial_projection.5 = (f32[512,1024]{1,0:T(8,128)S(1)}, f32[512,128]{1,0:T(8,128)S(1)}, f32[512,128]{1,0:T(8,128)S(1)}) custom-call(s32[12]{0:T(128)S(1)} %stack.51.places_ref, bf16[256,1280]{1,0:T(8,128)(2,1)S(1)} %collective-permute-done.3.refs_0_, bf16[256,1280]{1,0:T(8,128)(2,1)S(1)} %collective-permute-done.4.refs_1_, ...), custom_call_target="tpu_custom_call" | custom-call | flops 1 | bytes 1 | tf_op jit(solution)/shard_map/partial_projection/pallas_call | solution.py:100
  73.9 1.6 collective-permute-done.2.refs_1_
  75.6 2.5 %queries.2.refs_0_ = bf16[256,1024]{1,0:T(8,128)(2,1)S(1)} custom-call(s32[12]{0:T(128)S(1)} %stack.51.places_ref, bf16[256,1280]{1,0:T(8,128)(2,1)S(1)} %collective-permute-done.1.refs_0_, bf16[256,1280]{1,0:T(8,128)(2,1)S(1)} %collective-permute-done.2.refs_1_, bf16[5120,1024]{1,0:T(8,128)(2,1)S(1)} %bitcast.15, ...), custom_call_target="tpu_custom_call" | custom-call | flops 1 | bytes 1 | tf_op jit(solution)/shard_map/queries/pallas_call | solution.py:187
  78.1 1.1 keys_values.2.refs_0_.refs_2_
  79.5 8.7 %collective-permute-done.8.refs_1_.refs_2_ = bf16[256,1280]{1,0:T(8,128)(2,1)S(1)} collective-permute-done((bf16[256,1280]{1,0:T(8,128)(2,1)S(1)}, bf16[256,1280]{1,0:T(8,128)(2,1)S(1)}, u32[]{:S(2)}, u32[]{:S(2)}) %collective-permute-start.8) | collective-permute-done | bytes 655392 | tf_op jit(solution)/shard_map/ppermute | solution.py:462
  88.2 1.3 keys_values.3
  89.5 1.2 collective-permute-start.13
  90.7 1.6 collective-permute-start.14
  92.3 1.4 collective-permute-start.15
  94.0 0.9 collective-permute-start.17
  94.9 1.0 collective-permute-start.18
  96.5 2.5 %queries.3.refs_1_ = bf16[256,1024]{1,0:T(8,128)(2,1)S(1)} custom-call(s32[12]{0:T(128)S(1)} %stack.51.places_ref, bf16[256,1280]{1,0:T(8,128)(2,1)S(1)} %collective-permute-done.6.refs_0_.refs_1_, bf16[256,1280]{1,0:T(8,128)(2,1)S(1)} %collective-permute-done.8.refs_1_.refs_2_, bf16[5120,1024]{1,0:T(8,128)(2,1)S(1)} %bitcast.15, ...), custom_call_target="tpu_custom_call" | custom-call | flops 1 | bytes 1 | tf_op jit(solution)/shard_map/queries/pallas_call | solution.py:187
  100.5 3.6 %attention.3.rows_ref = bf16[128,1024]{1,0:T(8,128)(2,1)S(1)} custom-call(s32[12]{0:T(128)S(1)} %stack.51.places_ref, s32[1]{0:T(128)S(6)} %copy.14.length_ref, bf16[256,1024]{1,0:T(8,128)(2,1)S(1)} %queries.2.refs_0_, bf16[256,1024]{1,0:T(8,128)(2,1)S(1)} %queries.3.refs_1_, bf16[256,256]{1,0:T(8,128)(2,1)S(1)} %keys_values.2.refs_0_.refs_2_, ...), custom_call_target="tpu_custom_call" | custom-call | flops 1 | bytes 1 | tf_op jit(solution)/shard_map/attention/pallas_call | solution.py:276
  104.1 1.6 collective-permute-start.20
  105.7 0.9 mix.8.refs_0_
  106.6 0.9 mix.9.refs_0_
  107.5 1.3 collective-permute-start.23
  108.8 3.6 %attention.4.rows_ref = bf16[128,1024]{1,0:T(8,128)(2,1)S(1)} custom-call(s32[12]{0:T(128)S(1)} %stack.51.places_ref, s32[1]{0:T(128)S(6)} %copy.14.length_ref, bf16[256,1024]{1,0:T(8,128)(2,1)S(1)} %queries.2.refs_0_, bf16[256,1024]{1,0:T(8,128)(2,1)S(1)} %queries.3.refs_1_, bf16[256,256]{1,0:T(8,128)(2,1)S(1)} %keys_values.2.refs_0_.refs_2_, ...), custom_call_target="tpu_custom_call" | custom-call | flops 1 | bytes 1 | tf_op jit(solution)/shard_map/attention/pallas_call | solution.py:276
  112.4 1.4 mix_sent.3.refs_1_
  114.7 8.2 %collective-permute-start.22 = (bf16[128,1024]{1,0:T(8,128)(2,1)S(1)}, bf16[128,1024]{1,0:T(8,128)(2,1)S(1)}, u32[]{:S(2)}, u32[]{:S(2)}) collective-permute-start(bf16[128,1024]{1,0:T(8,128)(2,1)S(1)} %attention.4.rows_ref), channel_id=1, source_target_pairs={{0,1},{3,2},{4,5},{7,6},{8,9},{11,10},{12,13},{15,14},{16,17},{19,... | collective-permute-start | bytes 786440 | tf_op jit(solution)/shard_map/ppermute | solution.py:465
  122.9 5.6 %attention.5 = (bf16[128,1024]{1,0:T(8,128)(2,1)S(1)}, bf16[128,1024]{1,0:T(8,128)(2,1)S(1)}) custom-call(s32[12]{0:T(128)S(1)} %stack.51.places_ref, s32[1]{0:T(128)S(6)} %copy.14.length_ref, bf16[256,1024]{1,0:T(8,128)(2,1)S(1)} %queries.2.refs_0_, bf16[256,1024]{1,0:T(8,128)(2,1)S(1)} %queries.3.refs_1_, bf16[256,256]{1,0:T(8,128)(2,1)S(1)} %keys_values.2.refs_0_.refs_2_, ...), custom_call_target="tpu_custom_call" | custom-call | flops 1 | bytes 1 | tf_op jit(solution)/shard_map/attention/pallas_call | solution.py:276
  128.5 1.5 collective-permute-start.25
  130.0 0.9 mix.10.refs_0_
  130.9 0.9 mix.11.refs_0_
  132.7 4.4 %collective-permute-done.25.rows_ref = bf16[128,1024]{1,0:T(8,128)(2,1)S(1)} collective-permute-done((bf16[128,1024]{1,0:T(8,128)(2,1)S(1)}, bf16[128,1024]{1,0:T(8,128)(2,1)S(1)}, u32[]{:S(2)}, u32[]{:S(2)}) %collective-permute-start.25) | collective-permute-done | bytes 262176 | tf_op jit(solution)/shard_map/ppermute | solution.py:465
  137.1 4.4 %collective-permute-start.26 = (bf16[128,2560]{1,0:T(8,128)(2,1)S(1)}, bf16[128,2560]{1,0:T(8,128)(2,1)S(1)}, u32[]{:S(2)}, u32[]{:S(2)}) collective-permute-start(bf16[128,2560]{1,0:T(8,128)(2,1)S(1)} %mix.10.refs_0_), channel_id=1, source_target_pairs={{0,1},{3,2},{4,5},{7,6},{8,9},{11,10},{12,13},{15,14},{16,17},{19,... | collective-permute-start | bytes 1966088 | tf_op jit(solution)/shard_map/ppermute | solution.py:465
  141.5 1.4 mix_sent.4.refs_1_
  143.1 0.9 mix.12.refs_0_
  144.8 1.3 collective-permute-start.31
  146.1 0.9 mix.13.refs_0_
  147.2 1.3 collective-permute-start.29
  148.5 6.9 %collective-permute-done.26.refs_1_ = bf16[128,2560]{1,0:T(8,128)(2,1)S(1)} collective-permute-done((bf16[128,2560]{1,0:T(8,128)(2,1)S(1)}, bf16[128,2560]{1,0:T(8,128)(2,1)S(1)}, u32[]{:S(2)}, u32[]{:S(2)}) %collective-permute-start.26) | collective-permute-done | bytes 655392 | tf_op jit(solution)/shard_map/ppermute | solution.py:465
  155.6 4.4 %collective-permute-start.28 = (bf16[128,2560]{1,0:T(8,128)(2,1)S(1)}, bf16[128,2560]{1,0:T(8,128)(2,1)S(1)}, u32[]{:S(2)}, u32[]{:S(2)}) collective-permute-start(bf16[128,2560]{1,0:T(8,128)(2,1)S(1)} %mix.13.refs_0_), channel_id=1, source_target_pairs={{0,1},{3,2},{4,5},{7,6},{8,9},{11,10},{12,13},{15,14},{16,17},{19,... | collective-permute-start | bytes 1966088 | tf_op jit(solution)/shard_map/ppermute | solution.py:465
  160.7 0.9 mix.14.refs_0_
  161.6 0.9 mix.15.refs_0_
  162.5 1.4 mix_sent.5.refs_1_
  164.0 1.2 collective-permute-done.31.refs_2_
  165.1 1.2 added.14.refs_4_
  166.3 11.7 %collective-permute-done.29.refs_2_ = bf16[128,2560]{1,0:T(8,128)(2,1)S(1)} collective-permute-done((bf16[128,2560]{1,0:T(8,128)(2,1)S(1)}, bf16[128,2560]{1,0:T(8,128)(2,1)S(1)}, u32[]{:S(2)}, u32[]{:S(2)}) %collective-permute-start.29) | collective-permute-done | bytes 655392 | tf_op jit(solution)/shard_map/ppermute | solution.py:462
  178.0 1.2 added.15
  (70 shorter events, 8.0 us)
Async XLA Ops:
  0.0 7.8 %copy-start.2 = (bf16[5120,128]{1,0:T(8,128)(2,1)S(1)}, bf16[5120,128]{1,0:T(8,128)(2,1)}, u32[]{:S(2)}) copy-start(bf16[5120,128]{1,0:T(8,128)(2,1)} %refs_3_.7) | copy-start | bytes 3932164
  0.0 32.8 %collective-permute-start = (bf16[512,1280]{1,0:T(8,128)(2,1)}, bf16[512,1280]{1,0:T(8,128)(2,1)S(1)}, u32[]{:S(2)}, u32[]{:S(2)}) collective-permute-start(bf16[512,1280]{1,0:T(8,128)(2,1)} %refs_0_.1), channel_id=1, source_target_pairs={{0,1},{1,0},{2,3},{3,2},{4,5},{5,4},{6,7},{7,6},{8,9},{9,8},{10,11... | collective-permute-start | bytes 3932168 | tf_op jit(solution)/shard_map/ppermute | solution.py:456
  3.0 1.4 copy-start.4
  5.5 12.4 %collective-permute-start.3 = (bf16[256,1280]{1,0:T(8,128)(2,1)}, bf16[256,1280]{1,0:T(8,128)(2,1)S(1)}, u32[]{:S(2)}, u32[]{:S(2)}) collective-permute-start(bf16[256,1280]{1,0:T(8,128)(2,1)} %get-tuple-element.51), channel_id=1, source_target_pairs={{1,2},{2,1},{5,6},{6,5},{9,10},{10,9},{13,14},{14,13},{17,18},{18,... | collective-permute-start | bytes 1966088 | tf_op jit(solution)/shard_map/ppermute | solution.py:459
  6.2 13.6 %collective-permute-start.5 = (bf16[256,1280]{1,0:T(8,128)(2,1)}, bf16[256,1280]{1,0:T(8,128)(2,1)}, u32[]{:S(2)}, u32[]{:S(2)}) collective-permute-start(bf16[256,1280]{1,0:T(8,128)(2,1)} %get-tuple-element.56), channel_id=1, source_target_pairs={{1,2},{2,1},{5,6},{6,5},{9,10},{10,9},{13,14},{14,13},{17,18},{18,... | collective-permute-start | bytes 1966088 | tf_op jit(solution)/shard_map/ppermute | solution.py:459
  7.8 4.0 %copy-start.1 = (bf16[5120,1024]{1,0:T(8,128)(2,1)S(1)}, bf16[5120,1024]{1,0:T(8,128)(2,1)}, u32[]{:S(2)}) copy-start(bf16[5120,1024]{1,0:T(8,128)(2,1)} %refs_2_.8) | copy-start | bytes 31457284
  11.8 1.3 copy-start.3
  13.1 1.3 copy-start.5
  14.5 4.8 %copy-start = (bf16[1024,5120]{1,0:T(8,128)(2,1)S(1)}, bf16[1024,5120]{1,0:T(8,128)(2,1)}, u32[]{:S(2)}) copy-start(bf16[1024,5120]{1,0:T(8,128)(2,1)} %w_ref.19) | copy-start | bytes 31457284
  17.9 29.0 %collective-permute-start.4 = (bf16[256,1280]{1,0:T(8,128)(2,1)S(1)}, bf16[256,1280]{1,0:T(8,128)(2,1)S(1)}, u32[]{:S(2)}, u32[]{:S(2)}) collective-permute-start(bf16[256,1280]{1,0:T(8,128)(2,1)S(1)} %collective-permute-done.3.refs_0_), channel_id=1, source_target_pairs={{1,0},{2,3},{5,4},{6,7},{9,8},{10,11},{13,12},{14,15},{17,16},{18,... | collective-permute-start | bytes 1966088 | tf_op jit(solution)/shard_map/ppermute | solution.py:462
  32.9 19.9 %collective-permute-start.1 = (bf16[256,1280]{1,0:T(8,128)(2,1)S(1)}, bf16[256,1280]{1,0:T(8,128)(2,1)S(1)}, u32[]{:S(2)}, u32[]{:S(2)}) collective-permute-start(bf16[256,1280]{1,0:T(8,128)(2,1)S(1)} %get-tuple-element.49), channel_id=1, source_target_pairs={{1,2},{2,1},{5,6},{6,5},{9,10},{10,9},{13,14},{14,13},{17,18},{18,... | collective-permute-start | bytes 1966088 | tf_op jit(solution)/shard_map/ppermute | solution.py:459
  33.6 27.3 %collective-permute-start.7 = (bf16[256,1280]{1,0:T(8,128)(2,1)}, bf16[256,1280]{1,0:T(8,128)(2,1)S(1)}, u32[]{:S(2)}, u32[]{:S(2)}) collective-permute-start(bf16[256,1280]{1,0:T(8,128)(2,1)} %collective-permute-done.5.refs_2_), channel_id=1, source_target_pairs={{1,0},{2,3},{5,4},{6,7},{9,8},{10,11},{13,12},{14,15},{17,16},{18,... | collective-permute-start | bytes 1966088 | tf_op jit(solution)/shard_map/ppermute | solution.py:462
  46.9 16.5 %collective-permute-start.9 = (bf16[128,2560]{1,0:T(8,128)(2,1)S(1)}, bf16[128,2560]{1,0:T(8,128)(2,1)S(1)}, u32[]{:S(2)}, u32[]{:S(2)}) collective-permute-start(bf16[128,2560]{1,0:T(8,128)(2,1)S(1)} %eighth.2), channel_id=1, source_target_pairs={{0,1},{3,2},{4,5},{7,6},{8,9},{11,10},{12,13},{15,14},{16,17},{19,... | collective-permute-start | bytes 1966088 | tf_op jit(solution)/shard_map/ppermute | solution.py:465
  48.4 19.9 %slice-start = ((s8[10485760]{0:T(1024)(128)(4,1)}), s8[4194304]{0:T(1024)(128)(4,1)S(1)}, s32[]{:S(2)}) async-start(s8[10485760]{0:T(1024)(128)(4,1)} %bitcast.14), calls=%async_computation | async-start | bytes 8388608
  48.4 19.8 %slice-start.1 = ((s8[10485760]{0:T(1024)(128)(4,1)}), s8[4194304]{0:T(1024)(128)(4,1)S(1)}, s32[]{:S(2)}) async-start(s8[10485760]{0:T(1024)(128)(4,1)} %bitcast.14), calls=%async_computation.1 | async-start | bytes 8388608
  52.0 16.2 %slice-start.2 = ((s8[10485760]{0:T(1024)(128)(4,1)}), s8[2097152]{0:T(1024)(128)(4,1)S(1)}, s32[]{:S(2)}) async-start(s8[10485760]{0:T(1024)(128)(4,1)} %bitcast.14), calls=%async_computation.2 | async-start | bytes 4194304
  52.0 14.9 %collective-permute-start.6 = (bf16[256,1280]{1,0:T(8,128)(2,1)S(1)}, bf16[256,1280]{1,0:T(8,128)(2,1)S(1)}, u32[]{:S(2)}, u32[]{:S(2)}) collective-permute-start(bf16[256,1280]{1,0:T(8,128)(2,1)S(1)} %get-tuple-element.64), channel_id=1, source_target_pairs={{1,2},{2,1},{5,6},{6,5},{9,10},{10,9},{13,14},{14,13},{17,18},{18,... | collective-permute-start | bytes 1966088 | tf_op jit(solution)/shard_map/ppermute | solution.py:459
  52.9 22.7 %collective-permute-start.2 = (bf16[256,1280]{1,0:T(8,128)(2,1)S(1)}, bf16[256,1280]{1,0:T(8,128)(2,1)S(1)}, u32[]{:S(2)}, u32[]{:S(2)}) collective-permute-start(bf16[256,1280]{1,0:T(8,128)(2,1)S(1)} %collective-permute-done.1.refs_0_), channel_id=1, source_target_pairs={{1,0},{2,3},{5,4},{6,7},{9,8},{10,11},{13,12},{14,15},{17,16},{18,... | collective-permute-start | bytes 1966088 | tf_op jit(solution)/shard_map/ppermute | solution.py:462
  54.2 21.4 %copy-start.11 = (f32[128]{0:T(128)S(1)}, f32[128]{0:T(128)}, u32[]{:S(2)}) copy-start(f32[128]{0:T(128)} %param.18) | copy-start | bytes 1540
  54.8 20.8 %copy-start.6 = (f32[512,128]{1,0:T(8,128)S(1)}, f32[512,128]{1,0:T(8,128)}, u32[]{:S(2)}) copy-start(f32[512,128]{1,0:T(8,128)} %constant.29.clone.refs_5_.refs_7_.refs_8_) | copy-start | bytes 786436
  54.8 20.8 %copy-start.7 = (f32[512,128]{1,0:T(8,128)S(1)}, f32[512,128]{1,0:T(8,128)}, u32[]{:S(2)}) copy-start(f32[512,128]{1,0:T(8,128)} %constant.30.clone.refs_6_.refs_8_.refs_9_) | copy-start | bytes 786436
  60.9 0.8 copy-start.8
  61.8 17.4 %collective-permute-start.10 = (bf16[128,2560]{1,0:T(8,128)(2,1)S(1)}, bf16[128,2560]{1,0:T(8,128)(2,1)S(1)}, u32[]{:S(2)}, u32[]{:S(2)}) collective-permute-start(bf16[128,2560]{1,0:T(8,128)(2,1)S(1)} %eighth.3), channel_id=1, source_target_pairs={{0,1},{3,2},{4,5},{7,6},{8,9},{11,10},{12,13},{15,14},{16,17},{19,... | collective-permute-start | bytes 1966088 | tf_op jit(solution)/shard_map/ppermute | solution.py:465
  63.4 15.8 %collective-permute-start.11 = (bf16[128,2560]{1,0:T(8,128)(2,1)S(1)}, bf16[128,2560]{1,0:T(8,128)(2,1)S(1)}, u32[]{:S(2)}, u32[]{:S(2)}) collective-permute-start(bf16[128,2560]{1,0:T(8,128)(2,1)S(1)} %collective-permute-done.9.refs_0_), channel_id=1, source_target_pairs={{0,8},{4,12},{8,0},{12,4},{16,24},{20,28},{24,16},{28,20},{1,9},{5... | collective-permute-start | bytes 1966088 | tf_op jit(solution)/shard_map/ppermute | solution.py:468
  65.4 13.9 %collective-permute-start.12 = (bf16[128,2560]{1,0:T(8,128)(2,1)S(1)}, bf16[128,2560]{1,0:T(8,128)(2,1)S(1)}, u32[]{:S(2)}, u32[]{:S(2)}) collective-permute-start(bf16[128,2560]{1,0:T(8,128)(2,1)S(1)} %collective-permute-done.9.refs_0_), channel_id=1, source_target_pairs={{0,16},{4,20},{8,24},{12,28},{16,0},{20,4},{24,8},{28,12},{1,17},{... | collective-permute-start | bytes 1966088 | tf_op jit(solution)/shard_map/ppermute | solution.py:468
  66.9 21.3 %collective-permute-start.8 = (bf16[256,1280]{1,0:T(8,128)(2,1)S(1)}, bf16[256,1280]{1,0:T(8,128)(2,1)S(1)}, u32[]{:S(2)}, u32[]{:S(2)}) collective-permute-start(bf16[256,1280]{1,0:T(8,128)(2,1)S(1)} %collective-permute-done.6.refs_0_.refs_1_), channel_id=1, source_target_pairs={{1,0},{2,3},{5,4},{6,7},{9,8},{10,11},{13,12},{14,15},{17,16},{18,... | collective-permute-start | bytes 1966088 | tf_op jit(solution)/shard_map/ppermute | solution.py:462
  68.2 1.1 copy-start.9
  75.6 2.5 %copy-start.10 = (f32[128]{0:T(128)S(1)}, f32[128]{0:T(128)}, u32[]{:S(2)}) copy-start(f32[128]{0:T(128)} %param.19) | copy-start | bytes 1540
  79.2 9.0 %copy-start.12 = (s32[1,128]{1,0:T(1,128)S(1)}, s32[1,128]{1,0:T(1,128)}, u32[]{:S(2)}) copy-start(s32[1,128]{1,0:T(1,128)} %refs_10_.1) | copy-start | bytes 1540
  89.5 5.4 %collective-permute-start.13 = (bf16[128,256]{1,0:T(8,128)(2,1)S(1)}, bf16[128,256]{1,0:T(8,128)(2,1)S(1)}, u32[]{:S(2)}, u32[]{:S(2)}) collective-permute-start(bf16[128,256]{1,0:T(8,128)(2,1)S(1)} %get-tuple-element.76), channel_id=1, source_target_pairs={{0,28},{4,24},{8,20},{12,16},{16,12},{20,8},{24,4},{28,0},{1,29},{... | collective-permute-start | bytes 196616 | tf_op jit(solution)/shard_map/ppermute | solution.py:468
  90.7 5.3 %collective-permute-start.14 = (bf16[128,256]{1,0:T(8,128)(2,1)S(1)}, bf16[128,256]{1,0:T(8,128)(2,1)S(1)}, u32[]{:S(2)}, u32[]{:S(2)}) collective-permute-start(bf16[128,256]{1,0:T(8,128)(2,1)S(1)} %get-tuple-element.76), channel_id=1, source_target_pairs={{0,24},{4,28},{8,16},{12,20},{16,8},{20,12},{24,0},{28,4},{1,25},{... | collective-permute-start | bytes 196616 | tf_op jit(solution)/shard_map/ppermute | solution.py:468
  92.3 6.7 %collective-permute-start.15 = (bf16[128,256]{1,0:T(8,128)(2,1)S(1)}, bf16[128,256]{1,0:T(8,128)(2,1)S(1)}, u32[]{:S(2)}, u32[]{:S(2)}) collective-permute-start(bf16[128,256]{1,0:T(8,128)(2,1)S(1)} %get-tuple-element.76), channel_id=1, source_target_pairs={{0,20},{4,16},{8,28},{12,24},{16,4},{20,0},{24,12},{28,8},{1,21},{... | collective-permute-start | bytes 196616 | tf_op jit(solution)/shard_map/ppermute | solution.py:468
  93.6 5.7 %collective-permute-start.16 = (bf16[128,256]{1,0:T(8,128)(2,1)S(1)}, bf16[128,256]{1,0:T(8,128)(2,1)S(1)}, u32[]{:S(2)}, u32[]{:S(2)}) collective-permute-start(bf16[128,256]{1,0:T(8,128)(2,1)S(1)} %get-tuple-element.76), channel_id=1, source_target_pairs={{0,16},{4,20},{8,24},{12,28},{16,0},{20,4},{24,8},{28,12},{1,17},{... | collective-permute-start | bytes 196616 | tf_op jit(solution)/shard_map/ppermute | solution.py:468
  94.0 5.4 %collective-permute-start.17 = (bf16[128,256]{1,0:T(8,128)(2,1)S(1)}, bf16[128,256]{1,0:T(8,128)(2,1)S(1)}, u32[]{:S(2)}, u32[]{:S(2)}) collective-permute-start(bf16[128,256]{1,0:T(8,128)(2,1)S(1)} %get-tuple-element.76), channel_id=1, source_target_pairs={{0,12},{4,8},{8,4},{12,0},{16,28},{20,24},{24,20},{28,16},{1,13},{... | collective-permute-start | bytes 196616 | tf_op jit(solution)/shard_map/ppermute | solution.py:468
  94.9 4.9 %collective-permute-start.18 = (bf16[128,256]{1,0:T(8,128)(2,1)S(1)}, bf16[128,256]{1,0:T(8,128)(2,1)S(1)}, u32[]{:S(2)}, u32[]{:S(2)}) collective-permute-start(bf16[128,256]{1,0:T(8,128)(2,1)S(1)} %get-tuple-element.76), channel_id=1, source_target_pairs={{0,8},{4,12},{8,0},{12,4},{16,24},{20,28},{24,16},{28,20},{1,9},{5... | collective-permute-start | bytes 196616 | tf_op jit(solution)/shard_map/ppermute | solution.py:468
  96.0 3.8 %collective-permute-start.19 = (bf16[128,256]{1,0:T(8,128)(2,1)S(1)}, bf16[128,256]{1,0:T(8,128)(2,1)S(1)}, u32[]{:S(2)}, u32[]{:S(2)}) collective-permute-start(bf16[128,256]{1,0:T(8,128)(2,1)S(1)} %get-tuple-element.76), channel_id=1, source_target_pairs={{0,4},{4,0},{8,12},{12,8},{16,20},{20,16},{24,28},{28,24},{1,5},{5... | collective-permute-start | bytes 196616 | tf_op jit(solution)/shard_map/ppermute | solution.py:468
  99.8 12.7 %collective-permute-start.21 = (bf16[512,2560]{1,0:T(8,128)(2,1)S(1)}, bf16[512,2560]{1,0:T(8,128)(2,1)S(1)}, u32[]{:S(2)}, u32[]{:S(2)}) collective-permute-start(bf16[512,2560]{1,0:T(8,128)(2,1)S(1)} %joined.1.refs_0_), channel_id=1, source_target_pairs={{0,4},{4,0},{8,12},{12,8},{16,20},{20,16},{24,28},{28,24},{1,5},{5... | collective-permute-start | bytes 7864328 | tf_op jit(solution)/shard_map/ppermute | solution.py:468
  104.1 8.4 %collective-permute-start.20 = (bf16[128,1024]{1,0:T(8,128)(2,1)S(1)}, bf16[128,1024]{1,0:T(8,128)(2,1)S(1)}, u32[]{:S(2)}, u32[]{:S(2)}) collective-permute-start(bf16[128,1024]{1,0:T(8,128)(2,1)S(1)} %attention.3.rows_ref), channel_id=1, source_target_pairs={{0,1},{3,2},{4,5},{7,6},{8,9},{11,10},{12,13},{15,14},{16,17},{19,... | collective-permute-start | bytes 786440 | tf_op jit(solution)/shard_map/ppermute | solution.py:465
  107.5 24.3 %collective-permute-start.23 = (bf16[128,2560]{1,0:T(8,128)(2,1)S(1)}, bf16[128,2560]{1,0:T(8,128)(2,1)S(1)}, u32[]{:S(2)}, u32[]{:S(2)}) collective-permute-start(bf16[128,2560]{1,0:T(8,128)(2,1)S(1)} %mix.8.refs_0_), channel_id=1, source_target_pairs={{0,1},{3,2},{4,5},{7,6},{8,9},{11,10},{12,13},{15,14},{16,17},{19,... | collective-permute-start | bytes 1966088 | tf_op jit(solution)/shard_map/ppermute | solution.py:465
  114.0 23.1 %collective-permute-start.24 = (bf16[128,2560]{1,0:T(8,128)(2,1)S(1)}, bf16[128,2560]{1,0:T(8,128)(2,1)S(1)}, u32[]{:S(2)}, u32[]{:S(2)}) collective-permute-start(bf16[128,2560]{1,0:T(8,128)(2,1)S(1)} %added.8), channel_id=1, source_target_pairs={{1,2},{2,1},{5,6},{6,5},{9,10},{10,9},{13,14},{14,13},{17,18},{18,... | collective-permute-start | bytes 1966088 | tf_op jit(solution)/shard_map/ppermute | solution.py:459
  114.7 18.0 %collective-permute-start.22 = (bf16[128,1024]{1,0:T(8,128)(2,1)S(1)}, bf16[128,1024]{1,0:T(8,128)(2,1)S(1)}, u32[]{:S(2)}, u32[]{:S(2)}) collective-permute-start(bf16[128,1024]{1,0:T(8,128)(2,1)S(1)} %attention.4.rows_ref), channel_id=1, source_target_pairs={{0,1},{3,2},{4,5},{7,6},{8,9},{11,10},{12,13},{15,14},{16,17},{19,... | collective-permute-start | bytes 786440 | tf_op jit(solution)/shard_map/ppermute | solution.py:465
  128.5 8.6 %collective-permute-start.25 = (bf16[128,1024]{1,0:T(8,128)(2,1)S(1)}, bf16[128,1024]{1,0:T(8,128)(2,1)S(1)}, u32[]{:S(2)}, u32[]{:S(2)}) collective-permute-start(bf16[128,1024]{1,0:T(8,128)(2,1)S(1)} %get-tuple-element.88.rows_ref), channel_id=1, source_target_pairs={{0,1},{3,2},{4,5},{7,6},{8,9},{11,10},{12,13},{15,14},{16,17},{19,... | collective-permute-start | bytes 786440 | tf_op jit(solution)/shard_map/ppermute | solution.py:465
  132.0 15.0 %collective-permute-start.27 = (bf16[128,2560]{1,0:T(8,128)(2,1)S(1)}, bf16[128,2560]{1,0:T(8,128)(2,1)S(1)}, u32[]{:S(2)}, u32[]{:S(2)}) collective-permute-start(bf16[128,2560]{1,0:T(8,128)(2,1)S(1)} %added.9), channel_id=1, source_target_pairs={{1,2},{2,1},{5,6},{6,5},{9,10},{10,9},{13,14},{14,13},{17,18},{18,... | collective-permute-start | bytes 1966088 | tf_op jit(solution)/shard_map/ppermute | solution.py:459
  137.1 18.3 %collective-permute-start.26 = (bf16[128,2560]{1,0:T(8,128)(2,1)S(1)}, bf16[128,2560]{1,0:T(8,128)(2,1)S(1)}, u32[]{:S(2)}, u32[]{:S(2)}) collective-permute-start(bf16[128,2560]{1,0:T(8,128)(2,1)S(1)} %mix.10.refs_0_), channel_id=1, source_target_pairs={{0,1},{3,2},{4,5},{7,6},{8,9},{11,10},{12,13},{15,14},{16,17},{19,... | collective-permute-start | bytes 1966088 | tf_op jit(solution)/shard_map/ppermute | solution.py:465
  144.0 20.0 %collective-permute-start.32 = (bf16[128,2560]{1,0:T(8,128)(2,1)S(1)}, bf16[128,2560]{1,0:T(8,128)(2,1)S(1)}, u32[]{:S(2)}, u32[]{:S(2)}) collective-permute-start(bf16[128,2560]{1,0:T(8,128)(2,1)S(1)} %added.10), channel_id=1, source_target_pairs={{1,2},{2,1},{5,6},{6,5},{9,10},{10,9},{13,14},{14,13},{17,18},{18,... | collective-permute-start | bytes 1966088 | tf_op jit(solution)/shard_map/ppermute | solution.py:459
  144.8 20.3 %collective-permute-start.31 = (bf16[128,2560]{1,0:T(8,128)(2,1)S(1)}, bf16[128,2560]{1,0:T(8,128)(2,1)S(1)}, u32[]{:S(2)}, u32[]{:S(2)}) collective-permute-start(bf16[128,2560]{1,0:T(8,128)(2,1)S(1)} %added.11), channel_id=1, source_target_pairs={{1,0},{2,3},{5,4},{6,7},{9,8},{10,11},{13,12},{14,15},{17,16},{18,... | collective-permute-start | bytes 1966088 | tf_op jit(solution)/shard_map/ppermute | solution.py:462
  147.2 30.8 %collective-permute-start.29 = (bf16[128,2560]{1,0:T(8,128)(2,1)S(1)}, bf16[128,2560]{1,0:T(8,128)(2,1)S(1)}, u32[]{:S(2)}, u32[]{:S(2)}) collective-permute-start(bf16[128,2560]{1,0:T(8,128)(2,1)S(1)} %added.12), channel_id=1, source_target_pairs={{1,0},{2,3},{5,4},{6,7},{9,8},{10,11},{13,12},{14,15},{17,16},{18,... | collective-permute-start | bytes 1966088 | tf_op jit(solution)/shard_map/ppermute | solution.py:462
  155.6 22.4 %collective-permute-start.28 = (bf16[128,2560]{1,0:T(8,128)(2,1)S(1)}, bf16[128,2560]{1,0:T(8,128)(2,1)S(1)}, u32[]{:S(2)}, u32[]{:S(2)}) collective-permute-start(bf16[128,2560]{1,0:T(8,128)(2,1)S(1)} %mix.13.refs_0_), channel_id=1, source_target_pairs={{0,1},{3,2},{4,5},{7,6},{8,9},{11,10},{12,13},{15,14},{16,17},{19,... | collective-permute-start | bytes 1966088 | tf_op jit(solution)/shard_map/ppermute | solution.py:465
  160.0 17.9 %collective-permute-start.30 = (bf16[128,2560]{1,0:T(8,128)(2,1)S(1)}, bf16[128,2560]{1,0:T(8,128)(2,1)S(1)}, u32[]{:S(2)}, u32[]{:S(2)}) collective-permute-start(bf16[128,2560]{1,0:T(8,128)(2,1)S(1)} %added.13), channel_id=1, source_target_pairs={{1,2},{2,1},{5,6},{6,5},{9,10},{10,9},{13,14},{14,13},{17,18},{18,... | collective-permute-start | bytes 1966088 | tf_op jit(solution)/shard_map/ppermute | solution.py:459

commit v18 on v16

--- a/solution.py
+++ b/solution.py
@@ -569,7 +569,8 @@
     result = added(kept[1], near_sent, outward(out_right), third_right, half=1)
     near_in = inward(after(near[0], third_left))
     out_left, third_left = outward(out_left), across(third_left)
-    return added(kept[0], near_in, out_left, third_left, half=0, into=result)
+    kept[0] = added(kept[0], near_in, out_left)
+    return added(kept[0], third_left, half=0, into=result)
 
 
 def solution(mesh):

time: 177 us -> 176 us (level)
  no operation moved by 1% of the time
where the time goes in v18:
time: 176 us; the launch traced here: 175 us
  waiting for transfers between devices  59.8 us (34%)
  starting transfers between devices  54.8 us (31%)
  Pallas kernels  48.9 us (28%)
  local copies, waits for them, and re-layouts  10 us (6%)
    ppermute x6, waiting for transfers between devices, outward(): return lax.ppermute(array, 'tensor', [(1, 0), (2, 3)])  37.8 us
    ppermute x8, starting transfers between devices, inward(): return lax.ppermute(array, 'tensor', [(0, 1), (3, 2)])  26.9 us
    ppermute x1, waiting for transfers between devices, swap(): return lax.ppermute(array, 'tensor', [(0, 1), (1, 0), (2, 3), (3, 2)])  13 us
    pallas_call x3, Pallas kernels, attention(): pl.pallas_call(functools.partial(attention_kernel, slots, n_parts, len(ot...  12.7 us
    pallas_call x3, Pallas kernels, partial_projection(): pl.pallas_call(functools.partial(partial_kernel, [len(part) for part in p...  11.6 us
    ppermute x10, starting transfers between devices, between(): return lax.ppermute(array, 'cand', [(i, i ^ offset) for i in range(n_cand)])  10.5 us
    unnamed x32, local copies, waits for them, and re-layouts  9.93 us
    ppermute x8, waiting for transfers between devices, inward(): return lax.ppermute(array, 'tensor', [(0, 1), (3, 2)])  7.92 us
  transfers between devices with their start and end apart: 33, of which 13 were waited for; matrix products, arithmetic and copies ran while one was open for 0% of the time, Pallas kernels for 27%

profile of v18, /device:TPU:0, one launch (start us, length us, event | category | flops | bytes accessed | tf_op | source)
XLA Modules:
  0.0 174.9 jit_solution(4668044749302145086)
XLA Ops:
  0.0 3.0 %collective-permute-start = (bf16[512,1280]{1,0:T(8,128)(2,1)}, bf16[512,1280]{1,0:T(8,128)(2,1)S(1)}, u32[]{:S(2)}, u32[]{:S(2)}) collective-permute-start(bf16[512,1280]{1,0:T(8,128)(2,1)} %refs_0_.1), channel_id=1, source_target_pairs={{0,1},{1,0},{2,3},{3,2},{4,5},{5,4},{6,7},{7,6},{8,9},{9,8},{10,11... | collective-permute-start | bytes 3932168 | tf_op jit(solution)/shard_map/ppermute | solution.py:456
  3.0 1.3 copy-done.4
  4.4 1.2 halves.3
  6.2 1.5 collective-permute-start.5
  7.9 4.0 %copy-done.1 = bf16[5120,1024]{1,0:T(8,128)(2,1)S(1)} copy-done((bf16[5120,1024]{1,0:T(8,128)(2,1)S(1)}, bf16[5120,1024]{1,0:T(8,128)(2,1)}, u32[]{:S(2)}) %copy-start.1) | copy-done | bytes 10485784
  11.8 1.3 copy-done.3
  13.1 1.3 copy-done.5
  14.5 3.4 %partial_projection.3 = (f32[512,1024]{1,0:T(8,128)S(1)}, f32[512,128]{1,0:T(8,128)S(1)}, f32[512,128]{1,0:T(8,128)S(1)}) custom-call(s32[12]{0:T(128)S(1)} %stack.51.places_ref, bf16[512,1280]{1,0:T(8,128)(2,1)S(1)} %copy-done.5, bf16[5120,1024]{1,0:T(8,128)(2,1)S(1)} %copy-done.1, bf16[5120,128]{1,0:T(8,128)(2,1)S(1)} %copy-done.2, ...), custom_call_target="tpu_custom_call" | custom-call | flops 1 | bytes 1 | tf_op jit(solution)/shard_map/partial_projection/pallas_call | solution.py:100
  17.9 1.3 collective-permute-start.4
  19.8 13.0 %collective-permute-done.ref.refs_0_ = bf16[512,1280]{1,0:T(8,128)(2,1)S(1)} collective-permute-done((bf16[512,1280]{1,0:T(8,128)(2,1)}, bf16[512,1280]{1,0:T(8,128)(2,1)S(1)}, u32[]{:S(2)}, u32[]{:S(2)}) %collective-permute-start) | collective-permute-done | bytes 1310752 | tf_op jit(solution)/shard_map/ppermute | solution.py:456
  32.9 0.7 collective-permute-start.1
  33.6 1.3 collective-permute-start.7
  34.9 11.9 %collective-permute-done.4.refs_1_ = bf16[256,1280]{1,0:T(8,128)(2,1)S(1)} collective-permute-done((bf16[256,1280]{1,0:T(8,128)(2,1)S(1)}, bf16[256,1280]{1,0:T(8,128)(2,1)S(1)}, u32[]{:S(2)}, u32[]{:S(2)}) %collective-permute-start.4) | collective-permute-done | bytes 655392 | tf_op jit(solution)/shard_map/ppermute | solution.py:462
  46.9 1.5 collective-permute-start.9
  48.4 3.6 %partial_projection.4 = (f32[512,1024]{1,0:T(8,128)S(1)}, f32[512,128]{1,0:T(8,128)S(1)}, f32[512,128]{1,0:T(8,128)S(1)}) custom-call(s32[12]{0:T(128)S(1)} %stack.51.places_ref, bf16[512,1280]{1,0:T(8,128)(2,1)S(1)} %collective-permute-done.ref.refs_0_, bf16[5120,1024]{1,0:T(8,128)(2,1)S(1)} %copy-done.1, bf16[5120,128]{1,0:T(8,128)(2,1)S(1)} %copy-done.2, ...), custom_call_target="tpu_custom_call" | custom-call | flops 1 | bytes 1 | tf_op jit(solution)/shard_map/partial_projection/pallas_call | solution.py:100
  52.0 0.8 collective-permute-start.6
  52.9 1.3 collective-permute-start.2
  54.8 6.1 %collective-permute-done.7.refs_3_ = bf16[256,1280]{1,0:T(8,128)(2,1)S(1)} collective-permute-done((bf16[256,1280]{1,0:T(8,128)(2,1)}, bf16[256,1280]{1,0:T(8,128)(2,1)S(1)}, u32[]{:S(2)}, u32[]{:S(2)}) %collective-permute-start.7) | collective-permute-done | bytes 655392 | tf_op jit(solution)/shard_map/ppermute | solution.py:462
  60.9 0.8 copy-done.8
  61.8 1.6 collective-permute-start.10
  63.4 2.0 %collective-permute-start.11 = (bf16[128,2560]{1,0:T(8,128)(2,1)S(1)}, bf16[128,2560]{1,0:T(8,128)(2,1)S(1)}, u32[]{:S(2)}, u32[]{:S(2)}) collective-permute-start(bf16[128,2560]{1,0:T(8,128)(2,1)S(1)} %collective-permute-done.9.refs_0_), channel_id=1, source_target_pairs={{0,8},{4,12},{8,0},{12,4},{16,24},{20,28},{24,16},{28,20},{1,9},{5... | collective-permute-start | bytes 1966088 | tf_op jit(solution)/shard_map/ppermute | solution.py:468
  65.4 1.5 collective-permute-start.12
  66.9 1.3 collective-permute-start.8
  68.3 1.1 copy-done.9
  69.3 4.6 %partial_projection.5 = (f32[512,1024]{1,0:T(8,128)S(1)}, f32[512,128]{1,0:T(8,128)S(1)}, f32[512,128]{1,0:T(8,128)S(1)}) custom-call(s32[12]{0:T(128)S(1)} %stack.51.places_ref, bf16[256,1280]{1,0:T(8,128)(2,1)S(1)} %collective-permute-done.3.refs_0_, bf16[256,1280]{1,0:T(8,128)(2,1)S(1)} %collective-permute-done.4.refs_1_, ...), custom_call_target="tpu_custom_call" | custom-call | flops 1 | bytes 1 | tf_op jit(solution)/shard_map/partial_projection/pallas_call | solution.py:100
  73.9 1.6 collective-permute-done.2.refs_1_
  75.6 2.5 %queries.2.refs_0_ = bf16[256,1024]{1,0:T(8,128)(2,1)S(1)} custom-call(s32[12]{0:T(128)S(1)} %stack.51.places_ref, bf16[256,1280]{1,0:T(8,128)(2,1)S(1)} %collective-permute-done.1.refs_0_, bf16[256,1280]{1,0:T(8,128)(2,1)S(1)} %collective-permute-done.2.refs_1_, bf16[5120,1024]{1,0:T(8,128)(2,1)S(1)} %bitcast.15, ...), custom_call_target="tpu_custom_call" | custom-call | flops 1 | bytes 1 | tf_op jit(solution)/shard_map/queries/pallas_call | solution.py:187
  78.1 1.1 keys_values.2.refs_0_.refs_2_
  79.5 8.7 %collective-permute-done.8.refs_1_.refs_2_ = bf16[256,1280]{1,0:T(8,128)(2,1)S(1)} collective-permute-done((bf16[256,1280]{1,0:T(8,128)(2,1)S(1)}, bf16[256,1280]{1,0:T(8,128)(2,1)S(1)}, u32[]{:S(2)}, u32[]{:S(2)}) %collective-permute-start.8) | collective-permute-done | bytes 655392 | tf_op jit(solution)/shard_map/ppermute | solution.py:462
  88.2 1.3 keys_values.3
  89.5 1.2 collective-permute-start.13
  90.7 1.6 collective-permute-start.14
  92.3 1.4 collective-permute-start.15
  94.0 0.9 collective-permute-start.17
  94.9 1.0 collective-permute-start.18
  96.5 2.5 %queries.3.refs_1_ = bf16[256,1024]{1,0:T(8,128)(2,1)S(1)} custom-call(s32[12]{0:T(128)S(1)} %stack.51.places_ref, bf16[256,1280]{1,0:T(8,128)(2,1)S(1)} %collective-permute-done.6.refs_0_.refs_1_, bf16[256,1280]{1,0:T(8,128)(2,1)S(1)} %collective-permute-done.8.refs_1_.refs_2_, bf16[5120,1024]{1,0:T(8,128)(2,1)S(1)} %bitcast.15, ...), custom_call_target="tpu_custom_call" | custom-call | flops 1 | bytes 1 | tf_op jit(solution)/shard_map/queries/pallas_call | solution.py:187
  100.5 3.6 %attention.3.rows_ref = bf16[128,1024]{1,0:T(8,128)(2,1)S(1)} custom-call(s32[12]{0:T(128)S(1)} %stack.51.places_ref, s32[1]{0:T(128)S(6)} %copy.14.length_ref, bf16[256,1024]{1,0:T(8,128)(2,1)S(1)} %queries.2.refs_0_, bf16[256,1024]{1,0:T(8,128)(2,1)S(1)} %queries.3.refs_1_, bf16[256,256]{1,0:T(8,128)(2,1)S(1)} %keys_values.2.refs_0_.refs_2_, ...), custom_call_target="tpu_custom_call" | custom-call | flops 1 | bytes 1 | tf_op jit(solution)/shard_map/attention/pallas_call | solution.py:276
  104.1 1.6 collective-permute-start.20
  105.7 0.9 mix.8.refs_0_
  106.6 0.9 mix.9.refs_0_
  107.5 1.3 collective-permute-start.23
  108.8 3.6 %attention.4.rows_ref = bf16[128,1024]{1,0:T(8,128)(2,1)S(1)} custom-call(s32[12]{0:T(128)S(1)} %stack.51.places_ref, s32[1]{0:T(128)S(6)} %copy.14.length_ref, bf16[256,1024]{1,0:T(8,128)(2,1)S(1)} %queries.2.refs_0_, bf16[256,1024]{1,0:T(8,128)(2,1)S(1)} %queries.3.refs_1_, bf16[256,256]{1,0:T(8,128)(2,1)S(1)} %keys_values.2.refs_0_.refs_2_, ...), custom_call_target="tpu_custom_call" | custom-call | flops 1 | bytes 1 | tf_op jit(solution)/shard_map/attention/pallas_call | solution.py:276
  112.4 1.4 mix_sent.3.refs_1_
  114.7 8.2 %collective-permute-start.22 = (bf16[128,1024]{1,0:T(8,128)(2,1)S(1)}, bf16[128,1024]{1,0:T(8,128)(2,1)S(1)}, u32[]{:S(2)}, u32[]{:S(2)}) collective-permute-start(bf16[128,1024]{1,0:T(8,128)(2,1)S(1)} %attention.4.rows_ref), channel_id=1, source_target_pairs={{0,1},{3,2},{4,5},{7,6},{8,9},{11,10},{12,13},{15,14},{16,17},{19,... | collective-permute-start | bytes 786440 | tf_op jit(solution)/shard_map/ppermute | solution.py:465
  122.9 5.6 %attention.5 = (bf16[128,1024]{1,0:T(8,128)(2,1)S(1)}, bf16[128,1024]{1,0:T(8,128)(2,1)S(1)}) custom-call(s32[12]{0:T(128)S(1)} %stack.51.places_ref, s32[1]{0:T(128)S(6)} %copy.14.length_ref, bf16[256,1024]{1,0:T(8,128)(2,1)S(1)} %queries.2.refs_0_, bf16[256,1024]{1,0:T(8,128)(2,1)S(1)} %queries.3.refs_1_, bf16[256,256]{1,0:T(8,128)(2,1)S(1)} %keys_values.2.refs_0_.refs_2_, ...), custom_call_target="tpu_custom_call" | custom-call | flops 1 | bytes 1 | tf_op jit(solution)/shard_map/attention/pallas_call | solution.py:276
  128.5 0.9 mix.10.refs_0_
  129.4 0.9 mix.11.refs_0_
  130.5 0.9 collective-permute-start.26
  131.5 6.9 %collective-permute-start.25 = (bf16[128,2560]{1,0:T(8,128)(2,1)S(1)}, bf16[128,2560]{1,0:T(8,128)(2,1)S(1)}, u32[]{:S(2)}, u32[]{:S(2)}) collective-permute-start(bf16[128,2560]{1,0:T(8,128)(2,1)S(1)} %mix.10.refs_0_), channel_id=1, source_target_pairs={{0,1},{3,2},{4,5},{7,6},{8,9},{11,10},{12,13},{15,14},{16,17},{19,... | collective-permute-start | bytes 1966088 | tf_op jit(solution)/shard_map/ppermute | solution.py:465
  138.4 1.3 collective-permute-start.30
  139.7 1.4 mix_sent.4.refs_1_
  141.3 0.9 mix.12.refs_0_
  143.0 1.3 collective-permute-start.31
  144.3 0.9 mix.13.refs_0_
  145.4 1.3 collective-permute-start.28
  146.7 6.8 %collective-permute-done.25.refs_1_ = bf16[128,2560]{1,0:T(8,128)(2,1)S(1)} collective-permute-done((bf16[128,2560]{1,0:T(8,128)(2,1)S(1)}, bf16[128,2560]{1,0:T(8,128)(2,1)S(1)}, u32[]{:S(2)}, u32[]{:S(2)}) %collective-permute-start.25) | collective-permute-done | bytes 655392 | tf_op jit(solution)/shard_map/ppermute | solution.py:465
  153.7 4.4 %collective-permute-start.27 = (bf16[128,2560]{1,0:T(8,128)(2,1)S(1)}, bf16[128,2560]{1,0:T(8,128)(2,1)S(1)}, u32[]{:S(2)}, u32[]{:S(2)}) collective-permute-start(bf16[128,2560]{1,0:T(8,128)(2,1)S(1)} %mix.13.refs_0_), channel_id=1, source_target_pairs={{0,1},{3,2},{4,5},{7,6},{8,9},{11,10},{12,13},{15,14},{16,17},{19,... | collective-permute-start | bytes 1966088 | tf_op jit(solution)/shard_map/ppermute | solution.py:465
  158.1 1.0 collective-permute-done.30.rows_ref
  159.8 0.9 mix.14.refs_0_
  160.7 0.9 mix.15.refs_0_
  161.6 1.4 mix_sent.5.refs_1_
  163.0 1.2 added.16.refs_2_
  164.2 9.4 %collective-permute-done.28.refs_2_ = bf16[128,2560]{1,0:T(8,128)(2,1)S(1)} collective-permute-done((bf16[128,2560]{1,0:T(8,128)(2,1)S(1)}, bf16[128,2560]{1,0:T(8,128)(2,1)S(1)}, u32[]{:S(2)}, u32[]{:S(2)}) %collective-permute-start.28) | collective-permute-done | bytes 655392 | tf_op jit(solution)/shard_map/ppermute | solution.py:462
  173.9 1.0 added.17
  (71 shorter events, 7.6 us)
Async XLA Ops:
  0.0 7.8 %copy-start.2 = (bf16[5120,128]{1,0:T(8,128)(2,1)S(1)}, bf16[5120,128]{1,0:T(8,128)(2,1)}, u32[]{:S(2)}) copy-start(bf16[5120,128]{1,0:T(8,128)(2,1)} %refs_3_.7) | copy-start | bytes 3932164
  0.0 32.8 %collective-permute-start = (bf16[512,1280]{1,0:T(8,128)(2,1)}, bf16[512,1280]{1,0:T(8,128)(2,1)S(1)}, u32[]{:S(2)}, u32[]{:S(2)}) collective-permute-start(bf16[512,1280]{1,0:T(8,128)(2,1)} %refs_0_.1), channel_id=1, source_target_pairs={{0,1},{1,0},{2,3},{3,2},{4,5},{5,4},{6,7},{7,6},{8,9},{9,8},{10,11... | collective-permute-start | bytes 3932168 | tf_op jit(solution)/shard_map/ppermute | solution.py:456
  3.0 1.4 copy-start.4
  5.5 12.4 %collective-permute-start.3 = (bf16[256,1280]{1,0:T(8,128)(2,1)}, bf16[256,1280]{1,0:T(8,128)(2,1)S(1)}, u32[]{:S(2)}, u32[]{:S(2)}) collective-permute-start(bf16[256,1280]{1,0:T(8,128)(2,1)} %get-tuple-element.51), channel_id=1, source_target_pairs={{1,2},{2,1},{5,6},{6,5},{9,10},{10,9},{13,14},{14,13},{17,18},{18,... | collective-permute-start | bytes 1966088 | tf_op jit(solution)/shard_map/ppermute | solution.py:459
  6.2 13.6 %collective-permute-start.5 = (bf16[256,1280]{1,0:T(8,128)(2,1)}, bf16[256,1280]{1,0:T(8,128)(2,1)}, u32[]{:S(2)}, u32[]{:S(2)}) collective-permute-start(bf16[256,1280]{1,0:T(8,128)(2,1)} %get-tuple-element.56), channel_id=1, source_target_pairs={{1,2},{2,1},{5,6},{6,5},{9,10},{10,9},{13,14},{14,13},{17,18},{18,... | collective-permute-start | bytes 1966088 | tf_op jit(solution)/shard_map/ppermute | solution.py:459
  7.8 4.0 %copy-start.1 = (bf16[5120,1024]{1,0:T(8,128)(2,1)S(1)}, bf16[5120,1024]{1,0:T(8,128)(2,1)}, u32[]{:S(2)}) copy-start(bf16[5120,1024]{1,0:T(8,128)(2,1)} %refs_2_.8) | copy-start | bytes 31457284
  11.8 1.3 copy-start.3
  13.1 1.3 copy-start.5
  14.5 4.8 %copy-start = (bf16[1024,5120]{1,0:T(8,128)(2,1)S(1)}, bf16[1024,5120]{1,0:T(8,128)(2,1)}, u32[]{:S(2)}) copy-start(bf16[1024,5120]{1,0:T(8,128)(2,1)} %w_ref.19) | copy-start | bytes 31457284
  17.9 29.0 %collective-permute-start.4 = (bf16[256,1280]{1,0:T(8,128)(2,1)S(1)}, bf16[256,1280]{1,0:T(8,128)(2,1)S(1)}, u32[]{:S(2)}, u32[]{:S(2)}) collective-permute-start(bf16[256,1280]{1,0:T(8,128)(2,1)S(1)} %collective-permute-done.3.refs_0_), channel_id=1, source_target_pairs={{1,0},{2,3},{5,4},{6,7},{9,8},{10,11},{13,12},{14,15},{17,16},{18,... | collective-permute-start | bytes 1966088 | tf_op jit(solution)/shard_map/ppermute | solution.py:462
  32.9 19.9 %collective-permute-start.1 = (bf16[256,1280]{1,0:T(8,128)(2,1)S(1)}, bf16[256,1280]{1,0:T(8,128)(2,1)S(1)}, u32[]{:S(2)}, u32[]{:S(2)}) collective-permute-start(bf16[256,1280]{1,0:T(8,128)(2,1)S(1)} %get-tuple-element.49), channel_id=1, source_target_pairs={{1,2},{2,1},{5,6},{6,5},{9,10},{10,9},{13,14},{14,13},{17,18},{18,... | collective-permute-start | bytes 1966088 | tf_op jit(solution)/shard_map/ppermute | solution.py:459
  33.6 27.3 %collective-permute-start.7 = (bf16[256,1280]{1,0:T(8,128)(2,1)}, bf16[256,1280]{1,0:T(8,128)(2,1)S(1)}, u32[]{:S(2)}, u32[]{:S(2)}) collective-permute-start(bf16[256,1280]{1,0:T(8,128)(2,1)} %collective-permute-done.5.refs_2_), channel_id=1, source_target_pairs={{1,0},{2,3},{5,4},{6,7},{9,8},{10,11},{13,12},{14,15},{17,16},{18,... | collective-permute-start | bytes 1966088 | tf_op jit(solution)/shard_map/ppermute | solution.py:462
  46.9 16.5 %collective-permute-start.9 = (bf16[128,2560]{1,0:T(8,128)(2,1)S(1)}, bf16[128,2560]{1,0:T(8,128)(2,1)S(1)}, u32[]{:S(2)}, u32[]{:S(2)}) collective-permute-start(bf16[128,2560]{1,0:T(8,128)(2,1)S(1)} %eighth.2), channel_id=1, source_target_pairs={{0,1},{3,2},{4,5},{7,6},{8,9},{11,10},{12,13},{15,14},{16,17},{19,... | collective-permute-start | bytes 1966088 | tf_op jit(solution)/shard_map/ppermute | solution.py:465
  48.4 19.9 %slice-start = ((s8[10485760]{0:T(1024)(128)(4,1)}), s8[4194304]{0:T(1024)(128)(4,1)S(1)}, s32[]{:S(2)}) async-start(s8[10485760]{0:T(1024)(128)(4,1)} %bitcast.14), calls=%async_computation | async-start | bytes 8388608
  48.4 19.8 %slice-start.1 = ((s8[10485760]{0:T(1024)(128)(4,1)}), s8[4194304]{0:T(1024)(128)(4,1)S(1)}, s32[]{:S(2)}) async-start(s8[10485760]{0:T(1024)(128)(4,1)} %bitcast.14), calls=%async_computation.1 | async-start | bytes 8388608
  52.0 16.2 %slice-start.2 = ((s8[10485760]{0:T(1024)(128)(4,1)}), s8[2097152]{0:T(1024)(128)(4,1)S(1)}, s32[]{:S(2)}) async-start(s8[10485760]{0:T(1024)(128)(4,1)} %bitcast.14), calls=%async_computation.2 | async-start | bytes 4194304
  52.0 14.9 %collective-permute-start.6 = (bf16[256,1280]{1,0:T(8,128)(2,1)S(1)}, bf16[256,1280]{1,0:T(8,128)(2,1)S(1)}, u32[]{:S(2)}, u32[]{:S(2)}) collective-permute-start(bf16[256,1280]{1,0:T(8,128)(2,1)S(1)} %get-tuple-element.64), channel_id=1, source_target_pairs={{1,2},{2,1},{5,6},{6,5},{9,10},{10,9},{13,14},{14,13},{17,18},{18,... | collective-permute-start | bytes 1966088 | tf_op jit(solution)/shard_map/ppermute | solution.py:459
  52.9 22.7 %collective-permute-start.2 = (bf16[256,1280]{1,0:T(8,128)(2,1)S(1)}, bf16[256,1280]{1,0:T(8,128)(2,1)S(1)}, u32[]{:S(2)}, u32[]{:S(2)}) collective-permute-start(bf16[256,1280]{1,0:T(8,128)(2,1)S(1)} %collective-permute-done.1.refs_0_), channel_id=1, source_target_pairs={{1,0},{2,3},{5,4},{6,7},{9,8},{10,11},{13,12},{14,15},{17,16},{18,... | collective-permute-start | bytes 1966088 | tf_op jit(solution)/shard_map/ppermute | solution.py:462
  54.2 21.4 %copy-start.11 = (f32[128]{0:T(128)S(1)}, f32[128]{0:T(128)}, u32[]{:S(2)}) copy-start(f32[128]{0:T(128)} %param.18) | copy-start | bytes 1540
  54.8 20.8 %copy-start.6 = (f32[512,128]{1,0:T(8,128)S(1)}, f32[512,128]{1,0:T(8,128)}, u32[]{:S(2)}) copy-start(f32[512,128]{1,0:T(8,128)} %constant.29.clone.refs_5_.refs_7_.refs_8_) | copy-start | bytes 786436
  54.8 20.8 %copy-start.7 = (f32[512,128]{1,0:T(8,128)S(1)}, f32[512,128]{1,0:T(8,128)}, u32[]{:S(2)}) copy-start(f32[512,128]{1,0:T(8,128)} %constant.30.clone.refs_6_.refs_8_.refs_9_) | copy-start | bytes 786436
  60.9 0.8 copy-start.8
  61.8 17.4 %collective-permute-start.10 = (bf16[128,2560]{1,0:T(8,128)(2,1)S(1)}, bf16[128,2560]{1,0:T(8,128)(2,1)S(1)}, u32[]{:S(2)}, u32[]{:S(2)}) collective-permute-start(bf16[128,2560]{1,0:T(8,128)(2,1)S(1)} %eighth.3), channel_id=1, source_target_pairs={{0,1},{3,2},{4,5},{7,6},{8,9},{11,10},{12,13},{15,14},{16,17},{19,... | collective-permute-start | bytes 1966088 | tf_op jit(solution)/shard_map/ppermute | solution.py:465
  63.4 15.8 %collective-permute-start.11 = (bf16[128,2560]{1,0:T(8,128)(2,1)S(1)}, bf16[128,2560]{1,0:T(8,128)(2,1)S(1)}, u32[]{:S(2)}, u32[]{:S(2)}) collective-permute-start(bf16[128,2560]{1,0:T(8,128)(2,1)S(1)} %collective-permute-done.9.refs_0_), channel_id=1, source_target_pairs={{0,8},{4,12},{8,0},{12,4},{16,24},{20,28},{24,16},{28,20},{1,9},{5... | collective-permute-start | bytes 1966088 | tf_op jit(solution)/shard_map/ppermute | solution.py:468
  65.4 13.9 %collective-permute-start.12 = (bf16[128,2560]{1,0:T(8,128)(2,1)S(1)}, bf16[128,2560]{1,0:T(8,128)(2,1)S(1)}, u32[]{:S(2)}, u32[]{:S(2)}) collective-permute-start(bf16[128,2560]{1,0:T(8,128)(2,1)S(1)} %collective-permute-done.9.refs_0_), channel_id=1, source_target_pairs={{0,16},{4,20},{8,24},{12,28},{16,0},{20,4},{24,8},{28,12},{1,17},{... | collective-permute-start | bytes 1966088 | tf_op jit(solution)/shard_map/ppermute | solution.py:468
  66.9 21.3 %collective-permute-start.8 = (bf16[256,1280]{1,0:T(8,128)(2,1)S(1)}, bf16[256,1280]{1,0:T(8,128)(2,1)S(1)}, u32[]{:S(2)}, u32[]{:S(2)}) collective-permute-start(bf16[256,1280]{1,0:T(8,128)(2,1)S(1)} %collective-permute-done.6.refs_0_.refs_1_), channel_id=1, source_target_pairs={{1,0},{2,3},{5,4},{6,7},{9,8},{10,11},{13,12},{14,15},{17,16},{18,... | collective-permute-start | bytes 1966088 | tf_op jit(solution)/shard_map/ppermute | solution.py:462
  68.2 1.1 copy-start.9
  75.6 2.5 %copy-start.10 = (f32[128]{0:T(128)S(1)}, f32[128]{0:T(128)}, u32[]{:S(2)}) copy-start(f32[128]{0:T(128)} %param.19) | copy-start | bytes 1540
  79.2 9.0 %copy-start.12 = (s32[1,128]{1,0:T(1,128)S(1)}, s32[1,128]{1,0:T(1,128)}, u32[]{:S(2)}) copy-start(s32[1,128]{1,0:T(1,128)} %refs_10_.1) | copy-start | bytes 1540
  89.5 5.4 %collective-permute-start.13 = (bf16[128,256]{1,0:T(8,128)(2,1)S(1)}, bf16[128,256]{1,0:T(8,128)(2,1)S(1)}, u32[]{:S(2)}, u32[]{:S(2)}) collective-permute-start(bf16[128,256]{1,0:T(8,128)(2,1)S(1)} %get-tuple-element.76), channel_id=1, source_target_pairs={{0,28},{4,24},{8,20},{12,16},{16,12},{20,8},{24,4},{28,0},{1,29},{... | collective-permute-start | bytes 196616 | tf_op jit(solution)/shard_map/ppermute | solution.py:468
  90.7 5.3 %collective-permute-start.14 = (bf16[128,256]{1,0:T(8,128)(2,1)S(1)}, bf16[128,256]{1,0:T(8,128)(2,1)S(1)}, u32[]{:S(2)}, u32[]{:S(2)}) collective-permute-start(bf16[128,256]{1,0:T(8,128)(2,1)S(1)} %get-tuple-element.76), channel_id=1, source_target_pairs={{0,24},{4,28},{8,16},{12,20},{16,8},{20,12},{24,0},{28,4},{1,25},{... | collective-permute-start | bytes 196616 | tf_op jit(solution)/shard_map/ppermute | solution.py:468
  92.3 6.7 %collective-permute-start.15 = (bf16[128,256]{1,0:T(8,128)(2,1)S(1)}, bf16[128,256]{1,0:T(8,128)(2,1)S(1)}, u32[]{:S(2)}, u32[]{:S(2)}) collective-permute-start(bf16[128,256]{1,0:T(8,128)(2,1)S(1)} %get-tuple-element.76), channel_id=1, source_target_pairs={{0,20},{4,16},{8,28},{12,24},{16,4},{20,0},{24,12},{28,8},{1,21},{... | collective-permute-start | bytes 196616 | tf_op jit(solution)/shard_map/ppermute | solution.py:468
  93.6 5.7 %collective-permute-start.16 = (bf16[128,256]{1,0:T(8,128)(2,1)S(1)}, bf16[128,256]{1,0:T(8,128)(2,1)S(1)}, u32[]{:S(2)}, u32[]{:S(2)}) collective-permute-start(bf16[128,256]{1,0:T(8,128)(2,1)S(1)} %get-tuple-element.76), channel_id=1, source_target_pairs={{0,16},{4,20},{8,24},{12,28},{16,0},{20,4},{24,8},{28,12},{1,17},{... | collective-permute-start | bytes 196616 | tf_op jit(solution)/shard_map/ppermute | solution.py:468
  94.0 5.4 %collective-permute-start.17 = (bf16[128,256]{1,0:T(8,128)(2,1)S(1)}, bf16[128,256]{1,0:T(8,128)(2,1)S(1)}, u32[]{:S(2)}, u32[]{:S(2)}) collective-permute-start(bf16[128,256]{1,0:T(8,128)(2,1)S(1)} %get-tuple-element.76), channel_id=1, source_target_pairs={{0,12},{4,8},{8,4},{12,0},{16,28},{20,24},{24,20},{28,16},{1,13},{... | collective-permute-start | bytes 196616 | tf_op jit(solution)/shard_map/ppermute | solution.py:468
  94.9 4.9 %collective-permute-start.18 = (bf16[128,256]{1,0:T(8,128)(2,1)S(1)}, bf16[128,256]{1,0:T(8,128)(2,1)S(1)}, u32[]{:S(2)}, u32[]{:S(2)}) collective-permute-start(bf16[128,256]{1,0:T(8,128)(2,1)S(1)} %get-tuple-element.76), channel_id=1, source_target_pairs={{0,8},{4,12},{8,0},{12,4},{16,24},{20,28},{24,16},{28,20},{1,9},{5... | collective-permute-start | bytes 196616 | tf_op jit(solution)/shard_map/ppermute | solution.py:468
  96.0 3.8 %collective-permute-start.19 = (bf16[128,256]{1,0:T(8,128)(2,1)S(1)}, bf16[128,256]{1,0:T(8,128)(2,1)S(1)}, u32[]{:S(2)}, u32[]{:S(2)}) collective-permute-start(bf16[128,256]{1,0:T(8,128)(2,1)S(1)} %get-tuple-element.76), channel_id=1, source_target_pairs={{0,4},{4,0},{8,12},{12,8},{16,20},{20,16},{24,28},{28,24},{1,5},{5... | collective-permute-start | bytes 196616 | tf_op jit(solution)/shard_map/ppermute | solution.py:468
  99.8 12.7 %collective-permute-start.21 = (bf16[512,2560]{1,0:T(8,128)(2,1)S(1)}, bf16[512,2560]{1,0:T(8,128)(2,1)S(1)}, u32[]{:S(2)}, u32[]{:S(2)}) collective-permute-start(bf16[512,2560]{1,0:T(8,128)(2,1)S(1)} %joined.1.refs_0_), channel_id=1, source_target_pairs={{0,4},{4,0},{8,12},{12,8},{16,20},{20,16},{24,28},{28,24},{1,5},{5... | collective-permute-start | bytes 7864328 | tf_op jit(solution)/shard_map/ppermute | solution.py:468
  104.1 8.4 %collective-permute-start.20 = (bf16[128,1024]{1,0:T(8,128)(2,1)S(1)}, bf16[128,1024]{1,0:T(8,128)(2,1)S(1)}, u32[]{:S(2)}, u32[]{:S(2)}) collective-permute-start(bf16[128,1024]{1,0:T(8,128)(2,1)S(1)} %attention.3.rows_ref), channel_id=1, source_target_pairs={{0,1},{3,2},{4,5},{7,6},{8,9},{11,10},{12,13},{15,14},{16,17},{19,... | collective-permute-start | bytes 786440 | tf_op jit(solution)/shard_map/ppermute | solution.py:465
  107.5 22.8 %collective-permute-start.23 = (bf16[128,2560]{1,0:T(8,128)(2,1)S(1)}, bf16[128,2560]{1,0:T(8,128)(2,1)S(1)}, u32[]{:S(2)}, u32[]{:S(2)}) collective-permute-start(bf16[128,2560]{1,0:T(8,128)(2,1)S(1)} %mix.8.refs_0_), channel_id=1, source_target_pairs={{0,1},{3,2},{4,5},{7,6},{8,9},{11,10},{12,13},{15,14},{16,17},{19,... | collective-permute-start | bytes 1966088 | tf_op jit(solution)/shard_map/ppermute | solution.py:465
  114.0 17.5 %collective-permute-start.24 = (bf16[128,2560]{1,0:T(8,128)(2,1)S(1)}, bf16[128,2560]{1,0:T(8,128)(2,1)S(1)}, u32[]{:S(2)}, u32[]{:S(2)}) collective-permute-start(bf16[128,2560]{1,0:T(8,128)(2,1)S(1)} %added.9), channel_id=1, source_target_pairs={{1,2},{2,1},{5,6},{6,5},{9,10},{10,9},{13,14},{14,13},{17,18},{18,... | collective-permute-start | bytes 1966088 | tf_op jit(solution)/shard_map/ppermute | solution.py:459
  114.7 16.7 %collective-permute-start.22 = (bf16[128,1024]{1,0:T(8,128)(2,1)S(1)}, bf16[128,1024]{1,0:T(8,128)(2,1)S(1)}, u32[]{:S(2)}, u32[]{:S(2)}) collective-permute-start(bf16[128,1024]{1,0:T(8,128)(2,1)S(1)} %attention.4.rows_ref), channel_id=1, source_target_pairs={{0,1},{3,2},{4,5},{7,6},{8,9},{11,10},{12,13},{15,14},{16,17},{19,... | collective-permute-start | bytes 786440 | tf_op jit(solution)/shard_map/ppermute | solution.py:465
  130.5 14.8 %collective-permute-start.26 = (bf16[128,2560]{1,0:T(8,128)(2,1)S(1)}, bf16[128,2560]{1,0:T(8,128)(2,1)S(1)}, u32[]{:S(2)}, u32[]{:S(2)}) collective-permute-start(bf16[128,2560]{1,0:T(8,128)(2,1)S(1)} %added.10), channel_id=1, source_target_pairs={{1,2},{2,1},{5,6},{6,5},{9,10},{10,9},{13,14},{14,13},{17,18},{18,... | collective-permute-start | bytes 1966088 | tf_op jit(solution)/shard_map/ppermute | solution.py:459
  131.5 22.0 %collective-permute-start.25 = (bf16[128,2560]{1,0:T(8,128)(2,1)S(1)}, bf16[128,2560]{1,0:T(8,128)(2,1)S(1)}, u32[]{:S(2)}, u32[]{:S(2)}) collective-permute-start(bf16[128,2560]{1,0:T(8,128)(2,1)S(1)} %mix.10.refs_0_), channel_id=1, source_target_pairs={{0,1},{3,2},{4,5},{7,6},{8,9},{11,10},{12,13},{15,14},{16,17},{19,... | collective-permute-start | bytes 1966088 | tf_op jit(solution)/shard_map/ppermute | solution.py:465
  138.4 20.7 %collective-permute-start.30 = (bf16[128,1024]{1,0:T(8,128)(2,1)S(1)}, bf16[128,1024]{1,0:T(8,128)(2,1)S(1)}, u32[]{:S(2)}, u32[]{:S(2)}) collective-permute-start(bf16[128,1024]{1,0:T(8,128)(2,1)S(1)} %get-tuple-element.88.rows_ref), channel_id=1, source_target_pairs={{0,1},{3,2},{4,5},{7,6},{8,9},{11,10},{12,13},{15,14},{16,17},{19,... | collective-permute-start | bytes 786440 | tf_op jit(solution)/shard_map/ppermute | solution.py:465
  142.1 20.9 %collective-permute-start.32 = (bf16[128,2560]{1,0:T(8,128)(2,1)S(1)}, bf16[128,2560]{1,0:T(8,128)(2,1)S(1)}, u32[]{:S(2)}, u32[]{:S(2)}) collective-permute-start(bf16[128,2560]{1,0:T(8,128)(2,1)S(1)} %added.11), channel_id=1, source_target_pairs={{1,2},{2,1},{5,6},{6,5},{9,10},{10,9},{13,14},{14,13},{17,18},{18,... | collective-permute-start | bytes 1966088 | tf_op jit(solution)/shard_map/ppermute | solution.py:459
  143.0 20.0 %collective-permute-start.31 = (bf16[128,2560]{1,0:T(8,128)(2,1)S(1)}, bf16[128,2560]{1,0:T(8,128)(2,1)S(1)}, u32[]{:S(2)}, u32[]{:S(2)}) collective-permute-start(bf16[128,2560]{1,0:T(8,128)(2,1)S(1)} %added.12), channel_id=1, source_target_pairs={{1,0},{2,3},{5,4},{6,7},{9,8},{10,11},{13,12},{14,15},{17,16},{18,... | collective-permute-start | bytes 1966088 | tf_op jit(solution)/shard_map/ppermute | solution.py:462
  145.4 28.2 %collective-permute-start.28 = (bf16[128,2560]{1,0:T(8,128)(2,1)S(1)}, bf16[128,2560]{1,0:T(8,128)(2,1)S(1)}, u32[]{:S(2)}, u32[]{:S(2)}) collective-permute-start(bf16[128,2560]{1,0:T(8,128)(2,1)S(1)} %added.13), channel_id=1, source_target_pairs={{1,0},{2,3},{5,4},{6,7},{9,8},{10,11},{13,12},{14,15},{17,16},{18,... | collective-permute-start | bytes 1966088 | tf_op jit(solution)/shard_map/ppermute | solution.py:462
  153.7 20.0 %collective-permute-start.27 = (bf16[128,2560]{1,0:T(8,128)(2,1)S(1)}, bf16[128,2560]{1,0:T(8,128)(2,1)S(1)}, u32[]{:S(2)}, u32[]{:S(2)}) collective-permute-start(bf16[128,2560]{1,0:T(8,128)(2,1)S(1)} %mix.13.refs_0_), channel_id=1, source_target_pairs={{0,1},{3,2},{4,5},{7,6},{8,9},{11,10},{12,13},{15,14},{16,17},{19,... | collective-permute-start | bytes 1966088 | tf_op jit(solution)/shard_map/ppermute | solution.py:465
  159.1 14.8 %collective-permute-start.29 = (bf16[128,2560]{1,0:T(8,128)(2,1)S(1)}, bf16[128,2560]{1,0:T(8,128)(2,1)S(1)}, u32[]{:S(2)}, u32[]{:S(2)}) collective-permute-start(bf16[128,2560]{1,0:T(8,128)(2,1)S(1)} %added.14), channel_id=1, source_target_pairs={{1,2},{2,1},{5,6},{6,5},{9,10},{10,9},{13,14},{14,13},{17,18},{18,... | collective-permute-start | bytes 1966088 | tf_op jit(solution)/shard_map/ppermute | solution.py:459
